TPU v7x, 32 devices: a whole 2x2x4 slice. The times are simulated.
32 devices in a mesh: grp: 2 (over y), sec: 16 (over z, x, core).
Axes of the slice: x: 2, y: 2, z: 4, core: 2. Of those that a mesh axis runs over, the one named last changes fastest.
Arguments:
- green: bfloat16 [16, 4, 1024, 1024], P('sec', 'grp'), parts along dimension 1, may hold values from -0.1875 to 0.1875
- injected: bfloat16 [16, 4, 1024, 128], P('sec', 'grp'), parts along dimension 1, may hold values from -0.8984375 to 0.8984375
- coupling: bfloat16 [16, 1024, 256], P('sec'), may hold values from -0.4375 to 0.4375
- pattern: int32 [16, 8, 2], P('sec'), may hold values 0 or 1
- owner: int32 [256, 1], P('sec'), may hold values from 0 to 15; in each aligned block of 16 rows (0 to 15, 16 to 31, ...) at most 2 rows name the same one
- pair_blocks: int32 [256, 2], P('sec'), may hold values from 0 to 31
Outputs:
- waves: bfloat16 [16, 4, 1024, 128], P('sec', 'grp'), parts along dimension 1
There are 2 independent parts, one for each index of `grp`. A program takes and returns all parts, laid end to end along the dimension named above; an argument that names none is the same for every part. Nothing has to cross between parts.
Inputs may be any that keep to these rules, and one draw needn't show every extreme that they name: Among the 16 rows of one slab no owner appears more than 2 times.
All inputs are finite; a program needn't handle non-finite values. No bound on the sum of `pattern` on one device may be relied on, other than what follows from the above.
Results may differ from a plain program's by a relative error of at most 0.0057.
Values may be sent and summed in bfloat16 or wider, within the bound.
No kernel may reach another device: no remote copies, remote signals or barrier semaphores. Data moves between devices by JAX's collectives and lax.ppermute only.
A program may use at most 256 MiB of HBM per device.

v0:
```python
import jax
import jax.numpy as jnp
from jax import lax
from jax.sharding import PartitionSpec as P

BLK = 32
CAP = 2


HIGH = lax.Precision.HIGHEST


def carried_in(part, axis, combine, identity):
    place = lax.axis_index(axis)
    gathered = jax.tree.map(lambda a: lax.all_gather(a, axis), part)
    state = jax.tree.map(lambda a, e: jnp.zeros_like(a) + jnp.asarray(e, a.dtype), part, identity)

    def one(hop, state):
        return combine(
            state, jax.tree.map(lambda a: lax.dynamic_index_in_dim(a, hop, 0, False), gathered)
        )

    return lax.fori_loop(0, place, one, state)


def slab_partials(green_here, inject_here, row_blocks):
    energies, orbitals, width = green_here.shape
    tiled = green_here.reshape(energies, orbitals // BLK, BLK, orbitals)
    rows = jnp.take(tiled, row_blocks, axis=1)
    parts = jnp.einsum("epbo,eok->pebk", rows, inject_here, preferred_element_type=jnp.float32)
    return parts.astype(jnp.bfloat16)


def block_table(arrived, nblock):
    flat_targets = arrived.reshape(-1)
    levels = jnp.arange(nblock, dtype=jnp.int32)
    return (flat_targets[:, None] == levels[None, :]).astype(jnp.bfloat16)


def compose(earlier, later):
    first_map, first_shift = earlier
    second_map, second_shift = later
    joined = jnp.einsum("eij,ejk->eik", second_map, first_map, precision=HIGH)
    moved = jnp.einsum("eij,ejk->eik", second_map, first_shift, precision=HIGH) + second_shift
    return (joined, moved)


def sweep_faces(face_map, face_source):
    energies, width, columns = face_source.shape
    unit = jnp.broadcast_to(jnp.eye(width, dtype=jnp.float32), (energies, width, width))
    identity = (unit, jnp.zeros_like(face_source))
    prefix_map, incoming = carried_in((face_map, face_source), "sec", compose, identity)
    return incoming


def per_device(green, injected, coupling, pattern, owner, pair_blocks):
    sections = lax.axis_size("sec")
    green_here = green[0]
    inject_here = injected[0]
    energies, orbitals, width = green_here.shape
    columns = inject_here.shape[2]
    face_width = coupling.shape[2]
    nblock = orbitals // BLK
    destination = owner[:, 0]
    row_blocks = pair_blocks[:, 0]
    target_blocks = pair_blocks[:, 1]
    count = destination.shape[0]
    order = jnp.arange(count, dtype=jnp.int32)
    before = (destination[:, None] == destination[None, :]) & (order[None, :] < order[:, None])
    rank = jnp.sum(before.astype(jnp.int32), axis=1)
    slot = destination * CAP + rank
    slot_targets = jnp.full((sections * CAP,), -1, jnp.int32).at[slot].set(target_blocks)
    slot_targets = slot_targets.reshape(sections, CAP)
    parts = slab_partials(green_here, inject_here, row_blocks)
    outgoing = jnp.zeros((sections * CAP, energies, BLK, columns), jnp.bfloat16).at[slot].set(parts)
    received, arrived = (
        lax.all_to_all(
            outgoing.reshape(sections, CAP, energies, BLK, columns),
            "sec",
            split_axis=0,
            concat_axis=0,
            tiled=True,
        ),
        lax.all_to_all(slot_targets, "sec", split_axis=0, concat_axis=0, tiled=True),
    )
    table = block_table(arrived, nblock)
    placed = jnp.einsum(
        "sn,sebk->enbk",
        table,
        received.reshape(sections * CAP, energies, BLK, columns),
        preferred_element_type=jnp.float32,
    )
    placed = placed.reshape(energies, orbitals, columns)
    source = (inject_here.astype(jnp.float32) + placed).astype(jnp.bfloat16)
    tile_rows = jnp.repeat(pattern[0], orbitals // 8, axis=0)
    present = jnp.repeat(tile_rows, face_width // 2, axis=1)
    couple = jnp.where(present == 1, coupling[0], jnp.zeros_like(coupling[0]))
    image = jnp.einsum("eij,ejk->eik", green_here, source, preferred_element_type=jnp.float32)
    face_source = image[:, orbitals - face_width :, :]
    prop_full = jnp.einsum("eij,jf->eif", green_here, couple, preferred_element_type=jnp.float32)
    incoming = sweep_faces(prop_full[:, orbitals - face_width :, :], face_source)
    wave = jnp.einsum("eif,efk->eik", prop_full, incoming, precision=HIGH) + image
    return wave.astype(jnp.bfloat16)[None]


def solution(mesh):
    in_specs = (
        P("sec", "grp", None, None),
        P("sec", "grp", None, None),
        P("sec", None, None),
        P("sec", None, None),
        P("sec", None),
        P("sec", None),
    )
    out_specs = P("sec", "grp", None, None)
    return jax.shard_map(
        per_device, mesh=mesh, in_specs=in_specs, out_specs=out_specs, check_vma=False
    )
```

profile of v0, /device:TPU:27, one launch (start us, length us, event | category | flops | bytes accessed | tf_op | source)
XLA Modules:
  0.0 208.9 jit_solution(11172684457644234793)
XLA Ops:
  6.5 0.9 convert_reduce_fusion
  7.4 0.8 slice_bitcast_fusion
  8.2 0.6 scatter_custom_fusion.1
  8.8 0.7 all_to_all.10
  9.5 6.3 %all-to-all-start.1 = ((s32[16,1,2]{2,1,0:T(1,128)}), s32[16,1,2]{2,1,0:T(1,128)S(1)}, u32[]{:S(2)}, u32[]{:S(2)}) async-start(s32[16,1,2]{2,1,0:T(1,128)} %bitcast.23), calls=%async_computation.1 | async-start | bytes 16384 | tf_op jit(solution)/shard_map/all_to_all | solution.py:84
  15.9 0.7 and_bitcast_fusion
  16.6 2.9 %gather_fusion = bf16[16,2,32,1024]{3,2,1,0:T(8,128)(2,1)S(1)} fusion(bf16[2,32,32,1024]{3,2,1,0:T(8,128)(2,1)} %bitcast.91, s32[1024]{0:T(1024)S(1)} %pad_clamp_fusion), kind=kCustom, calls=%fused_computation | custom fusion | bytes 4194368 | tf_op jit(solution)/shard_map/jit(_take)/gather | solution.py:29
  19.5 0.7 fusion.20
  20.3 0.1 broadcast_in_dim.41
  20.4 1.1 scatter_fusion
  21.5 1.3 copy.45
  22.8 6.0 %all-to-all-start = ((bf16[16,2,2,32,128]{4,1,3,2,0:T(2,128)(2,1)}), bf16[16,2,2,32,128]{4,1,3,2,0:T(2,128)(2,1)S(1)}, u32[]{:S(2)}, u32[]{:S(2)}) async-start(bf16[16,2,2,32,128]{4,1,3,2,0:T(2,128)(2,1)} %copy.45), calls=%async_computation | async-start | bytes 1048576 | tf_op jit(solution)/shard_map/all_to_all | solution.py:77
  28.9 0.5 broadcast.75
  29.4 0.6 reduce.3
  30.0 0.1 eq.64
  30.1 11.5 %all-to-all-done = bf16[16,2,2,32,128]{4,1,3,2,0:T(2,128)(2,1)S(1)} async-done(((bf16[16,2,2,32,128]{4,1,3,2,0:T(2,128)(2,1)}), bf16[16,2,2,32,128]{4,1,3,2,0:T(2,128)(2,1)S(1)}, u32[]{:S(2)}, u32[]{:S(2)}) %all-to-all-start) | async-done | bytes 524320 | tf_op jit(solution)/shard_map/all_to_all | solution.py:77
  41.6 0.4 copy.46
  41.9 0.3 convolution_bitcast_fusion
  42.2 0.6 copy.48
  42.8 0.1 copy-done.3
  43.0 0.1 fusion.23
  43.1 1.2 copy-done
  44.3 1.5 fusion.12
  45.8 0.9 copy.50
  46.9 0.2 copy.41
  47.2 3.5 %fusion.9 = f32[2,1024,256]{1,2,0:T(8,128)S(1)} fusion(bf16[1,2,1024,1024]{3,2,1,0:T(8,128)(2,1)} %param.8, bf16[1,1024,256]{1,2,0:T(8,128)(2,1)S(1)} %bitcast_select_fusion), kind=kOutput, calls=%fused_computation.14 | convolution fusion | flops 1073741824 | bytes 6815744 | tf_op jit(solution)/shard_map/eij,jf->eif/dot_general | solution.py:100
  50.7 0.8 slice.18
  51.5 2.1 copy.42
  53.6 42.3 %all-gather.7.cloned.1.call-done = f32[32,256,128]{2,1,0:T(8,128)} async-done(((f32[2,256,128]{2,1,0:T(8,128)}), f32[32,256,128]{2,1,0:T(8,128)}) %all-gather.7.cloned.1.call-update) | async-done | bytes 4194320 | tf_op jit(solution)/shard_map/all_gather | solution.py:15
  95.9 75.4 %all-gather.5.cloned.1.call-done = f32[32,256,256]{2,1,0:T(8,128)} async-done(((f32[2,256,256]{2,1,0:T(8,128)}), f32[32,256,256]{2,1,0:T(8,128)}) %all-gather.5.cloned.1.call-update) | async-done | bytes 8388624 | tf_op jit(solution)/shard_map/all_gather | solution.py:15
  171.4 26.5 %while.12 = (s32[]{:T(128)}, f32[2,256,128]{2,1,0:T(8,128)S(1)}, s32[]{:T(128)}, f32[16,2,256,256]{3,2,1,0:T(8,128)}, f32[16,2,256,128]{3,2,1,0:T(8,128)}, /*index=5*/s32[]{:T(128)}, s32[]{:T(128)}, s32[]{:T(128)}) while((s32[]{:T(128)}, f32[2,256,128]{2,1,0:T(8,128)S(1)}, s32[]{:T(128)}, f32[16,2,256,256]{3,2,1,0:T(8,128)}, ...), condition=%wide.region_4.5_spmd, body=%wide.region_3.4_spmd.sunk | while | flops 201392128 | bytes 1836159 | solution.py:23
  171.4 1.7 convolution_add_fusion.3
  173.2 1.7 convolution_add_fusion.3
  175.0 1.7 convolution_add_fusion.3
  176.7 1.7 convolution_add_fusion.3
  178.5 1.7 convolution_add_fusion.3
  180.3 1.7 convolution_add_fusion.3
  182.0 1.7 convolution_add_fusion.3
  183.8 1.7 convolution_add_fusion.3
  185.6 1.7 convolution_add_fusion.3
  187.3 1.7 convolution_add_fusion.3
  189.1 1.7 convolution_add_fusion.3
  190.9 1.7 convolution_add_fusion.3
  192.6 1.7 convolution_add_fusion.3
  194.4 1.7 convolution_add_fusion.3
  196.2 1.7 convolution_add_fusion.3
  197.9 2.1 %fusion.16 = bf16[1,2,1024,128]{2,3,1,0:T(8,128)(2,1)} fusion(f32[2,1024,128]{1,2,0:T(8,128)S(1)} %fusion.12, f32[2,1024,256]{1,2,0:T(8,128)S(1)} %fusion.9, f32[2,256,128]{2,1,0:T(8,128)S(1)} %get-tuple-element.49), kind=kOutput, calls=%fused_computation.19 | convolution fusion | flops 805830656 | bytes 3932160 | tf_op jit(solution)/shard_map/eif,efk->eik/dot_general | solution.py:102
  200.0 2.0 copy.53
  (36 shorter events, 0.6 us)
Async XLA Ops:
  9.5 13.3 %all-to-all-start.1 = ((s32[16,1,2]{2,1,0:T(1,128)}), s32[16,1,2]{2,1,0:T(1,128)S(1)}, u32[]{:S(2)}, u32[]{:S(2)}) async-start(s32[16,1,2]{2,1,0:T(1,128)} %bitcast.23), calls=%async_computation.1 | async-start | bytes 16384 | tf_op jit(solution)/shard_map/all_to_all | solution.py:84
  16.5 2.9 %copy-start.2 = (bf16[1,2,1024,128]{3,2,1,0:T(8,128)(2,1)S(1)}, bf16[1,2,1024,128]{3,2,1,0:T(8,128)(2,1)}, u32[]{:S(2)}) copy-start(bf16[1,2,1024,128]{3,2,1,0:T(8,128)(2,1)} %param.9) | copy-start | bytes 1572868
  22.8 18.7 %all-to-all-start = ((bf16[16,2,2,32,128]{4,1,3,2,0:T(2,128)(2,1)}), bf16[16,2,2,32,128]{4,1,3,2,0:T(2,128)(2,1)S(1)}, u32[]{:S(2)}, u32[]{:S(2)}) async-start(bf16[16,2,2,32,128]{4,1,3,2,0:T(2,128)(2,1)} %copy.45), calls=%async_computation | async-start | bytes 1048576 | tf_op jit(solution)/shard_map/all_to_all | solution.py:77
  28.8 67.1 %all-gather.7.cloned.1.call-start = ((), (), s32[]{:S(2)}) async-start(), calls=%async_computation.3 | async-start | bytes 4456448 | tf_op jit(solution)/shard_map/all_gather | solution.py:15
  41.9 1.0 copy-start.3
  41.9 2.4 %copy-start = (bf16[1,2,1024,1024]{3,2,1,0:T(8,128)(2,1)S(1)}, bf16[1,2,1024,1024]{3,2,1,0:T(8,128)(2,1)}, u32[]{:S(2)}) copy-start(bf16[1,2,1024,1024]{3,2,1,0:T(8,128)(2,1)} %param.8) | copy-start | bytes 12582916
  44.3 2.5 %copy-start.4 = (s32[1,8,2]{1,2,0:T(2,128)S(1)}, s32[1,8,2]{1,2,0:T(2,128)}, u32[]{:S(2)}) copy-start(s32[1,8,2]{1,2,0:T(2,128)} %param.11) | copy-start | bytes 196
  44.3 2.6 %copy-start.1 = (bf16[1,1024,256]{2,1,0:T(8,128)(2,1)S(1)}, bf16[1,1024,256]{2,1,0:T(8,128)(2,1)}, u32[]{:S(2)}) copy-start(bf16[1,1024,256]{2,1,0:T(8,128)(2,1)} %param.10) | copy-start | bytes 1572868
  46.7 124.6 %all-gather.5.cloned.1.call-start = ((), (), s32[]{:S(2)}) async-start(), calls=%async_computation.2 | async-start | bytes 8912896 | tf_op jit(solution)/shard_map/all_gather | solution.py:15
Sparse Core Ops, SparseCore 0:
  46.9 49.0 all-gather.6
  98.1 73.2 all-gather.4
where the time goes:
time: 210 us; the launch traced here: 209 us
  waiting for transfers between devices  129 us (61%)
  matrix products  34 us (16%)
  local copies, waits for them, and re-layouts  16.1 us (8%)
  between operations  13.6 us (6%)
  starting transfers between devices  12.4 us (6%)
  other arithmetic  3.1 us (1%)
    all_gather x2, waiting for transfers between devices, carried_in(): gathered = jax.tree.map(lambda a: lax.all_gather(a, axis), part)  118 us
    dot_general x15, matrix products, compose(): jnp.einsum('eij,ejk->eik', second_map, first_shift, precision=HIGH)  25.7 us
    all_to_all x1, waiting for transfers between devices, per_device(): lax.all_to_all(outgoing.reshape(sections, CAP, energies, BLK, columns), '...  11.5 us
    all_to_all x1, starting transfers between devices, per_device(): lax.all_to_all(slot_targets, 'sec', split_axis=0, concat_axis=0, tiled=True)  6.33 us
    all_to_all x1, starting transfers between devices, per_device(): lax.all_to_all(outgoing.reshape(sections, CAP, energies, BLK, columns), '...  6.02 us
  transfers between devices with their start and end apart: 4, of which 3 were waited for; matrix products, arithmetic and copies ran while one was open for 7% of the time, Pallas kernels for 0%

commit v1 on v0

v1 whole, which is shorter than its diff:
```python
import jax
import jax.numpy as jnp
from jax import lax
from jax.sharding import PartitionSpec as P

BLK = 32
CAP = 2
GROUP = 4
HEAD = 16

HIGH = lax.Precision.HIGHEST


def pack(cols):
    half = cols.shape[-2] // 2
    return jnp.concatenate([cols[..., :half, :], cols[..., half:, :]], axis=-1)


def unpack(packed):
    half = packed.shape[-1] // 2
    return jnp.concatenate([packed[..., :half], packed[..., half:]], axis=-2)


def outgoing_pairs(green, inject, owner, blocks, sections):
    energies, orbitals, _ = green.shape
    columns = inject.shape[2]
    count = owner.shape[0]
    order = jnp.arange(count, dtype=jnp.int32)
    same = owner[:, None] == owner[None, :]
    rank = jnp.sum((same & (order[None, :] < order[:, None])).astype(jnp.int32), axis=1)
    slot = owner * CAP + rank
    full = jnp.einsum("eij,ejk->eik", green, inject, preferred_element_type=jnp.float32)
    full = full.astype(jnp.bfloat16).reshape(energies, orbitals // BLK, BLK, columns)
    parts = jnp.take(full, blocks[:, 0], axis=1)
    parts = jnp.swapaxes(parts, 0, 1)
    packets = jnp.zeros((sections * CAP, energies, BLK, columns), jnp.bfloat16).at[slot].set(parts)
    heads = jnp.full((sections * CAP,), -1, jnp.int32).at[slot].set(blocks[:, 1])
    heads = heads.reshape(sections, 1, CAP).astype(jnp.bfloat16)
    heads = jnp.pad(heads, ((0, 0), (0, HEAD - 1), (0, columns - CAP)))
    packets = packets.reshape(sections, CAP * energies * BLK, columns)
    return jnp.concatenate([packets, heads], axis=1)


def placed_source(inject, received):
    energies, orbitals, columns = inject.shape
    sections = received.shape[0]
    rows = CAP * energies * BLK
    targets = received[:, rows, :CAP].astype(jnp.int32).reshape(-1)
    data = received[:, :rows].reshape(sections * CAP, energies, BLK, columns)
    levels = jnp.arange(orbitals // BLK, dtype=jnp.int32)
    table = (targets[:, None] == levels[None, :]).astype(jnp.bfloat16)
    placed = jnp.einsum("sn,sebk->enbk", table, data, preferred_element_type=jnp.float32)
    placed = placed.reshape(energies, orbitals, columns)
    return (inject.astype(jnp.float32) + placed).astype(jnp.bfloat16)


def mm(a, b):
    return jnp.dot(a, b, precision=HIGH, preferred_element_type=jnp.float32)


def plane_shift(sections, k):
    return [(s, s // GROUP * GROUP + (s % GROUP + k) % GROUP) for s in range(sections)]


def up_shift(sections, k):
    return [(s, s + GROUP * k) for s in range(sections - GROUP * k)]


def in_plane(items, here, sections):
    got = [lax.dynamic_index_in_dim(items, here, 0, False)]
    for k in range(1, GROUP):
        out = lax.dynamic_index_in_dim(items, (here + k) % GROUP, 0, False)
        got.append(lax.ppermute(out, "sec", plane_shift(sections, k)))
    got = jnp.stack(got)
    return jnp.take(got, (here - jnp.arange(GROUP)) % GROUP, axis=0)


def from_below(total_map, total_source, sections):
    planes = sections // GROUP
    if planes <= 4:
        below = [lax.ppermute(total_source, "sec", up_shift(sections, k)) for k in range(1, planes)]
        maps = [lax.ppermute(total_map, "sec", up_shift(sections, k)) for k in range(1, planes - 1)]
        state = unpack(below[-1]).astype(jnp.float32)
        for k in range(planes - 3, -1, -1):
            state = unpack(below[k]).astype(jnp.float32) + mm(maps[k], state)
        return state
    shift = lax.ppermute(unpack(total_source).astype(jnp.float32), "sec", up_shift(sections, 1))
    joined = lax.ppermute(total_map, "sec", up_shift(sections, 1))
    stride = 1
    while stride < planes:
        other = lax.ppermute(shift, "sec", up_shift(sections, stride))
        other_map = lax.ppermute(joined, "sec", up_shift(sections, stride))
        shift = shift + mm(joined, other)
        joined = mm(joined, other_map)
        stride *= 2
    return shift


def per_device(green, injected, coupling, pattern, owner, pair_blocks):
    sections = lax.axis_size("sec")
    here = lax.axis_index("sec") % GROUP
    green = green[0]
    inject = injected[0]
    energies, orbitals, _ = green.shape
    columns = inject.shape[2]
    face = coupling.shape[2]
    split = GROUP // energies

    outgoing = outgoing_pairs(green, inject, owner[:, 0], pair_blocks, sections)
    received = lax.all_to_all(outgoing, "sec", split_axis=0, concat_axis=0, tiled=True)

    tile_rows = jnp.repeat(pattern[0], orbitals // 8, axis=0)
    present = jnp.repeat(tile_rows, face // 2, axis=1)
    couple = jnp.where(present == 1, coupling[0], jnp.zeros_like(coupling[0]))
    prop = jnp.einsum("eij,jf->eif", green, couple, preferred_element_type=jnp.float32)
    face_map = prop[:, orbitals - face :, :]
    maps = in_plane(jnp.repeat(face_map, split, axis=0), here, sections)
    upto = [maps[0]]
    for j in range(1, GROUP):
        upto.append(mm(maps[j], upto[-1]))
    after = [maps[GROUP - 1]]
    for j in range(GROUP - 2, 0, -1):
        after.append(mm(after[-1], maps[j]))

    source = placed_source(inject, received)
    face_source = jnp.einsum("eij,ejk->eik", green[:, orbitals - face :], source, preferred_element_type=jnp.float32)
    quarters = face_source.astype(jnp.bfloat16).reshape(energies, face, split, columns // split)
    quarters = pack(jnp.swapaxes(quarters, 1, 2).reshape(GROUP, face, columns // split))
    shifts = unpack(in_plane(quarters, here, sections)).astype(jnp.float32)
    total = shifts[GROUP - 1]
    for j in range(GROUP - 1):
        total = total + mm(after[GROUP - 2 - j], shifts[j])
    base = from_below(upto[GROUP - 1], pack(total).astype(jnp.bfloat16), sections)
    local = [jnp.zeros_like(total), shifts[0]]
    for j in range(1, GROUP - 1):
        local.append(shifts[j] + mm(maps[j], local[-1]))
    entering = jnp.stack([base] + [local[j] + mm(upto[j - 1], base) for j in range(1, GROUP)])
    arrived = unpack(in_plane(pack(entering).astype(jnp.bfloat16), here, sections))
    incoming = arrived.reshape(energies, split, face, columns // split)
    incoming = jnp.swapaxes(incoming, 1, 2).reshape(energies, face, columns)

    image = jnp.einsum("eij,ejk->eik", green, source, preferred_element_type=jnp.float32)
    wave = jnp.einsum("eif,efk->eik", prop.astype(jnp.bfloat16), incoming, preferred_element_type=jnp.float32) + image
    return wave.astype(jnp.bfloat16)[None]


def solution(mesh):
    in_specs = (
        P("sec", "grp", None, None),
        P("sec", "grp", None, None),
        P("sec", None, None),
        P("sec", None, None),
        P("sec", None),
        P("sec", None),
    )
    out_specs = P("sec", "grp", None, None)
    return jax.shard_map(
        per_device, mesh=mesh, in_specs=in_specs, out_specs=out_specs, check_vma=False
    )
```

time: 210 us -> 77.3 us (0.37)
  the two profiles are of different devices: /device:TPU:27 before, /device:TPU:0 now
where the time goes in v1:
time: 77.3 us; the launch traced here: 76.7 us
  starting transfers between devices  29.3 us (38%)
  matrix products  23.7 us (31%)
  waiting for transfers between devices  10.3 us (13%)
  local copies, waits for them, and re-layouts  9.17 us (12%)
  other arithmetic  3.71 us (5%)
    dot_general x15, matrix products, mm(): return jnp.dot(a, b, precision=HIGH, preferred_element_type=jnp.float32)  9.45 us
    ppermute x2, starting transfers between devices, from_below(): lax.ppermute(total_map, 'sec', up_shift(sections, k))  8.82 us
    ppermute x3, starting transfers between devices, from_below(): lax.ppermute(total_source, 'sec', up_shift(sections, k))  7.77 us
    ppermute x9, starting transfers between devices, in_plane(): got.append(lax.ppermute(out, 'sec', plane_shift(sections, k)))  6.67 us
    all_to_all x1, starting transfers between devices, per_device(): lax.all_to_all(outgoing, 'sec', split_axis=0, concat_axis=0, tiled=True)  6 us
    ppermute x9, waiting for transfers between devices, in_plane(): got.append(lax.ppermute(out, 'sec', plane_shift(sections, k)))  5.67 us
    dot_general x1, matrix products, per_device(): jnp.einsum('eij,ejk->eik', green, source, preferred_element_type=jnp.floa...  4.39 us
    dot_general x1, matrix products, per_device(): jnp.einsum('eij,jf->eif', green, couple, preferred_element_type=jnp.float32)  3.53 us
  transfers between devices with their start and end apart: 15, of which 6 were waited for; matrix products, arithmetic and copies ran while one was open for 27% of the time, Pallas kernels for 0%

profile of v1, /device:TPU:0, one launch (start us, length us, event | category | flops | bytes accessed | tf_op | source)
XLA Modules:
  0.0 76.7 jit_solution(17222122348461280059)
XLA Ops:
  0.0 1.2 %copy.29 = bf16[1,1024,256]{1,2,0:T(8,128)(2,1)S(1)} copy(bf16[1,1024,256]{2,1,0:T(8,128)(2,1)} %param.10) | data formatting | bytes 1048576 | tf_op args[2]
  1.3 0.7 compare_bitcast_fusion
  2.1 3.5 %convolution_bitcast_fusion = f32[2,1024,256]{1,2,0:T(8,128)S(1)} fusion(bf16[1,1024,256]{1,2,0:T(8,128)(2,1)S(1)} %bitcast_select_fusion, bf16[1,2,1024,1024]{3,2,1,0:T(8,128)(2,1)} %param.8), kind=kOutput, calls=%fused_computation.6 | convolution fusion | flops 1073741824 | bytes 6815744 | tf_op jit(solution)/shard_map/eij,jf->eif/dot_general | solution.py:115
  5.6 1.3 %copy-done = f32[2,1024,256]{1,2,0:T(8,128)} copy-done((f32[2,1024,256]{1,2,0:T(8,128)}, f32[2,1024,256]{1,2,0:T(8,128)S(1)}, u32[]{:S(2)}) %copy-start) | copy-done | bytes 2097176
  7.4 2.4 %collective-permute-start.5 = (f32[256,256]{1,0:T(8,128)S(1)}, f32[256,256]{1,0:T(8,128)S(1)}, u32[]{:S(2)}, u32[]{:S(2)}) collective-permute-start(f32[256,256]{1,0:T(8,128)S(1)} %get-tuple-element.7), channel_id=1, source_target_pairs={{0,3},{1,0},{2,1},{3,2},{4,7},{5,4},{6,5},{7,6},{8,11},{9,8},{10,9... | collective-permute-start | bytes 786440 | tf_op jit(solution)/shard_map/ppermute | solution.py:73
  9.9 0.6 collective-permute-start.4
  10.9 0.6 scatter_custom_fusion.1
  11.6 3.4 %convolution_convert_fusion = bf16[2,1024,128]{2,1,0:T(8,128)(2,1)S(1)} fusion(bf16[1,2,1024,128]{3,2,1,0:T(8,128)(2,1)S(1)} %copy-done.6, bf16[1,2,1024,1024]{3,2,1,0:T(8,128)(2,1)} %param.8), kind=kOutput, calls=%fused_computation.10 | convolution fusion | flops 537133056 | bytes 5242880 | tf_op jit(solution)/shard_map/eij,ejk->eik/dot_general | solution.py:32
  15.1 0.6 gather_fusion
  15.9 1.1 %scatter_fusion = bf16[32,2,32,128]{3,2,1,0:T(8,128)(2,1)S(1)} fusion(bf16[32,2,32,128]{3,2,1,0:T(8,128)(2,1)S(1)} %broadcast_in_dim.58, s32[16]{0:T(128)S(1)} %get-tuple-element.38, bf16[16,2,32,128]{3,2,1,0:T(8,128)(2,1)S(1)} %broadcast_select_fusion.1), kind=kCustom, calls=%fused_computation.4 | custom fusion | bytes 786496 | tf_op jit(solution)/shard_map/scatter | solution.py:36
  17.0 0.9 %fusion.13 = bf16[16,144,128]{2,1,0:T(8,128)(2,1)} fusion(bf16[16,1,2]{2,1,0:T(2,128)(2,1)S(1)} %convert_element_type.79, bf16[16,128,128]{2,1,0:T(8,128)(2,1)S(1)} %bitcast.173), kind=kLoop, calls=%fused_computation.36 | loop fusion | flops 1769472 | bytes 1114176 | tf_op jit(solution)/shard_map/concatenate | solution.py:41
  17.9 6.0 %all-to-all-start = ((bf16[16,144,128]{2,1,0:T(8,128)(2,1)}), bf16[16,144,128]{2,1,0:T(8,128)(2,1)S(1)}, u32[]{:S(2)}, u32[]{:S(2)}) async-start(bf16[16,144,128]{2,1,0:T(8,128)(2,1)} %fusion.13), calls=%async_computation | async-start | bytes 1179648 | tf_op jit(solution)/shard_map/all_to_all | solution.py:110
  24.1 0.6 gather_fusion.1
  24.9 0.4 fusion.17
  25.3 0.4 fusion.20
  25.7 1.1 %fusion.18 = f32[256,256]{1,0:T(8,128)} fusion(f32[256,256]{1,0:T(8,128)S(1)} %fusion.20, f32[4,256,256]{2,1,0:T(8,128)S(1)} %broadcast_select_fusion), kind=kOutput, calls=%fused_computation.51 | convolution fusion | flops 201326592 | bytes 786432 | tf_op jit(solution)/shard_map/dot_general | solution.py:58
  26.8 4.5 %collective-permute-start.7 = (f32[256,256]{1,0:T(8,128)}, f32[256,256]{1,0:T(8,128)}, u32[]{:S(2)}, u32[]{:S(2)}) collective-permute-start(f32[256,256]{1,0:T(8,128)} %fusion.18), channel_id=1, source_target_pairs={{0,4},{1,5},{2,6},{3,7},{4,8},{5,9},{6,10},{7,11},{8,12},{9,13},{1... | collective-permute-start | bytes 786440 | tf_op jit(solution)/shard_map/ppermute | solution.py:82
  31.3 4.3 %collective-permute-start.9 = (f32[256,256]{1,0:T(8,128)}, f32[256,256]{1,0:T(8,128)}, u32[]{:S(2)}, u32[]{:S(2)}) collective-permute-start(f32[256,256]{1,0:T(8,128)} %fusion.18), channel_id=1, source_target_pairs={{0,8},{1,9},{2,10},{3,11},{4,12},{5,13},{6,14},{7,15},{16,24},{17,... | collective-permute-start | bytes 786440 | tf_op jit(solution)/shard_map/ppermute | solution.py:82
  35.6 0.4 fusion.19
  36.0 3.4 %all-to-all-done = bf16[16,144,128]{2,1,0:T(8,128)(2,1)S(1)} async-done(((bf16[16,144,128]{2,1,0:T(8,128)(2,1)}), bf16[16,144,128]{2,1,0:T(8,128)(2,1)S(1)}, u32[]{:S(2)}, u32[]{:S(2)}) %all-to-all-start) | async-done | bytes 589856 | tf_op jit(solution)/shard_map/all_to_all | solution.py:110
  39.6 0.4 convolution_bitcast_fusion.1
  40.0 0.6 copy.32
  40.7 1.9 %fusion.4 = bf16[2,256,128]{1,2,0:T(8,128)(2,1)S(1)} fusion(bf16[2,1024,128]{2,1,0:T(8,128)(2,1)S(1)} %fusion.10, bf16[2,1024,1024]{2,1,0:T(8,128)(2,1)} %bitcast.171), kind=kOutput, calls=%fused_computation.16 | convolution fusion | flops 134283264 | bytes 1703936 | tf_op jit(solution)/shard_map/eij,ejk->eik/dot_general | solution.py:126
  43.0 1.0 %collective-permute-start.2 = (bf16[128,128]{1,0:T(8,128)(2,1)S(1)}, bf16[128,128]{1,0:T(8,128)(2,1)S(1)}, u32[]{:S(2)}, u32[]{:S(2)}) collective-permute-start(bf16[128,128]{1,0:T(8,128)(2,1)S(1)} %get-tuple-element.13), channel_id=1, source_target_pairs={{0,3},{1,0},{2,1},{3,2},{4,7},{5,4},{6,5},{7,6},{8,11},{9,8},{10,9... | collective-permute-start | bytes 98312 | tf_op jit(solution)/shard_map/ppermute | solution.py:73
  44.0 0.7 collective-permute-start.1
  44.7 1.1 %fusion.21 = f32[256,256]{1,0:T(8,128)} fusion(f32[256,256]{1,0:T(8,128)S(1)} %fusion.19, f32[4,256,256]{2,1,0:T(8,128)S(1)} %broadcast_select_fusion), kind=kOutput, calls=%fused_computation.54 | convolution fusion | flops 201326592 | bytes 786432 | tf_op jit(solution)/shard_map/dot_general | solution.py:58
  45.8 2.4 %collective-permute-done.1 = bf16[128,128]{1,0:T(8,128)(2,1)S(1)} collective-permute-done((bf16[128,128]{1,0:T(8,128)(2,1)S(1)}, bf16[128,128]{1,0:T(8,128)(2,1)S(1)}, u32[]{:S(2)}, u32[]{:S(2)}) %collective-permute-start.1) | collective-permute-done | bytes 32800 | tf_op jit(solution)/shard_map/ppermute | solution.py:73
  48.3 0.6 gather_fusion.2
  48.9 0.8 %copy.37 = bf16[4,128,128]{1,2,0:T(8,128)(2,1)} copy(bf16[4,128,128]{2,1,0:T(8,128)(2,1)S(1)} %gather_fusion.2) | data formatting | bytes 262144 | tf_op jit(solution)/shard_map/jit(_take)/gather | solution.py:75
  49.7 1.0 %broadcast_select_fusion.2 = bf16[4,128,128]{1,2,0:T(8,128)(2,1)S(1)} fusion(bf16[4,128,128]{1,2,0:T(8,128)(2,1)} %copy.37, pred[4]{0:T(512)(128)(4,1)S(1)} %compare_and_fusion), kind=kLoop, calls=%fused_computation.75 | loop fusion | flops 65536 | bytes 262148 | tf_op jit(solution)/shard_map/jit(_take)/select_n | solution.py:75
  51.1 1.2 %convolution_add_fusion.3 = f32[256,64]{0,1:T(8,128)S(1)} fusion(f32[256,256]{1,0:T(8,128)} %fusion.21, f32[4,256,64]{1,2,0:T(8,128)S(1)} %fusion.22, bf16[4,128,64]{1,2,0:T(8,128)(2,1)S(1)} %get-tuple-element.24, bf16[4,128,64]{1,2,0:T(8,128)(2,1)S(1)} %get-tuple-element.25), kind=kOutput, calls=%fused_computation.20 | convolution fusion | flops 50413568 | bytes 524288 | tf_op jit(solution)/shard_map/dot_general | solution.py:58
  52.6 0.3 fusion.8
  52.9 4.0 %collective-permute-start.6 = (bf16[128,128]{0,1:T(8,128)(2,1)S(1)}, bf16[128,128]{0,1:T(8,128)(2,1)S(1)}, u32[]{:S(2)}, u32[]{:S(2)}) collective-permute-start(bf16[128,128]{0,1:T(8,128)(2,1)S(1)} %pad_maximum_fusion.6), channel_id=1, source_target_pairs={{0,4},{1,5},{2,6},{3,7},{4,8},{5,9},{6,10},{7,11},{8,12},{9,13},{1... | collective-permute-start | bytes 98312 | tf_op jit(solution)/shard_map/ppermute | solution.py:81
  56.9 1.9 %collective-permute-start.10 = (bf16[128,128]{0,1:T(8,128)(2,1)S(1)}, bf16[128,128]{0,1:T(8,128)(2,1)S(1)}, u32[]{:S(2)}, u32[]{:S(2)}) collective-permute-start(bf16[128,128]{0,1:T(8,128)(2,1)S(1)} %pad_maximum_fusion.6), channel_id=1, source_target_pairs={{0,12},{1,13},{2,14},{3,15},{16,28},{17,29},{18,30},{19,31}} | collective-permute-start | bytes 98312 | tf_op jit(solution)/shard_map/ppermute | solution.py:81
  58.9 1.8 %collective-permute-start.8 = (bf16[128,128]{0,1:T(8,128)(2,1)S(1)}, bf16[128,128]{0,1:T(8,128)(2,1)S(1)}, u32[]{:S(2)}, u32[]{:S(2)}) collective-permute-start(bf16[128,128]{0,1:T(8,128)(2,1)S(1)} %pad_maximum_fusion.6), channel_id=1, source_target_pairs={{0,8},{1,9},{2,10},{3,11},{4,12},{5,13},{6,14},{7,15},{16,24},{17,... | collective-permute-start | bytes 98312 | tf_op jit(solution)/shard_map/ppermute | solution.py:81
  60.7 0.4 convolution_add_fusion.5
  61.1 1.2 %collective-permute-done.8 = bf16[128,128]{0,1:T(8,128)(2,1)S(1)} collective-permute-done((bf16[128,128]{0,1:T(8,128)(2,1)S(1)}, bf16[128,128]{0,1:T(8,128)(2,1)S(1)}, u32[]{:S(2)}, u32[]{:S(2)}) %collective-permute-start.8) | collective-permute-done | bytes 32800 | tf_op jit(solution)/shard_map/ppermute | solution.py:81
  62.3 1.2 %fusion.53 = f32[256,64]{0,1:T(8,128)S(1)} fusion(f32[256,256]{1,0:T(8,128)} %collective-permute-done.9, bf16[128,64]{0,1:T(8,128)(2,1)S(1)} %get-tuple-element.31, bf16[128,64]{0,1:T(8,128)(2,1)S(1)} %get-tuple-element.30), kind=kOutput, calls=%fused_computation.117 | convolution fusion | flops 50397184 | bytes 360448 | tf_op jit(solution)/shard_map/dot_general | solution.py:58
  63.5 1.3 %convert_add_fusion = f32[256,64]{0,1:T(8,128)S(1)} fusion(bf16[128,64]{0,1:T(8,128)(2,1)S(1)} %get-tuple-element.33, bf16[128,64]{0,1:T(8,128)(2,1)S(1)} %get-tuple-element.32, f32[256,256]{1,0:T(8,128)} %collective-permute-done.7, f32[256,64]{0,1:T(8,128)S(1)} %fusion.53, bf16[128,64]{0,1:T(8,128)(2,1)S(1)} %get-tuple-element.29, ...), kind=kOutput, calls=%fused_computation.92 | convolution fusion | flops 50495488 | bytes 458752 | tf_op jit(solution)/shard_map/dot_general | solution.py:58
  64.9 0.4 fusion.6
  65.2 0.4 fusion.7
  65.6 0.4 fusion.5
  66.2 1.5 %collective-permute-start.12 = (bf16[128,128]{0,1:T(8,128)(2,1)S(1)}, bf16[128,128]{0,1:T(8,128)(2,1)S(1)}, u32[]{:S(2)}, u32[]{:S(2)}) collective-permute-start(bf16[128,128]{0,1:T(8,128)(2,1)S(1)} %get-tuple-element.20), channel_id=1, source_target_pairs={{0,2},{1,3},{2,0},{3,1},{4,6},{5,7},{6,4},{7,5},{8,10},{9,11},{10,... | collective-permute-start | bytes 98312 | tf_op jit(solution)/shard_map/ppermute | solution.py:73
  67.8 2.3 %collective-permute-done.12 = bf16[128,128]{0,1:T(8,128)(2,1)S(1)} collective-permute-done((bf16[128,128]{0,1:T(8,128)(2,1)S(1)}, bf16[128,128]{0,1:T(8,128)(2,1)S(1)}, u32[]{:S(2)}, u32[]{:S(2)}) %collective-permute-start.12) | collective-permute-done | bytes 32800 | tf_op jit(solution)/shard_map/ppermute | solution.py:73
  70.2 0.8 %collective-permute-done.11 = bf16[128,128]{0,1:T(8,128)(2,1)S(1)} collective-permute-done((bf16[128,128]{0,1:T(8,128)(2,1)S(1)}, bf16[128,128]{0,1:T(8,128)(2,1)S(1)}, u32[]{:S(2)}, u32[]{:S(2)}) %collective-permute-start.11) | collective-permute-done | bytes 32800 | tf_op jit(solution)/shard_map/ppermute | solution.py:73
  71.0 0.6 gather_fusion.3
  71.8 0.5 fusion.11
  72.3 4.4 %fusion.2 = bf16[1,2,1024,128]{3,2,1,0:T(8,128)(2,1)} fusion(f32[2,1024,128]{2,1,0:T(8,128)S(1)} %fusion.11, bf16[2,1024,128]{2,1,0:T(8,128)(2,1)} %copy-done.8, bf16[1,2,1024,1024]{3,2,1,0:T(8,128)(2,1)} %param.8), kind=kOutput, calls=%fused_computation.12 | convolution fusion | flops 537395200 | bytes 6291456 | tf_op jit(solution)/shard_map/eij,ejk->eik/dot_general | solution.py:142
  (83 shorter events, 3.4 us)
Async XLA Ops:
  5.6 1.4 %copy-start = (f32[2,1024,256]{1,2,0:T(8,128)}, f32[2,1024,256]{1,2,0:T(8,128)S(1)}, u32[]{:S(2)}) copy-start(f32[2,1024,256]{1,2,0:T(8,128)S(1)} %convolution_bitcast_fusion) | copy-start | bytes 6291460
  7.0 3.7 %copy-start.10 = (s32[16,1]{0,1:T(1,128)S(1)}, s32[16,1]{0,1:T(1,128)}, u32[]{:S(2)}) copy-start(s32[16,1]{0,1:T(1,128)} %param.12) | copy-start | bytes 196
  7.0 3.9 %copy-start.9 = (s32[16,2]{0,1:T(2,128)S(1)}, s32[16,2]{0,1:T(2,128)}, u32[]{:S(2)}) copy-start(s32[16,2]{0,1:T(2,128)} %param.13) | copy-start | bytes 388
  7.0 4.7 %copy-start.6 = (bf16[1,2,1024,128]{3,2,1,0:T(8,128)(2,1)S(1)}, bf16[1,2,1024,128]{3,2,1,0:T(8,128)(2,1)}, u32[]{:S(2)}) copy-start(bf16[1,2,1024,128]{3,2,1,0:T(8,128)(2,1)} %param.9) | copy-start | bytes 1572868
  7.4 16.5 %collective-permute-start.5 = (f32[256,256]{1,0:T(8,128)S(1)}, f32[256,256]{1,0:T(8,128)S(1)}, u32[]{:S(2)}, u32[]{:S(2)}) collective-permute-start(f32[256,256]{1,0:T(8,128)S(1)} %get-tuple-element.7), channel_id=1, source_target_pairs={{0,3},{1,0},{2,1},{3,2},{4,7},{5,4},{6,5},{7,6},{8,11},{9,8},{10,9... | collective-permute-start | bytes 786440 | tf_op jit(solution)/shard_map/ppermute | solution.py:73
  9.9 14.1 %collective-permute-start.4 = (f32[256,256]{1,0:T(8,128)S(1)}, f32[256,256]{1,0:T(8,128)S(1)}, u32[]{:S(2)}, u32[]{:S(2)}) collective-permute-start(f32[256,256]{1,0:T(8,128)S(1)} %get-tuple-element.8), channel_id=1, source_target_pairs={{0,2},{1,3},{2,0},{3,1},{4,6},{5,7},{6,4},{7,5},{8,10},{9,11},{10,... | collective-permute-start | bytes 786440 | tf_op jit(solution)/shard_map/ppermute | solution.py:73
  10.5 13.4 %collective-permute-start.3 = (f32[256,256]{1,0:T(8,128)S(1)}, f32[256,256]{1,0:T(8,128)S(1)}, u32[]{:S(2)}, u32[]{:S(2)}) collective-permute-start(f32[256,256]{1,0:T(8,128)S(1)} %get-tuple-element.9), channel_id=1, source_target_pairs={{0,1},{1,2},{2,3},{3,0},{4,5},{5,6},{6,7},{7,4},{8,9},{9,10},{10,1... | collective-permute-start | bytes 786440 | tf_op jit(solution)/shard_map/ppermute | solution.py:73
  17.9 21.6 %all-to-all-start = ((bf16[16,144,128]{2,1,0:T(8,128)(2,1)}), bf16[16,144,128]{2,1,0:T(8,128)(2,1)S(1)}, u32[]{:S(2)}, u32[]{:S(2)}) async-start(bf16[16,144,128]{2,1,0:T(8,128)(2,1)} %fusion.13), calls=%async_computation | async-start | bytes 1179648 | tf_op jit(solution)/shard_map/all_to_all | solution.py:110
  24.9 15.8 %copy-start.7 = (bf16[1,2,1024,128]{3,2,1,0:T(8,128)(2,1)S(1)}, bf16[1,2,1024,128]{3,2,1,0:T(8,128)(2,1)}, u32[]{:S(2)}) copy-start(bf16[1,2,1024,128]{3,2,1,0:T(8,128)(2,1)} %param.9) | copy-start | bytes 1572868
  25.3 10.3 %copy-start.4 = (f32[256,256]{1,0:T(8,128)}, f32[256,256]{1,0:T(8,128)S(1)}, u32[]{:S(2)}) copy-start(f32[256,256]{1,0:T(8,128)S(1)} %fusion.17) | copy-start | bytes 786436
  25.6 5.6 %copy-start.2 = (f32[256,256]{1,0:T(8,128)}, f32[256,256]{1,0:T(8,128)S(1)}, u32[]{:S(2)}) copy-start(f32[256,256]{1,0:T(8,128)S(1)} %fusion.20) | copy-start | bytes 786436
  26.8 36.8 %collective-permute-start.7 = (f32[256,256]{1,0:T(8,128)}, f32[256,256]{1,0:T(8,128)}, u32[]{:S(2)}, u32[]{:S(2)}) collective-permute-start(f32[256,256]{1,0:T(8,128)} %fusion.18), channel_id=1, source_target_pairs={{0,4},{1,5},{2,6},{3,7},{4,8},{5,9},{6,10},{7,11},{8,12},{9,13},{1... | collective-permute-start | bytes 786440 | tf_op jit(solution)/shard_map/ppermute | solution.py:82
  31.3 31.0 %collective-permute-start.9 = (f32[256,256]{1,0:T(8,128)}, f32[256,256]{1,0:T(8,128)}, u32[]{:S(2)}, u32[]{:S(2)}) collective-permute-start(f32[256,256]{1,0:T(8,128)} %fusion.18), channel_id=1, source_target_pairs={{0,8},{1,9},{2,10},{3,11},{4,12},{5,13},{6,14},{7,15},{16,24},{17,... | collective-permute-start | bytes 786440 | tf_op jit(solution)/shard_map/ppermute | solution.py:82
  40.7 7.6 %copy-start.8 = (bf16[2,1024,128]{2,1,0:T(8,128)(2,1)}, bf16[2,1024,128]{2,1,0:T(8,128)(2,1)S(1)}, u32[]{:S(2)}) copy-start(bf16[2,1024,128]{2,1,0:T(8,128)(2,1)S(1)} %fusion.10) | copy-start | bytes 1572868
  43.0 2.8 %collective-permute-start.2 = (bf16[128,128]{1,0:T(8,128)(2,1)S(1)}, bf16[128,128]{1,0:T(8,128)(2,1)S(1)}, u32[]{:S(2)}, u32[]{:S(2)}) collective-permute-start(bf16[128,128]{1,0:T(8,128)(2,1)S(1)} %get-tuple-element.13), channel_id=1, source_target_pairs={{0,3},{1,0},{2,1},{3,2},{4,7},{5,4},{6,5},{7,6},{8,11},{9,8},{10,9... | collective-permute-start | bytes 98312 | tf_op jit(solution)/shard_map/ppermute | solution.py:73
  44.0 4.1 %collective-permute-start.1 = (bf16[128,128]{1,0:T(8,128)(2,1)S(1)}, bf16[128,128]{1,0:T(8,128)(2,1)S(1)}, u32[]{:S(2)}, u32[]{:S(2)}) collective-permute-start(bf16[128,128]{1,0:T(8,128)(2,1)S(1)} %get-tuple-element.12), channel_id=1, source_target_pairs={{0,2},{1,3},{2,0},{3,1},{4,6},{5,7},{6,4},{7,5},{8,10},{9,11},{10,... | collective-permute-start | bytes 98312 | tf_op jit(solution)/shard_map/ppermute | solution.py:73
  44.7 3.6 %collective-permute-start = (bf16[128,128]{1,0:T(8,128)(2,1)S(1)}, bf16[128,128]{1,0:T(8,128)(2,1)S(1)}, u32[]{:S(2)}, u32[]{:S(2)}) collective-permute-start(bf16[128,128]{1,0:T(8,128)(2,1)S(1)} %get-tuple-element.11), channel_id=1, source_target_pairs={{0,1},{1,2},{2,3},{3,0},{4,5},{5,6},{6,7},{7,4},{8,9},{9,10},{10,1... | collective-permute-start | bytes 98312 | tf_op jit(solution)/shard_map/ppermute | solution.py:73
  48.9 22.9 %copy-start.1 = (f32[2,1024,256]{1,2,0:T(8,128)S(1)}, f32[2,1024,256]{1,2,0:T(8,128)}, u32[]{:S(2)}) copy-start(f32[2,1024,256]{1,2,0:T(8,128)} %copy-done) | copy-start | bytes 6291460
  49.7 15.2 %copy-start.5 = (f32[256,256]{1,0:T(8,128)S(1)}, f32[256,256]{1,0:T(8,128)}, u32[]{:S(2)}) copy-start(f32[256,256]{1,0:T(8,128)} %copy-done.4) | copy-start | bytes 786436
  49.7 15.9 %copy-start.3 = (f32[256,256]{1,0:T(8,128)S(1)}, f32[256,256]{1,0:T(8,128)}, u32[]{:S(2)}) copy-start(f32[256,256]{1,0:T(8,128)} %copy-done.2) | copy-start | bytes 786436
  52.9 8.2 %collective-permute-start.6 = (bf16[128,128]{0,1:T(8,128)(2,1)S(1)}, bf16[128,128]{0,1:T(8,128)(2,1)S(1)}, u32[]{:S(2)}, u32[]{:S(2)}) collective-permute-start(bf16[128,128]{0,1:T(8,128)(2,1)S(1)} %pad_maximum_fusion.6), channel_id=1, source_target_pairs={{0,4},{1,5},{2,6},{3,7},{4,8},{5,9},{6,10},{7,11},{8,12},{9,13},{1... | collective-permute-start | bytes 98312 | tf_op jit(solution)/shard_map/ppermute | solution.py:81
  56.9 4.2 %collective-permute-start.10 = (bf16[128,128]{0,1:T(8,128)(2,1)S(1)}, bf16[128,128]{0,1:T(8,128)(2,1)S(1)}, u32[]{:S(2)}, u32[]{:S(2)}) collective-permute-start(bf16[128,128]{0,1:T(8,128)(2,1)S(1)} %pad_maximum_fusion.6), channel_id=1, source_target_pairs={{0,12},{1,13},{2,14},{3,15},{16,28},{17,29},{18,30},{19,31}} | collective-permute-start | bytes 98312 | tf_op jit(solution)/shard_map/ppermute | solution.py:81
  58.9 3.4 %collective-permute-start.8 = (bf16[128,128]{0,1:T(8,128)(2,1)S(1)}, bf16[128,128]{0,1:T(8,128)(2,1)S(1)}, u32[]{:S(2)}, u32[]{:S(2)}) collective-permute-start(bf16[128,128]{0,1:T(8,128)(2,1)S(1)} %pad_maximum_fusion.6), channel_id=1, source_target_pairs={{0,8},{1,9},{2,10},{3,11},{4,12},{5,13},{6,14},{7,15},{16,24},{17,... | collective-permute-start | bytes 98312 | tf_op jit(solution)/shard_map/ppermute | solution.py:81
  66.1 1.7 %collective-permute-start.13 = (bf16[128,128]{0,1:T(8,128)(2,1)S(1)}, bf16[128,128]{0,1:T(8,128)(2,1)S(1)}, u32[]{:S(2)}, u32[]{:S(2)}) collective-permute-start(bf16[128,128]{0,1:T(8,128)(2,1)S(1)} %get-tuple-element.21), channel_id=1, source_target_pairs={{0,3},{1,0},{2,1},{3,2},{4,7},{5,4},{6,5},{7,6},{8,11},{9,8},{10,9... | collective-permute-start | bytes 98312 | tf_op jit(solution)/shard_map/ppermute | solution.py:73
  66.2 4.0 %collective-permute-start.12 = (bf16[128,128]{0,1:T(8,128)(2,1)S(1)}, bf16[128,128]{0,1:T(8,128)(2,1)S(1)}, u32[]{:S(2)}, u32[]{:S(2)}) collective-permute-start(bf16[128,128]{0,1:T(8,128)(2,1)S(1)} %get-tuple-element.20), channel_id=1, source_target_pairs={{0,2},{1,3},{2,0},{3,1},{4,6},{5,7},{6,4},{7,5},{8,10},{9,11},{10,... | collective-permute-start | bytes 98312 | tf_op jit(solution)/shard_map/ppermute | solution.py:73
  67.7 3.3 %collective-permute-start.11 = (bf16[128,128]{0,1:T(8,128)(2,1)S(1)}, bf16[128,128]{0,1:T(8,128)(2,1)S(1)}, u32[]{:S(2)}, u32[]{:S(2)}) collective-permute-start(bf16[128,128]{0,1:T(8,128)(2,1)S(1)} %get-tuple-element.19), channel_id=1, source_target_pairs={{0,1},{1,2},{2,3},{3,0},{4,5},{5,6},{6,7},{7,4},{8,9},{9,10},{10,1... | collective-permute-start | bytes 98312 | tf_op jit(solution)/shard_map/ppermute | solution.py:73

commit v2 on v1

v2 whole, which is shorter than its diff:
```python
import functools

import jax
import jax.numpy as jnp
from jax import lax
from jax.experimental import pallas as pl
from jax.experimental.pallas import tpu as pltpu
from jax.sharding import PartitionSpec as P

BLK = 32
CAP = 2
GROUP = 4
HEAD = 16

HIGH = lax.Precision.HIGHEST
F32 = jnp.float32
BF16 = jnp.bfloat16
VMEM_BYTES = 40 * 1024 * 1024

IN_VMEM = pl.BlockSpec(memory_space=pltpu.VMEM)
IN_SMEM = pl.BlockSpec(memory_space=pltpu.SMEM)
IN_PLACE = pl.BlockSpec(memory_space=pl.ANY)


def shape(*dims, dtype=BF16):
    return jax.ShapeDtypeStruct(dims, dtype)


def call(body, name, ins, outs, scratch, flops, moved):
    return pl.pallas_call(
        body,
        name=name,
        in_specs=ins,
        out_shape=outs,
        out_specs=jax.tree.map(lambda _: IN_VMEM, outs),
        scratch_shapes=scratch,
        compiler_params=pltpu.CompilerParams(vmem_limit_bytes=VMEM_BYTES),
        cost_estimate=pl.CostEstimate(flops=flops, bytes_accessed=moved, transcendentals=0),
    )


def place():
    return lax.axis_index("sec") % GROUP


def dot(a, b):
    return jnp.dot(a, b, preferred_element_type=F32)


def dot_wide(a, b):
    return jnp.dot(a, b, precision=HIGH, preferred_element_type=F32)


def two_parts(x):
    high = x.astype(BF16)
    return high, (x - high.astype(F32)).astype(BF16)


def left_lanes(x):
    return lax.broadcasted_iota(jnp.int32, x.shape, 1) < x.shape[1] // 2


def swap_lanes(x):
    return pltpu.roll(x, x.shape[1] // 2, 1)


def pack(tall):
    half = tall.shape[0] // 2
    top, low = tall[:half], tall[half:]
    return jnp.where(left_lanes(top), top, swap_lanes(low))


def unpack(packed):
    return jnp.concatenate([packed, swap_lanes(packed)], axis=0)


def copies(green, held, sem, rows, steps):
    energies = green.shape[0]
    size = rows.size // steps
    out = []
    for e in range(energies):
        for c in range(steps):
            src = green.at[e, pl.ds(rows.start + c * size, size)]
            out.append((e, c * size, pltpu.make_async_copy(src, held.at[e, pl.ds(c * size, size)], sem.at[e, c])))
    return size, out


def pairs_kernel(owner, blocks, green, inject, out, held, full, slot_of, counts, sem):
    energies, orbitals, _ = green.shape
    sections = out.shape[0]
    count = owner.shape[0]
    size, moves = copies(green, held, sem, pl.ds(0, orbitals), sem.shape[1])
    for _, _, move in moves:
        move.start()
    out[...] = jnp.zeros_like(out)

    def clear(d, _):
        counts[d] = 0
        return 0

    lax.fori_loop(0, sections, clear, 0)
    rows = CAP * energies * BLK
    lane = lax.broadcasted_iota(jnp.int32, (HEAD, out.shape[2]), 1)
    none = jnp.where(lane < CAP, -1.0, 0.0).astype(BF16)

    def blank(d, _):
        out[d, rows : rows + HEAD, :] = none
        return 0

    lax.fori_loop(0, sections, blank, 0)

    def rank(q, _):
        d = owner[q]
        r = counts[d]
        counts[d] = r + 1
        slot_of[q] = r
        head = out[d, rows : rows + HEAD, :].astype(F32)
        head = jnp.where(lane == r, blocks[q, 1].astype(F32), head)
        out[d, rows : rows + HEAD, :] = head.astype(BF16)
        return 0

    lax.fori_loop(0, count, rank, 0)
    for e, first, move in moves:
        move.wait()
        full[e, first : first + size, :] = dot(held[e, first : first + size, :], inject[e]).astype(BF16)

    def fill(q, _):
        d, r = owner[q], slot_of[q]
        first = pl.multiple_of(blocks[q, 0] * BLK, BLK)
        for e in range(energies):
            to = pl.multiple_of((r * energies + e) * BLK, BLK)
            out[d, pl.ds(to, BLK), :] = full[e, pl.ds(first, BLK), :]
        return 0

    lax.fori_loop(0, count, fill, 0)


def outgoing_pairs(owner, blocks, green, inject, sections):
    energies, orbitals, _ = green.shape
    columns = inject.shape[2]
    steps = 4
    return call(
        pairs_kernel,
        "pairs",
        [IN_SMEM, IN_SMEM, IN_PLACE, IN_VMEM],
        shape(sections, CAP * energies * BLK + HEAD, columns),
        [
            pltpu.VMEM(green.shape, BF16),
            pltpu.VMEM(inject.shape, BF16),
            pltpu.SMEM(owner.shape, jnp.int32),
            pltpu.SMEM((sections,), jnp.int32),
            pltpu.SemaphoreType.DMA((energies, steps)),
        ],
        2 * energies * orbitals * orbitals * columns,
        2 * green.size,
    )(owner, blocks, green, inject)


def maps_kernel(pattern, green, coupling, face_map, couple, held, sem):
    energies, orbitals, _ = green.shape
    face = coupling.shape[1]
    size, moves = copies(green, held, sem, pl.ds(orbitals - face, face), sem.shape[1])
    for _, _, move in moves:
        move.start()
    high, wide = orbitals // pattern.shape[0], face // pattern.shape[1]
    for i in range(pattern.shape[0]):
        for j in range(pattern.shape[1]):
            at = (slice(i * high, (i + 1) * high), slice(j * wide, (j + 1) * wide))
            tile = coupling[at]
            couple[at] = jnp.where(pattern[i, j] == 1, tile, jnp.zeros_like(tile))
    for e, first, move in moves:
        move.wait()
        face_map[e, first : first + size, :] = dot(held[e, first : first + size, :], couple[...])


def face_maps(pattern, green, coupling):
    energies, orbitals, _ = green.shape
    face = coupling.shape[1]
    return call(
        maps_kernel,
        "face_maps",
        [IN_SMEM, IN_PLACE, IN_VMEM],
        [shape(energies, face, face, dtype=F32), shape(orbitals, face)],
        [pltpu.VMEM((energies, face, orbitals), BF16), pltpu.SemaphoreType.DMA((energies, 1))],
        2 * energies * face * orbitals * face,
        2 * energies * face * orbitals,
    )(pattern, green, coupling)


def product_kernel(green, right, out, held, sem):
    orbitals = green.shape[1]
    size, moves = copies(green, held, sem, pl.ds(0, orbitals), sem.shape[1])
    for _, _, move in moves:
        move.start()
    for e, first, move in moves:
        move.wait()
        factor = right[e] if len(right.shape) == 3 else right[...]
        out[e, first : first + size, :] = dot(held[e, first : first + size, :], factor).astype(out.dtype)


def product(green, right, dtype, name):
    energies, orbitals, _ = green.shape
    wide = right.shape[-1]
    return call(
        product_kernel,
        name,
        [IN_PLACE, IN_VMEM],
        shape(energies, orbitals, wide, dtype=dtype),
        [pltpu.VMEM(green.shape, BF16), pltpu.SemaphoreType.DMA((energies, 4))],
        2 * energies * orbitals * orbitals * wide,
        2 * green.size,
    )(green, right)


def chain_kernel(own, got1, got2, got3, total_out, after_out, within_out, upto_out, maps):
    here = place()
    split = GROUP // own.shape[0]
    maps[here] = own[here // split]
    for k, got in enumerate((got1, got2, got3), 1):
        maps[(here + GROUP - k) % GROUP] = got[...]
    first, second, third, fourth = (maps[j] for j in range(GROUP))
    face = first.shape[0]
    upto2 = dot_wide(second, first)
    upto3 = dot_wide(third, upto2)
    after1 = dot_wide(fourth, third)
    after0 = dot_wide(after1, second)
    total_out[...] = dot_wide(fourth, upto3).astype(total_out.dtype)
    for out, items in (
        (after_out, (after0, after1, fourth)),
        (within_out, (second, third, dot_wide(third, second))),
        (upto_out, (first, upto2, upto3)),
    ):
        for j, item in enumerate(items):
            high, low = two_parts(item)
            out[0, j * face : (j + 1) * face, :] = high
            out[1, j * face : (j + 1) * face, :] = low


def chain(own, got, total_dtype):
    face = own.shape[1]
    stack = shape(2, (GROUP - 1) * face, face)
    return call(
        chain_kernel,
        "chain_maps",
        [IN_VMEM] * GROUP,
        [shape(face, face, dtype=total_dtype), stack, stack, stack],
        [pltpu.VMEM((GROUP, face, face), F32)],
        2 * 6 * 6 * face**3,
        4 * 10 * face * face,
    )(own, *got)


def source_kernel(received, inject, green, source, own, send1, send2, send3, held, total, heads, targets, quarters, sem, head_sem):
    energies, orbitals, columns = inject.shape
    sections = received.shape[0]
    face = held.shape[1]
    size, moves = copies(green, held, sem, pl.ds(orbitals - face, face), sem.shape[1])
    for _, _, move in moves:
        move.start()
    rows = CAP * energies * BLK

    def read(s, _):
        block = received[s, rows : rows + HEAD, :].astype(F32)
        heads[pl.ds(s, 1), :] = block[:1].astype(jnp.int32)
        return 0

    lax.fori_loop(0, sections, read, 0, unroll=min(sections, 8))
    fetch = pltpu.make_async_copy(heads, targets, head_sem)
    fetch.start()
    total[...] = inject[...].astype(F32)
    fetch.wait()

    def add(s, _):
        for r in range(CAP):
            first = pl.multiple_of(jnp.maximum(targets[s, r], 0) * BLK, BLK)
            for e in range(energies):
                item = received[s, (r * energies + e) * BLK : (r * energies + e + 1) * BLK, :]
                total[e, pl.ds(first, BLK), :] += item.astype(F32)
        return 0

    lax.fori_loop(0, sections, add, 0, unroll=2)
    split = GROUP // energies
    for e in range(energies):
        source[e] = total[e].astype(BF16)
    for e, first, move in moves:
        move.wait()
        tall = dot(held[e], source[e])
        quarters[e * split] = pack(tall)
        half = face // 2
        quarters[e * split + 1] = jnp.where(left_lanes(tall[:half]), swap_lanes(tall[:half]), tall[half:])
    here = place()
    for k, out in enumerate((own, send1, send2, send3)):
        out[...] = quarters[(here + k) % GROUP].astype(BF16)


def placed_source(received, inject, green, face):
    energies, orbitals, columns = inject.shape
    sections = received.shape[0]
    quarter = shape(face // 2, columns)
    return call(
        source_kernel,
        "source_and_face",
        [IN_VMEM, IN_VMEM, IN_PLACE],
        [shape(*inject.shape), quarter, quarter, quarter, quarter],
        [
            pltpu.VMEM((energies, face, orbitals), BF16),
            pltpu.VMEM(inject.shape, F32),
            pltpu.VMEM((sections, columns), jnp.int32),
            pltpu.SMEM((sections, columns), jnp.int32),
            pltpu.VMEM((GROUP, face // 2, columns), F32),
            pltpu.SemaphoreType.DMA((energies, 1)),
            pltpu.SemaphoreType.DMA,
        ],
        2 * energies * face * orbitals * columns,
        2 * energies * face * orbitals + 2 * received.size,
    )(received, inject, green)


def gathered(refs, held):
    here = place()
    for k, ref in enumerate(refs):
        held[(here + GROUP - k) % GROUP] = ref[...]


def apply(parts, j, x):
    face = x.shape[0]
    at = slice(j * face, (j + 1) * face)
    return dot(parts[0, at, :], x) + dot(parts[1, at, :], x)


def total_kernel(own, got1, got2, got3, after, out, held):
    gathered((own, got1, got2, got3), held)
    total = unpack(held[GROUP - 1].astype(F32))
    for j in range(GROUP - 1):
        total = total + apply(after, j, unpack(held[j].astype(F32)).astype(BF16))
    out[...] = pack(total).astype(BF16)


def plane_total(shifts, after):
    half, columns = shifts[0].shape
    return call(
        total_kernel,
        "plane_total",
        [IN_VMEM] * (GROUP + 1),
        shape(half, columns),
        [pltpu.VMEM((GROUP, half, columns), BF16)],
        2 * after.size * columns,
        2 * after.size,
    )(*shifts, after)


def local_kernel(own, got1, got2, got3, within, out, held):
    gathered((own, got1, got2, got3), held)
    face = out.shape[0] // (GROUP - 1)
    first, second, third = (unpack(held[j].astype(F32)) for j in range(GROUP - 1))
    out[0:face] = first
    out[face : 2 * face] = second + apply(within, 0, first.astype(BF16))
    out[2 * face :] = third + apply(within, 1, second.astype(BF16)) + apply(within, 2, first.astype(BF16))


def plane_local(shifts, within):
    half, columns = shifts[0].shape
    return call(
        local_kernel,
        "plane_local",
        [IN_VMEM] * (GROUP + 1),
        shape((GROUP - 1) * 2 * half, columns, dtype=F32),
        [pltpu.VMEM((GROUP, half, columns), BF16)],
        2 * within.size * columns,
        2 * within.size,
    )(*shifts, within)


def entering_kernel(count, *refs):
    below, maps = refs[:count], refs[count : 2 * count - 1]
    upto, local, own, send1, send2, send3, held = refs[2 * count - 1 :]
    base = unpack(below[-1][...].astype(F32))
    for k in range(count - 2, -1, -1):
        high, low = two_parts(base)
        base = unpack(below[k][...].astype(F32)) + dot(maps[k][...], high) + dot(maps[k][...], low)
    high, low = two_parts(base)
    face = base.shape[0]
    held[0] = pack(base)
    for j in range(1, GROUP):
        at = slice((j - 1) * face, j * face)
        held[j] = pack(local[at, :] + dot(upto[0, at, :], high) + dot(upto[0, at, :], low) + dot(upto[1, at, :], high))
    here = place()
    for k, out in enumerate((own, send1, send2, send3)):
        out[...] = held[(here + k) % GROUP].astype(BF16)


def entering(below, maps, upto, local):
    half, columns = below[0].shape
    count = len(below)
    quarter = shape(half, columns)
    return call(
        functools.partial(entering_kernel, count),
        "entering",
        [IN_VMEM] * (2 * count + 1),
        [quarter] * GROUP,
        [pltpu.VMEM((GROUP, half, columns), F32)],
        3 * upto.size * columns,
        2 * upto.size + 4 * local.size,
    )(*below, *maps, upto, local)


def waves_kernel(own, got1, got2, got3, prop, image, out, held):
    gathered((own, got1, got2, got3), held)
    split = GROUP // prop.shape[0]
    for e in range(prop.shape[0]):
        near, far = held[e * split].astype(F32), held[e * split + 1].astype(F32)
        left = left_lanes(near)
        top = jnp.where(left, near, swap_lanes(far))
        low = jnp.where(left, swap_lanes(near), far)
        incoming = jnp.concatenate([top, low], axis=0).astype(BF16)
        out[e] = (dot(prop[e], incoming) + image[e]).astype(BF16)


def final_waves(arrived, prop, image):
    half, columns = arrived[0].shape
    return call(
        waves_kernel,
        "waves",
        [IN_VMEM] * (GROUP + 2),
        shape(*image.shape),
        [pltpu.VMEM((GROUP, half, columns), BF16)],
        2 * prop.size * columns,
        2 * prop.size + 6 * image.size,
    )(*arrived, prop, image)


def plane_shift(sections, k):
    return [(s, s // GROUP * GROUP + (s % GROUP + k) % GROUP) for s in range(sections)]


def up_shift(sections, k):
    return [(s, s + GROUP * k) for s in range(sections - GROUP * k)]


def in_plane(items, sections):
    return [lax.ppermute(item, "sec", plane_shift(sections, k)) for k, item in enumerate(items, 1)]


def spread(packed):
    half = packed.shape[1] // 2
    return jnp.concatenate([packed[:, :half], packed[:, half:]], axis=0)


def gather_below(total_map, total, sections):
    planes = sections // GROUP
    if planes <= 4:
        maps = [lax.ppermute(total_map, "sec", up_shift(sections, k)) for k in range(1, planes - 1)]
        below = [lax.ppermute(total, "sec", up_shift(sections, k)) for k in range(1, planes)]
        return below, maps
    shift = lax.ppermute(spread(total).astype(F32), "sec", up_shift(sections, 1))
    joined = lax.ppermute(total_map, "sec", up_shift(sections, 1))
    stride = 1
    while stride < planes:
        other = lax.ppermute(shift, "sec", up_shift(sections, stride))
        other_map = lax.ppermute(joined, "sec", up_shift(sections, stride))
        shift = shift + dot_wide(joined, other)
        joined = dot_wide(joined, other_map)
        stride *= 2
    half = shift.shape[0] // 2
    return [jnp.concatenate([shift[:half], shift[half:]], axis=1)], []


def per_device(green, injected, coupling, pattern, owner, pair_blocks):
    sections = lax.axis_size("sec")
    here = lax.axis_index("sec") % GROUP
    green, inject = green[0], injected[0]
    energies = green.shape[0]
    face = coupling.shape[2]
    split = GROUP // energies

    outgoing = outgoing_pairs(owner[:, 0], pair_blocks, green, inject, sections)
    received = lax.all_to_all(outgoing, "sec", split_axis=0, concat_axis=0, tiled=True)

    face_map, couple = face_maps(pattern[0], green, coupling[0])
    sent = [lax.dynamic_index_in_dim(face_map, (here + k) % GROUP // split, 0, False) for k in range(1, GROUP)]
    total_dtype = BF16 if sections // GROUP <= 4 else F32
    total_map, after, within, upto = chain(face_map, in_plane(sent, sections), total_dtype)
    prop = product(green, couple, BF16, "prop")

    source, own, *quarters = placed_source(received, inject, green, face)
    shifts = [own] + in_plane(quarters, sections)
    total = plane_total(shifts, after)
    below, maps = gather_below(total_map, total, sections)
    local = plane_local(shifts, within)
    own, *inner = entering(below, maps, upto, local)
    arrived = [own] + in_plane(inner, sections)
    image = product(green, source, F32, "image")
    return final_waves(arrived, prop, image)[None]


def solution(mesh):
    in_specs = (
        P("sec", "grp", None, None),
        P("sec", "grp", None, None),
        P("sec", None, None),
        P("sec", None, None),
        P("sec", None),
        P("sec", None),
    )
    out_specs = P("sec", "grp", None, None)
    return jax.shard_map(
        per_device, mesh=mesh, in_specs=in_specs, out_specs=out_specs, check_vma=False
    )
```

time: 77.3 us -> 65.1 us (0.84)
  matrix products: 23.7 us -> 0 us
  Pallas kernels: 0 us -> 20 us
  other arithmetic: 3.71 us -> 0 us
  waiting for transfers between devices: 10.3 us -> 7.53 us
  starting transfers between devices: 29.3 us -> 26.8 us
    dot_general x21 -> x0, matrix products: 23.7 us -> none  [the longest x15 9.45 us: mm(): return jnp.dot(a, b, precision=HIGH, preferred_element_type=jnp.float32)]
    pallas_call x0 -> x10, Pallas kernels: none -> 20 us  [the longest x2 6.37 us: product(): call(product_kernel, name, [IN_PLACE, IN_VMEM], shape(energies, orbitals,...]
    ppermute x14, waiting for transfers between devices: 6.84 us -> 0.04 us  [the longest x9 0.02 us: in_plane(): lax.ppermute(item, 'sec', plane_shift(sections, k))]
    unnamed x25 -> x19, local copies, waits for them, and re-layouts: 2.72 us -> 9.05 us
    all_to_all x1, waiting for transfers between devices: 3.42 us -> 7.49 us  [per_device(): lax.all_to_all(outgoing, 'sec', split_axis=0, concat_axis=0, tiled=True)]
    ppermute x14, starting transfers between devices: 23.3 us -> 19.3 us  [the longest x2 7.44 us: gather_below(): lax.ppermute(total_map, 'sec', up_shift(sections, k))]
    gather x5 -> x0, local copies, waits for them, and re-layouts: 3.14 us -> none  [the longest x4 2.54 us: in_plane(): return jnp.take(got, (here - jnp.arange(GROUP)) % GROUP, axis=0)]
    scatter x2 -> x0, local copies, waits for them, and re-layouts: 1.69 us -> none  [the longest x1 1.07 us: outgoing_pairs(): jnp.zeros((sections * CAP, energies, BLK, columns), jnp.bfloat16).at[slot]]
  transfers between devices with their start and end apart: 15 -> 15, of which waited for: 6 -> 1; matrix products, arithmetic and copies ran while one was open for 27% -> 1% of each run, Pallas kernels for 0% -> 20%
where the time goes in v2:
time: 65.1 us; the launch traced here: 64.6 us
  starting transfers between devices  26.8 us (41%)
  Pallas kernels  20 us (31%)
  local copies, waits for them, and re-layouts  9.89 us (15%)
  waiting for transfers between devices  7.53 us (12%)
    unnamed x19, local copies, waits for them, and re-layouts  9.05 us
    all_to_all x1, starting transfers between devices, per_device(): lax.all_to_all(outgoing, 'sec', split_axis=0, concat_axis=0, tiled=True)  7.5 us
    all_to_all x1, waiting for transfers between devices, per_device(): lax.all_to_all(outgoing, 'sec', split_axis=0, concat_axis=0, tiled=True)  7.49 us
    ppermute x2, starting transfers between devices, gather_below(): lax.ppermute(total_map, 'sec', up_shift(sections, k))  7.44 us
    ppermute x9, starting transfers between devices, in_plane(): lax.ppermute(item, 'sec', plane_shift(sections, k))  7.36 us
    pallas_call x2, Pallas kernels, product(): call(product_kernel, name, [IN_PLACE, IN_VMEM], shape(energies, orbitals,...  6.37 us
    pallas_call x1, Pallas kernels, outgoing_pairs(): call(pairs_kernel, 'pairs', [IN_SMEM, IN_SMEM, IN_PLACE, IN_VMEM], shape(...  4.79 us
    ppermute x3, starting transfers between devices, gather_below(): lax.ppermute(total, 'sec', up_shift(sections, k))  4.5 us
  transfers between devices with their start and end apart: 15, of which 1 were waited for; matrix products, arithmetic and copies ran while one was open for 1% of the time, Pallas kernels for 20%

profile of v2, /device:TPU:0, one launch (start us, length us, event | category | flops | bytes accessed | tf_op | source)
XLA Modules:
  0.0 64.6 jit_solution(13674387638454041039)
XLA Ops:
  0.0 0.8 %copy.7.blocks = s32[16,2]{1,0:T(8,128)S(1)} copy(s32[16,2]{0,1:T(2,128)} %param.11) | data formatting | bytes 256 | tf_op args[5]
  0.8 2.2 %copy-done = bf16[1,2,1024,1024]{3,2,1,0:T(8,128)(2,1)S(1)} copy-done((bf16[1,2,1024,1024]{3,2,1,0:T(8,128)(2,1)S(1)}, bf16[1,2,1024,1024]{3,2,1,0:T(8,128)(2,1)}, u32[]{:S(2)}) %copy-start) | copy-done | bytes 4194328
  3.0 1.0 %copy-done.4 = bf16[1,2,1024,128]{3,2,1,0:T(8,128)(2,1)S(1)} copy-done((bf16[1,2,1024,128]{3,2,1,0:T(8,128)(2,1)S(1)}, bf16[1,2,1024,128]{3,2,1,0:T(8,128)(2,1)}, u32[]{:S(2)}) %copy-start.4) | copy-done | bytes 524312
  4.0 0.7 %copy-done.7 = s32[16,1]{0,1:T(1,128)S(1)} copy-done((s32[16,1]{0,1:T(1,128)S(1)}, s32[16,1]{0,1:T(1,128)}, u32[]{:S(2)}) %copy-start.7) | copy-done | bytes 88
  4.7 4.8 %pairs.1 = bf16[16,144,128]{2,1,0:T(8,128)(2,1)} custom-call(s32[16]{0:T(128)S(1)} %bitcast.20, s32[16,2]{1,0:T(8,128)S(1)} %copy.7.blocks, bf16[2,1024,1024]{2,1,0:T(8,128)(2,1)S(1)} %bitcast.12, bf16[2,1024,128]{2,1,0:T(8,128)(2,1)S(1)} %bitcast.17), custom_call_target="tpu_custom_call" | custom-call | flops 536870912 | bytes 4194304 | tf_op jit(solution)/shard_map/pairs/pallas_call | solution.py:142
  9.5 0.0 copy-start.5
  9.5 7.5 %all-to-all-start = ((bf16[16,144,128]{2,1,0:T(8,128)(2,1)}), bf16[16,144,128]{2,1,0:T(8,128)(2,1)S(1)}, u32[]{:S(2)}, u32[]{:S(2)}) async-start(bf16[16,144,128]{2,1,0:T(8,128)(2,1)} %pairs.1), calls=%async_computation | async-start | bytes 1179648 | tf_op jit(solution)/shard_map/all_to_all | solution.py:477
  17.1 0.1 copy.8.pattern
  17.2 2.2 %copy-done.1 = bf16[1,2,1024,1024]{3,2,1,0:T(8,128)(2,1)S(1)} copy-done((bf16[1,2,1024,1024]{3,2,1,0:T(8,128)(2,1)S(1)}, bf16[1,2,1024,1024]{3,2,1,0:T(8,128)(2,1)}, u32[]{:S(2)}) %copy-start.1) | copy-done | bytes 4194328
  19.4 1.6 %face_maps.1 = (f32[2,256,256]{2,1,0:T(8,128)S(1)}, bf16[1024,256]{1,0:T(8,128)(2,1)S(1)}) custom-call(s32[8,2]{1,0:T(8,128)S(1)} %copy.8.pattern, bf16[2,1024,1024]{2,1,0:T(8,128)(2,1)S(1)} %bitcast.13, bf16[1024,256]{1,0:T(8,128)(2,1)S(1)} %bitcast.19), custom_call_target="tpu_custom_call" | custom-call | flops 268435456 | bytes 1048576 | tf_op jit(solution)/shard_map/face_maps/pallas_call | solution.py:179
  21.0 0.8 %dynamic-slice_bitcast_fusion = (f32[256,256]{1,0:T(8,128)S(1)}, f32[256,256]{1,0:T(8,128)S(1)}, f32[256,256]{1,0:T(8,128)}) fusion(f32[2,256,256]{2,1,0:T(8,128)S(1)} %get-tuple-element.24.own, s32[]{:T(128)S(6)} %select_n.48, s32[]{:T(128)S(6)} %select_n.45, s32[]{:T(128)S(6)} %select_n.42), kind=kLoop, calls=%fused_computation | loop fusion | bytes 1572876 | tf_op jit(solution)/shard_map/jit(dynamic_index_in_dim)/squeeze | solution.py:480
  21.8 0.3 collective-permute-start.3
  22.1 1.7 %collective-permute-start.4 = (f32[256,256]{1,0:T(8,128)S(1)}, f32[256,256]{1,0:T(8,128)S(1)}, u32[]{:S(2)}, u32[]{:S(2)}) collective-permute-start(f32[256,256]{1,0:T(8,128)S(1)} %get-tuple-element.36), channel_id=1, source_target_pairs={{0,2},{1,3},{2,0},{3,1},{4,6},{5,7},{6,4},{7,5},{8,10},{9,11},{10,... | collective-permute-start | bytes 786440 | tf_op jit(solution)/shard_map/ppermute | solution.py:441
  23.8 1.3 %collective-permute-start.5 = (f32[256,256]{1,0:T(8,128)S(1)}, f32[256,256]{1,0:T(8,128)S(1)}, u32[]{:S(2)}, u32[]{:S(2)}) collective-permute-start(f32[256,256]{1,0:T(8,128)S(1)} %get-tuple-element.35), channel_id=1, source_target_pairs={{0,3},{1,0},{2,1},{3,2},{4,7},{5,4},{6,5},{7,6},{8,11},{9,8},{10,9... | collective-permute-start | bytes 786440 | tf_op jit(solution)/shard_map/ppermute | solution.py:441
  25.1 7.5 %all-to-all-done.received = bf16[16,144,128]{2,1,0:T(8,128)(2,1)S(1)} async-done(((bf16[16,144,128]{2,1,0:T(8,128)(2,1)}), bf16[16,144,128]{2,1,0:T(8,128)(2,1)S(1)}, u32[]{:S(2)}, u32[]{:S(2)}) %all-to-all-start) | async-done | bytes 589856 | tf_op jit(solution)/shard_map/all_to_all | solution.py:477
  32.6 2.2 %copy-done.2 = bf16[1,2,1024,1024]{3,2,1,0:T(8,128)(2,1)S(1)} copy-done((bf16[1,2,1024,1024]{3,2,1,0:T(8,128)(2,1)S(1)}, bf16[1,2,1024,1024]{3,2,1,0:T(8,128)(2,1)}, u32[]{:S(2)}) %copy-start.2) | copy-done | bytes 4194328
  34.8 1.7 %source_and_face.1 = (bf16[2,1024,128]{2,1,0:T(8,128)(2,1)S(1)}, bf16[128,128]{1,0:T(8,128)(2,1)S(1)}, bf16[128,128]{1,0:T(8,128)(2,1)S(1)}, bf16[128,128]{1,0:T(8,128)(2,1)S(1)}, bf16[128,128]{1,0:T(8,128)(2,1)S(1)}) custom-call(bf16[16,144,128]{2,1,0:T(8,128)(2,1)S(1)} %all-to-all-done.received, bf16[2,1024,128]{2,1,0:T(8,128)(2,1)S(1)} %bitcast.18, ...), custom_call_target="tpu_custom_call" | custom-call | flops 134217728 | bytes 1638400 | tf_op jit(solution)/shard_map/source_and_face/pallas_call | solution.py:300
  36.5 0.1 collective-permute-start
  36.6 1.3 %collective-permute-start.1 = (bf16[128,128]{1,0:T(8,128)(2,1)S(1)}, bf16[128,128]{1,0:T(8,128)(2,1)S(1)}, u32[]{:S(2)}, u32[]{:S(2)}) collective-permute-start(bf16[128,128]{1,0:T(8,128)(2,1)S(1)} %get-tuple-element.22), channel_id=1, source_target_pairs={{0,2},{1,3},{2,0},{3,1},{4,6},{5,7},{6,4},{7,5},{8,10},{9,11},{10,... | collective-permute-start | bytes 98312 | tf_op jit(solution)/shard_map/ppermute | solution.py:441
  37.9 0.0 collective-permute-done.3.got1
  37.9 0.7 %collective-permute-start.2 = (bf16[128,128]{1,0:T(8,128)(2,1)S(1)}, bf16[128,128]{1,0:T(8,128)(2,1)S(1)}, u32[]{:S(2)}, u32[]{:S(2)}) collective-permute-start(bf16[128,128]{1,0:T(8,128)(2,1)S(1)} %get-tuple-element.23), channel_id=1, source_target_pairs={{0,3},{1,0},{2,1},{3,2},{4,7},{5,4},{6,5},{7,6},{8,11},{9,8},{10,9... | collective-permute-start | bytes 98312 | tf_op jit(solution)/shard_map/ppermute | solution.py:441
  38.6 0.0 collective-permute-done.4.got2
  38.6 0.0 collective-permute-done.5.got3
  38.6 2.1 %chain_maps.1 = (bf16[256,256]{1,0:T(8,128)(2,1)S(1)}, bf16[2,768,256]{2,1,0:T(8,128)(2,1)S(1)}, bf16[2,768,256]{2,1,0:T(8,128)(2,1)S(1)}, bf16[2,768,256]{2,1,0:T(8,128)(2,1)S(1)}) custom-call(f32[2,256,256]{2,1,0:T(8,128)S(1)} %get-tuple-element.24.own, f32[256,256]{1,0:T(8,128)S(1)} %collective-permute-done.3.got1, ...), custom_call_target="tpu_custom_call" | custom-call | flops 1207959552 | bytes 2621440 | tf_op jit(solution)/shard_map/chain_maps/pallas_call | solution.py:242
  40.7 4.3 %collective-permute-start.10 = (bf16[256,256]{1,0:T(8,128)(2,1)S(1)}, bf16[256,256]{1,0:T(8,128)(2,1)S(1)}, u32[]{:S(2)}, u32[]{:S(2)}) collective-permute-start(bf16[256,256]{1,0:T(8,128)(2,1)S(1)} %get-tuple-element.26), channel_id=1, source_target_pairs={{0,8},{1,9},{2,10},{3,11},{4,12},{5,13},{6,14},{7,15},{16,24},{17,... | collective-permute-start | bytes 393224 | tf_op jit(solution)/shard_map/ppermute | solution.py:452
  45.0 3.1 %collective-permute-start.9 = (bf16[256,256]{1,0:T(8,128)(2,1)S(1)}, bf16[256,256]{1,0:T(8,128)(2,1)S(1)}, u32[]{:S(2)}, u32[]{:S(2)}) collective-permute-start(bf16[256,256]{1,0:T(8,128)(2,1)S(1)} %get-tuple-element.26), channel_id=1, source_target_pairs={{0,4},{1,5},{2,6},{3,7},{4,8},{5,9},{6,10},{7,11},{8,12},{9,13},{1... | collective-permute-start | bytes 393224 | tf_op jit(solution)/shard_map/ppermute | solution.py:452
  48.1 0.0 collective-permute-done.got1
  48.1 0.0 collective-permute-done.1.got2
  48.1 0.0 collective-permute-done.2.got3
  48.1 0.5 plane_total.1
  48.7 1.9 %collective-permute-start.6 = (bf16[128,128]{1,0:T(8,128)(2,1)S(1)}, bf16[128,128]{1,0:T(8,128)(2,1)S(1)}, u32[]{:S(2)}, u32[]{:S(2)}) collective-permute-start(bf16[128,128]{1,0:T(8,128)(2,1)S(1)} %plane_total.1), channel_id=1, source_target_pairs={{0,4},{1,5},{2,6},{3,7},{4,8},{5,9},{6,10},{7,11},{8,12},{9,13},{1... | collective-permute-start | bytes 98312 | tf_op jit(solution)/shard_map/ppermute | solution.py:453
  50.6 1.3 %collective-permute-start.7 = (bf16[128,128]{1,0:T(8,128)(2,1)S(1)}, bf16[128,128]{1,0:T(8,128)(2,1)S(1)}, u32[]{:S(2)}, u32[]{:S(2)}) collective-permute-start(bf16[128,128]{1,0:T(8,128)(2,1)S(1)} %plane_total.1), channel_id=1, source_target_pairs={{0,8},{1,9},{2,10},{3,11},{4,12},{5,13},{6,14},{7,15},{16,24},{17,... | collective-permute-start | bytes 98312 | tf_op jit(solution)/shard_map/ppermute | solution.py:453
  51.9 1.3 %collective-permute-start.8 = (bf16[128,128]{1,0:T(8,128)(2,1)S(1)}, bf16[128,128]{1,0:T(8,128)(2,1)S(1)}, u32[]{:S(2)}, u32[]{:S(2)}) collective-permute-start(bf16[128,128]{1,0:T(8,128)(2,1)S(1)} %plane_total.1), channel_id=1, source_target_pairs={{0,12},{1,13},{2,14},{3,15},{16,28},{17,29},{18,30},{19,31}} | collective-permute-start | bytes 98312 | tf_op jit(solution)/shard_map/ppermute | solution.py:453
  53.2 3.7 %prop.1 = bf16[2,1024,256]{2,1,0:T(8,128)(2,1)S(1)} custom-call(bf16[2,1024,1024]{2,1,0:T(8,128)(2,1)S(1)} %bitcast.15, bf16[1024,256]{1,0:T(8,128)(2,1)S(1)} %get-tuple-element.33.right), custom_call_target="tpu_custom_call" | custom-call | flops 1073741824 | bytes 4194304 | tf_op jit(solution)/shard_map/prop/pallas_call | solution.py:204
  56.9 0.4 plane_local.1.refs_6_
  57.4 0.0 collective-permute-done.10.refs_4_
  57.4 0.0 collective-permute-done.9.refs_3_
  57.4 0.0 collective-permute-done.6.refs_0_
  57.4 0.0 collective-permute-done.7.refs_1_
  57.4 0.0 collective-permute-done.8.refs_2_
  57.4 1.1 %entering.1 = (bf16[128,128]{1,0:T(8,128)(2,1)S(1)}, bf16[128,128]{1,0:T(8,128)(2,1)S(1)}, bf16[128,128]{1,0:T(8,128)(2,1)S(1)}, bf16[128,128]{1,0:T(8,128)(2,1)S(1)}) custom-call(bf16[128,128]{1,0:T(8,128)(2,1)S(1)} %collective-permute-done.6.refs_0_, bf16[128,128]{1,0:T(8,128)(2,1)S(1)} %collective-permute-done.7.refs_1_, ...), custom_call_target="tpu_custom_call" | custom-call | flops 150994944 | bytes 1179648 | tf_op jit(solution)/shard_map/entering/pallas_call | solution.py:396
  58.5 0.2 collective-permute-start.11
  58.7 1.1 %collective-permute-start.12 = (bf16[128,128]{1,0:T(8,128)(2,1)S(1)}, bf16[128,128]{1,0:T(8,128)(2,1)S(1)}, u32[]{:S(2)}, u32[]{:S(2)}) collective-permute-start(bf16[128,128]{1,0:T(8,128)(2,1)S(1)} %get-tuple-element.31), channel_id=1, source_target_pairs={{0,2},{1,3},{2,0},{3,1},{4,6},{5,7},{6,4},{7,5},{8,10},{9,11},{10,... | collective-permute-start | bytes 98312 | tf_op jit(solution)/shard_map/ppermute | solution.py:441
  59.9 0.7 %collective-permute-start.13 = (bf16[128,128]{1,0:T(8,128)(2,1)S(1)}, bf16[128,128]{1,0:T(8,128)(2,1)S(1)}, u32[]{:S(2)}, u32[]{:S(2)}) collective-permute-start(bf16[128,128]{1,0:T(8,128)(2,1)S(1)} %get-tuple-element.32), channel_id=1, source_target_pairs={{0,3},{1,0},{2,1},{3,2},{4,7},{5,4},{6,5},{7,6},{8,11},{9,8},{10,9... | collective-permute-start | bytes 98312 | tf_op jit(solution)/shard_map/ppermute | solution.py:441
  60.6 2.6 %image.1 = f32[2,1024,128]{2,1,0:T(8,128)S(1)} custom-call(bf16[2,1024,1024]{2,1,0:T(8,128)(2,1)S(1)} %bitcast.16, bf16[2,1024,128]{2,1,0:T(8,128)(2,1)S(1)} %get-tuple-element.34.right), custom_call_target="tpu_custom_call" | custom-call | flops 536870912 | bytes 4194304 | tf_op jit(solution)/shard_map/image/pallas_call | solution.py:204
  63.2 0.0 collective-permute-done.11.got1
  63.3 0.0 collective-permute-done.13.got3
  63.3 1.3 %waves.1 = bf16[2,1024,128]{2,1,0:T(8,128)(2,1)} custom-call(bf16[128,128]{1,0:T(8,128)(2,1)S(1)} %get-tuple-element.29.own, bf16[128,128]{1,0:T(8,128)(2,1)S(1)} %collective-permute-done.11.got1, bf16[128,128]{1,0:T(8,128)(2,1)S(1)} %collective-permute-done.12.got2, bf16[128,128]{1,0:T(8,128)(2,1)S(1)} %collective-permute-done.13.got3, ...), custom_call_target="tpu_custom_call" | custom-call | flops 134217728 | bytes 2621440 | tf_op jit(solution)/shard_map/waves/pallas_call | solution.py:421
  (13 shorter events, 0.0 us)
Async XLA Ops:
  0.0 17.1 %copy-start.8 = (s32[1,8,2]{1,2,0:T(2,128)S(1)}, s32[1,8,2]{1,2,0:T(2,128)}, u32[]{:S(2)}) copy-start(s32[1,8,2]{1,2,0:T(2,128)} %param.9) | copy-start | bytes 196
  0.8 2.2 %copy-start = (bf16[1,2,1024,1024]{3,2,1,0:T(8,128)(2,1)S(1)}, bf16[1,2,1024,1024]{3,2,1,0:T(8,128)(2,1)}, u32[]{:S(2)}) copy-start(bf16[1,2,1024,1024]{3,2,1,0:T(8,128)(2,1)} %param.6) | copy-start | bytes 12582916
  3.0 1.0 %copy-start.4 = (bf16[1,2,1024,128]{3,2,1,0:T(8,128)(2,1)S(1)}, bf16[1,2,1024,128]{3,2,1,0:T(8,128)(2,1)}, u32[]{:S(2)}) copy-start(bf16[1,2,1024,128]{3,2,1,0:T(8,128)(2,1)} %param.7) | copy-start | bytes 1572868
  4.0 0.7 %copy-start.7 = (s32[16,1]{0,1:T(1,128)S(1)}, s32[16,1]{0,1:T(1,128)}, u32[]{:S(2)}) copy-start(s32[16,1]{0,1:T(1,128)} %param.10) | copy-start | bytes 196
  4.7 12.5 %copy-start.6 = (bf16[1,1024,256]{2,1,0:T(8,128)(2,1)S(1)}, bf16[1,1024,256]{2,1,0:T(8,128)(2,1)}, u32[]{:S(2)}) copy-start(bf16[1,1024,256]{2,1,0:T(8,128)(2,1)} %param.8) | copy-start | bytes 1572868
  9.5 23.1 %copy-start.5 = (bf16[1,2,1024,128]{3,2,1,0:T(8,128)(2,1)S(1)}, bf16[1,2,1024,128]{3,2,1,0:T(8,128)(2,1)}, u32[]{:S(2)}) copy-start(bf16[1,2,1024,128]{3,2,1,0:T(8,128)(2,1)} %param.7) | copy-start | bytes 1572868
  9.5 23.1 %all-to-all-start = ((bf16[16,144,128]{2,1,0:T(8,128)(2,1)}), bf16[16,144,128]{2,1,0:T(8,128)(2,1)S(1)}, u32[]{:S(2)}, u32[]{:S(2)}) async-start(bf16[16,144,128]{2,1,0:T(8,128)(2,1)} %pairs.1), calls=%async_computation | async-start | bytes 1179648 | tf_op jit(solution)/shard_map/all_to_all | solution.py:477
  17.2 2.2 %copy-start.1 = (bf16[1,2,1024,1024]{3,2,1,0:T(8,128)(2,1)S(1)}, bf16[1,2,1024,1024]{3,2,1,0:T(8,128)(2,1)}, u32[]{:S(2)}) copy-start(bf16[1,2,1024,1024]{3,2,1,0:T(8,128)(2,1)} %param.6) | copy-start | bytes 12582916
  21.8 16.1 %collective-permute-start.3 = (f32[256,256]{1,0:T(8,128)}, f32[256,256]{1,0:T(8,128)S(1)}, u32[]{:S(2)}, u32[]{:S(2)}) collective-permute-start(f32[256,256]{1,0:T(8,128)} %get-tuple-element.37), channel_id=1, source_target_pairs={{0,1},{1,2},{2,3},{3,0},{4,5},{5,6},{6,7},{7,4},{8,9},{9,10},{10,1... | collective-permute-start | bytes 786440 | tf_op jit(solution)/shard_map/ppermute | solution.py:441
  22.1 16.5 %collective-permute-start.4 = (f32[256,256]{1,0:T(8,128)S(1)}, f32[256,256]{1,0:T(8,128)S(1)}, u32[]{:S(2)}, u32[]{:S(2)}) collective-permute-start(f32[256,256]{1,0:T(8,128)S(1)} %get-tuple-element.36), channel_id=1, source_target_pairs={{0,2},{1,3},{2,0},{3,1},{4,6},{5,7},{6,4},{7,5},{8,10},{9,11},{10,... | collective-permute-start | bytes 786440 | tf_op jit(solution)/shard_map/ppermute | solution.py:441
  23.8 14.8 %collective-permute-start.5 = (f32[256,256]{1,0:T(8,128)S(1)}, f32[256,256]{1,0:T(8,128)S(1)}, u32[]{:S(2)}, u32[]{:S(2)}) collective-permute-start(f32[256,256]{1,0:T(8,128)S(1)} %get-tuple-element.35), channel_id=1, source_target_pairs={{0,3},{1,0},{2,1},{3,2},{4,7},{5,4},{6,5},{7,6},{8,11},{9,8},{10,9... | collective-permute-start | bytes 786440 | tf_op jit(solution)/shard_map/ppermute | solution.py:441
  32.6 2.2 %copy-start.2 = (bf16[1,2,1024,1024]{3,2,1,0:T(8,128)(2,1)S(1)}, bf16[1,2,1024,1024]{3,2,1,0:T(8,128)(2,1)}, u32[]{:S(2)}) copy-start(bf16[1,2,1024,1024]{3,2,1,0:T(8,128)(2,1)} %param.6) | copy-start | bytes 12582916
  34.8 18.4 %copy-start.3 = (bf16[1,2,1024,1024]{3,2,1,0:T(8,128)(2,1)S(1)}, bf16[1,2,1024,1024]{3,2,1,0:T(8,128)(2,1)}, u32[]{:S(2)}) copy-start(bf16[1,2,1024,1024]{3,2,1,0:T(8,128)(2,1)} %param.6) | copy-start | bytes 12582916
  36.5 11.6 %collective-permute-start = (bf16[128,128]{1,0:T(8,128)(2,1)S(1)}, bf16[128,128]{1,0:T(8,128)(2,1)S(1)}, u32[]{:S(2)}, u32[]{:S(2)}) collective-permute-start(bf16[128,128]{1,0:T(8,128)(2,1)S(1)} %get-tuple-element.21), channel_id=1, source_target_pairs={{0,1},{1,2},{2,3},{3,0},{4,5},{5,6},{6,7},{7,4},{8,9},{9,10},{10,1... | collective-permute-start | bytes 98312 | tf_op jit(solution)/shard_map/ppermute | solution.py:441
  36.6 11.6 %collective-permute-start.1 = (bf16[128,128]{1,0:T(8,128)(2,1)S(1)}, bf16[128,128]{1,0:T(8,128)(2,1)S(1)}, u32[]{:S(2)}, u32[]{:S(2)}) collective-permute-start(bf16[128,128]{1,0:T(8,128)(2,1)S(1)} %get-tuple-element.22), channel_id=1, source_target_pairs={{0,2},{1,3},{2,0},{3,1},{4,6},{5,7},{6,4},{7,5},{8,10},{9,11},{10,... | collective-permute-start | bytes 98312 | tf_op jit(solution)/shard_map/ppermute | solution.py:441
  37.9 10.3 %collective-permute-start.2 = (bf16[128,128]{1,0:T(8,128)(2,1)S(1)}, bf16[128,128]{1,0:T(8,128)(2,1)S(1)}, u32[]{:S(2)}, u32[]{:S(2)}) collective-permute-start(bf16[128,128]{1,0:T(8,128)(2,1)S(1)} %get-tuple-element.23), channel_id=1, source_target_pairs={{0,3},{1,0},{2,1},{3,2},{4,7},{5,4},{6,5},{7,6},{8,11},{9,8},{10,9... | collective-permute-start | bytes 98312 | tf_op jit(solution)/shard_map/ppermute | solution.py:441
  40.7 16.7 %collective-permute-start.10 = (bf16[256,256]{1,0:T(8,128)(2,1)S(1)}, bf16[256,256]{1,0:T(8,128)(2,1)S(1)}, u32[]{:S(2)}, u32[]{:S(2)}) collective-permute-start(bf16[256,256]{1,0:T(8,128)(2,1)S(1)} %get-tuple-element.26), channel_id=1, source_target_pairs={{0,8},{1,9},{2,10},{3,11},{4,12},{5,13},{6,14},{7,15},{16,24},{17,... | collective-permute-start | bytes 393224 | tf_op jit(solution)/shard_map/ppermute | solution.py:452
  45.0 12.4 %collective-permute-start.9 = (bf16[256,256]{1,0:T(8,128)(2,1)S(1)}, bf16[256,256]{1,0:T(8,128)(2,1)S(1)}, u32[]{:S(2)}, u32[]{:S(2)}) collective-permute-start(bf16[256,256]{1,0:T(8,128)(2,1)S(1)} %get-tuple-element.26), channel_id=1, source_target_pairs={{0,4},{1,5},{2,6},{3,7},{4,8},{5,9},{6,10},{7,11},{8,12},{9,13},{1... | collective-permute-start | bytes 393224 | tf_op jit(solution)/shard_map/ppermute | solution.py:452
  48.7 8.7 %collective-permute-start.6 = (bf16[128,128]{1,0:T(8,128)(2,1)S(1)}, bf16[128,128]{1,0:T(8,128)(2,1)S(1)}, u32[]{:S(2)}, u32[]{:S(2)}) collective-permute-start(bf16[128,128]{1,0:T(8,128)(2,1)S(1)} %plane_total.1), channel_id=1, source_target_pairs={{0,4},{1,5},{2,6},{3,7},{4,8},{5,9},{6,10},{7,11},{8,12},{9,13},{1... | collective-permute-start | bytes 98312 | tf_op jit(solution)/shard_map/ppermute | solution.py:453
  50.6 6.8 %collective-permute-start.7 = (bf16[128,128]{1,0:T(8,128)(2,1)S(1)}, bf16[128,128]{1,0:T(8,128)(2,1)S(1)}, u32[]{:S(2)}, u32[]{:S(2)}) collective-permute-start(bf16[128,128]{1,0:T(8,128)(2,1)S(1)} %plane_total.1), channel_id=1, source_target_pairs={{0,8},{1,9},{2,10},{3,11},{4,12},{5,13},{6,14},{7,15},{16,24},{17,... | collective-permute-start | bytes 98312 | tf_op jit(solution)/shard_map/ppermute | solution.py:453
  51.9 5.5 %collective-permute-start.8 = (bf16[128,128]{1,0:T(8,128)(2,1)S(1)}, bf16[128,128]{1,0:T(8,128)(2,1)S(1)}, u32[]{:S(2)}, u32[]{:S(2)}) collective-permute-start(bf16[128,128]{1,0:T(8,128)(2,1)S(1)} %plane_total.1), channel_id=1, source_target_pairs={{0,12},{1,13},{2,14},{3,15},{16,28},{17,29},{18,30},{19,31}} | collective-permute-start | bytes 98312 | tf_op jit(solution)/shard_map/ppermute | solution.py:453
  58.5 4.7 %collective-permute-start.11 = (bf16[128,128]{1,0:T(8,128)(2,1)S(1)}, bf16[128,128]{1,0:T(8,128)(2,1)S(1)}, u32[]{:S(2)}, u32[]{:S(2)}) collective-permute-start(bf16[128,128]{1,0:T(8,128)(2,1)S(1)} %get-tuple-element.30), channel_id=1, source_target_pairs={{0,1},{1,2},{2,3},{3,0},{4,5},{5,6},{6,7},{7,4},{8,9},{9,10},{10,1... | collective-permute-start | bytes 98312 | tf_op jit(solution)/shard_map/ppermute | solution.py:441
  58.7 4.5 %collective-permute-start.12 = (bf16[128,128]{1,0:T(8,128)(2,1)S(1)}, bf16[128,128]{1,0:T(8,128)(2,1)S(1)}, u32[]{:S(2)}, u32[]{:S(2)}) collective-permute-start(bf16[128,128]{1,0:T(8,128)(2,1)S(1)} %get-tuple-element.31), channel_id=1, source_target_pairs={{0,2},{1,3},{2,0},{3,1},{4,6},{5,7},{6,4},{7,5},{8,10},{9,11},{10,... | collective-permute-start | bytes 98312 | tf_op jit(solution)/shard_map/ppermute | solution.py:441
  59.9 3.4 %collective-permute-start.13 = (bf16[128,128]{1,0:T(8,128)(2,1)S(1)}, bf16[128,128]{1,0:T(8,128)(2,1)S(1)}, u32[]{:S(2)}, u32[]{:S(2)}) collective-permute-start(bf16[128,128]{1,0:T(8,128)(2,1)S(1)} %get-tuple-element.32), channel_id=1, source_target_pairs={{0,3},{1,0},{2,1},{3,2},{4,7},{5,4},{6,5},{7,6},{8,11},{9,8},{10,9... | collective-permute-start | bytes 98312 | tf_op jit(solution)/shard_map/ppermute | solution.py:441

commit v3 on v2

--- a/solution.py
+++ b/solution.py
@@ -15,10 +15,13 @@
 HIGH = lax.Precision.HIGHEST
 F32 = jnp.float32
 BF16 = jnp.bfloat16
-VMEM_BYTES = 40 * 1024 * 1024
+VMEM_SMALL = 16 * 1024 * 1024
+VMEM_LARGE = 60000000
+VMEM_WHOLE = 63400000
 
 IN_VMEM = pl.BlockSpec(memory_space=pltpu.VMEM)
 IN_SMEM = pl.BlockSpec(memory_space=pltpu.SMEM)
+IN_HBM = pl.BlockSpec(memory_space=pltpu.HBM)
 IN_PLACE = pl.BlockSpec(memory_space=pl.ANY)
 
 
@@ -26,7 +29,7 @@
     return jax.ShapeDtypeStruct(dims, dtype)
 
 
-def call(body, name, ins, outs, scratch, flops, moved):
+def call(body, name, ins, outs, scratch, flops, moved, vmem=VMEM_SMALL):
     return pl.pallas_call(
         body,
         name=name,
@@ -34,7 +37,7 @@
         out_shape=outs,
         out_specs=jax.tree.map(lambda _: IN_VMEM, outs),
         scratch_shapes=scratch,
-        compiler_params=pltpu.CompilerParams(vmem_limit_bytes=VMEM_BYTES),
+        compiler_params=pltpu.CompilerParams(vmem_limit_bytes=vmem),
         cost_estimate=pl.CostEstimate(flops=flops, bytes_accessed=moved, transcendentals=0),
     )
 
@@ -85,29 +88,39 @@
     return size, out
 
 
-def pairs_kernel(owner, blocks, green, inject, out, held, full, slot_of, counts, sem):
+def gathered(refs, held):
+    here = place()
+    for k, ref in enumerate(refs):
+        held[(here + GROUP - k) % GROUP] = ref[...]
+
+
+def pairs_kernel(owner_in, blocks_in, green, inject_in, out, owner, blocks, inject, held, full, slot_of, counts, sem, side):
     energies, orbitals, _ = green.shape
     sections = out.shape[0]
     count = owner.shape[0]
+    lists = [
+        pltpu.make_async_copy(owner_in, owner, side.at[0]),
+        pltpu.make_async_copy(blocks_in, blocks, side.at[1]),
+    ]
+    columns = pltpu.make_async_copy(inject_in, inject, side.at[2])
     size, moves = copies(green, held, sem, pl.ds(0, orbitals), sem.shape[1])
+    for move in (*lists, columns):
+        move.start()
     for _, _, move in moves:
         move.start()
-    out[...] = jnp.zeros_like(out)
-
-    def clear(d, _):
-        counts[d] = 0
-        return 0
-
-    lax.fori_loop(0, sections, clear, 0)
     rows = CAP * energies * BLK
     lane = lax.broadcasted_iota(jnp.int32, (HEAD, out.shape[2]), 1)
     none = jnp.where(lane < CAP, -1.0, 0.0).astype(BF16)
 
     def blank(d, _):
+        counts[d] = 0
+        out[d, :rows, :] = jnp.zeros((rows, out.shape[2]), BF16)
         out[d, rows : rows + HEAD, :] = none
         return 0
 
     lax.fori_loop(0, sections, blank, 0)
+    for move in lists:
+        move.wait()
 
     def rank(q, _):
         d = owner[q]
@@ -115,24 +128,25 @@
         counts[d] = r + 1
         slot_of[q] = r
         head = out[d, rows : rows + HEAD, :].astype(F32)
-        head = jnp.where(lane == r, blocks[q, 1].astype(F32), head)
+        head = jnp.where(lane == r, blocks[1, q].astype(F32), head)
         out[d, rows : rows + HEAD, :] = head.astype(BF16)
         return 0
 
     lax.fori_loop(0, count, rank, 0)
+    columns.wait()
     for e, first, move in moves:
         move.wait()
         full[e, first : first + size, :] = dot(held[e, first : first + size, :], inject[e]).astype(BF16)
 
     def fill(q, _):
         d, r = owner[q], slot_of[q]
-        first = pl.multiple_of(blocks[q, 0] * BLK, BLK)
+        first = pl.multiple_of(blocks[0, q] * BLK, BLK)
         for e in range(energies):
             to = pl.multiple_of((r * energies + e) * BLK, BLK)
             out[d, pl.ds(to, BLK), :] = full[e, pl.ds(first, BLK), :]
         return 0
 
-    lax.fori_loop(0, count, fill, 0)
+    lax.fori_loop(0, count, fill, 0, unroll=4)
 
 
 def outgoing_pairs(owner, blocks, green, inject, sections):
@@ -142,48 +156,72 @@
     return call(
         pairs_kernel,
         "pairs",
-        [IN_SMEM, IN_SMEM, IN_PLACE, IN_VMEM],
+        [IN_HBM] * 4,
         shape(sections, CAP * energies * BLK + HEAD, columns),
         [
+            pltpu.SMEM(owner.shape, jnp.int32),
+            pltpu.SMEM(blocks.shape, jnp.int32),
+            pltpu.VMEM(inject.shape, BF16),
             pltpu.VMEM(green.shape, BF16),
             pltpu.VMEM(inject.shape, BF16),
             pltpu.SMEM(owner.shape, jnp.int32),
             pltpu.SMEM((sections,), jnp.int32),
             pltpu.SemaphoreType.DMA((energies, steps)),
+            pltpu.SemaphoreType.DMA((3,)),
         ],
         2 * energies * orbitals * orbitals * columns,
         2 * green.size,
+        VMEM_WHOLE,
     )(owner, blocks, green, inject)
 
 
-def maps_kernel(pattern, green, coupling, face_map, couple, held, sem):
+def maps_kernel(pattern_in, green, coupling_in, couple, own, send1, send2, send3, pattern, coupling, held, maps, sem, side):
     energies, orbitals, _ = green.shape
     face = coupling.shape[1]
     size, moves = copies(green, held, sem, pl.ds(orbitals - face, face), sem.shape[1])
+    tiles = pltpu.make_async_copy(pattern_in, pattern, side.at[0])
+    whole = pltpu.make_async_copy(coupling_in, coupling, side.at[1])
+    tiles.start()
+    whole.start()
     for _, _, move in moves:
         move.start()
-    high, wide = orbitals // pattern.shape[0], face // pattern.shape[1]
-    for i in range(pattern.shape[0]):
-        for j in range(pattern.shape[1]):
+    tiles.wait()
+    whole.wait()
+    high, wide = orbitals // pattern.shape[1], face // pattern.shape[0]
+    for i in range(pattern.shape[1]):
+        for j in range(pattern.shape[0]):
             at = (slice(i * high, (i + 1) * high), slice(j * wide, (j + 1) * wide))
             tile = coupling[at]
-            couple[at] = jnp.where(pattern[i, j] == 1, tile, jnp.zeros_like(tile))
+            couple[at] = jnp.where(pattern[j, i] == 1, tile, jnp.zeros_like(tile))
     for e, first, move in moves:
         move.wait()
-        face_map[e, first : first + size, :] = dot(held[e, first : first + size, :], couple[...])
+        maps[e, first : first + size, :] = dot(held[e, first : first + size, :], couple[...])
+    here = place()
+    split = GROUP // energies
+    for k, out in enumerate((own, send1, send2, send3)):
+        out[...] = maps[(here + k) % GROUP // split]
 
 
 def face_maps(pattern, green, coupling):
     energies, orbitals, _ = green.shape
     face = coupling.shape[1]
+    square = shape(face, face, dtype=F32)
     return call(
         maps_kernel,
         "face_maps",
-        [IN_SMEM, IN_PLACE, IN_VMEM],
-        [shape(energies, face, face, dtype=F32), shape(orbitals, face)],
-        [pltpu.VMEM((energies, face, orbitals), BF16), pltpu.SemaphoreType.DMA((energies, 1))],
+        [IN_HBM] * 3,
+        [shape(orbitals, face)] + [square] * GROUP,
+        [
+            pltpu.SMEM(pattern.shape, jnp.int32),
+            pltpu.VMEM(coupling.shape, BF16),
+            pltpu.VMEM((energies, face, orbitals), BF16),
+            pltpu.VMEM((energies, face, face), F32),
+            pltpu.SemaphoreType.DMA((energies, 1)),
+            pltpu.SemaphoreType.DMA((2,)),
+        ],
         2 * energies * face * orbitals * face,
         2 * energies * face * orbitals,
+        VMEM_WHOLE,
     )(pattern, green, coupling)
 
 
@@ -204,40 +242,40 @@
     return call(
         product_kernel,
         name,
-        [IN_PLACE, IN_VMEM],
+        [IN_HBM, IN_VMEM],
         shape(energies, orbitals, wide, dtype=dtype),
         [pltpu.VMEM(green.shape, BF16), pltpu.SemaphoreType.DMA((energies, 4))],
         2 * energies * orbitals * orbitals * wide,
         2 * green.size,
+        VMEM_LARGE,
     )(green, right)
 
 
 def chain_kernel(own, got1, got2, got3, total_out, after_out, within_out, upto_out, maps):
-    here = place()
-    split = GROUP // own.shape[0]
-    maps[here] = own[here // split]
-    for k, got in enumerate((got1, got2, got3), 1):
-        maps[(here + GROUP - k) % GROUP] = got[...]
-    first, second, third, fourth = (maps[j] for j in range(GROUP))
-    face = first.shape[0]
-    upto2 = dot_wide(second, first)
-    upto3 = dot_wide(third, upto2)
-    after1 = dot_wide(fourth, third)
-    after0 = dot_wide(after1, second)
-    total_out[...] = dot_wide(fourth, upto3).astype(total_out.dtype)
+    gathered((own, got1, got2, got3), maps)
+    first, second, third, fourth = (two_parts(maps[j]) for j in range(GROUP))
+    face = own.shape[0]
+
+    def times(a, b):
+        return dot(a[0], b[0]) + (dot(a[0], b[1]) + dot(a[1], b[0]))
+
+    upto2 = two_parts(times(second, first))
+    upto3 = two_parts(times(third, upto2))
+    after1 = two_parts(times(fourth, third))
+    after0 = two_parts(times(after1, second))
+    total_out[...] = times(fourth, upto3).astype(total_out.dtype)
     for out, items in (
         (after_out, (after0, after1, fourth)),
-        (within_out, (second, third, dot_wide(third, second))),
+        (within_out, (second, third, two_parts(times(third, second)))),
         (upto_out, (first, upto2, upto3)),
     ):
-        for j, item in enumerate(items):
-            high, low = two_parts(item)
+        for j, (high, low) in enumerate(items):
             out[0, j * face : (j + 1) * face, :] = high
             out[1, j * face : (j + 1) * face, :] = low
 
 
-def chain(own, got, total_dtype):
-    face = own.shape[1]
+def chain(maps, total_dtype):
+    face = maps[0].shape[0]
     stack = shape(2, (GROUP - 1) * face, face)
     return call(
         chain_kernel,
@@ -245,13 +283,15 @@
         [IN_VMEM] * GROUP,
         [shape(face, face, dtype=total_dtype), stack, stack, stack],
         [pltpu.VMEM((GROUP, face, face), F32)],
-        2 * 6 * 6 * face**3,
+        2 * 6 * 3 * face**3,
         4 * 10 * face * face,
-    )(own, *got)
-
-
-def source_kernel(received, inject, green, source, own, send1, send2, send3, held, total, heads, targets, quarters, sem, head_sem):
+    )(*maps)
+
+
+def source_kernel(received, inject_in, green, _prop, _map, source, own, send1, send2, send3, held, inject, total, heads, targets, quarters, sem, head_sem, side):
     energies, orbitals, columns = inject.shape
+    columns_in = pltpu.make_async_copy(inject_in, inject, side)
+    columns_in.start()
     sections = received.shape[0]
     face = held.shape[1]
     size, moves = copies(green, held, sem, pl.ds(orbitals - face, face), sem.shape[1])
@@ -267,6 +307,7 @@
     lax.fori_loop(0, sections, read, 0, unroll=min(sections, 8))
     fetch = pltpu.make_async_copy(heads, targets, head_sem)
     fetch.start()
+    columns_in.wait()
     total[...] = inject[...].astype(F32)
     fetch.wait()
 
@@ -293,33 +334,30 @@
         out[...] = quarters[(here + k) % GROUP].astype(BF16)
 
 
-def placed_source(received, inject, green, face):
+def placed_source(received, inject, green, face, ready):
     energies, orbitals, columns = inject.shape
     sections = received.shape[0]
     quarter = shape(face // 2, columns)
     return call(
         source_kernel,
         "source_and_face",
-        [IN_VMEM, IN_VMEM, IN_PLACE],
+        [IN_VMEM, IN_HBM, IN_HBM, IN_PLACE, IN_PLACE],
         [shape(*inject.shape), quarter, quarter, quarter, quarter],
         [
             pltpu.VMEM((energies, face, orbitals), BF16),
+            pltpu.VMEM(inject.shape, BF16),
             pltpu.VMEM(inject.shape, F32),
             pltpu.VMEM((sections, columns), jnp.int32),
             pltpu.SMEM((sections, columns), jnp.int32),
             pltpu.VMEM((GROUP, face // 2, columns), F32),
             pltpu.SemaphoreType.DMA((energies, 1)),
             pltpu.SemaphoreType.DMA,
+            pltpu.SemaphoreType.DMA,
         ],
         2 * energies * face * orbitals * columns,
         2 * energies * face * orbitals + 2 * received.size,
-    )(received, inject, green)
-
-
-def gathered(refs, held):
-    here = place()
-    for k, ref in enumerate(refs):
-        held[(here + GROUP - k) % GROUP] = ref[...]
+        VMEM_LARGE,
+    )(received, inject, green, *ready)
 
 
 def apply(parts, j, x):
@@ -373,7 +411,7 @@
 
 def entering_kernel(count, *refs):
     below, maps = refs[:count], refs[count : 2 * count - 1]
-    upto, local, own, send1, send2, send3, held = refs[2 * count - 1 :]
+    upto, local, _image, own, send1, send2, send3, held = refs[2 * count - 1 :]
     base = unpack(below[-1][...].astype(F32))
     for k in range(count - 2, -1, -1):
         high, low = two_parts(base)
@@ -389,19 +427,19 @@
         out[...] = held[(here + k) % GROUP].astype(BF16)
 
 
-def entering(below, maps, upto, local):
+def entering(below, maps, upto, local, ready):
     half, columns = below[0].shape
     count = len(below)
     quarter = shape(half, columns)
     return call(
         functools.partial(entering_kernel, count),
         "entering",
-        [IN_VMEM] * (2 * count + 1),
+        [IN_VMEM] * (2 * count + 1) + [IN_PLACE],
         [quarter] * GROUP,
         [pltpu.VMEM((GROUP, half, columns), F32)],
         3 * upto.size * columns,
         2 * upto.size + 4 * local.size,
-    )(*below, *maps, upto, local)
+    )(*below, *maps, upto, local, ready)
 
 
 def waves_kernel(own, got1, got2, got3, prop, image, out, held):
@@ -467,29 +505,25 @@
 
 def per_device(green, injected, coupling, pattern, owner, pair_blocks):
     sections = lax.axis_size("sec")
-    here = lax.axis_index("sec") % GROUP
     green, inject = green[0], injected[0]
-    energies = green.shape[0]
     face = coupling.shape[2]
-    split = GROUP // energies
-
-    outgoing = outgoing_pairs(owner[:, 0], pair_blocks, green, inject, sections)
+
+    outgoing = outgoing_pairs(owner[:, 0], pair_blocks.T, green, inject, sections)
     received = lax.all_to_all(outgoing, "sec", split_axis=0, concat_axis=0, tiled=True)
 
-    face_map, couple = face_maps(pattern[0], green, coupling[0])
-    sent = [lax.dynamic_index_in_dim(face_map, (here + k) % GROUP // split, 0, False) for k in range(1, GROUP)]
+    couple, own_map, *sent = face_maps(pattern[0].T, green, coupling[0])
     total_dtype = BF16 if sections // GROUP <= 4 else F32
-    total_map, after, within, upto = chain(face_map, in_plane(sent, sections), total_dtype)
+    total_map, after, within, upto = chain([own_map] + in_plane(sent, sections), total_dtype)
     prop = product(green, couple, BF16, "prop")
 
-    source, own, *quarters = placed_source(received, inject, green, face)
+    source, own, *quarters = placed_source(received, inject, green, face, (prop, total_map))
     shifts = [own] + in_plane(quarters, sections)
     total = plane_total(shifts, after)
     below, maps = gather_below(total_map, total, sections)
     local = plane_local(shifts, within)
-    own, *inner = entering(below, maps, upto, local)
+    image = product(green, source, F32, "image")
+    own, *inner = entering(below, maps, upto, local, image)
     arrived = [own] + in_plane(inner, sections)
-    image = product(green, source, F32, "image")
     return final_waves(arrived, prop, image)[None]
 
 

time: 65.1 us -> 79.5 us (1.22)
  waiting for transfers between devices: 7.53 us -> 18 us
  Pallas kernels: 20 us -> 29.2 us
  local copies, waits for them, and re-layouts: 9.89 us -> 3.77 us
  starting transfers between devices: 26.8 us -> 27.6 us
    ppermute x9, waiting for transfers between devices: 0.02 us -> 18 us  [in_plane(): lax.ppermute(item, 'sec', plane_shift(sections, k))]
    pallas_call x5, Pallas kernels: 14.5 us -> 24.6 us  [the longest x2 12 us: product(): call(product_kernel, name, [IN_HBM, IN_VMEM], shape(energies, orbitals, w...]
    all_to_all x1, waiting for transfers between devices: 7.49 us -> 0.01 us  [per_device(): lax.all_to_all(outgoing, 'sec', split_axis=0, concat_axis=0, tiled=True)]
    unnamed x19 -> x16, local copies, waits for them, and re-layouts: 9.05 us -> 3.77 us
    ppermute x9, starting transfers between devices: 7.36 us -> 8.49 us  [in_plane(): lax.ppermute(item, 'sec', plane_shift(sections, k))]
    pallas_call x1, Pallas kernels: 2.09 us -> 1.19 us  [chain(): call(chain_kernel, 'chain_maps', [IN_VMEM] * GROUP, [shape(face, face, dt...]
    squeeze x2 -> x0, local copies, waits for them, and re-layouts: 0.85 us -> none  [the longest x1 0.77 us: per_device(): lax.dynamic_index_in_dim(face_map, (here + k) % GROUP // split, 0, False)]
  transfers between devices with their start and end apart: 15 -> 15, of which waited for: 1 -> 7; matrix products, arithmetic and copies ran while one was open for 1% -> 0% of each run, Pallas kernels for 20% -> 27%
where the time goes in v3:
time: 79.5 us; the launch traced here: 78.8 us
  Pallas kernels  29.2 us (37%)
  starting transfers between devices  27.6 us (35%)
  waiting for transfers between devices  18 us (23%)
  local copies, waits for them, and re-layouts  3.77 us (5%)
    ppermute x9, waiting for transfers between devices, in_plane(): lax.ppermute(item, 'sec', plane_shift(sections, k))  18 us
    pallas_call x2, Pallas kernels, product(): call(product_kernel, name, [IN_HBM, IN_VMEM], shape(energies, orbitals, w...  12 us
    ppermute x9, starting transfers between devices, in_plane(): lax.ppermute(item, 'sec', plane_shift(sections, k))  8.49 us
    all_to_all x1, starting transfers between devices, per_device(): lax.all_to_all(outgoing, 'sec', split_axis=0, concat_axis=0, tiled=True)  7.37 us
    ppermute x2, starting transfers between devices, gather_below(): lax.ppermute(total_map, 'sec', up_shift(sections, k))  6.98 us
    pallas_call x1, Pallas kernels, outgoing_pairs(): call(pairs_kernel, 'pairs', [IN_HBM] * 4, shape(sections, CAP * energies...  5.47 us
    ppermute x3, starting transfers between devices, gather_below(): lax.ppermute(total, 'sec', up_shift(sections, k))  4.77 us
    pallas_call x1, Pallas kernels, placed_source(): call(source_kernel, 'source_and_face', [IN_VMEM, IN_HBM, IN_HBM, IN_PLACE...  3.97 us
  transfers between devices with their start and end apart: 15, of which 7 were waited for; matrix products, arithmetic and copies ran while one was open for 0% of the time, Pallas kernels for 27%

profile of v3, /device:TPU:0, one launch (start us, length us, event | category | flops | bytes accessed | tf_op | source)
XLA Modules:
  0.0 78.8 jit_solution(8383670787986094343)
XLA Ops:
  0.0 5.5 %pairs.1 = bf16[16,144,128]{2,1,0:T(8,128)(2,1)} custom-call(s32[16]{0:T(128)} %bitcast.19, s32[2,16]{1,0:T(2,128)} %bitcast.17, bf16[2,1024,1024]{2,1,0:T(8,128)(2,1)} %bitcast.9, bf16[2,1024,128]{2,1,0:T(8,128)(2,1)} %bitcast.14), custom_call_target="tpu_custom_call" | custom-call | flops 536870912 | bytes 4194304 | tf_op jit(solution)/shard_map/pairs/pallas_call | solution.py:156
  5.5 7.4 %all-to-all-start = ((bf16[16,144,128]{2,1,0:T(8,128)(2,1)}), bf16[16,144,128]{2,1,0:T(8,128)(2,1)S(1)}, u32[]{:S(2)}, u32[]{:S(2)}) async-start(bf16[16,144,128]{2,1,0:T(8,128)(2,1)} %pairs.1), calls=%async_computation | async-start | bytes 1179648 | tf_op jit(solution)/shard_map/all_to_all | solution.py:512
  12.9 3.2 %face_maps.1 = (bf16[1024,256]{1,0:T(8,128)(2,1)}, f32[256,256]{1,0:T(8,128)}, f32[256,256]{1,0:T(8,128)}, f32[256,256]{1,0:T(8,128)}, f32[256,256]{1,0:T(8,128)}) custom-call(s32[2,8]{1,0:T(2,128)} %bitcast.18, bf16[2,1024,1024]{2,1,0:T(8,128)(2,1)} %bitcast.10, bf16[1024,256]{1,0:T(8,128)(2,1)} %bitcast.16), custom_call_target="tpu_custom_call" | custom-call | flops 268435456 | bytes 1048576 | tf_op jit(solution)/shard_map/face_maps/pallas_call | solution.py:209
  16.0 0.5 collective-permute-start
  16.5 1.7 %collective-permute-start.1 = (f32[256,256]{1,0:T(8,128)}, f32[256,256]{1,0:T(8,128)S(1)}, u32[]{:S(2)}, u32[]{:S(2)}) collective-permute-start(f32[256,256]{1,0:T(8,128)} %get-tuple-element.26), channel_id=1, source_target_pairs={{0,2},{1,3},{2,0},{3,1},{4,6},{5,7},{6,4},{7,5},{8,10},{9,11},{10,... | collective-permute-start | bytes 786440 | tf_op jit(solution)/shard_map/ppermute | solution.py:479
  18.2 1.3 %collective-permute-start.2 = (f32[256,256]{1,0:T(8,128)}, f32[256,256]{1,0:T(8,128)S(1)}, u32[]{:S(2)}, u32[]{:S(2)}) collective-permute-start(f32[256,256]{1,0:T(8,128)} %get-tuple-element.27), channel_id=1, source_target_pairs={{0,3},{1,0},{2,1},{3,2},{4,7},{5,4},{6,5},{7,6},{8,11},{9,8},{10,9... | collective-permute-start | bytes 786440 | tf_op jit(solution)/shard_map/ppermute | solution.py:479
  19.5 6.8 %collective-permute-done.got1 = f32[256,256]{1,0:T(8,128)S(1)} collective-permute-done((f32[256,256]{1,0:T(8,128)}, f32[256,256]{1,0:T(8,128)S(1)}, u32[]{:S(2)}, u32[]{:S(2)}) %collective-permute-start) | collective-permute-done | bytes 262176 | tf_op jit(solution)/shard_map/ppermute | solution.py:479
  26.3 2.6 %collective-permute-done.1.got2 = f32[256,256]{1,0:T(8,128)S(1)} collective-permute-done((f32[256,256]{1,0:T(8,128)}, f32[256,256]{1,0:T(8,128)S(1)}, u32[]{:S(2)}, u32[]{:S(2)}) %collective-permute-start.1) | collective-permute-done | bytes 262176 | tf_op jit(solution)/shard_map/ppermute | solution.py:479
  28.9 4.5 %collective-permute-done.2.got3 = f32[256,256]{1,0:T(8,128)S(1)} collective-permute-done((f32[256,256]{1,0:T(8,128)}, f32[256,256]{1,0:T(8,128)S(1)}, u32[]{:S(2)}, u32[]{:S(2)}) %collective-permute-start.2) | collective-permute-done | bytes 262176 | tf_op jit(solution)/shard_map/ppermute | solution.py:479
  33.4 0.9 %copy-done.6 = f32[256,256]{1,0:T(8,128)S(1)} copy-done((f32[256,256]{1,0:T(8,128)S(1)}, f32[256,256]{1,0:T(8,128)}, u32[]{:S(2)}) %copy-start.6) | copy-done | bytes 262168
  34.3 1.2 %chain_maps.1 = (bf16[256,256]{1,0:T(8,128)(2,1)S(1)}, bf16[2,768,256]{2,1,0:T(8,128)(2,1)S(1)}, bf16[2,768,256]{2,1,0:T(8,128)(2,1)S(1)}, bf16[2,768,256]{2,1,0:T(8,128)(2,1)S(1)}) custom-call(f32[256,256]{1,0:T(8,128)S(1)} %copy-done.6, f32[256,256]{1,0:T(8,128)S(1)} %collective-permute-done.got1, f32[256,256]{1,0:T(8,128)S(1)} %collective-permute-done.1.got2, ...), custom_call_target="tpu_custom_call" | custom-call | flops 603979776 | bytes 2621440 | tf_op jit(solution)/shard_map/chain_maps/pallas_call | solution.py:280
  35.5 0.0 copy-start.3
  35.5 4.3 %collective-permute-start.10 = (bf16[256,256]{1,0:T(8,128)(2,1)S(1)}, bf16[256,256]{1,0:T(8,128)(2,1)S(1)}, u32[]{:S(2)}, u32[]{:S(2)}) collective-permute-start(bf16[256,256]{1,0:T(8,128)(2,1)S(1)} %get-tuple-element.28._map), channel_id=1, source_target_pairs={{0,8},{1,9},{2,10},{3,11},{4,12},{5,13},{6,14},{7,15},{16,24},{17,... | collective-permute-start | bytes 393224 | tf_op jit(solution)/shard_map/ppermute | solution.py:490
  39.8 2.7 %collective-permute-start.9 = (bf16[256,256]{1,0:T(8,128)(2,1)S(1)}, bf16[256,256]{1,0:T(8,128)(2,1)S(1)}, u32[]{:S(2)}, u32[]{:S(2)}) collective-permute-start(bf16[256,256]{1,0:T(8,128)(2,1)S(1)} %get-tuple-element.28._map), channel_id=1, source_target_pairs={{0,4},{1,5},{2,6},{3,7},{4,8},{5,9},{6,10},{7,11},{8,12},{9,13},{1... | collective-permute-start | bytes 393224 | tf_op jit(solution)/shard_map/ppermute | solution.py:490
  42.5 6.5 %prop.1._prop = bf16[2,1024,256]{2,1,0:T(8,128)(2,1)} custom-call(bf16[2,1024,1024]{2,1,0:T(8,128)(2,1)} %bitcast.11, bf16[1024,256]{1,0:T(8,128)(2,1)} %get-tuple-element.23.right), custom_call_target="tpu_custom_call" | custom-call | flops 1073741824 | bytes 4194304 | tf_op jit(solution)/shard_map/prop/pallas_call | solution.py:242
  49.1 0.0 all-to-all-done.received
  49.1 0.0 copy-done.3
  49.1 0.8 %copy-done.7 = bf16[16,144,128]{2,1,0:T(8,128)(2,1)} copy-done((bf16[16,144,128]{2,1,0:T(8,128)(2,1)}, bf16[16,144,128]{2,1,0:T(8,128)(2,1)S(1)}, u32[]{:S(2)}) %copy-start.7) | copy-done | bytes 589848
  49.9 4.0 %source_and_face.1 = (bf16[2,1024,128]{2,1,0:T(8,128)(2,1)}, bf16[128,128]{1,0:T(8,128)(2,1)}, bf16[128,128]{1,0:T(8,128)(2,1)}, bf16[128,128]{1,0:T(8,128)(2,1)}, bf16[128,128]{1,0:T(8,128)(2,1)}) custom-call(bf16[16,144,128]{2,1,0:T(8,128)(2,1)} %copy-done.7, bf16[2,1024,128]{2,1,0:T(8,128)(2,1)} %bitcast.15, bf16[2,1024,1024]{2,1,0:T(8,128)(2,1)} %bitcast.12, ...), custom_call_target="tpu_custom_call" | custom-call | flops 134217728 | bytes 1638400 | tf_op jit(solution)/shard_map/source_and_face/pallas_call | solution.py:341
  53.9 0.3 collective-permute-start.3
  54.2 1.4 %collective-permute-start.4 = (bf16[128,128]{1,0:T(8,128)(2,1)}, bf16[128,128]{1,0:T(8,128)(2,1)S(1)}, u32[]{:S(2)}, u32[]{:S(2)}) collective-permute-start(bf16[128,128]{1,0:T(8,128)(2,1)} %get-tuple-element.31), channel_id=1, source_target_pairs={{0,2},{1,3},{2,0},{3,1},{4,6},{5,7},{6,4},{7,5},{8,10},{9,11},{10,... | collective-permute-start | bytes 98312 | tf_op jit(solution)/shard_map/ppermute | solution.py:479
  55.6 0.5 collective-permute-start.5
  56.1 1.4 %collective-permute-done.3.got1 = bf16[128,128]{1,0:T(8,128)(2,1)S(1)} collective-permute-done((bf16[128,128]{1,0:T(8,128)(2,1)}, bf16[128,128]{1,0:T(8,128)(2,1)S(1)}, u32[]{:S(2)}, u32[]{:S(2)}) %collective-permute-start.3) | collective-permute-done | bytes 32800 | tf_op jit(solution)/shard_map/ppermute | solution.py:479
  57.5 0.8 %collective-permute-done.4.got2 = bf16[128,128]{1,0:T(8,128)(2,1)S(1)} collective-permute-done((bf16[128,128]{1,0:T(8,128)(2,1)}, bf16[128,128]{1,0:T(8,128)(2,1)S(1)}, u32[]{:S(2)}, u32[]{:S(2)}) %collective-permute-start.4) | collective-permute-done | bytes 32800 | tf_op jit(solution)/shard_map/ppermute | solution.py:479
  58.3 0.0 collective-permute-done.5.got3
  58.3 0.8 copy-done.4
  59.1 0.5 plane_total.1
  59.6 2.2 %collective-permute-start.6 = (bf16[128,128]{1,0:T(8,128)(2,1)S(1)}, bf16[128,128]{1,0:T(8,128)(2,1)S(1)}, u32[]{:S(2)}, u32[]{:S(2)}) collective-permute-start(bf16[128,128]{1,0:T(8,128)(2,1)S(1)} %plane_total.1), channel_id=1, source_target_pairs={{0,4},{1,5},{2,6},{3,7},{4,8},{5,9},{6,10},{7,11},{8,12},{9,13},{1... | collective-permute-start | bytes 98312 | tf_op jit(solution)/shard_map/ppermute | solution.py:491
  61.8 1.3 %collective-permute-start.7 = (bf16[128,128]{1,0:T(8,128)(2,1)S(1)}, bf16[128,128]{1,0:T(8,128)(2,1)S(1)}, u32[]{:S(2)}, u32[]{:S(2)}) collective-permute-start(bf16[128,128]{1,0:T(8,128)(2,1)S(1)} %plane_total.1), channel_id=1, source_target_pairs={{0,8},{1,9},{2,10},{3,11},{4,12},{5,13},{6,14},{7,15},{16,24},{17,... | collective-permute-start | bytes 98312 | tf_op jit(solution)/shard_map/ppermute | solution.py:491
  63.1 1.3 %collective-permute-start.8 = (bf16[128,128]{1,0:T(8,128)(2,1)S(1)}, bf16[128,128]{1,0:T(8,128)(2,1)S(1)}, u32[]{:S(2)}, u32[]{:S(2)}) collective-permute-start(bf16[128,128]{1,0:T(8,128)(2,1)S(1)} %plane_total.1), channel_id=1, source_target_pairs={{0,12},{1,13},{2,14},{3,15},{16,28},{17,29},{18,30},{19,31}} | collective-permute-start | bytes 98312 | tf_op jit(solution)/shard_map/ppermute | solution.py:491
  64.4 0.0 copy-start
  64.4 5.5 %image.1.refs_7_ = f32[2,1024,128]{2,1,0:T(8,128)} custom-call(bf16[2,1024,1024]{2,1,0:T(8,128)(2,1)} %bitcast.13, bf16[2,1024,128]{2,1,0:T(8,128)(2,1)} %get-tuple-element.36.right), custom_call_target="tpu_custom_call" | custom-call | flops 536870912 | bytes 4194304 | tf_op jit(solution)/shard_map/image/pallas_call | solution.py:242
  69.9 0.4 plane_local.1.refs_6_
  70.4 0.0 collective-permute-done.10.refs_4_
  70.4 0.0 collective-permute-done.9.refs_3_
  70.4 0.0 collective-permute-done.6.refs_0_
  70.4 0.0 collective-permute-done.7.refs_1_
  70.4 0.0 collective-permute-done.8.refs_2_
  70.5 1.2 %copy-done.1 = f32[2,1024,128]{2,1,0:T(8,128)S(1)} copy-done((f32[2,1024,128]{2,1,0:T(8,128)S(1)}, f32[2,1024,128]{2,1,0:T(8,128)}, u32[]{:S(2)}) %copy-start.1) | copy-done | bytes 1048600
  71.7 1.1 %entering.1 = (bf16[128,128]{1,0:T(8,128)(2,1)S(1)}, bf16[128,128]{1,0:T(8,128)(2,1)S(1)}, bf16[128,128]{1,0:T(8,128)(2,1)S(1)}, bf16[128,128]{1,0:T(8,128)(2,1)S(1)}) custom-call(bf16[128,128]{1,0:T(8,128)(2,1)S(1)} %collective-permute-done.6.refs_0_, bf16[128,128]{1,0:T(8,128)(2,1)S(1)} %collective-permute-done.7.refs_1_, ...), custom_call_target="tpu_custom_call" | custom-call | flops 150994944 | bytes 1179648 | tf_op jit(solution)/shard_map/entering/pallas_call | solution.py:434
  72.8 0.5 collective-permute-start.11
  73.3 1.0 %collective-permute-start.12 = (bf16[128,128]{1,0:T(8,128)(2,1)S(1)}, bf16[128,128]{1,0:T(8,128)(2,1)S(1)}, u32[]{:S(2)}, u32[]{:S(2)}) collective-permute-start(bf16[128,128]{1,0:T(8,128)(2,1)S(1)} %get-tuple-element.39), channel_id=1, source_target_pairs={{0,2},{1,3},{2,0},{3,1},{4,6},{5,7},{6,4},{7,5},{8,10},{9,11},{10,... | collective-permute-start | bytes 98312 | tf_op jit(solution)/shard_map/ppermute | solution.py:479
  74.3 1.4 %collective-permute-start.13 = (bf16[128,128]{1,0:T(8,128)(2,1)S(1)}, bf16[128,128]{1,0:T(8,128)(2,1)S(1)}, u32[]{:S(2)}, u32[]{:S(2)}) collective-permute-start(bf16[128,128]{1,0:T(8,128)(2,1)S(1)} %get-tuple-element.40), channel_id=1, source_target_pairs={{0,3},{1,0},{2,1},{3,2},{4,7},{5,4},{6,5},{7,6},{8,11},{9,8},{10,9... | collective-permute-start | bytes 98312 | tf_op jit(solution)/shard_map/ppermute | solution.py:479
  75.7 0.5 collective-permute-done.11.got1
  76.1 1.3 %collective-permute-done.12.got2 = bf16[128,128]{1,0:T(8,128)(2,1)S(1)} collective-permute-done((bf16[128,128]{1,0:T(8,128)(2,1)S(1)}, bf16[128,128]{1,0:T(8,128)(2,1)S(1)}, u32[]{:S(2)}, u32[]{:S(2)}) %collective-permute-start.12) | collective-permute-done | bytes 32800 | tf_op jit(solution)/shard_map/ppermute | solution.py:479
  77.4 0.0 collective-permute-done.13.got3
  77.5 0.0 copy-done
  77.5 1.3 %waves.1 = bf16[2,1024,128]{2,1,0:T(8,128)(2,1)} custom-call(bf16[128,128]{1,0:T(8,128)(2,1)S(1)} %get-tuple-element.37.own, bf16[128,128]{1,0:T(8,128)(2,1)S(1)} %collective-permute-done.11.got1, bf16[128,128]{1,0:T(8,128)(2,1)S(1)} %collective-permute-done.12.got2, bf16[128,128]{1,0:T(8,128)(2,1)S(1)} %collective-permute-done.13.got3, ...), custom_call_target="tpu_custom_call" | custom-call | flops 134217728 | bytes 2621440 | tf_op jit(solution)/shard_map/waves/pallas_call | solution.py:459
  (8 shorter events, 0.0 us)
Async XLA Ops:
  5.5 43.6 %all-to-all-start = ((bf16[16,144,128]{2,1,0:T(8,128)(2,1)}), bf16[16,144,128]{2,1,0:T(8,128)(2,1)S(1)}, u32[]{:S(2)}, u32[]{:S(2)}) async-start(bf16[16,144,128]{2,1,0:T(8,128)(2,1)} %pairs.1), calls=%async_computation | async-start | bytes 1179648 | tf_op jit(solution)/shard_map/all_to_all | solution.py:512
  16.0 10.3 %collective-permute-start = (f32[256,256]{1,0:T(8,128)}, f32[256,256]{1,0:T(8,128)S(1)}, u32[]{:S(2)}, u32[]{:S(2)}) collective-permute-start(f32[256,256]{1,0:T(8,128)} %get-tuple-element.25), channel_id=1, source_target_pairs={{0,1},{1,2},{2,3},{3,0},{4,5},{5,6},{6,7},{7,4},{8,9},{9,10},{10,1... | collective-permute-start | bytes 786440 | tf_op jit(solution)/shard_map/ppermute | solution.py:479
  16.5 12.4 %collective-permute-start.1 = (f32[256,256]{1,0:T(8,128)}, f32[256,256]{1,0:T(8,128)S(1)}, u32[]{:S(2)}, u32[]{:S(2)}) collective-permute-start(f32[256,256]{1,0:T(8,128)} %get-tuple-element.26), channel_id=1, source_target_pairs={{0,2},{1,3},{2,0},{3,1},{4,6},{5,7},{6,4},{7,5},{8,10},{9,11},{10,... | collective-permute-start | bytes 786440 | tf_op jit(solution)/shard_map/ppermute | solution.py:479
  18.2 15.2 %collective-permute-start.2 = (f32[256,256]{1,0:T(8,128)}, f32[256,256]{1,0:T(8,128)S(1)}, u32[]{:S(2)}, u32[]{:S(2)}) collective-permute-start(f32[256,256]{1,0:T(8,128)} %get-tuple-element.27), channel_id=1, source_target_pairs={{0,3},{1,0},{2,1},{3,2},{4,7},{5,4},{6,5},{7,6},{8,11},{9,8},{10,9... | collective-permute-start | bytes 786440 | tf_op jit(solution)/shard_map/ppermute | solution.py:479
  33.4 0.9 %copy-start.6 = (f32[256,256]{1,0:T(8,128)S(1)}, f32[256,256]{1,0:T(8,128)}, u32[]{:S(2)}) copy-start(f32[256,256]{1,0:T(8,128)} %get-tuple-element.24.own) | copy-start | bytes 786436
  35.5 13.6 %copy-start.3 = (bf16[256,256]{1,0:T(8,128)(2,1)}, bf16[256,256]{1,0:T(8,128)(2,1)S(1)}, u32[]{:S(2)}) copy-start(bf16[256,256]{1,0:T(8,128)(2,1)S(1)} %get-tuple-element.28._map) | copy-start | bytes 393220
  35.5 34.9 %collective-permute-start.10 = (bf16[256,256]{1,0:T(8,128)(2,1)S(1)}, bf16[256,256]{1,0:T(8,128)(2,1)S(1)}, u32[]{:S(2)}, u32[]{:S(2)}) collective-permute-start(bf16[256,256]{1,0:T(8,128)(2,1)S(1)} %get-tuple-element.28._map), channel_id=1, source_target_pairs={{0,8},{1,9},{2,10},{3,11},{4,12},{5,13},{6,14},{7,15},{16,24},{17,... | collective-permute-start | bytes 393224 | tf_op jit(solution)/shard_map/ppermute | solution.py:490
  39.8 30.6 %collective-permute-start.9 = (bf16[256,256]{1,0:T(8,128)(2,1)S(1)}, bf16[256,256]{1,0:T(8,128)(2,1)S(1)}, u32[]{:S(2)}, u32[]{:S(2)}) collective-permute-start(bf16[256,256]{1,0:T(8,128)(2,1)S(1)} %get-tuple-element.28._map), channel_id=1, source_target_pairs={{0,4},{1,5},{2,6},{3,7},{4,8},{5,9},{6,10},{7,11},{8,12},{9,13},{1... | collective-permute-start | bytes 393224 | tf_op jit(solution)/shard_map/ppermute | solution.py:490
  49.1 0.8 %copy-start.7 = (bf16[16,144,128]{2,1,0:T(8,128)(2,1)}, bf16[16,144,128]{2,1,0:T(8,128)(2,1)S(1)}, u32[]{:S(2)}) copy-start(bf16[16,144,128]{2,1,0:T(8,128)(2,1)S(1)} %all-to-all-done.received) | copy-start | bytes 1769476
  53.9 3.6 %collective-permute-start.3 = (bf16[128,128]{1,0:T(8,128)(2,1)}, bf16[128,128]{1,0:T(8,128)(2,1)S(1)}, u32[]{:S(2)}, u32[]{:S(2)}) collective-permute-start(bf16[128,128]{1,0:T(8,128)(2,1)} %get-tuple-element.30), channel_id=1, source_target_pairs={{0,1},{1,2},{2,3},{3,0},{4,5},{5,6},{6,7},{7,4},{8,9},{9,10},{10,1... | collective-permute-start | bytes 98312 | tf_op jit(solution)/shard_map/ppermute | solution.py:479
  54.2 4.1 %collective-permute-start.4 = (bf16[128,128]{1,0:T(8,128)(2,1)}, bf16[128,128]{1,0:T(8,128)(2,1)S(1)}, u32[]{:S(2)}, u32[]{:S(2)}) collective-permute-start(bf16[128,128]{1,0:T(8,128)(2,1)} %get-tuple-element.31), channel_id=1, source_target_pairs={{0,2},{1,3},{2,0},{3,1},{4,6},{5,7},{6,4},{7,5},{8,10},{9,11},{10,... | collective-permute-start | bytes 98312 | tf_op jit(solution)/shard_map/ppermute | solution.py:479
  55.6 2.8 %collective-permute-start.5 = (bf16[128,128]{1,0:T(8,128)(2,1)}, bf16[128,128]{1,0:T(8,128)(2,1)S(1)}, u32[]{:S(2)}, u32[]{:S(2)}) collective-permute-start(bf16[128,128]{1,0:T(8,128)(2,1)} %get-tuple-element.32), channel_id=1, source_target_pairs={{0,3},{1,0},{2,1},{3,2},{4,7},{5,4},{6,5},{7,6},{8,11},{9,8},{10,9... | collective-permute-start | bytes 98312 | tf_op jit(solution)/shard_map/ppermute | solution.py:479
  58.3 0.8 copy-start.4
  59.1 10.8 %copy-start.5 = (bf16[128,128]{1,0:T(8,128)(2,1)S(1)}, bf16[128,128]{1,0:T(8,128)(2,1)}, u32[]{:S(2)}) copy-start(bf16[128,128]{1,0:T(8,128)(2,1)} %get-tuple-element.29.own) | copy-start | bytes 98308
  59.6 10.8 %collective-permute-start.6 = (bf16[128,128]{1,0:T(8,128)(2,1)S(1)}, bf16[128,128]{1,0:T(8,128)(2,1)S(1)}, u32[]{:S(2)}, u32[]{:S(2)}) collective-permute-start(bf16[128,128]{1,0:T(8,128)(2,1)S(1)} %plane_total.1), channel_id=1, source_target_pairs={{0,4},{1,5},{2,6},{3,7},{4,8},{5,9},{6,10},{7,11},{8,12},{9,13},{1... | collective-permute-start | bytes 98312 | tf_op jit(solution)/shard_map/ppermute | solution.py:491
  61.8 8.6 %collective-permute-start.7 = (bf16[128,128]{1,0:T(8,128)(2,1)S(1)}, bf16[128,128]{1,0:T(8,128)(2,1)S(1)}, u32[]{:S(2)}, u32[]{:S(2)}) collective-permute-start(bf16[128,128]{1,0:T(8,128)(2,1)S(1)} %plane_total.1), channel_id=1, source_target_pairs={{0,8},{1,9},{2,10},{3,11},{4,12},{5,13},{6,14},{7,15},{16,24},{17,... | collective-permute-start | bytes 98312 | tf_op jit(solution)/shard_map/ppermute | solution.py:491
  63.1 7.3 %collective-permute-start.8 = (bf16[128,128]{1,0:T(8,128)(2,1)S(1)}, bf16[128,128]{1,0:T(8,128)(2,1)S(1)}, u32[]{:S(2)}, u32[]{:S(2)}) collective-permute-start(bf16[128,128]{1,0:T(8,128)(2,1)S(1)} %plane_total.1), channel_id=1, source_target_pairs={{0,12},{1,13},{2,14},{3,15},{16,28},{17,29},{18,30},{19,31}} | collective-permute-start | bytes 98312 | tf_op jit(solution)/shard_map/ppermute | solution.py:491
  64.4 13.0 %copy-start = (bf16[2,1024,256]{2,1,0:T(8,128)(2,1)S(1)}, bf16[2,1024,256]{2,1,0:T(8,128)(2,1)}, u32[]{:S(2)}) copy-start(bf16[2,1024,256]{2,1,0:T(8,128)(2,1)} %prop.1._prop) | copy-start | bytes 3145732
  69.9 7.5 %copy-start.2 = (f32[2,1024,128]{2,1,0:T(8,128)S(1)}, f32[2,1024,128]{2,1,0:T(8,128)}, u32[]{:S(2)}) copy-start(f32[2,1024,128]{2,1,0:T(8,128)} %image.1.refs_7_) | copy-start | bytes 3145732
  70.4 1.2 %copy-start.1 = (f32[2,1024,128]{2,1,0:T(8,128)S(1)}, f32[2,1024,128]{2,1,0:T(8,128)}, u32[]{:S(2)}) copy-start(f32[2,1024,128]{2,1,0:T(8,128)} %image.1.refs_7_) | copy-start | bytes 3145732
  72.8 3.4 %collective-permute-start.11 = (bf16[128,128]{1,0:T(8,128)(2,1)S(1)}, bf16[128,128]{1,0:T(8,128)(2,1)S(1)}, u32[]{:S(2)}, u32[]{:S(2)}) collective-permute-start(bf16[128,128]{1,0:T(8,128)(2,1)S(1)} %get-tuple-element.38), channel_id=1, source_target_pairs={{0,1},{1,2},{2,3},{3,0},{4,5},{5,6},{6,7},{7,4},{8,9},{9,10},{10,1... | collective-permute-start | bytes 98312 | tf_op jit(solution)/shard_map/ppermute | solution.py:479
  73.3 4.2 %collective-permute-start.12 = (bf16[128,128]{1,0:T(8,128)(2,1)S(1)}, bf16[128,128]{1,0:T(8,128)(2,1)S(1)}, u32[]{:S(2)}, u32[]{:S(2)}) collective-permute-start(bf16[128,128]{1,0:T(8,128)(2,1)S(1)} %get-tuple-element.39), channel_id=1, source_target_pairs={{0,2},{1,3},{2,0},{3,1},{4,6},{5,7},{6,4},{7,5},{8,10},{9,11},{10,... | collective-permute-start | bytes 98312 | tf_op jit(solution)/shard_map/ppermute | solution.py:479
  74.3 3.2 %collective-permute-start.13 = (bf16[128,128]{1,0:T(8,128)(2,1)S(1)}, bf16[128,128]{1,0:T(8,128)(2,1)S(1)}, u32[]{:S(2)}, u32[]{:S(2)}) collective-permute-start(bf16[128,128]{1,0:T(8,128)(2,1)S(1)} %get-tuple-element.40), channel_id=1, source_target_pairs={{0,3},{1,0},{2,1},{3,2},{4,7},{5,4},{6,5},{7,6},{8,11},{9,8},{10,9... | collective-permute-start | bytes 98312 | tf_op jit(solution)/shard_map/ppermute | solution.py:479

commit v4 on v3

v4 whole, which is shorter than its diff:
```python
import functools

import jax
import jax.numpy as jnp
from jax import lax
from jax.experimental import pallas as pl
from jax.experimental.pallas import tpu as pltpu
from jax.sharding import PartitionSpec as P

BLK = 32
CAP = 2
GROUP = 4
HEAD = 16
CORES = 2

HIGH = lax.Precision.HIGHEST
F32 = jnp.float32
BF16 = jnp.bfloat16
VMEM_BYTES = 16 * 1024 * 1024

IN_VMEM = pl.BlockSpec(memory_space=pltpu.VMEM)
IN_SMEM = pl.BlockSpec(memory_space=pltpu.SMEM)
IN_PLACE = pl.BlockSpec(memory_space=pl.ANY)


def shape(*dims, dtype=BF16):
    return jax.ShapeDtypeStruct(dims, dtype)


def call(body, name, ins, outs, scratch, flops, moved):
    return pl.pallas_call(
        body,
        name=name,
        in_specs=ins,
        out_shape=outs,
        out_specs=jax.tree.map(lambda _: IN_VMEM, outs),
        scratch_shapes=scratch,
        compiler_params=pltpu.CompilerParams(vmem_limit_bytes=VMEM_BYTES),
        cost_estimate=pl.CostEstimate(flops=flops, bytes_accessed=moved, transcendentals=0),
    )


def place():
    return lax.axis_index("sec") % GROUP


def dot(a, b):
    return jnp.dot(a, b, preferred_element_type=F32)


def dot_wide(a, b):
    return jnp.dot(a, b, precision=HIGH, preferred_element_type=F32)


def two_parts(x):
    high = x.astype(BF16)
    return high, (x - high.astype(F32)).astype(BF16)


def left_lanes(x):
    return lax.broadcasted_iota(jnp.int32, x.shape, 1) < x.shape[1] // 2


def swap_lanes(x):
    return pltpu.roll(x, x.shape[1] // 2, 1)


def pack(tall):
    half = tall.shape[0] // 2
    top, low = tall[:half], tall[half:]
    return jnp.where(left_lanes(top), top, swap_lanes(low))


def unpack(packed):
    return jnp.concatenate([packed, swap_lanes(packed)], axis=0)


def pairs_kernel(owner, blocks, green, inject, out, full, slot_of, counts):
    energies = green.shape[0]
    sections = out.shape[0]
    count = owner.shape[0]
    rows = CAP * energies * BLK
    lane = lax.broadcasted_iota(jnp.int32, (HEAD, out.shape[2]), 1)
    none = jnp.where(lane < CAP, -1.0, 0.0).astype(BF16)

    def blank(d, _):
        counts[d] = 0
        out[d, :rows, :] = jnp.zeros((rows, out.shape[2]), BF16)
        out[d, rows : rows + HEAD, :] = none
        return 0

    lax.fori_loop(0, sections, blank, 0)

    def rank(q, _):
        d = owner[q]
        r = counts[d]
        counts[d] = r + 1
        slot_of[q] = r
        head = out[d, rows : rows + HEAD, :].astype(F32)
        head = jnp.where(lane == r, blocks[1, q].astype(F32), head)
        out[d, rows : rows + HEAD, :] = head.astype(BF16)
        return 0

    lax.fori_loop(0, count, rank, 0)
    for e in range(energies):
        full[e] = dot(green[e], inject[e]).astype(BF16)

    def fill(q, _):
        d, r = owner[q], slot_of[q]
        first = pl.multiple_of(blocks[0, q] * BLK, BLK)
        for e in range(energies):
            to = pl.multiple_of((r * energies + e) * BLK, BLK)
            out[d, pl.ds(to, BLK), :] = full[e, pl.ds(first, BLK), :]
        return 0

    lax.fori_loop(0, count, fill, 0, unroll=4)


def outgoing_pairs(owner, blocks, green, inject, sections):
    energies, orbitals, _ = green.shape
    columns = inject.shape[2]
    return call(
        pairs_kernel,
        "pairs",
        [IN_SMEM, IN_SMEM, IN_VMEM, IN_VMEM],
        shape(sections, CAP * energies * BLK + HEAD, columns),
        [
            pltpu.VMEM(inject.shape, BF16),
            pltpu.SMEM(owner.shape, jnp.int32),
            pltpu.SMEM((sections,), jnp.int32),
        ],
        2 * energies * orbitals * orbitals * columns,
        2 * green.size,
    )(owner, blocks, green, inject)


def maps_kernel(pattern, green, coupling, couple, own, other, maps):
    energies, orbitals, _ = green.shape
    face = coupling.shape[1]
    high, wide = orbitals // pattern.shape[1], face // pattern.shape[0]
    for i in range(pattern.shape[1]):
        for j in range(pattern.shape[0]):
            at = (slice(i * high, (i + 1) * high), slice(j * wide, (j + 1) * wide))
            tile = coupling[at]
            couple[at] = jnp.where(pattern[j, i] == 1, tile, jnp.zeros_like(tile))
    for e in range(energies):
        maps[e] = dot(green[e, orbitals - face :, :], couple[...])
    mine = place() // CORES
    own[...] = maps[mine]
    other[...] = maps[1 - mine]


def face_maps(pattern, green, coupling):
    energies, orbitals, _ = green.shape
    face = coupling.shape[1]
    square = shape(face, face, dtype=F32)
    return call(
        maps_kernel,
        "face_maps",
        [IN_SMEM, IN_VMEM, IN_VMEM],
        [shape(orbitals, face), square, square],
        [pltpu.VMEM((energies, face, face), F32)],
        2 * energies * face * orbitals * face,
        2 * energies * face * orbitals,
    )(pattern, green, coupling)


def product_kernel(green, right, out):
    for e in range(green.shape[0]):
        factor = right[e] if len(right.shape) == 3 else right[...]
        out[e] = dot(green[e], factor).astype(out.dtype)


def product(green, right, dtype, name):
    energies, orbitals, _ = green.shape
    wide = right.shape[-1]
    return call(
        product_kernel,
        name,
        [IN_VMEM, IN_VMEM],
        shape(energies, orbitals, wide, dtype=dtype),
        [],
        2 * energies * orbitals * orbitals * wide,
        2 * green.size,
    )(green, right)


def chain_kernel(own, near, across, far, _prop, total_out, after_out, within_out, upto_out, maps):
    here = place()
    opposite = (here + CORES) % GROUP
    for j, ref in ((here, own), (here ^ 1, near), (opposite, across), (opposite ^ 1, far)):
        maps[j] = ref[...]
    first, second, third, fourth = (two_parts(maps[j]) for j in range(GROUP))
    face = own.shape[0]

    def times(a, b):
        return dot(a[0], b[0]) + (dot(a[0], b[1]) + dot(a[1], b[0]))

    upto2 = two_parts(times(second, first))
    upto3 = two_parts(times(third, upto2))
    after1 = two_parts(times(fourth, third))
    after0 = two_parts(times(after1, second))
    total_out[...] = times(fourth, upto3).astype(total_out.dtype)
    for out, items in (
        (after_out, (after0, after1, fourth)),
        (within_out, (second, third, two_parts(times(third, second)))),
        (upto_out, (first, upto2, upto3)),
    ):
        for j, (high, low) in enumerate(items):
            out[0, j * face : (j + 1) * face, :] = high
            out[1, j * face : (j + 1) * face, :] = low


def chain(maps, total_dtype, ready):
    face = maps[0].shape[0]
    stack = shape(2, (GROUP - 1) * face, face)
    return call(
        chain_kernel,
        "chain_maps",
        [IN_VMEM] * GROUP + [IN_PLACE],
        [shape(face, face, dtype=total_dtype), stack, stack, stack],
        [pltpu.VMEM((GROUP, face, face), F32)],
        2 * 6 * 3 * face**3,
        4 * 10 * face * face,
    )(*maps, ready)


def source_kernel(received, inject, green, _map, source, quarters, total, heads, targets, sem):
    energies, orbitals, columns = inject.shape
    sections = received.shape[0]
    half = quarters.shape[1]
    rows = CAP * energies * BLK

    def read(s, _):
        block = received[s, rows : rows + HEAD, :].astype(F32)
        heads[pl.ds(s, 1), :] = block[:1].astype(jnp.int32)
        return 0

    lax.fori_loop(0, sections, read, 0, unroll=min(sections, 8))
    fetch = pltpu.make_async_copy(heads, targets, sem)
    fetch.start()
    total[...] = inject[...].astype(F32)
    fetch.wait()

    def add(s, _):
        for r in range(CAP):
            first = pl.multiple_of(jnp.maximum(targets[s, r], 0) * BLK, BLK)
            for e in range(energies):
                item = received[s, (r * energies + e) * BLK : (r * energies + e + 1) * BLK, :]
                total[e, pl.ds(first, BLK), :] += item.astype(F32)
        return 0

    lax.fori_loop(0, sections, add, 0, unroll=2)
    split = GROUP // energies
    for e in range(energies):
        source[e] = total[e].astype(BF16)
        tall = dot(green[e, orbitals - 2 * half :, :], source[e])
        quarters[e * split] = pack(tall).astype(BF16)
        second = jnp.where(left_lanes(tall[:half]), swap_lanes(tall[:half]), tall[half:])
        quarters[e * split + 1] = second.astype(BF16)


def placed_source(received, inject, green, face, ready):
    energies, orbitals, columns = inject.shape
    sections = received.shape[0]
    return call(
        source_kernel,
        "source_and_face",
        [IN_VMEM, IN_VMEM, IN_VMEM, IN_PLACE],
        [shape(*inject.shape), shape(GROUP, face // 2, columns)],
        [
            pltpu.VMEM(inject.shape, F32),
            pltpu.VMEM((sections, columns), jnp.int32),
            pltpu.SMEM((sections, columns), jnp.int32),
            pltpu.SemaphoreType.DMA,
        ],
        2 * energies * face * orbitals * columns,
        2 * energies * face * orbitals + 2 * received.size,
    )(received, inject, green, ready)


def apply(parts, j, x):
    face = x.shape[0]
    at = slice(j * face, (j + 1) * face)
    return dot(parts[0, at, :], x) + dot(parts[1, at, :], x)


def total_kernel(shifts, after, out):
    total = unpack(shifts[GROUP - 1].astype(F32))
    for j in range(GROUP - 1):
        total = total + apply(after, j, unpack(shifts[j].astype(F32)).astype(BF16))
    packed = pack(total).astype(BF16)
    for k in range(out.shape[0]):
        out[k] = packed


def plane_total(shifts, after, times):
    _, half, columns = shifts.shape
    return call(
        total_kernel,
        "plane_total",
        [IN_VMEM] * 2,
        shape(times, half, columns),
        [],
        2 * after.size * columns,
        2 * after.size,
    )(shifts, after)


def local_kernel(shifts, within, out):
    face = out.shape[0] // (GROUP - 1)
    first, second, third = (unpack(shifts[j].astype(F32)) for j in range(GROUP - 1))
    out[0:face] = first
    out[face : 2 * face] = second + apply(within, 0, first.astype(BF16))
    out[2 * face :] = third + apply(within, 1, second.astype(BF16)) + apply(within, 2, first.astype(BF16))


def plane_local(shifts, within):
    _, half, columns = shifts.shape
    return call(
        local_kernel,
        "plane_local",
        [IN_VMEM] * 2,
        shape((GROUP - 1) * 2 * half, columns, dtype=F32),
        [],
        2 * within.size * columns,
        2 * within.size,
    )(shifts, within)


def entering_kernel(below, *refs):
    maps, (upto, local, _image, out) = refs[:-4], refs[-4:]
    planes = below.shape[0]
    plane = lax.axis_index("sec") // GROUP

    def total_of(k):
        if planes == 1:
            return unpack(below[0].astype(F32))
        item = below[jnp.maximum(plane - k, 0)].astype(F32)
        return unpack(jnp.where(plane >= k, item, 0.0))

    base = total_of(planes - 1)
    for k in range(planes - 2, 0, -1):
        high, low = two_parts(base)
        base = total_of(k) + dot(maps[k - 1][...], high) + dot(maps[k - 1][...], low)
    high, low = two_parts(base)
    face = base.shape[0]
    out[0] = pack(base).astype(BF16)
    for j in range(1, GROUP):
        at = slice((j - 1) * face, j * face)
        state = local[at, :] + dot(upto[0, at, :], high) + dot(upto[0, at, :], low) + dot(upto[1, at, :], high)
        out[j] = pack(state).astype(BF16)


def entering(below, maps, upto, local, ready):
    _, half, columns = below.shape
    return call(
        entering_kernel,
        "entering",
        [IN_VMEM] * (3 + len(maps)) + [IN_PLACE],
        shape(GROUP, half, columns),
        [],
        3 * upto.size * columns,
        2 * upto.size + 4 * local.size,
    )(below, *maps, upto, local, ready)


def waves_kernel(arrived, prop, image, out):
    split = GROUP // prop.shape[0]
    for e in range(prop.shape[0]):
        near, far = arrived[e * split].astype(F32), arrived[e * split + 1].astype(F32)
        left = left_lanes(near)
        top = jnp.where(left, near, swap_lanes(far))
        low = jnp.where(left, swap_lanes(near), far)
        incoming = jnp.concatenate([top, low], axis=0).astype(BF16)
        out[e] = (dot(prop[e], incoming) + image[e]).astype(BF16)


def final_waves(arrived, prop, image):
    return call(
        waves_kernel,
        "waves",
        [IN_VMEM] * 3,
        shape(*image.shape),
        [],
        2 * prop.size * arrived.shape[2],
        2 * prop.size + 6 * image.size,
    )(arrived, prop, image)


def in_plane(sections, move):
    return [(s, s // GROUP * GROUP + move(s % GROUP)) for s in range(sections)]


def exchange(items, groups):
    return lax.all_to_all(items, "sec", split_axis=0, concat_axis=0, axis_index_groups=groups, tiled=True)


def plane_groups(sections):
    return [[p * GROUP + i for i in range(GROUP)] for p in range(sections // GROUP)]


def upward_groups(sections):
    return [list(range(i, sections, GROUP)) for i in range(GROUP)]


def up_shift(sections, k):
    return [(s, s + GROUP * k) for s in range(sections - GROUP * k)]


def spread(packed):
    half = packed.shape[1] // 2
    return jnp.concatenate([packed[:, :half], packed[:, half:]], axis=0)


def scan_below(total_map, total, sections):
    planes = sections // GROUP
    shift = lax.ppermute(spread(total).astype(F32), "sec", up_shift(sections, 1))
    joined = lax.ppermute(total_map, "sec", up_shift(sections, 1))
    stride = 1
    while stride < planes:
        other = lax.ppermute(shift, "sec", up_shift(sections, stride))
        other_map = lax.ppermute(joined, "sec", up_shift(sections, stride))
        shift = shift + dot_wide(joined, other)
        joined = dot_wide(joined, other_map)
        stride *= 2
    half = shift.shape[0] // 2
    return jnp.concatenate([shift[:half], shift[half:]], axis=1)[None]


def per_device(green, injected, coupling, pattern, owner, pair_blocks):
    sections = lax.axis_size("sec")
    green, inject = green[0], injected[0]
    face = coupling.shape[2]

    outgoing = outgoing_pairs(owner[:, 0], pair_blocks.T, green, inject, sections)
    received = lax.all_to_all(outgoing, "sec", split_axis=0, concat_axis=0, tiled=True)

    couple, own_map, other_map = face_maps(pattern[0].T, green, coupling[0])
    across = lax.ppermute(other_map, "sec", in_plane(sections, lambda i: (i + CORES) % GROUP))
    near = lax.ppermute(own_map, "sec", in_plane(sections, lambda i: i ^ 1))
    prop = product(green, couple, BF16, "prop")
    far = lax.ppermute(across, "sec", in_plane(sections, lambda i: i ^ 1))
    planes = sections // GROUP
    few = planes <= 4
    total_map, after, within, upto = chain([own_map, near, across, far], BF16 if few else F32, prop)
    maps = [lax.ppermute(total_map, "sec", up_shift(sections, k)) for k in range(1, planes - 1)] if few else []

    source, quarters = placed_source(received, inject, green, face, total_map)
    shifts = exchange(quarters, plane_groups(sections))
    total = plane_total(shifts, after, planes if few else 1)
    below = exchange(total, upward_groups(sections)) if few else scan_below(total_map, total[0], sections)
    local = plane_local(shifts, within)
    image = product(green, source, F32, "image")
    arrived = exchange(entering(below, maps, upto, local, image), plane_groups(sections))
    return final_waves(arrived, prop, image)[None]


def solution(mesh):
    in_specs = (
        P("sec", "grp", None, None),
        P("sec", "grp", None, None),
        P("sec", None, None),
        P("sec", None, None),
        P("sec", None),
        P("sec", None),
    )
    out_specs = P("sec", "grp", None, None)
    return jax.shard_map(
        per_device, mesh=mesh, in_specs=in_specs, out_specs=out_specs, check_vma=False
    )
```

time: 79.5 us -> 79.9 us (level)
  Pallas kernels: 29.2 us -> 13.6 us
  blocking collectives: 0 us -> 15.3 us
  local copies, waits for them, and re-layouts: 3.77 us -> 19 us
  waiting for transfers between devices: 18 us -> 9.57 us
  starting transfers between devices: 27.6 us -> 21.6 us
    pallas_call x10, Pallas kernels: 29.2 us -> 13.6 us  [the longest x1 2.95 us: outgoing_pairs(): call(pairs_kernel, 'pairs', [IN_SMEM, IN_SMEM, IN_VMEM, IN_VMEM], shape(s...]
    unnamed x16 -> x40, local copies, waits for them, and re-layouts: 3.77 us -> 19 us
    all_to_all x0 -> x2, blocking collectives: none -> 15.3 us  [exchange(): lax.all_to_all(items, 'sec', split_axis=0, concat_axis=0, axis_index_grou...]
    ppermute x14 -> x5, starting transfers between devices: 20.2 us -> 10.2 us  [the longest x2 8.2 us: per_device(): lax.ppermute(total_map, 'sec', up_shift(sections, k))]
    ppermute x14 -> x5, waiting for transfers between devices: 18 us -> 9.57 us  [the longest x1 9.29 us: per_device(): lax.ppermute(other_map, 'sec', in_plane(sections, lambda i: (i + CORES) %...]
    all_to_all x0 -> x1, starting transfers between devices: none -> 4 us  [exchange(): lax.all_to_all(items, 'sec', split_axis=0, concat_axis=0, axis_index_grou...]
  transfers between devices with their start and end apart: 15 -> 7, of which waited for: 7 -> 2; matrix products, arithmetic and copies ran while one was open for 0% -> 0% of each run, Pallas kernels for 27% -> 7%
where the time goes in v4:
time: 79.9 us; the launch traced here: 79.2 us
  starting transfers between devices  21.6 us (27%)
  local copies, waits for them, and re-layouts  19 us (24%)
  blocking collectives  15.3 us (19%)
  Pallas kernels  13.6 us (17%)
  waiting for transfers between devices  9.57 us (12%)
    unnamed x40, local copies, waits for them, and re-layouts  19 us
    all_to_all x2, blocking collectives, exchange(): lax.all_to_all(items, 'sec', split_axis=0, concat_axis=0, axis_index_grou...  15.3 us
    ppermute x1, waiting for transfers between devices, per_device(): lax.ppermute(other_map, 'sec', in_plane(sections, lambda i: (i + CORES) %...  9.29 us
    ppermute x2, starting transfers between devices, per_device(): lax.ppermute(total_map, 'sec', up_shift(sections, k))  8.2 us
    all_to_all x1, starting transfers between devices, per_device(): lax.all_to_all(outgoing, 'sec', split_axis=0, concat_axis=0, tiled=True)  7.37 us
    all_to_all x1, starting transfers between devices, exchange(): lax.all_to_all(items, 'sec', split_axis=0, concat_axis=0, axis_index_grou...  4 us
    pallas_call x1, Pallas kernels, outgoing_pairs(): call(pairs_kernel, 'pairs', [IN_SMEM, IN_SMEM, IN_VMEM, IN_VMEM], shape(s...  2.95 us
    pallas_call x2, Pallas kernels, product(): call(product_kernel, name, [IN_VMEM, IN_VMEM], shape(energies, orbitals,...  2.49 us
  transfers between devices with their start and end apart: 7, of which 2 were waited for; matrix products, arithmetic and copies ran while one was open for 0% of the time, Pallas kernels for 7%

profile of v4, /device:TPU:0, one launch (start us, length us, event | category | flops | bytes accessed | tf_op | source)
XLA Modules:
  0.0 79.2 jit_solution(15524896501418940951)
XLA Ops:
  0.0 2.2 %copy-done = bf16[1,2,1024,1024]{3,2,1,0:T(8,128)(2,1)S(1)} copy-done((bf16[1,2,1024,1024]{3,2,1,0:T(8,128)(2,1)S(1)}, bf16[1,2,1024,1024]{3,2,1,0:T(8,128)(2,1)}, u32[]{:S(2)}) %copy-start) | copy-done | bytes 4194328
  2.2 1.0 %copy-done.4 = bf16[1,2,1024,128]{3,2,1,0:T(8,128)(2,1)S(1)} copy-done((bf16[1,2,1024,128]{3,2,1,0:T(8,128)(2,1)S(1)}, bf16[1,2,1024,128]{3,2,1,0:T(8,128)(2,1)}, u32[]{:S(2)}) %copy-start.4) | copy-done | bytes 524312
  3.2 0.7 copy-done.17
  3.9 0.7 copy-done.19
  4.6 3.0 %pairs.1 = bf16[16,144,128]{2,1,0:T(8,128)(2,1)} custom-call(s32[16]{0:T(128)S(1)} %bitcast.19, s32[2,16]{1,0:T(2,128)S(1)} %bitcast.17, bf16[2,1024,1024]{2,1,0:T(8,128)(2,1)S(1)} %bitcast.9, bf16[2,1024,128]{2,1,0:T(8,128)(2,1)S(1)} %bitcast.14), custom_call_target="tpu_custom_call" | custom-call | flops 536870912 | bytes 4194304 | tf_op jit(solution)/shard_map/pairs/pallas_call | solution.py:122
  7.5 7.4 %all-to-all-start = ((bf16[16,144,128]{2,1,0:T(8,128)(2,1)}), bf16[16,144,128]{2,1,0:T(8,128)(2,1)S(1)}, u32[]{:S(2)}, u32[]{:S(2)}) async-start(bf16[16,144,128]{2,1,0:T(8,128)(2,1)} %pairs.1), calls=%async_computation | async-start | bytes 1179648 | tf_op jit(solution)/shard_map/all_to_all | solution.py:437
  14.9 0.0 copy-start.1
  14.9 2.2 %copy-done.1 = bf16[1,2,1024,1024]{3,2,1,0:T(8,128)(2,1)S(1)} copy-done((bf16[1,2,1024,1024]{3,2,1,0:T(8,128)(2,1)S(1)}, bf16[1,2,1024,1024]{3,2,1,0:T(8,128)(2,1)}, u32[]{:S(2)}) %copy-start.1) | copy-done | bytes 4194328
  17.1 1.1 %face_maps.1 = (bf16[1024,256]{1,0:T(8,128)(2,1)S(1)}, f32[256,256]{1,0:T(8,128)S(1)}, f32[256,256]{1,0:T(8,128)S(1)}) custom-call(s32[2,8]{1,0:T(2,128)S(1)} %bitcast.18, bf16[2,1024,1024]{2,1,0:T(8,128)(2,1)S(1)} %bitcast.10, bf16[1024,256]{1,0:T(8,128)(2,1)S(1)} %bitcast.16), custom_call_target="tpu_custom_call" | custom-call | flops 268435456 | bytes 1048576 | tf_op jit(solution)/shard_map/face_maps/pallas_call | solution.py:157
  18.2 0.0 copy-start.5
  18.2 2.0 %collective-permute-start.1 = (f32[256,256]{1,0:T(8,128)S(1)}, f32[256,256]{1,0:T(8,128)S(1)}, u32[]{:S(2)}, u32[]{:S(2)}) collective-permute-start(f32[256,256]{1,0:T(8,128)S(1)} %get-tuple-element.15), channel_id=1, source_target_pairs={{0,2},{1,3},{2,0},{3,1},{4,6},{5,7},{6,4},{7,5},{8,10},{9,11},{10,... | collective-permute-start | bytes 786440 | tf_op jit(solution)/shard_map/ppermute | solution.py:440
  20.2 0.0 collective-permute-start
  20.2 9.3 %collective-permute-done.1.across = f32[256,256]{1,0:T(8,128)S(1)} collective-permute-done((f32[256,256]{1,0:T(8,128)S(1)}, f32[256,256]{1,0:T(8,128)S(1)}, u32[]{:S(2)}, u32[]{:S(2)}) %collective-permute-start.1) | collective-permute-done | bytes 262176 | tf_op jit(solution)/shard_map/ppermute | solution.py:440
  29.5 0.0 collective-permute-start.2
  29.5 1.2 %prop.1._prop = bf16[2,1024,256]{2,1,0:T(8,128)(2,1)S(1)} custom-call(bf16[2,1024,1024]{2,1,0:T(8,128)(2,1)S(1)} %bitcast.11, bf16[1024,256]{1,0:T(8,128)(2,1)S(1)} %get-tuple-element.16.right), custom_call_target="tpu_custom_call" | custom-call | flops 1073741824 | bytes 4194304 | tf_op jit(solution)/shard_map/prop/pallas_call | solution.py:177
  30.7 0.0 collective-permute-done.near
  30.8 0.3 collective-permute-done.2.far
  31.0 1.7 %chain_maps.1 = (bf16[256,256]{1,0:T(8,128)(2,1)}, bf16[2,768,256]{2,1,0:T(8,128)(2,1)S(1)}, bf16[2,768,256]{2,1,0:T(8,128)(2,1)S(1)}, bf16[2,768,256]{2,1,0:T(8,128)(2,1)S(1)}) custom-call(f32[256,256]{1,0:T(8,128)S(1)} %get-tuple-element.14.own, f32[256,256]{1,0:T(8,128)S(1)} %collective-permute-done.near, f32[256,256]{1,0:T(8,128)S(1)} %collective-permute-done.1.across, ...), custom_call_target="tpu_custom_call" | custom-call | flops 603979776 | bytes 2621440 | tf_op jit(solution)/shard_map/chain_maps/pallas_call | solution.py:217
  32.8 0.9 %copy-done.6 = bf16[2,768,256]{2,1,0:T(8,128)(2,1)} copy-done((bf16[2,768,256]{2,1,0:T(8,128)(2,1)}, bf16[2,768,256]{2,1,0:T(8,128)(2,1)S(1)}, u32[]{:S(2)}) %copy-start.6) | copy-done | bytes 786456
  33.7 0.9 %copy-done.8 = bf16[2,768,256]{2,1,0:T(8,128)(2,1)} copy-done((bf16[2,768,256]{2,1,0:T(8,128)(2,1)}, bf16[2,768,256]{2,1,0:T(8,128)(2,1)S(1)}, u32[]{:S(2)}) %copy-start.8) | copy-done | bytes 786456
  34.6 0.0 all-to-all-done.received
  34.6 0.0 copy-done.5
  34.6 2.2 %copy-done.2 = bf16[1,2,1024,1024]{3,2,1,0:T(8,128)(2,1)S(1)} copy-done((bf16[1,2,1024,1024]{3,2,1,0:T(8,128)(2,1)S(1)}, bf16[1,2,1024,1024]{3,2,1,0:T(8,128)(2,1)}, u32[]{:S(2)}) %copy-start.2) | copy-done | bytes 4194328
  36.8 1.4 %source_and_face.1 = (bf16[2,1024,128]{2,1,0:T(8,128)(2,1)S(1)}, bf16[4,128,128]{2,1,0:T(8,128)(2,1)S(1)}) custom-call(bf16[16,144,128]{2,1,0:T(8,128)(2,1)S(1)} %all-to-all-done.received, bf16[2,1024,128]{2,1,0:T(8,128)(2,1)S(1)} %bitcast.15, bf16[2,1024,1024]{2,1,0:T(8,128)(2,1)S(1)} %bitcast.12, bf16[256,256]{1,0:T(8,128)(2,1)} %get-tuple-element.17._map), custom_call_target="tpu_custom_call" | custom-call | flops 134217728 | bytes 1638400 | tf_op jit(solution)/shard_map/source_and_face/pallas_call | solution.py:266
  38.2 0.0 copy-start.11
  38.2 0.8 copy-done.11
  39.0 8.3 %all_to_all.20.shifts = bf16[4,128,128]{2,1,0:T(8,128)(2,1)S(1)} all-to-all(bf16[4,128,128]{2,1,0:T(8,128)(2,1)S(1)} %get-tuple-element.18), channel_id=1, replica_groups={{0,1,2,3},{4,5,6,7},{8,9,10,11},{12,13,14,15},{16,17,18,19},{20,21,22,2..., dimensions={0} | all-to-all | bytes 262144 | tf_op jit(solution)/shard_map/all_to_all | solution.py:396
  47.2 1.2 %plane_total.1 = bf16[4,128,128]{2,1,0:T(8,128)(2,1)} custom-call(bf16[4,128,128]{2,1,0:T(8,128)(2,1)S(1)} %all_to_all.20.shifts, bf16[2,768,256]{2,1,0:T(8,128)(2,1)S(1)} %copy-done.7), custom_call_target="tpu_custom_call" | custom-call | flops 100663296 | bytes 786432 | tf_op jit(solution)/shard_map/plane_total/pallas_call | solution.py:299
  48.4 4.0 %all-to-all-start.2 = ((bf16[4,128,128]{2,1,0:T(8,128)(2,1)}), bf16[4,128,128]{2,1,0:T(8,128)(2,1)S(1)}, u32[]{:S(2)}, u32[]{:S(2)}) async-start(bf16[4,128,128]{2,1,0:T(8,128)(2,1)} %plane_total.1), calls=%async_computation.2 | async-start | bytes 262144 | tf_op jit(solution)/shard_map/all_to_all | solution.py:396
  52.4 4.8 %collective-permute-start.4 = (bf16[256,256]{1,0:T(8,128)(2,1)}, bf16[256,256]{1,0:T(8,128)(2,1)S(1)}, u32[]{:S(2)}, u32[]{:S(2)}) collective-permute-start(bf16[256,256]{1,0:T(8,128)(2,1)} %get-tuple-element.17._map), channel_id=1, source_target_pairs={{0,8},{1,9},{2,10},{3,11},{4,12},{5,13},{6,14},{7,15},{16,24},{17,... | collective-permute-start | bytes 393224 | tf_op jit(solution)/shard_map/ppermute | solution.py:447
  57.2 3.4 %collective-permute-start.3 = (bf16[256,256]{1,0:T(8,128)(2,1)}, bf16[256,256]{1,0:T(8,128)(2,1)S(1)}, u32[]{:S(2)}, u32[]{:S(2)}) collective-permute-start(bf16[256,256]{1,0:T(8,128)(2,1)} %get-tuple-element.17._map), channel_id=1, source_target_pairs={{0,4},{1,5},{2,6},{3,7},{4,8},{5,9},{6,10},{7,11},{8,12},{9,13},{1... | collective-permute-start | bytes 393224 | tf_op jit(solution)/shard_map/ppermute | solution.py:447
  60.6 0.0 copy-start.3
  60.6 2.2 %copy-done.3 = bf16[1,2,1024,1024]{3,2,1,0:T(8,128)(2,1)S(1)} copy-done((bf16[1,2,1024,1024]{3,2,1,0:T(8,128)(2,1)S(1)}, bf16[1,2,1024,1024]{3,2,1,0:T(8,128)(2,1)}, u32[]{:S(2)}) %copy-start.3) | copy-done | bytes 4194328
  62.8 1.0 %copy-done.12 = bf16[2,1024,128]{2,1,0:T(8,128)(2,1)S(1)} copy-done((bf16[2,1024,128]{2,1,0:T(8,128)(2,1)S(1)}, bf16[2,1024,128]{2,1,0:T(8,128)(2,1)}, u32[]{:S(2)}) %copy-start.12) | copy-done | bytes 524312
  63.8 1.2 %image.1.refs_4_ = f32[2,1024,128]{2,1,0:T(8,128)S(1)} custom-call(bf16[2,1024,1024]{2,1,0:T(8,128)(2,1)S(1)} %bitcast.13, bf16[2,1024,128]{2,1,0:T(8,128)(2,1)S(1)} %copy-done.12), custom_call_target="tpu_custom_call" | custom-call | flops 536870912 | bytes 4194304 | tf_op jit(solution)/shard_map/image/pallas_call | solution.py:177
  65.1 0.4 plane_local.1.refs_3_
  65.5 0.0 collective-permute-done.4.refs_1_
  65.5 0.0 copy-start.13
  65.5 0.6 copy-done.13
  66.2 0.0 collective-permute-done.3.refs_0_
  66.2 0.7 copy-done.15
  66.8 0.0 all-to-all-done.2.below
  66.8 1.1 %copy-done.9 = bf16[2,768,256]{2,1,0:T(8,128)(2,1)S(1)} copy-done((bf16[2,768,256]{2,1,0:T(8,128)(2,1)S(1)}, bf16[2,768,256]{2,1,0:T(8,128)(2,1)}, u32[]{:S(2)}) %copy-start.9) | copy-done | bytes 786456
  68.0 0.9 %copy-done.14 = bf16[256,256]{1,0:T(8,128)(2,1)S(1)} copy-done((bf16[256,256]{1,0:T(8,128)(2,1)S(1)}, bf16[256,256]{1,0:T(8,128)(2,1)}, u32[]{:S(2)}) %copy-start.14) | copy-done | bytes 131096
  68.9 0.9 %copy-done.16 = bf16[256,256]{1,0:T(8,128)(2,1)S(1)} copy-done((bf16[256,256]{1,0:T(8,128)(2,1)S(1)}, bf16[256,256]{1,0:T(8,128)(2,1)}, u32[]{:S(2)}) %copy-start.16) | copy-done | bytes 131096
  69.8 1.1 %entering.1 = bf16[4,128,128]{2,1,0:T(8,128)(2,1)S(1)} custom-call(bf16[4,128,128]{2,1,0:T(8,128)(2,1)S(1)} %all-to-all-done.2.below, bf16[256,256]{1,0:T(8,128)(2,1)S(1)} %copy-done.16, bf16[256,256]{1,0:T(8,128)(2,1)S(1)} %copy-done.14, bf16[2,768,256]{2,1,0:T(8,128)(2,1)S(1)} %copy-done.9, f32[768,128]{1,0:T(8,128)S(1)} %plane_local.1.refs_3_, ...), custom_call_target="tpu_custom_call" | custom-call | flops 150994944 | bytes 1179648 | tf_op jit(solution)/shard_map/entering/pallas_call | solution.py:357
  70.8 7.0 %all_to_all.21.arrived = bf16[4,128,128]{2,1,0:T(8,128)(2,1)S(1)} all-to-all(bf16[4,128,128]{2,1,0:T(8,128)(2,1)S(1)} %entering.1), channel_id=1, replica_groups={{0,1,2,3},{4,5,6,7},{8,9,10,11},{12,13,14,15},{16,17,18,19},{20,21,22,2..., dimensions={0} | all-to-all | bytes 262144 | tf_op jit(solution)/shard_map/all_to_all | solution.py:396
  77.9 1.3 %waves.1 = bf16[2,1024,128]{2,1,0:T(8,128)(2,1)} custom-call(bf16[4,128,128]{2,1,0:T(8,128)(2,1)S(1)} %all_to_all.21.arrived, bf16[2,1024,256]{2,1,0:T(8,128)(2,1)S(1)} %prop.1._prop, f32[2,1024,128]{2,1,0:T(8,128)S(1)} %image.1.refs_4_), custom_call_target="tpu_custom_call" | custom-call | flops 134217728 | bytes 2621440 | tf_op jit(solution)/shard_map/waves/pallas_call | solution.py:380
  (18 shorter events, 0.0 us)
Async XLA Ops:
  0.0 14.9 %copy-start.18 = (s32[1,8,2]{1,2,0:T(2,128)S(1)}, s32[1,8,2]{1,2,0:T(2,128)}, u32[]{:S(2)}) copy-start(s32[1,8,2]{1,2,0:T(2,128)} %param.9) | copy-start | bytes 196
  0.0 2.2 %copy-start = (bf16[1,2,1024,1024]{3,2,1,0:T(8,128)(2,1)S(1)}, bf16[1,2,1024,1024]{3,2,1,0:T(8,128)(2,1)}, u32[]{:S(2)}) copy-start(bf16[1,2,1024,1024]{3,2,1,0:T(8,128)(2,1)} %param.6) | copy-start | bytes 12582916
  2.2 1.0 %copy-start.4 = (bf16[1,2,1024,128]{3,2,1,0:T(8,128)(2,1)S(1)}, bf16[1,2,1024,128]{3,2,1,0:T(8,128)(2,1)}, u32[]{:S(2)}) copy-start(bf16[1,2,1024,128]{3,2,1,0:T(8,128)(2,1)} %param.7) | copy-start | bytes 1572868
  3.2 0.7 copy-start.17
  3.9 0.7 copy-start.19
  4.6 10.3 %copy-start.10 = (bf16[1,1024,256]{2,1,0:T(8,128)(2,1)S(1)}, bf16[1,1024,256]{2,1,0:T(8,128)(2,1)}, u32[]{:S(2)}) copy-start(bf16[1,1024,256]{2,1,0:T(8,128)(2,1)} %param.8) | copy-start | bytes 1572868
  7.5 27.1 %all-to-all-start = ((bf16[16,144,128]{2,1,0:T(8,128)(2,1)}), bf16[16,144,128]{2,1,0:T(8,128)(2,1)S(1)}, u32[]{:S(2)}, u32[]{:S(2)}) async-start(bf16[16,144,128]{2,1,0:T(8,128)(2,1)} %pairs.1), calls=%async_computation | async-start | bytes 1179648 | tf_op jit(solution)/shard_map/all_to_all | solution.py:437
  14.9 2.2 %copy-start.1 = (bf16[1,2,1024,1024]{3,2,1,0:T(8,128)(2,1)S(1)}, bf16[1,2,1024,1024]{3,2,1,0:T(8,128)(2,1)}, u32[]{:S(2)}) copy-start(bf16[1,2,1024,1024]{3,2,1,0:T(8,128)(2,1)} %param.6) | copy-start | bytes 12582916
  18.2 16.4 %copy-start.5 = (bf16[1,2,1024,128]{3,2,1,0:T(8,128)(2,1)S(1)}, bf16[1,2,1024,128]{3,2,1,0:T(8,128)(2,1)}, u32[]{:S(2)}) copy-start(bf16[1,2,1024,128]{3,2,1,0:T(8,128)(2,1)} %param.7) | copy-start | bytes 1572868
  18.2 11.3 %collective-permute-start.1 = (f32[256,256]{1,0:T(8,128)S(1)}, f32[256,256]{1,0:T(8,128)S(1)}, u32[]{:S(2)}, u32[]{:S(2)}) collective-permute-start(f32[256,256]{1,0:T(8,128)S(1)} %get-tuple-element.15), channel_id=1, source_target_pairs={{0,2},{1,3},{2,0},{3,1},{4,6},{5,7},{6,4},{7,5},{8,10},{9,11},{10,... | collective-permute-start | bytes 786440 | tf_op jit(solution)/shard_map/ppermute | solution.py:440
  20.2 10.6 %collective-permute-start = (f32[256,256]{1,0:T(8,128)S(1)}, f32[256,256]{1,0:T(8,128)S(1)}, u32[]{:S(2)}, u32[]{:S(2)}) collective-permute-start(f32[256,256]{1,0:T(8,128)S(1)} %get-tuple-element.14.own), channel_id=1, source_target_pairs={{0,1},{1,0},{2,3},{3,2},{4,5},{5,4},{6,7},{7,6},{8,9},{9,8},{10,11... | collective-permute-start | bytes 786440 | tf_op jit(solution)/shard_map/ppermute | solution.py:441
  29.5 1.5 %collective-permute-start.2 = (f32[256,256]{1,0:T(8,128)S(1)}, f32[256,256]{1,0:T(8,128)S(1)}, u32[]{:S(2)}, u32[]{:S(2)}) collective-permute-start(f32[256,256]{1,0:T(8,128)S(1)} %collective-permute-done.1.across), channel_id=1, source_target_pairs={{0,1},{1,0},{2,3},{3,2},{4,5},{5,4},{6,7},{7,6},{8,9},{9,8},{10,11... | collective-permute-start | bytes 786440 | tf_op jit(solution)/shard_map/ppermute | solution.py:443
  32.8 0.9 %copy-start.6 = (bf16[2,768,256]{2,1,0:T(8,128)(2,1)}, bf16[2,768,256]{2,1,0:T(8,128)(2,1)S(1)}, u32[]{:S(2)}) copy-start(bf16[2,768,256]{2,1,0:T(8,128)(2,1)S(1)} %get-tuple-element.19.after) | copy-start | bytes 2359300
  33.7 0.9 %copy-start.8 = (bf16[2,768,256]{2,1,0:T(8,128)(2,1)}, bf16[2,768,256]{2,1,0:T(8,128)(2,1)S(1)}, u32[]{:S(2)}) copy-start(bf16[2,768,256]{2,1,0:T(8,128)(2,1)S(1)} %get-tuple-element.20.refs_2_) | copy-start | bytes 2359300
  34.6 2.2 %copy-start.2 = (bf16[1,2,1024,1024]{3,2,1,0:T(8,128)(2,1)S(1)}, bf16[1,2,1024,1024]{3,2,1,0:T(8,128)(2,1)}, u32[]{:S(2)}) copy-start(bf16[1,2,1024,1024]{3,2,1,0:T(8,128)(2,1)} %param.6) | copy-start | bytes 12582916
  36.8 10.4 %copy-start.7 = (bf16[2,768,256]{2,1,0:T(8,128)(2,1)S(1)}, bf16[2,768,256]{2,1,0:T(8,128)(2,1)}, u32[]{:S(2)}) copy-start(bf16[2,768,256]{2,1,0:T(8,128)(2,1)} %copy-done.6) | copy-start | bytes 2359300
  38.2 0.8 %copy-start.11 = (bf16[2,1024,128]{2,1,0:T(8,128)(2,1)}, bf16[2,1024,128]{2,1,0:T(8,128)(2,1)S(1)}, u32[]{:S(2)}) copy-start(bf16[2,1024,128]{2,1,0:T(8,128)(2,1)S(1)} %get-tuple-element.22.right) | copy-start | bytes 1572868
  48.4 18.4 %all-to-all-start.2 = ((bf16[4,128,128]{2,1,0:T(8,128)(2,1)}), bf16[4,128,128]{2,1,0:T(8,128)(2,1)S(1)}, u32[]{:S(2)}, u32[]{:S(2)}) async-start(bf16[4,128,128]{2,1,0:T(8,128)(2,1)} %plane_total.1), calls=%async_computation.2 | async-start | bytes 262144 | tf_op jit(solution)/shard_map/all_to_all | solution.py:396
  52.4 13.1 %collective-permute-start.4 = (bf16[256,256]{1,0:T(8,128)(2,1)}, bf16[256,256]{1,0:T(8,128)(2,1)S(1)}, u32[]{:S(2)}, u32[]{:S(2)}) collective-permute-start(bf16[256,256]{1,0:T(8,128)(2,1)} %get-tuple-element.17._map), channel_id=1, source_target_pairs={{0,8},{1,9},{2,10},{3,11},{4,12},{5,13},{6,14},{7,15},{16,24},{17,... | collective-permute-start | bytes 393224 | tf_op jit(solution)/shard_map/ppermute | solution.py:447
  57.2 8.9 %collective-permute-start.3 = (bf16[256,256]{1,0:T(8,128)(2,1)}, bf16[256,256]{1,0:T(8,128)(2,1)S(1)}, u32[]{:S(2)}, u32[]{:S(2)}) collective-permute-start(bf16[256,256]{1,0:T(8,128)(2,1)} %get-tuple-element.17._map), channel_id=1, source_target_pairs={{0,4},{1,5},{2,6},{3,7},{4,8},{5,9},{6,10},{7,11},{8,12},{9,13},{1... | collective-permute-start | bytes 393224 | tf_op jit(solution)/shard_map/ppermute | solution.py:447
  60.6 2.2 %copy-start.3 = (bf16[1,2,1024,1024]{3,2,1,0:T(8,128)(2,1)S(1)}, bf16[1,2,1024,1024]{3,2,1,0:T(8,128)(2,1)}, u32[]{:S(2)}) copy-start(bf16[1,2,1024,1024]{3,2,1,0:T(8,128)(2,1)} %param.6) | copy-start | bytes 12582916
  62.8 1.0 %copy-start.12 = (bf16[2,1024,128]{2,1,0:T(8,128)(2,1)S(1)}, bf16[2,1024,128]{2,1,0:T(8,128)(2,1)}, u32[]{:S(2)}) copy-start(bf16[2,1024,128]{2,1,0:T(8,128)(2,1)} %copy-done.11) | copy-start | bytes 1572868
  65.5 0.6 copy-start.13
  66.2 0.7 copy-start.15
  66.8 1.1 %copy-start.9 = (bf16[2,768,256]{2,1,0:T(8,128)(2,1)S(1)}, bf16[2,768,256]{2,1,0:T(8,128)(2,1)}, u32[]{:S(2)}) copy-start(bf16[2,768,256]{2,1,0:T(8,128)(2,1)} %copy-done.8) | copy-start | bytes 2359300
  68.0 0.9 %copy-start.14 = (bf16[256,256]{1,0:T(8,128)(2,1)S(1)}, bf16[256,256]{1,0:T(8,128)(2,1)}, u32[]{:S(2)}) copy-start(bf16[256,256]{1,0:T(8,128)(2,1)} %copy-done.13) | copy-start | bytes 393220
  68.9 0.9 %copy-start.16 = (bf16[256,256]{1,0:T(8,128)(2,1)S(1)}, bf16[256,256]{1,0:T(8,128)(2,1)}, u32[]{:S(2)}) copy-start(bf16[256,256]{1,0:T(8,128)(2,1)} %copy-done.15) | copy-start | bytes 393220

commit v5 on v3

v5 whole, which is shorter than its diff:
```python
import functools

import jax
import jax.numpy as jnp
from jax import lax
from jax.experimental import pallas as pl
from jax.experimental.pallas import tpu as pltpu
from jax.sharding import PartitionSpec as P

BLK = 32
CAP = 2
GROUP = 4
HEAD = 16
CORES = 2

HIGH = lax.Precision.HIGHEST
F32 = jnp.float32
BF16 = jnp.bfloat16
VMEM_SMALL = 16 * 1024 * 1024
VMEM_WHOLE = 63400000

IN_VMEM = pl.BlockSpec(memory_space=pltpu.VMEM)
IN_SMEM = pl.BlockSpec(memory_space=pltpu.SMEM)
IN_HBM = pl.BlockSpec(memory_space=pltpu.HBM)
IN_PLACE = pl.BlockSpec(memory_space=pl.ANY)


def shape(*dims, dtype=BF16):
    return jax.ShapeDtypeStruct(dims, dtype)


def call(body, name, ins, outs, scratch, flops, moved, vmem=VMEM_SMALL):
    return pl.pallas_call(
        body,
        name=name,
        in_specs=ins,
        out_shape=outs,
        out_specs=jax.tree.map(lambda _: IN_VMEM, outs),
        scratch_shapes=scratch,
        compiler_params=pltpu.CompilerParams(vmem_limit_bytes=vmem),
        cost_estimate=pl.CostEstimate(flops=flops, bytes_accessed=moved, transcendentals=0),
    )


def place():
    return lax.axis_index("sec") % GROUP


def partners():
    here = place()
    across = (here + CORES) % GROUP
    return here, here ^ 1, across, across ^ 1


def dot(a, b):
    return jnp.dot(a, b, preferred_element_type=F32)


def dot_wide(a, b):
    return jnp.dot(a, b, precision=HIGH, preferred_element_type=F32)


def two_parts(x):
    high = x.astype(BF16)
    return high, (x - high.astype(F32)).astype(BF16)


def left_lanes(x):
    return lax.broadcasted_iota(jnp.int32, x.shape, 1) < x.shape[1] // 2


def swap_lanes(x):
    return pltpu.roll(x, x.shape[1] // 2, 1)


def pack(tall):
    half = tall.shape[0] // 2
    top, low = tall[:half], tall[half:]
    return jnp.where(left_lanes(top), top, swap_lanes(low))


def unpack(packed):
    return jnp.concatenate([packed, swap_lanes(packed)], axis=0)


def copies(green, held, sem, first, rows):
    energies, steps = sem.shape
    size = rows // steps
    out = []
    for e in range(energies):
        for c in range(steps):
            at = pl.ds(c * size, size)
            move = pltpu.make_async_copy(green.at[e, pl.ds(first + c * size, size)], held.at[e, at], sem.at[e, c])
            move.start(priority=(e * steps + c) % 2)
            out.append((e, slice(c * size, (c + 1) * size), move))
    return out


def pairs_kernel(owner_in, blocks_in, green, inject_in, out, owner, blocks, inject, held, full, slot_of, counts, sem, side):
    energies, orbitals, _ = green.shape
    sections = out.shape[0]
    count = owner.shape[0]
    lists = [
        pltpu.make_async_copy(owner_in, owner, side.at[0]),
        pltpu.make_async_copy(blocks_in, blocks, side.at[1]),
    ]
    columns = pltpu.make_async_copy(inject_in, inject, side.at[2])
    for move in lists:
        move.start()
    columns.start(priority=1)
    moves = copies(green, held, sem, 0, orbitals)
    rows = CAP * energies * BLK
    lane = lax.broadcasted_iota(jnp.int32, (HEAD, out.shape[2]), 1)
    none = jnp.where(lane < CAP, -1.0, 0.0).astype(BF16)

    def blank(d, _):
        counts[d] = 0
        out[d, :rows, :] = jnp.zeros((rows, out.shape[2]), BF16)
        out[d, rows : rows + HEAD, :] = none
        return 0

    lax.fori_loop(0, sections, blank, 0)
    for move in lists:
        move.wait()

    def rank(q, _):
        d = owner[q]
        r = counts[d]
        counts[d] = r + 1
        slot_of[q] = r
        head = out[d, rows : rows + HEAD, :].astype(F32)
        head = jnp.where(lane == r, blocks[1, q].astype(F32), head)
        out[d, rows : rows + HEAD, :] = head.astype(BF16)
        return 0

    lax.fori_loop(0, count, rank, 0)
    columns.wait()
    for e, at, move in moves:
        move.wait()
        full[e, at, :] = dot(held[e, at, :], inject[e]).astype(BF16)

    def fill(q, _):
        d, r = owner[q], slot_of[q]
        first = pl.multiple_of(blocks[0, q] * BLK, BLK)
        for e in range(energies):
            to = pl.multiple_of((r * energies + e) * BLK, BLK)
            out[d, pl.ds(to, BLK), :] = full[e, pl.ds(first, BLK), :]
        return 0

    lax.fori_loop(0, count, fill, 0, unroll=4)


def outgoing_pairs(owner, blocks, green, inject, sections):
    energies, orbitals, _ = green.shape
    columns = inject.shape[2]
    steps = 4
    return call(
        pairs_kernel,
        "pairs",
        [IN_HBM] * 4,
        shape(sections, CAP * energies * BLK + HEAD, columns),
        [
            pltpu.SMEM(owner.shape, jnp.int32),
            pltpu.SMEM(blocks.shape, jnp.int32),
            pltpu.VMEM(inject.shape, BF16),
            pltpu.VMEM(green.shape, BF16),
            pltpu.VMEM(inject.shape, BF16),
            pltpu.SMEM(owner.shape, jnp.int32),
            pltpu.SMEM((sections,), jnp.int32),
            pltpu.SemaphoreType.DMA((energies, steps)),
            pltpu.SemaphoreType.DMA((3,)),
        ],
        2 * energies * orbitals * orbitals * columns,
        2 * green.size,
        VMEM_WHOLE,
    )(owner, blocks, green, inject)


def maps_kernel(pattern_in, green, coupling_in, couple, own, other, held, pattern, coupling, maps, sem, side):
    energies, orbitals, _ = green.shape
    face = coupling.shape[1]
    tiles = pltpu.make_async_copy(pattern_in, pattern, side.at[0])
    whole = pltpu.make_async_copy(coupling_in, coupling, side.at[1])
    tiles.start()
    whole.start()
    moves = copies(green, held, sem, orbitals - face, face)
    tiles.wait()
    whole.wait()
    high, wide = orbitals // pattern.shape[1], face // pattern.shape[0]
    for i in range(pattern.shape[1]):
        for j in range(pattern.shape[0]):
            at = (slice(i * high, (i + 1) * high), slice(j * wide, (j + 1) * wide))
            tile = coupling[at]
            couple[at] = jnp.where(pattern[j, i] == 1, tile, jnp.zeros_like(tile))
    for e, at, move in moves:
        move.wait()
        maps[e, at, :] = dot(held[e, at, :], couple[...])
    mine = place() // CORES
    own[...] = maps[mine]
    other[...] = maps[1 - mine]


def face_maps(pattern, green, coupling):
    energies, orbitals, _ = green.shape
    face = coupling.shape[1]
    square = shape(face, face, dtype=F32)
    return call(
        maps_kernel,
        "face_maps",
        [IN_HBM] * 3,
        [shape(orbitals, face), square, square, shape(energies, face, orbitals)],
        [
            pltpu.SMEM(pattern.shape, jnp.int32),
            pltpu.VMEM(coupling.shape, BF16),
            pltpu.VMEM((energies, face, face), F32),
            pltpu.SemaphoreType.DMA((energies, 1)),
            pltpu.SemaphoreType.DMA((2,)),
        ],
        2 * energies * face * orbitals * face,
        2 * energies * face * orbitals,
        VMEM_WHOLE,
    )(pattern, green, coupling)


def prop_kernel(green, couple, out, held, sem):
    for e, at, move in copies(green, held, sem, 0, green.shape[1]):
        move.wait()
        out[e, at, :] = dot(held[e, at, :], couple[...]).astype(BF16)


def propagator(green, couple):
    energies, orbitals, _ = green.shape
    face = couple.shape[1]
    return call(
        prop_kernel,
        "prop",
        [IN_HBM, IN_VMEM],
        shape(energies, orbitals, face),
        [pltpu.VMEM(green.shape, BF16), pltpu.SemaphoreType.DMA((energies, 4))],
        2 * energies * orbitals * orbitals * face,
        2 * green.size,
        VMEM_WHOLE,
    )(green, couple)


def image_kernel(green, source, out):
    for e in range(green.shape[0]):
        out[e] = dot(green[e], source[e])


def images(green, source):
    return call(
        image_kernel,
        "image",
        [IN_VMEM] * 2,
        shape(*source.shape, dtype=F32),
        [],
        2 * green.size * source.shape[2],
        2 * green.size,
    )(green, source)


def times(a, b):
    return dot(a[0], b[0]) + (dot(a[0], b[1]) + dot(a[1], b[0]))


def chain_kernel(own, near, across, far, _tie, total_out, parts, maps):
    collect((own, near, across, far), maps)
    split = [two_parts(maps[j]) for j in range(GROUP)]
    lower, upper = two_parts(times(split[1], split[0])), two_parts(times(split[3], split[2]))
    total_out[...] = times(upper, lower).astype(total_out.dtype)
    for j, (high, low) in enumerate(split):
        parts[0, j] = high
        parts[1, j] = low


def chain(maps, total_dtype, tie):
    face = maps[0].shape[0]
    return call(
        chain_kernel,
        "chain_maps",
        [IN_VMEM] * GROUP + [IN_PLACE],
        [shape(face, face, dtype=total_dtype), shape(2, GROUP, face, face)],
        [pltpu.VMEM((GROUP, face, face), F32)],
        2 * 3 * 3 * face**3,
        4 * 10 * face * face,
    )(*maps, tie)


def source_kernel(received, inject, face_rows, _prop, source, own, near, across, far, quarters, total, heads, targets, sem):
    energies, orbitals, columns = inject.shape
    sections = received.shape[0]
    half = quarters.shape[1]
    rows = CAP * energies * BLK

    def read(s, _):
        block = received[s, rows : rows + HEAD, :].astype(F32)
        heads[pl.ds(s, 1), :] = block[:1].astype(jnp.int32)
        return 0

    lax.fori_loop(0, sections, read, 0, unroll=min(sections, 8))
    fetch = pltpu.make_async_copy(heads, targets, sem)
    fetch.start()
    total[...] = inject[...].astype(F32)
    fetch.wait()

    def add(s, _):
        for r in range(CAP):
            first = pl.multiple_of(jnp.maximum(targets[s, r], 0) * BLK, BLK)
            for e in range(energies):
                item = received[s, (r * energies + e) * BLK : (r * energies + e + 1) * BLK, :]
                total[e, pl.ds(first, BLK), :] += item.astype(F32)
        return 0

    lax.fori_loop(0, sections, add, 0, unroll=2)
    split = GROUP // energies
    for e in range(energies):
        source[e] = total[e].astype(BF16)
        tall = dot(face_rows[e], source[e])
        quarters[e * split] = pack(tall)
        second = jnp.where(left_lanes(tall[:half]), swap_lanes(tall[:half]), tall[half:])
        quarters[e * split + 1] = second
    deal(quarters, (own, near, across, far))


def placed_source(received, inject, face_rows, ready):
    face = face_rows.shape[1]
    energies, orbitals, columns = inject.shape
    sections = received.shape[0]
    return call(
        source_kernel,
        "source_and_face",
        [IN_VMEM, IN_VMEM, IN_VMEM, IN_PLACE],
        [shape(*inject.shape)] + [shape(face // 2, columns)] * GROUP,
        [
            pltpu.VMEM((GROUP, face // 2, columns), F32),
            pltpu.VMEM(inject.shape, F32),
            pltpu.VMEM((sections, columns), jnp.int32),
            pltpu.SMEM((sections, columns), jnp.int32),
            pltpu.SemaphoreType.DMA,
        ],
        2 * energies * face * orbitals * columns,
        2 * energies * face * orbitals + 2 * received.size,
    )(received, inject, face_rows, ready)


def deal(items, outs):
    for out, at in zip(outs, partners()):
        out[...] = items[at].astype(out.dtype)


def collect(refs, held):
    for ref, at in zip(refs, partners()):
        held[at] = ref[...]


def step(parts, j, shift, state):
    return unpack(shift.astype(F32)) + times((parts[0, j], parts[1, j]), two_parts(state))


def total_kernel(own, near, across, far, parts, out, shifts):
    collect((own, near, across, far), shifts)
    state = unpack(shifts[0].astype(F32))
    for j in range(1, GROUP):
        state = step(parts, j, shifts[j], state)
    out[...] = pack(state).astype(BF16)


def plane_total(shifts, parts):
    half, columns = shifts[0].shape
    return call(
        total_kernel,
        "plane_total",
        [IN_VMEM] * (GROUP + 1),
        shape(half, columns),
        [pltpu.VMEM((GROUP, half, columns), BF16)],
        3 * parts.size * columns,
        2 * parts.size,
    )(*shifts, parts)


def entering_kernel(count, *refs):
    below, maps = refs[:count], refs[count : 2 * count - 1]
    parts, _image = refs[2 * count - 1 : 2 * count + 1]
    arrived, out = refs[2 * count + 1 : 2 * count + 1 + GROUP], refs[2 * count + 1 + GROUP : -2]
    shifts, held = refs[-2:]
    collect(arrived, shifts)
    state = unpack(below[-1][...].astype(F32))
    for k in range(count - 2, -1, -1):
        high, low = two_parts(state)
        state = unpack(below[k][...].astype(F32)) + dot(maps[k][...], high) + dot(maps[k][...], low)
    held[0] = pack(state)
    for j in range(1, GROUP):
        state = step(parts, j - 1, shifts[j - 1], state)
        held[j] = pack(state)
    deal(held, out)


def entering(below, maps, parts, shifts, tie):
    half, columns = below[0].shape
    count = len(below)
    return call(
        functools.partial(entering_kernel, count),
        "entering",
        [IN_VMEM] * (2 * count) + [IN_PLACE] + [IN_VMEM] * GROUP,
        [shape(half, columns)] * GROUP,
        [pltpu.VMEM((GROUP, half, columns), BF16), pltpu.VMEM((GROUP, half, columns), F32)],
        4 * parts.size * columns,
        2 * parts.size,
    )(*below, *maps, parts, tie, *shifts)


def waves_kernel(own, near, across, far, prop, image, out, arrived):
    collect((own, near, across, far), arrived)
    split = GROUP // prop.shape[0]
    for e in range(prop.shape[0]):
        near, far = arrived[e * split].astype(F32), arrived[e * split + 1].astype(F32)
        left = left_lanes(near)
        top = jnp.where(left, near, swap_lanes(far))
        low = jnp.where(left, swap_lanes(near), far)
        incoming = jnp.concatenate([top, low], axis=0).astype(BF16)
        out[e] = (dot(prop[e], incoming) + image[e]).astype(BF16)


def final_waves(arrived, prop, image):
    half, columns = arrived[0].shape
    return call(
        waves_kernel,
        "waves",
        [IN_VMEM] * (GROUP + 2),
        shape(*image.shape),
        [pltpu.VMEM((GROUP, half, columns), BF16)],
        2 * prop.size * columns,
        2 * prop.size + 6 * image.size,
    )(*arrived, prop, image)


def to_near(item, sections):
    return lax.ppermute(item, "sec", [(s, s ^ 1) for s in range(sections)])


def to_across(item, sections):
    return lax.ppermute(item, "sec", [(s, s // GROUP * GROUP + (s % GROUP + CORES) % GROUP) for s in range(sections)])


def to_far(item, sections):
    return lax.ppermute(item, "sec", [(s, s // GROUP * GROUP + (s % GROUP + CORES) % GROUP ^ 1) for s in range(sections)])


def exchange(own, near, across, far, sections):
    across, far = to_across(across, sections), to_far(far, sections)
    return [own, to_near(near, sections), across, far]


def up_shift(sections, k):
    return [(s, s + GROUP * k) for s in range(sections - GROUP * k)]


def spread(packed):
    half = packed.shape[1] // 2
    return jnp.concatenate([packed[:, :half], packed[:, half:]], axis=0)


def gather_below(total_map, total, sections):
    planes = sections // GROUP
    if planes <= 4:
        below = [lax.ppermute(total, "sec", up_shift(sections, k)) for k in range(1, planes)]
        maps = [lax.ppermute(total_map, "sec", up_shift(sections, k)) for k in range(1, planes - 1)]
        return below, maps
    shift = lax.ppermute(spread(total).astype(F32), "sec", up_shift(sections, 1))
    joined = lax.ppermute(total_map, "sec", up_shift(sections, 1))
    stride = 1
    while stride < planes:
        other = lax.ppermute(shift, "sec", up_shift(sections, stride))
        other_map = lax.ppermute(joined, "sec", up_shift(sections, stride))
        shift = shift + dot_wide(joined, other)
        joined = dot_wide(joined, other_map)
        stride *= 2
    half = shift.shape[0] // 2
    return [jnp.concatenate([shift[:half], shift[half:]], axis=1)], []


def per_device(green, injected, coupling, pattern, owner, pair_blocks):
    sections = lax.axis_size("sec")
    green, inject = green[0], injected[0]

    outgoing = outgoing_pairs(owner[:, 0], pair_blocks.T, green, inject, sections)
    received = lax.all_to_all(outgoing, "sec", split_axis=0, concat_axis=0, tiled=True)

    couple, own_map, other_map, face_rows = face_maps(pattern[0].T, green, coupling[0])
    across = to_across(other_map, sections)
    near = to_near(own_map, sections)
    prop = propagator(green, couple)
    far = to_near(across, sections)

    source, *quarters = placed_source(received, inject, face_rows, prop)
    total_dtype = BF16 if sections // GROUP <= 4 else F32
    shifts = exchange(*quarters, sections)
    total_map, parts = chain([own_map, near, across, far], total_dtype, shifts[1])
    below, maps = gather_below(total_map, plane_total(shifts, parts), sections)
    image = images(green, source)
    arrived = exchange(*entering(below, maps, parts, shifts, image), sections)
    return final_waves(arrived, prop, image)[None]


def solution(mesh):
    in_specs = (
        P("sec", "grp", None, None),
        P("sec", "grp", None, None),
        P("sec", None, None),
        P("sec", None, None),
        P("sec", None),
        P("sec", None),
    )
    out_specs = P("sec", "grp", None, None)
    return jax.shard_map(
        per_device, mesh=mesh, in_specs=in_specs, out_specs=out_specs, check_vma=False
    )
```

time: 79.5 us -> 67.5 us (0.85)
  Pallas kernels: 29.2 us -> 22.5 us
  local copies, waits for them, and re-layouts: 3.77 us -> 1.39 us
  starting transfers between devices: 27.6 us -> 26.3 us
  waiting for transfers between devices: 18 us -> 16.7 us
    pallas_call x6 -> x5, Pallas kernels: 20.8 us -> 13.4 us  [the longest x1 6.73 us: propagator(): call(prop_kernel, 'prop', [IN_HBM, IN_VMEM], shape(energies, orbitals, fa...]
    ppermute x9, starting transfers between devices: 8.49 us -> 6.01 us  [the longest x3 4.19 us: to_across(): lax.ppermute(item, 'sec', [(s, s // GROUP * GROUP + (s % GROUP + CORES) %...]
    unnamed x16 -> x12, local copies, waits for them, and re-layouts: 3.77 us -> 1.39 us
    ppermute x9, waiting for transfers between devices: 18 us -> 16.4 us  [the longest x3 14.5 us: to_across(): lax.ppermute(item, 'sec', [(s, s // GROUP * GROUP + (s % GROUP + CORES) %...]
    ppermute x2, starting transfers between devices: 6.98 us -> 8.04 us  [gather_below(): lax.ppermute(total_map, 'sec', up_shift(sections, k))]
  transfers between devices with their start and end apart: 15 -> 15, of which waited for: 7 -> 7; matrix products, arithmetic and copies ran while one was open for 0% -> 0% of each run, Pallas kernels for 27% -> 20%
where the time goes in v5:
time: 67.5 us; the launch traced here: 67.1 us
  starting transfers between devices  26.3 us (39%)
  Pallas kernels  22.5 us (33%)
  waiting for transfers between devices  16.7 us (25%)
  local copies, waits for them, and re-layouts  1.39 us (2%)
    ppermute x3, waiting for transfers between devices, to_across(): lax.ppermute(item, 'sec', [(s, s // GROUP * GROUP + (s % GROUP + CORES) %...  14.5 us
    ppermute x2, starting transfers between devices, gather_below(): lax.ppermute(total_map, 'sec', up_shift(sections, k))  8.04 us
    all_to_all x1, starting transfers between devices, per_device(): lax.all_to_all(outgoing, 'sec', split_axis=0, concat_axis=0, tiled=True)  7.37 us
    pallas_call x1, Pallas kernels, propagator(): call(prop_kernel, 'prop', [IN_HBM, IN_VMEM], shape(energies, orbitals, fa...  6.73 us
    pallas_call x1, Pallas kernels, outgoing_pairs(): call(pairs_kernel, 'pairs', [IN_HBM] * 4, shape(sections, CAP * energies...  5.46 us
    ppermute x3, starting transfers between devices, gather_below(): lax.ppermute(total, 'sec', up_shift(sections, k))  4.91 us
    ppermute x3, starting transfers between devices, to_across(): lax.ppermute(item, 'sec', [(s, s // GROUP * GROUP + (s % GROUP + CORES) %...  4.19 us
    pallas_call x1, Pallas kernels, face_maps(): call(maps_kernel, 'face_maps', [IN_HBM] * 3, [shape(orbitals, face), squa...  3.15 us
  transfers between devices with their start and end apart: 15, of which 7 were waited for; matrix products, arithmetic and copies ran while one was open for 0% of the time, Pallas kernels for 20%

profile of v5, /device:TPU:0, one launch (start us, length us, event | category | flops | bytes accessed | tf_op | source)
XLA Modules:
  0.0 67.1 jit_solution(15493482801886592763)
XLA Ops:
  0.0 5.5 %pairs.1 = bf16[16,144,128]{2,1,0:T(8,128)(2,1)} custom-call(s32[16]{0:T(128)} %bitcast.18, s32[2,16]{1,0:T(2,128)} %bitcast.16, bf16[2,1024,1024]{2,1,0:T(8,128)(2,1)} %bitcast.9, bf16[2,1024,128]{2,1,0:T(8,128)(2,1)} %bitcast.13), custom_call_target="tpu_custom_call" | custom-call | flops 536870912 | bytes 4194304 | tf_op jit(solution)/shard_map/pairs/pallas_call | solution.py:157
  5.5 7.4 %all-to-all-start = ((bf16[16,144,128]{2,1,0:T(8,128)(2,1)}), bf16[16,144,128]{2,1,0:T(8,128)(2,1)S(1)}, u32[]{:S(2)}, u32[]{:S(2)}) async-start(bf16[16,144,128]{2,1,0:T(8,128)(2,1)} %pairs.1), calls=%async_computation | async-start | bytes 1179648 | tf_op jit(solution)/shard_map/all_to_all | solution.py:488
  12.8 0.0 copy-start.3
  12.9 3.1 %face_maps.1 = (bf16[1024,256]{1,0:T(8,128)(2,1)}, f32[256,256]{1,0:T(8,128)}, f32[256,256]{1,0:T(8,128)}, bf16[2,256,1024]{2,1,0:T(8,128)(2,1)}) custom-call(s32[2,8]{1,0:T(2,128)} %bitcast.17, bf16[2,1024,1024]{2,1,0:T(8,128)(2,1)} %bitcast.10, bf16[1024,256]{1,0:T(8,128)(2,1)} %bitcast.15), custom_call_target="tpu_custom_call" | custom-call | flops 268435456 | bytes 1048576 | tf_op jit(solution)/shard_map/face_maps/pallas_call | solution.py:207
  16.0 0.0 copy-start.4
  16.0 2.0 %collective-permute-start.4 = (f32[256,256]{1,0:T(8,128)}, f32[256,256]{1,0:T(8,128)S(1)}, u32[]{:S(2)}, u32[]{:S(2)}) collective-permute-start(f32[256,256]{1,0:T(8,128)} %get-tuple-element.27), channel_id=1, source_target_pairs={{0,2},{1,3},{2,0},{3,1},{4,6},{5,7},{6,4},{7,5},{8,10},{9,11},{10,... | collective-permute-start | bytes 786440 | tf_op jit(solution)/shard_map/ppermute | solution.py:443
  18.0 0.0 collective-permute-start.3
  18.0 9.6 %collective-permute-done.4.across = f32[256,256]{1,0:T(8,128)S(1)} collective-permute-done((f32[256,256]{1,0:T(8,128)}, f32[256,256]{1,0:T(8,128)S(1)}, u32[]{:S(2)}, u32[]{:S(2)}) %collective-permute-start.4) | collective-permute-done | bytes 262176 | tf_op jit(solution)/shard_map/ppermute | solution.py:443
  27.6 0.0 collective-permute-start.5
  27.6 6.7 %prop.1._prop = bf16[2,1024,256]{2,1,0:T(8,128)(2,1)} custom-call(bf16[2,1024,1024]{2,1,0:T(8,128)(2,1)} %bitcast.11, bf16[1024,256]{1,0:T(8,128)(2,1)} %get-tuple-element.21.couple), custom_call_target="tpu_custom_call" | custom-call | flops 1073741824 | bytes 4194304 | tf_op jit(solution)/shard_map/prop/pallas_call | solution.py:234
  34.4 0.0 all-to-all-done.received
  34.4 0.0 copy-start
  34.4 0.0 copy-done.3
  34.4 0.0 copy-done.4
  34.4 0.0 copy-start.1
  34.4 1.4 %copy-done.1 = bf16[2,1024,256]{2,1,0:T(8,128)(2,1)S(1)} copy-done((bf16[2,1024,256]{2,1,0:T(8,128)(2,1)S(1)}, bf16[2,1024,256]{2,1,0:T(8,128)(2,1)}, u32[]{:S(2)}) %copy-start.1) | copy-done | bytes 1048600
  35.8 1.4 %source_and_face.1 = (bf16[2,1024,128]{2,1,0:T(8,128)(2,1)S(1)}, bf16[128,128]{1,0:T(8,128)(2,1)S(1)}, bf16[128,128]{1,0:T(8,128)(2,1)S(1)}, bf16[128,128]{1,0:T(8,128)(2,1)S(1)}, bf16[128,128]{1,0:T(8,128)(2,1)S(1)}) custom-call(bf16[16,144,128]{2,1,0:T(8,128)(2,1)S(1)} %all-to-all-done.received, bf16[2,1024,128]{2,1,0:T(8,128)(2,1)S(1)} %bitcast.14, ...), custom_call_target="tpu_custom_call" | custom-call | flops 134217728 | bytes 1638400 | tf_op jit(solution)/shard_map/source_and_face/pallas_call | solution.py:330
  37.2 0.6 collective-permute-start
  37.8 0.0 collective-permute-done.3.near
  37.8 0.0 collective-permute-done.5.far
  37.8 0.9 %collective-permute-done._tie.near.refs_8_ = bf16[128,128]{1,0:T(8,128)(2,1)S(1)} collective-permute-done((bf16[128,128]{1,0:T(8,128)(2,1)S(1)}, bf16[128,128]{1,0:T(8,128)(2,1)S(1)}, u32[]{:S(2)}, u32[]{:S(2)}) %collective-permute-start) | collective-permute-done | bytes 32800 | tf_op jit(solution)/shard_map/ppermute | solution.py:439
  38.6 0.0 copy-done.5
  38.6 0.8 %chain_maps.1 = (bf16[256,256]{1,0:T(8,128)(2,1)S(1)}, bf16[2,4,256,256]{3,2,1,0:T(8,128)(2,1)S(1)}) custom-call(f32[256,256]{1,0:T(8,128)S(1)} %copy-done.5, f32[256,256]{1,0:T(8,128)S(1)} %collective-permute-done.3.near, f32[256,256]{1,0:T(8,128)S(1)} %collective-permute-done.4.across, f32[256,256]{1,0:T(8,128)S(1)} %collective-permute-done.5.far, ...), custom_call_target="tpu_custom_call" | custom-call | flops 301989888 | bytes 2621440 | tf_op jit(solution)/shard_map/chain_maps/pallas_call | solution.py:279
  39.5 5.4 %collective-permute-start.10 = (bf16[256,256]{1,0:T(8,128)(2,1)S(1)}, bf16[256,256]{1,0:T(8,128)(2,1)S(1)}, u32[]{:S(2)}, u32[]{:S(2)}) collective-permute-start(bf16[256,256]{1,0:T(8,128)(2,1)S(1)} %get-tuple-element.29), channel_id=1, source_target_pairs={{0,8},{1,9},{2,10},{3,11},{4,12},{5,13},{6,14},{7,15},{16,24},{17,... | collective-permute-start | bytes 393224 | tf_op jit(solution)/shard_map/ppermute | solution.py:468
  44.9 2.6 %collective-permute-start.9 = (bf16[256,256]{1,0:T(8,128)(2,1)S(1)}, bf16[256,256]{1,0:T(8,128)(2,1)S(1)}, u32[]{:S(2)}, u32[]{:S(2)}) collective-permute-start(bf16[256,256]{1,0:T(8,128)(2,1)S(1)} %get-tuple-element.29), channel_id=1, source_target_pairs={{0,4},{1,5},{2,6},{3,7},{4,8},{5,9},{6,10},{7,11},{8,12},{9,13},{1... | collective-permute-start | bytes 393224 | tf_op jit(solution)/shard_map/ppermute | solution.py:468
  47.5 1.5 %collective-permute-start.1 = (bf16[128,128]{1,0:T(8,128)(2,1)S(1)}, bf16[128,128]{1,0:T(8,128)(2,1)S(1)}, u32[]{:S(2)}, u32[]{:S(2)}) collective-permute-start(bf16[128,128]{1,0:T(8,128)(2,1)S(1)} %get-tuple-element.24), channel_id=1, source_target_pairs={{0,2},{1,3},{2,0},{3,1},{4,6},{5,7},{6,4},{7,5},{8,10},{9,11},{10,... | collective-permute-start | bytes 98312 | tf_op jit(solution)/shard_map/ppermute | solution.py:443
  49.0 0.0 collective-permute-start.2
  49.0 2.5 %collective-permute-done.1.across.refs_9_ = bf16[128,128]{1,0:T(8,128)(2,1)S(1)} collective-permute-done((bf16[128,128]{1,0:T(8,128)(2,1)S(1)}, bf16[128,128]{1,0:T(8,128)(2,1)S(1)}, u32[]{:S(2)}, u32[]{:S(2)}) %collective-permute-start.1) | collective-permute-done | bytes 32800 | tf_op jit(solution)/shard_map/ppermute | solution.py:443
  51.5 0.9 %collective-permute-done.2.far.refs_10_ = bf16[128,128]{1,0:T(8,128)(2,1)S(1)} collective-permute-done((bf16[128,128]{1,0:T(8,128)(2,1)S(1)}, bf16[128,128]{1,0:T(8,128)(2,1)S(1)}, u32[]{:S(2)}, u32[]{:S(2)}) %collective-permute-start.2) | collective-permute-done | bytes 32800 | tf_op jit(solution)/shard_map/ppermute | solution.py:447
  52.4 0.9 %plane_total.1 = bf16[128,128]{1,0:T(8,128)(2,1)S(1)} custom-call(bf16[128,128]{1,0:T(8,128)(2,1)S(1)} %get-tuple-element.22.own.refs_7_, bf16[128,128]{1,0:T(8,128)(2,1)S(1)} %collective-permute-done._tie.near.refs_8_, bf16[128,128]{1,0:T(8,128)(2,1)S(1)} %collective-permute-done.1.across.refs_9_, bf16[128,128]{1,0:T(8,128)(2,1)S(1)} %collective-permute-done.2.far.refs_10_, ...), custom_call_target="tpu_custom_call" | custom-call | flops 201326592 | bytes 1048576 | tf_op jit(solution)/shard_map/plane_total/pallas_call | solution.py:371
  53.3 0.0 copy-start.2
  53.4 2.3 %collective-permute-start.6 = (bf16[128,128]{1,0:T(8,128)(2,1)S(1)}, bf16[128,128]{1,0:T(8,128)(2,1)S(1)}, u32[]{:S(2)}, u32[]{:S(2)}) collective-permute-start(bf16[128,128]{1,0:T(8,128)(2,1)S(1)} %plane_total.1), channel_id=1, source_target_pairs={{0,4},{1,5},{2,6},{3,7},{4,8},{5,9},{6,10},{7,11},{8,12},{9,13},{1... | collective-permute-start | bytes 98312 | tf_op jit(solution)/shard_map/ppermute | solution.py:467
  55.7 1.3 %collective-permute-start.7 = (bf16[128,128]{1,0:T(8,128)(2,1)S(1)}, bf16[128,128]{1,0:T(8,128)(2,1)S(1)}, u32[]{:S(2)}, u32[]{:S(2)}) collective-permute-start(bf16[128,128]{1,0:T(8,128)(2,1)S(1)} %plane_total.1), channel_id=1, source_target_pairs={{0,8},{1,9},{2,10},{3,11},{4,12},{5,13},{6,14},{7,15},{16,24},{17,... | collective-permute-start | bytes 98312 | tf_op jit(solution)/shard_map/ppermute | solution.py:467
  57.0 1.3 %collective-permute-start.8 = (bf16[128,128]{1,0:T(8,128)(2,1)S(1)}, bf16[128,128]{1,0:T(8,128)(2,1)S(1)}, u32[]{:S(2)}, u32[]{:S(2)}) collective-permute-start(bf16[128,128]{1,0:T(8,128)(2,1)S(1)} %plane_total.1), channel_id=1, source_target_pairs={{0,12},{1,13},{2,14},{3,15},{16,28},{17,29},{18,30},{19,31}} | collective-permute-start | bytes 98312 | tf_op jit(solution)/shard_map/ppermute | solution.py:467
  58.3 1.2 %image.1.refs_6_ = f32[2,1024,128]{2,1,0:T(8,128)S(1)} custom-call(bf16[2,1024,1024]{2,1,0:T(8,128)(2,1)S(1)} %bitcast.12, bf16[2,1024,128]{2,1,0:T(8,128)(2,1)S(1)} %get-tuple-element.30.source), custom_call_target="tpu_custom_call" | custom-call | flops 536870912 | bytes 4194304 | tf_op jit(solution)/shard_map/image/pallas_call | solution.py:252
  59.5 0.0 collective-permute-done.6.refs_0_
  59.6 0.0 collective-permute-done.7.refs_1_
  59.6 0.3 collective-permute-done.8.refs_2_
  59.9 0.0 collective-permute-done.10.refs_4_
  59.9 0.0 collective-permute-done.9.refs_3_
  59.9 1.4 %entering.1 = (bf16[128,128]{1,0:T(8,128)(2,1)S(1)}, bf16[128,128]{1,0:T(8,128)(2,1)S(1)}, bf16[128,128]{1,0:T(8,128)(2,1)S(1)}, bf16[128,128]{1,0:T(8,128)(2,1)S(1)}) custom-call(bf16[128,128]{1,0:T(8,128)(2,1)S(1)} %collective-permute-done.6.refs_0_, bf16[128,128]{1,0:T(8,128)(2,1)S(1)} %collective-permute-done.7.refs_1_, ...), custom_call_target="tpu_custom_call" | custom-call | flops 268435456 | bytes 1048576 | tf_op jit(solution)/shard_map/entering/pallas_call | solution.py:402
  61.3 0.1 collective-permute-start.11
  61.4 0.7 %collective-permute-start.12 = (bf16[128,128]{1,0:T(8,128)(2,1)S(1)}, bf16[128,128]{1,0:T(8,128)(2,1)S(1)}, u32[]{:S(2)}, u32[]{:S(2)}) collective-permute-start(bf16[128,128]{1,0:T(8,128)(2,1)S(1)} %get-tuple-element.33), channel_id=1, source_target_pairs={{0,2},{1,3},{2,0},{3,1},{4,6},{5,7},{6,4},{7,5},{8,10},{9,11},{10,... | collective-permute-start | bytes 98312 | tf_op jit(solution)/shard_map/ppermute | solution.py:443
  62.1 1.2 %collective-permute-start.13 = (bf16[128,128]{1,0:T(8,128)(2,1)S(1)}, bf16[128,128]{1,0:T(8,128)(2,1)S(1)}, u32[]{:S(2)}, u32[]{:S(2)}) collective-permute-start(bf16[128,128]{1,0:T(8,128)(2,1)S(1)} %get-tuple-element.34), channel_id=1, source_target_pairs={{0,3},{1,2},{2,1},{3,0},{4,7},{5,6},{6,5},{7,4},{8,11},{9,10},{10,... | collective-permute-start | bytes 98312 | tf_op jit(solution)/shard_map/ppermute | solution.py:447
  63.2 0.0 collective-permute-done.11.near
  63.2 2.4 %collective-permute-done.12.across = bf16[128,128]{1,0:T(8,128)(2,1)S(1)} collective-permute-done((bf16[128,128]{1,0:T(8,128)(2,1)S(1)}, bf16[128,128]{1,0:T(8,128)(2,1)S(1)}, u32[]{:S(2)}, u32[]{:S(2)}) %collective-permute-start.12) | collective-permute-done | bytes 32800 | tf_op jit(solution)/shard_map/ppermute | solution.py:443
  65.6 0.1 collective-permute-done.13.far
  65.8 1.3 %waves.1 = bf16[2,1024,128]{2,1,0:T(8,128)(2,1)} custom-call(bf16[128,128]{1,0:T(8,128)(2,1)S(1)} %get-tuple-element.31.own, bf16[128,128]{1,0:T(8,128)(2,1)S(1)} %collective-permute-done.11.near, bf16[128,128]{1,0:T(8,128)(2,1)S(1)} %collective-permute-done.12.across, bf16[128,128]{1,0:T(8,128)(2,1)S(1)} %collective-permute-done.13.far, ...), custom_call_target="tpu_custom_call" | custom-call | flops 134217728 | bytes 2621440 | tf_op jit(solution)/shard_map/waves/pallas_call | solution.py:427
  (3 shorter events, 0.0 us)
Async XLA Ops:
  5.5 28.9 %all-to-all-start = ((bf16[16,144,128]{2,1,0:T(8,128)(2,1)}), bf16[16,144,128]{2,1,0:T(8,128)(2,1)S(1)}, u32[]{:S(2)}, u32[]{:S(2)}) async-start(bf16[16,144,128]{2,1,0:T(8,128)(2,1)} %pairs.1), calls=%async_computation | async-start | bytes 1179648 | tf_op jit(solution)/shard_map/all_to_all | solution.py:488
  12.8 21.5 %copy-start.3 = (bf16[1,2,1024,128]{3,2,1,0:T(8,128)(2,1)S(1)}, bf16[1,2,1024,128]{3,2,1,0:T(8,128)(2,1)}, u32[]{:S(2)}) copy-start(bf16[1,2,1024,128]{3,2,1,0:T(8,128)(2,1)} %param.7) | copy-start | bytes 1572868
  16.0 18.4 %copy-start.4 = (bf16[2,256,1024]{2,1,0:T(8,128)(2,1)S(1)}, bf16[2,256,1024]{2,1,0:T(8,128)(2,1)}, u32[]{:S(2)}) copy-start(bf16[2,256,1024]{2,1,0:T(8,128)(2,1)} %get-tuple-element.20.face_rows) | copy-start | bytes 3145732
  16.0 11.6 %collective-permute-start.4 = (f32[256,256]{1,0:T(8,128)}, f32[256,256]{1,0:T(8,128)S(1)}, u32[]{:S(2)}, u32[]{:S(2)}) collective-permute-start(f32[256,256]{1,0:T(8,128)} %get-tuple-element.27), channel_id=1, source_target_pairs={{0,2},{1,3},{2,0},{3,1},{4,6},{5,7},{6,4},{7,5},{8,10},{9,11},{10,... | collective-permute-start | bytes 786440 | tf_op jit(solution)/shard_map/ppermute | solution.py:443
  18.0 19.8 %collective-permute-start.3 = (f32[256,256]{1,0:T(8,128)}, f32[256,256]{1,0:T(8,128)S(1)}, u32[]{:S(2)}, u32[]{:S(2)}) collective-permute-start(f32[256,256]{1,0:T(8,128)} %get-tuple-element.26.own), channel_id=1, source_target_pairs={{0,1},{1,0},{2,3},{3,2},{4,5},{5,4},{6,7},{7,6},{8,9},{9,8},{10,11... | collective-permute-start | bytes 786440 | tf_op jit(solution)/shard_map/ppermute | solution.py:439
  27.6 10.2 %collective-permute-start.5 = (f32[256,256]{1,0:T(8,128)S(1)}, f32[256,256]{1,0:T(8,128)S(1)}, u32[]{:S(2)}, u32[]{:S(2)}) collective-permute-start(f32[256,256]{1,0:T(8,128)S(1)} %collective-permute-done.4.across), channel_id=1, source_target_pairs={{0,1},{1,0},{2,3},{3,2},{4,5},{5,4},{6,7},{7,6},{8,9},{9,8},{10,11... | collective-permute-start | bytes 786440 | tf_op jit(solution)/shard_map/ppermute | solution.py:439
  27.6 11.0 %copy-start.5 = (f32[256,256]{1,0:T(8,128)S(1)}, f32[256,256]{1,0:T(8,128)}, u32[]{:S(2)}) copy-start(f32[256,256]{1,0:T(8,128)} %get-tuple-element.26.own) | copy-start | bytes 786436
  34.4 23.9 %copy-start = (bf16[1,2,1024,1024]{3,2,1,0:T(8,128)(2,1)S(1)}, bf16[1,2,1024,1024]{3,2,1,0:T(8,128)(2,1)}, u32[]{:S(2)}) copy-start(bf16[1,2,1024,1024]{3,2,1,0:T(8,128)(2,1)} %param.6) | copy-start | bytes 12582916
  34.4 1.4 %copy-start.1 = (bf16[2,1024,256]{2,1,0:T(8,128)(2,1)S(1)}, bf16[2,1024,256]{2,1,0:T(8,128)(2,1)}, u32[]{:S(2)}) copy-start(bf16[2,1024,256]{2,1,0:T(8,128)(2,1)} %prop.1._prop) | copy-start | bytes 3145732
  37.2 1.4 %collective-permute-start = (bf16[128,128]{1,0:T(8,128)(2,1)S(1)}, bf16[128,128]{1,0:T(8,128)(2,1)S(1)}, u32[]{:S(2)}, u32[]{:S(2)}) collective-permute-start(bf16[128,128]{1,0:T(8,128)(2,1)S(1)} %get-tuple-element.23), channel_id=1, source_target_pairs={{0,1},{1,0},{2,3},{3,2},{4,5},{5,4},{6,7},{7,6},{8,9},{9,8},{10,11... | collective-permute-start | bytes 98312 | tf_op jit(solution)/shard_map/ppermute | solution.py:439
  39.5 20.4 %collective-permute-start.10 = (bf16[256,256]{1,0:T(8,128)(2,1)S(1)}, bf16[256,256]{1,0:T(8,128)(2,1)S(1)}, u32[]{:S(2)}, u32[]{:S(2)}) collective-permute-start(bf16[256,256]{1,0:T(8,128)(2,1)S(1)} %get-tuple-element.29), channel_id=1, source_target_pairs={{0,8},{1,9},{2,10},{3,11},{4,12},{5,13},{6,14},{7,15},{16,24},{17,... | collective-permute-start | bytes 393224 | tf_op jit(solution)/shard_map/ppermute | solution.py:468
  44.9 15.0 %collective-permute-start.9 = (bf16[256,256]{1,0:T(8,128)(2,1)S(1)}, bf16[256,256]{1,0:T(8,128)(2,1)S(1)}, u32[]{:S(2)}, u32[]{:S(2)}) collective-permute-start(bf16[256,256]{1,0:T(8,128)(2,1)S(1)} %get-tuple-element.29), channel_id=1, source_target_pairs={{0,4},{1,5},{2,6},{3,7},{4,8},{5,9},{6,10},{7,11},{8,12},{9,13},{1... | collective-permute-start | bytes 393224 | tf_op jit(solution)/shard_map/ppermute | solution.py:468
  47.5 4.0 %collective-permute-start.1 = (bf16[128,128]{1,0:T(8,128)(2,1)S(1)}, bf16[128,128]{1,0:T(8,128)(2,1)S(1)}, u32[]{:S(2)}, u32[]{:S(2)}) collective-permute-start(bf16[128,128]{1,0:T(8,128)(2,1)S(1)} %get-tuple-element.24), channel_id=1, source_target_pairs={{0,2},{1,3},{2,0},{3,1},{4,6},{5,7},{6,4},{7,5},{8,10},{9,11},{10,... | collective-permute-start | bytes 98312 | tf_op jit(solution)/shard_map/ppermute | solution.py:443
  49.0 3.4 %collective-permute-start.2 = (bf16[128,128]{1,0:T(8,128)(2,1)S(1)}, bf16[128,128]{1,0:T(8,128)(2,1)S(1)}, u32[]{:S(2)}, u32[]{:S(2)}) collective-permute-start(bf16[128,128]{1,0:T(8,128)(2,1)S(1)} %get-tuple-element.25), channel_id=1, source_target_pairs={{0,3},{1,2},{2,1},{3,0},{4,7},{5,6},{6,5},{7,4},{8,11},{9,10},{10,... | collective-permute-start | bytes 98312 | tf_op jit(solution)/shard_map/ppermute | solution.py:447
  53.3 12.4 %copy-start.2 = (bf16[2,1024,256]{2,1,0:T(8,128)(2,1)S(1)}, bf16[2,1024,256]{2,1,0:T(8,128)(2,1)}, u32[]{:S(2)}) copy-start(bf16[2,1024,256]{2,1,0:T(8,128)(2,1)} %prop.1._prop) | copy-start | bytes 3145732
  53.4 6.2 %collective-permute-start.6 = (bf16[128,128]{1,0:T(8,128)(2,1)S(1)}, bf16[128,128]{1,0:T(8,128)(2,1)S(1)}, u32[]{:S(2)}, u32[]{:S(2)}) collective-permute-start(bf16[128,128]{1,0:T(8,128)(2,1)S(1)} %plane_total.1), channel_id=1, source_target_pairs={{0,4},{1,5},{2,6},{3,7},{4,8},{5,9},{6,10},{7,11},{8,12},{9,13},{1... | collective-permute-start | bytes 98312 | tf_op jit(solution)/shard_map/ppermute | solution.py:467
  55.7 3.9 %collective-permute-start.7 = (bf16[128,128]{1,0:T(8,128)(2,1)S(1)}, bf16[128,128]{1,0:T(8,128)(2,1)S(1)}, u32[]{:S(2)}, u32[]{:S(2)}) collective-permute-start(bf16[128,128]{1,0:T(8,128)(2,1)S(1)} %plane_total.1), channel_id=1, source_target_pairs={{0,8},{1,9},{2,10},{3,11},{4,12},{5,13},{6,14},{7,15},{16,24},{17,... | collective-permute-start | bytes 98312 | tf_op jit(solution)/shard_map/ppermute | solution.py:467
  57.0 2.9 %collective-permute-start.8 = (bf16[128,128]{1,0:T(8,128)(2,1)S(1)}, bf16[128,128]{1,0:T(8,128)(2,1)S(1)}, u32[]{:S(2)}, u32[]{:S(2)}) collective-permute-start(bf16[128,128]{1,0:T(8,128)(2,1)S(1)} %plane_total.1), channel_id=1, source_target_pairs={{0,12},{1,13},{2,14},{3,15},{16,28},{17,29},{18,30},{19,31}} | collective-permute-start | bytes 98312 | tf_op jit(solution)/shard_map/ppermute | solution.py:467
  61.3 1.9 %collective-permute-start.11 = (bf16[128,128]{1,0:T(8,128)(2,1)S(1)}, bf16[128,128]{1,0:T(8,128)(2,1)S(1)}, u32[]{:S(2)}, u32[]{:S(2)}) collective-permute-start(bf16[128,128]{1,0:T(8,128)(2,1)S(1)} %get-tuple-element.32), channel_id=1, source_target_pairs={{0,1},{1,0},{2,3},{3,2},{4,5},{5,4},{6,7},{7,6},{8,9},{9,8},{10,11... | collective-permute-start | bytes 98312 | tf_op jit(solution)/shard_map/ppermute | solution.py:439
  61.4 4.3 %collective-permute-start.12 = (bf16[128,128]{1,0:T(8,128)(2,1)S(1)}, bf16[128,128]{1,0:T(8,128)(2,1)S(1)}, u32[]{:S(2)}, u32[]{:S(2)}) collective-permute-start(bf16[128,128]{1,0:T(8,128)(2,1)S(1)} %get-tuple-element.33), channel_id=1, source_target_pairs={{0,2},{1,3},{2,0},{3,1},{4,6},{5,7},{6,4},{7,5},{8,10},{9,11},{10,... | collective-permute-start | bytes 98312 | tf_op jit(solution)/shard_map/ppermute | solution.py:443
  62.1 3.7 %collective-permute-start.13 = (bf16[128,128]{1,0:T(8,128)(2,1)S(1)}, bf16[128,128]{1,0:T(8,128)(2,1)S(1)}, u32[]{:S(2)}, u32[]{:S(2)}) collective-permute-start(bf16[128,128]{1,0:T(8,128)(2,1)S(1)} %get-tuple-element.34), channel_id=1, source_target_pairs={{0,3},{1,2},{2,1},{3,0},{4,7},{5,6},{6,5},{7,4},{8,11},{9,10},{10,... | collective-permute-start | bytes 98312 | tf_op jit(solution)/shard_map/ppermute | solution.py:447

commit v6 on v5

--- a/solution.py
+++ b/solution.py
@@ -83,32 +83,39 @@
     return jnp.concatenate([packed, swap_lanes(packed)], axis=0)
 
 
-def copies(green, held, sem, first, rows):
-    energies, steps = sem.shape
-    size = rows // steps
-    out = []
-    for e in range(energies):
-        for c in range(steps):
-            at = pl.ds(c * size, size)
-            move = pltpu.make_async_copy(green.at[e, pl.ds(first + c * size, size)], held.at[e, at], sem.at[e, c])
-            move.start(priority=(e * steps + c) % 2)
-            out.append((e, slice(c * size, (c + 1) * size), move))
-    return out
-
-
-def pairs_kernel(owner_in, blocks_in, green, inject_in, out, owner, blocks, inject, held, full, slot_of, counts, sem, side):
+def fetch(green, held, sem):
+    moves = [pltpu.make_async_copy(green.at[e], held.at[e], sem.at[e]) for e in range(green.shape[0])]
+    for move in moves:
+        move.start()
+    return moves
+
+
+def mask_tiles(pattern, coupling):
+    high, wide = coupling.shape[0] // pattern.shape[1], coupling.shape[1] // pattern.shape[0]
+    for i in range(pattern.shape[1]):
+        for j in range(pattern.shape[0]):
+            at = (slice(i * high, (i + 1) * high), slice(j * wide, (j + 1) * wide))
+            tile = coupling[at]
+            coupling[at] = jnp.where(pattern[j, i] == 1, tile, jnp.zeros_like(tile))
+
+
+def first_kernel(
+    owner_in, blocks_in, pattern_in, green, inject_in, coupling_in, out, own, other,
+    owner, blocks, pattern, inject, coupling, held, full, maps, slot_of, counts, sem, side,
+):
     energies, orbitals, _ = green.shape
     sections = out.shape[0]
     count = owner.shape[0]
-    lists = [
-        pltpu.make_async_copy(owner_in, owner, side.at[0]),
-        pltpu.make_async_copy(blocks_in, blocks, side.at[1]),
+    face = coupling.shape[1]
+    small = [
+        pltpu.make_async_copy(src, dst, side.at[k])
+        for k, (src, dst) in enumerate(
+            ((owner_in, owner), (blocks_in, blocks), (pattern_in, pattern), (inject_in, inject), (coupling_in, coupling))
+        )
     ]
-    columns = pltpu.make_async_copy(inject_in, inject, side.at[2])
-    for move in lists:
+    for move in small:
         move.start()
-    columns.start(priority=1)
-    moves = copies(green, held, sem, 0, orbitals)
+    moves = fetch(green, held, sem)
     rows = CAP * energies * BLK
     lane = lax.broadcasted_iota(jnp.int32, (HEAD, out.shape[2]), 1)
     none = jnp.where(lane < CAP, -1.0, 0.0).astype(BF16)
@@ -120,7 +127,7 @@
         return 0
 
     lax.fori_loop(0, sections, blank, 0)
-    for move in lists:
+    for move in small:
         move.wait()
 
     def rank(q, _):
@@ -134,113 +141,89 @@
         return 0
 
     lax.fori_loop(0, count, rank, 0)
-    columns.wait()
-    for e, at, move in moves:
+    mask_tiles(pattern, coupling)
+    for e, move in enumerate(moves):
         move.wait()
-        full[e, at, :] = dot(held[e, at, :], inject[e]).astype(BF16)
-
-    def fill(q, _):
-        d, r = owner[q], slot_of[q]
-        first = pl.multiple_of(blocks[0, q] * BLK, BLK)
-        for e in range(energies):
-            to = pl.multiple_of((r * energies + e) * BLK, BLK)
-            out[d, pl.ds(to, BLK), :] = full[e, pl.ds(first, BLK), :]
-        return 0
-
-    lax.fori_loop(0, count, fill, 0, unroll=4)
-
-
-def outgoing_pairs(owner, blocks, green, inject, sections):
+        full[e] = dot(held[e], inject[e]).astype(BF16)
+        maps[e] = dot(held[e, orbitals - face :, :], coupling[...])
+
+        def fill(q, _):
+            first = pl.multiple_of(blocks[0, q] * BLK, BLK)
+            to = pl.multiple_of((slot_of[q] * energies + e) * BLK, BLK)
+            out[owner[q], pl.ds(to, BLK), :] = full[e, pl.ds(first, BLK), :]
+            return 0
+
+        lax.fori_loop(0, count, fill, 0, unroll=4)
+    mine = place() // CORES
+    own[...] = maps[mine]
+    other[...] = maps[1 - mine]
+
+
+def pairs_and_maps(owner, blocks, pattern, green, inject, coupling, sections):
     energies, orbitals, _ = green.shape
-    columns = inject.shape[2]
-    steps = 4
-    return call(
-        pairs_kernel,
-        "pairs",
-        [IN_HBM] * 4,
-        shape(sections, CAP * energies * BLK + HEAD, columns),
+    columns, face = inject.shape[2], coupling.shape[1]
+    square = shape(face, face, dtype=F32)
+    return call(
+        first_kernel,
+        "pairs_and_maps",
+        [IN_HBM] * 6,
+        [shape(sections, CAP * energies * BLK + HEAD, columns), square, square],
         [
             pltpu.SMEM(owner.shape, jnp.int32),
             pltpu.SMEM(blocks.shape, jnp.int32),
+            pltpu.SMEM(pattern.shape, jnp.int32),
             pltpu.VMEM(inject.shape, BF16),
+            pltpu.VMEM(coupling.shape, BF16),
             pltpu.VMEM(green.shape, BF16),
             pltpu.VMEM(inject.shape, BF16),
+            pltpu.VMEM((energies, face, face), F32),
             pltpu.SMEM(owner.shape, jnp.int32),
             pltpu.SMEM((sections,), jnp.int32),
-            pltpu.SemaphoreType.DMA((energies, steps)),
-            pltpu.SemaphoreType.DMA((3,)),
+            pltpu.SemaphoreType.DMA((energies,)),
+            pltpu.SemaphoreType.DMA((5,)),
         ],
-        2 * energies * orbitals * orbitals * columns,
+        2 * green.size * (columns + face // 4),
         2 * green.size,
         VMEM_WHOLE,
-    )(owner, blocks, green, inject)
-
-
-def maps_kernel(pattern_in, green, coupling_in, couple, own, other, held, pattern, coupling, maps, sem, side):
+    )(owner, blocks, pattern, green, inject, coupling)
+
+
+def prop_kernel(pattern_in, green, coupling_in, _tie, out, face_rows, pattern, coupling, held, sem, side):
     energies, orbitals, _ = green.shape
     face = coupling.shape[1]
     tiles = pltpu.make_async_copy(pattern_in, pattern, side.at[0])
     whole = pltpu.make_async_copy(coupling_in, coupling, side.at[1])
     tiles.start()
     whole.start()
-    moves = copies(green, held, sem, orbitals - face, face)
+    moves = fetch(green, held, sem)
     tiles.wait()
     whole.wait()
-    high, wide = orbitals // pattern.shape[1], face // pattern.shape[0]
-    for i in range(pattern.shape[1]):
-        for j in range(pattern.shape[0]):
-            at = (slice(i * high, (i + 1) * high), slice(j * wide, (j + 1) * wide))
-            tile = coupling[at]
-            couple[at] = jnp.where(pattern[j, i] == 1, tile, jnp.zeros_like(tile))
-    for e, at, move in moves:
+    mask_tiles(pattern, coupling)
+    for e, move in enumerate(moves):
         move.wait()
-        maps[e, at, :] = dot(held[e, at, :], couple[...])
-    mine = place() // CORES
-    own[...] = maps[mine]
-    other[...] = maps[1 - mine]
-
-
-def face_maps(pattern, green, coupling):
+        out[e] = dot(held[e], coupling[...]).astype(BF16)
+        face_rows[e] = held[e, orbitals - face :, :]
+
+
+def propagator(pattern, green, coupling, tie):
     energies, orbitals, _ = green.shape
     face = coupling.shape[1]
-    square = shape(face, face, dtype=F32)
-    return call(
-        maps_kernel,
-        "face_maps",
-        [IN_HBM] * 3,
-        [shape(orbitals, face), square, square, shape(energies, face, orbitals)],
+    return call(
+        prop_kernel,
+        "prop",
+        [IN_HBM] * 3 + [IN_PLACE],
+        [shape(energies, orbitals, face), shape(energies, face, orbitals)],
         [
             pltpu.SMEM(pattern.shape, jnp.int32),
             pltpu.VMEM(coupling.shape, BF16),
-            pltpu.VMEM((energies, face, face), F32),
-            pltpu.SemaphoreType.DMA((energies, 1)),
+            pltpu.VMEM(green.shape, BF16),
+            pltpu.SemaphoreType.DMA((energies,)),
             pltpu.SemaphoreType.DMA((2,)),
         ],
-        2 * energies * face * orbitals * face,
-        2 * energies * face * orbitals,
-        VMEM_WHOLE,
-    )(pattern, green, coupling)
-
-
-def prop_kernel(green, couple, out, held, sem):
-    for e, at, move in copies(green, held, sem, 0, green.shape[1]):
-        move.wait()
-        out[e, at, :] = dot(held[e, at, :], couple[...]).astype(BF16)
-
-
-def propagator(green, couple):
-    energies, orbitals, _ = green.shape
-    face = couple.shape[1]
-    return call(
-        prop_kernel,
-        "prop",
-        [IN_HBM, IN_VMEM],
-        shape(energies, orbitals, face),
-        [pltpu.VMEM(green.shape, BF16), pltpu.SemaphoreType.DMA((energies, 4))],
-        2 * energies * orbitals * orbitals * face,
+        2 * green.size * face,
         2 * green.size,
         VMEM_WHOLE,
-    )(green, couple)
+    )(pattern, green, coupling, tie)
 
 
 def image_kernel(green, source, out):
@@ -264,30 +247,34 @@
     return dot(a[0], b[0]) + (dot(a[0], b[1]) + dot(a[1], b[0]))
 
 
-def chain_kernel(own, near, across, far, _tie, total_out, parts, maps):
+def chain_kernel(own, near, across, far, total_out, parts, maps, total):
     collect((own, near, across, far), maps)
     split = [two_parts(maps[j]) for j in range(GROUP)]
     lower, upper = two_parts(times(split[1], split[0])), two_parts(times(split[3], split[2]))
-    total_out[...] = times(upper, lower).astype(total_out.dtype)
+    total[...] = times(upper, lower)
+    rows = total_out.shape[0]
+    core = place() % CORES if rows < total.shape[0] else 0
+    total_out[...] = total[pl.ds(pl.multiple_of(core * rows, rows), rows), :].astype(total_out.dtype)
     for j, (high, low) in enumerate(split):
         parts[0, j] = high
         parts[1, j] = low
 
 
-def chain(maps, total_dtype, tie):
+def chain(maps, few):
     face = maps[0].shape[0]
+    total = shape(face // CORES, face) if few else shape(face, face, dtype=F32)
     return call(
         chain_kernel,
         "chain_maps",
-        [IN_VMEM] * GROUP + [IN_PLACE],
-        [shape(face, face, dtype=total_dtype), shape(2, GROUP, face, face)],
-        [pltpu.VMEM((GROUP, face, face), F32)],
+        [IN_VMEM] * GROUP,
+        [total, shape(2, GROUP, face, face)],
+        [pltpu.VMEM((GROUP, face, face), F32), pltpu.VMEM((face, face), F32)],
         2 * 3 * 3 * face**3,
         4 * 10 * face * face,
-    )(*maps, tie)
-
-
-def source_kernel(received, inject, face_rows, _prop, source, own, near, across, far, quarters, total, heads, targets, sem):
+    )(*maps)
+
+
+def source_kernel(received, inject, face_rows, _map, source, own, near, across, far, quarters, total, heads, targets, sem):
     energies, orbitals, columns = inject.shape
     sections = received.shape[0]
     half = quarters.shape[1]
@@ -380,15 +367,18 @@
 
 
 def entering_kernel(count, *refs):
-    below, maps = refs[:count], refs[count : 2 * count - 1]
-    parts, _image = refs[2 * count - 1 : 2 * count + 1]
-    arrived, out = refs[2 * count + 1 : 2 * count + 1 + GROUP], refs[2 * count + 1 + GROUP : -2]
+    below, maps = refs[:count], refs[count : 3 * count - 2]
+    parts, _image = refs[3 * count - 2 : 3 * count]
+    arrived, out = refs[3 * count : 3 * count + GROUP], refs[3 * count + GROUP : -2]
     shifts, held = refs[-2:]
     collect(arrived, shifts)
+    first_core = place() % CORES == 0
     state = unpack(below[-1][...].astype(F32))
     for k in range(count - 2, -1, -1):
         high, low = two_parts(state)
-        state = unpack(below[k][...].astype(F32)) + dot(maps[k][...], high) + dot(maps[k][...], low)
+        mine, other = (dot(half[...], high) + dot(half[...], low) for half in maps[2 * k : 2 * k + 2])
+        top, bottom = jnp.where(first_core, mine, other), jnp.where(first_core, other, mine)
+        state = unpack(below[k][...].astype(F32)) + jnp.concatenate([top, bottom], axis=0)
     held[0] = pack(state)
     for j in range(1, GROUP):
         state = step(parts, j - 1, shifts[j - 1], state)
@@ -402,7 +392,7 @@
     return call(
         functools.partial(entering_kernel, count),
         "entering",
-        [IN_VMEM] * (2 * count) + [IN_PLACE] + [IN_VMEM] * GROUP,
+        [IN_VMEM] * (3 * count - 1) + [IN_PLACE] + [IN_VMEM] * GROUP,
         [shape(half, columns)] * GROUP,
         [pltpu.VMEM((GROUP, half, columns), BF16), pltpu.VMEM((GROUP, half, columns), F32)],
         4 * parts.size * columns,
@@ -461,43 +451,54 @@
     return jnp.concatenate([packed[:, :half], packed[:, half:]], axis=0)
 
 
-def gather_below(total_map, total, sections):
-    planes = sections // GROUP
-    if planes <= 4:
-        below = [lax.ppermute(total, "sec", up_shift(sections, k)) for k in range(1, planes)]
-        maps = [lax.ppermute(total_map, "sec", up_shift(sections, k)) for k in range(1, planes - 1)]
-        return below, maps
+def maps_below(total_map, sections):
+    out = []
+    for k in range(1, sections // GROUP - 1):
+        half = lax.ppermute(total_map, "sec", up_shift(sections, k))
+        out += [half, to_near(half, sections)]
+    return out
+
+
+def totals_below(total, sections):
+    return [lax.ppermute(total, "sec", up_shift(sections, k)) for k in range(1, sections // GROUP)]
+
+
+def scan_below(total_map, total, sections):
     shift = lax.ppermute(spread(total).astype(F32), "sec", up_shift(sections, 1))
     joined = lax.ppermute(total_map, "sec", up_shift(sections, 1))
     stride = 1
-    while stride < planes:
+    while stride < sections // GROUP:
         other = lax.ppermute(shift, "sec", up_shift(sections, stride))
         other_map = lax.ppermute(joined, "sec", up_shift(sections, stride))
         shift = shift + dot_wide(joined, other)
         joined = dot_wide(joined, other_map)
         stride *= 2
     half = shift.shape[0] // 2
-    return [jnp.concatenate([shift[:half], shift[half:]], axis=1)], []
+    return [jnp.concatenate([shift[:half], shift[half:]], axis=1)]
 
 
 def per_device(green, injected, coupling, pattern, owner, pair_blocks):
     sections = lax.axis_size("sec")
     green, inject = green[0], injected[0]
 
-    outgoing = outgoing_pairs(owner[:, 0], pair_blocks.T, green, inject, sections)
-    received = lax.all_to_all(outgoing, "sec", split_axis=0, concat_axis=0, tiled=True)
-
-    couple, own_map, other_map, face_rows = face_maps(pattern[0].T, green, coupling[0])
+    coupling, tiles = coupling[0], pattern[0].T
+    outgoing, own_map, other_map = pairs_and_maps(
+        owner[:, 0], pair_blocks.T, tiles, green, inject, coupling, sections
+    )
     across = to_across(other_map, sections)
     near = to_near(own_map, sections)
-    prop = propagator(green, couple)
     far = to_near(across, sections)
-
-    source, *quarters = placed_source(received, inject, face_rows, prop)
-    total_dtype = BF16 if sections // GROUP <= 4 else F32
+    received = lax.all_to_all(outgoing, "sec", split_axis=0, concat_axis=0, tiled=True)
+
+    few = sections // GROUP <= 4
+    total_map, parts = chain([own_map, near, across, far], few)
+    maps = maps_below(total_map, sections) if few else []
+    prop, face_rows = propagator(tiles, green, coupling, total_map)
+
+    source, *quarters = placed_source(received, inject, face_rows, total_map)
     shifts = exchange(*quarters, sections)
-    total_map, parts = chain([own_map, near, across, far], total_dtype, shifts[1])
-    below, maps = gather_below(total_map, plane_total(shifts, parts), sections)
+    total = plane_total(shifts, parts)
+    below = totals_below(total, sections) if few else scan_below(total_map, total, sections)
     image = images(green, source)
     arrived = exchange(*entering(below, maps, parts, shifts, image), sections)
     return final_waves(arrived, prop, image)[None]

time: 67.5 us -> 69.6 us (1.031)
  Pallas kernels: 22.5 us -> 18.5 us
  local copies, waits for them, and re-layouts: 1.39 us -> 5.21 us
  waiting for transfers between devices: 16.7 us -> 18 us
  starting transfers between devices: 26.3 us -> 27.2 us
    pallas_call x4 -> x3, Pallas kernels: 16.2 us -> 12.2 us  [the longest x1 5.72 us: pairs_and_maps(): call(first_kernel, 'pairs_and_maps', [IN_HBM] * 6, [shape(sections, CAP *...]
    unnamed x12 -> x14, local copies, waits for them, and re-layouts: 1.39 us -> 5.21 us
    ppermute x3, waiting for transfers between devices: 14.5 us -> 15.7 us  [to_across(): lax.ppermute(item, 'sec', [(s, s // GROUP * GROUP + (s % GROUP + CORES) %...]
    ppermute x2, starting transfers between devices: 1.17 us -> 2.3 us  [to_far(): lax.ppermute(item, 'sec', [(s, s // GROUP * GROUP + (s % GROUP + CORES) %...]
    ppermute x3, starting transfers between devices: 4.19 us -> 3.34 us  [to_across(): lax.ppermute(item, 'sec', [(s, s // GROUP * GROUP + (s % GROUP + CORES) %...]
    ppermute x4 -> x6, waiting for transfers between devices: 0.86 us -> 1.54 us  [to_near(): return lax.ppermute(item, 'sec', [(s, s ^ 1) for s in range(sections)])]
  transfers between devices with their start and end apart: 15 -> 17, of which waited for: 7 -> 5; matrix products, arithmetic and copies ran while one was open for 0% -> 0% of each run, Pallas kernels for 20% -> 14%
where the time goes in v6:
time: 69.6 us; the launch traced here: 69.2 us
  starting transfers between devices  27.2 us (39%)
  Pallas kernels  18.5 us (27%)
  waiting for transfers between devices  18 us (26%)
  local copies, waits for them, and re-layouts  5.21 us (7%)
    ppermute x3, waiting for transfers between devices, to_across(): lax.ppermute(item, 'sec', [(s, s // GROUP * GROUP + (s % GROUP + CORES) %...  15.7 us
    ppermute x2, starting transfers between devices, maps_below(): half = lax.ppermute(total_map, 'sec', up_shift(sections, k))  8.94 us
    all_to_all x1, starting transfers between devices, per_device(): lax.all_to_all(outgoing, 'sec', split_axis=0, concat_axis=0, tiled=True)  7.5 us
    pallas_call x1, Pallas kernels, pairs_and_maps(): call(first_kernel, 'pairs_and_maps', [IN_HBM] * 6, [shape(sections, CAP *...  5.72 us
    pallas_call x1, Pallas kernels, propagator(): call(prop_kernel, 'prop', [IN_HBM] * 3 + [IN_PLACE], [shape(energies, orb...  5.58 us
    unnamed x14, local copies, waits for them, and re-layouts  5.21 us
    ppermute x3, starting transfers between devices, totals_below(): lax.ppermute(total, 'sec', up_shift(sections, k))  4.5 us
    ppermute x3, starting transfers between devices, to_across(): lax.ppermute(item, 'sec', [(s, s // GROUP * GROUP + (s % GROUP + CORES) %...  3.34 us
  transfers between devices with their start and end apart: 17, of which 5 were waited for; matrix products, arithmetic and copies ran while one was open for 0% of the time, Pallas kernels for 14%

profile of v6, /device:TPU:0, one launch (start us, length us, event | category | flops | bytes accessed | tf_op | source)
XLA Modules:
  0.0 69.2 jit_solution(17945301454441785197)
XLA Ops:
  0.0 5.7 %pairs_and_maps.1 = (bf16[16,144,128]{2,1,0:T(8,128)(2,1)}, f32[256,256]{1,0:T(8,128)}, f32[256,256]{1,0:T(8,128)}) custom-call(s32[16]{0:T(128)} %bitcast.19, s32[2,16]{1,0:T(2,128)} %bitcast.18, s32[2,8]{1,0:T(2,128)} %bitcast.16, bf16[2,1024,1024]{2,1,0:T(8,128)(2,1)} %bitcast.9, bf16[2,1024,128]{2,1,0:T(8,128)(2,1)} %bitcast.12, bf16[1024,256]{1,0:T(8,128)(2,1)} %bitcast.14), custom_call_target="tpu_custom_call" | custom-call | flops 805306368 | bytes 4194304 | tf_op jit(solution)/shard_map/pairs_and_maps/pallas_call | solution.py:166
  5.7 0.0 copy-start.1
  5.7 7.5 %all-to-all-start = ((bf16[16,144,128]{2,1,0:T(8,128)(2,1)}), bf16[16,144,128]{2,1,0:T(8,128)(2,1)S(1)}, u32[]{:S(2)}, u32[]{:S(2)}) async-start(bf16[16,144,128]{2,1,0:T(8,128)(2,1)} %get-tuple-element.21), calls=%async_computation | async-start | bytes 1179648 | tf_op jit(solution)/shard_map/all_to_all | solution.py:491
  13.2 1.9 %collective-permute-start.1 = (f32[256,256]{1,0:T(8,128)}, f32[256,256]{1,0:T(8,128)S(1)}, u32[]{:S(2)}, u32[]{:S(2)}) collective-permute-start(f32[256,256]{1,0:T(8,128)} %get-tuple-element.23), channel_id=1, source_target_pairs={{0,2},{1,3},{2,0},{3,1},{4,6},{5,7},{6,4},{7,5},{8,10},{9,11},{10,... | collective-permute-start | bytes 786440 | tf_op jit(solution)/shard_map/ppermute | solution.py:433
  15.2 0.0 collective-permute-start
  15.2 11.8 %collective-permute-done.1.across = f32[256,256]{1,0:T(8,128)S(1)} collective-permute-done((f32[256,256]{1,0:T(8,128)}, f32[256,256]{1,0:T(8,128)S(1)}, u32[]{:S(2)}, u32[]{:S(2)}) %collective-permute-start.1) | collective-permute-done | bytes 262176 | tf_op jit(solution)/shard_map/ppermute | solution.py:433
  27.0 0.0 collective-permute-start.2
  27.0 0.0 collective-permute-done.near
  27.0 1.5 %collective-permute-done.2.far = f32[256,256]{1,0:T(8,128)S(1)} collective-permute-done((f32[256,256]{1,0:T(8,128)S(1)}, f32[256,256]{1,0:T(8,128)S(1)}, u32[]{:S(2)}, u32[]{:S(2)}) %collective-permute-start.2) | collective-permute-done | bytes 262176 | tf_op jit(solution)/shard_map/ppermute | solution.py:429
  28.6 0.9 %copy-done.6 = f32[256,256]{1,0:T(8,128)S(1)} copy-done((f32[256,256]{1,0:T(8,128)S(1)}, f32[256,256]{1,0:T(8,128)}, u32[]{:S(2)}) %copy-start.6) | copy-done | bytes 262168
  29.5 0.9 %chain_maps.1 = (bf16[128,256]{1,0:T(8,128)(2,1)S(1)}, bf16[2,4,256,256]{3,2,1,0:T(8,128)(2,1)S(1)}) custom-call(f32[256,256]{1,0:T(8,128)S(1)} %copy-done.6, f32[256,256]{1,0:T(8,128)S(1)} %collective-permute-done.near, f32[256,256]{1,0:T(8,128)S(1)} %collective-permute-done.1.across, f32[256,256]{1,0:T(8,128)S(1)} %collective-permute-done.2.far), custom_call_target="tpu_custom_call" | custom-call | flops 301989888 | bytes 2621440 | tf_op jit(solution)/shard_map/chain_maps/pallas_call | solution.py:266
  30.4 0.0 copy-start.4
  30.4 3.9 %collective-permute-start.9 = (bf16[128,256]{1,0:T(8,128)(2,1)S(1)}, bf16[128,256]{1,0:T(8,128)(2,1)S(1)}, u32[]{:S(2)}, u32[]{:S(2)}) collective-permute-start(bf16[128,256]{1,0:T(8,128)(2,1)S(1)} %get-tuple-element.24._tie._map), channel_id=1, source_target_pairs={{0,4},{1,5},{2,6},{3,7},{4,8},{5,9},{6,10},{7,11},{8,12},{9,13},{1... | collective-permute-start | bytes 196616 | tf_op jit(solution)/shard_map/ppermute | solution.py:457
  34.3 5.1 %collective-permute-start.11 = (bf16[128,256]{1,0:T(8,128)(2,1)S(1)}, bf16[128,256]{1,0:T(8,128)(2,1)S(1)}, u32[]{:S(2)}, u32[]{:S(2)}) collective-permute-start(bf16[128,256]{1,0:T(8,128)(2,1)S(1)} %get-tuple-element.24._tie._map), channel_id=1, source_target_pairs={{0,8},{1,9},{2,10},{3,11},{4,12},{5,13},{6,14},{7,15},{16,24},{17,... | collective-permute-start | bytes 196616 | tf_op jit(solution)/shard_map/ppermute | solution.py:457
  39.4 5.6 %prop.1 = (bf16[2,1024,256]{2,1,0:T(8,128)(2,1)}, bf16[2,256,1024]{2,1,0:T(8,128)(2,1)}) custom-call(s32[2,8]{1,0:T(2,128)} %bitcast.17, bf16[2,1024,1024]{2,1,0:T(8,128)(2,1)} %bitcast.10, bf16[1024,256]{1,0:T(8,128)(2,1)} %bitcast.15, bf16[128,256]{1,0:T(8,128)(2,1)} %copy-done.4), custom_call_target="tpu_custom_call" | custom-call | flops 1073741824 | bytes 4194304 | tf_op jit(solution)/shard_map/prop/pallas_call | solution.py:211
  44.9 0.0 all-to-all-done.received
  45.0 1.2 %copy-done.3 = bf16[2,256,1024]{2,1,0:T(8,128)(2,1)S(1)} copy-done((bf16[2,256,1024]{2,1,0:T(8,128)(2,1)S(1)}, bf16[2,256,1024]{2,1,0:T(8,128)(2,1)}, u32[]{:S(2)}) %copy-start.3) | copy-done | bytes 1048600
  46.2 0.8 %copy-done.5 = bf16[128,256]{1,0:T(8,128)(2,1)S(1)} copy-done((bf16[128,256]{1,0:T(8,128)(2,1)S(1)}, bf16[128,256]{1,0:T(8,128)(2,1)}, u32[]{:S(2)}) %copy-start.5) | copy-done | bytes 65560
  47.0 1.4 %source_and_face.1 = (bf16[2,1024,128]{2,1,0:T(8,128)(2,1)S(1)}, bf16[128,128]{1,0:T(8,128)(2,1)S(1)}, bf16[128,128]{1,0:T(8,128)(2,1)S(1)}, bf16[128,128]{1,0:T(8,128)(2,1)S(1)}, bf16[128,128]{1,0:T(8,128)(2,1)S(1)}) custom-call(bf16[16,144,128]{2,1,0:T(8,128)(2,1)S(1)} %all-to-all-done.received, bf16[2,1024,128]{2,1,0:T(8,128)(2,1)S(1)} %bitcast.13, ...), custom_call_target="tpu_custom_call" | custom-call | flops 134217728 | bytes 1638400 | tf_op jit(solution)/shard_map/source_and_face/pallas_call | solution.py:317
  48.4 0.1 collective-permute-start.3
  48.5 0.1 collective-permute-start.4
  48.6 1.8 %collective-permute-start.5 = (bf16[128,128]{1,0:T(8,128)(2,1)S(1)}, bf16[128,128]{1,0:T(8,128)(2,1)S(1)}, u32[]{:S(2)}, u32[]{:S(2)}) collective-permute-start(bf16[128,128]{1,0:T(8,128)(2,1)S(1)} %get-tuple-element.29), channel_id=1, source_target_pairs={{0,3},{1,2},{2,1},{3,0},{4,7},{5,6},{6,5},{7,4},{8,11},{9,10},{10,... | collective-permute-start | bytes 98312 | tf_op jit(solution)/shard_map/ppermute | solution.py:437
  50.4 0.0 collective-permute-done.9.refs_3_
  50.4 0.3 collective-permute-start.10
  50.7 0.0 collective-permute-done.11.refs_5_
  50.7 0.2 collective-permute-start.12
  50.9 0.0 collective-permute-done.3.near.refs_10_
  50.9 1.8 %collective-permute-done.4.across.refs_11_ = bf16[128,128]{1,0:T(8,128)(2,1)S(1)} collective-permute-done((bf16[128,128]{1,0:T(8,128)(2,1)S(1)}, bf16[128,128]{1,0:T(8,128)(2,1)S(1)}, u32[]{:S(2)}, u32[]{:S(2)}) %collective-permute-start.4) | collective-permute-done | bytes 32800 | tf_op jit(solution)/shard_map/ppermute | solution.py:433
  52.7 0.0 collective-permute-done.5.far.refs_12_
  52.7 0.9 %plane_total.1 = bf16[128,128]{1,0:T(8,128)(2,1)S(1)} custom-call(bf16[128,128]{1,0:T(8,128)(2,1)S(1)} %get-tuple-element.26.own.refs_9_, bf16[128,128]{1,0:T(8,128)(2,1)S(1)} %collective-permute-done.3.near.refs_10_, bf16[128,128]{1,0:T(8,128)(2,1)S(1)} %collective-permute-done.4.across.refs_11_, bf16[128,128]{1,0:T(8,128)(2,1)S(1)} %collective-permute-done.5.far.refs_12_, ...), custom_call_target="tpu_custom_call" | custom-call | flops 201326592 | bytes 1048576 | tf_op jit(solution)/shard_map/plane_total/pallas_call | solution.py:358
  53.6 1.3 %collective-permute-start.6 = (bf16[128,128]{1,0:T(8,128)(2,1)S(1)}, bf16[128,128]{1,0:T(8,128)(2,1)S(1)}, u32[]{:S(2)}, u32[]{:S(2)}) collective-permute-start(bf16[128,128]{1,0:T(8,128)(2,1)S(1)} %plane_total.1), channel_id=1, source_target_pairs={{0,4},{1,5},{2,6},{3,7},{4,8},{5,9},{6,10},{7,11},{8,12},{9,13},{1... | collective-permute-start | bytes 98312 | tf_op jit(solution)/shard_map/ppermute | solution.py:463
  54.9 1.9 %collective-permute-start.7 = (bf16[128,128]{1,0:T(8,128)(2,1)S(1)}, bf16[128,128]{1,0:T(8,128)(2,1)S(1)}, u32[]{:S(2)}, u32[]{:S(2)}) collective-permute-start(bf16[128,128]{1,0:T(8,128)(2,1)S(1)} %plane_total.1), channel_id=1, source_target_pairs={{0,8},{1,9},{2,10},{3,11},{4,12},{5,13},{6,14},{7,15},{16,24},{17,... | collective-permute-start | bytes 98312 | tf_op jit(solution)/shard_map/ppermute | solution.py:463
  56.9 1.3 %collective-permute-start.8 = (bf16[128,128]{1,0:T(8,128)(2,1)S(1)}, bf16[128,128]{1,0:T(8,128)(2,1)S(1)}, u32[]{:S(2)}, u32[]{:S(2)}) collective-permute-start(bf16[128,128]{1,0:T(8,128)(2,1)S(1)} %plane_total.1), channel_id=1, source_target_pairs={{0,12},{1,13},{2,14},{3,15},{16,28},{17,29},{18,30},{19,31}} | collective-permute-start | bytes 98312 | tf_op jit(solution)/shard_map/ppermute | solution.py:463
  58.2 0.0 copy-start
  58.2 2.2 %copy-done = bf16[1,2,1024,1024]{3,2,1,0:T(8,128)(2,1)S(1)} copy-done((bf16[1,2,1024,1024]{3,2,1,0:T(8,128)(2,1)S(1)}, bf16[1,2,1024,1024]{3,2,1,0:T(8,128)(2,1)}, u32[]{:S(2)}) %copy-start) | copy-done | bytes 4194328
  60.4 1.2 %image.1.refs_8_ = f32[2,1024,128]{2,1,0:T(8,128)S(1)} custom-call(bf16[2,1024,1024]{2,1,0:T(8,128)(2,1)S(1)} %bitcast.11, bf16[2,1024,128]{2,1,0:T(8,128)(2,1)S(1)} %get-tuple-element.31.source), custom_call_target="tpu_custom_call" | custom-call | flops 536870912 | bytes 4194304 | tf_op jit(solution)/shard_map/image/pallas_call | solution.py:235
  61.6 0.0 collective-permute-done.10.refs_4_
  61.6 0.0 collective-permute-done.12.refs_6_
  61.6 0.0 collective-permute-done.6.refs_0_
  61.6 0.0 collective-permute-done.8.refs_2_
  61.6 1.4 %entering.1 = (bf16[128,128]{1,0:T(8,128)(2,1)S(1)}, bf16[128,128]{1,0:T(8,128)(2,1)S(1)}, bf16[128,128]{1,0:T(8,128)(2,1)S(1)}, bf16[128,128]{1,0:T(8,128)(2,1)S(1)}) custom-call(bf16[128,128]{1,0:T(8,128)(2,1)S(1)} %collective-permute-done.6.refs_0_, bf16[128,128]{1,0:T(8,128)(2,1)S(1)} %collective-permute-done.7.refs_1_, ...), custom_call_target="tpu_custom_call" | custom-call | flops 268435456 | bytes 1048576 | tf_op jit(solution)/shard_map/entering/pallas_call | solution.py:392
  63.1 0.1 collective-permute-start.13
  63.2 1.3 %collective-permute-start.14 = (bf16[128,128]{1,0:T(8,128)(2,1)S(1)}, bf16[128,128]{1,0:T(8,128)(2,1)S(1)}, u32[]{:S(2)}, u32[]{:S(2)}) collective-permute-start(bf16[128,128]{1,0:T(8,128)(2,1)S(1)} %get-tuple-element.34), channel_id=1, source_target_pairs={{0,2},{1,3},{2,0},{3,1},{4,6},{5,7},{6,4},{7,5},{8,10},{9,11},{10,... | collective-permute-start | bytes 98312 | tf_op jit(solution)/shard_map/ppermute | solution.py:433
  64.5 0.5 collective-permute-start.15
  65.0 0.0 collective-permute-done.13.near
  65.0 2.1 %collective-permute-done.14.across = bf16[128,128]{1,0:T(8,128)(2,1)S(1)} collective-permute-done((bf16[128,128]{1,0:T(8,128)(2,1)S(1)}, bf16[128,128]{1,0:T(8,128)(2,1)S(1)}, u32[]{:S(2)}, u32[]{:S(2)}) %collective-permute-start.14) | collective-permute-done | bytes 32800 | tf_op jit(solution)/shard_map/ppermute | solution.py:433
  67.1 0.7 %collective-permute-done.15.far = bf16[128,128]{1,0:T(8,128)(2,1)S(1)} collective-permute-done((bf16[128,128]{1,0:T(8,128)(2,1)S(1)}, bf16[128,128]{1,0:T(8,128)(2,1)S(1)}, u32[]{:S(2)}, u32[]{:S(2)}) %collective-permute-start.15) | collective-permute-done | bytes 32800 | tf_op jit(solution)/shard_map/ppermute | solution.py:437
  67.9 1.3 %waves.1 = bf16[2,1024,128]{2,1,0:T(8,128)(2,1)} custom-call(bf16[128,128]{1,0:T(8,128)(2,1)S(1)} %get-tuple-element.32.own, bf16[128,128]{1,0:T(8,128)(2,1)S(1)} %collective-permute-done.13.near, bf16[128,128]{1,0:T(8,128)(2,1)S(1)} %collective-permute-done.14.across, bf16[128,128]{1,0:T(8,128)(2,1)S(1)} %collective-permute-done.15.far, ...), custom_call_target="tpu_custom_call" | custom-call | flops 134217728 | bytes 2621440 | tf_op jit(solution)/shard_map/waves/pallas_call | solution.py:417
  (8 shorter events, 0.0 us)
Async XLA Ops:
  5.7 39.2 %copy-start.1 = (bf16[1,2,1024,128]{3,2,1,0:T(8,128)(2,1)S(1)}, bf16[1,2,1024,128]{3,2,1,0:T(8,128)(2,1)}, u32[]{:S(2)}) copy-start(bf16[1,2,1024,128]{3,2,1,0:T(8,128)(2,1)} %param.7) | copy-start | bytes 1572868
  5.7 39.2 %all-to-all-start = ((bf16[16,144,128]{2,1,0:T(8,128)(2,1)}), bf16[16,144,128]{2,1,0:T(8,128)(2,1)S(1)}, u32[]{:S(2)}, u32[]{:S(2)}) async-start(bf16[16,144,128]{2,1,0:T(8,128)(2,1)} %get-tuple-element.21), calls=%async_computation | async-start | bytes 1179648 | tf_op jit(solution)/shard_map/all_to_all | solution.py:491
  13.2 13.8 %collective-permute-start.1 = (f32[256,256]{1,0:T(8,128)}, f32[256,256]{1,0:T(8,128)S(1)}, u32[]{:S(2)}, u32[]{:S(2)}) collective-permute-start(f32[256,256]{1,0:T(8,128)} %get-tuple-element.23), channel_id=1, source_target_pairs={{0,2},{1,3},{2,0},{3,1},{4,6},{5,7},{6,4},{7,5},{8,10},{9,11},{10,... | collective-permute-start | bytes 786440 | tf_op jit(solution)/shard_map/ppermute | solution.py:433
  15.2 11.9 %collective-permute-start = (f32[256,256]{1,0:T(8,128)}, f32[256,256]{1,0:T(8,128)S(1)}, u32[]{:S(2)}, u32[]{:S(2)}) collective-permute-start(f32[256,256]{1,0:T(8,128)} %get-tuple-element.22.own), channel_id=1, source_target_pairs={{0,1},{1,0},{2,3},{3,2},{4,5},{5,4},{6,7},{7,6},{8,9},{9,8},{10,11... | collective-permute-start | bytes 786440 | tf_op jit(solution)/shard_map/ppermute | solution.py:429
  27.0 1.5 %collective-permute-start.2 = (f32[256,256]{1,0:T(8,128)S(1)}, f32[256,256]{1,0:T(8,128)S(1)}, u32[]{:S(2)}, u32[]{:S(2)}) collective-permute-start(f32[256,256]{1,0:T(8,128)S(1)} %collective-permute-done.1.across), channel_id=1, source_target_pairs={{0,1},{1,0},{2,3},{3,2},{4,5},{5,4},{6,7},{7,6},{8,9},{9,8},{10,11... | collective-permute-start | bytes 786440 | tf_op jit(solution)/shard_map/ppermute | solution.py:429
  28.6 1.0 %copy-start.6 = (f32[256,256]{1,0:T(8,128)S(1)}, f32[256,256]{1,0:T(8,128)}, u32[]{:S(2)}) copy-start(f32[256,256]{1,0:T(8,128)} %get-tuple-element.22.own) | copy-start | bytes 786436
  30.4 9.0 %copy-start.4 = (bf16[128,256]{1,0:T(8,128)(2,1)}, bf16[128,256]{1,0:T(8,128)(2,1)S(1)}, u32[]{:S(2)}) copy-start(bf16[128,256]{1,0:T(8,128)(2,1)S(1)} %get-tuple-element.24._tie._map) | copy-start | bytes 196612
  30.4 20.0 %collective-permute-start.9 = (bf16[128,256]{1,0:T(8,128)(2,1)S(1)}, bf16[128,256]{1,0:T(8,128)(2,1)S(1)}, u32[]{:S(2)}, u32[]{:S(2)}) collective-permute-start(bf16[128,256]{1,0:T(8,128)(2,1)S(1)} %get-tuple-element.24._tie._map), channel_id=1, source_target_pairs={{0,4},{1,5},{2,6},{3,7},{4,8},{5,9},{6,10},{7,11},{8,12},{9,13},{1... | collective-permute-start | bytes 196616 | tf_op jit(solution)/shard_map/ppermute | solution.py:457
  34.3 16.5 %collective-permute-start.11 = (bf16[128,256]{1,0:T(8,128)(2,1)S(1)}, bf16[128,256]{1,0:T(8,128)(2,1)S(1)}, u32[]{:S(2)}, u32[]{:S(2)}) collective-permute-start(bf16[128,256]{1,0:T(8,128)(2,1)S(1)} %get-tuple-element.24._tie._map), channel_id=1, source_target_pairs={{0,8},{1,9},{2,10},{3,11},{4,12},{5,13},{6,14},{7,15},{16,24},{17,... | collective-permute-start | bytes 196616 | tf_op jit(solution)/shard_map/ppermute | solution.py:457
  45.0 1.2 %copy-start.3 = (bf16[2,256,1024]{2,1,0:T(8,128)(2,1)S(1)}, bf16[2,256,1024]{2,1,0:T(8,128)(2,1)}, u32[]{:S(2)}) copy-start(bf16[2,256,1024]{2,1,0:T(8,128)(2,1)} %get-tuple-element.25.face_rows) | copy-start | bytes 3145732
  46.2 0.8 %copy-start.5 = (bf16[128,256]{1,0:T(8,128)(2,1)S(1)}, bf16[128,256]{1,0:T(8,128)(2,1)}, u32[]{:S(2)}) copy-start(bf16[128,256]{1,0:T(8,128)(2,1)} %copy-done.4) | copy-start | bytes 196612
  48.4 2.5 %collective-permute-start.3 = (bf16[128,128]{1,0:T(8,128)(2,1)S(1)}, bf16[128,128]{1,0:T(8,128)(2,1)S(1)}, u32[]{:S(2)}, u32[]{:S(2)}) collective-permute-start(bf16[128,128]{1,0:T(8,128)(2,1)S(1)} %get-tuple-element.27), channel_id=1, source_target_pairs={{0,1},{1,0},{2,3},{3,2},{4,5},{5,4},{6,7},{7,6},{8,9},{9,8},{10,11... | collective-permute-start | bytes 98312 | tf_op jit(solution)/shard_map/ppermute | solution.py:429
  48.5 4.2 %collective-permute-start.4 = (bf16[128,128]{1,0:T(8,128)(2,1)S(1)}, bf16[128,128]{1,0:T(8,128)(2,1)S(1)}, u32[]{:S(2)}, u32[]{:S(2)}) collective-permute-start(bf16[128,128]{1,0:T(8,128)(2,1)S(1)} %get-tuple-element.28), channel_id=1, source_target_pairs={{0,2},{1,3},{2,0},{3,1},{4,6},{5,7},{6,4},{7,5},{8,10},{9,11},{10,... | collective-permute-start | bytes 98312 | tf_op jit(solution)/shard_map/ppermute | solution.py:433
  48.6 4.1 %collective-permute-start.5 = (bf16[128,128]{1,0:T(8,128)(2,1)S(1)}, bf16[128,128]{1,0:T(8,128)(2,1)S(1)}, u32[]{:S(2)}, u32[]{:S(2)}) collective-permute-start(bf16[128,128]{1,0:T(8,128)(2,1)S(1)} %get-tuple-element.29), channel_id=1, source_target_pairs={{0,3},{1,2},{2,1},{3,0},{4,7},{5,6},{6,5},{7,4},{8,11},{9,10},{10,... | collective-permute-start | bytes 98312 | tf_op jit(solution)/shard_map/ppermute | solution.py:437
  50.4 11.2 %collective-permute-start.10 = (bf16[128,256]{1,0:T(8,128)(2,1)S(1)}, bf16[128,256]{1,0:T(8,128)(2,1)S(1)}, u32[]{:S(2)}, u32[]{:S(2)}) collective-permute-start(bf16[128,256]{1,0:T(8,128)(2,1)S(1)} %collective-permute-done.9.refs_3_), channel_id=1, source_target_pairs={{0,1},{1,0},{2,3},{3,2},{4,5},{5,4},{6,7},{7,6},{8,9},{9,8},{10,11... | collective-permute-start | bytes 196616 | tf_op jit(solution)/shard_map/ppermute | solution.py:429
  50.7 10.9 %collective-permute-start.12 = (bf16[128,256]{1,0:T(8,128)(2,1)S(1)}, bf16[128,256]{1,0:T(8,128)(2,1)S(1)}, u32[]{:S(2)}, u32[]{:S(2)}) collective-permute-start(bf16[128,256]{1,0:T(8,128)(2,1)S(1)} %collective-permute-done.11.refs_5_), channel_id=1, source_target_pairs={{0,1},{1,0},{2,3},{3,2},{4,5},{5,4},{6,7},{7,6},{8,9},{9,8},{10,11... | collective-permute-start | bytes 196616 | tf_op jit(solution)/shard_map/ppermute | solution.py:429
  52.7 15.2 %copy-start.2 = (bf16[2,1024,256]{2,1,0:T(8,128)(2,1)S(1)}, bf16[2,1024,256]{2,1,0:T(8,128)(2,1)}, u32[]{:S(2)}) copy-start(bf16[2,1024,256]{2,1,0:T(8,128)(2,1)} %get-tuple-element.36.prop) | copy-start | bytes 3145732
  53.6 8.0 %collective-permute-start.6 = (bf16[128,128]{1,0:T(8,128)(2,1)S(1)}, bf16[128,128]{1,0:T(8,128)(2,1)S(1)}, u32[]{:S(2)}, u32[]{:S(2)}) collective-permute-start(bf16[128,128]{1,0:T(8,128)(2,1)S(1)} %plane_total.1), channel_id=1, source_target_pairs={{0,4},{1,5},{2,6},{3,7},{4,8},{5,9},{6,10},{7,11},{8,12},{9,13},{1... | collective-permute-start | bytes 98312 | tf_op jit(solution)/shard_map/ppermute | solution.py:463
  54.9 6.7 %collective-permute-start.7 = (bf16[128,128]{1,0:T(8,128)(2,1)S(1)}, bf16[128,128]{1,0:T(8,128)(2,1)S(1)}, u32[]{:S(2)}, u32[]{:S(2)}) collective-permute-start(bf16[128,128]{1,0:T(8,128)(2,1)S(1)} %plane_total.1), channel_id=1, source_target_pairs={{0,8},{1,9},{2,10},{3,11},{4,12},{5,13},{6,14},{7,15},{16,24},{17,... | collective-permute-start | bytes 98312 | tf_op jit(solution)/shard_map/ppermute | solution.py:463
  56.9 4.8 %collective-permute-start.8 = (bf16[128,128]{1,0:T(8,128)(2,1)S(1)}, bf16[128,128]{1,0:T(8,128)(2,1)S(1)}, u32[]{:S(2)}, u32[]{:S(2)}) collective-permute-start(bf16[128,128]{1,0:T(8,128)(2,1)S(1)} %plane_total.1), channel_id=1, source_target_pairs={{0,12},{1,13},{2,14},{3,15},{16,28},{17,29},{18,30},{19,31}} | collective-permute-start | bytes 98312 | tf_op jit(solution)/shard_map/ppermute | solution.py:463
  58.2 2.2 %copy-start = (bf16[1,2,1024,1024]{3,2,1,0:T(8,128)(2,1)S(1)}, bf16[1,2,1024,1024]{3,2,1,0:T(8,128)(2,1)}, u32[]{:S(2)}) copy-start(bf16[1,2,1024,1024]{3,2,1,0:T(8,128)(2,1)} %param.6) | copy-start | bytes 12582916
  63.1 1.9 %collective-permute-start.13 = (bf16[128,128]{1,0:T(8,128)(2,1)S(1)}, bf16[128,128]{1,0:T(8,128)(2,1)S(1)}, u32[]{:S(2)}, u32[]{:S(2)}) collective-permute-start(bf16[128,128]{1,0:T(8,128)(2,1)S(1)} %get-tuple-element.33), channel_id=1, source_target_pairs={{0,1},{1,0},{2,3},{3,2},{4,5},{5,4},{6,7},{7,6},{8,9},{9,8},{10,11... | collective-permute-start | bytes 98312 | tf_op jit(solution)/shard_map/ppermute | solution.py:429
  63.2 4.0 %collective-permute-start.14 = (bf16[128,128]{1,0:T(8,128)(2,1)S(1)}, bf16[128,128]{1,0:T(8,128)(2,1)S(1)}, u32[]{:S(2)}, u32[]{:S(2)}) collective-permute-start(bf16[128,128]{1,0:T(8,128)(2,1)S(1)} %get-tuple-element.34), channel_id=1, source_target_pairs={{0,2},{1,3},{2,0},{3,1},{4,6},{5,7},{6,4},{7,5},{8,10},{9,11},{10,... | collective-permute-start | bytes 98312 | tf_op jit(solution)/shard_map/ppermute | solution.py:433
  64.5 3.3 %collective-permute-start.15 = (bf16[128,128]{1,0:T(8,128)(2,1)S(1)}, bf16[128,128]{1,0:T(8,128)(2,1)S(1)}, u32[]{:S(2)}, u32[]{:S(2)}) collective-permute-start(bf16[128,128]{1,0:T(8,128)(2,1)S(1)} %get-tuple-element.35), channel_id=1, source_target_pairs={{0,3},{1,2},{2,1},{3,0},{4,7},{5,6},{6,5},{7,4},{8,11},{9,10},{10,... | collective-permute-start | bytes 98312 | tf_op jit(solution)/shard_map/ppermute | solution.py:437

commit v7 on v6

--- a/solution.py
+++ b/solution.py
@@ -18,6 +18,7 @@
 BF16 = jnp.bfloat16
 VMEM_SMALL = 16 * 1024 * 1024
 VMEM_WHOLE = 63400000
+PEAK = 1.15e9
 
 IN_VMEM = pl.BlockSpec(memory_space=pltpu.VMEM)
 IN_SMEM = pl.BlockSpec(memory_space=pltpu.SMEM)
@@ -29,16 +30,18 @@
     return jax.ShapeDtypeStruct(dims, dtype)
 
 
-def call(body, name, ins, outs, scratch, flops, moved, vmem=VMEM_SMALL):
+def call(body, name, ins, outs, scratch, micros, vmem=VMEM_SMALL, aliases=None):
+    places = list(range(len(outs))) if isinstance(outs, list) else 0
     return pl.pallas_call(
         body,
         name=name,
         in_specs=ins,
         out_shape=outs,
-        out_specs=jax.tree.map(lambda _: IN_VMEM, outs),
+        out_specs=jax.tree.map(lambda k: IN_PLACE if k in (aliases or {}).values() else IN_VMEM, places),
+        input_output_aliases=aliases or {},
         scratch_shapes=scratch,
         compiler_params=pltpu.CompilerParams(vmem_limit_bytes=vmem),
-        cost_estimate=pl.CostEstimate(flops=flops, bytes_accessed=moved, transcendentals=0),
+        cost_estimate=pl.CostEstimate(flops=int(micros * PEAK), bytes_accessed=0, transcendentals=0),
     )
 
 
@@ -182,48 +185,32 @@
             pltpu.SemaphoreType.DMA((energies,)),
             pltpu.SemaphoreType.DMA((5,)),
         ],
-        2 * green.size * (columns + face // 4),
-        2 * green.size,
+        5.6,
         VMEM_WHOLE,
     )(owner, blocks, pattern, green, inject, coupling)
 
 
-def prop_kernel(pattern_in, green, coupling_in, _tie, out, face_rows, pattern, coupling, held, sem, side):
+def prop_kernel(pattern, green, coupling, out, face_rows, couple):
+    energies, orbitals, _ = green.shape
+    face = couple.shape[1]
+    couple[...] = coupling[...]
+    mask_tiles(pattern, couple)
+    for e in range(energies):
+        out[e] = dot(green[e], couple[...]).astype(BF16)
+        face_rows[e] = green[e, orbitals - face :, :]
+
+
+def propagator(pattern, green, coupling):
     energies, orbitals, _ = green.shape
     face = coupling.shape[1]
-    tiles = pltpu.make_async_copy(pattern_in, pattern, side.at[0])
-    whole = pltpu.make_async_copy(coupling_in, coupling, side.at[1])
-    tiles.start()
-    whole.start()
-    moves = fetch(green, held, sem)
-    tiles.wait()
-    whole.wait()
-    mask_tiles(pattern, coupling)
-    for e, move in enumerate(moves):
-        move.wait()
-        out[e] = dot(held[e], coupling[...]).astype(BF16)
-        face_rows[e] = held[e, orbitals - face :, :]
-
-
-def propagator(pattern, green, coupling, tie):
-    energies, orbitals, _ = green.shape
-    face = coupling.shape[1]
     return call(
         prop_kernel,
         "prop",
-        [IN_HBM] * 3 + [IN_PLACE],
+        [IN_SMEM, IN_VMEM, IN_VMEM],
         [shape(energies, orbitals, face), shape(energies, face, orbitals)],
-        [
-            pltpu.SMEM(pattern.shape, jnp.int32),
-            pltpu.VMEM(coupling.shape, BF16),
-            pltpu.VMEM(green.shape, BF16),
-            pltpu.SemaphoreType.DMA((energies,)),
-            pltpu.SemaphoreType.DMA((2,)),
-        ],
-        2 * green.size * face,
-        2 * green.size,
-        VMEM_WHOLE,
-    )(pattern, green, coupling, tie)
+        [pltpu.VMEM(coupling.shape, BF16)],
+        1.6,
+    )(pattern, green, coupling)
 
 
 def image_kernel(green, source, out):
@@ -238,8 +225,7 @@
         [IN_VMEM] * 2,
         shape(*source.shape, dtype=F32),
         [],
-        2 * green.size * source.shape[2],
-        2 * green.size,
+        1.2,
     )(green, source)
 
 
@@ -247,11 +233,12 @@
     return dot(a[0], b[0]) + (dot(a[0], b[1]) + dot(a[1], b[0]))
 
 
-def chain_kernel(own, near, across, far, total_out, parts, maps, total):
+def chain_kernel(own, near, across, far, total_out, whole, parts, maps, total):
     collect((own, near, across, far), maps)
     split = [two_parts(maps[j]) for j in range(GROUP)]
     lower, upper = two_parts(times(split[1], split[0])), two_parts(times(split[3], split[2]))
     total[...] = times(upper, lower)
+    whole[0], whole[1] = two_parts(total[...])
     rows = total_out.shape[0]
     core = place() % CORES if rows < total.shape[0] else 0
     total_out[...] = total[pl.ds(pl.multiple_of(core * rows, rows), rows), :].astype(total_out.dtype)
@@ -267,14 +254,13 @@
         chain_kernel,
         "chain_maps",
         [IN_VMEM] * GROUP,
-        [total, shape(2, GROUP, face, face)],
+        [total, shape(2, face, face), shape(2, GROUP, face, face)],
         [pltpu.VMEM((GROUP, face, face), F32), pltpu.VMEM((face, face), F32)],
-        2 * 3 * 3 * face**3,
-        4 * 10 * face * face,
+        0.9,
     )(*maps)
 
 
-def source_kernel(received, inject, face_rows, _map, source, own, near, across, far, quarters, total, heads, targets, sem):
+def source_kernel(received, inject, face_rows, _map, source, own, near, across, far, _same_map, quarters, total, heads, targets, sem):
     energies, orbitals, columns = inject.shape
     sections = received.shape[0]
     half = quarters.shape[1]
@@ -310,7 +296,7 @@
     deal(quarters, (own, near, across, far))
 
 
-def placed_source(received, inject, face_rows, ready):
+def placed_source(received, inject, face_rows, passed):
     face = face_rows.shape[1]
     energies, orbitals, columns = inject.shape
     sections = received.shape[0]
@@ -318,7 +304,7 @@
         source_kernel,
         "source_and_face",
         [IN_VMEM, IN_VMEM, IN_VMEM, IN_PLACE],
-        [shape(*inject.shape)] + [shape(face // 2, columns)] * GROUP,
+        [shape(*inject.shape)] + [shape(face // 2, columns)] * GROUP + [shape(*passed.shape, dtype=passed.dtype)],
         [
             pltpu.VMEM((GROUP, face // 2, columns), F32),
             pltpu.VMEM(inject.shape, F32),
@@ -326,9 +312,9 @@
             pltpu.SMEM((sections, columns), jnp.int32),
             pltpu.SemaphoreType.DMA,
         ],
-        2 * energies * face * orbitals * columns,
-        2 * energies * face * orbitals + 2 * received.size,
-    )(received, inject, face_rows, ready)
+        1.4,
+        aliases={3: 1 + GROUP},
+    )(received, inject, face_rows, passed)
 
 
 def deal(items, outs):
@@ -345,7 +331,7 @@
     return unpack(shift.astype(F32)) + times((parts[0, j], parts[1, j]), two_parts(state))
 
 
-def total_kernel(own, near, across, far, parts, out, shifts):
+def total_kernel(own, near, across, far, parts, _map, out, _same_map, shifts):
     collect((own, near, across, far), shifts)
     state = unpack(shifts[0].astype(F32))
     for j in range(1, GROUP):
@@ -353,32 +339,42 @@
     out[...] = pack(state).astype(BF16)
 
 
-def plane_total(shifts, parts):
+def plane_total(shifts, parts, passed):
     half, columns = shifts[0].shape
     return call(
         total_kernel,
         "plane_total",
-        [IN_VMEM] * (GROUP + 1),
-        shape(half, columns),
+        [IN_VMEM] * (GROUP + 1) + [IN_PLACE],
+        [shape(half, columns), shape(*passed.shape, dtype=passed.dtype)],
         [pltpu.VMEM((GROUP, half, columns), BF16)],
-        3 * parts.size * columns,
-        2 * parts.size,
-    )(*shifts, parts)
-
-
-def entering_kernel(count, *refs):
-    below, maps = refs[:count], refs[count : 3 * count - 2]
-    parts, _image = refs[3 * count - 2 : 3 * count]
-    arrived, out = refs[3 * count : 3 * count + GROUP], refs[3 * count + GROUP : -2]
-    shifts, held = refs[-2:]
+        0.9,
+        aliases={GROUP + 1: 1},
+    )(*shifts, parts, passed)
+
+
+def pair_kernel(total, below, whole, out):
+    state = unpack(below[...].astype(F32))
+    state = unpack(total[...].astype(F32)) + times((whole[0], whole[1]), two_parts(state))
+    out[...] = pack(state).astype(BF16)
+
+
+def pair_total(total, below, whole):
+    return call(pair_kernel, "pair_total", [IN_VMEM] * 3, shape(*total.shape), [], 0.5)(total, below, whole)
+
+
+def entering_kernel(below, second, mine_map, other_map, parts, _image, *refs):
+    arrived, out = refs[:GROUP], refs[GROUP : 2 * GROUP]
+    shifts, held = refs[2 * GROUP :]
     collect(arrived, shifts)
+    twice = unpack(second[...].astype(F32)).astype(BF16)
+    mine, other = dot(mine_map[...], twice), dot(other_map[...], twice)
     first_core = place() % CORES == 0
-    state = unpack(below[-1][...].astype(F32))
-    for k in range(count - 2, -1, -1):
-        high, low = two_parts(state)
-        mine, other = (dot(half[...], high) + dot(half[...], low) for half in maps[2 * k : 2 * k + 2])
-        top, bottom = jnp.where(first_core, mine, other), jnp.where(first_core, other, mine)
-        state = unpack(below[k][...].astype(F32)) + jnp.concatenate([top, bottom], axis=0)
+    top, bottom = jnp.where(first_core, mine, other), jnp.where(first_core, other, mine)
+    state = unpack(below[...].astype(F32)) + jnp.concatenate([top, bottom], axis=0)
+    sweep_plane(state, parts, shifts, held, out)
+
+
+def sweep_plane(state, parts, shifts, held, out):
     held[0] = pack(state)
     for j in range(1, GROUP):
         state = step(parts, j - 1, shifts[j - 1], state)
@@ -386,18 +382,34 @@
     deal(held, out)
 
 
-def entering(below, maps, parts, shifts, tie):
-    half, columns = below[0].shape
-    count = len(below)
-    return call(
-        functools.partial(entering_kernel, count),
+def entering(below, second, maps, parts, shifts, tie):
+    half, columns = below.shape
+    return call(
+        entering_kernel,
         "entering",
-        [IN_VMEM] * (3 * count - 1) + [IN_PLACE] + [IN_VMEM] * GROUP,
+        [IN_VMEM] * 5 + [IN_PLACE] + [IN_VMEM] * GROUP,
         [shape(half, columns)] * GROUP,
         [pltpu.VMEM((GROUP, half, columns), BF16), pltpu.VMEM((GROUP, half, columns), F32)],
-        4 * parts.size * columns,
-        2 * parts.size,
-    )(*below, *maps, parts, tie, *shifts)
+        1.4,
+    )(below, second, *maps, parts, tie, *shifts)
+
+
+def entering_from_kernel(base, parts, *refs):
+    shifts, held = refs[2 * GROUP :]
+    collect(refs[:GROUP], shifts)
+    sweep_plane(unpack(base[...]), parts, shifts, held, refs[GROUP : 2 * GROUP])
+
+
+def entering_from(base, parts, shifts):
+    half, columns = base.shape
+    return call(
+        entering_from_kernel,
+        "entering",
+        [IN_VMEM] * (2 + GROUP),
+        [shape(half, columns)] * GROUP,
+        [pltpu.VMEM((GROUP, half, columns), BF16), pltpu.VMEM((GROUP, half, columns), F32)],
+        1.4,
+    )(base, parts, *shifts)
 
 
 def waves_kernel(own, near, across, far, prop, image, out, arrived):
@@ -420,8 +432,7 @@
         [IN_VMEM] * (GROUP + 2),
         shape(*image.shape),
         [pltpu.VMEM((GROUP, half, columns), BF16)],
-        2 * prop.size * columns,
-        2 * prop.size + 6 * image.size,
+        1.3,
     )(*arrived, prop, image)
 
 
@@ -451,16 +462,8 @@
     return jnp.concatenate([packed[:, :half], packed[:, half:]], axis=0)
 
 
-def maps_below(total_map, sections):
-    out = []
-    for k in range(1, sections // GROUP - 1):
-        half = lax.ppermute(total_map, "sec", up_shift(sections, k))
-        out += [half, to_near(half, sections)]
-    return out
-
-
-def totals_below(total, sections):
-    return [lax.ppermute(total, "sec", up_shift(sections, k)) for k in range(1, sections // GROUP)]
+def upward(item, k, sections):
+    return lax.ppermute(item, "sec", up_shift(sections, k))
 
 
 def scan_below(total_map, total, sections):
@@ -474,7 +477,7 @@
         joined = dot_wide(joined, other_map)
         stride *= 2
     half = shift.shape[0] // 2
-    return [jnp.concatenate([shift[:half], shift[half:]], axis=1)]
+    return jnp.concatenate([shift[:half], shift[half:]], axis=1)
 
 
 def per_device(green, injected, coupling, pattern, owner, pair_blocks):
@@ -487,20 +490,25 @@
     )
     across = to_across(other_map, sections)
     near = to_near(own_map, sections)
+    received = lax.all_to_all(outgoing, "sec", split_axis=0, concat_axis=0, tiled=True)
+    prop, face_rows = propagator(tiles, green, coupling)
+
+    source, *quarters, across = placed_source(received, inject, face_rows, across)
+    shifts = exchange(*quarters, sections)
     far = to_near(across, sections)
-    received = lax.all_to_all(outgoing, "sec", split_axis=0, concat_axis=0, tiled=True)
-
     few = sections // GROUP <= 4
-    total_map, parts = chain([own_map, near, across, far], few)
-    maps = maps_below(total_map, sections) if few else []
-    prop, face_rows = propagator(tiles, green, coupling, total_map)
-
-    source, *quarters = placed_source(received, inject, face_rows, total_map)
-    shifts = exchange(*quarters, sections)
-    total = plane_total(shifts, parts)
-    below = totals_below(total, sections) if few else scan_below(total_map, total, sections)
+    total_map, whole, parts = chain([own_map, near, across, far], few)
+    total, total_map = plane_total(shifts, parts, total_map)
     image = images(green, source)
-    arrived = exchange(*entering(below, maps, parts, shifts, image), sections)
+    if few:
+        below = upward(total, 1, sections)
+        map_below = upward(total_map, 1, sections)
+        second = upward(pair_total(total, below, whole), 2, sections)
+        maps = (map_below, to_near(map_below, sections))
+        entered = entering(below, second, maps, parts, shifts, image)
+    else:
+        entered = entering_from(scan_below(total_map, total, sections), parts, shifts)
+    arrived = exchange(*entered, sections)
     return final_waves(arrived, prop, image)[None]
 
 

time: 69.6 us -> 58.1 us (0.83)
  waiting for transfers between devices: 18 us -> 14.2 us
  starting transfers between devices: 27.2 us -> 23.5 us
  Pallas kernels: 18.5 us -> 15.5 us
  local copies, waits for them, and re-layouts: 5.21 us -> 4.43 us
    ppermute x3, waiting for transfers between devices: 15.7 us -> 10.4 us  [to_across(): lax.ppermute(item, 'sec', [(s, s // GROUP * GROUP + (s % GROUP + CORES) %...]
    ppermute x5 -> x3, starting transfers between devices: 13.4 us -> 9.92 us  [upward(): return lax.ppermute(item, 'sec', up_shift(sections, k))]
    pallas_call x4 -> x5, Pallas kernels: 8.82 us -> 5.31 us  [the longest x1 1.94 us: propagator(): call(prop_kernel, 'prop', [IN_SMEM, IN_VMEM, IN_VMEM], [shape(energies, o...]
    ppermute x2, starting transfers between devices: 2.3 us -> 0.52 us  [to_far(): lax.ppermute(item, 'sec', [(s, s // GROUP * GROUP + (s % GROUP + CORES) %...]
    all_to_all x1, waiting for transfers between devices: 0.01 us -> 1.77 us  [per_device(): lax.all_to_all(outgoing, 'sec', split_axis=0, concat_axis=0, tiled=True)]
    ppermute x6 -> x5, waiting for transfers between devices: 1.54 us -> 0.01 us  [to_near(): return lax.ppermute(item, 'sec', [(s, s ^ 1) for s in range(sections)])]
    ppermute x3, starting transfers between devices: 3.34 us -> 4.62 us  [to_across(): lax.ppermute(item, 'sec', [(s, s // GROUP * GROUP + (s % GROUP + CORES) %...]
    ppermute x2, waiting for transfers between devices: 0.71 us -> 1.77 us  [to_far(): lax.ppermute(item, 'sec', [(s, s // GROUP * GROUP + (s % GROUP + CORES) %...]
  transfers between devices with their start and end apart: 17 -> 14, of which waited for: 5 -> 7; matrix products, arithmetic and copies ran while one was open for 0% -> 0% of each run, Pallas kernels for 14% -> 10%
where the time goes in v7:
time: 58.1 us; the launch traced here: 57.8 us
  starting transfers between devices  23.5 us (40%)
  Pallas kernels  15.5 us (27%)
  waiting for transfers between devices  14.2 us (24%)
  local copies, waits for them, and re-layouts  4.43 us (8%)
    ppermute x3, waiting for transfers between devices, to_across(): lax.ppermute(item, 'sec', [(s, s // GROUP * GROUP + (s % GROUP + CORES) %...  10.4 us
    ppermute x3, starting transfers between devices, upward(): return lax.ppermute(item, 'sec', up_shift(sections, k))  9.92 us
    all_to_all x1, starting transfers between devices, per_device(): lax.all_to_all(outgoing, 'sec', split_axis=0, concat_axis=0, tiled=True)  7.5 us
    pallas_call x1, Pallas kernels, pairs_and_maps(): call(first_kernel, 'pairs_and_maps', [IN_HBM] * 6, [shape(sections, CAP *...  6.19 us
    ppermute x3, starting transfers between devices, to_across(): lax.ppermute(item, 'sec', [(s, s // GROUP * GROUP + (s % GROUP + CORES) %...  4.62 us
    unnamed x16, local copies, waits for them, and re-layouts  4.43 us
    pallas_call x1, Pallas kernels, propagator(): call(prop_kernel, 'prop', [IN_SMEM, IN_VMEM, IN_VMEM], [shape(energies, o...  1.94 us
    ppermute x2, waiting for transfers between devices, to_far(): lax.ppermute(item, 'sec', [(s, s // GROUP * GROUP + (s % GROUP + CORES) %...  1.77 us
  transfers between devices with their start and end apart: 14, of which 7 were waited for; matrix products, arithmetic and copies ran while one was open for 0% of the time, Pallas kernels for 10%

profile of v7, /device:TPU:0, one launch (start us, length us, event | category | flops | bytes accessed | tf_op | source)
XLA Modules:
  0.0 57.8 jit_solution(13163217607462717969)
XLA Ops:
  0.0 6.2 %pairs_and_maps.1 = (bf16[16,144,128]{2,1,0:T(8,128)(2,1)}, f32[256,256]{1,0:T(8,128)}, f32[256,256]{1,0:T(8,128)}) custom-call(s32[16]{0:T(128)} %bitcast.19, s32[2,16]{1,0:T(2,128)} %bitcast.18, s32[2,8]{1,0:T(2,128)} %bitcast.16, bf16[2,1024,1024]{2,1,0:T(8,128)(2,1)} %bitcast.9, bf16[2,1024,128]{2,1,0:T(8,128)(2,1)} %bitcast.14, bf16[1024,256]{1,0:T(8,128)(2,1)} %bitcast.12), custom_call_target="tpu_custom_call" | custom-call | flops 6440000000 | tf_op jit(solution)/shard_map/pairs_and_maps/pallas_call | solution.py:169
  6.2 0.0 copy-start.3
  6.2 7.5 %all-to-all-start = ((bf16[16,144,128]{2,1,0:T(8,128)(2,1)}), bf16[16,144,128]{2,1,0:T(8,128)(2,1)S(1)}, u32[]{:S(2)}, u32[]{:S(2)}) async-start(bf16[16,144,128]{2,1,0:T(8,128)(2,1)} %get-tuple-element.25), calls=%async_computation | async-start | bytes 1179648 | tf_op jit(solution)/shard_map/all_to_all | solution.py:493
  13.7 1.9 %collective-permute-start = (f32[256,256]{1,0:T(8,128)}, f32[256,256]{1,0:T(8,128)S(1)}, u32[]{:S(2)}, u32[]{:S(2)}) collective-permute-start(f32[256,256]{1,0:T(8,128)} %get-tuple-element.27), channel_id=1, source_target_pairs={{0,2},{1,3},{2,0},{3,1},{4,6},{5,7},{6,4},{7,5},{8,10},{9,11},{10,... | collective-permute-start | bytes 786440 | tf_op jit(solution)/shard_map/ppermute | solution.py:444
  15.6 0.0 collective-permute-start.4
  15.7 0.0 copy-done.2
  15.7 0.0 copy-done.5
  15.7 0.0 copy-start
  15.7 2.2 %copy-done = bf16[1,2,1024,1024]{3,2,1,0:T(8,128)(2,1)S(1)} copy-done((bf16[1,2,1024,1024]{3,2,1,0:T(8,128)(2,1)S(1)}, bf16[1,2,1024,1024]{3,2,1,0:T(8,128)(2,1)}, u32[]{:S(2)}) %copy-start) | copy-done | bytes 4194328
  17.9 1.9 %prop.1 = (bf16[2,1024,256]{2,1,0:T(8,128)(2,1)S(1)}, bf16[2,256,1024]{2,1,0:T(8,128)(2,1)S(1)}) custom-call(s32[2,8]{1,0:T(2,128)S(1)} %bitcast.17, bf16[2,1024,1024]{2,1,0:T(8,128)(2,1)S(1)} %bitcast.10, bf16[1024,256]{1,0:T(8,128)(2,1)S(1)} %bitcast.13), custom_call_target="tpu_custom_call" | custom-call | flops 1840000000 | tf_op jit(solution)/shard_map/prop/pallas_call | solution.py:206
  19.8 0.0 copy-start.6
  19.8 1.0 %copy-done.6 = bf16[2,256,1024]{2,1,0:T(8,128)(2,1)} copy-done((bf16[2,256,1024]{2,1,0:T(8,128)(2,1)}, bf16[2,256,1024]{2,1,0:T(8,128)(2,1)S(1)}, u32[]{:S(2)}) %copy-start.6) | copy-done | bytes 1048600
  20.8 6.7 %collective-permute-done._map = f32[256,256]{1,0:T(8,128)S(1)} collective-permute-done((f32[256,256]{1,0:T(8,128)}, f32[256,256]{1,0:T(8,128)S(1)}, u32[]{:S(2)}, u32[]{:S(2)}) %collective-permute-start) | collective-permute-done | bytes 262176 | tf_op jit(solution)/shard_map/ppermute | solution.py:444
  27.5 1.8 %all-to-all-done.received = bf16[16,144,128]{2,1,0:T(8,128)(2,1)S(1)} async-done(((bf16[16,144,128]{2,1,0:T(8,128)(2,1)}), bf16[16,144,128]{2,1,0:T(8,128)(2,1)S(1)}, u32[]{:S(2)}, u32[]{:S(2)}) %all-to-all-start) | async-done | bytes 589856 | tf_op jit(solution)/shard_map/all_to_all | solution.py:493
  29.3 0.0 copy-done.3
  29.3 1.2 %copy-done.7 = bf16[2,256,1024]{2,1,0:T(8,128)(2,1)S(1)} copy-done((bf16[2,256,1024]{2,1,0:T(8,128)(2,1)S(1)}, bf16[2,256,1024]{2,1,0:T(8,128)(2,1)}, u32[]{:S(2)}) %copy-start.7) | copy-done | bytes 1048600
  30.5 1.4 %source_and_face.1 = (bf16[2,1024,128]{2,1,0:T(8,128)(2,1)S(1)}, bf16[128,128]{1,0:T(8,128)(2,1)S(1)}, bf16[128,128]{1,0:T(8,128)(2,1)S(1)}, bf16[128,128]{1,0:T...) custom-call(bf16[16,144,128]{2,1,0:T(8,128)(2,1)S(1)} %all-to-all-done.rec, ...), custom_call_target="tpu_custom_call", output_to_operand_aliasing={{5}: (3, {})} | custom-call | flops 1610000000 | tf_op jit(solution)/shard_map/source_and_face/pallas_call | solution.py:303
  31.9 0.1 collective-permute-start.5
  32.0 0.5 collective-permute-start.1
  32.5 0.9 %collective-permute-start.2 = (bf16[128,128]{1,0:T(8,128)(2,1)S(1)}, bf16[128,128]{1,0:T(8,128)(2,1)S(1)}, u32[]{:S(2)}, u32[]{:S(2)}) collective-permute-start(bf16[128,128]{1,0:T(8,128)(2,1)S(1)} %get-tuple-element.30), channel_id=1, source_target_pairs={{0,2},{1,3},{2,0},{3,1},{4,6},{5,7},{6,4},{7,5},{8,10},{9,11},{10,... | collective-permute-start | bytes 98312 | tf_op jit(solution)/shard_map/ppermute | solution.py:444
  33.4 0.5 collective-permute-start.3
  33.9 0.0 collective-permute-done.4.near
  33.9 0.0 collective-permute-done.5.far
  33.9 0.0 copy-done.4
  33.9 0.9 %chain_maps.1 = (bf16[128,256]{1,0:T(8,128)(2,1)S(1)}, bf16[2,256,256]{2,1,0:T(8,128)(2,1)S(1)}, bf16[2,4,256,256]{3,2,1,0:T(8,128)(2,1)S(1)}) custom-call(f32[256,256]{1,0:T(8,128)S(1)} %copy-done.4, f32[256,256]{1,0:T(8,128)S(1)} %collective-permute-done.4.near, f32[256,256]{1,0:T(8,128)S(1)} %get-tuple-element.33.across, ...), custom_call_target="tpu_custom_call" | custom-call | flops 1035000000 | tf_op jit(solution)/shard_map/chain_maps/pallas_call | solution.py:253
  34.8 0.0 collective-permute-done.1.near.refs_1_
  34.8 1.6 %collective-permute-done.2.across.refs_2_ = bf16[128,128]{1,0:T(8,128)(2,1)S(1)} collective-permute-done((bf16[128,128]{1,0:T(8,128)(2,1)S(1)}, bf16[128,128]{1,0:T(8,128)(2,1)S(1)}, u32[]{:S(2)}, u32[]{:S(2)}) %collective-permute-start.2) | collective-permute-done | bytes 32800 | tf_op jit(solution)/shard_map/ppermute | solution.py:444
  36.4 0.4 collective-permute-done.3.far.refs_3_
  36.8 0.9 %plane_total.1 = (bf16[128,128]{1,0:T(8,128)(2,1)S(1)}, bf16[128,256]{1,0:T(8,128)(2,1)S(1)}) custom-call(bf16[128,128]{1,0:T(8,128)(2,1)S(1)} %get-tuple-element.28.own.refs_0_, bf16[128,128]{1,0:T(8,128)(2,1)S(1)} %collective-permute-done.1.near.refs_1_, ...), custom_call_target="tpu_custom_call", output_to_operand_aliasing={{1}: (5, {})} | custom-call | flops 1035000000 | tf_op jit(solution)/shard_map/plane_total/pallas_call | solution.py:344
  37.7 3.8 %collective-permute-start.6 = (bf16[128,128]{1,0:T(8,128)(2,1)S(1)}, bf16[128,128]{1,0:T(8,128)(2,1)S(1)}, u32[]{:S(2)}, u32[]{:S(2)}) collective-permute-start(bf16[128,128]{1,0:T(8,128)(2,1)S(1)} %get-tuple-element.36.total), channel_id=1, source_target_pairs={{0,4},{1,5},{2,6},{3,7},{4,8},{5,9},{6,10},{7,11},{8,12},{9,13},{1... | collective-permute-start | bytes 98312 | tf_op jit(solution)/shard_map/ppermute | solution.py:466
  41.5 2.8 %collective-permute-start.8 = (bf16[128,256]{1,0:T(8,128)(2,1)S(1)}, bf16[128,256]{1,0:T(8,128)(2,1)S(1)}, u32[]{:S(2)}, u32[]{:S(2)}) collective-permute-start(bf16[128,256]{1,0:T(8,128)(2,1)S(1)} %get-tuple-element.38), channel_id=1, source_target_pairs={{0,4},{1,5},{2,6},{3,7},{4,8},{5,9},{6,10},{7,11},{8,12},{9,13},{1... | collective-permute-start | bytes 196616 | tf_op jit(solution)/shard_map/ppermute | solution.py:466
  44.3 0.0 collective-permute-done.6.below
  44.3 0.4 pair_total.1
  44.7 3.3 %collective-permute-start.7 = (bf16[128,128]{1,0:T(8,128)(2,1)S(1)}, bf16[128,128]{1,0:T(8,128)(2,1)S(1)}, u32[]{:S(2)}, u32[]{:S(2)}) collective-permute-start(bf16[128,128]{1,0:T(8,128)(2,1)S(1)} %pair_total.1), channel_id=1, source_target_pairs={{0,8},{1,9},{2,10},{3,11},{4,12},{5,13},{6,14},{7,15},{16,24},{17,... | collective-permute-start | bytes 98312 | tf_op jit(solution)/shard_map/ppermute | solution.py:466
  48.0 0.0 collective-permute-done.8.mine_map
  48.1 0.1 collective-permute-start.9
  48.1 0.0 copy-done.1
  48.1 1.2 %image.1._image = f32[2,1024,128]{2,1,0:T(8,128)S(1)} custom-call(bf16[2,1024,1024]{2,1,0:T(8,128)(2,1)S(1)} %bitcast.11, bf16[2,1024,128]{2,1,0:T(8,128)(2,1)S(1)} %get-tuple-element.39.source), custom_call_target="tpu_custom_call" | custom-call | flops 1380000000 | tf_op jit(solution)/shard_map/image/pallas_call | solution.py:222
  49.4 0.2 collective-permute-done.7.second
  49.6 0.0 collective-permute-done.9.other_map
  49.6 1.2 %entering.1 = (bf16[128,128]{1,0:T(8,128)(2,1)S(1)}, bf16[128,128]{1,0:T(8,128)(2,1)S(1)}, bf16[128,128]{1,0:T(8,128)(2,1)S(1)}, bf16[128,128]{1,0:T(8,128)(2,1)S(1)}) custom-call(bf16[128,128]{1,0:T(8,128)(2,1)S(1)} %collective-permute-done.6.below, bf16[128,128]{1,0:T(8,128)(2,1)S(1)} %collective-permute-done.7.second, ...), custom_call_target="tpu_custom_call" | custom-call | flops 1610000000 | tf_op jit(solution)/shard_map/entering/pallas_call | solution.py:387
  50.8 0.3 collective-permute-start.10
  51.1 1.8 %collective-permute-start.11 = (bf16[128,128]{1,0:T(8,128)(2,1)S(1)}, bf16[128,128]{1,0:T(8,128)(2,1)S(1)}, u32[]{:S(2)}, u32[]{:S(2)}) collective-permute-start(bf16[128,128]{1,0:T(8,128)(2,1)S(1)} %get-tuple-element.42), channel_id=1, source_target_pairs={{0,2},{1,3},{2,0},{3,1},{4,6},{5,7},{6,4},{7,5},{8,10},{9,11},{10,... | collective-permute-start | bytes 98312 | tf_op jit(solution)/shard_map/ppermute | solution.py:444
  52.9 0.0 collective-permute-start.12
  52.9 0.0 collective-permute-done.10.near
  52.9 2.1 %collective-permute-done.11.across = bf16[128,128]{1,0:T(8,128)(2,1)S(1)} collective-permute-done((bf16[128,128]{1,0:T(8,128)(2,1)S(1)}, bf16[128,128]{1,0:T(8,128)(2,1)S(1)}, u32[]{:S(2)}, u32[]{:S(2)}) %collective-permute-start.11) | collective-permute-done | bytes 32800 | tf_op jit(solution)/shard_map/ppermute | solution.py:444
  55.1 1.4 %collective-permute-done.12.far = bf16[128,128]{1,0:T(8,128)(2,1)S(1)} collective-permute-done((bf16[128,128]{1,0:T(8,128)(2,1)S(1)}, bf16[128,128]{1,0:T(8,128)(2,1)S(1)}, u32[]{:S(2)}, u32[]{:S(2)}) %collective-permute-start.12) | collective-permute-done | bytes 32800 | tf_op jit(solution)/shard_map/ppermute | solution.py:448
  56.5 1.3 %waves.1 = bf16[2,1024,128]{2,1,0:T(8,128)(2,1)} custom-call(bf16[128,128]{1,0:T(8,128)(2,1)S(1)} %get-tuple-element.40.own, bf16[128,128]{1,0:T(8,128)(2,1)S(1)} %collective-permute-done.10.near, bf16[128,128]{1,0:T(8,128)(2,1)S(1)} %collective-permute-done.11.across, bf16[128,128]{1,0:T(8,128)(2,1)S(1)} %collective-permute-done.12.far, ...), custom_call_target="tpu_custom_call" | custom-call | flops 1495000064 | tf_op jit(solution)/shard_map/waves/pallas_call | solution.py:429
  (5 shorter events, 0.0 us)
Async XLA Ops:
  0.0 15.7 %copy-start.2 = (bf16[1,1024,256]{2,1,0:T(8,128)(2,1)S(1)}, bf16[1,1024,256]{2,1,0:T(8,128)(2,1)}, u32[]{:S(2)}) copy-start(bf16[1,1024,256]{2,1,0:T(8,128)(2,1)} %param.8) | copy-start | bytes 1572868
  0.0 15.7 %copy-start.5 = (s32[1,8,2]{1,2,0:T(2,128)S(1)}, s32[1,8,2]{1,2,0:T(2,128)}, u32[]{:S(2)}) copy-start(s32[1,8,2]{1,2,0:T(2,128)} %param.9) | copy-start | bytes 196
  6.2 23.1 %copy-start.3 = (bf16[1,2,1024,128]{3,2,1,0:T(8,128)(2,1)S(1)}, bf16[1,2,1024,128]{3,2,1,0:T(8,128)(2,1)}, u32[]{:S(2)}) copy-start(bf16[1,2,1024,128]{3,2,1,0:T(8,128)(2,1)} %param.7) | copy-start | bytes 1572868
  6.2 23.1 %all-to-all-start = ((bf16[16,144,128]{2,1,0:T(8,128)(2,1)}), bf16[16,144,128]{2,1,0:T(8,128)(2,1)S(1)}, u32[]{:S(2)}, u32[]{:S(2)}) async-start(bf16[16,144,128]{2,1,0:T(8,128)(2,1)} %get-tuple-element.25), calls=%async_computation | async-start | bytes 1179648 | tf_op jit(solution)/shard_map/all_to_all | solution.py:493
  13.7 13.8 %collective-permute-start = (f32[256,256]{1,0:T(8,128)}, f32[256,256]{1,0:T(8,128)S(1)}, u32[]{:S(2)}, u32[]{:S(2)}) collective-permute-start(f32[256,256]{1,0:T(8,128)} %get-tuple-element.27), channel_id=1, source_target_pairs={{0,2},{1,3},{2,0},{3,1},{4,6},{5,7},{6,4},{7,5},{8,10},{9,11},{10,... | collective-permute-start | bytes 786440 | tf_op jit(solution)/shard_map/ppermute | solution.py:444
  15.6 18.3 %collective-permute-start.4 = (f32[256,256]{1,0:T(8,128)}, f32[256,256]{1,0:T(8,128)S(1)}, u32[]{:S(2)}, u32[]{:S(2)}) collective-permute-start(f32[256,256]{1,0:T(8,128)} %get-tuple-element.32.own), channel_id=1, source_target_pairs={{0,1},{1,0},{2,3},{3,2},{4,5},{5,4},{6,7},{7,6},{8,9},{9,8},{10,11... | collective-permute-start | bytes 786440 | tf_op jit(solution)/shard_map/ppermute | solution.py:440
  15.7 2.2 %copy-start = (bf16[1,2,1024,1024]{3,2,1,0:T(8,128)(2,1)S(1)}, bf16[1,2,1024,1024]{3,2,1,0:T(8,128)(2,1)}, u32[]{:S(2)}) copy-start(bf16[1,2,1024,1024]{3,2,1,0:T(8,128)(2,1)} %param.6) | copy-start | bytes 12582916
  19.8 1.0 %copy-start.6 = (bf16[2,256,1024]{2,1,0:T(8,128)(2,1)}, bf16[2,256,1024]{2,1,0:T(8,128)(2,1)S(1)}, u32[]{:S(2)}) copy-start(bf16[2,256,1024]{2,1,0:T(8,128)(2,1)S(1)} %get-tuple-element.26.face_rows) | copy-start | bytes 3145732
  20.8 13.1 %copy-start.4 = (f32[256,256]{1,0:T(8,128)S(1)}, f32[256,256]{1,0:T(8,128)}, u32[]{:S(2)}) copy-start(f32[256,256]{1,0:T(8,128)} %get-tuple-element.32.own) | copy-start | bytes 786436
  29.3 1.2 %copy-start.7 = (bf16[2,256,1024]{2,1,0:T(8,128)(2,1)S(1)}, bf16[2,256,1024]{2,1,0:T(8,128)(2,1)}, u32[]{:S(2)}) copy-start(bf16[2,256,1024]{2,1,0:T(8,128)(2,1)} %copy-done.6) | copy-start | bytes 3145732
  31.9 2.0 %collective-permute-start.5 = (f32[256,256]{1,0:T(8,128)S(1)}, f32[256,256]{1,0:T(8,128)S(1)}, u32[]{:S(2)}, u32[]{:S(2)}) collective-permute-start(f32[256,256]{1,0:T(8,128)S(1)} %get-tuple-element.33.across), channel_id=1, source_target_pairs={{0,1},{1,0},{2,3},{3,2},{4,5},{5,4},{6,7},{7,6},{8,9},{9,8},{10,11... | collective-permute-start | bytes 786440 | tf_op jit(solution)/shard_map/ppermute | solution.py:440
  32.0 2.8 %collective-permute-start.1 = (bf16[128,128]{1,0:T(8,128)(2,1)S(1)}, bf16[128,128]{1,0:T(8,128)(2,1)S(1)}, u32[]{:S(2)}, u32[]{:S(2)}) collective-permute-start(bf16[128,128]{1,0:T(8,128)(2,1)S(1)} %get-tuple-element.29), channel_id=1, source_target_pairs={{0,1},{1,0},{2,3},{3,2},{4,5},{5,4},{6,7},{7,6},{8,9},{9,8},{10,11... | collective-permute-start | bytes 98312 | tf_op jit(solution)/shard_map/ppermute | solution.py:440
  32.5 3.9 %collective-permute-start.2 = (bf16[128,128]{1,0:T(8,128)(2,1)S(1)}, bf16[128,128]{1,0:T(8,128)(2,1)S(1)}, u32[]{:S(2)}, u32[]{:S(2)}) collective-permute-start(bf16[128,128]{1,0:T(8,128)(2,1)S(1)} %get-tuple-element.30), channel_id=1, source_target_pairs={{0,2},{1,3},{2,0},{3,1},{4,6},{5,7},{6,4},{7,5},{8,10},{9,11},{10,... | collective-permute-start | bytes 98312 | tf_op jit(solution)/shard_map/ppermute | solution.py:444
  33.4 14.7 %copy-start.1 = (bf16[1,2,1024,1024]{3,2,1,0:T(8,128)(2,1)S(1)}, bf16[1,2,1024,1024]{3,2,1,0:T(8,128)(2,1)}, u32[]{:S(2)}) copy-start(bf16[1,2,1024,1024]{3,2,1,0:T(8,128)(2,1)} %param.6) | copy-start | bytes 12582916
  33.4 3.4 %collective-permute-start.3 = (bf16[128,128]{1,0:T(8,128)(2,1)S(1)}, bf16[128,128]{1,0:T(8,128)(2,1)S(1)}, u32[]{:S(2)}, u32[]{:S(2)}) collective-permute-start(bf16[128,128]{1,0:T(8,128)(2,1)S(1)} %get-tuple-element.31), channel_id=1, source_target_pairs={{0,3},{1,2},{2,1},{3,0},{4,7},{5,6},{6,5},{7,4},{8,11},{9,10},{10,... | collective-permute-start | bytes 98312 | tf_op jit(solution)/shard_map/ppermute | solution.py:448
  37.7 6.6 %collective-permute-start.6 = (bf16[128,128]{1,0:T(8,128)(2,1)S(1)}, bf16[128,128]{1,0:T(8,128)(2,1)S(1)}, u32[]{:S(2)}, u32[]{:S(2)}) collective-permute-start(bf16[128,128]{1,0:T(8,128)(2,1)S(1)} %get-tuple-element.36.total), channel_id=1, source_target_pairs={{0,4},{1,5},{2,6},{3,7},{4,8},{5,9},{6,10},{7,11},{8,12},{9,13},{1... | collective-permute-start | bytes 98312 | tf_op jit(solution)/shard_map/ppermute | solution.py:466
  41.5 6.5 %collective-permute-start.8 = (bf16[128,256]{1,0:T(8,128)(2,1)S(1)}, bf16[128,256]{1,0:T(8,128)(2,1)S(1)}, u32[]{:S(2)}, u32[]{:S(2)}) collective-permute-start(bf16[128,256]{1,0:T(8,128)(2,1)S(1)} %get-tuple-element.38), channel_id=1, source_target_pairs={{0,4},{1,5},{2,6},{3,7},{4,8},{5,9},{6,10},{7,11},{8,12},{9,13},{1... | collective-permute-start | bytes 196616 | tf_op jit(solution)/shard_map/ppermute | solution.py:466
  44.7 4.9 %collective-permute-start.7 = (bf16[128,128]{1,0:T(8,128)(2,1)S(1)}, bf16[128,128]{1,0:T(8,128)(2,1)S(1)}, u32[]{:S(2)}, u32[]{:S(2)}) collective-permute-start(bf16[128,128]{1,0:T(8,128)(2,1)S(1)} %pair_total.1), channel_id=1, source_target_pairs={{0,8},{1,9},{2,10},{3,11},{4,12},{5,13},{6,14},{7,15},{16,24},{17,... | collective-permute-start | bytes 98312 | tf_op jit(solution)/shard_map/ppermute | solution.py:466
  48.1 1.6 %collective-permute-start.9 = (bf16[128,256]{1,0:T(8,128)(2,1)S(1)}, bf16[128,256]{1,0:T(8,128)(2,1)S(1)}, u32[]{:S(2)}, u32[]{:S(2)}) collective-permute-start(bf16[128,256]{1,0:T(8,128)(2,1)S(1)} %collective-permute-done.8.mine_map), channel_id=1, source_target_pairs={{0,1},{1,0},{2,3},{3,2},{4,5},{5,4},{6,7},{7,6},{8,9},{9,8},{10,11... | collective-permute-start | bytes 196616 | tf_op jit(solution)/shard_map/ppermute | solution.py:440
  50.8 2.1 %collective-permute-start.10 = (bf16[128,128]{1,0:T(8,128)(2,1)S(1)}, bf16[128,128]{1,0:T(8,128)(2,1)S(1)}, u32[]{:S(2)}, u32[]{:S(2)}) collective-permute-start(bf16[128,128]{1,0:T(8,128)(2,1)S(1)} %get-tuple-element.41), channel_id=1, source_target_pairs={{0,1},{1,0},{2,3},{3,2},{4,5},{5,4},{6,7},{7,6},{8,9},{9,8},{10,11... | collective-permute-start | bytes 98312 | tf_op jit(solution)/shard_map/ppermute | solution.py:440
  51.1 3.9 %collective-permute-start.11 = (bf16[128,128]{1,0:T(8,128)(2,1)S(1)}, bf16[128,128]{1,0:T(8,128)(2,1)S(1)}, u32[]{:S(2)}, u32[]{:S(2)}) collective-permute-start(bf16[128,128]{1,0:T(8,128)(2,1)S(1)} %get-tuple-element.42), channel_id=1, source_target_pairs={{0,2},{1,3},{2,0},{3,1},{4,6},{5,7},{6,4},{7,5},{8,10},{9,11},{10,... | collective-permute-start | bytes 98312 | tf_op jit(solution)/shard_map/ppermute | solution.py:444
  52.9 3.6 %collective-permute-start.12 = (bf16[128,128]{1,0:T(8,128)(2,1)S(1)}, bf16[128,128]{1,0:T(8,128)(2,1)S(1)}, u32[]{:S(2)}, u32[]{:S(2)}) collective-permute-start(bf16[128,128]{1,0:T(8,128)(2,1)S(1)} %get-tuple-element.43), channel_id=1, source_target_pairs={{0,3},{1,2},{2,1},{3,0},{4,7},{5,6},{6,5},{7,4},{8,11},{9,10},{10,... | collective-permute-start | bytes 98312 | tf_op jit(solution)/shard_map/ppermute | solution.py:448

commit v8 on v6

--- a/solution.py
+++ b/solution.py
@@ -17,7 +17,9 @@
 F32 = jnp.float32
 BF16 = jnp.bfloat16
 VMEM_SMALL = 16 * 1024 * 1024
+VMEM_MOST = 60500000
 VMEM_WHOLE = 63400000
+PEAK = 1.15e9
 
 IN_VMEM = pl.BlockSpec(memory_space=pltpu.VMEM)
 IN_SMEM = pl.BlockSpec(memory_space=pltpu.SMEM)
@@ -29,16 +31,18 @@
     return jax.ShapeDtypeStruct(dims, dtype)
 
 
-def call(body, name, ins, outs, scratch, flops, moved, vmem=VMEM_SMALL):
+def call(body, name, ins, outs, scratch, micros, vmem=VMEM_SMALL, aliases=None):
+    places = list(range(len(outs))) if isinstance(outs, list) else 0
     return pl.pallas_call(
         body,
         name=name,
         in_specs=ins,
         out_shape=outs,
-        out_specs=jax.tree.map(lambda _: IN_VMEM, outs),
+        out_specs=jax.tree.map(lambda k: IN_PLACE if k in (aliases or {}).values() else IN_VMEM, places),
+        input_output_aliases=aliases or {},
         scratch_shapes=scratch,
         compiler_params=pltpu.CompilerParams(vmem_limit_bytes=vmem),
-        cost_estimate=pl.CostEstimate(flops=flops, bytes_accessed=moved, transcendentals=0),
+        cost_estimate=pl.CostEstimate(flops=int(micros * PEAK), bytes_accessed=0, transcendentals=0),
     )
 
 
@@ -182,15 +186,12 @@
             pltpu.SemaphoreType.DMA((energies,)),
             pltpu.SemaphoreType.DMA((5,)),
         ],
-        2 * green.size * (columns + face // 4),
-        2 * green.size,
+        5.6,
         VMEM_WHOLE,
     )(owner, blocks, pattern, green, inject, coupling)
 
 
-def prop_kernel(pattern_in, green, coupling_in, _tie, out, face_rows, pattern, coupling, held, sem, side):
-    energies, orbitals, _ = green.shape
-    face = coupling.shape[1]
+def prop_kernel(pattern_in, green, coupling_in, out, pattern, coupling, held, sem, side):
     tiles = pltpu.make_async_copy(pattern_in, pattern, side.at[0])
     whole = pltpu.make_async_copy(coupling_in, coupling, side.at[1])
     tiles.start()
@@ -202,17 +203,15 @@
     for e, move in enumerate(moves):
         move.wait()
         out[e] = dot(held[e], coupling[...]).astype(BF16)
-        face_rows[e] = held[e, orbitals - face :, :]
-
-
-def propagator(pattern, green, coupling, tie):
+
+
+def propagator(pattern, green, coupling):
     energies, orbitals, _ = green.shape
-    face = coupling.shape[1]
     return call(
         prop_kernel,
         "prop",
-        [IN_HBM] * 3 + [IN_PLACE],
-        [shape(energies, orbitals, face), shape(energies, face, orbitals)],
+        [IN_HBM] * 3,
+        shape(energies, orbitals, coupling.shape[1]),
         [
             pltpu.SMEM(pattern.shape, jnp.int32),
             pltpu.VMEM(coupling.shape, BF16),
@@ -220,10 +219,34 @@
             pltpu.SemaphoreType.DMA((energies,)),
             pltpu.SemaphoreType.DMA((2,)),
         ],
-        2 * green.size * face,
-        2 * green.size,
+        5.0,
         VMEM_WHOLE,
-    )(pattern, green, coupling, tie)
+    )(pattern, green, coupling)
+
+
+def rows_kernel(green, out, sem):
+    face = out.shape[1]
+    moves = [
+        pltpu.make_async_copy(green.at[e, pl.ds(green.shape[1] - face, face)], out.at[e], sem.at[e])
+        for e in range(green.shape[0])
+    ]
+    for move in moves:
+        move.start()
+    for move in moves:
+        move.wait()
+
+
+def face_rows_of(green, face):
+    energies, _, orbitals = green.shape
+    return call(
+        rows_kernel,
+        "face_rows",
+        [IN_HBM],
+        shape(energies, face, orbitals),
+        [pltpu.SemaphoreType.DMA((energies,))],
+        1.5,
+        VMEM_MOST,
+    )(green)
 
 
 def image_kernel(green, source, out):
@@ -238,8 +261,7 @@
         [IN_VMEM] * 2,
         shape(*source.shape, dtype=F32),
         [],
-        2 * green.size * source.shape[2],
-        2 * green.size,
+        1.2,
     )(green, source)
 
 
@@ -269,12 +291,11 @@
         [IN_VMEM] * GROUP,
         [total, shape(2, GROUP, face, face)],
         [pltpu.VMEM((GROUP, face, face), F32), pltpu.VMEM((face, face), F32)],
-        2 * 3 * 3 * face**3,
-        4 * 10 * face * face,
+        0.9,
     )(*maps)
 
 
-def source_kernel(received, inject, face_rows, _map, source, own, near, across, far, quarters, total, heads, targets, sem):
+def source_kernel(received, inject, face_rows, _prop, _map, source, own, near, across, far, _same_map, quarters, total, heads, targets, sem):
     energies, orbitals, columns = inject.shape
     sections = received.shape[0]
     half = quarters.shape[1]
@@ -310,15 +331,15 @@
     deal(quarters, (own, near, across, far))
 
 
-def placed_source(received, inject, face_rows, ready):
+def placed_source(received, inject, face_rows, prop, passed):
     face = face_rows.shape[1]
     energies, orbitals, columns = inject.shape
     sections = received.shape[0]
     return call(
         source_kernel,
         "source_and_face",
-        [IN_VMEM, IN_VMEM, IN_VMEM, IN_PLACE],
-        [shape(*inject.shape)] + [shape(face // 2, columns)] * GROUP,
+        [IN_VMEM, IN_VMEM, IN_VMEM, IN_PLACE, IN_PLACE],
+        [shape(*inject.shape)] + [shape(face // 2, columns)] * GROUP + [shape(*passed.shape, dtype=passed.dtype)],
         [
             pltpu.VMEM((GROUP, face // 2, columns), F32),
             pltpu.VMEM(inject.shape, F32),
@@ -326,9 +347,9 @@
             pltpu.SMEM((sections, columns), jnp.int32),
             pltpu.SemaphoreType.DMA,
         ],
-        2 * energies * face * orbitals * columns,
-        2 * energies * face * orbitals + 2 * received.size,
-    )(received, inject, face_rows, ready)
+        1.4,
+        aliases={4: 1 + GROUP},
+    )(received, inject, face_rows, prop, passed)
 
 
 def deal(items, outs):
@@ -361,8 +382,7 @@
         [IN_VMEM] * (GROUP + 1),
         shape(half, columns),
         [pltpu.VMEM((GROUP, half, columns), BF16)],
-        3 * parts.size * columns,
-        2 * parts.size,
+        0.9,
     )(*shifts, parts)
 
 
@@ -379,6 +399,10 @@
         mine, other = (dot(half[...], high) + dot(half[...], low) for half in maps[2 * k : 2 * k + 2])
         top, bottom = jnp.where(first_core, mine, other), jnp.where(first_core, other, mine)
         state = unpack(below[k][...].astype(F32)) + jnp.concatenate([top, bottom], axis=0)
+    sweep_plane(state, parts, shifts, held, out)
+
+
+def sweep_plane(state, parts, shifts, held, out):
     held[0] = pack(state)
     for j in range(1, GROUP):
         state = step(parts, j - 1, shifts[j - 1], state)
@@ -395,9 +419,26 @@
         [IN_VMEM] * (3 * count - 1) + [IN_PLACE] + [IN_VMEM] * GROUP,
         [shape(half, columns)] * GROUP,
         [pltpu.VMEM((GROUP, half, columns), BF16), pltpu.VMEM((GROUP, half, columns), F32)],
-        4 * parts.size * columns,
-        2 * parts.size,
+        1.4,
     )(*below, *maps, parts, tie, *shifts)
+
+
+def entering_from_kernel(base, parts, *refs):
+    shifts, held = refs[2 * GROUP :]
+    collect(refs[:GROUP], shifts)
+    sweep_plane(unpack(base[...]), parts, shifts, held, refs[GROUP : 2 * GROUP])
+
+
+def entering_from(base, parts, shifts):
+    half, columns = base.shape
+    return call(
+        entering_from_kernel,
+        "entering",
+        [IN_VMEM] * (2 + GROUP),
+        [shape(half, columns)] * GROUP,
+        [pltpu.VMEM((GROUP, half, columns), BF16), pltpu.VMEM((GROUP, half, columns), F32)],
+        1.4,
+    )(base, parts, *shifts)
 
 
 def waves_kernel(own, near, across, far, prop, image, out, arrived):
@@ -420,8 +461,7 @@
         [IN_VMEM] * (GROUP + 2),
         shape(*image.shape),
         [pltpu.VMEM((GROUP, half, columns), BF16)],
-        2 * prop.size * columns,
-        2 * prop.size + 6 * image.size,
+        1.3,
     )(*arrived, prop, image)
 
 
@@ -451,16 +491,8 @@
     return jnp.concatenate([packed[:, :half], packed[:, half:]], axis=0)
 
 
-def maps_below(total_map, sections):
-    out = []
-    for k in range(1, sections // GROUP - 1):
-        half = lax.ppermute(total_map, "sec", up_shift(sections, k))
-        out += [half, to_near(half, sections)]
-    return out
-
-
-def totals_below(total, sections):
-    return [lax.ppermute(total, "sec", up_shift(sections, k)) for k in range(1, sections // GROUP)]
+def upward(item, k, sections):
+    return lax.ppermute(item, "sec", up_shift(sections, k))
 
 
 def scan_below(total_map, total, sections):
@@ -474,7 +506,7 @@
         joined = dot_wide(joined, other_map)
         stride *= 2
     half = shift.shape[0] // 2
-    return [jnp.concatenate([shift[:half], shift[half:]], axis=1)]
+    return jnp.concatenate([shift[:half], shift[half:]], axis=1)
 
 
 def per_device(green, injected, coupling, pattern, owner, pair_blocks):
@@ -487,20 +519,26 @@
     )
     across = to_across(other_map, sections)
     near = to_near(own_map, sections)
+    received = lax.all_to_all(outgoing, "sec", split_axis=0, concat_axis=0, tiled=True)
+    prop = propagator(tiles, green, coupling)
+    face_rows = face_rows_of(green, coupling.shape[1])
+
+    source, *quarters, across = placed_source(received, inject, face_rows, prop, across)
+    shifts = exchange(*quarters, sections)
     far = to_near(across, sections)
-    received = lax.all_to_all(outgoing, "sec", split_axis=0, concat_axis=0, tiled=True)
-
-    few = sections // GROUP <= 4
-    total_map, parts = chain([own_map, near, across, far], few)
-    maps = maps_below(total_map, sections) if few else []
-    prop, face_rows = propagator(tiles, green, coupling, total_map)
-
-    source, *quarters = placed_source(received, inject, face_rows, total_map)
-    shifts = exchange(*quarters, sections)
-    total = plane_total(shifts, parts)
-    below = totals_below(total, sections) if few else scan_below(total_map, total, sections)
+    planes = sections // GROUP
+    total_map, parts = chain([own_map, near, across, far], planes <= 4)
     image = images(green, source)
-    arrived = exchange(*entering(below, maps, parts, shifts, image), sections)
+    if planes <= 4:
+        halves = [upward(total_map, k, sections) for k in range(1, planes - 1)]
+        maps = [half for mine in halves for half in (mine, to_near(mine, sections))]
+        total = plane_total(shifts, parts)
+        below = [upward(total, k, sections) for k in range(1, planes)]
+        entered = entering(below, maps, parts, shifts, image)
+    else:
+        total = plane_total(shifts, parts)
+        entered = entering_from(scan_below(total_map, total, sections), parts, shifts)
+    arrived = exchange(*entered, sections)
     return final_waves(arrived, prop, image)[None]
 
 

time: 69.6 us -> 55.8 us (0.80)
  waiting for transfers between devices: 18 us -> 8.62 us
  local copies, waits for them, and re-layouts: 5.21 us -> 1.25 us
  starting transfers between devices: 27.2 us -> 24.9 us
  Pallas kernels: 18.5 us -> 20.5 us
    ppermute x3, waiting for transfers between devices: 15.7 us -> 6.41 us  [to_across(): lax.ppermute(item, 'sec', [(s, s // GROUP * GROUP + (s % GROUP + CORES) %...]
    unnamed x14 -> x10, local copies, waits for them, and re-layouts: 5.21 us -> 1.25 us
    ppermute x5, starting transfers between devices: 13.4 us -> 11 us  [upward(): return lax.ppermute(item, 'sec', up_shift(sections, k))]
    pallas_call x1 -> x2, Pallas kernels: 5.58 us -> 7.61 us  [the longest x1 5.26 us: propagator(): call(prop_kernel, 'prop', [IN_HBM] * 3, shape(energies, orbitals, couplin...]
    all_to_all x1, waiting for transfers between devices: 0.01 us -> 1.77 us  [per_device(): lax.all_to_all(outgoing, 'sec', split_axis=0, concat_axis=0, tiled=True)]
    ppermute x6, waiting for transfers between devices: 1.54 us -> 0.02 us  [to_near(): return lax.ppermute(item, 'sec', [(s, s ^ 1) for s in range(sections)])]
    ppermute x2, starting transfers between devices: 2.3 us -> 1.24 us  [to_far(): lax.ppermute(item, 'sec', [(s, s // GROUP * GROUP + (s % GROUP + CORES) %...]
    ppermute x6, starting transfers between devices: 0.66 us -> 1.38 us  [to_near(): return lax.ppermute(item, 'sec', [(s, s ^ 1) for s in range(sections)])]
  transfers between devices with their start and end apart: 17 -> 17, of which waited for: 5 -> 4; matrix products, arithmetic and copies ran while one was open for 0% -> 0% of each run, Pallas kernels for 14% -> 22%
where the time goes in v8:
time: 55.8 us; the launch traced here: 55.5 us
  starting transfers between devices  24.9 us (45%)
  Pallas kernels  20.5 us (37%)
  waiting for transfers between devices  8.62 us (15%)
  local copies, waits for them, and re-layouts  1.25 us (2%)
    ppermute x5, starting transfers between devices, upward(): return lax.ppermute(item, 'sec', up_shift(sections, k))  11 us
    all_to_all x1, starting transfers between devices, per_device(): lax.all_to_all(outgoing, 'sec', split_axis=0, concat_axis=0, tiled=True)  7.37 us
    ppermute x3, waiting for transfers between devices, to_across(): lax.ppermute(item, 'sec', [(s, s // GROUP * GROUP + (s % GROUP + CORES) %...  6.41 us
    pallas_call x1, Pallas kernels, pairs_and_maps(): call(first_kernel, 'pairs_and_maps', [IN_HBM] * 6, [shape(sections, CAP *...  5.74 us
    pallas_call x1, Pallas kernels, propagator(): call(prop_kernel, 'prop', [IN_HBM] * 3, shape(energies, orbitals, couplin...  5.26 us
    ppermute x3, starting transfers between devices, to_across(): lax.ppermute(item, 'sec', [(s, s // GROUP * GROUP + (s % GROUP + CORES) %...  3.81 us
    pallas_call x1, Pallas kernels, face_rows_of(): call(rows_kernel, 'face_rows', [IN_HBM], shape(energies, face, orbitals),...  2.35 us
    all_to_all x1, waiting for transfers between devices, per_device(): lax.all_to_all(outgoing, 'sec', split_axis=0, concat_axis=0, tiled=True)  1.77 us
  transfers between devices with their start and end apart: 17, of which 4 were waited for; matrix products, arithmetic and copies ran while one was open for 0% of the time, Pallas kernels for 22%

profile of v8, /device:TPU:0, one launch (start us, length us, event | category | flops | bytes accessed | tf_op | source)
XLA Modules:
  0.0 55.5 jit_solution(1848843955810704040)
XLA Ops:
  0.0 5.7 %pairs_and_maps.1 = (bf16[16,144,128]{2,1,0:T(8,128)(2,1)}, f32[256,256]{1,0:T(8,128)}, f32[256,256]{1,0:T(8,128)}) custom-call(s32[16]{0:T(128)} %bitcast.20, s32[2,16]{1,0:T(2,128)} %bitcast.17, s32[2,8]{1,0:T(2,128)} %bitcast.18, bf16[2,1024,1024]{2,1,0:T(8,128)(2,1)} %bitcast.9, bf16[2,1024,128]{2,1,0:T(8,128)(2,1)} %bitcast.13, bf16[1024,256]{1,0:T(8,128)(2,1)} %bitcast.15), custom_call_target="tpu_custom_call" | custom-call | flops 6440000000 | tf_op jit(solution)/shard_map/pairs_and_maps/pallas_call | solution.py:170
  5.7 7.4 %all-to-all-start = ((bf16[16,144,128]{2,1,0:T(8,128)(2,1)}), bf16[16,144,128]{2,1,0:T(8,128)(2,1)S(1)}, u32[]{:S(2)}, u32[]{:S(2)}) async-start(bf16[16,144,128]{2,1,0:T(8,128)(2,1)} %get-tuple-element.20), calls=%async_computation | async-start | bytes 1179648 | tf_op jit(solution)/shard_map/all_to_all | solution.py:522
  13.1 1.9 %collective-permute-start = (f32[256,256]{1,0:T(8,128)}, f32[256,256]{1,0:T(8,128)S(1)}, u32[]{:S(2)}, u32[]{:S(2)}) collective-permute-start(f32[256,256]{1,0:T(8,128)} %get-tuple-element.21), channel_id=1, source_target_pairs={{0,2},{1,3},{2,0},{3,1},{4,6},{5,7},{6,4},{7,5},{8,10},{9,11},{10,... | collective-permute-start | bytes 786440 | tf_op jit(solution)/shard_map/ppermute | solution.py:473
  15.0 0.0 collective-permute-start.4
  15.1 5.3 %prop.1._prop = bf16[2,1024,256]{2,1,0:T(8,128)(2,1)} custom-call(s32[2,8]{1,0:T(2,128)} %bitcast.19, bf16[2,1024,1024]{2,1,0:T(8,128)(2,1)} %bitcast.10, bf16[1024,256]{1,0:T(8,128)(2,1)} %bitcast.16), custom_call_target="tpu_custom_call" | custom-call | flops 5750000128 | tf_op jit(solution)/shard_map/prop/pallas_call | solution.py:210
  20.3 0.0 copy-start.1
  20.3 0.0 copy-start.4
  20.3 2.4 %face_rows.1 = bf16[2,256,1024]{2,1,0:T(8,128)(2,1)} custom-call(bf16[2,1024,1024]{2,1,0:T(8,128)(2,1)} %bitcast.11), custom_call_target="tpu_custom_call" | custom-call | flops 1724999936 | tf_op jit(solution)/shard_map/face_rows/pallas_call | solution.py:241
  22.7 0.0 copy-start.2
  22.7 4.2 %collective-permute-done._map = f32[256,256]{1,0:T(8,128)S(1)} collective-permute-done((f32[256,256]{1,0:T(8,128)}, f32[256,256]{1,0:T(8,128)S(1)}, u32[]{:S(2)}, u32[]{:S(2)}) %collective-permute-start) | collective-permute-done | bytes 262176 | tf_op jit(solution)/shard_map/ppermute | solution.py:473
  26.9 1.8 %all-to-all-done.received = bf16[16,144,128]{2,1,0:T(8,128)(2,1)S(1)} async-done(((bf16[16,144,128]{2,1,0:T(8,128)(2,1)}), bf16[16,144,128]{2,1,0:T(8,128)(2,1)S(1)}, u32[]{:S(2)}, u32[]{:S(2)}) %all-to-all-start) | async-done | bytes 589856 | tf_op jit(solution)/shard_map/all_to_all | solution.py:522
  28.7 1.2 %copy-done.3 = bf16[2,256,1024]{2,1,0:T(8,128)(2,1)S(1)} copy-done((bf16[2,256,1024]{2,1,0:T(8,128)(2,1)S(1)}, bf16[2,256,1024]{2,1,0:T(8,128)(2,1)}, u32[]{:S(2)}) %copy-start.3) | copy-done | bytes 1048600
  29.9 1.4 %source_and_face.1 = (bf16[2,1024,128]{2,1,0:T(8,128)(2,1)S(1)}, bf16[128,128]{1,0:T(8,128)(2,1)S(1)}, bf16[128,128]{1,0:T(8,128)(2,1)S(1)}, bf16[128,128]{1,0:T...) custom-call(bf16[16,144,128]{2,1,0:T(8,128)(2,1)S(1)} %all-to-all-done.rec, ...), custom_call_target="tpu_custom_call", output_to_operand_aliasing={{5}: (4, {})} | custom-call | flops 1610000000 | tf_op jit(solution)/shard_map/source_and_face/pallas_call | solution.py:338
  31.3 0.0 copy-start
  31.3 0.1 collective-permute-start.5
  31.4 0.5 collective-permute-start.1
  31.9 0.9 %collective-permute-start.2 = (bf16[128,128]{1,0:T(8,128)(2,1)S(1)}, bf16[128,128]{1,0:T(8,128)(2,1)S(1)}, u32[]{:S(2)}, u32[]{:S(2)}) collective-permute-start(bf16[128,128]{1,0:T(8,128)(2,1)S(1)} %get-tuple-element.24), channel_id=1, source_target_pairs={{0,2},{1,3},{2,0},{3,1},{4,6},{5,7},{6,4},{7,5},{8,10},{9,11},{10,... | collective-permute-start | bytes 98312 | tf_op jit(solution)/shard_map/ppermute | solution.py:473
  32.8 0.5 collective-permute-start.3
  33.3 0.0 collective-permute-done.4.near
  33.3 0.0 collective-permute-done.5.far
  33.3 0.9 %chain_maps.1 = (bf16[128,256]{1,0:T(8,128)(2,1)S(1)}, bf16[2,4,256,256]{3,2,1,0:T(8,128)(2,1)S(1)}) custom-call(f32[256,256]{1,0:T(8,128)S(1)} %copy-done.2, f32[256,256]{1,0:T(8,128)S(1)} %collective-permute-done.4.near, f32[256,256]{1,0:T(8,128)S(1)} %get-tuple-element.27.across, f32[256,256]{1,0:T(8,128)S(1)} %collective-permute-done.5.far), custom_call_target="tpu_custom_call" | custom-call | flops 1035000000 | tf_op jit(solution)/shard_map/chain_maps/pallas_call | solution.py:288
  34.2 4.5 %collective-permute-start.11 = (bf16[128,256]{1,0:T(8,128)(2,1)S(1)}, bf16[128,256]{1,0:T(8,128)(2,1)S(1)}, u32[]{:S(2)}, u32[]{:S(2)}) collective-permute-start(bf16[128,256]{1,0:T(8,128)(2,1)S(1)} %get-tuple-element.29), channel_id=1, source_target_pairs={{0,8},{1,9},{2,10},{3,11},{4,12},{5,13},{6,14},{7,15},{16,24},{17,... | collective-permute-start | bytes 196616 | tf_op jit(solution)/shard_map/ppermute | solution.py:495
  38.7 2.7 %collective-permute-start.9 = (bf16[128,256]{1,0:T(8,128)(2,1)S(1)}, bf16[128,256]{1,0:T(8,128)(2,1)S(1)}, u32[]{:S(2)}, u32[]{:S(2)}) collective-permute-start(bf16[128,256]{1,0:T(8,128)(2,1)S(1)} %get-tuple-element.29), channel_id=1, source_target_pairs={{0,4},{1,5},{2,6},{3,7},{4,8},{5,9},{6,10},{7,11},{8,12},{9,13},{1... | collective-permute-start | bytes 196616 | tf_op jit(solution)/shard_map/ppermute | solution.py:495
  41.4 0.0 collective-permute-done.1.near.refs_10_
  41.4 0.0 collective-permute-done.2.across.refs_11_
  41.4 0.0 collective-permute-done.3.far.refs_12_
  41.4 0.9 %plane_total.1 = bf16[128,128]{1,0:T(8,128)(2,1)S(1)} custom-call(bf16[128,128]{1,0:T(8,128)(2,1)S(1)} %get-tuple-element.22.own.refs_9_, bf16[128,128]{1,0:T(8,128)(2,1)S(1)} %collective-permute-done.1.near.refs_10_, bf16[128,128]{1,0:T(8,128)(2,1)S(1)} %collective-permute-done.2.across.refs_11_, bf16[128,128]{1,0:T(8,128)(2,1)S(1)} %collective-permute-done.3.far.refs_12_, ...), custom_call_target="tpu_custom_call" | custom-call | flops 1035000000 | tf_op jit(solution)/shard_map/plane_total/pallas_call | solution.py:379
  42.4 1.3 %collective-permute-start.8 = (bf16[128,128]{1,0:T(8,128)(2,1)S(1)}, bf16[128,128]{1,0:T(8,128)(2,1)S(1)}, u32[]{:S(2)}, u32[]{:S(2)}) collective-permute-start(bf16[128,128]{1,0:T(8,128)(2,1)S(1)} %plane_total.1), channel_id=1, source_target_pairs={{0,12},{1,13},{2,14},{3,15},{16,28},{17,29},{18,30},{19,31}} | collective-permute-start | bytes 98312 | tf_op jit(solution)/shard_map/ppermute | solution.py:495
  43.7 1.3 %collective-permute-start.7 = (bf16[128,128]{1,0:T(8,128)(2,1)S(1)}, bf16[128,128]{1,0:T(8,128)(2,1)S(1)}, u32[]{:S(2)}, u32[]{:S(2)}) collective-permute-start(bf16[128,128]{1,0:T(8,128)(2,1)S(1)} %plane_total.1), channel_id=1, source_target_pairs={{0,8},{1,9},{2,10},{3,11},{4,12},{5,13},{6,14},{7,15},{16,24},{17,... | collective-permute-start | bytes 98312 | tf_op jit(solution)/shard_map/ppermute | solution.py:495
  45.0 1.3 %collective-permute-start.6 = (bf16[128,128]{1,0:T(8,128)(2,1)S(1)}, bf16[128,128]{1,0:T(8,128)(2,1)S(1)}, u32[]{:S(2)}, u32[]{:S(2)}) collective-permute-start(bf16[128,128]{1,0:T(8,128)(2,1)S(1)} %plane_total.1), channel_id=1, source_target_pairs={{0,4},{1,5},{2,6},{3,7},{4,8},{5,9},{6,10},{7,11},{8,12},{9,13},{1... | collective-permute-start | bytes 98312 | tf_op jit(solution)/shard_map/ppermute | solution.py:495
  46.3 0.0 collective-permute-done.11.refs_5_
  46.3 0.2 collective-permute-start.12
  46.5 0.0 collective-permute-done.9.refs_3_
  46.5 0.3 collective-permute-start.10
  46.9 1.2 %image.1.refs_8_ = f32[2,1024,128]{2,1,0:T(8,128)S(1)} custom-call(bf16[2,1024,1024]{2,1,0:T(8,128)(2,1)S(1)} %bitcast.12, bf16[2,1024,128]{2,1,0:T(8,128)(2,1)S(1)} %get-tuple-element.30.source), custom_call_target="tpu_custom_call" | custom-call | flops 1380000000 | tf_op jit(solution)/shard_map/image/pallas_call | solution.py:258
  48.1 0.0 collective-permute-done.8.refs_2_
  48.1 0.0 collective-permute-done.7.refs_1_
  48.1 0.0 collective-permute-done.6.refs_0_
  48.1 0.0 collective-permute-done.12.refs_6_
  48.2 0.0 collective-permute-done.10.refs_4_
  48.2 1.4 %entering.1 = (bf16[128,128]{1,0:T(8,128)(2,1)S(1)}, bf16[128,128]{1,0:T(8,128)(2,1)S(1)}, bf16[128,128]{1,0:T(8,128)(2,1)S(1)}, bf16[128,128]{1,0:T(8,128)(2,1)S(1)}) custom-call(bf16[128,128]{1,0:T(8,128)(2,1)S(1)} %collective-permute-done.6.refs_0_, bf16[128,128]{1,0:T(8,128)(2,1)S(1)} %collective-permute-done.7.refs_1_, ...), custom_call_target="tpu_custom_call" | custom-call | flops 1610000000 | tf_op jit(solution)/shard_map/entering/pallas_call | solution.py:416
  49.6 0.2 collective-permute-start.13
  49.8 1.0 %collective-permute-start.14 = (bf16[128,128]{1,0:T(8,128)(2,1)S(1)}, bf16[128,128]{1,0:T(8,128)(2,1)S(1)}, u32[]{:S(2)}, u32[]{:S(2)}) collective-permute-start(bf16[128,128]{1,0:T(8,128)(2,1)S(1)} %get-tuple-element.33), channel_id=1, source_target_pairs={{0,2},{1,3},{2,0},{3,1},{4,6},{5,7},{6,4},{7,5},{8,10},{9,11},{10,... | collective-permute-start | bytes 98312 | tf_op jit(solution)/shard_map/ppermute | solution.py:473
  50.8 0.7 %collective-permute-start.15 = (bf16[128,128]{1,0:T(8,128)(2,1)S(1)}, bf16[128,128]{1,0:T(8,128)(2,1)S(1)}, u32[]{:S(2)}, u32[]{:S(2)}) collective-permute-start(bf16[128,128]{1,0:T(8,128)(2,1)S(1)} %get-tuple-element.34), channel_id=1, source_target_pairs={{0,3},{1,2},{2,1},{3,0},{4,7},{5,6},{6,5},{7,4},{8,11},{9,10},{10,... | collective-permute-start | bytes 98312 | tf_op jit(solution)/shard_map/ppermute | solution.py:477
  51.5 0.0 collective-permute-done.13.near
  51.5 2.2 %collective-permute-done.14.across = bf16[128,128]{1,0:T(8,128)(2,1)S(1)} collective-permute-done((bf16[128,128]{1,0:T(8,128)(2,1)S(1)}, bf16[128,128]{1,0:T(8,128)(2,1)S(1)}, u32[]{:S(2)}, u32[]{:S(2)}) %collective-permute-start.14) | collective-permute-done | bytes 32800 | tf_op jit(solution)/shard_map/ppermute | solution.py:473
  53.7 0.4 collective-permute-done.15.far
  54.2 1.3 %waves.1 = bf16[2,1024,128]{2,1,0:T(8,128)(2,1)} custom-call(bf16[128,128]{1,0:T(8,128)(2,1)S(1)} %get-tuple-element.31.own, bf16[128,128]{1,0:T(8,128)(2,1)S(1)} %collective-permute-done.13.near, bf16[128,128]{1,0:T(8,128)(2,1)S(1)} %collective-permute-done.14.across, bf16[128,128]{1,0:T(8,128)(2,1)S(1)} %collective-permute-done.15.far, ...), custom_call_target="tpu_custom_call" | custom-call | flops 1495000064 | tf_op jit(solution)/shard_map/waves/pallas_call | solution.py:458
  (5 shorter events, 0.0 us)
Async XLA Ops:
  5.7 22.9 %all-to-all-start = ((bf16[16,144,128]{2,1,0:T(8,128)(2,1)}), bf16[16,144,128]{2,1,0:T(8,128)(2,1)S(1)}, u32[]{:S(2)}, u32[]{:S(2)}) async-start(bf16[16,144,128]{2,1,0:T(8,128)(2,1)} %get-tuple-element.20), calls=%async_computation | async-start | bytes 1179648 | tf_op jit(solution)/shard_map/all_to_all | solution.py:522
  13.1 13.8 %collective-permute-start = (f32[256,256]{1,0:T(8,128)}, f32[256,256]{1,0:T(8,128)S(1)}, u32[]{:S(2)}, u32[]{:S(2)}) collective-permute-start(f32[256,256]{1,0:T(8,128)} %get-tuple-element.21), channel_id=1, source_target_pairs={{0,2},{1,3},{2,0},{3,1},{4,6},{5,7},{6,4},{7,5},{8,10},{9,11},{10,... | collective-permute-start | bytes 786440 | tf_op jit(solution)/shard_map/ppermute | solution.py:473
  15.0 18.3 %collective-permute-start.4 = (f32[256,256]{1,0:T(8,128)}, f32[256,256]{1,0:T(8,128)S(1)}, u32[]{:S(2)}, u32[]{:S(2)}) collective-permute-start(f32[256,256]{1,0:T(8,128)} %get-tuple-element.26.own), channel_id=1, source_target_pairs={{0,1},{1,0},{2,3},{3,2},{4,5},{5,4},{6,7},{7,6},{8,9},{9,8},{10,11... | collective-permute-start | bytes 786440 | tf_op jit(solution)/shard_map/ppermute | solution.py:469
  20.3 8.4 %copy-start.1 = (bf16[1,2,1024,128]{3,2,1,0:T(8,128)(2,1)S(1)}, bf16[1,2,1024,128]{3,2,1,0:T(8,128)(2,1)}, u32[]{:S(2)}) copy-start(bf16[1,2,1024,128]{3,2,1,0:T(8,128)(2,1)} %param.7) | copy-start | bytes 1572868
  20.3 8.3 %copy-start.4 = (bf16[2,1024,256]{2,1,0:T(8,128)(2,1)S(1)}, bf16[2,1024,256]{2,1,0:T(8,128)(2,1)}, u32[]{:S(2)}) copy-start(bf16[2,1024,256]{2,1,0:T(8,128)(2,1)} %prop.1._prop) | copy-start | bytes 3145732
  22.7 10.6 %copy-start.2 = (f32[256,256]{1,0:T(8,128)S(1)}, f32[256,256]{1,0:T(8,128)}, u32[]{:S(2)}) copy-start(f32[256,256]{1,0:T(8,128)} %get-tuple-element.26.own) | copy-start | bytes 786436
  28.7 1.2 %copy-start.3 = (bf16[2,256,1024]{2,1,0:T(8,128)(2,1)S(1)}, bf16[2,256,1024]{2,1,0:T(8,128)(2,1)}, u32[]{:S(2)}) copy-start(bf16[2,256,1024]{2,1,0:T(8,128)(2,1)} %face_rows.1) | copy-start | bytes 3145732
  31.3 15.6 %copy-start = (bf16[1,2,1024,1024]{3,2,1,0:T(8,128)(2,1)S(1)}, bf16[1,2,1024,1024]{3,2,1,0:T(8,128)(2,1)}, u32[]{:S(2)}) copy-start(bf16[1,2,1024,1024]{3,2,1,0:T(8,128)(2,1)} %param.6) | copy-start | bytes 12582916
  31.3 2.0 %collective-permute-start.5 = (f32[256,256]{1,0:T(8,128)S(1)}, f32[256,256]{1,0:T(8,128)S(1)}, u32[]{:S(2)}, u32[]{:S(2)}) collective-permute-start(f32[256,256]{1,0:T(8,128)S(1)} %get-tuple-element.27.across), channel_id=1, source_target_pairs={{0,1},{1,0},{2,3},{3,2},{4,5},{5,4},{6,7},{7,6},{8,9},{9,8},{10,11... | collective-permute-start | bytes 786440 | tf_op jit(solution)/shard_map/ppermute | solution.py:469
  31.4 10.0 %collective-permute-start.1 = (bf16[128,128]{1,0:T(8,128)(2,1)S(1)}, bf16[128,128]{1,0:T(8,128)(2,1)S(1)}, u32[]{:S(2)}, u32[]{:S(2)}) collective-permute-start(bf16[128,128]{1,0:T(8,128)(2,1)S(1)} %get-tuple-element.23), channel_id=1, source_target_pairs={{0,1},{1,0},{2,3},{3,2},{4,5},{5,4},{6,7},{7,6},{8,9},{9,8},{10,11... | collective-permute-start | bytes 98312 | tf_op jit(solution)/shard_map/ppermute | solution.py:469
  31.9 9.5 %collective-permute-start.2 = (bf16[128,128]{1,0:T(8,128)(2,1)S(1)}, bf16[128,128]{1,0:T(8,128)(2,1)S(1)}, u32[]{:S(2)}, u32[]{:S(2)}) collective-permute-start(bf16[128,128]{1,0:T(8,128)(2,1)S(1)} %get-tuple-element.24), channel_id=1, source_target_pairs={{0,2},{1,3},{2,0},{3,1},{4,6},{5,7},{6,4},{7,5},{8,10},{9,11},{10,... | collective-permute-start | bytes 98312 | tf_op jit(solution)/shard_map/ppermute | solution.py:473
  32.8 8.6 %collective-permute-start.3 = (bf16[128,128]{1,0:T(8,128)(2,1)S(1)}, bf16[128,128]{1,0:T(8,128)(2,1)S(1)}, u32[]{:S(2)}, u32[]{:S(2)}) collective-permute-start(bf16[128,128]{1,0:T(8,128)(2,1)S(1)} %get-tuple-element.25), channel_id=1, source_target_pairs={{0,3},{1,2},{2,1},{3,0},{4,7},{5,6},{6,5},{7,4},{8,11},{9,10},{10,... | collective-permute-start | bytes 98312 | tf_op jit(solution)/shard_map/ppermute | solution.py:477
  34.2 12.1 %collective-permute-start.11 = (bf16[128,256]{1,0:T(8,128)(2,1)S(1)}, bf16[128,256]{1,0:T(8,128)(2,1)S(1)}, u32[]{:S(2)}, u32[]{:S(2)}) collective-permute-start(bf16[128,256]{1,0:T(8,128)(2,1)S(1)} %get-tuple-element.29), channel_id=1, source_target_pairs={{0,8},{1,9},{2,10},{3,11},{4,12},{5,13},{6,14},{7,15},{16,24},{17,... | collective-permute-start | bytes 196616 | tf_op jit(solution)/shard_map/ppermute | solution.py:495
  38.7 7.8 %collective-permute-start.9 = (bf16[128,256]{1,0:T(8,128)(2,1)S(1)}, bf16[128,256]{1,0:T(8,128)(2,1)S(1)}, u32[]{:S(2)}, u32[]{:S(2)}) collective-permute-start(bf16[128,256]{1,0:T(8,128)(2,1)S(1)} %get-tuple-element.29), channel_id=1, source_target_pairs={{0,4},{1,5},{2,6},{3,7},{4,8},{5,9},{6,10},{7,11},{8,12},{9,13},{1... | collective-permute-start | bytes 196616 | tf_op jit(solution)/shard_map/ppermute | solution.py:495
  42.4 5.7 %collective-permute-start.8 = (bf16[128,128]{1,0:T(8,128)(2,1)S(1)}, bf16[128,128]{1,0:T(8,128)(2,1)S(1)}, u32[]{:S(2)}, u32[]{:S(2)}) collective-permute-start(bf16[128,128]{1,0:T(8,128)(2,1)S(1)} %plane_total.1), channel_id=1, source_target_pairs={{0,12},{1,13},{2,14},{3,15},{16,28},{17,29},{18,30},{19,31}} | collective-permute-start | bytes 98312 | tf_op jit(solution)/shard_map/ppermute | solution.py:495
  43.7 4.4 %collective-permute-start.7 = (bf16[128,128]{1,0:T(8,128)(2,1)S(1)}, bf16[128,128]{1,0:T(8,128)(2,1)S(1)}, u32[]{:S(2)}, u32[]{:S(2)}) collective-permute-start(bf16[128,128]{1,0:T(8,128)(2,1)S(1)} %plane_total.1), channel_id=1, source_target_pairs={{0,8},{1,9},{2,10},{3,11},{4,12},{5,13},{6,14},{7,15},{16,24},{17,... | collective-permute-start | bytes 98312 | tf_op jit(solution)/shard_map/ppermute | solution.py:495
  45.0 3.2 %collective-permute-start.6 = (bf16[128,128]{1,0:T(8,128)(2,1)S(1)}, bf16[128,128]{1,0:T(8,128)(2,1)S(1)}, u32[]{:S(2)}, u32[]{:S(2)}) collective-permute-start(bf16[128,128]{1,0:T(8,128)(2,1)S(1)} %plane_total.1), channel_id=1, source_target_pairs={{0,4},{1,5},{2,6},{3,7},{4,8},{5,9},{6,10},{7,11},{8,12},{9,13},{1... | collective-permute-start | bytes 98312 | tf_op jit(solution)/shard_map/ppermute | solution.py:495
  46.3 1.9 %collective-permute-start.12 = (bf16[128,256]{1,0:T(8,128)(2,1)S(1)}, bf16[128,256]{1,0:T(8,128)(2,1)S(1)}, u32[]{:S(2)}, u32[]{:S(2)}) collective-permute-start(bf16[128,256]{1,0:T(8,128)(2,1)S(1)} %collective-permute-done.11.refs_5_), channel_id=1, source_target_pairs={{0,1},{1,0},{2,3},{3,2},{4,5},{5,4},{6,7},{7,6},{8,9},{9,8},{10,11... | collective-permute-start | bytes 196616 | tf_op jit(solution)/shard_map/ppermute | solution.py:469
  46.5 1.6 %collective-permute-start.10 = (bf16[128,256]{1,0:T(8,128)(2,1)S(1)}, bf16[128,256]{1,0:T(8,128)(2,1)S(1)}, u32[]{:S(2)}, u32[]{:S(2)}) collective-permute-start(bf16[128,256]{1,0:T(8,128)(2,1)S(1)} %collective-permute-done.9.refs_3_), channel_id=1, source_target_pairs={{0,1},{1,0},{2,3},{3,2},{4,5},{5,4},{6,7},{7,6},{8,9},{9,8},{10,11... | collective-permute-start | bytes 196616 | tf_op jit(solution)/shard_map/ppermute | solution.py:469
  49.6 1.9 %collective-permute-start.13 = (bf16[128,128]{1,0:T(8,128)(2,1)S(1)}, bf16[128,128]{1,0:T(8,128)(2,1)S(1)}, u32[]{:S(2)}, u32[]{:S(2)}) collective-permute-start(bf16[128,128]{1,0:T(8,128)(2,1)S(1)} %get-tuple-element.32), channel_id=1, source_target_pairs={{0,1},{1,0},{2,3},{3,2},{4,5},{5,4},{6,7},{7,6},{8,9},{9,8},{10,11... | collective-permute-start | bytes 98312 | tf_op jit(solution)/shard_map/ppermute | solution.py:469
  49.8 3.9 %collective-permute-start.14 = (bf16[128,128]{1,0:T(8,128)(2,1)S(1)}, bf16[128,128]{1,0:T(8,128)(2,1)S(1)}, u32[]{:S(2)}, u32[]{:S(2)}) collective-permute-start(bf16[128,128]{1,0:T(8,128)(2,1)S(1)} %get-tuple-element.33), channel_id=1, source_target_pairs={{0,2},{1,3},{2,0},{3,1},{4,6},{5,7},{6,4},{7,5},{8,10},{9,11},{10,... | collective-permute-start | bytes 98312 | tf_op jit(solution)/shard_map/ppermute | solution.py:473
  50.8 3.4 %collective-permute-start.15 = (bf16[128,128]{1,0:T(8,128)(2,1)S(1)}, bf16[128,128]{1,0:T(8,128)(2,1)S(1)}, u32[]{:S(2)}, u32[]{:S(2)}) collective-permute-start(bf16[128,128]{1,0:T(8,128)(2,1)S(1)} %get-tuple-element.34), channel_id=1, source_target_pairs={{0,3},{1,2},{2,1},{3,0},{4,7},{5,6},{6,5},{7,4},{8,11},{9,10},{10,... | collective-permute-start | bytes 98312 | tf_op jit(solution)/shard_map/ppermute | solution.py:477

commit v9 on v8

--- a/solution.py
+++ b/solution.py
@@ -87,13 +87,6 @@
     return jnp.concatenate([packed, swap_lanes(packed)], axis=0)
 
 
-def fetch(green, held, sem):
-    moves = [pltpu.make_async_copy(green.at[e], held.at[e], sem.at[e]) for e in range(green.shape[0])]
-    for move in moves:
-        move.start()
-    return moves
-
-
 def mask_tiles(pattern, coupling):
     high, wide = coupling.shape[0] // pattern.shape[1], coupling.shape[1] // pattern.shape[0]
     for i in range(pattern.shape[1]):
@@ -103,23 +96,34 @@
             coupling[at] = jnp.where(pattern[j, i] == 1, tile, jnp.zeros_like(tile))
 
 
-def first_kernel(
-    owner_in, blocks_in, pattern_in, green, inject_in, coupling_in, out, own, other,
-    owner, blocks, pattern, inject, coupling, held, full, maps, slot_of, counts, sem, side,
-):
+def pairs_kernel(owner_in, blocks_in, green, inject_in, out, owner, blocks, inject, held, product, slot_of, counts, sem, side):
     energies, orbitals, _ = green.shape
     sections = out.shape[0]
     count = owner.shape[0]
-    face = coupling.shape[1]
+    named = held.shape[1] < orbitals
     small = [
         pltpu.make_async_copy(src, dst, side.at[k])
-        for k, (src, dst) in enumerate(
-            ((owner_in, owner), (blocks_in, blocks), (pattern_in, pattern), (inject_in, inject), (coupling_in, coupling))
-        )
+        for k, (src, dst) in enumerate(((owner_in, owner), (blocks_in, blocks), (inject_in, inject)))
     ]
     for move in small:
         move.start()
-    moves = fetch(green, held, sem)
+
+    def copy_of(e, q):
+        first = pl.multiple_of(blocks[0, q] * BLK, BLK)
+        to = pl.multiple_of(q * BLK, BLK)
+        return pltpu.make_async_copy(green.at[e, pl.ds(first, BLK)], held.at[e, pl.ds(to, BLK)], sem.at[e])
+
+    def whole(e):
+        return pltpu.make_async_copy(green.at[e], held.at[e], sem.at[e])
+
+    if not named:
+        for e in range(energies):
+            whole(e).start()
+    for move in small[:2]:
+        move.wait()
+    if named:
+        for e in range(energies):
+            lax.fori_loop(0, count, lambda q, _, e=e: copy_of(e, q).start(), None, unroll=4)
     rows = CAP * energies * BLK
     lane = lax.broadcasted_iota(jnp.int32, (HEAD, out.shape[2]), 1)
     none = jnp.where(lane < CAP, -1.0, 0.0).astype(BF16)
@@ -131,8 +135,6 @@
         return 0
 
     lax.fori_loop(0, sections, blank, 0)
-    for move in small:
-        move.wait()
 
     def rank(q, _):
         d = owner[q]
@@ -145,108 +147,86 @@
         return 0
 
     lax.fori_loop(0, count, rank, 0)
-    mask_tiles(pattern, coupling)
-    for e, move in enumerate(moves):
-        move.wait()
-        full[e] = dot(held[e], inject[e]).astype(BF16)
-        maps[e] = dot(held[e, orbitals - face :, :], coupling[...])
+    small[2].wait()
+    for e in range(energies):
+        whole_held = pltpu.make_async_copy(green.at[e, pl.ds(0, held.shape[1])], held.at[e], sem.at[e])
+        whole_held.wait()
+        product[...] = dot(held[e], inject[e]).astype(BF16)
 
         def fill(q, _):
-            first = pl.multiple_of(blocks[0, q] * BLK, BLK)
+            first = pl.multiple_of((q if named else blocks[0, q]) * BLK, BLK)
             to = pl.multiple_of((slot_of[q] * energies + e) * BLK, BLK)
-            out[owner[q], pl.ds(to, BLK), :] = full[e, pl.ds(first, BLK), :]
+            out[owner[q], pl.ds(to, BLK), :] = product[pl.ds(first, BLK), :]
             return 0
 
         lax.fori_loop(0, count, fill, 0, unroll=4)
+
+
+def outgoing_pairs(owner, blocks, green, inject, sections):
+    energies, orbitals, _ = green.shape
+    columns = inject.shape[2]
+    rows = min(orbitals, owner.shape[0] * BLK)
+    return call(
+        pairs_kernel,
+        "pairs",
+        [IN_HBM] * 4,
+        shape(sections, CAP * energies * BLK + HEAD, columns),
+        [
+            pltpu.SMEM(owner.shape, jnp.int32),
+            pltpu.SMEM(blocks.shape, jnp.int32),
+            pltpu.VMEM(inject.shape, BF16),
+            pltpu.VMEM((energies, rows, orbitals), BF16),
+            pltpu.VMEM((rows, columns), BF16),
+            pltpu.SMEM(owner.shape, jnp.int32),
+            pltpu.SMEM((sections,), jnp.int32),
+            pltpu.SemaphoreType.DMA((energies,)),
+            pltpu.SemaphoreType.DMA((3,)),
+        ],
+        4.0,
+        VMEM_WHOLE,
+    )(owner, blocks, green, inject)
+
+
+def maps_kernel(pattern, green, coupling, couple, own, other, maps):
+    energies, orbitals, _ = green.shape
+    face = coupling.shape[1]
+    couple[...] = coupling[...]
+    mask_tiles(pattern, couple)
+    for e in range(energies):
+        maps[e] = dot(green[e, orbitals - face :, :], couple[...])
     mine = place() // CORES
     own[...] = maps[mine]
     other[...] = maps[1 - mine]
 
 
-def pairs_and_maps(owner, blocks, pattern, green, inject, coupling, sections):
-    energies, orbitals, _ = green.shape
-    columns, face = inject.shape[2], coupling.shape[1]
+def face_maps(pattern, green, coupling):
+    orbitals, face = coupling.shape
     square = shape(face, face, dtype=F32)
     return call(
-        first_kernel,
-        "pairs_and_maps",
-        [IN_HBM] * 6,
-        [shape(sections, CAP * energies * BLK + HEAD, columns), square, square],
-        [
-            pltpu.SMEM(owner.shape, jnp.int32),
-            pltpu.SMEM(blocks.shape, jnp.int32),
-            pltpu.SMEM(pattern.shape, jnp.int32),
-            pltpu.VMEM(inject.shape, BF16),
-            pltpu.VMEM(coupling.shape, BF16),
-            pltpu.VMEM(green.shape, BF16),
-            pltpu.VMEM(inject.shape, BF16),
-            pltpu.VMEM((energies, face, face), F32),
-            pltpu.SMEM(owner.shape, jnp.int32),
-            pltpu.SMEM((sections,), jnp.int32),
-            pltpu.SemaphoreType.DMA((energies,)),
-            pltpu.SemaphoreType.DMA((5,)),
-        ],
-        5.6,
-        VMEM_WHOLE,
-    )(owner, blocks, pattern, green, inject, coupling)
-
-
-def prop_kernel(pattern_in, green, coupling_in, out, pattern, coupling, held, sem, side):
-    tiles = pltpu.make_async_copy(pattern_in, pattern, side.at[0])
-    whole = pltpu.make_async_copy(coupling_in, coupling, side.at[1])
-    tiles.start()
-    whole.start()
-    moves = fetch(green, held, sem)
-    tiles.wait()
-    whole.wait()
-    mask_tiles(pattern, coupling)
-    for e, move in enumerate(moves):
-        move.wait()
-        out[e] = dot(held[e], coupling[...]).astype(BF16)
-
-
-def propagator(pattern, green, coupling):
+        maps_kernel,
+        "face_maps",
+        [IN_SMEM, IN_VMEM, IN_VMEM],
+        [shape(orbitals, face), square, square],
+        [pltpu.VMEM((green.shape[0], face, face), F32)],
+        1.1,
+    )(pattern, green, coupling)
+
+
+def prop_kernel(green, couple, out):
+    for e in range(green.shape[0]):
+        out[e] = dot(green[e], couple[...]).astype(BF16)
+
+
+def propagator(green, couple):
     energies, orbitals, _ = green.shape
     return call(
         prop_kernel,
         "prop",
-        [IN_HBM] * 3,
-        shape(energies, orbitals, coupling.shape[1]),
-        [
-            pltpu.SMEM(pattern.shape, jnp.int32),
-            pltpu.VMEM(coupling.shape, BF16),
-            pltpu.VMEM(green.shape, BF16),
-            pltpu.SemaphoreType.DMA((energies,)),
-            pltpu.SemaphoreType.DMA((2,)),
-        ],
-        5.0,
-        VMEM_WHOLE,
-    )(pattern, green, coupling)
-
-
-def rows_kernel(green, out, sem):
-    face = out.shape[1]
-    moves = [
-        pltpu.make_async_copy(green.at[e, pl.ds(green.shape[1] - face, face)], out.at[e], sem.at[e])
-        for e in range(green.shape[0])
-    ]
-    for move in moves:
-        move.start()
-    for move in moves:
-        move.wait()
-
-
-def face_rows_of(green, face):
-    energies, _, orbitals = green.shape
-    return call(
-        rows_kernel,
-        "face_rows",
-        [IN_HBM],
-        shape(energies, face, orbitals),
-        [pltpu.SemaphoreType.DMA((energies,))],
-        1.5,
-        VMEM_MOST,
-    )(green)
+        [IN_VMEM, IN_VMEM],
+        shape(energies, orbitals, couple.shape[1]),
+        [],
+        1.3,
+    )(green, couple)
 
 
 def image_kernel(green, source, out):
@@ -295,8 +275,17 @@
     )(*maps)
 
 
-def source_kernel(received, inject, face_rows, _prop, _map, source, own, near, across, far, _same_map, quarters, total, heads, targets, sem):
+def source_kernel(
+    received, inject, green, _prop, _map, source, own, near, across, far, _same_map, face_rows, quarters, total, heads, targets, sem, rows_sem
+):
     energies, orbitals, columns = inject.shape
+    face = face_rows.shape[1]
+    moves = [
+        pltpu.make_async_copy(green.at[e, pl.ds(orbitals - face, face)], face_rows.at[e], rows_sem.at[e])
+        for e in range(energies)
+    ]
+    for move in moves:
+        move.start()
     sections = received.shape[0]
     half = quarters.shape[1]
     rows = CAP * energies * BLK
@@ -324,6 +313,7 @@
     split = GROUP // energies
     for e in range(energies):
         source[e] = total[e].astype(BF16)
+        moves[e].wait()
         tall = dot(face_rows[e], source[e])
         quarters[e * split] = pack(tall)
         second = jnp.where(left_lanes(tall[:half]), swap_lanes(tall[:half]), tall[half:])
@@ -331,25 +321,28 @@
     deal(quarters, (own, near, across, far))
 
 
-def placed_source(received, inject, face_rows, prop, passed):
-    face = face_rows.shape[1]
+def placed_source(received, inject, green, prop, passed):
+    face = passed.shape[0]
     energies, orbitals, columns = inject.shape
     sections = received.shape[0]
     return call(
         source_kernel,
         "source_and_face",
-        [IN_VMEM, IN_VMEM, IN_VMEM, IN_PLACE, IN_PLACE],
+        [IN_VMEM, IN_VMEM, IN_HBM, IN_PLACE, IN_PLACE],
         [shape(*inject.shape)] + [shape(face // 2, columns)] * GROUP + [shape(*passed.shape, dtype=passed.dtype)],
         [
+            pltpu.VMEM((energies, face, orbitals), BF16),
             pltpu.VMEM((GROUP, face // 2, columns), F32),
             pltpu.VMEM(inject.shape, F32),
             pltpu.VMEM((sections, columns), jnp.int32),
             pltpu.SMEM((sections, columns), jnp.int32),
             pltpu.SemaphoreType.DMA,
+            pltpu.SemaphoreType.DMA((energies,)),
         ],
-        1.4,
+        1.8,
+        VMEM_MOST,
         aliases={4: 1 + GROUP},
-    )(received, inject, face_rows, prop, passed)
+    )(received, inject, green, prop, passed)
 
 
 def deal(items, outs):
@@ -514,16 +507,15 @@
     green, inject = green[0], injected[0]
 
     coupling, tiles = coupling[0], pattern[0].T
-    outgoing, own_map, other_map = pairs_and_maps(
-        owner[:, 0], pair_blocks.T, tiles, green, inject, coupling, sections
-    )
+    outgoing = outgoing_pairs(owner[:, 0], pair_blocks.T, green, inject, sections)
+    received = lax.all_to_all(outgoing, "sec", split_axis=0, concat_axis=0, tiled=True)
+
+    couple, own_map, other_map = face_maps(tiles, green, coupling)
     across = to_across(other_map, sections)
     near = to_near(own_map, sections)
-    received = lax.all_to_all(outgoing, "sec", split_axis=0, concat_axis=0, tiled=True)
-    prop = propagator(tiles, green, coupling)
-    face_rows = face_rows_of(green, coupling.shape[1])
-
-    source, *quarters, across = placed_source(received, inject, face_rows, prop, across)
+    prop = propagator(green, couple)
+
+    source, *quarters, across = placed_source(received, inject, green, prop, across)
     shifts = exchange(*quarters, sections)
     far = to_near(across, sections)
     planes = sections // GROUP

time: 55.8 us -> 59.7 us (1.070)
  local copies, waits for them, and re-layouts: 1.25 us -> 5.7 us
  Pallas kernels: 20.5 us -> 16.3 us
  waiting for transfers between devices: 8.62 us -> 11.2 us
  starting transfers between devices: 24.9 us -> 25.7 us
    unnamed x10 -> x24, local copies, waits for them, and re-layouts: 1.25 us -> 5.7 us
    pallas_call x4, Pallas kernels: 14.7 us -> 10.5 us  [the longest x1 4.51 us: outgoing_pairs(): call(pairs_kernel, 'pairs', [IN_HBM] * 4, shape(sections, CAP * energies...]
    ppermute x3, waiting for transfers between devices: 6.41 us -> 9.19 us  [to_across(): lax.ppermute(item, 'sec', [(s, s // GROUP * GROUP + (s % GROUP + CORES) %...]
    ppermute x3, starting transfers between devices: 3.81 us -> 5.77 us  [to_across(): lax.ppermute(item, 'sec', [(s, s // GROUP * GROUP + (s % GROUP + CORES) %...]
    ppermute x2, starting transfers between devices: 1.24 us -> 0.31 us  [to_far(): lax.ppermute(item, 'sec', [(s, s // GROUP * GROUP + (s % GROUP + CORES) %...]
    all_to_all x1, waiting for transfers between devices: 1.77 us -> 0.97 us  [per_device(): lax.all_to_all(outgoing, 'sec', split_axis=0, concat_axis=0, tiled=True)]
    ppermute x2, waiting for transfers between devices: 0.41 us -> 1.01 us  [to_far(): lax.ppermute(item, 'sec', [(s, s // GROUP * GROUP + (s % GROUP + CORES) %...]
  transfers between devices with their start and end apart: 17 -> 17, of which waited for: 4 -> 4; matrix products, arithmetic and copies ran while one was open for 0% -> 0% of each run, Pallas kernels for 22% -> 15%
where the time goes in v9:
time: 59.7 us; the launch traced here: 59.1 us
  starting transfers between devices  25.7 us (43%)
  Pallas kernels  16.3 us (27%)
  waiting for transfers between devices  11.2 us (19%)
  local copies, waits for them, and re-layouts  5.7 us (10%)
    ppermute x5, starting transfers between devices, upward(): return lax.ppermute(item, 'sec', up_shift(sections, k))  11 us
    ppermute x3, waiting for transfers between devices, to_across(): lax.ppermute(item, 'sec', [(s, s // GROUP * GROUP + (s % GROUP + CORES) %...  9.19 us
    all_to_all x1, starting transfers between devices, per_device(): lax.all_to_all(outgoing, 'sec', split_axis=0, concat_axis=0, tiled=True)  7.27 us
    ppermute x3, starting transfers between devices, to_across(): lax.ppermute(item, 'sec', [(s, s // GROUP * GROUP + (s % GROUP + CORES) %...  5.77 us
    unnamed x24, local copies, waits for them, and re-layouts  5.7 us
    pallas_call x1, Pallas kernels, outgoing_pairs(): call(pairs_kernel, 'pairs', [IN_HBM] * 4, shape(sections, CAP * energies...  4.51 us
    pallas_call x1, Pallas kernels, placed_source(): call(source_kernel, 'source_and_face', [IN_VMEM, IN_VMEM, IN_HBM, IN_PLAC...  3.66 us
    pallas_call x1, Pallas kernels, entering(): call(functools.partial(entering_kernel, count), 'entering', [IN_VMEM] * (...  1.43 us
  transfers between devices with their start and end apart: 17, of which 4 were waited for; matrix products, arithmetic and copies ran while one was open for 0% of the time, Pallas kernels for 15%

profile of v9, /device:TPU:0, one launch (start us, length us, event | category | flops | bytes accessed | tf_op | source)
XLA Modules:
  0.0 59.1 jit_solution(17615232747662087255)
XLA Ops:
  0.0 4.5 %pairs.1 = bf16[16,144,128]{2,1,0:T(8,128)(2,1)} custom-call(s32[16]{0:T(128)} %bitcast.19, s32[2,16]{1,0:T(2,128)} %bitcast.18, bf16[2,1024,1024]{2,1,0:T(8,128)(2,1)} %bitcast.9, bf16[2,1024,128]{2,1,0:T(8,128)(2,1)} %bitcast.16), custom_call_target="tpu_custom_call" | custom-call | flops 4600000000 | tf_op jit(solution)/shard_map/pairs/pallas_call | solution.py:169
  4.5 7.3 %all-to-all-start = ((bf16[16,144,128]{2,1,0:T(8,128)(2,1)}), bf16[16,144,128]{2,1,0:T(8,128)(2,1)S(1)}, u32[]{:S(2)}, u32[]{:S(2)}) async-start(bf16[16,144,128]{2,1,0:T(8,128)(2,1)} %pairs.1), calls=%async_computation | async-start | bytes 1179648 | tf_op jit(solution)/shard_map/all_to_all | solution.py:511
  11.8 0.0 copy-start
  11.8 2.2 %copy-done = bf16[1,2,1024,1024]{3,2,1,0:T(8,128)(2,1)S(1)} copy-done((bf16[1,2,1024,1024]{3,2,1,0:T(8,128)(2,1)S(1)}, bf16[1,2,1024,1024]{3,2,1,0:T(8,128)(2,1)}, u32[]{:S(2)}) %copy-start) | copy-done | bytes 4194328
  14.0 1.1 %face_maps.1 = (bf16[1024,256]{1,0:T(8,128)(2,1)S(1)}, f32[256,256]{1,0:T(8,128)S(1)}, f32[256,256]{1,0:T(8,128)S(1)}) custom-call(s32[2,8]{1,0:T(2,128)S(1)} %bitcast.15, bf16[2,1024,1024]{2,1,0:T(8,128)(2,1)S(1)} %bitcast.11, bf16[1024,256]{1,0:T(8,128)(2,1)S(1)} %bitcast.14), custom_call_target="tpu_custom_call" | custom-call | flops 1264999936 | tf_op jit(solution)/shard_map/face_maps/pallas_call | solution.py:205
  15.1 2.0 %collective-permute-start = (f32[256,256]{1,0:T(8,128)S(1)}, f32[256,256]{1,0:T(8,128)S(1)}, u32[]{:S(2)}, u32[]{:S(2)}) collective-permute-start(f32[256,256]{1,0:T(8,128)S(1)} %get-tuple-element.21), channel_id=1, source_target_pairs={{0,2},{1,3},{2,0},{3,1},{4,6},{5,7},{6,4},{7,5},{8,10},{9,11},{10,... | collective-permute-start | bytes 786440 | tf_op jit(solution)/shard_map/ppermute | solution.py:466
  17.1 0.0 collective-permute-start.4
  17.1 1.2 %prop.1._prop = bf16[2,1024,256]{2,1,0:T(8,128)(2,1)S(1)} custom-call(bf16[2,1024,1024]{2,1,0:T(8,128)(2,1)S(1)} %bitcast.12, bf16[1024,256]{1,0:T(8,128)(2,1)S(1)} %get-tuple-element.20.couple), custom_call_target="tpu_custom_call" | custom-call | flops 1495000064 | tf_op jit(solution)/shard_map/prop/pallas_call | solution.py:222
  18.3 1.0 %copy-done.2 = bf16[2,1024,256]{2,1,0:T(8,128)(2,1)} copy-done((bf16[2,1024,256]{2,1,0:T(8,128)(2,1)}, bf16[2,1024,256]{2,1,0:T(8,128)(2,1)S(1)}, u32[]{:S(2)}) %copy-start.2) | copy-done | bytes 1048600
  19.3 7.1 %collective-permute-done._map = f32[256,256]{1,0:T(8,128)S(1)} collective-permute-done((f32[256,256]{1,0:T(8,128)S(1)}, f32[256,256]{1,0:T(8,128)S(1)}, u32[]{:S(2)}, u32[]{:S(2)}) %collective-permute-start) | collective-permute-done | bytes 262176 | tf_op jit(solution)/shard_map/ppermute | solution.py:466
  26.4 1.0 %all-to-all-done.received = bf16[16,144,128]{2,1,0:T(8,128)(2,1)S(1)} async-done(((bf16[16,144,128]{2,1,0:T(8,128)(2,1)}), bf16[16,144,128]{2,1,0:T(8,128)(2,1)S(1)}, u32[]{:S(2)}, u32[]{:S(2)}) %all-to-all-start) | async-done | bytes 589856 | tf_op jit(solution)/shard_map/all_to_all | solution.py:511
  27.3 0.8 %copy-done.11 = bf16[16,144,128]{2,1,0:T(8,128)(2,1)} copy-done((bf16[16,144,128]{2,1,0:T(8,128)(2,1)}, bf16[16,144,128]{2,1,0:T(8,128)(2,1)S(1)}, u32[]{:S(2)}) %copy-start.11) | copy-done | bytes 589848
  28.2 3.7 %source_and_face.1 = (bf16[2,1024,128]{2,1,0:T(8,128)(2,1)}, bf16[128,128]{1,0:T(8,128)(2,1)}, bf16[128,128]{1,0:T(8,128)(2,1)}, bf16[128,128]{1,0:T(8,128)(2,1)...) custom-call(bf16[16,144,128]{2,1,0:T(8,128)(2,1)} %copy-done.11, ...), custom_call_target="tpu_custom_call", output_to_operand_aliasing={{5}: (4, {})} | custom-call | flops 2070000000 | tf_op jit(solution)/shard_map/source_and_face/pallas_call | solution.py:328
  31.8 0.0 copy-start.1
  31.8 0.0 copy-start.5
  31.9 0.1 collective-permute-start.5
  31.9 0.5 collective-permute-start.1
  32.4 2.3 %collective-permute-start.2 = (bf16[128,128]{1,0:T(8,128)(2,1)}, bf16[128,128]{1,0:T(8,128)(2,1)S(1)}, u32[]{:S(2)}, u32[]{:S(2)}) collective-permute-start(bf16[128,128]{1,0:T(8,128)(2,1)} %get-tuple-element.24), channel_id=1, source_target_pairs={{0,2},{1,3},{2,0},{3,1},{4,6},{5,7},{6,4},{7,5},{8,10},{9,11},{10,... | collective-permute-start | bytes 98312 | tf_op jit(solution)/shard_map/ppermute | solution.py:466
  34.7 0.0 collective-permute-start.3
  34.7 0.0 collective-permute-done.4.near
  34.7 0.0 collective-permute-done.5.far
  34.8 0.9 %copy-done.8 = f32[256,256]{1,0:T(8,128)S(1)} copy-done((f32[256,256]{1,0:T(8,128)S(1)}, f32[256,256]{1,0:T(8,128)}, u32[]{:S(2)}) %copy-start.8) | copy-done | bytes 262168
  35.7 0.9 %chain_maps.1 = (bf16[128,256]{1,0:T(8,128)(2,1)S(1)}, bf16[2,4,256,256]{3,2,1,0:T(8,128)(2,1)S(1)}) custom-call(f32[256,256]{1,0:T(8,128)S(1)} %get-tuple-element.26.own, f32[256,256]{1,0:T(8,128)S(1)} %collective-permute-done.4.near, f32[256,256]{1,0:T(8,128)S(1)} %copy-done.8, f32[256,256]{1,0:T(8,128)S(1)} %collective-permute-done.5.far), custom_call_target="tpu_custom_call" | custom-call | flops 1035000000 | tf_op jit(solution)/shard_map/chain_maps/pallas_call | solution.py:268
  36.6 4.2 %collective-permute-start.11 = (bf16[128,256]{1,0:T(8,128)(2,1)S(1)}, bf16[128,256]{1,0:T(8,128)(2,1)S(1)}, u32[]{:S(2)}, u32[]{:S(2)}) collective-permute-start(bf16[128,256]{1,0:T(8,128)(2,1)S(1)} %get-tuple-element.29), channel_id=1, source_target_pairs={{0,8},{1,9},{2,10},{3,11},{4,12},{5,13},{6,14},{7,15},{16,24},{17,... | collective-permute-start | bytes 196616 | tf_op jit(solution)/shard_map/ppermute | solution.py:488
  40.8 2.9 %collective-permute-start.9 = (bf16[128,256]{1,0:T(8,128)(2,1)S(1)}, bf16[128,256]{1,0:T(8,128)(2,1)S(1)}, u32[]{:S(2)}, u32[]{:S(2)}) collective-permute-start(bf16[128,256]{1,0:T(8,128)(2,1)S(1)} %get-tuple-element.29), channel_id=1, source_target_pairs={{0,4},{1,5},{2,6},{3,7},{4,8},{5,9},{6,10},{7,11},{8,12},{9,13},{1... | collective-permute-start | bytes 196616 | tf_op jit(solution)/shard_map/ppermute | solution.py:488
  43.7 0.0 collective-permute-done.1.near.refs_10_
  43.7 0.0 collective-permute-done.2.across.refs_11_
  43.7 0.0 collective-permute-done.3.far.refs_12_
  43.7 0.7 %copy-done.9 = bf16[128,128]{1,0:T(8,128)(2,1)S(1)} copy-done((bf16[128,128]{1,0:T(8,128)(2,1)S(1)}, bf16[128,128]{1,0:T(8,128)(2,1)}, u32[]{:S(2)}) %copy-start.9) | copy-done | bytes 32792
  44.5 0.9 %plane_total.1 = bf16[128,128]{1,0:T(8,128)(2,1)S(1)} custom-call(bf16[128,128]{1,0:T(8,128)(2,1)S(1)} %copy-done.9, bf16[128,128]{1,0:T(8,128)(2,1)S(1)} %collective-permute-done.1.near.refs_10_, bf16[128,128]{1,0:T(8,128)(2,1)S(1)} %collective-permute-done.2.across.refs_11_, bf16[128,128]{1,0:T(8,128)(2,1)S(1)} %collective-permute-done.3.far.refs_12_, ...), custom_call_target="tpu_custom_call" | custom-call | flops 1035000000 | tf_op jit(solution)/shard_map/plane_total/pallas_call | solution.py:372
  45.4 1.3 %collective-permute-start.8 = (bf16[128,128]{1,0:T(8,128)(2,1)S(1)}, bf16[128,128]{1,0:T(8,128)(2,1)S(1)}, u32[]{:S(2)}, u32[]{:S(2)}) collective-permute-start(bf16[128,128]{1,0:T(8,128)(2,1)S(1)} %plane_total.1), channel_id=1, source_target_pairs={{0,12},{1,13},{2,14},{3,15},{16,28},{17,29},{18,30},{19,31}} | collective-permute-start | bytes 98312 | tf_op jit(solution)/shard_map/ppermute | solution.py:488
  46.7 1.3 %collective-permute-start.7 = (bf16[128,128]{1,0:T(8,128)(2,1)S(1)}, bf16[128,128]{1,0:T(8,128)(2,1)S(1)}, u32[]{:S(2)}, u32[]{:S(2)}) collective-permute-start(bf16[128,128]{1,0:T(8,128)(2,1)S(1)} %plane_total.1), channel_id=1, source_target_pairs={{0,8},{1,9},{2,10},{3,11},{4,12},{5,13},{6,14},{7,15},{16,24},{17,... | collective-permute-start | bytes 98312 | tf_op jit(solution)/shard_map/ppermute | solution.py:488
  48.0 1.3 %collective-permute-start.6 = (bf16[128,128]{1,0:T(8,128)(2,1)S(1)}, bf16[128,128]{1,0:T(8,128)(2,1)S(1)}, u32[]{:S(2)}, u32[]{:S(2)}) collective-permute-start(bf16[128,128]{1,0:T(8,128)(2,1)S(1)} %plane_total.1), channel_id=1, source_target_pairs={{0,4},{1,5},{2,6},{3,7},{4,8},{5,9},{6,10},{7,11},{8,12},{9,13},{1... | collective-permute-start | bytes 98312 | tf_op jit(solution)/shard_map/ppermute | solution.py:488
  49.3 0.0 collective-permute-done.11.refs_5_
  49.4 0.1 collective-permute-start.12
  49.5 0.0 collective-permute-done.9.refs_3_
  49.5 0.4 collective-permute-start.10
  49.9 1.2 %image.1.refs_8_ = f32[2,1024,128]{2,1,0:T(8,128)S(1)} custom-call(bf16[2,1024,1024]{2,1,0:T(8,128)(2,1)S(1)} %bitcast.13, bf16[2,1024,128]{2,1,0:T(8,128)(2,1)S(1)} %copy-done.5), custom_call_target="tpu_custom_call" | custom-call | flops 1380000000 | tf_op jit(solution)/shard_map/image/pallas_call | solution.py:238
  51.2 0.0 collective-permute-done.8.refs_2_
  51.2 0.0 collective-permute-done.7.refs_1_
  51.2 0.0 collective-permute-done.10.refs_4_
  51.3 1.4 %entering.1 = (bf16[128,128]{1,0:T(8,128)(2,1)S(1)}, bf16[128,128]{1,0:T(8,128)(2,1)S(1)}, bf16[128,128]{1,0:T(8,128)(2,1)S(1)}, bf16[128,128]{1,0:T(8,128)(2,1)S(1)}) custom-call(bf16[128,128]{1,0:T(8,128)(2,1)S(1)} %collective-permute-done.6.refs_0_, bf16[128,128]{1,0:T(8,128)(2,1)S(1)} %collective-permute-done.7.refs_1_, ...), custom_call_target="tpu_custom_call" | custom-call | flops 1610000000 | tf_op jit(solution)/shard_map/entering/pallas_call | solution.py:409
  52.7 0.2 collective-permute-start.13
  52.9 1.5 %collective-permute-start.14 = (bf16[128,128]{1,0:T(8,128)(2,1)S(1)}, bf16[128,128]{1,0:T(8,128)(2,1)S(1)}, u32[]{:S(2)}, u32[]{:S(2)}) collective-permute-start(bf16[128,128]{1,0:T(8,128)(2,1)S(1)} %get-tuple-element.33), channel_id=1, source_target_pairs={{0,2},{1,3},{2,0},{3,1},{4,6},{5,7},{6,4},{7,5},{8,10},{9,11},{10,... | collective-permute-start | bytes 98312 | tf_op jit(solution)/shard_map/ppermute | solution.py:466
  54.3 0.3 collective-permute-start.15
  54.6 2.1 %collective-permute-done.14.across = bf16[128,128]{1,0:T(8,128)(2,1)S(1)} collective-permute-done((bf16[128,128]{1,0:T(8,128)(2,1)S(1)}, bf16[128,128]{1,0:T(8,128)(2,1)S(1)}, u32[]{:S(2)}, u32[]{:S(2)}) %collective-permute-start.14) | collective-permute-done | bytes 32800 | tf_op jit(solution)/shard_map/ppermute | solution.py:466
  56.8 1.0 %collective-permute-done.15.far = bf16[128,128]{1,0:T(8,128)(2,1)S(1)} collective-permute-done((bf16[128,128]{1,0:T(8,128)(2,1)S(1)}, bf16[128,128]{1,0:T(8,128)(2,1)S(1)}, u32[]{:S(2)}, u32[]{:S(2)}) %collective-permute-start.15) | collective-permute-done | bytes 32800 | tf_op jit(solution)/shard_map/ppermute | solution.py:470
  57.8 1.3 %waves.1 = bf16[2,1024,128]{2,1,0:T(8,128)(2,1)} custom-call(bf16[128,128]{1,0:T(8,128)(2,1)S(1)} %get-tuple-element.31.own, bf16[128,128]{1,0:T(8,128)(2,1)S(1)} %collective-permute-done.13.near, bf16[128,128]{1,0:T(8,128)(2,1)S(1)} %collective-permute-done.14.across, bf16[128,128]{1,0:T(8,128)(2,1)S(1)} %collective-permute-done.15.far, ...), custom_call_target="tpu_custom_call" | custom-call | flops 1495000064 | tf_op jit(solution)/shard_map/waves/pallas_call | solution.py:451
  (19 shorter events, 0.0 us)
Async XLA Ops:
  0.0 11.8 %copy-start.4 = (bf16[1,1024,256]{2,1,0:T(8,128)(2,1)S(1)}, bf16[1,1024,256]{2,1,0:T(8,128)(2,1)}, u32[]{:S(2)}) copy-start(bf16[1,1024,256]{2,1,0:T(8,128)(2,1)} %param.8) | copy-start | bytes 1572868
  0.0 11.8 %copy-start.6 = (s32[1,8,2]{1,2,0:T(2,128)S(1)}, s32[1,8,2]{1,2,0:T(2,128)}, u32[]{:S(2)}) copy-start(s32[1,8,2]{1,2,0:T(2,128)} %param.9) | copy-start | bytes 196
  4.5 22.8 %all-to-all-start = ((bf16[16,144,128]{2,1,0:T(8,128)(2,1)}), bf16[16,144,128]{2,1,0:T(8,128)(2,1)S(1)}, u32[]{:S(2)}, u32[]{:S(2)}) async-start(bf16[16,144,128]{2,1,0:T(8,128)(2,1)} %pairs.1), calls=%async_computation | async-start | bytes 1179648 | tf_op jit(solution)/shard_map/all_to_all | solution.py:511
  11.8 2.2 %copy-start = (bf16[1,2,1024,1024]{3,2,1,0:T(8,128)(2,1)S(1)}, bf16[1,2,1024,1024]{3,2,1,0:T(8,128)(2,1)}, u32[]{:S(2)}) copy-start(bf16[1,2,1024,1024]{3,2,1,0:T(8,128)(2,1)} %param.6) | copy-start | bytes 12582916
  15.1 11.3 %collective-permute-start = (f32[256,256]{1,0:T(8,128)S(1)}, f32[256,256]{1,0:T(8,128)S(1)}, u32[]{:S(2)}, u32[]{:S(2)}) collective-permute-start(f32[256,256]{1,0:T(8,128)S(1)} %get-tuple-element.21), channel_id=1, source_target_pairs={{0,2},{1,3},{2,0},{3,1},{4,6},{5,7},{6,4},{7,5},{8,10},{9,11},{10,... | collective-permute-start | bytes 786440 | tf_op jit(solution)/shard_map/ppermute | solution.py:466
  17.1 17.7 %collective-permute-start.4 = (f32[256,256]{1,0:T(8,128)S(1)}, f32[256,256]{1,0:T(8,128)S(1)}, u32[]{:S(2)}, u32[]{:S(2)}) collective-permute-start(f32[256,256]{1,0:T(8,128)S(1)} %get-tuple-element.26.own), channel_id=1, source_target_pairs={{0,1},{1,0},{2,3},{3,2},{4,5},{5,4},{6,7},{7,6},{8,9},{9,8},{10,11... | collective-permute-start | bytes 786440 | tf_op jit(solution)/shard_map/ppermute | solution.py:462
  18.3 1.0 %copy-start.2 = (bf16[2,1024,256]{2,1,0:T(8,128)(2,1)}, bf16[2,1024,256]{2,1,0:T(8,128)(2,1)S(1)}, u32[]{:S(2)}) copy-start(bf16[2,1024,256]{2,1,0:T(8,128)(2,1)S(1)} %prop.1._prop) | copy-start | bytes 3145732
  26.4 1.0 %copy-start.7 = (f32[256,256]{1,0:T(8,128)}, f32[256,256]{1,0:T(8,128)S(1)}, u32[]{:S(2)}) copy-start(f32[256,256]{1,0:T(8,128)S(1)} %collective-permute-done._map) | copy-start | bytes 786436
  27.3 0.8 %copy-start.11 = (bf16[16,144,128]{2,1,0:T(8,128)(2,1)}, bf16[16,144,128]{2,1,0:T(8,128)(2,1)S(1)}, u32[]{:S(2)}) copy-start(bf16[16,144,128]{2,1,0:T(8,128)(2,1)S(1)} %all-to-all-done.received) | copy-start | bytes 1769476
  31.8 18.1 %copy-start.1 = (bf16[1,2,1024,1024]{3,2,1,0:T(8,128)(2,1)S(1)}, bf16[1,2,1024,1024]{3,2,1,0:T(8,128)(2,1)}, u32[]{:S(2)}) copy-start(bf16[1,2,1024,1024]{3,2,1,0:T(8,128)(2,1)} %param.6) | copy-start | bytes 12582916
  31.8 18.1 %copy-start.5 = (bf16[2,1024,128]{2,1,0:T(8,128)(2,1)S(1)}, bf16[2,1024,128]{2,1,0:T(8,128)(2,1)}, u32[]{:S(2)}) copy-start(bf16[2,1024,128]{2,1,0:T(8,128)(2,1)} %get-tuple-element.30.source) | copy-start | bytes 1572868
  31.9 2.9 %collective-permute-start.5 = (f32[256,256]{1,0:T(8,128)}, f32[256,256]{1,0:T(8,128)S(1)}, u32[]{:S(2)}, u32[]{:S(2)}) collective-permute-start(f32[256,256]{1,0:T(8,128)} %get-tuple-element.27.across), channel_id=1, source_target_pairs={{0,1},{1,0},{2,3},{3,2},{4,5},{5,4},{6,7},{7,6},{8,9},{9,8},{10,11... | collective-permute-start | bytes 786440 | tf_op jit(solution)/shard_map/ppermute | solution.py:462
  31.9 11.8 %collective-permute-start.1 = (bf16[128,128]{1,0:T(8,128)(2,1)}, bf16[128,128]{1,0:T(8,128)(2,1)S(1)}, u32[]{:S(2)}, u32[]{:S(2)}) collective-permute-start(bf16[128,128]{1,0:T(8,128)(2,1)} %get-tuple-element.23), channel_id=1, source_target_pairs={{0,1},{1,0},{2,3},{3,2},{4,5},{5,4},{6,7},{7,6},{8,9},{9,8},{10,11... | collective-permute-start | bytes 98312 | tf_op jit(solution)/shard_map/ppermute | solution.py:462
  32.4 11.3 %collective-permute-start.2 = (bf16[128,128]{1,0:T(8,128)(2,1)}, bf16[128,128]{1,0:T(8,128)(2,1)S(1)}, u32[]{:S(2)}, u32[]{:S(2)}) collective-permute-start(bf16[128,128]{1,0:T(8,128)(2,1)} %get-tuple-element.24), channel_id=1, source_target_pairs={{0,2},{1,3},{2,0},{3,1},{4,6},{5,7},{6,4},{7,5},{8,10},{9,11},{10,... | collective-permute-start | bytes 98312 | tf_op jit(solution)/shard_map/ppermute | solution.py:466
  34.7 9.0 %collective-permute-start.3 = (bf16[128,128]{1,0:T(8,128)(2,1)}, bf16[128,128]{1,0:T(8,128)(2,1)S(1)}, u32[]{:S(2)}, u32[]{:S(2)}) collective-permute-start(bf16[128,128]{1,0:T(8,128)(2,1)} %get-tuple-element.25), channel_id=1, source_target_pairs={{0,3},{1,2},{2,1},{3,0},{4,7},{5,6},{6,5},{7,4},{8,11},{9,10},{10,... | collective-permute-start | bytes 98312 | tf_op jit(solution)/shard_map/ppermute | solution.py:470
  34.7 1.0 %copy-start.8 = (f32[256,256]{1,0:T(8,128)S(1)}, f32[256,256]{1,0:T(8,128)}, u32[]{:S(2)}) copy-start(f32[256,256]{1,0:T(8,128)} %get-tuple-element.27.across) | copy-start | bytes 786436
  36.6 12.8 %collective-permute-start.11 = (bf16[128,256]{1,0:T(8,128)(2,1)S(1)}, bf16[128,256]{1,0:T(8,128)(2,1)S(1)}, u32[]{:S(2)}, u32[]{:S(2)}) collective-permute-start(bf16[128,256]{1,0:T(8,128)(2,1)S(1)} %get-tuple-element.29), channel_id=1, source_target_pairs={{0,8},{1,9},{2,10},{3,11},{4,12},{5,13},{6,14},{7,15},{16,24},{17,... | collective-permute-start | bytes 196616 | tf_op jit(solution)/shard_map/ppermute | solution.py:488
  40.8 8.7 %collective-permute-start.9 = (bf16[128,256]{1,0:T(8,128)(2,1)S(1)}, bf16[128,256]{1,0:T(8,128)(2,1)S(1)}, u32[]{:S(2)}, u32[]{:S(2)}) collective-permute-start(bf16[128,256]{1,0:T(8,128)(2,1)S(1)} %get-tuple-element.29), channel_id=1, source_target_pairs={{0,4},{1,5},{2,6},{3,7},{4,8},{5,9},{6,10},{7,11},{8,12},{9,13},{1... | collective-permute-start | bytes 196616 | tf_op jit(solution)/shard_map/ppermute | solution.py:488
  43.7 0.8 %copy-start.9 = (bf16[128,128]{1,0:T(8,128)(2,1)S(1)}, bf16[128,128]{1,0:T(8,128)(2,1)}, u32[]{:S(2)}) copy-start(bf16[128,128]{1,0:T(8,128)(2,1)} %get-tuple-element.22.own.refs_9_) | copy-start | bytes 98308
  44.5 6.8 %copy-start.10 = (bf16[128,128]{1,0:T(8,128)(2,1)S(1)}, bf16[128,128]{1,0:T(8,128)(2,1)}, u32[]{:S(2)}) copy-start(bf16[128,128]{1,0:T(8,128)(2,1)} %get-tuple-element.22.own.refs_9_) | copy-start | bytes 98308
  45.4 5.8 %collective-permute-start.8 = (bf16[128,128]{1,0:T(8,128)(2,1)S(1)}, bf16[128,128]{1,0:T(8,128)(2,1)S(1)}, u32[]{:S(2)}, u32[]{:S(2)}) collective-permute-start(bf16[128,128]{1,0:T(8,128)(2,1)S(1)} %plane_total.1), channel_id=1, source_target_pairs={{0,12},{1,13},{2,14},{3,15},{16,28},{17,29},{18,30},{19,31}} | collective-permute-start | bytes 98312 | tf_op jit(solution)/shard_map/ppermute | solution.py:488
  46.7 4.5 %collective-permute-start.7 = (bf16[128,128]{1,0:T(8,128)(2,1)S(1)}, bf16[128,128]{1,0:T(8,128)(2,1)S(1)}, u32[]{:S(2)}, u32[]{:S(2)}) collective-permute-start(bf16[128,128]{1,0:T(8,128)(2,1)S(1)} %plane_total.1), channel_id=1, source_target_pairs={{0,8},{1,9},{2,10},{3,11},{4,12},{5,13},{6,14},{7,15},{16,24},{17,... | collective-permute-start | bytes 98312 | tf_op jit(solution)/shard_map/ppermute | solution.py:488
  48.0 3.2 %collective-permute-start.6 = (bf16[128,128]{1,0:T(8,128)(2,1)S(1)}, bf16[128,128]{1,0:T(8,128)(2,1)S(1)}, u32[]{:S(2)}, u32[]{:S(2)}) collective-permute-start(bf16[128,128]{1,0:T(8,128)(2,1)S(1)} %plane_total.1), channel_id=1, source_target_pairs={{0,4},{1,5},{2,6},{3,7},{4,8},{5,9},{6,10},{7,11},{8,12},{9,13},{1... | collective-permute-start | bytes 98312 | tf_op jit(solution)/shard_map/ppermute | solution.py:488
  49.4 1.9 %collective-permute-start.12 = (bf16[128,256]{1,0:T(8,128)(2,1)S(1)}, bf16[128,256]{1,0:T(8,128)(2,1)S(1)}, u32[]{:S(2)}, u32[]{:S(2)}) collective-permute-start(bf16[128,256]{1,0:T(8,128)(2,1)S(1)} %collective-permute-done.11.refs_5_), channel_id=1, source_target_pairs={{0,1},{1,0},{2,3},{3,2},{4,5},{5,4},{6,7},{7,6},{8,9},{9,8},{10,11... | collective-permute-start | bytes 196616 | tf_op jit(solution)/shard_map/ppermute | solution.py:462
  49.5 1.7 %collective-permute-start.10 = (bf16[128,256]{1,0:T(8,128)(2,1)S(1)}, bf16[128,256]{1,0:T(8,128)(2,1)S(1)}, u32[]{:S(2)}, u32[]{:S(2)}) collective-permute-start(bf16[128,256]{1,0:T(8,128)(2,1)S(1)} %collective-permute-done.9.refs_3_), channel_id=1, source_target_pairs={{0,1},{1,0},{2,3},{3,2},{4,5},{5,4},{6,7},{7,6},{8,9},{9,8},{10,11... | collective-permute-start | bytes 196616 | tf_op jit(solution)/shard_map/ppermute | solution.py:462
  51.2 6.6 %copy-start.3 = (bf16[2,1024,256]{2,1,0:T(8,128)(2,1)S(1)}, bf16[2,1024,256]{2,1,0:T(8,128)(2,1)}, u32[]{:S(2)}) copy-start(bf16[2,1024,256]{2,1,0:T(8,128)(2,1)} %copy-done.2) | copy-start | bytes 3145732
  52.7 1.9 %collective-permute-start.13 = (bf16[128,128]{1,0:T(8,128)(2,1)S(1)}, bf16[128,128]{1,0:T(8,128)(2,1)S(1)}, u32[]{:S(2)}, u32[]{:S(2)}) collective-permute-start(bf16[128,128]{1,0:T(8,128)(2,1)S(1)} %get-tuple-element.32), channel_id=1, source_target_pairs={{0,1},{1,0},{2,3},{3,2},{4,5},{5,4},{6,7},{7,6},{8,9},{9,8},{10,11... | collective-permute-start | bytes 98312 | tf_op jit(solution)/shard_map/ppermute | solution.py:462
  52.9 3.9 %collective-permute-start.14 = (bf16[128,128]{1,0:T(8,128)(2,1)S(1)}, bf16[128,128]{1,0:T(8,128)(2,1)S(1)}, u32[]{:S(2)}, u32[]{:S(2)}) collective-permute-start(bf16[128,128]{1,0:T(8,128)(2,1)S(1)} %get-tuple-element.33), channel_id=1, source_target_pairs={{0,2},{1,3},{2,0},{3,1},{4,6},{5,7},{6,4},{7,5},{8,10},{9,11},{10,... | collective-permute-start | bytes 98312 | tf_op jit(solution)/shard_map/ppermute | solution.py:466
  54.3 3.4 %collective-permute-start.15 = (bf16[128,128]{1,0:T(8,128)(2,1)S(1)}, bf16[128,128]{1,0:T(8,128)(2,1)S(1)}, u32[]{:S(2)}, u32[]{:S(2)}) collective-permute-start(bf16[128,128]{1,0:T(8,128)(2,1)S(1)} %get-tuple-element.34), channel_id=1, source_target_pairs={{0,3},{1,2},{2,1},{3,0},{4,7},{5,6},{6,5},{7,4},{8,11},{9,10},{10,... | collective-permute-start | bytes 98312 | tf_op jit(solution)/shard_map/ppermute | solution.py:470

commit v10 on v9

--- a/solution.py
+++ b/solution.py
@@ -17,7 +17,6 @@
 F32 = jnp.float32
 BF16 = jnp.bfloat16
 VMEM_SMALL = 16 * 1024 * 1024
-VMEM_MOST = 60500000
 VMEM_WHOLE = 63400000
 PEAK = 1.15e9
 
@@ -187,13 +186,15 @@
     )(owner, blocks, green, inject)
 
 
-def maps_kernel(pattern, green, coupling, couple, own, other, maps):
+def maps_kernel(pattern, green, coupling, own, other, face_rows, couple, maps):
     energies, orbitals, _ = green.shape
     face = coupling.shape[1]
     couple[...] = coupling[...]
     mask_tiles(pattern, couple)
     for e in range(energies):
-        maps[e] = dot(green[e, orbitals - face :, :], couple[...])
+        rows = green[e, orbitals - face :, :]
+        face_rows[e] = rows
+        maps[e] = dot(rows, couple[...])
     mine = place() // CORES
     own[...] = maps[mine]
     other[...] = maps[1 - mine]
@@ -206,86 +207,60 @@
         maps_kernel,
         "face_maps",
         [IN_SMEM, IN_VMEM, IN_VMEM],
-        [shape(orbitals, face), square, square],
-        [pltpu.VMEM((green.shape[0], face, face), F32)],
-        1.1,
+        [square, square, shape(green.shape[0], face, orbitals)],
+        [pltpu.VMEM(coupling.shape, BF16), pltpu.VMEM((green.shape[0], face, face), F32)],
+        1.2,
     )(pattern, green, coupling)
 
 
-def prop_kernel(green, couple, out):
+def products_kernel(pattern, green, coupling, source, image, prop, couple):
+    couple[...] = coupling[...]
+    mask_tiles(pattern, couple)
     for e in range(green.shape[0]):
-        out[e] = dot(green[e], couple[...]).astype(BF16)
-
-
-def propagator(green, couple):
+        image[e] = dot(green[e], source[e])
+        prop[e] = dot(green[e], couple[...]).astype(BF16)
+
+
+def products(pattern, green, coupling, source):
     energies, orbitals, _ = green.shape
     return call(
-        prop_kernel,
-        "prop",
-        [IN_VMEM, IN_VMEM],
-        shape(energies, orbitals, couple.shape[1]),
-        [],
-        1.3,
-    )(green, couple)
-
-
-def image_kernel(green, source, out):
-    for e in range(green.shape[0]):
-        out[e] = dot(green[e], source[e])
-
-
-def images(green, source):
-    return call(
-        image_kernel,
-        "image",
-        [IN_VMEM] * 2,
-        shape(*source.shape, dtype=F32),
-        [],
-        1.2,
-    )(green, source)
+        products_kernel,
+        "image_and_prop",
+        [IN_SMEM] + [IN_VMEM] * 3,
+        [shape(*source.shape, dtype=F32), shape(energies, orbitals, coupling.shape[1])],
+        [pltpu.VMEM(coupling.shape, BF16)],
+        2.4,
+    )(pattern, green, coupling, source)
 
 
 def times(a, b):
     return dot(a[0], b[0]) + (dot(a[0], b[1]) + dot(a[1], b[0]))
 
 
-def chain_kernel(own, near, across, far, total_out, parts, maps, total):
+def chain_kernel(own, near, across, far, total_out, parts, maps):
     collect((own, near, across, far), maps)
     split = [two_parts(maps[j]) for j in range(GROUP)]
     lower, upper = two_parts(times(split[1], split[0])), two_parts(times(split[3], split[2]))
-    total[...] = times(upper, lower)
-    rows = total_out.shape[0]
-    core = place() % CORES if rows < total.shape[0] else 0
-    total_out[...] = total[pl.ds(pl.multiple_of(core * rows, rows), rows), :].astype(total_out.dtype)
+    total_out[...] = times(upper, lower).astype(total_out.dtype)
     for j, (high, low) in enumerate(split):
         parts[0, j] = high
         parts[1, j] = low
 
 
-def chain(maps, few):
+def chain(maps, dtype):
     face = maps[0].shape[0]
-    total = shape(face // CORES, face) if few else shape(face, face, dtype=F32)
     return call(
         chain_kernel,
         "chain_maps",
         [IN_VMEM] * GROUP,
-        [total, shape(2, GROUP, face, face)],
-        [pltpu.VMEM((GROUP, face, face), F32), pltpu.VMEM((face, face), F32)],
+        [shape(face, face, dtype=dtype), shape(2, GROUP, face, face)],
+        [pltpu.VMEM((GROUP, face, face), F32)],
         0.9,
     )(*maps)
 
 
-def source_kernel(
-    received, inject, green, _prop, _map, source, own, near, across, far, _same_map, face_rows, quarters, total, heads, targets, sem, rows_sem
-):
+def source_kernel(received, inject, face_rows, _map, source, own, near, across, far, _same_map, quarters, total, heads, targets, sem):
     energies, orbitals, columns = inject.shape
-    face = face_rows.shape[1]
-    moves = [
-        pltpu.make_async_copy(green.at[e, pl.ds(orbitals - face, face)], face_rows.at[e], rows_sem.at[e])
-        for e in range(energies)
-    ]
-    for move in moves:
-        move.start()
     sections = received.shape[0]
     half = quarters.shape[1]
     rows = CAP * energies * BLK
@@ -313,7 +288,6 @@
     split = GROUP // energies
     for e in range(energies):
         source[e] = total[e].astype(BF16)
-        moves[e].wait()
         tall = dot(face_rows[e], source[e])
         quarters[e * split] = pack(tall)
         second = jnp.where(left_lanes(tall[:half]), swap_lanes(tall[:half]), tall[half:])
@@ -321,28 +295,25 @@
     deal(quarters, (own, near, across, far))
 
 
-def placed_source(received, inject, green, prop, passed):
-    face = passed.shape[0]
+def placed_source(received, inject, face_rows, passed):
+    face = face_rows.shape[1]
     energies, orbitals, columns = inject.shape
     sections = received.shape[0]
     return call(
         source_kernel,
         "source_and_face",
-        [IN_VMEM, IN_VMEM, IN_HBM, IN_PLACE, IN_PLACE],
+        [IN_VMEM, IN_VMEM, IN_VMEM, IN_PLACE],
         [shape(*inject.shape)] + [shape(face // 2, columns)] * GROUP + [shape(*passed.shape, dtype=passed.dtype)],
         [
-            pltpu.VMEM((energies, face, orbitals), BF16),
             pltpu.VMEM((GROUP, face // 2, columns), F32),
             pltpu.VMEM(inject.shape, F32),
             pltpu.VMEM((sections, columns), jnp.int32),
             pltpu.SMEM((sections, columns), jnp.int32),
             pltpu.SemaphoreType.DMA,
-            pltpu.SemaphoreType.DMA((energies,)),
         ],
-        1.8,
-        VMEM_MOST,
-        aliases={4: 1 + GROUP},
-    )(received, inject, green, prop, passed)
+        1.4,
+        aliases={3: 1 + GROUP},
+    )(received, inject, face_rows, passed)
 
 
 def deal(items, outs):
@@ -375,23 +346,20 @@
         [IN_VMEM] * (GROUP + 1),
         shape(half, columns),
         [pltpu.VMEM((GROUP, half, columns), BF16)],
-        0.9,
+        3.0,
     )(*shifts, parts)
 
 
-def entering_kernel(count, *refs):
-    below, maps = refs[:count], refs[count : 3 * count - 2]
-    parts, _image = refs[3 * count - 2 : 3 * count]
-    arrived, out = refs[3 * count : 3 * count + GROUP], refs[3 * count + GROUP : -2]
-    shifts, held = refs[-2:]
+def entering_kernel(first, second, third, got, other, parts, _image, *refs):
+    arrived, out = refs[:GROUP], refs[GROUP : 2 * GROUP]
+    shifts, held = refs[2 * GROUP :]
     collect(arrived, shifts)
     first_core = place() % CORES == 0
-    state = unpack(below[-1][...].astype(F32))
-    for k in range(count - 2, -1, -1):
+    state = unpack(third[...].astype(F32))
+    for below, (one, two) in ((second, (other, got)), (first, (got, other))):
+        factor = jnp.where(first_core, one[...], two[...])
         high, low = two_parts(state)
-        mine, other = (dot(half[...], high) + dot(half[...], low) for half in maps[2 * k : 2 * k + 2])
-        top, bottom = jnp.where(first_core, mine, other), jnp.where(first_core, other, mine)
-        state = unpack(below[k][...].astype(F32)) + jnp.concatenate([top, bottom], axis=0)
+        state = unpack(below[...].astype(F32)) + dot(factor, high) + dot(factor, low)
     sweep_plane(state, parts, shifts, held, out)
 
 
@@ -405,11 +373,10 @@
 
 def entering(below, maps, parts, shifts, tie):
     half, columns = below[0].shape
-    count = len(below)
-    return call(
-        functools.partial(entering_kernel, count),
+    return call(
+        entering_kernel,
         "entering",
-        [IN_VMEM] * (3 * count - 1) + [IN_PLACE] + [IN_VMEM] * GROUP,
+        [IN_VMEM] * 6 + [IN_PLACE] + [IN_VMEM] * GROUP,
         [shape(half, columns)] * GROUP,
         [pltpu.VMEM((GROUP, half, columns), BF16), pltpu.VMEM((GROUP, half, columns), F32)],
         1.4,
@@ -482,6 +449,17 @@
 def spread(packed):
     half = packed.shape[1] // 2
     return jnp.concatenate([packed[:, :half], packed[:, half:]], axis=0)
+
+
+def maps_up(total_map, sections):
+    pairs = []
+    for i in range(GROUP):
+        if i % CORES == 0:
+            pairs += [(GROUP + i, 2 * GROUP + i), (2 * GROUP + i, 3 * GROUP + i)]
+        else:
+            pairs += [(GROUP + i, 3 * GROUP + i)]
+    got = lax.ppermute(total_map, "sec", pairs)
+    return got, to_near(got, sections)
 
 
 def upward(item, k, sections):
@@ -510,22 +488,20 @@
     outgoing = outgoing_pairs(owner[:, 0], pair_blocks.T, green, inject, sections)
     received = lax.all_to_all(outgoing, "sec", split_axis=0, concat_axis=0, tiled=True)
 
-    couple, own_map, other_map = face_maps(tiles, green, coupling)
+    own_map, other_map, face_rows = face_maps(tiles, green, coupling)
     across = to_across(other_map, sections)
     near = to_near(own_map, sections)
-    prop = propagator(green, couple)
-
-    source, *quarters, across = placed_source(received, inject, green, prop, across)
+
+    source, *quarters, across = placed_source(received, inject, face_rows, across)
     shifts = exchange(*quarters, sections)
     far = to_near(across, sections)
-    planes = sections // GROUP
-    total_map, parts = chain([own_map, near, across, far], planes <= 4)
-    image = images(green, source)
-    if planes <= 4:
-        halves = [upward(total_map, k, sections) for k in range(1, planes - 1)]
-        maps = [half for mine in halves for half in (mine, to_near(mine, sections))]
+    four = sections // GROUP == 4
+    total_map, parts = chain([own_map, near, across, far], BF16 if four else F32)
+    image, prop = products(tiles, green, coupling, source)
+    if four:
+        maps = maps_up(total_map, sections)
         total = plane_total(shifts, parts)
-        below = [upward(total, k, sections) for k in range(1, planes)]
+        below = [upward(total, k, sections) for k in range(1, 4)]
         entered = entering(below, maps, parts, shifts, image)
     else:
         total = plane_total(shifts, parts)

time: 59.7 us -> 55.5 us (0.930)
  waiting for transfers between devices: 11.2 us -> 15.2 us
  local copies, waits for them, and re-layouts: 5.7 us -> 2.2 us
  starting transfers between devices: 25.7 us -> 22.9 us
  Pallas kernels: 16.3 us -> 14.6 us
    ppermute x3, waiting for transfers between devices: 9.19 us -> 12.8 us  [to_across(): lax.ppermute(item, 'sec', [(s, s // GROUP * GROUP + (s % GROUP + CORES) %...]
    unnamed x24 -> x10, local copies, waits for them, and re-layouts: 5.7 us -> 2.2 us
    ppermute x5 -> x3, starting transfers between devices: 11 us -> 8.51 us  [upward(): return lax.ppermute(item, 'sec', up_shift(sections, k))]
    pallas_call x6 -> x5, Pallas kernels: 9.51 us -> 7.83 us  [the longest x1 3.04 us: products(): call(products_kernel, 'image_and_prop', [IN_SMEM] + [IN_VMEM] * 3, [shape...]
    ppermute x3, starting transfers between devices: 5.77 us -> 4.21 us  [to_across(): lax.ppermute(item, 'sec', [(s, s // GROUP * GROUP + (s % GROUP + CORES) %...]
    ppermute x0 -> x1, starting transfers between devices: none -> 0.67 us  [maps_up(): got = lax.ppermute(total_map, 'sec', pairs)]
    ppermute x6 -> x5, starting transfers between devices: 1.31 us -> 1.19 us  [to_near(): return lax.ppermute(item, 'sec', [(s, s ^ 1) for s in range(sections)])]
  transfers between devices with their start and end apart: 17 -> 15, of which waited for: 4 -> 6; matrix products, arithmetic and copies ran while one was open for 0% -> 0% of each run, Pallas kernels for 15% -> 13%
where the time goes in v10:
time: 55.5 us; the launch traced here: 55.1 us
  starting transfers between devices  22.9 us (41%)
  waiting for transfers between devices  15.2 us (27%)
  Pallas kernels  14.6 us (26%)
  local copies, waits for them, and re-layouts  2.2 us (4%)
    ppermute x3, waiting for transfers between devices, to_across(): lax.ppermute(item, 'sec', [(s, s // GROUP * GROUP + (s % GROUP + CORES) %...  12.8 us
    ppermute x3, starting transfers between devices, upward(): return lax.ppermute(item, 'sec', up_shift(sections, k))  8.51 us
    all_to_all x1, starting transfers between devices, per_device(): lax.all_to_all(outgoing, 'sec', split_axis=0, concat_axis=0, tiled=True)  7.54 us
    pallas_call x1, Pallas kernels, outgoing_pairs(): call(pairs_kernel, 'pairs', [IN_HBM] * 4, shape(sections, CAP * energies...  4.48 us
    ppermute x3, starting transfers between devices, to_across(): lax.ppermute(item, 'sec', [(s, s // GROUP * GROUP + (s % GROUP + CORES) %...  4.21 us
    pallas_call x1, Pallas kernels, products(): call(products_kernel, 'image_and_prop', [IN_SMEM] + [IN_VMEM] * 3, [shape...  3.04 us
    unnamed x10, local copies, waits for them, and re-layouts  2.2 us
    ppermute x2, waiting for transfers between devices, to_far(): lax.ppermute(item, 'sec', [(s, s // GROUP * GROUP + (s % GROUP + CORES) %...  1.43 us
  transfers between devices with their start and end apart: 15, of which 6 were waited for; matrix products, arithmetic and copies ran while one was open for 0% of the time, Pallas kernels for 13%

profile of v10, /device:TPU:0, one launch (start us, length us, event | category | flops | bytes accessed | tf_op | source)
XLA Modules:
  0.0 55.1 jit_solution(3560241271517342158)
XLA Ops:
  0.0 0.0 copy-start.3
  0.0 0.0 copy-start.4
  0.0 4.5 %pairs.1 = bf16[16,144,128]{2,1,0:T(8,128)(2,1)} custom-call(s32[16]{0:T(128)} %bitcast.19, s32[2,16]{1,0:T(2,128)} %bitcast.18, bf16[2,1024,1024]{2,1,0:T(8,128)(2,1)} %bitcast.9, bf16[2,1024,128]{2,1,0:T(8,128)(2,1)} %bitcast.12), custom_call_target="tpu_custom_call" | custom-call | flops 4600000000 | tf_op jit(solution)/shard_map/pairs/pallas_call | solution.py:168
  4.5 0.0 copy-start.2
  4.5 7.5 %all-to-all-start = ((bf16[16,144,128]{2,1,0:T(8,128)(2,1)}), bf16[16,144,128]{2,1,0:T(8,128)(2,1)S(1)}, u32[]{:S(2)}, u32[]{:S(2)}) async-start(bf16[16,144,128]{2,1,0:T(8,128)(2,1)} %pairs.1), calls=%async_computation | async-start | bytes 1179648 | tf_op jit(solution)/shard_map/all_to_all | solution.py:489
  12.1 0.0 copy-done.3
  12.1 0.0 copy-done.4
  12.1 0.0 copy-start
  12.1 2.2 %copy-done = bf16[1,2,1024,1024]{3,2,1,0:T(8,128)(2,1)S(1)} copy-done((bf16[1,2,1024,1024]{3,2,1,0:T(8,128)(2,1)S(1)}, bf16[1,2,1024,1024]{3,2,1,0:T(8,128)(2,1)}, u32[]{:S(2)}) %copy-start) | copy-done | bytes 4194328
  14.3 1.1 %face_maps.1 = (f32[256,256]{1,0:T(8,128)S(1)}, f32[256,256]{1,0:T(8,128)S(1)}, bf16[2,256,1024]{2,1,0:T(8,128)(2,1)S(1)}) custom-call(s32[2,8]{1,0:T(2,128)S(1)} %bitcast.16, bf16[2,1024,1024]{2,1,0:T(8,128)(2,1)S(1)} %bitcast.10, bf16[1024,256]{1,0:T(8,128)(2,1)S(1)} %bitcast.14), custom_call_target="tpu_custom_call" | custom-call | flops 1380000000 | tf_op jit(solution)/shard_map/face_maps/pallas_call | solution.py:206
  15.4 2.0 %collective-permute-start = (f32[256,256]{1,0:T(8,128)S(1)}, f32[256,256]{1,0:T(8,128)S(1)}, u32[]{:S(2)}, u32[]{:S(2)}) collective-permute-start(f32[256,256]{1,0:T(8,128)S(1)} %get-tuple-element.23), channel_id=1, source_target_pairs={{0,2},{1,3},{2,0},{3,1},{4,6},{5,7},{6,4},{7,5},{8,10},{9,11},{10,... | collective-permute-start | bytes 786440 | tf_op jit(solution)/shard_map/ppermute | solution.py:433
  17.4 0.0 collective-permute-start.4
  17.4 9.3 %collective-permute-done._map = f32[256,256]{1,0:T(8,128)S(1)} collective-permute-done((f32[256,256]{1,0:T(8,128)S(1)}, f32[256,256]{1,0:T(8,128)S(1)}, u32[]{:S(2)}, u32[]{:S(2)}) %collective-permute-start) | collective-permute-done | bytes 262176 | tf_op jit(solution)/shard_map/ppermute | solution.py:433
  26.7 0.9 %all-to-all-done.received = bf16[16,144,128]{2,1,0:T(8,128)(2,1)S(1)} async-done(((bf16[16,144,128]{2,1,0:T(8,128)(2,1)}), bf16[16,144,128]{2,1,0:T(8,128)(2,1)S(1)}, u32[]{:S(2)}, u32[]{:S(2)}) %all-to-all-start) | async-done | bytes 589856 | tf_op jit(solution)/shard_map/all_to_all | solution.py:489
  27.6 0.0 copy-done.2
  27.6 1.4 %source_and_face.1 = (bf16[2,1024,128]{2,1,0:T(8,128)(2,1)S(1)}, bf16[128,128]{1,0:T(8,128)(2,1)S(1)}, bf16[128,128]{1,0:T(8,128)(2,1)S(1)}, bf16[128,128]{1,0:T...) custom-call(bf16[16,144,128]{2,1,0:T(8,128)(2,1)S(1)} %all-to-all-done.rec, ...), custom_call_target="tpu_custom_call", output_to_operand_aliasing={{5}: (3, {})} | custom-call | flops 1610000000 | tf_op jit(solution)/shard_map/source_and_face/pallas_call | solution.py:302
  29.0 0.1 collective-permute-start.5
  29.1 0.5 collective-permute-start.1
  29.6 1.6 %collective-permute-start.2 = (bf16[128,128]{1,0:T(8,128)(2,1)S(1)}, bf16[128,128]{1,0:T(8,128)(2,1)S(1)}, u32[]{:S(2)}, u32[]{:S(2)}) collective-permute-start(bf16[128,128]{1,0:T(8,128)(2,1)S(1)} %get-tuple-element.26), channel_id=1, source_target_pairs={{0,2},{1,3},{2,0},{3,1},{4,6},{5,7},{6,4},{7,5},{8,10},{9,11},{10,... | collective-permute-start | bytes 98312 | tf_op jit(solution)/shard_map/ppermute | solution.py:433
  31.2 0.0 collective-permute-start.3
  31.2 0.0 collective-permute-done.4.near
  31.2 0.0 collective-permute-done.5.far
  31.2 0.8 %chain_maps.1 = (bf16[256,256]{1,0:T(8,128)(2,1)S(1)}, bf16[2,4,256,256]{3,2,1,0:T(8,128)(2,1)S(1)}) custom-call(f32[256,256]{1,0:T(8,128)S(1)} %get-tuple-element.28.own, f32[256,256]{1,0:T(8,128)S(1)} %collective-permute-done.4.near, f32[256,256]{1,0:T(8,128)S(1)} %get-tuple-element.29.across, f32[256,256]{1,0:T(8,128)S(1)} %collective-permute-done.5.far), custom_call_target="tpu_custom_call" | custom-call | flops 1035000000 | tf_op jit(solution)/shard_map/chain_maps/pallas_call | solution.py:252
  32.1 0.7 %collective-permute-start.9 = (bf16[256,256]{1,0:T(8,128)(2,1)S(1)}, bf16[256,256]{1,0:T(8,128)(2,1)S(1)}, u32[]{:S(2)}, u32[]{:S(2)}) collective-permute-start(bf16[256,256]{1,0:T(8,128)(2,1)S(1)} %get-tuple-element.31), channel_id=1, source_target_pairs={{4,8},{8,12},{5,13},{6,10},{10,14},{7,15},{20,24},{24,28},{21,29},... | collective-permute-start | bytes 393224 | tf_op jit(solution)/shard_map/ppermute | solution.py:461
  32.7 0.0 collective-permute-done.1.near.refs_1_
  32.8 0.8 %collective-permute-done.2.across.refs_2_ = bf16[128,128]{1,0:T(8,128)(2,1)S(1)} collective-permute-done((bf16[128,128]{1,0:T(8,128)(2,1)S(1)}, bf16[128,128]{1,0:T(8,128)(2,1)S(1)}, u32[]{:S(2)}, u32[]{:S(2)}) %collective-permute-start.2) | collective-permute-done | bytes 32800 | tf_op jit(solution)/shard_map/ppermute | solution.py:433
  33.5 1.4 %collective-permute-done.3.far.refs_3_ = bf16[128,128]{1,0:T(8,128)(2,1)S(1)} collective-permute-done((bf16[128,128]{1,0:T(8,128)(2,1)S(1)}, bf16[128,128]{1,0:T(8,128)(2,1)S(1)}, u32[]{:S(2)}, u32[]{:S(2)}) %collective-permute-start.3) | collective-permute-done | bytes 32800 | tf_op jit(solution)/shard_map/ppermute | solution.py:437
  34.9 0.0 copy-start.1
  34.9 0.9 %plane_total.1 = bf16[128,128]{1,0:T(8,128)(2,1)S(1)} custom-call(bf16[128,128]{1,0:T(8,128)(2,1)S(1)} %get-tuple-element.24.own.refs_0_, bf16[128,128]{1,0:T(8,128)(2,1)S(1)} %collective-permute-done.1.near.refs_1_, bf16[128,128]{1,0:T(8,128)(2,1)S(1)} %collective-permute-done.2.across.refs_2_, bf16[128,128]{1,0:T(8,128)(2,1)S(1)} %collective-permute-done.3.far.refs_3_, ...), custom_call_target="tpu_custom_call" | custom-call | flops 3449999872 | tf_op jit(solution)/shard_map/plane_total/pallas_call | solution.py:343
  35.8 4.7 %collective-permute-start.8 = (bf16[128,128]{1,0:T(8,128)(2,1)S(1)}, bf16[128,128]{1,0:T(8,128)(2,1)S(1)}, u32[]{:S(2)}, u32[]{:S(2)}) collective-permute-start(bf16[128,128]{1,0:T(8,128)(2,1)S(1)} %plane_total.1), channel_id=1, source_target_pairs={{0,12},{1,13},{2,14},{3,15},{16,28},{17,29},{18,30},{19,31}} | collective-permute-start | bytes 98312 | tf_op jit(solution)/shard_map/ppermute | solution.py:466
  40.6 1.3 %collective-permute-start.7 = (bf16[128,128]{1,0:T(8,128)(2,1)S(1)}, bf16[128,128]{1,0:T(8,128)(2,1)S(1)}, u32[]{:S(2)}, u32[]{:S(2)}) collective-permute-start(bf16[128,128]{1,0:T(8,128)(2,1)S(1)} %plane_total.1), channel_id=1, source_target_pairs={{0,8},{1,9},{2,10},{3,11},{4,12},{5,13},{6,14},{7,15},{16,24},{17,... | collective-permute-start | bytes 98312 | tf_op jit(solution)/shard_map/ppermute | solution.py:466
  41.9 2.5 %collective-permute-start.6 = (bf16[128,128]{1,0:T(8,128)(2,1)S(1)}, bf16[128,128]{1,0:T(8,128)(2,1)S(1)}, u32[]{:S(2)}, u32[]{:S(2)}) collective-permute-start(bf16[128,128]{1,0:T(8,128)(2,1)S(1)} %plane_total.1), channel_id=1, source_target_pairs={{0,4},{1,5},{2,6},{3,7},{4,8},{5,9},{6,10},{7,11},{8,12},{9,13},{1... | collective-permute-start | bytes 98312 | tf_op jit(solution)/shard_map/ppermute | solution.py:466
  44.4 0.0 collective-permute-done.9.got
  44.4 0.1 collective-permute-start.10
  44.5 0.0 copy-done.1
  44.5 3.0 %image_and_prop.1 = (f32[2,1024,128]{2,1,0:T(8,128)S(1)}, bf16[2,1024,256]{2,1,0:T(8,128)(2,1)S(1)}) custom-call(s32[2,8]{1,0:T(2,128)S(1)} %bitcast.17, bf16[2,1024,1024]{2,1,0:T(8,128)(2,1)S(1)} %bitcast.11, bf16[1024,256]{1,0:T(8,128)(2,1)S(1)} %bitcast.15, bf16[2,1024,128]{2,1,0:T(8,128)(2,1)S(1)} %get-tuple-element.32.source), custom_call_target="tpu_custom_call" | custom-call | flops 2760000000 | tf_op jit(solution)/shard_map/image_and_prop/pallas_call | solution.py:226
  47.5 0.0 collective-permute-done.8.third
  47.5 0.0 collective-permute-done.7.second
  47.5 0.0 collective-permute-done.6.first
  47.5 0.0 collective-permute-done.10.other
  47.5 1.4 %entering.1 = (bf16[128,128]{1,0:T(8,128)(2,1)S(1)}, bf16[128,128]{1,0:T(8,128)(2,1)S(1)}, bf16[128,128]{1,0:T(8,128)(2,1)S(1)}, bf16[128,128]{1,0:T(8,128)(2,1)S(1)}) custom-call(bf16[128,128]{1,0:T(8,128)(2,1)S(1)} %collective-permute-done.6.first, bf16[128,128]{1,0:T(8,128)(2,1)S(1)} %collective-permute-done.7.second, ...), custom_call_target="tpu_custom_call" | custom-call | flops 1610000000 | tf_op jit(solution)/shard_map/entering/pallas_call | solution.py:376
  49.0 0.6 collective-permute-start.11
  49.5 0.6 %collective-permute-start.12 = (bf16[128,128]{1,0:T(8,128)(2,1)S(1)}, bf16[128,128]{1,0:T(8,128)(2,1)S(1)}, u32[]{:S(2)}, u32[]{:S(2)}) collective-permute-start(bf16[128,128]{1,0:T(8,128)(2,1)S(1)} %get-tuple-element.36), channel_id=1, source_target_pairs={{0,2},{1,3},{2,0},{3,1},{4,6},{5,7},{6,4},{7,5},{8,10},{9,11},{10,... | collective-permute-start | bytes 98312 | tf_op jit(solution)/shard_map/ppermute | solution.py:433
  50.1 0.8 %collective-permute-start.13 = (bf16[128,128]{1,0:T(8,128)(2,1)S(1)}, bf16[128,128]{1,0:T(8,128)(2,1)S(1)}, u32[]{:S(2)}, u32[]{:S(2)}) collective-permute-start(bf16[128,128]{1,0:T(8,128)(2,1)S(1)} %get-tuple-element.37), channel_id=1, source_target_pairs={{0,3},{1,2},{2,1},{3,0},{4,7},{5,6},{6,5},{7,4},{8,11},{9,10},{10,... | collective-permute-start | bytes 98312 | tf_op jit(solution)/shard_map/ppermute | solution.py:437
  50.9 0.0 collective-permute-done.11.near
  51.0 2.8 %collective-permute-done.12.across = bf16[128,128]{1,0:T(8,128)(2,1)S(1)} collective-permute-done((bf16[128,128]{1,0:T(8,128)(2,1)S(1)}, bf16[128,128]{1,0:T(8,128)(2,1)S(1)}, u32[]{:S(2)}, u32[]{:S(2)}) %collective-permute-start.12) | collective-permute-done | bytes 32800 | tf_op jit(solution)/shard_map/ppermute | solution.py:433
  53.8 0.1 collective-permute-done.13.far
  53.8 1.3 %waves.1 = bf16[2,1024,128]{2,1,0:T(8,128)(2,1)} custom-call(bf16[128,128]{1,0:T(8,128)(2,1)S(1)} %get-tuple-element.34.own, bf16[128,128]{1,0:T(8,128)(2,1)S(1)} %collective-permute-done.11.near, bf16[128,128]{1,0:T(8,128)(2,1)S(1)} %collective-permute-done.12.across, bf16[128,128]{1,0:T(8,128)(2,1)S(1)} %collective-permute-done.13.far, ...), custom_call_target="tpu_custom_call" | custom-call | flops 1495000064 | tf_op jit(solution)/shard_map/waves/pallas_call | solution.py:418
Async XLA Ops:
  0.0 12.1 %copy-start.3 = (bf16[1,1024,256]{2,1,0:T(8,128)(2,1)S(1)}, bf16[1,1024,256]{2,1,0:T(8,128)(2,1)}, u32[]{:S(2)}) copy-start(bf16[1,1024,256]{2,1,0:T(8,128)(2,1)} %param.8) | copy-start | bytes 1572868
  0.0 12.1 %copy-start.4 = (s32[1,8,2]{1,2,0:T(2,128)S(1)}, s32[1,8,2]{1,2,0:T(2,128)}, u32[]{:S(2)}) copy-start(s32[1,8,2]{1,2,0:T(2,128)} %param.9) | copy-start | bytes 196
  4.5 23.1 %copy-start.2 = (bf16[1,2,1024,128]{3,2,1,0:T(8,128)(2,1)S(1)}, bf16[1,2,1024,128]{3,2,1,0:T(8,128)(2,1)}, u32[]{:S(2)}) copy-start(bf16[1,2,1024,128]{3,2,1,0:T(8,128)(2,1)} %param.7) | copy-start | bytes 1572868
  4.5 23.1 %all-to-all-start = ((bf16[16,144,128]{2,1,0:T(8,128)(2,1)}), bf16[16,144,128]{2,1,0:T(8,128)(2,1)S(1)}, u32[]{:S(2)}, u32[]{:S(2)}) async-start(bf16[16,144,128]{2,1,0:T(8,128)(2,1)} %pairs.1), calls=%async_computation | async-start | bytes 1179648 | tf_op jit(solution)/shard_map/all_to_all | solution.py:489
  12.1 2.2 %copy-start = (bf16[1,2,1024,1024]{3,2,1,0:T(8,128)(2,1)S(1)}, bf16[1,2,1024,1024]{3,2,1,0:T(8,128)(2,1)}, u32[]{:S(2)}) copy-start(bf16[1,2,1024,1024]{3,2,1,0:T(8,128)(2,1)} %param.6) | copy-start | bytes 12582916
  15.4 11.3 %collective-permute-start = (f32[256,256]{1,0:T(8,128)S(1)}, f32[256,256]{1,0:T(8,128)S(1)}, u32[]{:S(2)}, u32[]{:S(2)}) collective-permute-start(f32[256,256]{1,0:T(8,128)S(1)} %get-tuple-element.23), channel_id=1, source_target_pairs={{0,2},{1,3},{2,0},{3,1},{4,6},{5,7},{6,4},{7,5},{8,10},{9,11},{10,... | collective-permute-start | bytes 786440 | tf_op jit(solution)/shard_map/ppermute | solution.py:433
  17.4 13.8 %collective-permute-start.4 = (f32[256,256]{1,0:T(8,128)S(1)}, f32[256,256]{1,0:T(8,128)S(1)}, u32[]{:S(2)}, u32[]{:S(2)}) collective-permute-start(f32[256,256]{1,0:T(8,128)S(1)} %get-tuple-element.28.own), channel_id=1, source_target_pairs={{0,1},{1,0},{2,3},{3,2},{4,5},{5,4},{6,7},{7,6},{8,9},{9,8},{10,11... | collective-permute-start | bytes 786440 | tf_op jit(solution)/shard_map/ppermute | solution.py:429
  29.0 2.2 %collective-permute-start.5 = (f32[256,256]{1,0:T(8,128)S(1)}, f32[256,256]{1,0:T(8,128)S(1)}, u32[]{:S(2)}, u32[]{:S(2)}) collective-permute-start(f32[256,256]{1,0:T(8,128)S(1)} %get-tuple-element.29.across), channel_id=1, source_target_pairs={{0,1},{1,0},{2,3},{3,2},{4,5},{5,4},{6,7},{7,6},{8,9},{9,8},{10,11... | collective-permute-start | bytes 786440 | tf_op jit(solution)/shard_map/ppermute | solution.py:429
  29.1 3.6 %collective-permute-start.1 = (bf16[128,128]{1,0:T(8,128)(2,1)S(1)}, bf16[128,128]{1,0:T(8,128)(2,1)S(1)}, u32[]{:S(2)}, u32[]{:S(2)}) collective-permute-start(bf16[128,128]{1,0:T(8,128)(2,1)S(1)} %get-tuple-element.25), channel_id=1, source_target_pairs={{0,1},{1,0},{2,3},{3,2},{4,5},{5,4},{6,7},{7,6},{8,9},{9,8},{10,11... | collective-permute-start | bytes 98312 | tf_op jit(solution)/shard_map/ppermute | solution.py:429
  29.6 3.9 %collective-permute-start.2 = (bf16[128,128]{1,0:T(8,128)(2,1)S(1)}, bf16[128,128]{1,0:T(8,128)(2,1)S(1)}, u32[]{:S(2)}, u32[]{:S(2)}) collective-permute-start(bf16[128,128]{1,0:T(8,128)(2,1)S(1)} %get-tuple-element.26), channel_id=1, source_target_pairs={{0,2},{1,3},{2,0},{3,1},{4,6},{5,7},{6,4},{7,5},{8,10},{9,11},{10,... | collective-permute-start | bytes 98312 | tf_op jit(solution)/shard_map/ppermute | solution.py:433
  31.2 3.7 %collective-permute-start.3 = (bf16[128,128]{1,0:T(8,128)(2,1)S(1)}, bf16[128,128]{1,0:T(8,128)(2,1)S(1)}, u32[]{:S(2)}, u32[]{:S(2)}) collective-permute-start(bf16[128,128]{1,0:T(8,128)(2,1)S(1)} %get-tuple-element.27), channel_id=1, source_target_pairs={{0,3},{1,2},{2,1},{3,0},{4,7},{5,6},{6,5},{7,4},{8,11},{9,10},{10,... | collective-permute-start | bytes 98312 | tf_op jit(solution)/shard_map/ppermute | solution.py:437
  32.1 12.3 %collective-permute-start.9 = (bf16[256,256]{1,0:T(8,128)(2,1)S(1)}, bf16[256,256]{1,0:T(8,128)(2,1)S(1)}, u32[]{:S(2)}, u32[]{:S(2)}) collective-permute-start(bf16[256,256]{1,0:T(8,128)(2,1)S(1)} %get-tuple-element.31), channel_id=1, source_target_pairs={{4,8},{8,12},{5,13},{6,10},{10,14},{7,15},{20,24},{24,28},{21,29},... | collective-permute-start | bytes 393224 | tf_op jit(solution)/shard_map/ppermute | solution.py:461
  34.9 9.6 %copy-start.1 = (bf16[1,2,1024,1024]{3,2,1,0:T(8,128)(2,1)S(1)}, bf16[1,2,1024,1024]{3,2,1,0:T(8,128)(2,1)}, u32[]{:S(2)}) copy-start(bf16[1,2,1024,1024]{3,2,1,0:T(8,128)(2,1)} %param.6) | copy-start | bytes 12582916
  35.8 11.7 %collective-permute-start.8 = (bf16[128,128]{1,0:T(8,128)(2,1)S(1)}, bf16[128,128]{1,0:T(8,128)(2,1)S(1)}, u32[]{:S(2)}, u32[]{:S(2)}) collective-permute-start(bf16[128,128]{1,0:T(8,128)(2,1)S(1)} %plane_total.1), channel_id=1, source_target_pairs={{0,12},{1,13},{2,14},{3,15},{16,28},{17,29},{18,30},{19,31}} | collective-permute-start | bytes 98312 | tf_op jit(solution)/shard_map/ppermute | solution.py:466
  40.6 6.9 %collective-permute-start.7 = (bf16[128,128]{1,0:T(8,128)(2,1)S(1)}, bf16[128,128]{1,0:T(8,128)(2,1)S(1)}, u32[]{:S(2)}, u32[]{:S(2)}) collective-permute-start(bf16[128,128]{1,0:T(8,128)(2,1)S(1)} %plane_total.1), channel_id=1, source_target_pairs={{0,8},{1,9},{2,10},{3,11},{4,12},{5,13},{6,14},{7,15},{16,24},{17,... | collective-permute-start | bytes 98312 | tf_op jit(solution)/shard_map/ppermute | solution.py:466
  41.9 5.6 %collective-permute-start.6 = (bf16[128,128]{1,0:T(8,128)(2,1)S(1)}, bf16[128,128]{1,0:T(8,128)(2,1)S(1)}, u32[]{:S(2)}, u32[]{:S(2)}) collective-permute-start(bf16[128,128]{1,0:T(8,128)(2,1)S(1)} %plane_total.1), channel_id=1, source_target_pairs={{0,4},{1,5},{2,6},{3,7},{4,8},{5,9},{6,10},{7,11},{8,12},{9,13},{1... | collective-permute-start | bytes 98312 | tf_op jit(solution)/shard_map/ppermute | solution.py:466
  44.4 3.2 %collective-permute-start.10 = (bf16[256,256]{1,0:T(8,128)(2,1)S(1)}, bf16[256,256]{1,0:T(8,128)(2,1)S(1)}, u32[]{:S(2)}, u32[]{:S(2)}) collective-permute-start(bf16[256,256]{1,0:T(8,128)(2,1)S(1)} %collective-permute-done.9.got), channel_id=1, source_target_pairs={{0,1},{1,0},{2,3},{3,2},{4,5},{5,4},{6,7},{7,6},{8,9},{9,8},{10,11... | collective-permute-start | bytes 393224 | tf_op jit(solution)/shard_map/ppermute | solution.py:429
  49.0 2.0 %collective-permute-start.11 = (bf16[128,128]{1,0:T(8,128)(2,1)S(1)}, bf16[128,128]{1,0:T(8,128)(2,1)S(1)}, u32[]{:S(2)}, u32[]{:S(2)}) collective-permute-start(bf16[128,128]{1,0:T(8,128)(2,1)S(1)} %get-tuple-element.35), channel_id=1, source_target_pairs={{0,1},{1,0},{2,3},{3,2},{4,5},{5,4},{6,7},{7,6},{8,9},{9,8},{10,11... | collective-permute-start | bytes 98312 | tf_op jit(solution)/shard_map/ppermute | solution.py:429
  49.5 4.2 %collective-permute-start.12 = (bf16[128,128]{1,0:T(8,128)(2,1)S(1)}, bf16[128,128]{1,0:T(8,128)(2,1)S(1)}, u32[]{:S(2)}, u32[]{:S(2)}) collective-permute-start(bf16[128,128]{1,0:T(8,128)(2,1)S(1)} %get-tuple-element.36), channel_id=1, source_target_pairs={{0,2},{1,3},{2,0},{3,1},{4,6},{5,7},{6,4},{7,5},{8,10},{9,11},{10,... | collective-permute-start | bytes 98312 | tf_op jit(solution)/shard_map/ppermute | solution.py:433
  50.1 3.7 %collective-permute-start.13 = (bf16[128,128]{1,0:T(8,128)(2,1)S(1)}, bf16[128,128]{1,0:T(8,128)(2,1)S(1)}, u32[]{:S(2)}, u32[]{:S(2)}) collective-permute-start(bf16[128,128]{1,0:T(8,128)(2,1)S(1)} %get-tuple-element.37), channel_id=1, source_target_pairs={{0,3},{1,2},{2,1},{3,0},{4,7},{5,6},{6,5},{7,4},{8,11},{9,10},{10,... | collective-permute-start | bytes 98312 | tf_op jit(solution)/shard_map/ppermute | solution.py:437

commit v11 on v10

--- a/solution.py
+++ b/solution.py
@@ -186,7 +186,7 @@
     )(owner, blocks, green, inject)
 
 
-def maps_kernel(pattern, green, coupling, own, other, face_rows, couple, maps):
+def maps_kernel(pattern, green, coupling, _token, own, other, face_rows, couple, maps):
     energies, orbitals, _ = green.shape
     face = coupling.shape[1]
     couple[...] = coupling[...]
@@ -200,44 +200,74 @@
     other[...] = maps[1 - mine]
 
 
-def face_maps(pattern, green, coupling):
+def face_maps(pattern, green, coupling, token):
     orbitals, face = coupling.shape
     square = shape(face, face, dtype=F32)
     return call(
         maps_kernel,
         "face_maps",
-        [IN_SMEM, IN_VMEM, IN_VMEM],
+        [IN_SMEM, IN_VMEM, IN_VMEM, IN_PLACE],
         [square, square, shape(green.shape[0], face, orbitals)],
         [pltpu.VMEM(coupling.shape, BF16), pltpu.VMEM((green.shape[0], face, face), F32)],
         1.2,
+    )(pattern, green, coupling, token)
+
+
+def fetch(green, held, sem):
+    moves = [pltpu.make_async_copy(green.at[e], held.at[e], sem.at[e]) for e in range(green.shape[0])]
+    for move in moves:
+        move.start()
+    return moves
+
+
+def prop_kernel(pattern_in, green, coupling_in, out, token, pattern, coupling, held, sem, side):
+    token[...] = jnp.zeros_like(token)
+    tiles = pltpu.make_async_copy(pattern_in, pattern, side.at[0])
+    whole = pltpu.make_async_copy(coupling_in, coupling, side.at[1])
+    tiles.start()
+    whole.start()
+    moves = fetch(green, held, sem)
+    tiles.wait()
+    whole.wait()
+    mask_tiles(pattern, coupling)
+    for e, move in enumerate(moves):
+        move.wait()
+        out[e] = dot(held[e], coupling[...]).astype(BF16)
+
+
+def propagator(pattern, green, coupling):
+    energies, orbitals, _ = green.shape
+    return call(
+        prop_kernel,
+        "prop",
+        [IN_HBM] * 3,
+        [shape(energies, orbitals, coupling.shape[1]), shape(8, 128, dtype=F32)],
+        [
+            pltpu.SMEM(pattern.shape, jnp.int32),
+            pltpu.VMEM(coupling.shape, BF16),
+            pltpu.VMEM(green.shape, BF16),
+            pltpu.SemaphoreType.DMA((energies,)),
+            pltpu.SemaphoreType.DMA((2,)),
+        ],
+        5.0,
+        VMEM_WHOLE,
     )(pattern, green, coupling)
 
 
-def products_kernel(pattern, green, coupling, source, image, prop, couple):
-    couple[...] = coupling[...]
-    mask_tiles(pattern, couple)
+def image_kernel(green, source, out):
     for e in range(green.shape[0]):
-        image[e] = dot(green[e], source[e])
-        prop[e] = dot(green[e], couple[...]).astype(BF16)
-
-
-def products(pattern, green, coupling, source):
-    energies, orbitals, _ = green.shape
-    return call(
-        products_kernel,
-        "image_and_prop",
-        [IN_SMEM] + [IN_VMEM] * 3,
-        [shape(*source.shape, dtype=F32), shape(energies, orbitals, coupling.shape[1])],
-        [pltpu.VMEM(coupling.shape, BF16)],
-        2.4,
-    )(pattern, green, coupling, source)
+        out[e] = dot(green[e], source[e])
+
+
+def images(green, source):
+    return call(image_kernel, "image", [IN_VMEM] * 2, shape(*source.shape, dtype=F32), [], 1.2)(green, source)
 
 
 def times(a, b):
     return dot(a[0], b[0]) + (dot(a[0], b[1]) + dot(a[1], b[0]))
 
 
-def chain_kernel(own, near, across, far, total_out, parts, maps):
+def chain_kernel(own, near, across, far, _image, total_out, parts, maps):
     collect((own, near, across, far), maps)
     split = [two_parts(maps[j]) for j in range(GROUP)]
     lower, upper = two_parts(times(split[1], split[0])), two_parts(times(split[3], split[2]))
@@ -247,16 +277,16 @@
         parts[1, j] = low
 
 
-def chain(maps, dtype):
+def chain(maps, dtype, tie):
     face = maps[0].shape[0]
     return call(
         chain_kernel,
         "chain_maps",
-        [IN_VMEM] * GROUP,
+        [IN_VMEM] * GROUP + [IN_PLACE],
         [shape(face, face, dtype=dtype), shape(2, GROUP, face, face)],
         [pltpu.VMEM((GROUP, face, face), F32)],
         0.9,
-    )(*maps)
+    )(*maps, tie)
 
 
 def source_kernel(received, inject, face_rows, _map, source, own, near, across, far, _same_map, quarters, total, heads, targets, sem):
@@ -292,7 +322,8 @@
         quarters[e * split] = pack(tall)
         second = jnp.where(left_lanes(tall[:half]), swap_lanes(tall[:half]), tall[half:])
         quarters[e * split + 1] = second
-    deal(quarters, (own, near, across, far))
+    for out, at in zip((own, near, across, far), partners()):
+        out[...] = quarters[at].astype(BF16)
 
 
 def placed_source(received, inject, face_rows, passed):
@@ -316,11 +347,6 @@
     )(received, inject, face_rows, passed)
 
 
-def deal(items, outs):
-    for out, at in zip(outs, partners()):
-        out[...] = items[at].astype(out.dtype)
-
-
 def collect(refs, held):
     for ref, at in zip(refs, partners()):
         held[at] = ref[...]
@@ -330,10 +356,11 @@
     return unpack(shift.astype(F32)) + times((parts[0, j], parts[1, j]), two_parts(state))
 
 
-def total_kernel(own, near, across, far, parts, out, shifts):
+def total_kernel(own, near, across, far, parts, out, local, shifts):
     collect((own, near, across, far), shifts)
     state = unpack(shifts[0].astype(F32))
     for j in range(1, GROUP):
+        local[j - 1] = state
         state = step(parts, j, shifts[j], state)
     out[...] = pack(state).astype(BF16)
 
@@ -344,65 +371,71 @@
         total_kernel,
         "plane_total",
         [IN_VMEM] * (GROUP + 1),
-        shape(half, columns),
+        [shape(half, columns), shape(GROUP - 1, 2 * half, columns, dtype=F32)],
         [pltpu.VMEM((GROUP, half, columns), BF16)],
         3.0,
     )(*shifts, parts)
 
 
-def entering_kernel(first, second, third, got, other, parts, _image, *refs):
-    arrived, out = refs[:GROUP], refs[GROUP : 2 * GROUP]
-    shifts, held = refs[2 * GROUP :]
-    collect(arrived, shifts)
+def upto_kernel(parts, _total, out):
+    maps = (parts[0, 0], parts[1, 0])
+    for j in range(1, GROUP - 1):
+        maps = two_parts(times((parts[0, j], parts[1, j]), maps))
+        out[0, j - 1], out[1, j - 1] = maps
+
+
+def maps_upto(parts, tie):
+    _, _, face, _ = parts.shape
+    return call(
+        upto_kernel, "maps_upto", [IN_VMEM, IN_PLACE], shape(2, GROUP - 2, face, face), [], 3.0
+    )(parts, tie)
+
+
+def sweep_plane(state, parts, upto, local, out):
+    two = two_parts(state)
+    held = [pack(state)]
+    for j in range(1, GROUP):
+        maps = (parts[0, 0], parts[1, 0]) if j == 1 else (upto[0, j - 2], upto[1, j - 2])
+        held.append(pack(local[j - 1] + times(maps, two)))
+    own, near, across, work = out
+    for j, item in enumerate(held):
+        work[j] = item
+    here, at_near, at_across, at_far = partners()
+    own[...] = work[here].astype(BF16)
+    near[...] = work[at_near].astype(BF16)
+    across[0] = work[at_across].astype(BF16)
+    across[1] = work[at_far].astype(BF16)
+
+
+def entering_kernel(first, second, third, got, other, parts, upto, local, *out):
     first_core = place() % CORES == 0
     state = unpack(third[...].astype(F32))
     for below, (one, two) in ((second, (other, got)), (first, (got, other))):
         factor = jnp.where(first_core, one[...], two[...])
         high, low = two_parts(state)
         state = unpack(below[...].astype(F32)) + dot(factor, high) + dot(factor, low)
-    sweep_plane(state, parts, shifts, held, out)
-
-
-def sweep_plane(state, parts, shifts, held, out):
-    held[0] = pack(state)
-    for j in range(1, GROUP):
-        state = step(parts, j - 1, shifts[j - 1], state)
-        held[j] = pack(state)
-    deal(held, out)
-
-
-def entering(below, maps, parts, shifts, tie):
-    half, columns = below[0].shape
-    return call(
-        entering_kernel,
+    sweep_plane(state, parts, upto, local, out)
+
+
+def entering_from_kernel(base, parts, upto, local, *out):
+    sweep_plane(unpack(base[...]), parts, upto, local, out)
+
+
+def entering(body, args):
+    half, columns = args[0].shape
+    return call(
+        body,
         "entering",
-        [IN_VMEM] * 6 + [IN_PLACE] + [IN_VMEM] * GROUP,
-        [shape(half, columns)] * GROUP,
-        [pltpu.VMEM((GROUP, half, columns), BF16), pltpu.VMEM((GROUP, half, columns), F32)],
+        [IN_VMEM] * len(args),
+        [shape(half, columns), shape(half, columns), shape(CORES, half, columns)],
+        [pltpu.VMEM((GROUP, half, columns), F32)],
         1.4,
-    )(*below, *maps, parts, tie, *shifts)
-
-
-def entering_from_kernel(base, parts, *refs):
-    shifts, held = refs[2 * GROUP :]
-    collect(refs[:GROUP], shifts)
-    sweep_plane(unpack(base[...]), parts, shifts, held, refs[GROUP : 2 * GROUP])
-
-
-def entering_from(base, parts, shifts):
-    half, columns = base.shape
-    return call(
-        entering_from_kernel,
-        "entering",
-        [IN_VMEM] * (2 + GROUP),
-        [shape(half, columns)] * GROUP,
-        [pltpu.VMEM((GROUP, half, columns), BF16), pltpu.VMEM((GROUP, half, columns), F32)],
-        1.4,
-    )(base, parts, *shifts)
+    )(*args)
 
 
 def waves_kernel(own, near, across, far, prop, image, out, arrived):
-    collect((own, near, across, far), arrived)
+    for at, item in zip(partners(), (own[...], near[...], across[0], far[1])):
+        arrived[at] = item
     split = GROUP // prop.shape[0]
     for e in range(prop.shape[0]):
         near, far = arrived[e * split].astype(F32), arrived[e * split + 1].astype(F32)
@@ -440,6 +473,11 @@
 def exchange(own, near, across, far, sections):
     across, far = to_across(across, sections), to_far(far, sections)
     return [own, to_near(near, sections), across, far]
+
+
+def exchange_by_chip(own, near, across, sections):
+    across = to_across(across, sections)
+    return [own, to_near(near, sections), across, to_near(across, sections)]
 
 
 def up_shift(sections, k):
@@ -488,25 +526,27 @@
     outgoing = outgoing_pairs(owner[:, 0], pair_blocks.T, green, inject, sections)
     received = lax.all_to_all(outgoing, "sec", split_axis=0, concat_axis=0, tiled=True)
 
-    own_map, other_map, face_rows = face_maps(tiles, green, coupling)
+    prop, token = propagator(tiles, green, coupling)
+    own_map, other_map, face_rows = face_maps(tiles, green, coupling, token)
     across = to_across(other_map, sections)
     near = to_near(own_map, sections)
 
     source, *quarters, across = placed_source(received, inject, face_rows, across)
     shifts = exchange(*quarters, sections)
     far = to_near(across, sections)
+    image = images(green, source)
     four = sections // GROUP == 4
-    total_map, parts = chain([own_map, near, across, far], BF16 if four else F32)
-    image, prop = products(tiles, green, coupling, source)
+    total_map, parts = chain([own_map, near, across, far], BF16 if four else F32, image)
+    maps = maps_up(total_map, sections) if four else []
+    total, local = plane_total(shifts, parts)
+    upto = maps_upto(parts, total)
     if four:
-        maps = maps_up(total_map, sections)
-        total = plane_total(shifts, parts)
         below = [upward(total, k, sections) for k in range(1, 4)]
-        entered = entering(below, maps, parts, shifts, image)
+        entered = entering(entering_kernel, (*below, *maps, parts, upto, local))
     else:
-        total = plane_total(shifts, parts)
-        entered = entering_from(scan_below(total_map, total, sections), parts, shifts)
-    arrived = exchange(*entered, sections)
+        base = scan_below(total_map, total, sections)
+        entered = entering(entering_from_kernel, (base, parts, upto, local))
+    arrived = exchange_by_chip(*entered, sections)
     return final_waves(arrived, prop, image)[None]
 
 

time: 55.5 us -> 58.4 us (1.052)
  Pallas kernels: 14.6 us -> 18.8 us
  waiting for transfers between devices: 15.2 us -> 13.3 us
  local copies, waits for them, and re-layouts: 2.2 us -> 2.89 us
    pallas_call x5 -> x7, Pallas kernels: 7.36 us -> 11.6 us  [the longest x1 5.75 us: propagator(): call(prop_kernel, 'prop', [IN_HBM] * 3, [shape(energies, orbitals, coupli...]
    ppermute x3, waiting for transfers between devices: 12.8 us -> 11.3 us  [to_across(): lax.ppermute(item, 'sec', [(s, s // GROUP * GROUP + (s % GROUP + CORES) %...]
    ppermute x2 -> x1, waiting for transfers between devices: 1.43 us -> 0.3 us  [to_far(): lax.ppermute(item, 'sec', [(s, s // GROUP * GROUP + (s % GROUP + CORES) %...]
    all_to_all x1, waiting for transfers between devices: 0.92 us -> 0.01 us  [per_device(): lax.all_to_all(outgoing, 'sec', split_axis=0, concat_axis=0, tiled=True)]
    ppermute x5 -> x6, waiting for transfers between devices: 0.01 us -> 0.87 us  [to_near(): return lax.ppermute(item, 'sec', [(s, s ^ 1) for s in range(sections)])]
    ppermute x3, waiting for transfers between devices: 0.01 us -> 0.78 us  [upward(): return lax.ppermute(item, 'sec', up_shift(sections, k))]
    unnamed x10 -> x14, local copies, waits for them, and re-layouts: 2.2 us -> 2.89 us
    ppermute x5 -> x6, starting transfers between devices: 1.19 us -> 1.15 us  [to_near(): return lax.ppermute(item, 'sec', [(s, s ^ 1) for s in range(sections)])]
  transfers between devices with their start and end apart: 15 -> 15, of which waited for: 6 -> 5; matrix products, arithmetic and copies ran while one was open for 0% -> 0% of each run, Pallas kernels for 13% -> 21%
where the time goes in v11:
time: 58.4 us; the launch traced here: 57.9 us
  starting transfers between devices  22.7 us (39%)
  Pallas kernels  18.8 us (32%)
  waiting for transfers between devices  13.3 us (23%)
  local copies, waits for them, and re-layouts  2.89 us (5%)
    ppermute x3, waiting for transfers between devices, to_across(): lax.ppermute(item, 'sec', [(s, s // GROUP * GROUP + (s % GROUP + CORES) %...  11.3 us
    ppermute x3, starting transfers between devices, upward(): return lax.ppermute(item, 'sec', up_shift(sections, k))  8.92 us
    all_to_all x1, starting transfers between devices, per_device(): lax.all_to_all(outgoing, 'sec', split_axis=0, concat_axis=0, tiled=True)  7.24 us
    pallas_call x1, Pallas kernels, propagator(): call(prop_kernel, 'prop', [IN_HBM] * 3, [shape(energies, orbitals, coupli...  5.75 us
    pallas_call x1, Pallas kernels, outgoing_pairs(): call(pairs_kernel, 'pairs', [IN_HBM] * 4, shape(sections, CAP * energies...  4.43 us
    ppermute x3, starting transfers between devices, to_across(): lax.ppermute(item, 'sec', [(s, s // GROUP * GROUP + (s % GROUP + CORES) %...  4.12 us
    unnamed x14, local copies, waits for them, and re-layouts  2.89 us
    pallas_call x1, Pallas kernels, placed_source(): call(source_kernel, 'source_and_face', [IN_VMEM, IN_VMEM, IN_VMEM, IN_PLA...  1.41 us
  transfers between devices with their start and end apart: 15, of which 5 were waited for; matrix products, arithmetic and copies ran while one was open for 0% of the time, Pallas kernels for 21%

profile of v11, /device:TPU:0, one launch (start us, length us, event | category | flops | bytes accessed | tf_op | source)
XLA Modules:
  0.0 57.9 jit_solution(6305858908373733796)
XLA Ops:
  0.0 4.4 %pairs.1 = bf16[16,144,128]{2,1,0:T(8,128)(2,1)} custom-call(s32[16]{0:T(128)} %bitcast.20, s32[2,16]{1,0:T(2,128)} %bitcast.19, bf16[2,1024,1024]{2,1,0:T(8,128)(2,1)} %bitcast.9, bf16[2,1024,128]{2,1,0:T(8,128)(2,1)} %bitcast.15), custom_call_target="tpu_custom_call" | custom-call | flops 4600000000 | tf_op jit(solution)/shard_map/pairs/pallas_call | solution.py:168
  4.4 7.2 %all-to-all-start = ((bf16[16,144,128]{2,1,0:T(8,128)(2,1)}), bf16[16,144,128]{2,1,0:T(8,128)(2,1)S(1)}, u32[]{:S(2)}, u32[]{:S(2)}) async-start(bf16[16,144,128]{2,1,0:T(8,128)(2,1)} %pairs.1), calls=%async_computation | async-start | bytes 1179648 | tf_op jit(solution)/shard_map/all_to_all | solution.py:527
  11.7 0.0 copy-start.2
  11.7 0.0 copy-start.4
  11.7 5.7 %prop.1 = (bf16[2,1024,256]{2,1,0:T(8,128)(2,1)}, f32[8,128]{1,0:T(8,128)}) custom-call(s32[2,8]{1,0:T(2,128)} %bitcast.17, bf16[2,1024,1024]{2,1,0:T(8,128)(2,1)} %bitcast.10, bf16[1024,256]{1,0:T(8,128)(2,1)} %bitcast.13), custom_call_target="tpu_custom_call" | custom-call | flops 5750000128 | tf_op jit(solution)/shard_map/prop/pallas_call | solution.py:240
  17.5 0.0 copy-done.2
  17.5 0.0 copy-start
  17.5 2.2 %copy-done = bf16[1,2,1024,1024]{3,2,1,0:T(8,128)(2,1)S(1)} copy-done((bf16[1,2,1024,1024]{3,2,1,0:T(8,128)(2,1)S(1)}, bf16[1,2,1024,1024]{3,2,1,0:T(8,128)(2,1)}, u32[]{:S(2)}) %copy-start) | copy-done | bytes 4194328
  19.7 0.7 %copy-done.6 = f32[8,128]{1,0:T(8,128)S(1)} copy-done((f32[8,128]{1,0:T(8,128)S(1)}, f32[8,128]{1,0:T(8,128)}, u32[]{:S(2)}) %copy-start.6) | copy-done | bytes 4120
  20.4 1.1 %face_maps.1 = (f32[256,256]{1,0:T(8,128)S(1)}, f32[256,256]{1,0:T(8,128)S(1)}, bf16[2,256,1024]{2,1,0:T(8,128)(2,1)S(1)}) custom-call(s32[2,8]{1,0:T(2,128)S(1)} %bitcast.18, bf16[2,1024,1024]{2,1,0:T(8,128)(2,1)S(1)} %bitcast.11, bf16[1024,256]{1,0:T(8,128)(2,1)S(1)} %bitcast.14, f32[8,128]{1,0:T(8,128)S(1)} %copy-done.6), custom_call_target="tpu_custom_call" | custom-call | flops 1380000000 | tf_op jit(solution)/shard_map/face_maps/pallas_call | solution.py:206
  21.5 2.0 %collective-permute-start = (f32[256,256]{1,0:T(8,128)S(1)}, f32[256,256]{1,0:T(8,128)S(1)}, u32[]{:S(2)}, u32[]{:S(2)}) collective-permute-start(f32[256,256]{1,0:T(8,128)S(1)} %get-tuple-element.25), channel_id=1, source_target_pairs={{0,2},{1,3},{2,0},{3,1},{4,6},{5,7},{6,4},{7,5},{8,10},{9,11},{10,... | collective-permute-start | bytes 786440 | tf_op jit(solution)/shard_map/ppermute | solution.py:466
  23.5 0.0 collective-permute-start.4
  23.5 8.3 %collective-permute-done._map = f32[256,256]{1,0:T(8,128)S(1)} collective-permute-done((f32[256,256]{1,0:T(8,128)S(1)}, f32[256,256]{1,0:T(8,128)S(1)}, u32[]{:S(2)}, u32[]{:S(2)}) %collective-permute-start) | collective-permute-done | bytes 262176 | tf_op jit(solution)/shard_map/ppermute | solution.py:466
  31.8 0.0 all-to-all-done.received
  31.8 0.0 copy-done.3
  31.8 1.4 %source_and_face.1 = (bf16[2,1024,128]{2,1,0:T(8,128)(2,1)S(1)}, bf16[128,128]{1,0:T(8,128)(2,1)S(1)}, bf16[128,128]{1,0:T(8,128)(2,1)S(1)}, bf16[128,128]{1,0:T...) custom-call(bf16[16,144,128]{2,1,0:T(8,128)(2,1)S(1)} %all-to-all-done.rec, ...), custom_call_target="tpu_custom_call", output_to_operand_aliasing={{5}: (3, {})} | custom-call | flops 1610000000 | tf_op jit(solution)/shard_map/source_and_face/pallas_call | solution.py:333
  33.2 0.1 collective-permute-start.5
  33.3 0.5 collective-permute-start.1
  33.8 0.9 %collective-permute-start.2 = (bf16[128,128]{1,0:T(8,128)(2,1)S(1)}, bf16[128,128]{1,0:T(8,128)(2,1)S(1)}, u32[]{:S(2)}, u32[]{:S(2)}) collective-permute-start(bf16[128,128]{1,0:T(8,128)(2,1)S(1)} %get-tuple-element.28), channel_id=1, source_target_pairs={{0,2},{1,3},{2,0},{3,1},{4,6},{5,7},{6,4},{7,5},{8,10},{9,11},{10,... | collective-permute-start | bytes 98312 | tf_op jit(solution)/shard_map/ppermute | solution.py:466
  34.6 0.6 collective-permute-start.3
  35.2 1.2 %image.1._image = f32[2,1024,128]{2,1,0:T(8,128)S(1)} custom-call(bf16[2,1024,1024]{2,1,0:T(8,128)(2,1)S(1)} %bitcast.12, bf16[2,1024,128]{2,1,0:T(8,128)(2,1)S(1)} %get-tuple-element.32.source), custom_call_target="tpu_custom_call" | custom-call | flops 1380000000 | tf_op jit(solution)/shard_map/image/pallas_call | solution.py:263
  36.4 0.0 collective-permute-done.4.near
  36.4 0.0 collective-permute-done.5.far
  36.5 0.8 %chain_maps.1 = (bf16[256,256]{1,0:T(8,128)(2,1)S(1)}, bf16[2,4,256,256]{3,2,1,0:T(8,128)(2,1)S(1)}) custom-call(f32[256,256]{1,0:T(8,128)S(1)} %get-tuple-element.30.own, f32[256,256]{1,0:T(8,128)S(1)} %collective-permute-done.4.near, f32[256,256]{1,0:T(8,128)S(1)} %get-tuple-element.31.across, f32[256,256]{1,0:T(8,128)S(1)} %collective-permute-done.5.far, ...), custom_call_target="tpu_custom_call" | custom-call | flops 1035000000 | tf_op jit(solution)/shard_map/chain_maps/pallas_call | solution.py:282
  37.3 0.7 %collective-permute-start.9 = (bf16[256,256]{1,0:T(8,128)(2,1)S(1)}, bf16[256,256]{1,0:T(8,128)(2,1)S(1)}, u32[]{:S(2)}, u32[]{:S(2)}) collective-permute-start(bf16[256,256]{1,0:T(8,128)(2,1)S(1)} %get-tuple-element.35), channel_id=1, source_target_pairs={{4,8},{8,12},{5,13},{6,10},{10,14},{7,15},{20,24},{24,28},{21,29},... | collective-permute-start | bytes 393224 | tf_op jit(solution)/shard_map/ppermute | solution.py:499
  38.0 0.0 collective-permute-done.1.near
  38.0 0.0 collective-permute-done.2.across
  38.0 0.3 collective-permute-done.3.far
  38.3 0.9 %plane_total.1 = (bf16[128,128]{1,0:T(8,128)(2,1)S(1)}, f32[3,256,128]{2,1,0:T(8,128)S(1)}) custom-call(bf16[128,128]{1,0:T(8,128)(2,1)S(1)} %get-tuple-element.26.own, bf16[128,128]{1,0:T(8,128)(2,1)S(1)} %collective-permute-done.1.near, bf16[128,128]{1,0:T(8,128)(2,1)S(1)} %collective-permute-done.2.across, ...), custom_call_target="tpu_custom_call" | custom-call | flops 3449999872 | tf_op jit(solution)/shard_map/plane_total/pallas_call | solution.py:370
  39.2 5.2 %collective-permute-start.8 = (bf16[128,128]{1,0:T(8,128)(2,1)S(1)}, bf16[128,128]{1,0:T(8,128)(2,1)S(1)}, u32[]{:S(2)}, u32[]{:S(2)}) collective-permute-start(bf16[128,128]{1,0:T(8,128)(2,1)S(1)} %get-tuple-element.34._total), channel_id=1, source_target_pairs={{0,12},{1,13},{2,14},{3,15},{16,28},{17,29},{18,30},{19,31}} | collective-permute-start | bytes 98312 | tf_op jit(solution)/shard_map/ppermute | solution.py:504
  44.4 1.6 %collective-permute-start.7 = (bf16[128,128]{1,0:T(8,128)(2,1)S(1)}, bf16[128,128]{1,0:T(8,128)(2,1)S(1)}, u32[]{:S(2)}, u32[]{:S(2)}) collective-permute-start(bf16[128,128]{1,0:T(8,128)(2,1)S(1)} %get-tuple-element.34._total), channel_id=1, source_target_pairs={{0,8},{1,9},{2,10},{3,11},{4,12},{5,13},{6,14},{7,15},{16,24},{17,... | collective-permute-start | bytes 98312 | tf_op jit(solution)/shard_map/ppermute | solution.py:504
  46.0 2.1 %collective-permute-start.6 = (bf16[128,128]{1,0:T(8,128)(2,1)S(1)}, bf16[128,128]{1,0:T(8,128)(2,1)S(1)}, u32[]{:S(2)}, u32[]{:S(2)}) collective-permute-start(bf16[128,128]{1,0:T(8,128)(2,1)S(1)} %get-tuple-element.34._total), channel_id=1, source_target_pairs={{0,4},{1,5},{2,6},{3,7},{4,8},{5,9},{6,10},{7,11},{8,12},{9,13},{1... | collective-permute-start | bytes 98312 | tf_op jit(solution)/shard_map/ppermute | solution.py:504
  48.2 0.0 collective-permute-done.9.got
  48.2 0.1 collective-permute-start.10
  48.3 0.7 %maps_upto.1.upto = bf16[2,2,256,256]{3,2,1,0:T(8,128)(2,1)S(1)} custom-call(bf16[2,4,256,256]{3,2,1,0:T(8,128)(2,1)S(1)} %get-tuple-element.33.parts, bf16[128,128]{1,0:T(8,128)(2,1)S(1)} %get-tuple-element.34._total), custom_call_target="tpu_custom_call" | custom-call | flops 3449999872 | tf_op jit(solution)/shard_map/maps_upto/pallas_call | solution.py:389
  49.0 0.0 copy-start.5
  49.0 0.0 collective-permute-done.8.third
  49.0 0.0 collective-permute-done.7.second
  49.0 0.8 %collective-permute-done.6.first = bf16[128,128]{1,0:T(8,128)(2,1)S(1)} collective-permute-done((bf16[128,128]{1,0:T(8,128)(2,1)S(1)}, bf16[128,128]{1,0:T(8,128)(2,1)S(1)}, u32[]{:S(2)}, u32[]{:S(2)}) %collective-permute-start.6) | collective-permute-done | bytes 32800 | tf_op jit(solution)/shard_map/ppermute | solution.py:504
  49.8 0.0 collective-permute-done.10.other
  49.8 1.1 %entering.1 = (bf16[128,128]{1,0:T(8,128)(2,1)S(1)}, bf16[128,128]{1,0:T(8,128)(2,1)S(1)}, bf16[2,128,128]{2,1,0:T(8,128)(2,1)S(1)}) custom-call(bf16[128,128]{1,0:T(8,128)(2,1)S(1)} %collective-permute-done.6.first, bf16[128,128]{1,0:T(8,128)(2,1)S(1)} %collective-permute-done.7.second, bf16[128,128]{1,0:T(8,128)(2,1)S(1)} %collective-permute-done.8.third, ...), custom_call_target="tpu_custom_call" | custom-call | flops 1610000000 | tf_op jit(solution)/shard_map/entering/pallas_call | solution.py:426
  50.9 1.3 %collective-permute-start.12 = (bf16[2,128,128]{2,1,0:T(8,128)(2,1)S(1)}, bf16[2,128,128]{2,1,0:T(8,128)(2,1)S(1)}, u32[]{:S(2)}, u32[]{:S(2)}) collective-permute-start(bf16[2,128,128]{2,1,0:T(8,128)(2,1)S(1)} %get-tuple-element.39), channel_id=1, source_target_pairs={{0,2},{1,3},{2,0},{3,1},{4,6},{5,7},{6,4},{7,5},{8,10},{9,11},{10,... | collective-permute-start | bytes 196616 | tf_op jit(solution)/shard_map/ppermute | solution.py:466
  52.1 3.1 %collective-permute-done.12.across = bf16[2,128,128]{2,1,0:T(8,128)(2,1)S(1)} collective-permute-done((bf16[2,128,128]{2,1,0:T(8,128)(2,1)S(1)}, bf16[2,128,128]{2,1,0:T(8,128)(2,1)S(1)}, u32[]{:S(2)}, u32[]{:S(2)}) %collective-permute-start.12) | collective-permute-done | bytes 65568 | tf_op jit(solution)/shard_map/ppermute | solution.py:466
  55.2 0.0 collective-permute-start.13
  55.2 0.5 collective-permute-start.11
  55.7 0.9 %collective-permute-done.11.near = bf16[128,128]{1,0:T(8,128)(2,1)S(1)} collective-permute-done((bf16[128,128]{1,0:T(8,128)(2,1)S(1)}, bf16[128,128]{1,0:T(8,128)(2,1)S(1)}, u32[]{:S(2)}, u32[]{:S(2)}) %collective-permute-start.11) | collective-permute-done | bytes 32800 | tf_op jit(solution)/shard_map/ppermute | solution.py:462
  56.6 0.0 collective-permute-done.13.far
  56.6 1.3 %waves.1 = bf16[2,1024,128]{2,1,0:T(8,128)(2,1)} custom-call(bf16[128,128]{1,0:T(8,128)(2,1)S(1)} %get-tuple-element.37.own, bf16[128,128]{1,0:T(8,128)(2,1)S(1)} %collective-permute-done.11.near, bf16[2,128,128]{2,1,0:T(8,128)(2,1)S(1)} %collective-permute-done.12.across, bf16[2,128,128]{2,1,0:T(8,128)(2,1)S(1)} %collective-permute-done.13.far, ...), custom_call_target="tpu_custom_call" | custom-call | flops 1495000064 | tf_op jit(solution)/shard_map/waves/pallas_call | solution.py:451
  (6 shorter events, 0.0 us)
Async XLA Ops:
  4.4 27.3 %all-to-all-start = ((bf16[16,144,128]{2,1,0:T(8,128)(2,1)}), bf16[16,144,128]{2,1,0:T(8,128)(2,1)S(1)}, u32[]{:S(2)}, u32[]{:S(2)}) async-start(bf16[16,144,128]{2,1,0:T(8,128)(2,1)} %pairs.1), calls=%async_computation | async-start | bytes 1179648 | tf_op jit(solution)/shard_map/all_to_all | solution.py:527
  11.7 5.8 %copy-start.2 = (bf16[1,1024,256]{2,1,0:T(8,128)(2,1)S(1)}, bf16[1,1024,256]{2,1,0:T(8,128)(2,1)}, u32[]{:S(2)}) copy-start(bf16[1,1024,256]{2,1,0:T(8,128)(2,1)} %param.8) | copy-start | bytes 1572868
  11.7 5.8 %copy-start.4 = (s32[1,8,2]{1,2,0:T(2,128)S(1)}, s32[1,8,2]{1,2,0:T(2,128)}, u32[]{:S(2)}) copy-start(s32[1,8,2]{1,2,0:T(2,128)} %param.9) | copy-start | bytes 196
  17.5 2.2 %copy-start = (bf16[1,2,1024,1024]{3,2,1,0:T(8,128)(2,1)S(1)}, bf16[1,2,1024,1024]{3,2,1,0:T(8,128)(2,1)}, u32[]{:S(2)}) copy-start(bf16[1,2,1024,1024]{3,2,1,0:T(8,128)(2,1)} %param.6) | copy-start | bytes 12582916
  19.7 0.7 %copy-start.6 = (f32[8,128]{1,0:T(8,128)S(1)}, f32[8,128]{1,0:T(8,128)}, u32[]{:S(2)}) copy-start(f32[8,128]{1,0:T(8,128)} %get-tuple-element.23._token) | copy-start | bytes 12292
  20.4 11.4 %copy-start.3 = (bf16[1,2,1024,128]{3,2,1,0:T(8,128)(2,1)S(1)}, bf16[1,2,1024,128]{3,2,1,0:T(8,128)(2,1)}, u32[]{:S(2)}) copy-start(bf16[1,2,1024,128]{3,2,1,0:T(8,128)(2,1)} %param.7) | copy-start | bytes 1572868
  21.5 10.3 %collective-permute-start = (f32[256,256]{1,0:T(8,128)S(1)}, f32[256,256]{1,0:T(8,128)S(1)}, u32[]{:S(2)}, u32[]{:S(2)}) collective-permute-start(f32[256,256]{1,0:T(8,128)S(1)} %get-tuple-element.25), channel_id=1, source_target_pairs={{0,2},{1,3},{2,0},{3,1},{4,6},{5,7},{6,4},{7,5},{8,10},{9,11},{10,... | collective-permute-start | bytes 786440 | tf_op jit(solution)/shard_map/ppermute | solution.py:466
  23.5 13.0 %collective-permute-start.4 = (f32[256,256]{1,0:T(8,128)S(1)}, f32[256,256]{1,0:T(8,128)S(1)}, u32[]{:S(2)}, u32[]{:S(2)}) collective-permute-start(f32[256,256]{1,0:T(8,128)S(1)} %get-tuple-element.30.own), channel_id=1, source_target_pairs={{0,1},{1,0},{2,3},{3,2},{4,5},{5,4},{6,7},{7,6},{8,9},{9,8},{10,11... | collective-permute-start | bytes 786440 | tf_op jit(solution)/shard_map/ppermute | solution.py:462
  31.8 3.4 %copy-start.1 = (bf16[1,2,1024,1024]{3,2,1,0:T(8,128)(2,1)S(1)}, bf16[1,2,1024,1024]{3,2,1,0:T(8,128)(2,1)}, u32[]{:S(2)}) copy-start(bf16[1,2,1024,1024]{3,2,1,0:T(8,128)(2,1)} %param.6) | copy-start | bytes 12582916
  33.2 3.3 %collective-permute-start.5 = (f32[256,256]{1,0:T(8,128)S(1)}, f32[256,256]{1,0:T(8,128)S(1)}, u32[]{:S(2)}, u32[]{:S(2)}) collective-permute-start(f32[256,256]{1,0:T(8,128)S(1)} %get-tuple-element.31.across), channel_id=1, source_target_pairs={{0,1},{1,0},{2,3},{3,2},{4,5},{5,4},{6,7},{7,6},{8,9},{9,8},{10,11... | collective-permute-start | bytes 786440 | tf_op jit(solution)/shard_map/ppermute | solution.py:462
  33.3 4.7 %collective-permute-start.1 = (bf16[128,128]{1,0:T(8,128)(2,1)S(1)}, bf16[128,128]{1,0:T(8,128)(2,1)S(1)}, u32[]{:S(2)}, u32[]{:S(2)}) collective-permute-start(bf16[128,128]{1,0:T(8,128)(2,1)S(1)} %get-tuple-element.27), channel_id=1, source_target_pairs={{0,1},{1,0},{2,3},{3,2},{4,5},{5,4},{6,7},{7,6},{8,9},{9,8},{10,11... | collective-permute-start | bytes 98312 | tf_op jit(solution)/shard_map/ppermute | solution.py:462
  33.8 4.2 %collective-permute-start.2 = (bf16[128,128]{1,0:T(8,128)(2,1)S(1)}, bf16[128,128]{1,0:T(8,128)(2,1)S(1)}, u32[]{:S(2)}, u32[]{:S(2)}) collective-permute-start(bf16[128,128]{1,0:T(8,128)(2,1)S(1)} %get-tuple-element.28), channel_id=1, source_target_pairs={{0,2},{1,3},{2,0},{3,1},{4,6},{5,7},{6,4},{7,5},{8,10},{9,11},{10,... | collective-permute-start | bytes 98312 | tf_op jit(solution)/shard_map/ppermute | solution.py:466
  34.6 3.7 %collective-permute-start.3 = (bf16[128,128]{1,0:T(8,128)(2,1)S(1)}, bf16[128,128]{1,0:T(8,128)(2,1)S(1)}, u32[]{:S(2)}, u32[]{:S(2)}) collective-permute-start(bf16[128,128]{1,0:T(8,128)(2,1)S(1)} %get-tuple-element.29), channel_id=1, source_target_pairs={{0,3},{1,2},{2,1},{3,0},{4,7},{5,6},{6,5},{7,4},{8,11},{9,10},{10,... | collective-permute-start | bytes 98312 | tf_op jit(solution)/shard_map/ppermute | solution.py:470
  37.3 10.9 %collective-permute-start.9 = (bf16[256,256]{1,0:T(8,128)(2,1)S(1)}, bf16[256,256]{1,0:T(8,128)(2,1)S(1)}, u32[]{:S(2)}, u32[]{:S(2)}) collective-permute-start(bf16[256,256]{1,0:T(8,128)(2,1)S(1)} %get-tuple-element.35), channel_id=1, source_target_pairs={{4,8},{8,12},{5,13},{6,10},{10,14},{7,15},{20,24},{24,28},{21,29},... | collective-permute-start | bytes 393224 | tf_op jit(solution)/shard_map/ppermute | solution.py:499
  39.2 9.7 %collective-permute-start.8 = (bf16[128,128]{1,0:T(8,128)(2,1)S(1)}, bf16[128,128]{1,0:T(8,128)(2,1)S(1)}, u32[]{:S(2)}, u32[]{:S(2)}) collective-permute-start(bf16[128,128]{1,0:T(8,128)(2,1)S(1)} %get-tuple-element.34._total), channel_id=1, source_target_pairs={{0,12},{1,13},{2,14},{3,15},{16,28},{17,29},{18,30},{19,31}} | collective-permute-start | bytes 98312 | tf_op jit(solution)/shard_map/ppermute | solution.py:504
  44.4 4.6 %collective-permute-start.7 = (bf16[128,128]{1,0:T(8,128)(2,1)S(1)}, bf16[128,128]{1,0:T(8,128)(2,1)S(1)}, u32[]{:S(2)}, u32[]{:S(2)}) collective-permute-start(bf16[128,128]{1,0:T(8,128)(2,1)S(1)} %get-tuple-element.34._total), channel_id=1, source_target_pairs={{0,8},{1,9},{2,10},{3,11},{4,12},{5,13},{6,14},{7,15},{16,24},{17,... | collective-permute-start | bytes 98312 | tf_op jit(solution)/shard_map/ppermute | solution.py:504
  46.0 3.7 %collective-permute-start.6 = (bf16[128,128]{1,0:T(8,128)(2,1)S(1)}, bf16[128,128]{1,0:T(8,128)(2,1)S(1)}, u32[]{:S(2)}, u32[]{:S(2)}) collective-permute-start(bf16[128,128]{1,0:T(8,128)(2,1)S(1)} %get-tuple-element.34._total), channel_id=1, source_target_pairs={{0,4},{1,5},{2,6},{3,7},{4,8},{5,9},{6,10},{7,11},{8,12},{9,13},{1... | collective-permute-start | bytes 98312 | tf_op jit(solution)/shard_map/ppermute | solution.py:504
  48.2 1.6 %collective-permute-start.10 = (bf16[256,256]{1,0:T(8,128)(2,1)S(1)}, bf16[256,256]{1,0:T(8,128)(2,1)S(1)}, u32[]{:S(2)}, u32[]{:S(2)}) collective-permute-start(bf16[256,256]{1,0:T(8,128)(2,1)S(1)} %collective-permute-done.9.got), channel_id=1, source_target_pairs={{0,1},{1,0},{2,3},{3,2},{4,5},{5,4},{6,7},{7,6},{8,9},{9,8},{10,11... | collective-permute-start | bytes 393224 | tf_op jit(solution)/shard_map/ppermute | solution.py:462
  49.0 7.6 %copy-start.5 = (bf16[2,1024,256]{2,1,0:T(8,128)(2,1)S(1)}, bf16[2,1024,256]{2,1,0:T(8,128)(2,1)}, u32[]{:S(2)}) copy-start(bf16[2,1024,256]{2,1,0:T(8,128)(2,1)} %get-tuple-element.40.prop) | copy-start | bytes 3145732
  50.9 4.3 %collective-permute-start.12 = (bf16[2,128,128]{2,1,0:T(8,128)(2,1)S(1)}, bf16[2,128,128]{2,1,0:T(8,128)(2,1)S(1)}, u32[]{:S(2)}, u32[]{:S(2)}) collective-permute-start(bf16[2,128,128]{2,1,0:T(8,128)(2,1)S(1)} %get-tuple-element.39), channel_id=1, source_target_pairs={{0,2},{1,3},{2,0},{3,1},{4,6},{5,7},{6,4},{7,5},{8,10},{9,11},{10,... | collective-permute-start | bytes 196616 | tf_op jit(solution)/shard_map/ppermute | solution.py:466
  55.2 1.4 %collective-permute-start.13 = (bf16[2,128,128]{2,1,0:T(8,128)(2,1)S(1)}, bf16[2,128,128]{2,1,0:T(8,128)(2,1)S(1)}, u32[]{:S(2)}, u32[]{:S(2)}) collective-permute-start(bf16[2,128,128]{2,1,0:T(8,128)(2,1)S(1)} %collective-permute-done.12.across), channel_id=1, source_target_pairs={{0,1},{1,0},{2,3},{3,2},{4,5},{5,4},{6,7},{7,6},{8,9},{9,8},{10,11... | collective-permute-start | bytes 196616 | tf_op jit(solution)/shard_map/ppermute | solution.py:462
  55.2 1.4 %collective-permute-start.11 = (bf16[128,128]{1,0:T(8,128)(2,1)S(1)}, bf16[128,128]{1,0:T(8,128)(2,1)S(1)}, u32[]{:S(2)}, u32[]{:S(2)}) collective-permute-start(bf16[128,128]{1,0:T(8,128)(2,1)S(1)} %get-tuple-element.38), channel_id=1, source_target_pairs={{0,1},{1,0},{2,3},{3,2},{4,5},{5,4},{6,7},{7,6},{8,9},{9,8},{10,11... | collective-permute-start | bytes 98312 | tf_op jit(solution)/shard_map/ppermute | solution.py:462

commit v12 on v11

--- a/solution.py
+++ b/solution.py
@@ -17,6 +17,7 @@
 F32 = jnp.float32
 BF16 = jnp.bfloat16
 VMEM_SMALL = 16 * 1024 * 1024
+VMEM_MOST = 61900000
 VMEM_WHOLE = 63400000
 PEAK = 1.15e9
 
@@ -186,7 +187,7 @@
     )(owner, blocks, green, inject)
 
 
-def maps_kernel(pattern, green, coupling, _token, own, other, face_rows, couple, maps):
+def maps_kernel(pattern, green, coupling, own, other, face_rows, couple, maps):
     energies, orbitals, _ = green.shape
     face = coupling.shape[1]
     couple[...] = coupling[...]
@@ -200,17 +201,17 @@
     other[...] = maps[1 - mine]
 
 
-def face_maps(pattern, green, coupling, token):
+def face_maps(pattern, green, coupling):
     orbitals, face = coupling.shape
     square = shape(face, face, dtype=F32)
     return call(
         maps_kernel,
         "face_maps",
-        [IN_SMEM, IN_VMEM, IN_VMEM, IN_PLACE],
+        [IN_SMEM, IN_VMEM, IN_VMEM],
         [square, square, shape(green.shape[0], face, orbitals)],
         [pltpu.VMEM(coupling.shape, BF16), pltpu.VMEM((green.shape[0], face, face), F32)],
         1.2,
-    )(pattern, green, coupling, token)
+    )(pattern, green, coupling)
 
 
 def fetch(green, held, sem):
@@ -220,8 +221,7 @@
     return moves
 
 
-def prop_kernel(pattern_in, green, coupling_in, out, token, pattern, coupling, held, sem, side):
-    token[...] = jnp.zeros_like(token)
+def prop_kernel(pattern_in, green, coupling_in, _rows, out, _same_rows, pattern, coupling, held, sem, side):
     tiles = pltpu.make_async_copy(pattern_in, pattern, side.at[0])
     whole = pltpu.make_async_copy(coupling_in, coupling, side.at[1])
     tiles.start()
@@ -235,13 +235,13 @@
         out[e] = dot(held[e], coupling[...]).astype(BF16)
 
 
-def propagator(pattern, green, coupling):
+def propagator(pattern, green, coupling, passed):
     energies, orbitals, _ = green.shape
     return call(
         prop_kernel,
         "prop",
-        [IN_HBM] * 3,
-        [shape(energies, orbitals, coupling.shape[1]), shape(8, 128, dtype=F32)],
+        [IN_HBM] * 3 + [IN_PLACE],
+        [shape(energies, orbitals, coupling.shape[1]), shape(*passed.shape)],
         [
             pltpu.SMEM(pattern.shape, jnp.int32),
             pltpu.VMEM(coupling.shape, BF16),
@@ -250,8 +250,9 @@
             pltpu.SemaphoreType.DMA((2,)),
         ],
         5.0,
-        VMEM_WHOLE,
-    )(pattern, green, coupling)
+        VMEM_MOST,
+        aliases={3: 1},
+    )(pattern, green, coupling, passed)
 
 
 def image_kernel(green, source, out):
@@ -397,14 +398,11 @@
     for j in range(1, GROUP):
         maps = (parts[0, 0], parts[1, 0]) if j == 1 else (upto[0, j - 2], upto[1, j - 2])
         held.append(pack(local[j - 1] + times(maps, two)))
-    own, near, across, work = out
+    work = out[GROUP]
     for j, item in enumerate(held):
         work[j] = item
-    here, at_near, at_across, at_far = partners()
-    own[...] = work[here].astype(BF16)
-    near[...] = work[at_near].astype(BF16)
-    across[0] = work[at_across].astype(BF16)
-    across[1] = work[at_far].astype(BF16)
+    for ref, at in zip(out, partners()):
+        ref[...] = work[at].astype(BF16)
 
 
 def entering_kernel(first, second, third, got, other, parts, upto, local, *out):
@@ -427,15 +425,14 @@
         body,
         "entering",
         [IN_VMEM] * len(args),
-        [shape(half, columns), shape(half, columns), shape(CORES, half, columns)],
+        [shape(half, columns)] * GROUP,
         [pltpu.VMEM((GROUP, half, columns), F32)],
         1.4,
     )(*args)
 
 
 def waves_kernel(own, near, across, far, prop, image, out, arrived):
-    for at, item in zip(partners(), (own[...], near[...], across[0], far[1])):
-        arrived[at] = item
+    collect((own, near, across, far), arrived)
     split = GROUP // prop.shape[0]
     for e in range(prop.shape[0]):
         near, far = arrived[e * split].astype(F32), arrived[e * split + 1].astype(F32)
@@ -473,11 +470,6 @@
 def exchange(own, near, across, far, sections):
     across, far = to_across(across, sections), to_far(far, sections)
     return [own, to_near(near, sections), across, far]
-
-
-def exchange_by_chip(own, near, across, sections):
-    across = to_across(across, sections)
-    return [own, to_near(near, sections), across, to_near(across, sections)]
 
 
 def up_shift(sections, k):
@@ -526,10 +518,10 @@
     outgoing = outgoing_pairs(owner[:, 0], pair_blocks.T, green, inject, sections)
     received = lax.all_to_all(outgoing, "sec", split_axis=0, concat_axis=0, tiled=True)
 
-    prop, token = propagator(tiles, green, coupling)
-    own_map, other_map, face_rows = face_maps(tiles, green, coupling, token)
+    own_map, other_map, face_rows = face_maps(tiles, green, coupling)
     across = to_across(other_map, sections)
     near = to_near(own_map, sections)
+    prop, face_rows = propagator(tiles, green, coupling, face_rows)
 
     source, *quarters, across = placed_source(received, inject, face_rows, across)
     shifts = exchange(*quarters, sections)
@@ -546,7 +538,7 @@
     else:
         base = scan_below(total_map, total, sections)
         entered = entering(entering_from_kernel, (base, parts, upto, local))
-    arrived = exchange_by_chip(*entered, sections)
+    arrived = exchange(*entered, sections)
     return final_waves(arrived, prop, image)[None]
 
 

time: 58.4 us -> 54.8 us (0.938)
  waiting for transfers between devices: 13.3 us -> 8.74 us
  local copies, waits for them, and re-layouts: 2.89 us -> 4.52 us
    ppermute x3, waiting for transfers between devices: 11.3 us -> 6.58 us  [to_across(): lax.ppermute(item, 'sec', [(s, s // GROUP * GROUP + (s % GROUP + CORES) %...]
    unnamed x14 -> x16, local copies, waits for them, and re-layouts: 2.89 us -> 4.52 us
    ppermute x1 -> x2, waiting for transfers between devices: 0.3 us -> 1.5 us  [to_far(): lax.ppermute(item, 'sec', [(s, s // GROUP * GROUP + (s % GROUP + CORES) %...]
    ppermute x6 -> x5, waiting for transfers between devices: 0.87 us -> 0.01 us  [to_near(): return lax.ppermute(item, 'sec', [(s, s ^ 1) for s in range(sections)])]
    ppermute x3, starting transfers between devices: 8.92 us -> 8.26 us  [upward(): return lax.ppermute(item, 'sec', up_shift(sections, k))]
where the time goes in v12:
time: 54.8 us; the launch traced here: 54.3 us
  starting transfers between devices  22.5 us (41%)
  Pallas kernels  18.3 us (33%)
  waiting for transfers between devices  8.74 us (16%)
  local copies, waits for them, and re-layouts  4.52 us (8%)
    ppermute x3, starting transfers between devices, upward(): return lax.ppermute(item, 'sec', up_shift(sections, k))  8.26 us
    all_to_all x1, starting transfers between devices, per_device(): lax.all_to_all(outgoing, 'sec', split_axis=0, concat_axis=0, tiled=True)  7.41 us
    ppermute x3, waiting for transfers between devices, to_across(): lax.ppermute(item, 'sec', [(s, s // GROUP * GROUP + (s % GROUP + CORES) %...  6.58 us
    pallas_call x1, Pallas kernels, propagator(): call(prop_kernel, 'prop', [IN_HBM] * 3 + [IN_PLACE], [shape(energies, orb...  5.34 us
    ppermute x3, starting transfers between devices, to_across(): lax.ppermute(item, 'sec', [(s, s // GROUP * GROUP + (s % GROUP + CORES) %...  4.69 us
    unnamed x16, local copies, waits for them, and re-layouts  4.52 us
    pallas_call x1, Pallas kernels, outgoing_pairs(): call(pairs_kernel, 'pairs', [IN_HBM] * 4, shape(sections, CAP * energies...  4.42 us
    ppermute x2, waiting for transfers between devices, to_far(): lax.ppermute(item, 'sec', [(s, s // GROUP * GROUP + (s % GROUP + CORES) %...  1.5 us
  transfers between devices with their start and end apart: 15, of which 5 were waited for; matrix products, arithmetic and copies ran while one was open for 0% of the time, Pallas kernels for 21%

profile of v12, /device:TPU:0, one launch (start us, length us, event | category | flops | bytes accessed | tf_op | source)
XLA Modules:
  0.0 54.3 jit_solution(18250974728987478460)
XLA Ops:
  0.0 4.4 %pairs.1 = bf16[16,144,128]{2,1,0:T(8,128)(2,1)} custom-call(s32[16]{0:T(128)} %bitcast.20, s32[2,16]{1,0:T(2,128)} %bitcast.19, bf16[2,1024,1024]{2,1,0:T(8,128)(2,1)} %bitcast.9, bf16[2,1024,128]{2,1,0:T(8,128)(2,1)} %bitcast.15), custom_call_target="tpu_custom_call" | custom-call | flops 4600000000 | tf_op jit(solution)/shard_map/pairs/pallas_call | solution.py:169
  4.4 7.4 %all-to-all-start = ((bf16[16,144,128]{2,1,0:T(8,128)(2,1)}), bf16[16,144,128]{2,1,0:T(8,128)(2,1)S(1)}, u32[]{:S(2)}, u32[]{:S(2)}) async-start(bf16[16,144,128]{2,1,0:T(8,128)(2,1)} %pairs.1), calls=%async_computation | async-start | bytes 1179648 | tf_op jit(solution)/shard_map/all_to_all | solution.py:519
  11.8 0.0 copy-done.2
  11.9 0.0 copy-done.4
  11.9 0.0 copy-start
  11.9 2.2 %copy-done = bf16[1,2,1024,1024]{3,2,1,0:T(8,128)(2,1)S(1)} copy-done((bf16[1,2,1024,1024]{3,2,1,0:T(8,128)(2,1)S(1)}, bf16[1,2,1024,1024]{3,2,1,0:T(8,128)(2,1)}, u32[]{:S(2)}) %copy-start) | copy-done | bytes 4194328
  14.1 1.1 %face_maps.1 = (f32[256,256]{1,0:T(8,128)S(1)}, f32[256,256]{1,0:T(8,128)S(1)}, bf16[2,256,1024]{2,1,0:T(8,128)(2,1)S(1)}) custom-call(s32[2,8]{1,0:T(2,128)S(1)} %bitcast.18, bf16[2,1024,1024]{2,1,0:T(8,128)(2,1)S(1)} %bitcast.11, bf16[1024,256]{1,0:T(8,128)(2,1)S(1)} %bitcast.14), custom_call_target="tpu_custom_call" | custom-call | flops 1380000000 | tf_op jit(solution)/shard_map/face_maps/pallas_call | solution.py:207
  15.2 0.0 copy-start.5
  15.2 0.9 %copy-done.5 = bf16[2,256,1024]{2,1,0:T(8,128)(2,1)} copy-done((bf16[2,256,1024]{2,1,0:T(8,128)(2,1)}, bf16[2,256,1024]{2,1,0:T(8,128)(2,1)S(1)}, u32[]{:S(2)}) %copy-start.5) | copy-done | bytes 1048600
  16.1 1.9 %collective-permute-start = (f32[256,256]{1,0:T(8,128)S(1)}, f32[256,256]{1,0:T(8,128)S(1)}, u32[]{:S(2)}, u32[]{:S(2)}) collective-permute-start(f32[256,256]{1,0:T(8,128)S(1)} %get-tuple-element.26), channel_id=1, source_target_pairs={{0,2},{1,3},{2,0},{3,1},{4,6},{5,7},{6,4},{7,5},{8,10},{9,11},{10,... | collective-permute-start | bytes 786440 | tf_op jit(solution)/shard_map/ppermute | solution.py:463
  18.1 0.0 collective-permute-start.4
  18.1 5.3 %prop.1 = (bf16[2,1024,256]{2,1,0:T(8,128)(2,1)}, bf16[2,256,1024]{2,1,0:T(8,128)(2,1)}) custom-call(s32[2,8]{1,0:T(2,128)} %bitcast.17, bf16[2,1024,1024]{2,1,0:T(8,128)(2,1)} %bitcast.10, bf16[1024,256]{1,0:T(8,128)(2,1)} %bitcast.13, bf16[2,256,1024]{2,1,0:T(8,128)(2,1)} %copy-done.5), custom_call_target="tpu_custom_call", output_to_operand_aliasing={{1}: (3, {})} | custom-call | flops 5750000128 | tf_op jit(solution)/shard_map/prop/pallas_call | solution.py:240
  23.4 4.5 %collective-permute-done._map = f32[256,256]{1,0:T(8,128)S(1)} collective-permute-done((f32[256,256]{1,0:T(8,128)S(1)}, f32[256,256]{1,0:T(8,128)S(1)}, u32[]{:S(2)}, u32[]{:S(2)}) %collective-permute-start) | collective-permute-done | bytes 262176 | tf_op jit(solution)/shard_map/ppermute | solution.py:463
  27.9 0.0 all-to-all-done.received
  27.9 0.0 copy-done.3
  27.9 1.4 %copy-done.6 = bf16[2,256,1024]{2,1,0:T(8,128)(2,1)S(1)} copy-done((bf16[2,256,1024]{2,1,0:T(8,128)(2,1)S(1)}, bf16[2,256,1024]{2,1,0:T(8,128)(2,1)}, u32[]{:S(2)}) %copy-start.6) | copy-done | bytes 1048600
  29.3 1.4 %source_and_face.1 = (bf16[2,1024,128]{2,1,0:T(8,128)(2,1)S(1)}, bf16[128,128]{1,0:T(8,128)(2,1)S(1)}, bf16[128,128]{1,0:T(8,128)(2,1)S(1)}, bf16[128,128]{1,0:T...) custom-call(bf16[16,144,128]{2,1,0:T(8,128)(2,1)S(1)} %all-to-all-done.rec, ...), custom_call_target="tpu_custom_call", output_to_operand_aliasing={{5}: (3, {})} | custom-call | flops 1610000000 | tf_op jit(solution)/shard_map/source_and_face/pallas_call | solution.py:334
  30.7 0.1 collective-permute-start.5
  30.7 0.5 collective-permute-start.1
  31.2 1.5 %collective-permute-start.2 = (bf16[128,128]{1,0:T(8,128)(2,1)S(1)}, bf16[128,128]{1,0:T(8,128)(2,1)S(1)}, u32[]{:S(2)}, u32[]{:S(2)}) collective-permute-start(bf16[128,128]{1,0:T(8,128)(2,1)S(1)} %get-tuple-element.29), channel_id=1, source_target_pairs={{0,2},{1,3},{2,0},{3,1},{4,6},{5,7},{6,4},{7,5},{8,10},{9,11},{10,... | collective-permute-start | bytes 98312 | tf_op jit(solution)/shard_map/ppermute | solution.py:463
  32.7 0.0 collective-permute-start.3
  32.7 1.2 %image.1._image = f32[2,1024,128]{2,1,0:T(8,128)S(1)} custom-call(bf16[2,1024,1024]{2,1,0:T(8,128)(2,1)S(1)} %bitcast.12, bf16[2,1024,128]{2,1,0:T(8,128)(2,1)S(1)} %get-tuple-element.33.source), custom_call_target="tpu_custom_call" | custom-call | flops 1380000000 | tf_op jit(solution)/shard_map/image/pallas_call | solution.py:264
  34.0 0.0 collective-permute-done.4.near
  34.0 0.0 collective-permute-done.5.far
  34.0 0.8 %chain_maps.1 = (bf16[256,256]{1,0:T(8,128)(2,1)S(1)}, bf16[2,4,256,256]{3,2,1,0:T(8,128)(2,1)S(1)}) custom-call(f32[256,256]{1,0:T(8,128)S(1)} %get-tuple-element.31.own, f32[256,256]{1,0:T(8,128)S(1)} %collective-permute-done.4.near, f32[256,256]{1,0:T(8,128)S(1)} %get-tuple-element.32.across, f32[256,256]{1,0:T(8,128)S(1)} %collective-permute-done.5.far, ...), custom_call_target="tpu_custom_call" | custom-call | flops 1035000000 | tf_op jit(solution)/shard_map/chain_maps/pallas_call | solution.py:283
  34.9 0.7 %collective-permute-start.9 = (bf16[256,256]{1,0:T(8,128)(2,1)S(1)}, bf16[256,256]{1,0:T(8,128)(2,1)S(1)}, u32[]{:S(2)}, u32[]{:S(2)}) collective-permute-start(bf16[256,256]{1,0:T(8,128)(2,1)S(1)} %get-tuple-element.36), channel_id=1, source_target_pairs={{4,8},{8,12},{5,13},{6,10},{10,14},{7,15},{20,24},{24,28},{21,29},... | collective-permute-start | bytes 393224 | tf_op jit(solution)/shard_map/ppermute | solution.py:491
  35.5 0.0 collective-permute-done.1.near
  35.5 0.0 collective-permute-done.2.across
  35.5 0.9 %collective-permute-done.3.far = bf16[128,128]{1,0:T(8,128)(2,1)S(1)} collective-permute-done((bf16[128,128]{1,0:T(8,128)(2,1)S(1)}, bf16[128,128]{1,0:T(8,128)(2,1)S(1)}, u32[]{:S(2)}, u32[]{:S(2)}) %collective-permute-start.3) | collective-permute-done | bytes 32800 | tf_op jit(solution)/shard_map/ppermute | solution.py:467
  36.4 0.9 %plane_total.1 = (bf16[128,128]{1,0:T(8,128)(2,1)S(1)}, f32[3,256,128]{2,1,0:T(8,128)S(1)}) custom-call(bf16[128,128]{1,0:T(8,128)(2,1)S(1)} %get-tuple-element.27.own, bf16[128,128]{1,0:T(8,128)(2,1)S(1)} %collective-permute-done.1.near, bf16[128,128]{1,0:T(8,128)(2,1)S(1)} %collective-permute-done.2.across, ...), custom_call_target="tpu_custom_call" | custom-call | flops 3449999872 | tf_op jit(solution)/shard_map/plane_total/pallas_call | solution.py:371
  37.3 4.5 %collective-permute-start.8 = (bf16[128,128]{1,0:T(8,128)(2,1)S(1)}, bf16[128,128]{1,0:T(8,128)(2,1)S(1)}, u32[]{:S(2)}, u32[]{:S(2)}) collective-permute-start(bf16[128,128]{1,0:T(8,128)(2,1)S(1)} %get-tuple-element.35._total), channel_id=1, source_target_pairs={{0,12},{1,13},{2,14},{3,15},{16,28},{17,29},{18,30},{19,31}} | collective-permute-start | bytes 98312 | tf_op jit(solution)/shard_map/ppermute | solution.py:496
  41.9 1.8 %collective-permute-start.7 = (bf16[128,128]{1,0:T(8,128)(2,1)S(1)}, bf16[128,128]{1,0:T(8,128)(2,1)S(1)}, u32[]{:S(2)}, u32[]{:S(2)}) collective-permute-start(bf16[128,128]{1,0:T(8,128)(2,1)S(1)} %get-tuple-element.35._total), channel_id=1, source_target_pairs={{0,8},{1,9},{2,10},{3,11},{4,12},{5,13},{6,14},{7,15},{16,24},{17,... | collective-permute-start | bytes 98312 | tf_op jit(solution)/shard_map/ppermute | solution.py:496
  43.7 1.9 %collective-permute-start.6 = (bf16[128,128]{1,0:T(8,128)(2,1)S(1)}, bf16[128,128]{1,0:T(8,128)(2,1)S(1)}, u32[]{:S(2)}, u32[]{:S(2)}) collective-permute-start(bf16[128,128]{1,0:T(8,128)(2,1)S(1)} %get-tuple-element.35._total), channel_id=1, source_target_pairs={{0,4},{1,5},{2,6},{3,7},{4,8},{5,9},{6,10},{7,11},{8,12},{9,13},{1... | collective-permute-start | bytes 98312 | tf_op jit(solution)/shard_map/ppermute | solution.py:496
  45.6 0.0 collective-permute-done.9.got
  45.6 0.2 collective-permute-start.10
  45.9 0.7 %maps_upto.1.upto = bf16[2,2,256,256]{3,2,1,0:T(8,128)(2,1)S(1)} custom-call(bf16[2,4,256,256]{3,2,1,0:T(8,128)(2,1)S(1)} %get-tuple-element.34.parts, bf16[128,128]{1,0:T(8,128)(2,1)S(1)} %get-tuple-element.35._total), custom_call_target="tpu_custom_call" | custom-call | flops 3449999872 | tf_op jit(solution)/shard_map/maps_upto/pallas_call | solution.py:390
  46.6 0.0 collective-permute-done.8.third
  46.6 0.0 collective-permute-done.7.second
  46.6 0.6 %collective-permute-done.6.first = bf16[128,128]{1,0:T(8,128)(2,1)S(1)} collective-permute-done((bf16[128,128]{1,0:T(8,128)(2,1)S(1)}, bf16[128,128]{1,0:T(8,128)(2,1)S(1)}, u32[]{:S(2)}, u32[]{:S(2)}) %collective-permute-start.6) | collective-permute-done | bytes 32800 | tf_op jit(solution)/shard_map/ppermute | solution.py:496
  47.2 0.0 collective-permute-done.10.other
  47.2 1.1 %entering.1 = (bf16[128,128]{1,0:T(8,128)(2,1)S(1)}, bf16[128,128]{1,0:T(8,128)(2,1)S(1)}, bf16[128,128]{1,0:T(8,128)(2,1)S(1)}, bf16[128,128]{1,0:T(8,128)(2,1)S(1)}) custom-call(bf16[128,128]{1,0:T(8,128)(2,1)S(1)} %collective-permute-done.6.first, bf16[128,128]{1,0:T(8,128)(2,1)S(1)} %collective-permute-done.7.second, ...), custom_call_target="tpu_custom_call" | custom-call | flops 1610000000 | tf_op jit(solution)/shard_map/entering/pallas_call | solution.py:424
  48.3 0.1 collective-permute-start.11
  48.4 1.3 %collective-permute-start.12 = (bf16[128,128]{1,0:T(8,128)(2,1)S(1)}, bf16[128,128]{1,0:T(8,128)(2,1)S(1)}, u32[]{:S(2)}, u32[]{:S(2)}) collective-permute-start(bf16[128,128]{1,0:T(8,128)(2,1)S(1)} %get-tuple-element.40), channel_id=1, source_target_pairs={{0,2},{1,3},{2,0},{3,1},{4,6},{5,7},{6,4},{7,5},{8,10},{9,11},{10,... | collective-permute-start | bytes 98312 | tf_op jit(solution)/shard_map/ppermute | solution.py:463
  49.7 0.6 %collective-permute-start.13 = (bf16[128,128]{1,0:T(8,128)(2,1)S(1)}, bf16[128,128]{1,0:T(8,128)(2,1)S(1)}, u32[]{:S(2)}, u32[]{:S(2)}) collective-permute-start(bf16[128,128]{1,0:T(8,128)(2,1)S(1)} %get-tuple-element.41), channel_id=1, source_target_pairs={{0,3},{1,2},{2,1},{3,0},{4,7},{5,6},{6,5},{7,4},{8,11},{9,10},{10,... | collective-permute-start | bytes 98312 | tf_op jit(solution)/shard_map/ppermute | solution.py:467
  50.2 0.0 collective-permute-done.11.near
  50.2 2.1 %collective-permute-done.12.across = bf16[128,128]{1,0:T(8,128)(2,1)S(1)} collective-permute-done((bf16[128,128]{1,0:T(8,128)(2,1)S(1)}, bf16[128,128]{1,0:T(8,128)(2,1)S(1)}, u32[]{:S(2)}, u32[]{:S(2)}) %collective-permute-start.12) | collective-permute-done | bytes 32800 | tf_op jit(solution)/shard_map/ppermute | solution.py:463
  52.4 0.6 %collective-permute-done.13.far = bf16[128,128]{1,0:T(8,128)(2,1)S(1)} collective-permute-done((bf16[128,128]{1,0:T(8,128)(2,1)S(1)}, bf16[128,128]{1,0:T(8,128)(2,1)S(1)}, u32[]{:S(2)}, u32[]{:S(2)}) %collective-permute-start.13) | collective-permute-done | bytes 32800 | tf_op jit(solution)/shard_map/ppermute | solution.py:467
  53.0 1.3 %waves.1 = bf16[2,1024,128]{2,1,0:T(8,128)(2,1)} custom-call(bf16[128,128]{1,0:T(8,128)(2,1)S(1)} %get-tuple-element.38.own, bf16[128,128]{1,0:T(8,128)(2,1)S(1)} %collective-permute-done.11.near, bf16[128,128]{1,0:T(8,128)(2,1)S(1)} %collective-permute-done.12.across, bf16[128,128]{1,0:T(8,128)(2,1)S(1)} %collective-permute-done.13.far, ...), custom_call_target="tpu_custom_call" | custom-call | flops 1495000064 | tf_op jit(solution)/shard_map/waves/pallas_call | solution.py:448
  (8 shorter events, 0.0 us)
Async XLA Ops:
  0.0 11.9 %copy-start.2 = (bf16[1,1024,256]{2,1,0:T(8,128)(2,1)S(1)}, bf16[1,1024,256]{2,1,0:T(8,128)(2,1)}, u32[]{:S(2)}) copy-start(bf16[1,1024,256]{2,1,0:T(8,128)(2,1)} %param.8) | copy-start | bytes 1572868
  0.0 11.9 %copy-start.4 = (s32[1,8,2]{1,2,0:T(2,128)S(1)}, s32[1,8,2]{1,2,0:T(2,128)}, u32[]{:S(2)}) copy-start(s32[1,8,2]{1,2,0:T(2,128)} %param.9) | copy-start | bytes 196
  4.4 23.5 %all-to-all-start = ((bf16[16,144,128]{2,1,0:T(8,128)(2,1)}), bf16[16,144,128]{2,1,0:T(8,128)(2,1)S(1)}, u32[]{:S(2)}, u32[]{:S(2)}) async-start(bf16[16,144,128]{2,1,0:T(8,128)(2,1)} %pairs.1), calls=%async_computation | async-start | bytes 1179648 | tf_op jit(solution)/shard_map/all_to_all | solution.py:519
  11.9 2.2 %copy-start = (bf16[1,2,1024,1024]{3,2,1,0:T(8,128)(2,1)S(1)}, bf16[1,2,1024,1024]{3,2,1,0:T(8,128)(2,1)}, u32[]{:S(2)}) copy-start(bf16[1,2,1024,1024]{3,2,1,0:T(8,128)(2,1)} %param.6) | copy-start | bytes 12582916
  15.2 1.0 %copy-start.5 = (bf16[2,256,1024]{2,1,0:T(8,128)(2,1)}, bf16[2,256,1024]{2,1,0:T(8,128)(2,1)S(1)}, u32[]{:S(2)}) copy-start(bf16[2,256,1024]{2,1,0:T(8,128)(2,1)S(1)} %get-tuple-element.24._rows) | copy-start | bytes 3145732
  16.1 11.7 %collective-permute-start = (f32[256,256]{1,0:T(8,128)S(1)}, f32[256,256]{1,0:T(8,128)S(1)}, u32[]{:S(2)}, u32[]{:S(2)}) collective-permute-start(f32[256,256]{1,0:T(8,128)S(1)} %get-tuple-element.26), channel_id=1, source_target_pairs={{0,2},{1,3},{2,0},{3,1},{4,6},{5,7},{6,4},{7,5},{8,10},{9,11},{10,... | collective-permute-start | bytes 786440 | tf_op jit(solution)/shard_map/ppermute | solution.py:463
  18.1 15.9 %collective-permute-start.4 = (f32[256,256]{1,0:T(8,128)S(1)}, f32[256,256]{1,0:T(8,128)S(1)}, u32[]{:S(2)}, u32[]{:S(2)}) collective-permute-start(f32[256,256]{1,0:T(8,128)S(1)} %get-tuple-element.31.own), channel_id=1, source_target_pairs={{0,1},{1,0},{2,3},{3,2},{4,5},{5,4},{6,7},{7,6},{8,9},{9,8},{10,11... | collective-permute-start | bytes 786440 | tf_op jit(solution)/shard_map/ppermute | solution.py:459
  18.1 9.8 %copy-start.3 = (bf16[1,2,1024,128]{3,2,1,0:T(8,128)(2,1)S(1)}, bf16[1,2,1024,128]{3,2,1,0:T(8,128)(2,1)}, u32[]{:S(2)}) copy-start(bf16[1,2,1024,128]{3,2,1,0:T(8,128)(2,1)} %param.7) | copy-start | bytes 1572868
  27.9 4.9 %copy-start.1 = (bf16[1,2,1024,1024]{3,2,1,0:T(8,128)(2,1)S(1)}, bf16[1,2,1024,1024]{3,2,1,0:T(8,128)(2,1)}, u32[]{:S(2)}) copy-start(bf16[1,2,1024,1024]{3,2,1,0:T(8,128)(2,1)} %param.6) | copy-start | bytes 12582916
  27.9 1.4 %copy-start.6 = (bf16[2,256,1024]{2,1,0:T(8,128)(2,1)S(1)}, bf16[2,256,1024]{2,1,0:T(8,128)(2,1)}, u32[]{:S(2)}) copy-start(bf16[2,256,1024]{2,1,0:T(8,128)(2,1)} %get-tuple-element.25.face_rows) | copy-start | bytes 3145732
  30.7 3.3 %collective-permute-start.5 = (f32[256,256]{1,0:T(8,128)S(1)}, f32[256,256]{1,0:T(8,128)S(1)}, u32[]{:S(2)}, u32[]{:S(2)}) collective-permute-start(f32[256,256]{1,0:T(8,128)S(1)} %get-tuple-element.32.across), channel_id=1, source_target_pairs={{0,1},{1,0},{2,3},{3,2},{4,5},{5,4},{6,7},{7,6},{8,9},{9,8},{10,11... | collective-permute-start | bytes 786440 | tf_op jit(solution)/shard_map/ppermute | solution.py:459
  30.7 4.8 %collective-permute-start.1 = (bf16[128,128]{1,0:T(8,128)(2,1)S(1)}, bf16[128,128]{1,0:T(8,128)(2,1)S(1)}, u32[]{:S(2)}, u32[]{:S(2)}) collective-permute-start(bf16[128,128]{1,0:T(8,128)(2,1)S(1)} %get-tuple-element.28), channel_id=1, source_target_pairs={{0,1},{1,0},{2,3},{3,2},{4,5},{5,4},{6,7},{7,6},{8,9},{9,8},{10,11... | collective-permute-start | bytes 98312 | tf_op jit(solution)/shard_map/ppermute | solution.py:459
  31.2 4.3 %collective-permute-start.2 = (bf16[128,128]{1,0:T(8,128)(2,1)S(1)}, bf16[128,128]{1,0:T(8,128)(2,1)S(1)}, u32[]{:S(2)}, u32[]{:S(2)}) collective-permute-start(bf16[128,128]{1,0:T(8,128)(2,1)S(1)} %get-tuple-element.29), channel_id=1, source_target_pairs={{0,2},{1,3},{2,0},{3,1},{4,6},{5,7},{6,4},{7,5},{8,10},{9,11},{10,... | collective-permute-start | bytes 98312 | tf_op jit(solution)/shard_map/ppermute | solution.py:463
  32.7 3.7 %collective-permute-start.3 = (bf16[128,128]{1,0:T(8,128)(2,1)S(1)}, bf16[128,128]{1,0:T(8,128)(2,1)S(1)}, u32[]{:S(2)}, u32[]{:S(2)}) collective-permute-start(bf16[128,128]{1,0:T(8,128)(2,1)S(1)} %get-tuple-element.30), channel_id=1, source_target_pairs={{0,3},{1,2},{2,1},{3,0},{4,7},{5,6},{6,5},{7,4},{8,11},{9,10},{10,... | collective-permute-start | bytes 98312 | tf_op jit(solution)/shard_map/ppermute | solution.py:467
  34.9 10.8 %collective-permute-start.9 = (bf16[256,256]{1,0:T(8,128)(2,1)S(1)}, bf16[256,256]{1,0:T(8,128)(2,1)S(1)}, u32[]{:S(2)}, u32[]{:S(2)}) collective-permute-start(bf16[256,256]{1,0:T(8,128)(2,1)S(1)} %get-tuple-element.36), channel_id=1, source_target_pairs={{4,8},{8,12},{5,13},{6,10},{10,14},{7,15},{20,24},{24,28},{21,29},... | collective-permute-start | bytes 393224 | tf_op jit(solution)/shard_map/ppermute | solution.py:491
  37.3 9.2 %collective-permute-start.8 = (bf16[128,128]{1,0:T(8,128)(2,1)S(1)}, bf16[128,128]{1,0:T(8,128)(2,1)S(1)}, u32[]{:S(2)}, u32[]{:S(2)}) collective-permute-start(bf16[128,128]{1,0:T(8,128)(2,1)S(1)} %get-tuple-element.35._total), channel_id=1, source_target_pairs={{0,12},{1,13},{2,14},{3,15},{16,28},{17,29},{18,30},{19,31}} | collective-permute-start | bytes 98312 | tf_op jit(solution)/shard_map/ppermute | solution.py:496
  41.9 4.7 %collective-permute-start.7 = (bf16[128,128]{1,0:T(8,128)(2,1)S(1)}, bf16[128,128]{1,0:T(8,128)(2,1)S(1)}, u32[]{:S(2)}, u32[]{:S(2)}) collective-permute-start(bf16[128,128]{1,0:T(8,128)(2,1)S(1)} %get-tuple-element.35._total), channel_id=1, source_target_pairs={{0,8},{1,9},{2,10},{3,11},{4,12},{5,13},{6,14},{7,15},{16,24},{17,... | collective-permute-start | bytes 98312 | tf_op jit(solution)/shard_map/ppermute | solution.py:496
  43.7 3.5 %collective-permute-start.6 = (bf16[128,128]{1,0:T(8,128)(2,1)S(1)}, bf16[128,128]{1,0:T(8,128)(2,1)S(1)}, u32[]{:S(2)}, u32[]{:S(2)}) collective-permute-start(bf16[128,128]{1,0:T(8,128)(2,1)S(1)} %get-tuple-element.35._total), channel_id=1, source_target_pairs={{0,4},{1,5},{2,6},{3,7},{4,8},{5,9},{6,10},{7,11},{8,12},{9,13},{1... | collective-permute-start | bytes 98312 | tf_op jit(solution)/shard_map/ppermute | solution.py:496
  45.6 1.6 %collective-permute-start.10 = (bf16[256,256]{1,0:T(8,128)(2,1)S(1)}, bf16[256,256]{1,0:T(8,128)(2,1)S(1)}, u32[]{:S(2)}, u32[]{:S(2)}) collective-permute-start(bf16[256,256]{1,0:T(8,128)(2,1)S(1)} %collective-permute-done.9.got), channel_id=1, source_target_pairs={{0,1},{1,0},{2,3},{3,2},{4,5},{5,4},{6,7},{7,6},{8,9},{9,8},{10,11... | collective-permute-start | bytes 393224 | tf_op jit(solution)/shard_map/ppermute | solution.py:459
  46.6 6.5 %copy-start.7 = (bf16[2,1024,256]{2,1,0:T(8,128)(2,1)S(1)}, bf16[2,1024,256]{2,1,0:T(8,128)(2,1)}, u32[]{:S(2)}) copy-start(bf16[2,1024,256]{2,1,0:T(8,128)(2,1)} %get-tuple-element.42.prop) | copy-start | bytes 3145732
  48.3 1.9 %collective-permute-start.11 = (bf16[128,128]{1,0:T(8,128)(2,1)S(1)}, bf16[128,128]{1,0:T(8,128)(2,1)S(1)}, u32[]{:S(2)}, u32[]{:S(2)}) collective-permute-start(bf16[128,128]{1,0:T(8,128)(2,1)S(1)} %get-tuple-element.39), channel_id=1, source_target_pairs={{0,1},{1,0},{2,3},{3,2},{4,5},{5,4},{6,7},{7,6},{8,9},{9,8},{10,11... | collective-permute-start | bytes 98312 | tf_op jit(solution)/shard_map/ppermute | solution.py:459
  48.4 4.0 %collective-permute-start.12 = (bf16[128,128]{1,0:T(8,128)(2,1)S(1)}, bf16[128,128]{1,0:T(8,128)(2,1)S(1)}, u32[]{:S(2)}, u32[]{:S(2)}) collective-permute-start(bf16[128,128]{1,0:T(8,128)(2,1)S(1)} %get-tuple-element.40), channel_id=1, source_target_pairs={{0,2},{1,3},{2,0},{3,1},{4,6},{5,7},{6,4},{7,5},{8,10},{9,11},{10,... | collective-permute-start | bytes 98312 | tf_op jit(solution)/shard_map/ppermute | solution.py:463
  49.7 3.3 %collective-permute-start.13 = (bf16[128,128]{1,0:T(8,128)(2,1)S(1)}, bf16[128,128]{1,0:T(8,128)(2,1)S(1)}, u32[]{:S(2)}, u32[]{:S(2)}) collective-permute-start(bf16[128,128]{1,0:T(8,128)(2,1)S(1)} %get-tuple-element.41), channel_id=1, source_target_pairs={{0,3},{1,2},{2,1},{3,0},{4,7},{5,6},{6,5},{7,4},{8,11},{9,10},{10,... | collective-permute-start | bytes 98312 | tf_op jit(solution)/shard_map/ppermute | solution.py:467

commit v13 on v12

--- a/solution.py
+++ b/solution.py
@@ -17,7 +17,6 @@
 F32 = jnp.float32
 BF16 = jnp.bfloat16
 VMEM_SMALL = 16 * 1024 * 1024
-VMEM_MOST = 61900000
 VMEM_WHOLE = 63400000
 PEAK = 1.15e9
 
@@ -214,45 +213,23 @@
     )(pattern, green, coupling)
 
 
-def fetch(green, held, sem):
-    moves = [pltpu.make_async_copy(green.at[e], held.at[e], sem.at[e]) for e in range(green.shape[0])]
-    for move in moves:
-        move.start()
-    return moves
-
-
-def prop_kernel(pattern_in, green, coupling_in, _rows, out, _same_rows, pattern, coupling, held, sem, side):
-    tiles = pltpu.make_async_copy(pattern_in, pattern, side.at[0])
-    whole = pltpu.make_async_copy(coupling_in, coupling, side.at[1])
-    tiles.start()
-    whole.start()
-    moves = fetch(green, held, sem)
-    tiles.wait()
-    whole.wait()
-    mask_tiles(pattern, coupling)
-    for e, move in enumerate(moves):
-        move.wait()
-        out[e] = dot(held[e], coupling[...]).astype(BF16)
-
-
-def propagator(pattern, green, coupling, passed):
+def prop_kernel(pattern, green, coupling, _tie, out, couple):
+    couple[...] = coupling[...]
+    mask_tiles(pattern, couple)
+    for e in range(green.shape[0]):
+        out[e] = dot(green[e], couple[...]).astype(BF16)
+
+
+def propagator(pattern, green, coupling, tie):
     energies, orbitals, _ = green.shape
     return call(
         prop_kernel,
         "prop",
-        [IN_HBM] * 3 + [IN_PLACE],
-        [shape(energies, orbitals, coupling.shape[1]), shape(*passed.shape)],
-        [
-            pltpu.SMEM(pattern.shape, jnp.int32),
-            pltpu.VMEM(coupling.shape, BF16),
-            pltpu.VMEM(green.shape, BF16),
-            pltpu.SemaphoreType.DMA((energies,)),
-            pltpu.SemaphoreType.DMA((2,)),
-        ],
-        5.0,
-        VMEM_MOST,
-        aliases={3: 1},
-    )(pattern, green, coupling, passed)
+        [IN_SMEM, IN_VMEM, IN_VMEM, IN_PLACE],
+        shape(energies, orbitals, coupling.shape[1]),
+        [pltpu.VMEM(coupling.shape, BF16)],
+        1.5,
+    )(pattern, green, coupling, tie)
 
 
 def image_kernel(green, source, out):
@@ -521,7 +498,6 @@
     own_map, other_map, face_rows = face_maps(tiles, green, coupling)
     across = to_across(other_map, sections)
     near = to_near(own_map, sections)
-    prop, face_rows = propagator(tiles, green, coupling, face_rows)
 
     source, *quarters, across = placed_source(received, inject, face_rows, across)
     shifts = exchange(*quarters, sections)
@@ -539,6 +515,7 @@
         base = scan_below(total_map, total, sections)
         entered = entering(entering_from_kernel, (base, parts, upto, local))
     arrived = exchange(*entered, sections)
+    prop = propagator(tiles, green, coupling, entered[0])
     return final_waves(arrived, prop, image)[None]
 
 

time: 54.8 us -> 53.3 us (0.973)
  waiting for transfers between devices: 8.74 us -> 12.7 us
  Pallas kernels: 18.3 us -> 15 us
  local copies, waits for them, and re-layouts: 4.52 us -> 2.2 us
    pallas_call x1, Pallas kernels: 5.34 us -> 1.92 us  [propagator(): call(prop_kernel, 'prop', [IN_SMEM, IN_VMEM, IN_VMEM, IN_PLACE], shape(en...]
    ppermute x3, waiting for transfers between devices: 6.58 us -> 9.47 us  [to_across(): lax.ppermute(item, 'sec', [(s, s // GROUP * GROUP + (s % GROUP + CORES) %...]
    unnamed x16 -> x10, local copies, waits for them, and re-layouts: 4.52 us -> 2.2 us
    all_to_all x1, waiting for transfers between devices: 0.01 us -> 0.94 us  [per_device(): lax.all_to_all(outgoing, 'sec', split_axis=0, concat_axis=0, tiled=True)]
  transfers between devices with their start and end apart: 15 -> 15, of which waited for: 5 -> 6; matrix products, arithmetic and copies ran while one was open for 0% -> 0% of each run, Pallas kernels for 21% -> 15%
where the time goes in v13:
time: 53.3 us; the launch traced here: 52.8 us
  starting transfers between devices  22.7 us (43%)
  Pallas kernels  15 us (28%)
  waiting for transfers between devices  12.7 us (24%)
  local copies, waits for them, and re-layouts  2.2 us (4%)
    ppermute x3, waiting for transfers between devices, to_across(): lax.ppermute(item, 'sec', [(s, s // GROUP * GROUP + (s % GROUP + CORES) %...  9.47 us
    ppermute x3, starting transfers between devices, upward(): return lax.ppermute(item, 'sec', up_shift(sections, k))  8.39 us
    all_to_all x1, starting transfers between devices, per_device(): lax.all_to_all(outgoing, 'sec', split_axis=0, concat_axis=0, tiled=True)  7.43 us
    ppermute x3, starting transfers between devices, to_across(): lax.ppermute(item, 'sec', [(s, s // GROUP * GROUP + (s % GROUP + CORES) %...  4.87 us
    pallas_call x1, Pallas kernels, outgoing_pairs(): call(pairs_kernel, 'pairs', [IN_HBM] * 4, shape(sections, CAP * energies...  4.47 us
    unnamed x10, local copies, waits for them, and re-layouts  2.2 us
    pallas_call x1, Pallas kernels, propagator(): call(prop_kernel, 'prop', [IN_SMEM, IN_VMEM, IN_VMEM, IN_PLACE], shape(en...  1.92 us
    ppermute x2, waiting for transfers between devices, to_far(): lax.ppermute(item, 'sec', [(s, s // GROUP * GROUP + (s % GROUP + CORES) %...  1.49 us
  transfers between devices with their start and end apart: 15, of which 6 were waited for; matrix products, arithmetic and copies ran while one was open for 0% of the time, Pallas kernels for 15%

profile of v13, /device:TPU:0, one launch (start us, length us, event | category | flops | bytes accessed | tf_op | source)
XLA Modules:
  0.0 52.8 jit_solution(4999455109762301609)
XLA Ops:
  0.0 0.0 copy-start.3
  0.0 4.5 %pairs.1 = bf16[16,144,128]{2,1,0:T(8,128)(2,1)} custom-call(s32[16]{0:T(128)} %bitcast.20, s32[2,16]{1,0:T(2,128)} %bitcast.19, bf16[2,1024,1024]{2,1,0:T(8,128)(2,1)} %bitcast.9, bf16[2,1024,128]{2,1,0:T(8,128)(2,1)} %bitcast.13), custom_call_target="tpu_custom_call" | custom-call | flops 4600000000 | tf_op jit(solution)/shard_map/pairs/pallas_call | solution.py:168
  4.5 0.0 copy-start.2
  4.5 7.4 %all-to-all-start = ((bf16[16,144,128]{2,1,0:T(8,128)(2,1)}), bf16[16,144,128]{2,1,0:T(8,128)(2,1)S(1)}, u32[]{:S(2)}, u32[]{:S(2)}) async-start(bf16[16,144,128]{2,1,0:T(8,128)(2,1)} %pairs.1), calls=%async_computation | async-start | bytes 1179648 | tf_op jit(solution)/shard_map/all_to_all | solution.py:496
  11.9 0.0 copy-done.3
  11.9 0.0 copy-done.4
  11.9 0.0 copy-start
  12.0 2.2 %copy-done = bf16[1,2,1024,1024]{3,2,1,0:T(8,128)(2,1)S(1)} copy-done((bf16[1,2,1024,1024]{3,2,1,0:T(8,128)(2,1)S(1)}, bf16[1,2,1024,1024]{3,2,1,0:T(8,128)(2,1)}, u32[]{:S(2)}) %copy-start) | copy-done | bytes 4194328
  14.1 1.1 %face_maps.1 = (f32[256,256]{1,0:T(8,128)S(1)}, f32[256,256]{1,0:T(8,128)S(1)}, bf16[2,256,1024]{2,1,0:T(8,128)(2,1)S(1)}) custom-call(s32[2,8]{1,0:T(2,128)S(1)} %bitcast.17, bf16[2,1024,1024]{2,1,0:T(8,128)(2,1)S(1)} %bitcast.10, bf16[1024,256]{1,0:T(8,128)(2,1)S(1)} %bitcast.15), custom_call_target="tpu_custom_call" | custom-call | flops 1380000000 | tf_op jit(solution)/shard_map/face_maps/pallas_call | solution.py:206
  15.3 2.0 %collective-permute-start = (f32[256,256]{1,0:T(8,128)S(1)}, f32[256,256]{1,0:T(8,128)S(1)}, u32[]{:S(2)}, u32[]{:S(2)}) collective-permute-start(f32[256,256]{1,0:T(8,128)S(1)} %get-tuple-element.23), channel_id=1, source_target_pairs={{0,2},{1,3},{2,0},{3,1},{4,6},{5,7},{6,4},{7,5},{8,10},{9,11},{10,... | collective-permute-start | bytes 786440 | tf_op jit(solution)/shard_map/ppermute | solution.py:440
  17.2 0.0 collective-permute-start.4
  17.2 9.3 %collective-permute-done._map = f32[256,256]{1,0:T(8,128)S(1)} collective-permute-done((f32[256,256]{1,0:T(8,128)S(1)}, f32[256,256]{1,0:T(8,128)S(1)}, u32[]{:S(2)}, u32[]{:S(2)}) %collective-permute-start) | collective-permute-done | bytes 262176 | tf_op jit(solution)/shard_map/ppermute | solution.py:440
  26.5 0.9 %all-to-all-done.received = bf16[16,144,128]{2,1,0:T(8,128)(2,1)S(1)} async-done(((bf16[16,144,128]{2,1,0:T(8,128)(2,1)}), bf16[16,144,128]{2,1,0:T(8,128)(2,1)S(1)}, u32[]{:S(2)}, u32[]{:S(2)}) %all-to-all-start) | async-done | bytes 589856 | tf_op jit(solution)/shard_map/all_to_all | solution.py:496
  27.5 0.0 copy-done.2
  27.5 1.4 %source_and_face.1 = (bf16[2,1024,128]{2,1,0:T(8,128)(2,1)S(1)}, bf16[128,128]{1,0:T(8,128)(2,1)S(1)}, bf16[128,128]{1,0:T(8,128)(2,1)S(1)}, bf16[128,128]{1,0:T...) custom-call(bf16[16,144,128]{2,1,0:T(8,128)(2,1)S(1)} %all-to-all-done.rec, ...), custom_call_target="tpu_custom_call", output_to_operand_aliasing={{5}: (3, {})} | custom-call | flops 1610000000 | tf_op jit(solution)/shard_map/source_and_face/pallas_call | solution.py:311
  28.9 0.1 collective-permute-start.5
  29.0 0.5 collective-permute-start.1
  29.5 1.6 %collective-permute-start.2 = (bf16[128,128]{1,0:T(8,128)(2,1)S(1)}, bf16[128,128]{1,0:T(8,128)(2,1)S(1)}, u32[]{:S(2)}, u32[]{:S(2)}) collective-permute-start(bf16[128,128]{1,0:T(8,128)(2,1)S(1)} %get-tuple-element.26), channel_id=1, source_target_pairs={{0,2},{1,3},{2,0},{3,1},{4,6},{5,7},{6,4},{7,5},{8,10},{9,11},{10,... | collective-permute-start | bytes 98312 | tf_op jit(solution)/shard_map/ppermute | solution.py:440
  31.1 0.0 collective-permute-start.3
  31.1 0.0 copy-done.1
  31.1 1.2 %image.1._image = f32[2,1024,128]{2,1,0:T(8,128)S(1)} custom-call(bf16[2,1024,1024]{2,1,0:T(8,128)(2,1)S(1)} %bitcast.11, bf16[2,1024,128]{2,1,0:T(8,128)(2,1)S(1)} %get-tuple-element.30.source), custom_call_target="tpu_custom_call" | custom-call | flops 1380000000 | tf_op jit(solution)/shard_map/image/pallas_call | solution.py:241
  32.4 0.0 collective-permute-done.4.near
  32.4 0.0 collective-permute-done.5.far
  32.4 0.8 %chain_maps.1 = (bf16[256,256]{1,0:T(8,128)(2,1)S(1)}, bf16[2,4,256,256]{3,2,1,0:T(8,128)(2,1)S(1)}) custom-call(f32[256,256]{1,0:T(8,128)S(1)} %get-tuple-element.28.own, f32[256,256]{1,0:T(8,128)S(1)} %collective-permute-done.4.near, f32[256,256]{1,0:T(8,128)S(1)} %get-tuple-element.29.across, f32[256,256]{1,0:T(8,128)S(1)} %collective-permute-done.5.far, ...), custom_call_target="tpu_custom_call" | custom-call | flops 1035000000 | tf_op jit(solution)/shard_map/chain_maps/pallas_call | solution.py:260
  33.2 0.7 %collective-permute-start.9 = (bf16[256,256]{1,0:T(8,128)(2,1)S(1)}, bf16[256,256]{1,0:T(8,128)(2,1)S(1)}, u32[]{:S(2)}, u32[]{:S(2)}) collective-permute-start(bf16[256,256]{1,0:T(8,128)(2,1)S(1)} %get-tuple-element.33), channel_id=1, source_target_pairs={{4,8},{8,12},{5,13},{6,10},{10,14},{7,15},{20,24},{24,28},{21,29},... | collective-permute-start | bytes 393224 | tf_op jit(solution)/shard_map/ppermute | solution.py:468
  33.9 0.0 collective-permute-done.1.near
  33.9 0.0 collective-permute-done.2.across
  33.9 0.9 %collective-permute-done.3.far = bf16[128,128]{1,0:T(8,128)(2,1)S(1)} collective-permute-done((bf16[128,128]{1,0:T(8,128)(2,1)S(1)}, bf16[128,128]{1,0:T(8,128)(2,1)S(1)}, u32[]{:S(2)}, u32[]{:S(2)}) %collective-permute-start.3) | collective-permute-done | bytes 32800 | tf_op jit(solution)/shard_map/ppermute | solution.py:444
  34.8 0.9 %plane_total.1 = (bf16[128,128]{1,0:T(8,128)(2,1)S(1)}, f32[3,256,128]{2,1,0:T(8,128)S(1)}) custom-call(bf16[128,128]{1,0:T(8,128)(2,1)S(1)} %get-tuple-element.24.own, bf16[128,128]{1,0:T(8,128)(2,1)S(1)} %collective-permute-done.1.near, bf16[128,128]{1,0:T(8,128)(2,1)S(1)} %collective-permute-done.2.across, ...), custom_call_target="tpu_custom_call" | custom-call | flops 3449999872 | tf_op jit(solution)/shard_map/plane_total/pallas_call | solution.py:348
  35.7 4.6 %collective-permute-start.8 = (bf16[128,128]{1,0:T(8,128)(2,1)S(1)}, bf16[128,128]{1,0:T(8,128)(2,1)S(1)}, u32[]{:S(2)}, u32[]{:S(2)}) collective-permute-start(bf16[128,128]{1,0:T(8,128)(2,1)S(1)} %get-tuple-element.32._total), channel_id=1, source_target_pairs={{0,12},{1,13},{2,14},{3,15},{16,28},{17,29},{18,30},{19,31}} | collective-permute-start | bytes 98312 | tf_op jit(solution)/shard_map/ppermute | solution.py:473
  40.4 1.6 %collective-permute-start.7 = (bf16[128,128]{1,0:T(8,128)(2,1)S(1)}, bf16[128,128]{1,0:T(8,128)(2,1)S(1)}, u32[]{:S(2)}, u32[]{:S(2)}) collective-permute-start(bf16[128,128]{1,0:T(8,128)(2,1)S(1)} %get-tuple-element.32._total), channel_id=1, source_target_pairs={{0,8},{1,9},{2,10},{3,11},{4,12},{5,13},{6,14},{7,15},{16,24},{17,... | collective-permute-start | bytes 98312 | tf_op jit(solution)/shard_map/ppermute | solution.py:473
  42.0 2.1 %collective-permute-start.6 = (bf16[128,128]{1,0:T(8,128)(2,1)S(1)}, bf16[128,128]{1,0:T(8,128)(2,1)S(1)}, u32[]{:S(2)}, u32[]{:S(2)}) collective-permute-start(bf16[128,128]{1,0:T(8,128)(2,1)S(1)} %get-tuple-element.32._total), channel_id=1, source_target_pairs={{0,4},{1,5},{2,6},{3,7},{4,8},{5,9},{6,10},{7,11},{8,12},{9,13},{1... | collective-permute-start | bytes 98312 | tf_op jit(solution)/shard_map/ppermute | solution.py:473
  44.1 0.0 collective-permute-done.9.got
  44.1 0.1 collective-permute-start.10
  44.2 0.7 %maps_upto.1.upto = bf16[2,2,256,256]{3,2,1,0:T(8,128)(2,1)S(1)} custom-call(bf16[2,4,256,256]{3,2,1,0:T(8,128)(2,1)S(1)} %get-tuple-element.31.parts, bf16[128,128]{1,0:T(8,128)(2,1)S(1)} %get-tuple-element.32._total), custom_call_target="tpu_custom_call" | custom-call | flops 3449999872 | tf_op jit(solution)/shard_map/maps_upto/pallas_call | solution.py:367
  44.9 0.0 collective-permute-done.8.third
  44.9 0.0 collective-permute-done.7.second
  44.9 0.8 %collective-permute-done.6.first = bf16[128,128]{1,0:T(8,128)(2,1)S(1)} collective-permute-done((bf16[128,128]{1,0:T(8,128)(2,1)S(1)}, bf16[128,128]{1,0:T(8,128)(2,1)S(1)}, u32[]{:S(2)}, u32[]{:S(2)}) %collective-permute-start.6) | collective-permute-done | bytes 32800 | tf_op jit(solution)/shard_map/ppermute | solution.py:473
  45.7 0.0 collective-permute-done.10.other
  45.7 1.1 %entering.1 = (bf16[128,128]{1,0:T(8,128)(2,1)S(1)}, bf16[128,128]{1,0:T(8,128)(2,1)S(1)}, bf16[128,128]{1,0:T(8,128)(2,1)S(1)}, bf16[128,128]{1,0:T(8,128)(2,1)S(1)}) custom-call(bf16[128,128]{1,0:T(8,128)(2,1)S(1)} %collective-permute-done.6.first, bf16[128,128]{1,0:T(8,128)(2,1)S(1)} %collective-permute-done.7.second, ...), custom_call_target="tpu_custom_call" | custom-call | flops 1610000000 | tf_op jit(solution)/shard_map/entering/pallas_call | solution.py:401
  46.8 0.1 collective-permute-start.11
  46.9 1.3 %collective-permute-start.12 = (bf16[128,128]{1,0:T(8,128)(2,1)S(1)}, bf16[128,128]{1,0:T(8,128)(2,1)S(1)}, u32[]{:S(2)}, u32[]{:S(2)}) collective-permute-start(bf16[128,128]{1,0:T(8,128)(2,1)S(1)} %get-tuple-element.37), channel_id=1, source_target_pairs={{0,2},{1,3},{2,0},{3,1},{4,6},{5,7},{6,4},{7,5},{8,10},{9,11},{10,... | collective-permute-start | bytes 98312 | tf_op jit(solution)/shard_map/ppermute | solution.py:440
  48.1 0.6 %collective-permute-start.13 = (bf16[128,128]{1,0:T(8,128)(2,1)S(1)}, bf16[128,128]{1,0:T(8,128)(2,1)S(1)}, u32[]{:S(2)}, u32[]{:S(2)}) collective-permute-start(bf16[128,128]{1,0:T(8,128)(2,1)S(1)} %get-tuple-element.38), channel_id=1, source_target_pairs={{0,3},{1,2},{2,1},{3,0},{4,7},{5,6},{6,5},{7,4},{8,11},{9,10},{10,... | collective-permute-start | bytes 98312 | tf_op jit(solution)/shard_map/ppermute | solution.py:444
  48.7 1.9 %prop.1 = bf16[2,1024,256]{2,1,0:T(8,128)(2,1)S(1)} custom-call(s32[2,8]{1,0:T(2,128)S(1)} %bitcast.18, bf16[2,1024,1024]{2,1,0:T(8,128)(2,1)S(1)} %bitcast.12, bf16[1024,256]{1,0:T(8,128)(2,1)S(1)} %bitcast.16, bf16[128,128]{1,0:T(8,128)(2,1)S(1)} %get-tuple-element.35._tie.own), custom_call_target="tpu_custom_call" | custom-call | flops 1724999936 | tf_op jit(solution)/shard_map/prop/pallas_call | solution.py:225
  50.7 0.0 collective-permute-done.11.near
  50.7 0.2 collective-permute-done.12.across
  50.9 0.6 %collective-permute-done.13.far = bf16[128,128]{1,0:T(8,128)(2,1)S(1)} collective-permute-done((bf16[128,128]{1,0:T(8,128)(2,1)S(1)}, bf16[128,128]{1,0:T(8,128)(2,1)S(1)}, u32[]{:S(2)}, u32[]{:S(2)}) %collective-permute-start.13) | collective-permute-done | bytes 32800 | tf_op jit(solution)/shard_map/ppermute | solution.py:444
  51.5 1.3 %waves.1 = bf16[2,1024,128]{2,1,0:T(8,128)(2,1)} custom-call(bf16[128,128]{1,0:T(8,128)(2,1)S(1)} %get-tuple-element.35._tie.own, bf16[128,128]{1,0:T(8,128)(2,1)S(1)} %collective-permute-done.11.near, bf16[128,128]{1,0:T(8,128)(2,1)S(1)} %collective-permute-done.12.across, bf16[128,128]{1,0:T(8,128)(2,1)S(1)} %collective-permute-done.13.far, ...), custom_call_target="tpu_custom_call" | custom-call | flops 1495000064 | tf_op jit(solution)/shard_map/waves/pallas_call | solution.py:425
  (2 shorter events, 0.0 us)
Async XLA Ops:
  0.0 11.9 %copy-start.3 = (bf16[1,1024,256]{2,1,0:T(8,128)(2,1)S(1)}, bf16[1,1024,256]{2,1,0:T(8,128)(2,1)}, u32[]{:S(2)}) copy-start(bf16[1,1024,256]{2,1,0:T(8,128)(2,1)} %param.8) | copy-start | bytes 1572868
  0.0 11.9 %copy-start.4 = (s32[1,8,2]{1,2,0:T(2,128)S(1)}, s32[1,8,2]{1,2,0:T(2,128)}, u32[]{:S(2)}) copy-start(s32[1,8,2]{1,2,0:T(2,128)} %param.9) | copy-start | bytes 196
  4.5 23.0 %copy-start.2 = (bf16[1,2,1024,128]{3,2,1,0:T(8,128)(2,1)S(1)}, bf16[1,2,1024,128]{3,2,1,0:T(8,128)(2,1)}, u32[]{:S(2)}) copy-start(bf16[1,2,1024,128]{3,2,1,0:T(8,128)(2,1)} %param.7) | copy-start | bytes 1572868
  4.5 23.0 %all-to-all-start = ((bf16[16,144,128]{2,1,0:T(8,128)(2,1)}), bf16[16,144,128]{2,1,0:T(8,128)(2,1)S(1)}, u32[]{:S(2)}, u32[]{:S(2)}) async-start(bf16[16,144,128]{2,1,0:T(8,128)(2,1)} %pairs.1), calls=%async_computation | async-start | bytes 1179648 | tf_op jit(solution)/shard_map/all_to_all | solution.py:496
  11.9 2.2 %copy-start = (bf16[1,2,1024,1024]{3,2,1,0:T(8,128)(2,1)S(1)}, bf16[1,2,1024,1024]{3,2,1,0:T(8,128)(2,1)}, u32[]{:S(2)}) copy-start(bf16[1,2,1024,1024]{3,2,1,0:T(8,128)(2,1)} %param.6) | copy-start | bytes 12582916
  15.3 11.3 %collective-permute-start = (f32[256,256]{1,0:T(8,128)S(1)}, f32[256,256]{1,0:T(8,128)S(1)}, u32[]{:S(2)}, u32[]{:S(2)}) collective-permute-start(f32[256,256]{1,0:T(8,128)S(1)} %get-tuple-element.23), channel_id=1, source_target_pairs={{0,2},{1,3},{2,0},{3,1},{4,6},{5,7},{6,4},{7,5},{8,10},{9,11},{10,... | collective-permute-start | bytes 786440 | tf_op jit(solution)/shard_map/ppermute | solution.py:440
  17.2 15.1 %collective-permute-start.4 = (f32[256,256]{1,0:T(8,128)S(1)}, f32[256,256]{1,0:T(8,128)S(1)}, u32[]{:S(2)}, u32[]{:S(2)}) collective-permute-start(f32[256,256]{1,0:T(8,128)S(1)} %get-tuple-element.28.own), channel_id=1, source_target_pairs={{0,1},{1,0},{2,3},{3,2},{4,5},{5,4},{6,7},{7,6},{8,9},{9,8},{10,11... | collective-permute-start | bytes 786440 | tf_op jit(solution)/shard_map/ppermute | solution.py:436
  27.5 3.6 %copy-start.1 = (bf16[1,2,1024,1024]{3,2,1,0:T(8,128)(2,1)S(1)}, bf16[1,2,1024,1024]{3,2,1,0:T(8,128)(2,1)}, u32[]{:S(2)}) copy-start(bf16[1,2,1024,1024]{3,2,1,0:T(8,128)(2,1)} %param.6) | copy-start | bytes 12582916
  28.9 3.5 %collective-permute-start.5 = (f32[256,256]{1,0:T(8,128)S(1)}, f32[256,256]{1,0:T(8,128)S(1)}, u32[]{:S(2)}, u32[]{:S(2)}) collective-permute-start(f32[256,256]{1,0:T(8,128)S(1)} %get-tuple-element.29.across), channel_id=1, source_target_pairs={{0,1},{1,0},{2,3},{3,2},{4,5},{5,4},{6,7},{7,6},{8,9},{9,8},{10,11... | collective-permute-start | bytes 786440 | tf_op jit(solution)/shard_map/ppermute | solution.py:436
  29.0 4.9 %collective-permute-start.1 = (bf16[128,128]{1,0:T(8,128)(2,1)S(1)}, bf16[128,128]{1,0:T(8,128)(2,1)S(1)}, u32[]{:S(2)}, u32[]{:S(2)}) collective-permute-start(bf16[128,128]{1,0:T(8,128)(2,1)S(1)} %get-tuple-element.25), channel_id=1, source_target_pairs={{0,1},{1,0},{2,3},{3,2},{4,5},{5,4},{6,7},{7,6},{8,9},{9,8},{10,11... | collective-permute-start | bytes 98312 | tf_op jit(solution)/shard_map/ppermute | solution.py:436
  29.5 4.4 %collective-permute-start.2 = (bf16[128,128]{1,0:T(8,128)(2,1)S(1)}, bf16[128,128]{1,0:T(8,128)(2,1)S(1)}, u32[]{:S(2)}, u32[]{:S(2)}) collective-permute-start(bf16[128,128]{1,0:T(8,128)(2,1)S(1)} %get-tuple-element.26), channel_id=1, source_target_pairs={{0,2},{1,3},{2,0},{3,1},{4,6},{5,7},{6,4},{7,5},{8,10},{9,11},{10,... | collective-permute-start | bytes 98312 | tf_op jit(solution)/shard_map/ppermute | solution.py:440
  31.1 3.7 %collective-permute-start.3 = (bf16[128,128]{1,0:T(8,128)(2,1)S(1)}, bf16[128,128]{1,0:T(8,128)(2,1)S(1)}, u32[]{:S(2)}, u32[]{:S(2)}) collective-permute-start(bf16[128,128]{1,0:T(8,128)(2,1)S(1)} %get-tuple-element.27), channel_id=1, source_target_pairs={{0,3},{1,2},{2,1},{3,0},{4,7},{5,6},{6,5},{7,4},{8,11},{9,10},{10,... | collective-permute-start | bytes 98312 | tf_op jit(solution)/shard_map/ppermute | solution.py:444
  33.2 10.9 %collective-permute-start.9 = (bf16[256,256]{1,0:T(8,128)(2,1)S(1)}, bf16[256,256]{1,0:T(8,128)(2,1)S(1)}, u32[]{:S(2)}, u32[]{:S(2)}) collective-permute-start(bf16[256,256]{1,0:T(8,128)(2,1)S(1)} %get-tuple-element.33), channel_id=1, source_target_pairs={{4,8},{8,12},{5,13},{6,10},{10,14},{7,15},{20,24},{24,28},{21,29},... | collective-permute-start | bytes 393224 | tf_op jit(solution)/shard_map/ppermute | solution.py:468
  35.7 9.2 %collective-permute-start.8 = (bf16[128,128]{1,0:T(8,128)(2,1)S(1)}, bf16[128,128]{1,0:T(8,128)(2,1)S(1)}, u32[]{:S(2)}, u32[]{:S(2)}) collective-permute-start(bf16[128,128]{1,0:T(8,128)(2,1)S(1)} %get-tuple-element.32._total), channel_id=1, source_target_pairs={{0,12},{1,13},{2,14},{3,15},{16,28},{17,29},{18,30},{19,31}} | collective-permute-start | bytes 98312 | tf_op jit(solution)/shard_map/ppermute | solution.py:473
  40.4 4.6 %collective-permute-start.7 = (bf16[128,128]{1,0:T(8,128)(2,1)S(1)}, bf16[128,128]{1,0:T(8,128)(2,1)S(1)}, u32[]{:S(2)}, u32[]{:S(2)}) collective-permute-start(bf16[128,128]{1,0:T(8,128)(2,1)S(1)} %get-tuple-element.32._total), channel_id=1, source_target_pairs={{0,8},{1,9},{2,10},{3,11},{4,12},{5,13},{6,14},{7,15},{16,24},{17,... | collective-permute-start | bytes 98312 | tf_op jit(solution)/shard_map/ppermute | solution.py:473
  42.0 3.7 %collective-permute-start.6 = (bf16[128,128]{1,0:T(8,128)(2,1)S(1)}, bf16[128,128]{1,0:T(8,128)(2,1)S(1)}, u32[]{:S(2)}, u32[]{:S(2)}) collective-permute-start(bf16[128,128]{1,0:T(8,128)(2,1)S(1)} %get-tuple-element.32._total), channel_id=1, source_target_pairs={{0,4},{1,5},{2,6},{3,7},{4,8},{5,9},{6,10},{7,11},{8,12},{9,13},{1... | collective-permute-start | bytes 98312 | tf_op jit(solution)/shard_map/ppermute | solution.py:473
  44.1 1.6 %collective-permute-start.10 = (bf16[256,256]{1,0:T(8,128)(2,1)S(1)}, bf16[256,256]{1,0:T(8,128)(2,1)S(1)}, u32[]{:S(2)}, u32[]{:S(2)}) collective-permute-start(bf16[256,256]{1,0:T(8,128)(2,1)S(1)} %collective-permute-done.9.got), channel_id=1, source_target_pairs={{0,1},{1,0},{2,3},{3,2},{4,5},{5,4},{6,7},{7,6},{8,9},{9,8},{10,11... | collective-permute-start | bytes 393224 | tf_op jit(solution)/shard_map/ppermute | solution.py:436
  46.8 3.9 %collective-permute-start.11 = (bf16[128,128]{1,0:T(8,128)(2,1)S(1)}, bf16[128,128]{1,0:T(8,128)(2,1)S(1)}, u32[]{:S(2)}, u32[]{:S(2)}) collective-permute-start(bf16[128,128]{1,0:T(8,128)(2,1)S(1)} %get-tuple-element.36), channel_id=1, source_target_pairs={{0,1},{1,0},{2,3},{3,2},{4,5},{5,4},{6,7},{7,6},{8,9},{9,8},{10,11... | collective-permute-start | bytes 98312 | tf_op jit(solution)/shard_map/ppermute | solution.py:436
  46.9 4.0 %collective-permute-start.12 = (bf16[128,128]{1,0:T(8,128)(2,1)S(1)}, bf16[128,128]{1,0:T(8,128)(2,1)S(1)}, u32[]{:S(2)}, u32[]{:S(2)}) collective-permute-start(bf16[128,128]{1,0:T(8,128)(2,1)S(1)} %get-tuple-element.37), channel_id=1, source_target_pairs={{0,2},{1,3},{2,0},{3,1},{4,6},{5,7},{6,4},{7,5},{8,10},{9,11},{10,... | collective-permute-start | bytes 98312 | tf_op jit(solution)/shard_map/ppermute | solution.py:440
  48.1 3.3 %collective-permute-start.13 = (bf16[128,128]{1,0:T(8,128)(2,1)S(1)}, bf16[128,128]{1,0:T(8,128)(2,1)S(1)}, u32[]{:S(2)}, u32[]{:S(2)}) collective-permute-start(bf16[128,128]{1,0:T(8,128)(2,1)S(1)} %get-tuple-element.38), channel_id=1, source_target_pairs={{0,3},{1,2},{2,1},{3,0},{4,7},{5,6},{6,5},{7,4},{8,11},{9,10},{10,... | collective-permute-start | bytes 98312 | tf_op jit(solution)/shard_map/ppermute | solution.py:444

commit v14 on v13

--- a/solution.py
+++ b/solution.py
@@ -10,7 +10,7 @@
 BLK = 32
 CAP = 2
 GROUP = 4
-HEAD = 16
+HEAD = 8
 CORES = 2
 
 HIGH = lax.Precision.HIGHEST
@@ -232,20 +232,22 @@
     )(pattern, green, coupling, tie)
 
 
-def image_kernel(green, source, out):
+def image_kernel(green, source, _tie, out):
     for e in range(green.shape[0]):
         out[e] = dot(green[e], source[e])
 
 
-def images(green, source):
-    return call(image_kernel, "image", [IN_VMEM] * 2, shape(*source.shape, dtype=F32), [], 1.2)(green, source)
+def images(green, source, tie):
+    return call(
+        image_kernel, "image", [IN_VMEM] * 2 + [IN_PLACE], shape(*source.shape, dtype=F32), [], 1.2
+    )(green, source, tie)
 
 
 def times(a, b):
     return dot(a[0], b[0]) + (dot(a[0], b[1]) + dot(a[1], b[0]))
 
 
-def chain_kernel(own, near, across, far, _image, total_out, parts, maps):
+def chain_kernel(own, near, across, far, total_out, parts, maps):
     collect((own, near, across, far), maps)
     split = [two_parts(maps[j]) for j in range(GROUP)]
     lower, upper = two_parts(times(split[1], split[0])), two_parts(times(split[3], split[2]))
@@ -255,16 +257,16 @@
         parts[1, j] = low
 
 
-def chain(maps, dtype, tie):
+def chain(maps, dtype):
     face = maps[0].shape[0]
     return call(
         chain_kernel,
         "chain_maps",
-        [IN_VMEM] * GROUP + [IN_PLACE],
+        [IN_VMEM] * GROUP,
         [shape(face, face, dtype=dtype), shape(2, GROUP, face, face)],
         [pltpu.VMEM((GROUP, face, face), F32)],
         0.9,
-    )(*maps, tie)
+    )(*maps)
 
 
 def source_kernel(received, inject, face_rows, _map, source, own, near, across, far, _same_map, quarters, total, heads, targets, sem):
@@ -382,7 +384,7 @@
         ref[...] = work[at].astype(BF16)
 
 
-def entering_kernel(first, second, third, got, other, parts, upto, local, *out):
+def entering_kernel(_image, first, second, third, got, other, parts, upto, local, *out):
     first_core = place() % CORES == 0
     state = unpack(third[...].astype(F32))
     for below, (one, two) in ((second, (other, got)), (first, (got, other))):
@@ -392,20 +394,20 @@
     sweep_plane(state, parts, upto, local, out)
 
 
-def entering_from_kernel(base, parts, upto, local, *out):
+def entering_from_kernel(_image, base, parts, upto, local, *out):
     sweep_plane(unpack(base[...]), parts, upto, local, out)
 
 
-def entering(body, args):
+def entering(body, tie, args):
     half, columns = args[0].shape
     return call(
         body,
         "entering",
-        [IN_VMEM] * len(args),
+        [IN_PLACE] + [IN_VMEM] * len(args),
         [shape(half, columns)] * GROUP,
         [pltpu.VMEM((GROUP, half, columns), F32)],
         1.4,
-    )(*args)
+    )(tie, *args)
 
 
 def waves_kernel(own, near, across, far, prop, image, out, arrived):
@@ -502,18 +504,18 @@
     source, *quarters, across = placed_source(received, inject, face_rows, across)
     shifts = exchange(*quarters, sections)
     far = to_near(across, sections)
-    image = images(green, source)
     four = sections // GROUP == 4
-    total_map, parts = chain([own_map, near, across, far], BF16 if four else F32, image)
+    total_map, parts = chain([own_map, near, across, far], BF16 if four else F32)
     maps = maps_up(total_map, sections) if four else []
     total, local = plane_total(shifts, parts)
     upto = maps_upto(parts, total)
+    image = images(green, source, total)
     if four:
         below = [upward(total, k, sections) for k in range(1, 4)]
-        entered = entering(entering_kernel, (*below, *maps, parts, upto, local))
+        entered = entering(entering_kernel, image, (*below, *maps, parts, upto, local))
     else:
         base = scan_below(total_map, total, sections)
-        entered = entering(entering_from_kernel, (base, parts, upto, local))
+        entered = entering(entering_from_kernel, image, (base, parts, upto, local))
     arrived = exchange(*entered, sections)
     prop = propagator(tiles, green, coupling, entered[0])
     return final_waves(arrived, prop, image)[None]

time: 53.3 us -> 53.8 us (level)
    ppermute x3, waiting for transfers between devices: 9.47 us -> 11.4 us  [to_across(): lax.ppermute(item, 'sec', [(s, s // GROUP * GROUP + (s % GROUP + CORES) %...]
    all_to_all x1, waiting for transfers between devices: 0.94 us -> 0.01 us  [per_device(): lax.all_to_all(outgoing, 'sec', split_axis=0, concat_axis=0, tiled=True)]
    ppermute x3, waiting for transfers between devices: 0.79 us -> 0.01 us  [upward(): return lax.ppermute(item, 'sec', up_shift(sections, k))]
    ppermute x3, starting transfers between devices: 4.87 us -> 4.32 us  [to_across(): lax.ppermute(item, 'sec', [(s, s // GROUP * GROUP + (s % GROUP + CORES) %...]
  transfers between devices with their start and end apart: 15 -> 15, of which waited for: 6 -> 5; matrix products, arithmetic and copies ran while one was open for 0% -> 0% of each run, Pallas kernels for 15% -> 15%
where the time goes in v14:
time: 53.8 us; the launch traced here: 53.4 us
  starting transfers between devices  22.8 us (42%)
  Pallas kernels  15.1 us (28%)
  waiting for transfers between devices  13 us (24%)
  local copies, waits for them, and re-layouts  2.2 us (4%)
    ppermute x3, waiting for transfers between devices, to_across(): lax.ppermute(item, 'sec', [(s, s // GROUP * GROUP + (s % GROUP + CORES) %...  11.4 us
    ppermute x3, starting transfers between devices, upward(): return lax.ppermute(item, 'sec', up_shift(sections, k))  8.51 us
    all_to_all x1, starting transfers between devices, per_device(): lax.all_to_all(outgoing, 'sec', split_axis=0, concat_axis=0, tiled=True)  7.39 us
    pallas_call x1, Pallas kernels, outgoing_pairs(): call(pairs_kernel, 'pairs', [IN_HBM] * 4, shape(sections, CAP * energies...  4.52 us
    ppermute x3, starting transfers between devices, to_across(): lax.ppermute(item, 'sec', [(s, s // GROUP * GROUP + (s % GROUP + CORES) %...  4.32 us
    unnamed x10, local copies, waits for them, and re-layouts  2.2 us
    pallas_call x1, Pallas kernels, propagator(): call(prop_kernel, 'prop', [IN_SMEM, IN_VMEM, IN_VMEM, IN_PLACE], shape(en...  1.93 us
    ppermute x2, waiting for transfers between devices, to_far(): lax.ppermute(item, 'sec', [(s, s // GROUP * GROUP + (s % GROUP + CORES) %...  1.6 us
  transfers between devices with their start and end apart: 15, of which 5 were waited for; matrix products, arithmetic and copies ran while one was open for 0% of the time, Pallas kernels for 15%

profile of v14, /device:TPU:0, one launch (start us, length us, event | category | flops | bytes accessed | tf_op | source)
XLA Modules:
  0.0 53.4 jit_solution(2963539894005039998)
XLA Ops:
  0.0 4.5 %pairs.1 = bf16[16,136,128]{2,1,0:T(8,128)(2,1)} custom-call(s32[16]{0:T(128)} %bitcast.20, s32[2,16]{1,0:T(2,128)} %bitcast.19, bf16[2,1024,1024]{2,1,0:T(8,128)(2,1)} %bitcast.9, bf16[2,1024,128]{2,1,0:T(8,128)(2,1)} %bitcast.13), custom_call_target="tpu_custom_call" | custom-call | flops 4600000000 | tf_op jit(solution)/shard_map/pairs/pallas_call | solution.py:168
  4.5 0.0 copy-start.2
  4.5 7.4 %all-to-all-start = ((bf16[16,136,128]{2,1,0:T(8,128)(2,1)}), bf16[16,136,128]{2,1,0:T(8,128)(2,1)S(1)}, u32[]{:S(2)}, u32[]{:S(2)}) async-start(bf16[16,136,128]{2,1,0:T(8,128)(2,1)} %pairs.1), calls=%async_computation | async-start | bytes 1114112 | tf_op jit(solution)/shard_map/all_to_all | solution.py:498
  11.9 0.0 copy-done.3
  12.0 0.0 copy-done.4
  12.0 0.0 copy-start
  12.0 2.2 %copy-done = bf16[1,2,1024,1024]{3,2,1,0:T(8,128)(2,1)S(1)} copy-done((bf16[1,2,1024,1024]{3,2,1,0:T(8,128)(2,1)S(1)}, bf16[1,2,1024,1024]{3,2,1,0:T(8,128)(2,1)}, u32[]{:S(2)}) %copy-start) | copy-done | bytes 4194328
  14.2 1.1 %face_maps.1 = (f32[256,256]{1,0:T(8,128)S(1)}, f32[256,256]{1,0:T(8,128)S(1)}, bf16[2,256,1024]{2,1,0:T(8,128)(2,1)S(1)}) custom-call(s32[2,8]{1,0:T(2,128)S(1)} %bitcast.17, bf16[2,1024,1024]{2,1,0:T(8,128)(2,1)S(1)} %bitcast.10, bf16[1024,256]{1,0:T(8,128)(2,1)S(1)} %bitcast.15), custom_call_target="tpu_custom_call" | custom-call | flops 1380000000 | tf_op jit(solution)/shard_map/face_maps/pallas_call | solution.py:206
  15.3 2.0 %collective-permute-start = (f32[256,256]{1,0:T(8,128)S(1)}, f32[256,256]{1,0:T(8,128)S(1)}, u32[]{:S(2)}, u32[]{:S(2)}) collective-permute-start(f32[256,256]{1,0:T(8,128)S(1)} %get-tuple-element.23), channel_id=1, source_target_pairs={{0,2},{1,3},{2,0},{3,1},{4,6},{5,7},{6,4},{7,5},{8,10},{9,11},{10,... | collective-permute-start | bytes 786440 | tf_op jit(solution)/shard_map/ppermute | solution.py:442
  17.3 0.0 collective-permute-start.4
  17.3 9.9 %collective-permute-done._map = f32[256,256]{1,0:T(8,128)S(1)} collective-permute-done((f32[256,256]{1,0:T(8,128)S(1)}, f32[256,256]{1,0:T(8,128)S(1)}, u32[]{:S(2)}, u32[]{:S(2)}) %collective-permute-start) | collective-permute-done | bytes 262176 | tf_op jit(solution)/shard_map/ppermute | solution.py:442
  27.2 0.0 all-to-all-done.received
  27.2 0.0 copy-done.2
  27.2 1.4 %source_and_face.1 = (bf16[2,1024,128]{2,1,0:T(8,128)(2,1)S(1)}, bf16[128,128]{1,0:T(8,128)(2,1)S(1)}, bf16[128,128]{1,0:T(8,128)(2,1)S(1)}, bf16[128,128]{1,0:T...) custom-call(bf16[16,136,128]{2,1,0:T(8,128)(2,1)S(1)} %all-to-all-done.rec, ...), custom_call_target="tpu_custom_call", output_to_operand_aliasing={{5}: (3, {})} | custom-call | flops 1610000000 | tf_op jit(solution)/shard_map/source_and_face/pallas_call | solution.py:313
  28.6 0.1 collective-permute-start.5
  28.7 0.5 collective-permute-start.1
  29.2 1.7 %collective-permute-start.2 = (bf16[128,128]{1,0:T(8,128)(2,1)S(1)}, bf16[128,128]{1,0:T(8,128)(2,1)S(1)}, u32[]{:S(2)}, u32[]{:S(2)}) collective-permute-start(bf16[128,128]{1,0:T(8,128)(2,1)S(1)} %get-tuple-element.27), channel_id=1, source_target_pairs={{0,2},{1,3},{2,0},{3,1},{4,6},{5,7},{6,4},{7,5},{8,10},{9,11},{10,... | collective-permute-start | bytes 98312 | tf_op jit(solution)/shard_map/ppermute | solution.py:442
  30.8 0.0 collective-permute-start.3
  30.8 0.0 collective-permute-done.4.near
  30.8 0.0 collective-permute-done.5.far
  30.9 0.8 %chain_maps.1 = (bf16[256,256]{1,0:T(8,128)(2,1)S(1)}, bf16[2,4,256,256]{3,2,1,0:T(8,128)(2,1)S(1)}) custom-call(f32[256,256]{1,0:T(8,128)S(1)} %get-tuple-element.29.own, f32[256,256]{1,0:T(8,128)S(1)} %collective-permute-done.4.near, f32[256,256]{1,0:T(8,128)S(1)} %get-tuple-element.30.across, f32[256,256]{1,0:T(8,128)S(1)} %collective-permute-done.5.far), custom_call_target="tpu_custom_call" | custom-call | flops 1035000000 | tf_op jit(solution)/shard_map/chain_maps/pallas_call | solution.py:262
  31.7 0.7 %collective-permute-start.9 = (bf16[256,256]{1,0:T(8,128)(2,1)S(1)}, bf16[256,256]{1,0:T(8,128)(2,1)S(1)}, u32[]{:S(2)}, u32[]{:S(2)}) collective-permute-start(bf16[256,256]{1,0:T(8,128)(2,1)S(1)} %get-tuple-element.33), channel_id=1, source_target_pairs={{4,8},{8,12},{5,13},{6,10},{10,14},{7,15},{20,24},{24,28},{21,29},... | collective-permute-start | bytes 393224 | tf_op jit(solution)/shard_map/ppermute | solution.py:470
  32.4 0.0 collective-permute-done.1.near
  32.4 0.7 %collective-permute-done.2.across = bf16[128,128]{1,0:T(8,128)(2,1)S(1)} collective-permute-done((bf16[128,128]{1,0:T(8,128)(2,1)S(1)}, bf16[128,128]{1,0:T(8,128)(2,1)S(1)}, u32[]{:S(2)}, u32[]{:S(2)}) %collective-permute-start.2) | collective-permute-done | bytes 32800 | tf_op jit(solution)/shard_map/ppermute | solution.py:442
  33.1 1.4 %collective-permute-done.3.far = bf16[128,128]{1,0:T(8,128)(2,1)S(1)} collective-permute-done((bf16[128,128]{1,0:T(8,128)(2,1)S(1)}, bf16[128,128]{1,0:T(8,128)(2,1)S(1)}, u32[]{:S(2)}, u32[]{:S(2)}) %collective-permute-start.3) | collective-permute-done | bytes 32800 | tf_op jit(solution)/shard_map/ppermute | solution.py:446
  34.5 0.9 %plane_total.1 = (bf16[128,128]{1,0:T(8,128)(2,1)S(1)}, f32[3,256,128]{2,1,0:T(8,128)S(1)}) custom-call(bf16[128,128]{1,0:T(8,128)(2,1)S(1)} %get-tuple-element.25.own, bf16[128,128]{1,0:T(8,128)(2,1)S(1)} %collective-permute-done.1.near, bf16[128,128]{1,0:T(8,128)(2,1)S(1)} %collective-permute-done.2.across, ...), custom_call_target="tpu_custom_call" | custom-call | flops 3449999872 | tf_op jit(solution)/shard_map/plane_total/pallas_call | solution.py:350
  35.5 0.0 copy-start.1
  35.5 4.7 %collective-permute-start.8 = (bf16[128,128]{1,0:T(8,128)(2,1)S(1)}, bf16[128,128]{1,0:T(8,128)(2,1)S(1)}, u32[]{:S(2)}, u32[]{:S(2)}) collective-permute-start(bf16[128,128]{1,0:T(8,128)(2,1)S(1)} %get-tuple-element.32._tie._total), channel_id=1, source_target_pairs={{0,12},{1,13},{2,14},{3,15},{16,28},{17,29},{18,30},{19,31}} | collective-permute-start | bytes 98312 | tf_op jit(solution)/shard_map/ppermute | solution.py:475
  40.2 1.3 %collective-permute-start.7 = (bf16[128,128]{1,0:T(8,128)(2,1)S(1)}, bf16[128,128]{1,0:T(8,128)(2,1)S(1)}, u32[]{:S(2)}, u32[]{:S(2)}) collective-permute-start(bf16[128,128]{1,0:T(8,128)(2,1)S(1)} %get-tuple-element.32._tie._total), channel_id=1, source_target_pairs={{0,8},{1,9},{2,10},{3,11},{4,12},{5,13},{6,14},{7,15},{16,24},{17,... | collective-permute-start | bytes 98312 | tf_op jit(solution)/shard_map/ppermute | solution.py:475
  41.5 2.5 %collective-permute-start.6 = (bf16[128,128]{1,0:T(8,128)(2,1)S(1)}, bf16[128,128]{1,0:T(8,128)(2,1)S(1)}, u32[]{:S(2)}, u32[]{:S(2)}) collective-permute-start(bf16[128,128]{1,0:T(8,128)(2,1)S(1)} %get-tuple-element.32._tie._total), channel_id=1, source_target_pairs={{0,4},{1,5},{2,6},{3,7},{4,8},{5,9},{6,10},{7,11},{8,12},{9,13},{1... | collective-permute-start | bytes 98312 | tf_op jit(solution)/shard_map/ppermute | solution.py:475
  44.0 0.0 collective-permute-done.9.got
  44.0 0.1 collective-permute-start.10
  44.1 0.7 %maps_upto.1.upto = bf16[2,2,256,256]{3,2,1,0:T(8,128)(2,1)S(1)} custom-call(bf16[2,4,256,256]{3,2,1,0:T(8,128)(2,1)S(1)} %get-tuple-element.31.parts, bf16[128,128]{1,0:T(8,128)(2,1)S(1)} %get-tuple-element.32._tie._total), custom_call_target="tpu_custom_call" | custom-call | flops 3449999872 | tf_op jit(solution)/shard_map/maps_upto/pallas_call | solution.py:369
  44.8 0.0 copy-done.1
  44.8 1.2 %image.1._image = f32[2,1024,128]{2,1,0:T(8,128)S(1)} custom-call(bf16[2,1024,1024]{2,1,0:T(8,128)(2,1)S(1)} %bitcast.11, bf16[2,1024,128]{2,1,0:T(8,128)(2,1)S(1)} %get-tuple-element.24.source, bf16[128,128]{1,0:T(8,128)(2,1)S(1)} %get-tuple-element.32._tie._total), custom_call_target="tpu_custom_call" | custom-call | flops 1380000000 | tf_op jit(solution)/shard_map/image/pallas_call | solution.py:241
  46.0 0.0 collective-permute-done.8.third
  46.0 0.0 collective-permute-done.7.second
  46.0 0.0 collective-permute-done.6.first
  46.1 0.0 collective-permute-done.10.other
  46.1 1.1 %entering.1 = (bf16[128,128]{1,0:T(8,128)(2,1)S(1)}, bf16[128,128]{1,0:T(8,128)(2,1)S(1)}, bf16[128,128]{1,0:T(8,128)(2,1)S(1)}, bf16[128,128]{1,0:T(8,128)(2,1)S(1)}) custom-call(f32[2,1024,128]{2,1,0:T(8,128)S(1)} %image.1._image, bf16[128,128]{1,0:T(8,128)(2,1)S(1)} %collective-permute-done.6.first, bf16[128,128]{1,0:T(8,128)(2,1)S(1)} %collective-permute-done.7.second, ...), custom_call_target="tpu_custom_call" | custom-call | flops 1610000000 | tf_op jit(solution)/shard_map/entering/pallas_call | solution.py:403
  47.2 0.6 %collective-permute-start.11 = (bf16[128,128]{1,0:T(8,128)(2,1)S(1)}, bf16[128,128]{1,0:T(8,128)(2,1)S(1)}, u32[]{:S(2)}, u32[]{:S(2)}) collective-permute-start(bf16[128,128]{1,0:T(8,128)(2,1)S(1)} %get-tuple-element.36), channel_id=1, source_target_pairs={{0,1},{1,0},{2,3},{3,2},{4,5},{5,4},{6,7},{7,6},{8,9},{9,8},{10,11... | collective-permute-start | bytes 98312 | tf_op jit(solution)/shard_map/ppermute | solution.py:438
  47.7 0.7 %collective-permute-start.12 = (bf16[128,128]{1,0:T(8,128)(2,1)S(1)}, bf16[128,128]{1,0:T(8,128)(2,1)S(1)}, u32[]{:S(2)}, u32[]{:S(2)}) collective-permute-start(bf16[128,128]{1,0:T(8,128)(2,1)S(1)} %get-tuple-element.37), channel_id=1, source_target_pairs={{0,2},{1,3},{2,0},{3,1},{4,6},{5,7},{6,4},{7,5},{8,10},{9,11},{10,... | collective-permute-start | bytes 98312 | tf_op jit(solution)/shard_map/ppermute | solution.py:442
  48.4 0.8 %collective-permute-start.13 = (bf16[128,128]{1,0:T(8,128)(2,1)S(1)}, bf16[128,128]{1,0:T(8,128)(2,1)S(1)}, u32[]{:S(2)}, u32[]{:S(2)}) collective-permute-start(bf16[128,128]{1,0:T(8,128)(2,1)S(1)} %get-tuple-element.38), channel_id=1, source_target_pairs={{0,3},{1,2},{2,1},{3,0},{4,7},{5,6},{6,5},{7,4},{8,11},{9,10},{10,... | collective-permute-start | bytes 98312 | tf_op jit(solution)/shard_map/ppermute | solution.py:446
  49.1 1.9 %prop.1 = bf16[2,1024,256]{2,1,0:T(8,128)(2,1)S(1)} custom-call(s32[2,8]{1,0:T(2,128)S(1)} %bitcast.18, bf16[2,1024,1024]{2,1,0:T(8,128)(2,1)S(1)} %bitcast.12, bf16[1024,256]{1,0:T(8,128)(2,1)S(1)} %bitcast.16, bf16[128,128]{1,0:T(8,128)(2,1)S(1)} %get-tuple-element.35._tie.own), custom_call_target="tpu_custom_call" | custom-call | flops 1724999936 | tf_op jit(solution)/shard_map/prop/pallas_call | solution.py:225
  51.1 0.0 collective-permute-done.11.near
  51.1 0.8 %collective-permute-done.12.across = bf16[128,128]{1,0:T(8,128)(2,1)S(1)} collective-permute-done((bf16[128,128]{1,0:T(8,128)(2,1)S(1)}, bf16[128,128]{1,0:T(8,128)(2,1)S(1)}, u32[]{:S(2)}, u32[]{:S(2)}) %collective-permute-start.12) | collective-permute-done | bytes 32800 | tf_op jit(solution)/shard_map/ppermute | solution.py:442
  51.9 0.2 collective-permute-done.13.far
  52.1 1.3 %waves.1 = bf16[2,1024,128]{2,1,0:T(8,128)(2,1)} custom-call(bf16[128,128]{1,0:T(8,128)(2,1)S(1)} %get-tuple-element.35._tie.own, bf16[128,128]{1,0:T(8,128)(2,1)S(1)} %collective-permute-done.11.near, bf16[128,128]{1,0:T(8,128)(2,1)S(1)} %collective-permute-done.12.across, bf16[128,128]{1,0:T(8,128)(2,1)S(1)} %collective-permute-done.13.far, ...), custom_call_target="tpu_custom_call" | custom-call | flops 1495000064 | tf_op jit(solution)/shard_map/waves/pallas_call | solution.py:427
  (2 shorter events, 0.0 us)
Async XLA Ops:
  0.0 11.9 %copy-start.3 = (bf16[1,1024,256]{2,1,0:T(8,128)(2,1)S(1)}, bf16[1,1024,256]{2,1,0:T(8,128)(2,1)}, u32[]{:S(2)}) copy-start(bf16[1,1024,256]{2,1,0:T(8,128)(2,1)} %param.8) | copy-start | bytes 1572868
  0.0 12.0 %copy-start.4 = (s32[1,8,2]{1,2,0:T(2,128)S(1)}, s32[1,8,2]{1,2,0:T(2,128)}, u32[]{:S(2)}) copy-start(s32[1,8,2]{1,2,0:T(2,128)} %param.9) | copy-start | bytes 196
  4.5 22.7 %copy-start.2 = (bf16[1,2,1024,128]{3,2,1,0:T(8,128)(2,1)S(1)}, bf16[1,2,1024,128]{3,2,1,0:T(8,128)(2,1)}, u32[]{:S(2)}) copy-start(bf16[1,2,1024,128]{3,2,1,0:T(8,128)(2,1)} %param.7) | copy-start | bytes 1572868
  4.5 22.6 %all-to-all-start = ((bf16[16,136,128]{2,1,0:T(8,128)(2,1)}), bf16[16,136,128]{2,1,0:T(8,128)(2,1)S(1)}, u32[]{:S(2)}, u32[]{:S(2)}) async-start(bf16[16,136,128]{2,1,0:T(8,128)(2,1)} %pairs.1), calls=%async_computation | async-start | bytes 1114112 | tf_op jit(solution)/shard_map/all_to_all | solution.py:498
  12.0 2.2 %copy-start = (bf16[1,2,1024,1024]{3,2,1,0:T(8,128)(2,1)S(1)}, bf16[1,2,1024,1024]{3,2,1,0:T(8,128)(2,1)}, u32[]{:S(2)}) copy-start(bf16[1,2,1024,1024]{3,2,1,0:T(8,128)(2,1)} %param.6) | copy-start | bytes 12582916
  15.3 11.9 %collective-permute-start = (f32[256,256]{1,0:T(8,128)S(1)}, f32[256,256]{1,0:T(8,128)S(1)}, u32[]{:S(2)}, u32[]{:S(2)}) collective-permute-start(f32[256,256]{1,0:T(8,128)S(1)} %get-tuple-element.23), channel_id=1, source_target_pairs={{0,2},{1,3},{2,0},{3,1},{4,6},{5,7},{6,4},{7,5},{8,10},{9,11},{10,... | collective-permute-start | bytes 786440 | tf_op jit(solution)/shard_map/ppermute | solution.py:442
  17.3 13.6 %collective-permute-start.4 = (f32[256,256]{1,0:T(8,128)S(1)}, f32[256,256]{1,0:T(8,128)S(1)}, u32[]{:S(2)}, u32[]{:S(2)}) collective-permute-start(f32[256,256]{1,0:T(8,128)S(1)} %get-tuple-element.29.own), channel_id=1, source_target_pairs={{0,1},{1,0},{2,3},{3,2},{4,5},{5,4},{6,7},{7,6},{8,9},{9,8},{10,11... | collective-permute-start | bytes 786440 | tf_op jit(solution)/shard_map/ppermute | solution.py:438
  28.6 2.2 %collective-permute-start.5 = (f32[256,256]{1,0:T(8,128)S(1)}, f32[256,256]{1,0:T(8,128)S(1)}, u32[]{:S(2)}, u32[]{:S(2)}) collective-permute-start(f32[256,256]{1,0:T(8,128)S(1)} %get-tuple-element.30.across), channel_id=1, source_target_pairs={{0,1},{1,0},{2,3},{3,2},{4,5},{5,4},{6,7},{7,6},{8,9},{9,8},{10,11... | collective-permute-start | bytes 786440 | tf_op jit(solution)/shard_map/ppermute | solution.py:438
  28.7 3.7 %collective-permute-start.1 = (bf16[128,128]{1,0:T(8,128)(2,1)S(1)}, bf16[128,128]{1,0:T(8,128)(2,1)S(1)}, u32[]{:S(2)}, u32[]{:S(2)}) collective-permute-start(bf16[128,128]{1,0:T(8,128)(2,1)S(1)} %get-tuple-element.26), channel_id=1, source_target_pairs={{0,1},{1,0},{2,3},{3,2},{4,5},{5,4},{6,7},{7,6},{8,9},{9,8},{10,11... | collective-permute-start | bytes 98312 | tf_op jit(solution)/shard_map/ppermute | solution.py:438
  29.2 3.9 %collective-permute-start.2 = (bf16[128,128]{1,0:T(8,128)(2,1)S(1)}, bf16[128,128]{1,0:T(8,128)(2,1)S(1)}, u32[]{:S(2)}, u32[]{:S(2)}) collective-permute-start(bf16[128,128]{1,0:T(8,128)(2,1)S(1)} %get-tuple-element.27), channel_id=1, source_target_pairs={{0,2},{1,3},{2,0},{3,1},{4,6},{5,7},{6,4},{7,5},{8,10},{9,11},{10,... | collective-permute-start | bytes 98312 | tf_op jit(solution)/shard_map/ppermute | solution.py:442
  30.8 3.7 %collective-permute-start.3 = (bf16[128,128]{1,0:T(8,128)(2,1)S(1)}, bf16[128,128]{1,0:T(8,128)(2,1)S(1)}, u32[]{:S(2)}, u32[]{:S(2)}) collective-permute-start(bf16[128,128]{1,0:T(8,128)(2,1)S(1)} %get-tuple-element.28), channel_id=1, source_target_pairs={{0,3},{1,2},{2,1},{3,0},{4,7},{5,6},{6,5},{7,4},{8,11},{9,10},{10,... | collective-permute-start | bytes 98312 | tf_op jit(solution)/shard_map/ppermute | solution.py:446
  31.7 12.3 %collective-permute-start.9 = (bf16[256,256]{1,0:T(8,128)(2,1)S(1)}, bf16[256,256]{1,0:T(8,128)(2,1)S(1)}, u32[]{:S(2)}, u32[]{:S(2)}) collective-permute-start(bf16[256,256]{1,0:T(8,128)(2,1)S(1)} %get-tuple-element.33), channel_id=1, source_target_pairs={{4,8},{8,12},{5,13},{6,10},{10,14},{7,15},{20,24},{24,28},{21,29},... | collective-permute-start | bytes 393224 | tf_op jit(solution)/shard_map/ppermute | solution.py:470
  35.5 9.3 %copy-start.1 = (bf16[1,2,1024,1024]{3,2,1,0:T(8,128)(2,1)S(1)}, bf16[1,2,1024,1024]{3,2,1,0:T(8,128)(2,1)}, u32[]{:S(2)}) copy-start(bf16[1,2,1024,1024]{3,2,1,0:T(8,128)(2,1)} %param.6) | copy-start | bytes 12582916
  35.5 10.6 %collective-permute-start.8 = (bf16[128,128]{1,0:T(8,128)(2,1)S(1)}, bf16[128,128]{1,0:T(8,128)(2,1)S(1)}, u32[]{:S(2)}, u32[]{:S(2)}) collective-permute-start(bf16[128,128]{1,0:T(8,128)(2,1)S(1)} %get-tuple-element.32._tie._total), channel_id=1, source_target_pairs={{0,12},{1,13},{2,14},{3,15},{16,28},{17,29},{18,30},{19,31}} | collective-permute-start | bytes 98312 | tf_op jit(solution)/shard_map/ppermute | solution.py:475
  40.2 5.8 %collective-permute-start.7 = (bf16[128,128]{1,0:T(8,128)(2,1)S(1)}, bf16[128,128]{1,0:T(8,128)(2,1)S(1)}, u32[]{:S(2)}, u32[]{:S(2)}) collective-permute-start(bf16[128,128]{1,0:T(8,128)(2,1)S(1)} %get-tuple-element.32._tie._total), channel_id=1, source_target_pairs={{0,8},{1,9},{2,10},{3,11},{4,12},{5,13},{6,14},{7,15},{16,24},{17,... | collective-permute-start | bytes 98312 | tf_op jit(solution)/shard_map/ppermute | solution.py:475
  41.5 4.5 %collective-permute-start.6 = (bf16[128,128]{1,0:T(8,128)(2,1)S(1)}, bf16[128,128]{1,0:T(8,128)(2,1)S(1)}, u32[]{:S(2)}, u32[]{:S(2)}) collective-permute-start(bf16[128,128]{1,0:T(8,128)(2,1)S(1)} %get-tuple-element.32._tie._total), channel_id=1, source_target_pairs={{0,4},{1,5},{2,6},{3,7},{4,8},{5,9},{6,10},{7,11},{8,12},{9,13},{1... | collective-permute-start | bytes 98312 | tf_op jit(solution)/shard_map/ppermute | solution.py:475
  44.0 2.0 %collective-permute-start.10 = (bf16[256,256]{1,0:T(8,128)(2,1)S(1)}, bf16[256,256]{1,0:T(8,128)(2,1)S(1)}, u32[]{:S(2)}, u32[]{:S(2)}) collective-permute-start(bf16[256,256]{1,0:T(8,128)(2,1)S(1)} %collective-permute-done.9.got), channel_id=1, source_target_pairs={{0,1},{1,0},{2,3},{3,2},{4,5},{5,4},{6,7},{7,6},{8,9},{9,8},{10,11... | collective-permute-start | bytes 393224 | tf_op jit(solution)/shard_map/ppermute | solution.py:438
  47.2 3.9 %collective-permute-start.11 = (bf16[128,128]{1,0:T(8,128)(2,1)S(1)}, bf16[128,128]{1,0:T(8,128)(2,1)S(1)}, u32[]{:S(2)}, u32[]{:S(2)}) collective-permute-start(bf16[128,128]{1,0:T(8,128)(2,1)S(1)} %get-tuple-element.36), channel_id=1, source_target_pairs={{0,1},{1,0},{2,3},{3,2},{4,5},{5,4},{6,7},{7,6},{8,9},{9,8},{10,11... | collective-permute-start | bytes 98312 | tf_op jit(solution)/shard_map/ppermute | solution.py:438
  47.7 4.2 %collective-permute-start.12 = (bf16[128,128]{1,0:T(8,128)(2,1)S(1)}, bf16[128,128]{1,0:T(8,128)(2,1)S(1)}, u32[]{:S(2)}, u32[]{:S(2)}) collective-permute-start(bf16[128,128]{1,0:T(8,128)(2,1)S(1)} %get-tuple-element.37), channel_id=1, source_target_pairs={{0,2},{1,3},{2,0},{3,1},{4,6},{5,7},{6,4},{7,5},{8,10},{9,11},{10,... | collective-permute-start | bytes 98312 | tf_op jit(solution)/shard_map/ppermute | solution.py:442
  48.4 3.7 %collective-permute-start.13 = (bf16[128,128]{1,0:T(8,128)(2,1)S(1)}, bf16[128,128]{1,0:T(8,128)(2,1)S(1)}, u32[]{:S(2)}, u32[]{:S(2)}) collective-permute-start(bf16[128,128]{1,0:T(8,128)(2,1)S(1)} %get-tuple-element.38), channel_id=1, source_target_pairs={{0,3},{1,2},{2,1},{3,0},{4,7},{5,6},{6,5},{7,4},{8,11},{9,10},{10,... | collective-permute-start | bytes 98312 | tf_op jit(solution)/shard_map/ppermute | solution.py:446

commit v15 on v14

--- a/solution.py
+++ b/solution.py
@@ -247,23 +247,25 @@
     return dot(a[0], b[0]) + (dot(a[0], b[1]) + dot(a[1], b[0]))
 
 
-def chain_kernel(own, near, across, far, total_out, parts, maps):
+def chain_kernel(own, near, across, far, total_out, sent_out, parts, maps):
     collect((own, near, across, far), maps)
     split = [two_parts(maps[j]) for j in range(GROUP)]
     lower, upper = two_parts(times(split[1], split[0])), two_parts(times(split[3], split[2]))
-    total_out[...] = times(upper, lower).astype(total_out.dtype)
+    total = times(upper, lower)
+    total_out[...] = total
+    sent_out[...] = total.astype(BF16)
     for j, (high, low) in enumerate(split):
         parts[0, j] = high
         parts[1, j] = low
 
 
-def chain(maps, dtype):
+def chain(maps):
     face = maps[0].shape[0]
     return call(
         chain_kernel,
         "chain_maps",
         [IN_VMEM] * GROUP,
-        [shape(face, face, dtype=dtype), shape(2, GROUP, face, face)],
+        [shape(face, face, dtype=F32), shape(face, face), shape(2, GROUP, face, face)],
         [pltpu.VMEM((GROUP, face, face), F32)],
         0.9,
     )(*maps)
@@ -384,13 +386,20 @@
         ref[...] = work[at].astype(BF16)
 
 
-def entering_kernel(_image, first, second, third, got, other, parts, upto, local, *out):
-    first_core = place() % CORES == 0
-    state = unpack(third[...].astype(F32))
-    for below, (one, two) in ((second, (other, got)), (first, (got, other))):
-        factor = jnp.where(first_core, one[...], two[...])
-        high, low = two_parts(state)
-        state = unpack(below[...].astype(F32)) + dot(factor, high) + dot(factor, low)
+def pair_kernel(total, below, whole, _image, out):
+    state = unpack(total[...].astype(F32)) + times(two_parts(whole[...]), two_parts(unpack(below[...].astype(F32))))
+    out[...] = pack(state).astype(BF16)
+
+
+def pair_total(total, below, whole, tie):
+    return call(
+        pair_kernel, "pair_total", [IN_VMEM] * 3 + [IN_PLACE], shape(*total.shape), [], 0.5
+    )(total, below, whole, tie)
+
+
+def entering_kernel(_image, below, first, second, got, parts, upto, local, *out):
+    high, low = two_parts(unpack(second[...].astype(F32)))
+    state = unpack(below[...].astype(F32) + first[...].astype(F32)) + dot(got[...], high) + dot(got[...], low)
     sweep_plane(state, parts, upto, local, out)
 
 
@@ -460,19 +469,9 @@
     return jnp.concatenate([packed[:, :half], packed[:, half:]], axis=0)
 
 
-def maps_up(total_map, sections):
-    pairs = []
-    for i in range(GROUP):
-        if i % CORES == 0:
-            pairs += [(GROUP + i, 2 * GROUP + i), (2 * GROUP + i, 3 * GROUP + i)]
-        else:
-            pairs += [(GROUP + i, 3 * GROUP + i)]
-    got = lax.ppermute(total_map, "sec", pairs)
-    return got, to_near(got, sections)
-
-
-def upward(item, k, sections):
-    return lax.ppermute(item, "sec", up_shift(sections, k))
+def between(item, *planes):
+    pairs = [(p * GROUP + i, q * GROUP + i) for p, q in planes for i in range(GROUP)]
+    return lax.ppermute(item, "sec", pairs)
 
 
 def scan_below(total_map, total, sections):
@@ -505,16 +504,18 @@
     shifts = exchange(*quarters, sections)
     far = to_near(across, sections)
     four = sections // GROUP == 4
-    total_map, parts = chain([own_map, near, across, far], BF16 if four else F32)
-    maps = maps_up(total_map, sections) if four else []
+    whole, sent, parts = chain([own_map, near, across, far])
+    got = between(sent, (2, 3)) if four else None
     total, local = plane_total(shifts, parts)
     upto = maps_upto(parts, total)
     image = images(green, source, total)
     if four:
-        below = [upward(total, k, sections) for k in range(1, 4)]
-        entered = entering(entering_kernel, image, (*below, *maps, parts, upto, local))
+        below = between(total, (0, 1), (2, 3))
+        pair = pair_total(total, below, whole, image)
+        first, second = between(pair, (1, 2)), between(pair, (1, 3))
+        entered = entering(entering_kernel, image, (below, first, second, got, parts, upto, local))
     else:
-        base = scan_below(total_map, total, sections)
+        base = scan_below(whole, total, sections)
         entered = entering(entering_from_kernel, image, (base, parts, upto, local))
     arrived = exchange(*entered, sections)
     prop = propagator(tiles, green, coupling, entered[0])

time: 53.8 us -> 54 us (level)
  the two profiles are of different devices: /device:TPU:0 before, /device:TPU:25 now
where the time goes in v15:
time: 54 us; the launch traced here: 53.7 us
  starting transfers between devices  19.5 us (36%)
  waiting for transfers between devices  16.4 us (30%)
  Pallas kernels  15.4 us (29%)
  local copies, waits for them, and re-layouts  2.2 us (4%)
    ppermute x3, waiting for transfers between devices, to_across(): lax.ppermute(item, 'sec', [(s, s // GROUP * GROUP + (s % GROUP + CORES) %...  8.58 us
    all_to_all x1, starting transfers between devices, per_device(): lax.all_to_all(outgoing, 'sec', split_axis=0, concat_axis=0, tiled=True)  6.26 us
    ppermute x4, waiting for transfers between devices, between(): return lax.ppermute(item, 'sec', pairs)  5.33 us
    ppermute x4, starting transfers between devices, between(): return lax.ppermute(item, 'sec', pairs)  4.67 us
    pallas_call x1, Pallas kernels, outgoing_pairs(): call(pairs_kernel, 'pairs', [IN_HBM] * 4, shape(sections, CAP * energies...  4.6 us
    ppermute x4, starting transfers between devices, to_near(): return lax.ppermute(item, 'sec', [(s, s ^ 1) for s in range(sections)])  3.52 us
    ppermute x3, starting transfers between devices, to_across(): lax.ppermute(item, 'sec', [(s, s // GROUP * GROUP + (s % GROUP + CORES) %...  2.77 us
    ppermute x2, waiting for transfers between devices, to_far(): lax.ppermute(item, 'sec', [(s, s // GROUP * GROUP + (s % GROUP + CORES) %...  2.52 us
  transfers between devices with their start and end apart: 14, of which 5 were waited for; matrix products, arithmetic and copies ran while one was open for 0% of the time, Pallas kernels for 14%

profile of v15, /device:TPU:25, one launch (start us, length us, event | category | flops | bytes accessed | tf_op | source)
XLA Modules:
  0.0 53.7 jit_solution(2716221628157651427)
XLA Ops:
  0.0 0.0 copy-start.3
  0.0 0.0 copy-start.4
  0.0 4.6 %pairs.1 = bf16[16,136,128]{2,1,0:T(8,128)(2,1)} custom-call(s32[16]{0:T(128)} %bitcast.20, s32[2,16]{1,0:T(2,128)} %bitcast.19, bf16[2,1024,1024]{2,1,0:T(8,128)(2,1)} %bitcast.9, bf16[2,1024,128]{2,1,0:T(8,128)(2,1)} %bitcast.13), custom_call_target="tpu_custom_call" | custom-call | flops 4600000000 | tf_op jit(solution)/shard_map/pairs/pallas_call | solution.py:168
  4.6 0.0 copy-start.2
  4.6 6.3 %all-to-all-start = ((bf16[16,136,128]{2,1,0:T(8,128)(2,1)}), bf16[16,136,128]{2,1,0:T(8,128)(2,1)S(1)}, u32[]{:S(2)}, u32[]{:S(2)}) async-start(bf16[16,136,128]{2,1,0:T(8,128)(2,1)} %pairs.1), calls=%async_computation | async-start | bytes 1114112 | tf_op jit(solution)/shard_map/all_to_all | solution.py:497
  10.9 0.0 copy-done.3
  10.9 0.0 copy-done.4
  10.9 0.0 copy-start
  10.9 2.2 %copy-done = bf16[1,2,1024,1024]{3,2,1,0:T(8,128)(2,1)S(1)} copy-done((bf16[1,2,1024,1024]{3,2,1,0:T(8,128)(2,1)S(1)}, bf16[1,2,1024,1024]{3,2,1,0:T(8,128)(2,1)}, u32[]{:S(2)}) %copy-start) | copy-done | bytes 4194328
  13.1 1.1 %face_maps.1 = (f32[256,256]{1,0:T(8,128)S(1)}, f32[256,256]{1,0:T(8,128)S(1)}, bf16[2,256,1024]{2,1,0:T(8,128)(2,1)S(1)}) custom-call(s32[2,8]{1,0:T(2,128)S(1)} %bitcast.17, bf16[2,1024,1024]{2,1,0:T(8,128)(2,1)S(1)} %bitcast.10, bf16[1024,256]{1,0:T(8,128)(2,1)S(1)} %bitcast.15), custom_call_target="tpu_custom_call" | custom-call | flops 1380000000 | tf_op jit(solution)/shard_map/face_maps/pallas_call | solution.py:206
  14.2 1.2 %collective-permute-start = (f32[256,256]{1,0:T(8,128)S(1)}, f32[256,256]{1,0:T(8,128)S(1)}, u32[]{:S(2)}, u32[]{:S(2)}) collective-permute-start(f32[256,256]{1,0:T(8,128)S(1)} %get-tuple-element.24), channel_id=1, source_target_pairs={{0,2},{1,3},{2,0},{3,1},{4,6},{5,7},{6,4},{7,5},{8,10},{9,11},{10,... | collective-permute-start | bytes 786440 | tf_op jit(solution)/shard_map/ppermute | solution.py:451
  15.5 0.6 %collective-permute-start.4 = (f32[256,256]{1,0:T(8,128)S(1)}, f32[256,256]{1,0:T(8,128)S(1)}, u32[]{:S(2)}, u32[]{:S(2)}) collective-permute-start(f32[256,256]{1,0:T(8,128)S(1)} %get-tuple-element.30.own), channel_id=1, source_target_pairs={{0,1},{1,0},{2,3},{3,2},{4,5},{5,4},{6,7},{7,6},{8,9},{9,8},{10,11... | collective-permute-start | bytes 786440 | tf_op jit(solution)/shard_map/ppermute | solution.py:447
  16.1 8.6 %collective-permute-done._map = f32[256,256]{1,0:T(8,128)S(1)} collective-permute-done((f32[256,256]{1,0:T(8,128)S(1)}, f32[256,256]{1,0:T(8,128)S(1)}, u32[]{:S(2)}, u32[]{:S(2)}) %collective-permute-start) | collective-permute-done | bytes 262176 | tf_op jit(solution)/shard_map/ppermute | solution.py:451
  24.7 0.0 all-to-all-done.received
  24.7 0.0 copy-done.2
  24.7 1.4 %source_and_face.1 = (bf16[2,1024,128]{2,1,0:T(8,128)(2,1)S(1)}, bf16[128,128]{1,0:T(8,128)(2,1)S(1)}, bf16[128,128]{1,0:T(8,128)(2,1)S(1)}, bf16[128,128]{1,0:T...) custom-call(bf16[16,136,128]{2,1,0:T(8,128)(2,1)S(1)} %all-to-all-done.rec, ...), custom_call_target="tpu_custom_call", output_to_operand_aliasing={{5}: (3, {})} | custom-call | flops 1610000000 | tf_op jit(solution)/shard_map/source_and_face/pallas_call | solution.py:315
  26.1 1.0 %collective-permute-start.5 = (f32[256,256]{1,0:T(8,128)S(1)}, f32[256,256]{1,0:T(8,128)S(1)}, u32[]{:S(2)}, u32[]{:S(2)}) collective-permute-start(f32[256,256]{1,0:T(8,128)S(1)} %get-tuple-element.31.across), channel_id=1, source_target_pairs={{0,1},{1,0},{2,3},{3,2},{4,5},{5,4},{6,7},{7,6},{8,9},{9,8},{10,11... | collective-permute-start | bytes 786440 | tf_op jit(solution)/shard_map/ppermute | solution.py:447
  27.1 0.1 collective-permute-start.1
  27.2 1.1 %collective-permute-start.2 = (bf16[128,128]{1,0:T(8,128)(2,1)S(1)}, bf16[128,128]{1,0:T(8,128)(2,1)S(1)}, u32[]{:S(2)}, u32[]{:S(2)}) collective-permute-start(bf16[128,128]{1,0:T(8,128)(2,1)S(1)} %get-tuple-element.28), channel_id=1, source_target_pairs={{0,2},{1,3},{2,0},{3,1},{4,6},{5,7},{6,4},{7,5},{8,10},{9,11},{10,... | collective-permute-start | bytes 98312 | tf_op jit(solution)/shard_map/ppermute | solution.py:451
  28.3 0.9 %collective-permute-start.3 = (bf16[128,128]{1,0:T(8,128)(2,1)S(1)}, bf16[128,128]{1,0:T(8,128)(2,1)S(1)}, u32[]{:S(2)}, u32[]{:S(2)}) collective-permute-start(bf16[128,128]{1,0:T(8,128)(2,1)S(1)} %get-tuple-element.29), channel_id=1, source_target_pairs={{0,3},{1,2},{2,1},{3,0},{4,7},{5,6},{6,5},{7,4},{8,11},{9,10},{10,... | collective-permute-start | bytes 98312 | tf_op jit(solution)/shard_map/ppermute | solution.py:455
  29.2 0.0 collective-permute-done.4.near
  29.2 0.0 collective-permute-done.5.far
  29.2 0.8 %chain_maps.1 = (f32[256,256]{1,0:T(8,128)S(1)}, bf16[256,256]{1,0:T(8,128)(2,1)S(1)}, bf16[2,4,256,256]{3,2,1,0:T(8,128)(2,1)S(1)}) custom-call(f32[256,256]{1,0:T(8,128)S(1)} %get-tuple-element.30.own, f32[256,256]{1,0:T(8,128)S(1)} %collective-permute-done.4.near, f32[256,256]{1,0:T(8,128)S(1)} %get-tuple-element.31.across, ...), custom_call_target="tpu_custom_call" | custom-call | flops 1035000000 | tf_op jit(solution)/shard_map/chain_maps/pallas_call | solution.py:264
  30.1 0.0 collective-permute-done.1.near
  30.1 0.0 collective-permute-done.2.across
  30.1 2.1 %collective-permute-done.3.far = bf16[128,128]{1,0:T(8,128)(2,1)S(1)} collective-permute-done((bf16[128,128]{1,0:T(8,128)(2,1)S(1)}, bf16[128,128]{1,0:T(8,128)(2,1)S(1)}, u32[]{:S(2)}, u32[]{:S(2)}) %collective-permute-start.3) | collective-permute-done | bytes 32800 | tf_op jit(solution)/shard_map/ppermute | solution.py:455
  32.3 0.9 %plane_total.1 = (bf16[128,128]{1,0:T(8,128)(2,1)S(1)}, f32[3,256,128]{2,1,0:T(8,128)S(1)}) custom-call(bf16[128,128]{1,0:T(8,128)(2,1)S(1)} %get-tuple-element.26.own, bf16[128,128]{1,0:T(8,128)(2,1)S(1)} %collective-permute-done.1.near, bf16[128,128]{1,0:T(8,128)(2,1)S(1)} %collective-permute-done.2.across, ...), custom_call_target="tpu_custom_call" | custom-call | flops 3449999872 | tf_op jit(solution)/shard_map/plane_total/pallas_call | solution.py:352
  33.2 1.4 %collective-permute-start.6 = (bf16[128,128]{1,0:T(8,128)(2,1)S(1)}, bf16[128,128]{1,0:T(8,128)(2,1)S(1)}, u32[]{:S(2)}, u32[]{:S(2)}) collective-permute-start(bf16[128,128]{1,0:T(8,128)(2,1)S(1)} %get-tuple-element.33._tie.total._total), channel_id=1, source_target_pairs={{0,4},{1,5},{2,6},{3,7},{8,12},{9,13},{10,14},{11,15},{16,20},{17,... | collective-permute-start | bytes 98312 | tf_op jit(solution)/shard_map/ppermute | solution.py:474
  34.6 0.0 copy-done.1
  34.6 1.2 %image.1._image = f32[2,1024,128]{2,1,0:T(8,128)S(1)} custom-call(bf16[2,1024,1024]{2,1,0:T(8,128)(2,1)S(1)} %bitcast.11, bf16[2,1024,128]{2,1,0:T(8,128)(2,1)S(1)} %get-tuple-element.25.source, bf16[128,128]{1,0:T(8,128)(2,1)S(1)} %get-tuple-element.33._tie.total._total), custom_call_target="tpu_custom_call" | custom-call | flops 1380000000 | tf_op jit(solution)/shard_map/image/pallas_call | solution.py:241
  35.9 1.3 %collective-permute-start.9 = (bf16[256,256]{1,0:T(8,128)(2,1)S(1)}, bf16[256,256]{1,0:T(8,128)(2,1)S(1)}, u32[]{:S(2)}, u32[]{:S(2)}) collective-permute-start(bf16[256,256]{1,0:T(8,128)(2,1)S(1)} %get-tuple-element.35), channel_id=1, source_target_pairs={{8,12},{9,13},{10,14},{11,15},{24,28},{25,29},{26,30},{27,31}} | collective-permute-start | bytes 393224 | tf_op jit(solution)/shard_map/ppermute | solution.py:474
  37.2 0.8 %collective-permute-done.6.below = bf16[128,128]{1,0:T(8,128)(2,1)S(1)} collective-permute-done((bf16[128,128]{1,0:T(8,128)(2,1)S(1)}, bf16[128,128]{1,0:T(8,128)(2,1)S(1)}, u32[]{:S(2)}, u32[]{:S(2)}) %collective-permute-start.6) | collective-permute-done | bytes 32800 | tf_op jit(solution)/shard_map/ppermute | solution.py:474
  38.0 0.4 pair_total.1
  38.4 0.7 %collective-permute-start.7 = (bf16[128,128]{1,0:T(8,128)(2,1)S(1)}, bf16[128,128]{1,0:T(8,128)(2,1)S(1)}, u32[]{:S(2)}, u32[]{:S(2)}) collective-permute-start(bf16[128,128]{1,0:T(8,128)(2,1)S(1)} %pair_total.1), channel_id=1, source_target_pairs={{4,8},{5,9},{6,10},{7,11},{20,24},{21,25},{22,26},{23,27}} | collective-permute-start | bytes 98312 | tf_op jit(solution)/shard_map/ppermute | solution.py:474
  39.1 1.3 %collective-permute-start.8 = (bf16[128,128]{1,0:T(8,128)(2,1)S(1)}, bf16[128,128]{1,0:T(8,128)(2,1)S(1)}, u32[]{:S(2)}, u32[]{:S(2)}) collective-permute-start(bf16[128,128]{1,0:T(8,128)(2,1)S(1)} %pair_total.1), channel_id=1, source_target_pairs={{4,12},{5,13},{6,14},{7,15},{20,28},{21,29},{22,30},{23,31}} | collective-permute-start | bytes 98312 | tf_op jit(solution)/shard_map/ppermute | solution.py:474
  40.4 0.7 %maps_upto.1.upto = bf16[2,2,256,256]{3,2,1,0:T(8,128)(2,1)S(1)} custom-call(bf16[2,4,256,256]{3,2,1,0:T(8,128)(2,1)S(1)} %get-tuple-element.32.parts, bf16[128,128]{1,0:T(8,128)(2,1)S(1)} %get-tuple-element.33._tie.total._total), custom_call_target="tpu_custom_call" | custom-call | flops 3449999872 | tf_op jit(solution)/shard_map/maps_upto/pallas_call | solution.py:371
  41.0 0.0 collective-permute-done.7.first
  41.0 4.5 %collective-permute-done.8.second = bf16[128,128]{1,0:T(8,128)(2,1)S(1)} collective-permute-done((bf16[128,128]{1,0:T(8,128)(2,1)S(1)}, bf16[128,128]{1,0:T(8,128)(2,1)S(1)}, u32[]{:S(2)}, u32[]{:S(2)}) %collective-permute-start.8) | collective-permute-done | bytes 32800 | tf_op jit(solution)/shard_map/ppermute | solution.py:474
  45.6 0.0 collective-permute-done.9.got
  45.6 0.9 %entering.1 = (bf16[128,128]{1,0:T(8,128)(2,1)S(1)}, bf16[128,128]{1,0:T(8,128)(2,1)S(1)}, bf16[128,128]{1,0:T(8,128)(2,1)S(1)}, bf16[128,128]{1,0:T(8,128)(2,1)S(1)}) custom-call(f32[2,1024,128]{2,1,0:T(8,128)S(1)} %image.1._image, bf16[128,128]{1,0:T(8,128)(2,1)S(1)} %collective-permute-done.6.below, bf16[128,128]{1,0:T(8,128)(2,1)S(1)} %collective-permute-done.7.first, ...), custom_call_target="tpu_custom_call" | custom-call | flops 1610000000 | tf_op jit(solution)/shard_map/entering/pallas_call | solution.py:412
  46.5 1.8 %collective-permute-start.10 = (bf16[128,128]{1,0:T(8,128)(2,1)S(1)}, bf16[128,128]{1,0:T(8,128)(2,1)S(1)}, u32[]{:S(2)}, u32[]{:S(2)}) collective-permute-start(bf16[128,128]{1,0:T(8,128)(2,1)S(1)} %get-tuple-element.38), channel_id=1, source_target_pairs={{0,1},{1,0},{2,3},{3,2},{4,5},{5,4},{6,7},{7,6},{8,9},{9,8},{10,11... | collective-permute-start | bytes 98312 | tf_op jit(solution)/shard_map/ppermute | solution.py:447
  48.3 0.4 collective-permute-start.11
  48.7 1.3 %collective-permute-start.12 = (bf16[128,128]{1,0:T(8,128)(2,1)S(1)}, bf16[128,128]{1,0:T(8,128)(2,1)S(1)}, u32[]{:S(2)}, u32[]{:S(2)}) collective-permute-start(bf16[128,128]{1,0:T(8,128)(2,1)S(1)} %get-tuple-element.40), channel_id=1, source_target_pairs={{0,3},{1,2},{2,1},{3,0},{4,7},{5,6},{6,5},{7,4},{8,11},{9,10},{10,... | collective-permute-start | bytes 98312 | tf_op jit(solution)/shard_map/ppermute | solution.py:455
  50.0 1.9 %prop.1 = bf16[2,1024,256]{2,1,0:T(8,128)(2,1)S(1)} custom-call(s32[2,8]{1,0:T(2,128)S(1)} %bitcast.18, bf16[2,1024,1024]{2,1,0:T(8,128)(2,1)S(1)} %bitcast.12, bf16[1024,256]{1,0:T(8,128)(2,1)S(1)} %bitcast.16, bf16[128,128]{1,0:T(8,128)(2,1)S(1)} %get-tuple-element.37._tie.own), custom_call_target="tpu_custom_call" | custom-call | flops 1724999936 | tf_op jit(solution)/shard_map/prop/pallas_call | solution.py:225
  51.9 0.0 collective-permute-done.10.near
  51.9 0.0 collective-permute-done.11.across
  52.0 0.4 collective-permute-done.12.far
  52.3 1.3 %waves.1 = bf16[2,1024,128]{2,1,0:T(8,128)(2,1)} custom-call(bf16[128,128]{1,0:T(8,128)(2,1)S(1)} %get-tuple-element.37._tie.own, bf16[128,128]{1,0:T(8,128)(2,1)S(1)} %collective-permute-done.10.near, bf16[128,128]{1,0:T(8,128)(2,1)S(1)} %collective-permute-done.11.across, bf16[128,128]{1,0:T(8,128)(2,1)S(1)} %collective-permute-done.12.far, ...), custom_call_target="tpu_custom_call" | custom-call | flops 1495000064 | tf_op jit(solution)/shard_map/waves/pallas_call | solution.py:436
  (1 shorter events, 0.0 us)
Async XLA Ops:
  0.0 10.9 %copy-start.3 = (bf16[1,1024,256]{2,1,0:T(8,128)(2,1)S(1)}, bf16[1,1024,256]{2,1,0:T(8,128)(2,1)}, u32[]{:S(2)}) copy-start(bf16[1,1024,256]{2,1,0:T(8,128)(2,1)} %param.8) | copy-start | bytes 1572868
  0.0 10.9 %copy-start.4 = (s32[1,8,2]{1,2,0:T(2,128)S(1)}, s32[1,8,2]{1,2,0:T(2,128)}, u32[]{:S(2)}) copy-start(s32[1,8,2]{1,2,0:T(2,128)} %param.9) | copy-start | bytes 196
  4.6 20.1 %copy-start.2 = (bf16[1,2,1024,128]{3,2,1,0:T(8,128)(2,1)S(1)}, bf16[1,2,1024,128]{3,2,1,0:T(8,128)(2,1)}, u32[]{:S(2)}) copy-start(bf16[1,2,1024,128]{3,2,1,0:T(8,128)(2,1)} %param.7) | copy-start | bytes 1572868
  4.6 20.1 %all-to-all-start = ((bf16[16,136,128]{2,1,0:T(8,128)(2,1)}), bf16[16,136,128]{2,1,0:T(8,128)(2,1)S(1)}, u32[]{:S(2)}, u32[]{:S(2)}) async-start(bf16[16,136,128]{2,1,0:T(8,128)(2,1)} %pairs.1), calls=%async_computation | async-start | bytes 1114112 | tf_op jit(solution)/shard_map/all_to_all | solution.py:497
  10.9 2.2 %copy-start = (bf16[1,2,1024,1024]{3,2,1,0:T(8,128)(2,1)S(1)}, bf16[1,2,1024,1024]{3,2,1,0:T(8,128)(2,1)}, u32[]{:S(2)}) copy-start(bf16[1,2,1024,1024]{3,2,1,0:T(8,128)(2,1)} %param.6) | copy-start | bytes 12582916
  14.2 10.5 %collective-permute-start = (f32[256,256]{1,0:T(8,128)S(1)}, f32[256,256]{1,0:T(8,128)S(1)}, u32[]{:S(2)}, u32[]{:S(2)}) collective-permute-start(f32[256,256]{1,0:T(8,128)S(1)} %get-tuple-element.24), channel_id=1, source_target_pairs={{0,2},{1,3},{2,0},{3,1},{4,6},{5,7},{6,4},{7,5},{8,10},{9,11},{10,... | collective-permute-start | bytes 786440 | tf_op jit(solution)/shard_map/ppermute | solution.py:451
  15.5 13.8 %collective-permute-start.4 = (f32[256,256]{1,0:T(8,128)S(1)}, f32[256,256]{1,0:T(8,128)S(1)}, u32[]{:S(2)}, u32[]{:S(2)}) collective-permute-start(f32[256,256]{1,0:T(8,128)S(1)} %get-tuple-element.30.own), channel_id=1, source_target_pairs={{0,1},{1,0},{2,3},{3,2},{4,5},{5,4},{6,7},{7,6},{8,9},{9,8},{10,11... | collective-permute-start | bytes 786440 | tf_op jit(solution)/shard_map/ppermute | solution.py:447
  26.1 3.1 %collective-permute-start.5 = (f32[256,256]{1,0:T(8,128)S(1)}, f32[256,256]{1,0:T(8,128)S(1)}, u32[]{:S(2)}, u32[]{:S(2)}) collective-permute-start(f32[256,256]{1,0:T(8,128)S(1)} %get-tuple-element.31.across), channel_id=1, source_target_pairs={{0,1},{1,0},{2,3},{3,2},{4,5},{5,4},{6,7},{7,6},{8,9},{9,8},{10,11... | collective-permute-start | bytes 786440 | tf_op jit(solution)/shard_map/ppermute | solution.py:447
  27.1 3.0 %collective-permute-start.1 = (bf16[128,128]{1,0:T(8,128)(2,1)S(1)}, bf16[128,128]{1,0:T(8,128)(2,1)S(1)}, u32[]{:S(2)}, u32[]{:S(2)}) collective-permute-start(bf16[128,128]{1,0:T(8,128)(2,1)S(1)} %get-tuple-element.27), channel_id=1, source_target_pairs={{0,1},{1,0},{2,3},{3,2},{4,5},{5,4},{6,7},{7,6},{8,9},{9,8},{10,11... | collective-permute-start | bytes 98312 | tf_op jit(solution)/shard_map/ppermute | solution.py:447
  27.2 2.9 %collective-permute-start.2 = (bf16[128,128]{1,0:T(8,128)(2,1)S(1)}, bf16[128,128]{1,0:T(8,128)(2,1)S(1)}, u32[]{:S(2)}, u32[]{:S(2)}) collective-permute-start(bf16[128,128]{1,0:T(8,128)(2,1)S(1)} %get-tuple-element.28), channel_id=1, source_target_pairs={{0,2},{1,3},{2,0},{3,1},{4,6},{5,7},{6,4},{7,5},{8,10},{9,11},{10,... | collective-permute-start | bytes 98312 | tf_op jit(solution)/shard_map/ppermute | solution.py:451
  28.3 4.0 %collective-permute-start.3 = (bf16[128,128]{1,0:T(8,128)(2,1)S(1)}, bf16[128,128]{1,0:T(8,128)(2,1)S(1)}, u32[]{:S(2)}, u32[]{:S(2)}) collective-permute-start(bf16[128,128]{1,0:T(8,128)(2,1)S(1)} %get-tuple-element.29), channel_id=1, source_target_pairs={{0,3},{1,2},{2,1},{3,0},{4,7},{5,6},{6,5},{7,4},{8,11},{9,10},{10,... | collective-permute-start | bytes 98312 | tf_op jit(solution)/shard_map/ppermute | solution.py:455
  32.3 2.4 %copy-start.1 = (bf16[1,2,1024,1024]{3,2,1,0:T(8,128)(2,1)S(1)}, bf16[1,2,1024,1024]{3,2,1,0:T(8,128)(2,1)}, u32[]{:S(2)}) copy-start(bf16[1,2,1024,1024]{3,2,1,0:T(8,128)(2,1)} %param.6) | copy-start | bytes 12582916
  33.2 4.8 %collective-permute-start.6 = (bf16[128,128]{1,0:T(8,128)(2,1)S(1)}, bf16[128,128]{1,0:T(8,128)(2,1)S(1)}, u32[]{:S(2)}, u32[]{:S(2)}) collective-permute-start(bf16[128,128]{1,0:T(8,128)(2,1)S(1)} %get-tuple-element.33._tie.total._total), channel_id=1, source_target_pairs={{0,4},{1,5},{2,6},{3,7},{8,12},{9,13},{10,14},{11,15},{16,20},{17,... | collective-permute-start | bytes 98312 | tf_op jit(solution)/shard_map/ppermute | solution.py:474
  35.9 9.7 %collective-permute-start.9 = (bf16[256,256]{1,0:T(8,128)(2,1)S(1)}, bf16[256,256]{1,0:T(8,128)(2,1)S(1)}, u32[]{:S(2)}, u32[]{:S(2)}) collective-permute-start(bf16[256,256]{1,0:T(8,128)(2,1)S(1)} %get-tuple-element.35), channel_id=1, source_target_pairs={{8,12},{9,13},{10,14},{11,15},{24,28},{25,29},{26,30},{27,31}} | collective-permute-start | bytes 393224 | tf_op jit(solution)/shard_map/ppermute | solution.py:474
  38.4 2.7 %collective-permute-start.7 = (bf16[128,128]{1,0:T(8,128)(2,1)S(1)}, bf16[128,128]{1,0:T(8,128)(2,1)S(1)}, u32[]{:S(2)}, u32[]{:S(2)}) collective-permute-start(bf16[128,128]{1,0:T(8,128)(2,1)S(1)} %pair_total.1), channel_id=1, source_target_pairs={{4,8},{5,9},{6,10},{7,11},{20,24},{21,25},{22,26},{23,27}} | collective-permute-start | bytes 98312 | tf_op jit(solution)/shard_map/ppermute | solution.py:474
  39.1 6.5 %collective-permute-start.8 = (bf16[128,128]{1,0:T(8,128)(2,1)S(1)}, bf16[128,128]{1,0:T(8,128)(2,1)S(1)}, u32[]{:S(2)}, u32[]{:S(2)}) collective-permute-start(bf16[128,128]{1,0:T(8,128)(2,1)S(1)} %pair_total.1), channel_id=1, source_target_pairs={{4,12},{5,13},{6,14},{7,15},{20,28},{21,29},{22,30},{23,31}} | collective-permute-start | bytes 98312 | tf_op jit(solution)/shard_map/ppermute | solution.py:474
  46.5 5.5 %collective-permute-start.10 = (bf16[128,128]{1,0:T(8,128)(2,1)S(1)}, bf16[128,128]{1,0:T(8,128)(2,1)S(1)}, u32[]{:S(2)}, u32[]{:S(2)}) collective-permute-start(bf16[128,128]{1,0:T(8,128)(2,1)S(1)} %get-tuple-element.38), channel_id=1, source_target_pairs={{0,1},{1,0},{2,3},{3,2},{4,5},{5,4},{6,7},{7,6},{8,9},{9,8},{10,11... | collective-permute-start | bytes 98312 | tf_op jit(solution)/shard_map/ppermute | solution.py:447
  48.3 3.7 %collective-permute-start.11 = (bf16[128,128]{1,0:T(8,128)(2,1)S(1)}, bf16[128,128]{1,0:T(8,128)(2,1)S(1)}, u32[]{:S(2)}, u32[]{:S(2)}) collective-permute-start(bf16[128,128]{1,0:T(8,128)(2,1)S(1)} %get-tuple-element.39), channel_id=1, source_target_pairs={{0,2},{1,3},{2,0},{3,1},{4,6},{5,7},{6,4},{7,5},{8,10},{9,11},{10,... | collective-permute-start | bytes 98312 | tf_op jit(solution)/shard_map/ppermute | solution.py:451
  48.7 3.6 %collective-permute-start.12 = (bf16[128,128]{1,0:T(8,128)(2,1)S(1)}, bf16[128,128]{1,0:T(8,128)(2,1)S(1)}, u32[]{:S(2)}, u32[]{:S(2)}) collective-permute-start(bf16[128,128]{1,0:T(8,128)(2,1)S(1)} %get-tuple-element.40), channel_id=1, source_target_pairs={{0,3},{1,2},{2,1},{3,0},{4,7},{5,6},{6,5},{7,4},{8,11},{9,10},{10,... | collective-permute-start | bytes 98312 | tf_op jit(solution)/shard_map/ppermute | solution.py:455

commit v16 on v15

--- a/solution.py
+++ b/solution.py
@@ -386,15 +386,15 @@
         ref[...] = work[at].astype(BF16)
 
 
-def pair_kernel(total, below, whole, _image, out):
+def pair_kernel(total, below, whole, _image, _upto, out):
     state = unpack(total[...].astype(F32)) + times(two_parts(whole[...]), two_parts(unpack(below[...].astype(F32))))
     out[...] = pack(state).astype(BF16)
 
 
-def pair_total(total, below, whole, tie):
-    return call(
-        pair_kernel, "pair_total", [IN_VMEM] * 3 + [IN_PLACE], shape(*total.shape), [], 0.5
-    )(total, below, whole, tie)
+def pair_total(total, below, whole, *ties):
+    return call(
+        pair_kernel, "pair_total", [IN_VMEM] * 3 + [IN_PLACE] * 2, shape(*total.shape), [], 0.5
+    )(total, below, whole, *ties)
 
 
 def entering_kernel(_image, below, first, second, got, parts, upto, local, *out):
@@ -510,9 +510,9 @@
     upto = maps_upto(parts, total)
     image = images(green, source, total)
     if four:
-        below = between(total, (0, 1), (2, 3))
-        pair = pair_total(total, below, whole, image)
-        first, second = between(pair, (1, 2)), between(pair, (1, 3))
+        below = between(total, (0, 1))
+        pair = pair_total(total, below, whole, image, upto)
+        first, second = between(pair, (1, 2), (2, 3)), between(pair, (1, 3))
         entered = entering(entering_kernel, image, (below, first, second, got, parts, upto, local))
     else:
         base = scan_below(whole, total, sections)

time: 54 us -> 53.5 us (level)
  the two profiles are of different devices: /device:TPU:25 before, /device:TPU:21 now
where the time goes in v16:
time: 53.5 us; the launch traced here: 53.1 us
  starting transfers between devices  21.4 us (40%)
  Pallas kernels  15.1 us (28%)
  waiting for transfers between devices  14.2 us (27%)
  local copies, waits for them, and re-layouts  2.2 us (4%)
    ppermute x3, waiting for transfers between devices, to_across(): lax.ppermute(item, 'sec', [(s, s // GROUP * GROUP + (s % GROUP + CORES) %...  9.03 us
    all_to_all x1, starting transfers between devices, per_device(): lax.all_to_all(outgoing, 'sec', split_axis=0, concat_axis=0, tiled=True)  6.61 us
    ppermute x4, starting transfers between devices, between(): return lax.ppermute(item, 'sec', pairs)  5.8 us
    pallas_call x1, Pallas kernels, outgoing_pairs(): call(pairs_kernel, 'pairs', [IN_HBM] * 4, shape(sections, CAP * energies...  4.37 us
    ppermute x4, starting transfers between devices, to_near(): return lax.ppermute(item, 'sec', [(s, s ^ 1) for s in range(sections)])  3.95 us
    ppermute x4, waiting for transfers between devices, between(): return lax.ppermute(item, 'sec', pairs)  2.73 us
    ppermute x3, starting transfers between devices, to_across(): lax.ppermute(item, 'sec', [(s, s // GROUP * GROUP + (s % GROUP + CORES) %...  2.64 us
    ppermute x2, waiting for transfers between devices, to_far(): lax.ppermute(item, 'sec', [(s, s // GROUP * GROUP + (s % GROUP + CORES) %...  2.39 us
  transfers between devices with their start and end apart: 14, of which 4 were waited for; matrix products, arithmetic and copies ran while one was open for 0% of the time, Pallas kernels for 14%

profile of v16, /device:TPU:21, one launch (start us, length us, event | category | flops | bytes accessed | tf_op | source)
XLA Modules:
  0.0 53.1 jit_solution(5587765589947372948)
XLA Ops:
  0.0 0.0 copy-start.3
  0.0 4.4 %pairs.1 = bf16[16,136,128]{2,1,0:T(8,128)(2,1)} custom-call(s32[16]{0:T(128)} %bitcast.20, s32[2,16]{1,0:T(2,128)} %bitcast.19, bf16[2,1024,1024]{2,1,0:T(8,128)(2,1)} %bitcast.9, bf16[2,1024,128]{2,1,0:T(8,128)(2,1)} %bitcast.13), custom_call_target="tpu_custom_call" | custom-call | flops 4600000000 | tf_op jit(solution)/shard_map/pairs/pallas_call | solution.py:168
  4.4 0.0 copy-start.2
  4.4 6.6 %all-to-all-start = ((bf16[16,136,128]{2,1,0:T(8,128)(2,1)}), bf16[16,136,128]{2,1,0:T(8,128)(2,1)S(1)}, u32[]{:S(2)}, u32[]{:S(2)}) async-start(bf16[16,136,128]{2,1,0:T(8,128)(2,1)} %pairs.1), calls=%async_computation | async-start | bytes 1114112 | tf_op jit(solution)/shard_map/all_to_all | solution.py:497
  11.0 0.0 copy-done.3
  11.0 0.0 copy-done.4
  11.0 0.0 copy-start
  11.0 2.2 %copy-done = bf16[1,2,1024,1024]{3,2,1,0:T(8,128)(2,1)S(1)} copy-done((bf16[1,2,1024,1024]{3,2,1,0:T(8,128)(2,1)S(1)}, bf16[1,2,1024,1024]{3,2,1,0:T(8,128)(2,1)}, u32[]{:S(2)}) %copy-start) | copy-done | bytes 4194328
  13.2 1.1 %face_maps.1 = (f32[256,256]{1,0:T(8,128)S(1)}, f32[256,256]{1,0:T(8,128)S(1)}, bf16[2,256,1024]{2,1,0:T(8,128)(2,1)S(1)}) custom-call(s32[2,8]{1,0:T(2,128)S(1)} %bitcast.17, bf16[2,1024,1024]{2,1,0:T(8,128)(2,1)S(1)} %bitcast.10, bf16[1024,256]{1,0:T(8,128)(2,1)S(1)} %bitcast.15), custom_call_target="tpu_custom_call" | custom-call | flops 1380000000 | tf_op jit(solution)/shard_map/face_maps/pallas_call | solution.py:206
  14.3 1.2 %collective-permute-start = (f32[256,256]{1,0:T(8,128)S(1)}, f32[256,256]{1,0:T(8,128)S(1)}, u32[]{:S(2)}, u32[]{:S(2)}) collective-permute-start(f32[256,256]{1,0:T(8,128)S(1)} %get-tuple-element.24), channel_id=1, source_target_pairs={{0,2},{1,3},{2,0},{3,1},{4,6},{5,7},{6,4},{7,5},{8,10},{9,11},{10,... | collective-permute-start | bytes 786440 | tf_op jit(solution)/shard_map/ppermute | solution.py:451
  15.6 0.6 %collective-permute-start.4 = (f32[256,256]{1,0:T(8,128)S(1)}, f32[256,256]{1,0:T(8,128)S(1)}, u32[]{:S(2)}, u32[]{:S(2)}) collective-permute-start(f32[256,256]{1,0:T(8,128)S(1)} %get-tuple-element.30.own), channel_id=1, source_target_pairs={{0,1},{1,0},{2,3},{3,2},{4,5},{5,4},{6,7},{7,6},{8,9},{9,8},{10,11... | collective-permute-start | bytes 786440 | tf_op jit(solution)/shard_map/ppermute | solution.py:447
  16.2 9.0 %collective-permute-done._map = f32[256,256]{1,0:T(8,128)S(1)} collective-permute-done((f32[256,256]{1,0:T(8,128)S(1)}, f32[256,256]{1,0:T(8,128)S(1)}, u32[]{:S(2)}, u32[]{:S(2)}) %collective-permute-start) | collective-permute-done | bytes 262176 | tf_op jit(solution)/shard_map/ppermute | solution.py:451
  25.3 0.0 all-to-all-done.received
  25.3 0.0 copy-done.2
  25.3 1.4 %source_and_face.1 = (bf16[2,1024,128]{2,1,0:T(8,128)(2,1)S(1)}, bf16[128,128]{1,0:T(8,128)(2,1)S(1)}, bf16[128,128]{1,0:T(8,128)(2,1)S(1)}, bf16[128,128]{1,0:T...) custom-call(bf16[16,136,128]{2,1,0:T(8,128)(2,1)S(1)} %all-to-all-done.rec, ...), custom_call_target="tpu_custom_call", output_to_operand_aliasing={{5}: (3, {})} | custom-call | flops 1610000000 | tf_op jit(solution)/shard_map/source_and_face/pallas_call | solution.py:315
  26.7 1.3 %collective-permute-start.5 = (f32[256,256]{1,0:T(8,128)S(1)}, f32[256,256]{1,0:T(8,128)S(1)}, u32[]{:S(2)}, u32[]{:S(2)}) collective-permute-start(f32[256,256]{1,0:T(8,128)S(1)} %get-tuple-element.31.across), channel_id=1, source_target_pairs={{0,1},{1,0},{2,3},{3,2},{4,5},{5,4},{6,7},{7,6},{8,9},{9,8},{10,11... | collective-permute-start | bytes 786440 | tf_op jit(solution)/shard_map/ppermute | solution.py:447
  28.0 0.1 collective-permute-start.1
  28.1 1.0 %collective-permute-start.2 = (bf16[128,128]{1,0:T(8,128)(2,1)S(1)}, bf16[128,128]{1,0:T(8,128)(2,1)S(1)}, u32[]{:S(2)}, u32[]{:S(2)}) collective-permute-start(bf16[128,128]{1,0:T(8,128)(2,1)S(1)} %get-tuple-element.28), channel_id=1, source_target_pairs={{0,2},{1,3},{2,0},{3,1},{4,6},{5,7},{6,4},{7,5},{8,10},{9,11},{10,... | collective-permute-start | bytes 98312 | tf_op jit(solution)/shard_map/ppermute | solution.py:451
  29.1 1.1 %collective-permute-start.3 = (bf16[128,128]{1,0:T(8,128)(2,1)S(1)}, bf16[128,128]{1,0:T(8,128)(2,1)S(1)}, u32[]{:S(2)}, u32[]{:S(2)}) collective-permute-start(bf16[128,128]{1,0:T(8,128)(2,1)S(1)} %get-tuple-element.29), channel_id=1, source_target_pairs={{0,3},{1,2},{2,1},{3,0},{4,7},{5,6},{6,5},{7,4},{8,11},{9,10},{10,... | collective-permute-start | bytes 98312 | tf_op jit(solution)/shard_map/ppermute | solution.py:455
  30.1 0.0 collective-permute-done.4.near
  30.1 0.0 collective-permute-done.5.far
  30.1 0.8 %chain_maps.1 = (f32[256,256]{1,0:T(8,128)S(1)}, bf16[256,256]{1,0:T(8,128)(2,1)S(1)}, bf16[2,4,256,256]{3,2,1,0:T(8,128)(2,1)S(1)}) custom-call(f32[256,256]{1,0:T(8,128)S(1)} %get-tuple-element.30.own, f32[256,256]{1,0:T(8,128)S(1)} %collective-permute-done.4.near, f32[256,256]{1,0:T(8,128)S(1)} %get-tuple-element.31.across, ...), custom_call_target="tpu_custom_call" | custom-call | flops 1035000000 | tf_op jit(solution)/shard_map/chain_maps/pallas_call | solution.py:264
  31.0 0.0 collective-permute-done.1.near
  31.0 0.0 collective-permute-done.2.across
  31.0 2.0 %collective-permute-done.3.far = bf16[128,128]{1,0:T(8,128)(2,1)S(1)} collective-permute-done((bf16[128,128]{1,0:T(8,128)(2,1)S(1)}, bf16[128,128]{1,0:T(8,128)(2,1)S(1)}, u32[]{:S(2)}, u32[]{:S(2)}) %collective-permute-start.3) | collective-permute-done | bytes 32800 | tf_op jit(solution)/shard_map/ppermute | solution.py:455
  33.0 0.9 %plane_total.1 = (bf16[128,128]{1,0:T(8,128)(2,1)S(1)}, f32[3,256,128]{2,1,0:T(8,128)S(1)}) custom-call(bf16[128,128]{1,0:T(8,128)(2,1)S(1)} %get-tuple-element.26.own, bf16[128,128]{1,0:T(8,128)(2,1)S(1)} %collective-permute-done.1.near, bf16[128,128]{1,0:T(8,128)(2,1)S(1)} %collective-permute-done.2.across, ...), custom_call_target="tpu_custom_call" | custom-call | flops 3449999872 | tf_op jit(solution)/shard_map/plane_total/pallas_call | solution.py:352
  34.0 0.0 copy-start.1
  34.0 0.8 %collective-permute-start.6 = (bf16[128,128]{1,0:T(8,128)(2,1)S(1)}, bf16[128,128]{1,0:T(8,128)(2,1)S(1)}, u32[]{:S(2)}, u32[]{:S(2)}) collective-permute-start(bf16[128,128]{1,0:T(8,128)(2,1)S(1)} %get-tuple-element.33._tie._total.total), channel_id=1, source_target_pairs={{0,4},{1,5},{2,6},{3,7},{16,20},{17,21},{18,22},{19,23}} | collective-permute-start | bytes 98312 | tf_op jit(solution)/shard_map/ppermute | solution.py:474
  34.8 0.7 %maps_upto.1._upto.upto = bf16[2,2,256,256]{3,2,1,0:T(8,128)(2,1)S(1)} custom-call(bf16[2,4,256,256]{3,2,1,0:T(8,128)(2,1)S(1)} %get-tuple-element.32.parts, bf16[128,128]{1,0:T(8,128)(2,1)S(1)} %get-tuple-element.33._tie._total.total), custom_call_target="tpu_custom_call" | custom-call | flops 3449999872 | tf_op jit(solution)/shard_map/maps_upto/pallas_call | solution.py:371
  35.5 2.4 %collective-permute-start.9 = (bf16[256,256]{1,0:T(8,128)(2,1)S(1)}, bf16[256,256]{1,0:T(8,128)(2,1)S(1)}, u32[]{:S(2)}, u32[]{:S(2)}) collective-permute-start(bf16[256,256]{1,0:T(8,128)(2,1)S(1)} %get-tuple-element.35), channel_id=1, source_target_pairs={{8,12},{9,13},{10,14},{11,15},{24,28},{25,29},{26,30},{27,31}} | collective-permute-start | bytes 393224 | tf_op jit(solution)/shard_map/ppermute | solution.py:474
  37.9 0.0 copy-done.1
  37.9 1.2 %image.1._image = f32[2,1024,128]{2,1,0:T(8,128)S(1)} custom-call(bf16[2,1024,1024]{2,1,0:T(8,128)(2,1)S(1)} %bitcast.11, bf16[2,1024,128]{2,1,0:T(8,128)(2,1)S(1)} %get-tuple-element.25.source, bf16[128,128]{1,0:T(8,128)(2,1)S(1)} %get-tuple-element.33._tie._total.total), custom_call_target="tpu_custom_call" | custom-call | flops 1380000000 | tf_op jit(solution)/shard_map/image/pallas_call | solution.py:241
  39.2 0.0 collective-permute-done.6.below
  39.2 0.4 pair_total.1
  39.6 0.7 %collective-permute-start.8 = (bf16[128,128]{1,0:T(8,128)(2,1)S(1)}, bf16[128,128]{1,0:T(8,128)(2,1)S(1)}, u32[]{:S(2)}, u32[]{:S(2)}) collective-permute-start(bf16[128,128]{1,0:T(8,128)(2,1)S(1)} %pair_total.1), channel_id=1, source_target_pairs={{4,12},{5,13},{6,14},{7,15},{20,28},{21,29},{22,30},{23,31}} | collective-permute-start | bytes 98312 | tf_op jit(solution)/shard_map/ppermute | solution.py:474
  40.2 1.9 %collective-permute-start.7 = (bf16[128,128]{1,0:T(8,128)(2,1)S(1)}, bf16[128,128]{1,0:T(8,128)(2,1)S(1)}, u32[]{:S(2)}, u32[]{:S(2)}) collective-permute-start(bf16[128,128]{1,0:T(8,128)(2,1)S(1)} %pair_total.1), channel_id=1, source_target_pairs={{4,8},{5,9},{6,10},{7,11},{8,12},{9,13},{10,14},{11,15},{20,24},{2... | collective-permute-start | bytes 98312 | tf_op jit(solution)/shard_map/ppermute | solution.py:474
  42.2 0.0 collective-permute-done.8.second
  42.2 2.7 %collective-permute-done.7.first = bf16[128,128]{1,0:T(8,128)(2,1)S(1)} collective-permute-done((bf16[128,128]{1,0:T(8,128)(2,1)S(1)}, bf16[128,128]{1,0:T(8,128)(2,1)S(1)}, u32[]{:S(2)}, u32[]{:S(2)}) %collective-permute-start.7) | collective-permute-done | bytes 32800 | tf_op jit(solution)/shard_map/ppermute | solution.py:474
  44.9 0.0 collective-permute-done.9.got
  44.9 0.9 %entering.1 = (bf16[128,128]{1,0:T(8,128)(2,1)S(1)}, bf16[128,128]{1,0:T(8,128)(2,1)S(1)}, bf16[128,128]{1,0:T(8,128)(2,1)S(1)}, bf16[128,128]{1,0:T(8,128)(2,1)S(1)}) custom-call(f32[2,1024,128]{2,1,0:T(8,128)S(1)} %image.1._image, bf16[128,128]{1,0:T(8,128)(2,1)S(1)} %collective-permute-done.6.below, bf16[128,128]{1,0:T(8,128)(2,1)S(1)} %collective-permute-done.7.first, ...), custom_call_target="tpu_custom_call" | custom-call | flops 1610000000 | tf_op jit(solution)/shard_map/entering/pallas_call | solution.py:412
  45.8 1.9 %collective-permute-start.10 = (bf16[128,128]{1,0:T(8,128)(2,1)S(1)}, bf16[128,128]{1,0:T(8,128)(2,1)S(1)}, u32[]{:S(2)}, u32[]{:S(2)}) collective-permute-start(bf16[128,128]{1,0:T(8,128)(2,1)S(1)} %get-tuple-element.38), channel_id=1, source_target_pairs={{0,1},{1,0},{2,3},{3,2},{4,5},{5,4},{6,7},{7,6},{8,9},{9,8},{10,11... | collective-permute-start | bytes 98312 | tf_op jit(solution)/shard_map/ppermute | solution.py:447
  47.7 0.4 collective-permute-start.11
  48.1 1.3 %collective-permute-start.12 = (bf16[128,128]{1,0:T(8,128)(2,1)S(1)}, bf16[128,128]{1,0:T(8,128)(2,1)S(1)}, u32[]{:S(2)}, u32[]{:S(2)}) collective-permute-start(bf16[128,128]{1,0:T(8,128)(2,1)S(1)} %get-tuple-element.40), channel_id=1, source_target_pairs={{0,3},{1,2},{2,1},{3,0},{4,7},{5,6},{6,5},{7,4},{8,11},{9,10},{10,... | collective-permute-start | bytes 98312 | tf_op jit(solution)/shard_map/ppermute | solution.py:455
  49.4 1.9 %prop.1 = bf16[2,1024,256]{2,1,0:T(8,128)(2,1)S(1)} custom-call(s32[2,8]{1,0:T(2,128)S(1)} %bitcast.18, bf16[2,1024,1024]{2,1,0:T(8,128)(2,1)S(1)} %bitcast.12, bf16[1024,256]{1,0:T(8,128)(2,1)S(1)} %bitcast.16, bf16[128,128]{1,0:T(8,128)(2,1)S(1)} %get-tuple-element.37._tie.own), custom_call_target="tpu_custom_call" | custom-call | flops 1724999936 | tf_op jit(solution)/shard_map/prop/pallas_call | solution.py:225
  51.4 0.0 collective-permute-done.10.near
  51.4 0.0 collective-permute-done.11.across
  51.4 0.4 collective-permute-done.12.far
  51.7 1.3 %waves.1 = bf16[2,1024,128]{2,1,0:T(8,128)(2,1)} custom-call(bf16[128,128]{1,0:T(8,128)(2,1)S(1)} %get-tuple-element.37._tie.own, bf16[128,128]{1,0:T(8,128)(2,1)S(1)} %collective-permute-done.10.near, bf16[128,128]{1,0:T(8,128)(2,1)S(1)} %collective-permute-done.11.across, bf16[128,128]{1,0:T(8,128)(2,1)S(1)} %collective-permute-done.12.far, ...), custom_call_target="tpu_custom_call" | custom-call | flops 1495000064 | tf_op jit(solution)/shard_map/waves/pallas_call | solution.py:436
  (1 shorter events, 0.0 us)
Async XLA Ops:
  0.0 11.0 %copy-start.3 = (bf16[1,1024,256]{2,1,0:T(8,128)(2,1)S(1)}, bf16[1,1024,256]{2,1,0:T(8,128)(2,1)}, u32[]{:S(2)}) copy-start(bf16[1,1024,256]{2,1,0:T(8,128)(2,1)} %param.8) | copy-start | bytes 1572868
  0.0 11.0 %copy-start.4 = (s32[1,8,2]{1,2,0:T(2,128)S(1)}, s32[1,8,2]{1,2,0:T(2,128)}, u32[]{:S(2)}) copy-start(s32[1,8,2]{1,2,0:T(2,128)} %param.9) | copy-start | bytes 196
  4.4 20.9 %copy-start.2 = (bf16[1,2,1024,128]{3,2,1,0:T(8,128)(2,1)S(1)}, bf16[1,2,1024,128]{3,2,1,0:T(8,128)(2,1)}, u32[]{:S(2)}) copy-start(bf16[1,2,1024,128]{3,2,1,0:T(8,128)(2,1)} %param.7) | copy-start | bytes 1572868
  4.4 20.9 %all-to-all-start = ((bf16[16,136,128]{2,1,0:T(8,128)(2,1)}), bf16[16,136,128]{2,1,0:T(8,128)(2,1)S(1)}, u32[]{:S(2)}, u32[]{:S(2)}) async-start(bf16[16,136,128]{2,1,0:T(8,128)(2,1)} %pairs.1), calls=%async_computation | async-start | bytes 1114112 | tf_op jit(solution)/shard_map/all_to_all | solution.py:497
  11.0 2.2 %copy-start = (bf16[1,2,1024,1024]{3,2,1,0:T(8,128)(2,1)S(1)}, bf16[1,2,1024,1024]{3,2,1,0:T(8,128)(2,1)}, u32[]{:S(2)}) copy-start(bf16[1,2,1024,1024]{3,2,1,0:T(8,128)(2,1)} %param.6) | copy-start | bytes 12582916
  14.3 10.9 %collective-permute-start = (f32[256,256]{1,0:T(8,128)S(1)}, f32[256,256]{1,0:T(8,128)S(1)}, u32[]{:S(2)}, u32[]{:S(2)}) collective-permute-start(f32[256,256]{1,0:T(8,128)S(1)} %get-tuple-element.24), channel_id=1, source_target_pairs={{0,2},{1,3},{2,0},{3,1},{4,6},{5,7},{6,4},{7,5},{8,10},{9,11},{10,... | collective-permute-start | bytes 786440 | tf_op jit(solution)/shard_map/ppermute | solution.py:451
  15.6 14.5 %collective-permute-start.4 = (f32[256,256]{1,0:T(8,128)S(1)}, f32[256,256]{1,0:T(8,128)S(1)}, u32[]{:S(2)}, u32[]{:S(2)}) collective-permute-start(f32[256,256]{1,0:T(8,128)S(1)} %get-tuple-element.30.own), channel_id=1, source_target_pairs={{0,1},{1,0},{2,3},{3,2},{4,5},{5,4},{6,7},{7,6},{8,9},{9,8},{10,11... | collective-permute-start | bytes 786440 | tf_op jit(solution)/shard_map/ppermute | solution.py:447
  26.7 3.5 %collective-permute-start.5 = (f32[256,256]{1,0:T(8,128)S(1)}, f32[256,256]{1,0:T(8,128)S(1)}, u32[]{:S(2)}, u32[]{:S(2)}) collective-permute-start(f32[256,256]{1,0:T(8,128)S(1)} %get-tuple-element.31.across), channel_id=1, source_target_pairs={{0,1},{1,0},{2,3},{3,2},{4,5},{5,4},{6,7},{7,6},{8,9},{9,8},{10,11... | collective-permute-start | bytes 786440 | tf_op jit(solution)/shard_map/ppermute | solution.py:447
  28.0 3.0 %collective-permute-start.1 = (bf16[128,128]{1,0:T(8,128)(2,1)S(1)}, bf16[128,128]{1,0:T(8,128)(2,1)S(1)}, u32[]{:S(2)}, u32[]{:S(2)}) collective-permute-start(bf16[128,128]{1,0:T(8,128)(2,1)S(1)} %get-tuple-element.27), channel_id=1, source_target_pairs={{0,1},{1,0},{2,3},{3,2},{4,5},{5,4},{6,7},{7,6},{8,9},{9,8},{10,11... | collective-permute-start | bytes 98312 | tf_op jit(solution)/shard_map/ppermute | solution.py:447
  28.1 2.9 %collective-permute-start.2 = (bf16[128,128]{1,0:T(8,128)(2,1)S(1)}, bf16[128,128]{1,0:T(8,128)(2,1)S(1)}, u32[]{:S(2)}, u32[]{:S(2)}) collective-permute-start(bf16[128,128]{1,0:T(8,128)(2,1)S(1)} %get-tuple-element.28), channel_id=1, source_target_pairs={{0,2},{1,3},{2,0},{3,1},{4,6},{5,7},{6,4},{7,5},{8,10},{9,11},{10,... | collective-permute-start | bytes 98312 | tf_op jit(solution)/shard_map/ppermute | solution.py:451
  29.1 4.0 %collective-permute-start.3 = (bf16[128,128]{1,0:T(8,128)(2,1)S(1)}, bf16[128,128]{1,0:T(8,128)(2,1)S(1)}, u32[]{:S(2)}, u32[]{:S(2)}) collective-permute-start(bf16[128,128]{1,0:T(8,128)(2,1)S(1)} %get-tuple-element.29), channel_id=1, source_target_pairs={{0,3},{1,2},{2,1},{3,0},{4,7},{5,6},{6,5},{7,4},{8,11},{9,10},{10,... | collective-permute-start | bytes 98312 | tf_op jit(solution)/shard_map/ppermute | solution.py:455
  34.0 3.9 %copy-start.1 = (bf16[1,2,1024,1024]{3,2,1,0:T(8,128)(2,1)S(1)}, bf16[1,2,1024,1024]{3,2,1,0:T(8,128)(2,1)}, u32[]{:S(2)}) copy-start(bf16[1,2,1024,1024]{3,2,1,0:T(8,128)(2,1)} %param.6) | copy-start | bytes 12582916
  34.0 5.2 %collective-permute-start.6 = (bf16[128,128]{1,0:T(8,128)(2,1)S(1)}, bf16[128,128]{1,0:T(8,128)(2,1)S(1)}, u32[]{:S(2)}, u32[]{:S(2)}) collective-permute-start(bf16[128,128]{1,0:T(8,128)(2,1)S(1)} %get-tuple-element.33._tie._total.total), channel_id=1, source_target_pairs={{0,4},{1,5},{2,6},{3,7},{16,20},{17,21},{18,22},{19,23}} | collective-permute-start | bytes 98312 | tf_op jit(solution)/shard_map/ppermute | solution.py:474
  35.5 9.4 %collective-permute-start.9 = (bf16[256,256]{1,0:T(8,128)(2,1)S(1)}, bf16[256,256]{1,0:T(8,128)(2,1)S(1)}, u32[]{:S(2)}, u32[]{:S(2)}) collective-permute-start(bf16[256,256]{1,0:T(8,128)(2,1)S(1)} %get-tuple-element.35), channel_id=1, source_target_pairs={{8,12},{9,13},{10,14},{11,15},{24,28},{25,29},{26,30},{27,31}} | collective-permute-start | bytes 393224 | tf_op jit(solution)/shard_map/ppermute | solution.py:474
  39.6 2.6 %collective-permute-start.8 = (bf16[128,128]{1,0:T(8,128)(2,1)S(1)}, bf16[128,128]{1,0:T(8,128)(2,1)S(1)}, u32[]{:S(2)}, u32[]{:S(2)}) collective-permute-start(bf16[128,128]{1,0:T(8,128)(2,1)S(1)} %pair_total.1), channel_id=1, source_target_pairs={{4,12},{5,13},{6,14},{7,15},{20,28},{21,29},{22,30},{23,31}} | collective-permute-start | bytes 98312 | tf_op jit(solution)/shard_map/ppermute | solution.py:474
  40.2 4.7 %collective-permute-start.7 = (bf16[128,128]{1,0:T(8,128)(2,1)S(1)}, bf16[128,128]{1,0:T(8,128)(2,1)S(1)}, u32[]{:S(2)}, u32[]{:S(2)}) collective-permute-start(bf16[128,128]{1,0:T(8,128)(2,1)S(1)} %pair_total.1), channel_id=1, source_target_pairs={{4,8},{5,9},{6,10},{7,11},{8,12},{9,13},{10,14},{11,15},{20,24},{2... | collective-permute-start | bytes 98312 | tf_op jit(solution)/shard_map/ppermute | solution.py:474
  45.8 5.6 %collective-permute-start.10 = (bf16[128,128]{1,0:T(8,128)(2,1)S(1)}, bf16[128,128]{1,0:T(8,128)(2,1)S(1)}, u32[]{:S(2)}, u32[]{:S(2)}) collective-permute-start(bf16[128,128]{1,0:T(8,128)(2,1)S(1)} %get-tuple-element.38), channel_id=1, source_target_pairs={{0,1},{1,0},{2,3},{3,2},{4,5},{5,4},{6,7},{7,6},{8,9},{9,8},{10,11... | collective-permute-start | bytes 98312 | tf_op jit(solution)/shard_map/ppermute | solution.py:447
  47.7 3.7 %collective-permute-start.11 = (bf16[128,128]{1,0:T(8,128)(2,1)S(1)}, bf16[128,128]{1,0:T(8,128)(2,1)S(1)}, u32[]{:S(2)}, u32[]{:S(2)}) collective-permute-start(bf16[128,128]{1,0:T(8,128)(2,1)S(1)} %get-tuple-element.39), channel_id=1, source_target_pairs={{0,2},{1,3},{2,0},{3,1},{4,6},{5,7},{6,4},{7,5},{8,10},{9,11},{10,... | collective-permute-start | bytes 98312 | tf_op jit(solution)/shard_map/ppermute | solution.py:451
  48.1 3.6 %collective-permute-start.12 = (bf16[128,128]{1,0:T(8,128)(2,1)S(1)}, bf16[128,128]{1,0:T(8,128)(2,1)S(1)}, u32[]{:S(2)}, u32[]{:S(2)}) collective-permute-start(bf16[128,128]{1,0:T(8,128)(2,1)S(1)} %get-tuple-element.40), channel_id=1, source_target_pairs={{0,3},{1,2},{2,1},{3,0},{4,7},{5,6},{6,5},{7,4},{8,11},{9,10},{10,... | collective-permute-start | bytes 98312 | tf_op jit(solution)/shard_map/ppermute | solution.py:455

commit v17 on v16

--- a/solution.py
+++ b/solution.py
@@ -232,22 +232,11 @@
     )(pattern, green, coupling, tie)
 
 
-def image_kernel(green, source, _tie, out):
-    for e in range(green.shape[0]):
-        out[e] = dot(green[e], source[e])
-
-
-def images(green, source, tie):
-    return call(
-        image_kernel, "image", [IN_VMEM] * 2 + [IN_PLACE], shape(*source.shape, dtype=F32), [], 1.2
-    )(green, source, tie)
-
-
 def times(a, b):
     return dot(a[0], b[0]) + (dot(a[0], b[1]) + dot(a[1], b[0]))
 
 
-def chain_kernel(own, near, across, far, total_out, sent_out, parts, maps):
+def chain_kernel(own, near, across, far, _tie, total_out, sent_out, parts, maps):
     collect((own, near, across, far), maps)
     split = [two_parts(maps[j]) for j in range(GROUP)]
     lower, upper = two_parts(times(split[1], split[0])), two_parts(times(split[3], split[2]))
@@ -259,19 +248,19 @@
         parts[1, j] = low
 
 
-def chain(maps):
+def chain(maps, tie):
     face = maps[0].shape[0]
     return call(
         chain_kernel,
         "chain_maps",
-        [IN_VMEM] * GROUP,
+        [IN_VMEM] * GROUP + [IN_PLACE],
         [shape(face, face, dtype=F32), shape(face, face), shape(2, GROUP, face, face)],
         [pltpu.VMEM((GROUP, face, face), F32)],
         0.9,
-    )(*maps)
-
-
-def source_kernel(received, inject, face_rows, _map, source, own, near, across, far, _same_map, quarters, total, heads, targets, sem):
+    )(*maps, tie)
+
+
+def source_kernel(received, inject, face_rows, source, own, near, across, far, quarters, total, heads, targets, sem):
     energies, orbitals, columns = inject.shape
     sections = received.shape[0]
     half = quarters.shape[1]
@@ -308,15 +297,15 @@
         out[...] = quarters[at].astype(BF16)
 
 
-def placed_source(received, inject, face_rows, passed):
+def placed_source(received, inject, face_rows):
     face = face_rows.shape[1]
     energies, orbitals, columns = inject.shape
     sections = received.shape[0]
     return call(
         source_kernel,
         "source_and_face",
-        [IN_VMEM, IN_VMEM, IN_VMEM, IN_PLACE],
-        [shape(*inject.shape)] + [shape(face // 2, columns)] * GROUP + [shape(*passed.shape, dtype=passed.dtype)],
+        [IN_VMEM, IN_VMEM, IN_VMEM],
+        [shape(*inject.shape)] + [shape(face // 2, columns)] * GROUP,
         [
             pltpu.VMEM((GROUP, face // 2, columns), F32),
             pltpu.VMEM(inject.shape, F32),
@@ -325,8 +314,7 @@
             pltpu.SemaphoreType.DMA,
         ],
         1.4,
-        aliases={3: 1 + GROUP},
-    )(received, inject, face_rows, passed)
+    )(received, inject, face_rows)
 
 
 def collect(refs, held):
@@ -359,18 +347,38 @@
     )(*shifts, parts)
 
 
-def upto_kernel(parts, _total, out):
-    maps = (parts[0, 0], parts[1, 0])
-    for j in range(1, GROUP - 1):
-        maps = two_parts(times((parts[0, j], parts[1, j]), maps))
-        out[0, j - 1], out[1, j - 1] = maps
-
-
-def maps_upto(parts, tie):
+def work_kernel(early, *refs):
+    green, source, parts, _tie = refs[:4]
+    held, (image, upto) = refs[4:-2], refs[-2:]
+    low_plane = lax.axis_index("sec") // GROUP < 2
+
+    @pl.when(low_plane if early else jnp.logical_not(low_plane))
+    def _():
+        for e in range(green.shape[0]):
+            image[e] = dot(green[e], source[e])
+        maps = (parts[0, 0], parts[1, 0])
+        for j in range(1, GROUP - 1):
+            maps = two_parts(times((parts[0, j], parts[1, j]), maps))
+            upto[0, j - 1], upto[1, j - 1] = maps
+
+    if held:
+
+        @pl.when(low_plane)
+        def _():
+            image[...] = held[0][...]
+            upto[...] = held[1][...]
+
+
+def image_and_maps(green, source, parts, tie, held=()):
     _, _, face, _ = parts.shape
     return call(
-        upto_kernel, "maps_upto", [IN_VMEM, IN_PLACE], shape(2, GROUP - 2, face, face), [], 3.0
-    )(parts, tie)
+        functools.partial(work_kernel, not held),
+        "image_and_maps",
+        [IN_VMEM] * 3 + [IN_PLACE] + [IN_VMEM] * len(held),
+        [shape(*source.shape, dtype=F32), shape(2, GROUP - 2, face, face)],
+        [],
+        2.0,
+    )(green, source, parts, tie, *held)
 
 
 def sweep_plane(state, parts, upto, local, out):
@@ -397,26 +405,26 @@
     )(total, below, whole, *ties)
 
 
-def entering_kernel(_image, below, first, second, got, parts, upto, local, *out):
+def entering_kernel(below, first, second, got, parts, upto, local, *out):
     high, low = two_parts(unpack(second[...].astype(F32)))
     state = unpack(below[...].astype(F32) + first[...].astype(F32)) + dot(got[...], high) + dot(got[...], low)
     sweep_plane(state, parts, upto, local, out)
 
 
-def entering_from_kernel(_image, base, parts, upto, local, *out):
+def entering_from_kernel(base, parts, upto, local, *out):
     sweep_plane(unpack(base[...]), parts, upto, local, out)
 
 
-def entering(body, tie, args):
+def entering(body, args):
     half, columns = args[0].shape
     return call(
         body,
         "entering",
-        [IN_PLACE] + [IN_VMEM] * len(args),
+        [IN_VMEM] * len(args),
         [shape(half, columns)] * GROUP,
         [pltpu.VMEM((GROUP, half, columns), F32)],
         1.4,
-    )(tie, *args)
+    )(*args)
 
 
 def waves_kernel(own, near, across, far, prop, image, out, arrived):
@@ -500,23 +508,25 @@
     across = to_across(other_map, sections)
     near = to_near(own_map, sections)
 
-    source, *quarters, across = placed_source(received, inject, face_rows, across)
+    far = to_near(across, sections)
+
+    source, *quarters = placed_source(received, inject, face_rows)
     shifts = exchange(*quarters, sections)
-    far = to_near(across, sections)
     four = sections // GROUP == 4
-    whole, sent, parts = chain([own_map, near, across, far])
+    whole, sent, parts = chain([own_map, near, across, far], quarters[0])
     got = between(sent, (2, 3)) if four else None
     total, local = plane_total(shifts, parts)
-    upto = maps_upto(parts, total)
-    image = images(green, source, total)
+    early = image_and_maps(green, source, parts, total)
     if four:
         below = between(total, (0, 1))
-        pair = pair_total(total, below, whole, image, upto)
-        first, second = between(pair, (1, 2), (2, 3)), between(pair, (1, 3))
-        entered = entering(entering_kernel, image, (below, first, second, got, parts, upto, local))
+        pair = pair_total(total, below, whole, *early)
+        second, first = between(pair, (1, 3)), between(pair, (1, 2), (2, 3))
+        image, upto = image_and_maps(green, source, parts, pair, early)
+        entered = entering(entering_kernel, (below, first, second, got, parts, upto, local))
     else:
         base = scan_below(whole, total, sections)
-        entered = entering(entering_from_kernel, image, (base, parts, upto, local))
+        image, upto = image_and_maps(green, source, parts, base, early)
+        entered = entering(entering_from_kernel, (base, parts, upto, local))
     arrived = exchange(*entered, sections)
     prop = propagator(tiles, green, coupling, entered[0])
     return final_waves(arrived, prop, image)[None]

time: 53.5 us -> 54.4 us (1.017)
  the two profiles are of different devices: /device:TPU:21 before, /device:TPU:17 now
where the time goes in v17:
time: 54.4 us; the launch traced here: 54.1 us
  starting transfers between devices  22 us (40%)
  Pallas kernels  15.3 us (28%)
  waiting for transfers between devices  11.7 us (22%)
  local copies, waits for them, and re-layouts  4.85 us (9%)
    ppermute x3, waiting for transfers between devices, to_across(): lax.ppermute(item, 'sec', [(s, s // GROUP * GROUP + (s % GROUP + CORES) %...  9.04 us
    all_to_all x1, starting transfers between devices, per_device(): lax.all_to_all(outgoing, 'sec', split_axis=0, concat_axis=0, tiled=True)  6.57 us
    ppermute x4, starting transfers between devices, between(): return lax.ppermute(item, 'sec', pairs)  6.34 us
    unnamed x14, local copies, waits for them, and re-layouts  4.85 us
    pallas_call x1, Pallas kernels, outgoing_pairs(): call(pairs_kernel, 'pairs', [IN_HBM] * 4, shape(sections, CAP * energies...  4.68 us
    ppermute x4, starting transfers between devices, to_near(): return lax.ppermute(item, 'sec', [(s, s ^ 1) for s in range(sections)])  4.08 us
    ppermute x3, starting transfers between devices, to_across(): lax.ppermute(item, 'sec', [(s, s // GROUP * GROUP + (s % GROUP + CORES) %...  2.62 us
    ppermute x2, starting transfers between devices, to_far(): lax.ppermute(item, 'sec', [(s, s // GROUP * GROUP + (s % GROUP + CORES) %...  2.4 us
  transfers between devices with their start and end apart: 14, of which 3 were waited for; matrix products, arithmetic and copies ran while one was open for 0% of the time, Pallas kernels for 16%

profile of v17, /device:TPU:17, one launch (start us, length us, event | category | flops | bytes accessed | tf_op | source)
XLA Modules:
  0.0 54.1 jit_solution(1601852036215970708)
XLA Ops:
  0.0 4.7 %pairs.1 = bf16[16,136,128]{2,1,0:T(8,128)(2,1)} custom-call(s32[16]{0:T(128)} %bitcast.21, s32[2,16]{1,0:T(2,128)} %bitcast.20, bf16[2,1024,1024]{2,1,0:T(8,128)(2,1)} %bitcast.9, bf16[2,1024,128]{2,1,0:T(8,128)(2,1)} %bitcast.14), custom_call_target="tpu_custom_call" | custom-call | flops 4600000000 | tf_op jit(solution)/shard_map/pairs/pallas_call | solution.py:168
  4.7 0.0 copy-start.2
  4.7 6.6 %all-to-all-start = ((bf16[16,136,128]{2,1,0:T(8,128)(2,1)}), bf16[16,136,128]{2,1,0:T(8,128)(2,1)S(1)}, u32[]{:S(2)}, u32[]{:S(2)}) async-start(bf16[16,136,128]{2,1,0:T(8,128)(2,1)} %pairs.1), calls=%async_computation | async-start | bytes 1114112 | tf_op jit(solution)/shard_map/all_to_all | solution.py:505
  11.3 0.0 copy-done.3
  11.3 0.0 copy-done.4
  11.3 0.0 copy-start
  11.3 2.2 %copy-done = bf16[1,2,1024,1024]{3,2,1,0:T(8,128)(2,1)S(1)} copy-done((bf16[1,2,1024,1024]{3,2,1,0:T(8,128)(2,1)S(1)}, bf16[1,2,1024,1024]{3,2,1,0:T(8,128)(2,1)}, u32[]{:S(2)}) %copy-start) | copy-done | bytes 4194328
  13.5 1.1 %face_maps.1 = (f32[256,256]{1,0:T(8,128)S(1)}, f32[256,256]{1,0:T(8,128)S(1)}, bf16[2,256,1024]{2,1,0:T(8,128)(2,1)S(1)}) custom-call(s32[2,8]{1,0:T(2,128)S(1)} %bitcast.18, bf16[2,1024,1024]{2,1,0:T(8,128)(2,1)S(1)} %bitcast.10, bf16[1024,256]{1,0:T(8,128)(2,1)S(1)} %bitcast.16), custom_call_target="tpu_custom_call" | custom-call | flops 1380000000 | tf_op jit(solution)/shard_map/face_maps/pallas_call | solution.py:206
  14.6 0.0 copy-start.5
  14.6 1.0 %copy-done.5 = bf16[2,256,1024]{2,1,0:T(8,128)(2,1)} copy-done((bf16[2,256,1024]{2,1,0:T(8,128)(2,1)}, bf16[2,256,1024]{2,1,0:T(8,128)(2,1)S(1)}, u32[]{:S(2)}) %copy-start.5) | copy-done | bytes 1048600
  15.6 1.2 %collective-permute-start.4 = (f32[256,256]{1,0:T(8,128)S(1)}, f32[256,256]{1,0:T(8,128)S(1)}, u32[]{:S(2)}, u32[]{:S(2)}) collective-permute-start(f32[256,256]{1,0:T(8,128)S(1)} %get-tuple-element.32), channel_id=1, source_target_pairs={{0,2},{1,3},{2,0},{3,1},{4,6},{5,7},{6,4},{7,5},{8,10},{9,11},{10,... | collective-permute-start | bytes 786440 | tf_op jit(solution)/shard_map/ppermute | solution.py:459
  16.8 0.6 %collective-permute-start.3 = (f32[256,256]{1,0:T(8,128)S(1)}, f32[256,256]{1,0:T(8,128)S(1)}, u32[]{:S(2)}, u32[]{:S(2)}) collective-permute-start(f32[256,256]{1,0:T(8,128)S(1)} %get-tuple-element.31.own), channel_id=1, source_target_pairs={{0,1},{1,0},{2,3},{3,2},{4,5},{5,4},{6,7},{7,6},{8,9},{9,8},{10,11... | collective-permute-start | bytes 786440 | tf_op jit(solution)/shard_map/ppermute | solution.py:455
  17.5 9.0 %collective-permute-done.4.across = f32[256,256]{1,0:T(8,128)S(1)} collective-permute-done((f32[256,256]{1,0:T(8,128)S(1)}, f32[256,256]{1,0:T(8,128)S(1)}, u32[]{:S(2)}, u32[]{:S(2)}) %collective-permute-start.4) | collective-permute-done | bytes 262176 | tf_op jit(solution)/shard_map/ppermute | solution.py:459
  26.5 0.9 %collective-permute-start.5 = (f32[256,256]{1,0:T(8,128)S(1)}, f32[256,256]{1,0:T(8,128)S(1)}, u32[]{:S(2)}, u32[]{:S(2)}) collective-permute-start(f32[256,256]{1,0:T(8,128)S(1)} %collective-permute-done.4.across), channel_id=1, source_target_pairs={{0,1},{1,0},{2,3},{3,2},{4,5},{5,4},{6,7},{7,6},{8,9},{9,8},{10,11... | collective-permute-start | bytes 786440 | tf_op jit(solution)/shard_map/ppermute | solution.py:455
  27.4 0.0 all-to-all-done.received
  27.4 1.2 %copy-done.6 = bf16[2,256,1024]{2,1,0:T(8,128)(2,1)S(1)} copy-done((bf16[2,256,1024]{2,1,0:T(8,128)(2,1)S(1)}, bf16[2,256,1024]{2,1,0:T(8,128)(2,1)}, u32[]{:S(2)}) %copy-start.6) | copy-done | bytes 1048600
  28.6 1.4 %source_and_face.1 = (bf16[2,1024,128]{2,1,0:T(8,128)(2,1)S(1)}, bf16[128,128]{1,0:T(8,128)(2,1)S(1)}, bf16[128,128]{1,0:T(8,128)(2,1)S(1)}, bf16[128,128]{1,0:T(8,128)(2,1)S(1)}, bf16[128,128]{1,0:T(8,128)(2,1)S(1)}) custom-call(bf16[16,136,128]{2,1,0:T(8,128)(2,1)S(1)} %all-to-all-done.received, bf16[2,1024,128]{2,1,0:T(8,128)(2,1)S(1)} %bitcast.15, ...), custom_call_target="tpu_custom_call" | custom-call | flops 1610000000 | tf_op jit(solution)/shard_map/source_and_face/pallas_call | solution.py:304
  30.0 0.1 collective-permute-start
  30.1 0.8 %collective-permute-start.1 = (bf16[128,128]{1,0:T(8,128)(2,1)S(1)}, bf16[128,128]{1,0:T(8,128)(2,1)S(1)}, u32[]{:S(2)}, u32[]{:S(2)}) collective-permute-start(bf16[128,128]{1,0:T(8,128)(2,1)S(1)} %get-tuple-element.29), channel_id=1, source_target_pairs={{0,2},{1,3},{2,0},{3,1},{4,6},{5,7},{6,4},{7,5},{8,10},{9,11},{10,... | collective-permute-start | bytes 98312 | tf_op jit(solution)/shard_map/ppermute | solution.py:459
  30.9 1.3 %collective-permute-start.2 = (bf16[128,128]{1,0:T(8,128)(2,1)S(1)}, bf16[128,128]{1,0:T(8,128)(2,1)S(1)}, u32[]{:S(2)}, u32[]{:S(2)}) collective-permute-start(bf16[128,128]{1,0:T(8,128)(2,1)S(1)} %get-tuple-element.30), channel_id=1, source_target_pairs={{0,3},{1,2},{2,1},{3,0},{4,7},{5,6},{6,5},{7,4},{8,11},{9,10},{10,... | collective-permute-start | bytes 98312 | tf_op jit(solution)/shard_map/ppermute | solution.py:463
  32.2 0.0 collective-permute-done.3.near
  32.2 0.0 collective-permute-done.5.far
  32.2 0.8 %chain_maps.1 = (f32[256,256]{1,0:T(8,128)S(1)}, bf16[256,256]{1,0:T(8,128)(2,1)S(1)}, bf16[2,4,256,256]{3,2,1,0:T(8,128)(2,1)S(1)}) custom-call(f32[256,256]{1,0:T(8,128)S(1)} %get-tuple-element.31.own, f32[256,256]{1,0:T(8,128)S(1)} %collective-permute-done.3.near, f32[256,256]{1,0:T(8,128)S(1)} %collective-permute-done.4.across, ...), custom_call_target="tpu_custom_call" | custom-call | flops 1035000000 | tf_op jit(solution)/shard_map/chain_maps/pallas_call | solution.py:253
  33.1 2.3 %collective-permute-start.9 = (bf16[256,256]{1,0:T(8,128)(2,1)S(1)}, bf16[256,256]{1,0:T(8,128)(2,1)S(1)}, u32[]{:S(2)}, u32[]{:S(2)}) collective-permute-start(bf16[256,256]{1,0:T(8,128)(2,1)S(1)} %get-tuple-element.39), channel_id=1, source_target_pairs={{8,12},{9,13},{10,14},{11,15},{24,28},{25,29},{26,30},{27,31}} | collective-permute-start | bytes 393224 | tf_op jit(solution)/shard_map/ppermute | solution.py:482
  35.4 0.0 collective-permute-done.near
  35.4 0.0 collective-permute-done.1.across
  35.4 0.0 collective-permute-done.2.far
  35.4 0.0 copy-start.1
  35.5 1.0 %plane_total.1 = (bf16[128,128]{1,0:T(8,128)(2,1)S(1)}, f32[3,256,128]{2,1,0:T(8,128)S(1)}) custom-call(bf16[128,128]{1,0:T(8,128)(2,1)S(1)} %get-tuple-element.27._tie.own, bf16[128,128]{1,0:T(8,128)(2,1)S(1)} %collective-permute-done.near, bf16[128,128]{1,0:T(8,128)(2,1)S(1)} %collective-permute-done.1.across, ...), custom_call_target="tpu_custom_call" | custom-call | flops 3449999872 | tf_op jit(solution)/shard_map/plane_total/pallas_call | solution.py:340
  36.4 0.8 %collective-permute-start.6 = (bf16[128,128]{1,0:T(8,128)(2,1)S(1)}, bf16[128,128]{1,0:T(8,128)(2,1)S(1)}, u32[]{:S(2)}, u32[]{:S(2)}) collective-permute-start(bf16[128,128]{1,0:T(8,128)(2,1)S(1)} %get-tuple-element.34.refs_3_.total), channel_id=1, source_target_pairs={{0,4},{1,5},{2,6},{3,7},{16,20},{17,21},{18,22},{19,23}} | collective-permute-start | bytes 98312 | tf_op jit(solution)/shard_map/ppermute | solution.py:482
  37.2 0.4 copy-done.1
  37.6 0.0 collective-permute-done.6.below
  37.6 0.4 pair_total.1.refs_3_
  38.0 0.7 %collective-permute-start.8 = (bf16[128,128]{1,0:T(8,128)(2,1)S(1)}, bf16[128,128]{1,0:T(8,128)(2,1)S(1)}, u32[]{:S(2)}, u32[]{:S(2)}) collective-permute-start(bf16[128,128]{1,0:T(8,128)(2,1)S(1)} %pair_total.1.refs_3_), channel_id=1, source_target_pairs={{4,12},{5,13},{6,14},{7,15},{20,28},{21,29},{22,30},{23,31}} | collective-permute-start | bytes 98312 | tf_op jit(solution)/shard_map/ppermute | solution.py:482
  38.7 2.5 %collective-permute-start.7 = (bf16[128,128]{1,0:T(8,128)(2,1)S(1)}, bf16[128,128]{1,0:T(8,128)(2,1)S(1)}, u32[]{:S(2)}, u32[]{:S(2)}) collective-permute-start(bf16[128,128]{1,0:T(8,128)(2,1)S(1)} %pair_total.1.refs_3_), channel_id=1, source_target_pairs={{4,8},{5,9},{6,10},{7,11},{8,12},{9,13},{10,14},{11,15},{20,24},{2... | collective-permute-start | bytes 98312 | tf_op jit(solution)/shard_map/ppermute | solution.py:482
  41.2 1.8 %image_and_maps.3 = (f32[2,1024,128]{2,1,0:T(8,128)S(1)}, bf16[2,2,256,256]{3,2,1,0:T(8,128)(2,1)S(1)}) custom-call(bf16[2,1024,1024]{2,1,0:T(8,128)(2,1)S(1)} %bitcast.12, bf16[2,1024,128]{2,1,0:T(8,128)(2,1)S(1)} %get-tuple-element.36.refs_1_, bf16[2,4,256,256]{3,2,1,0:T(8,128)(2,1)S(1)} %get-tuple-element.33.parts.refs_2_, ...), custom_call_target="tpu_custom_call" | custom-call | flops 2300000000 | tf_op jit(solution)/shard_map/image_and_maps/pallas_call | solution.py:374
  43.0 0.0 collective-permute-done.8.second
  43.0 2.3 %collective-permute-done.7.first = bf16[128,128]{1,0:T(8,128)(2,1)S(1)} collective-permute-done((bf16[128,128]{1,0:T(8,128)(2,1)S(1)}, bf16[128,128]{1,0:T(8,128)(2,1)S(1)}, u32[]{:S(2)}, u32[]{:S(2)}) %collective-permute-start.7) | collective-permute-done | bytes 32800 | tf_op jit(solution)/shard_map/ppermute | solution.py:482
  45.4 0.0 collective-permute-done.9.got
  45.4 0.9 %entering.1 = (bf16[128,128]{1,0:T(8,128)(2,1)S(1)}, bf16[128,128]{1,0:T(8,128)(2,1)S(1)}, bf16[128,128]{1,0:T(8,128)(2,1)S(1)}, bf16[128,128]{1,0:T(8,128)(2,1)S(1)}) custom-call(bf16[128,128]{1,0:T(8,128)(2,1)S(1)} %collective-permute-done.6.below, bf16[128,128]{1,0:T(8,128)(2,1)S(1)} %collective-permute-done.7.first, ...), custom_call_target="tpu_custom_call" | custom-call | flops 1610000000 | tf_op jit(solution)/shard_map/entering/pallas_call | solution.py:420
  46.2 2.5 %collective-permute-start.10 = (bf16[128,128]{1,0:T(8,128)(2,1)S(1)}, bf16[128,128]{1,0:T(8,128)(2,1)S(1)}, u32[]{:S(2)}, u32[]{:S(2)}) collective-permute-start(bf16[128,128]{1,0:T(8,128)(2,1)S(1)} %get-tuple-element.43), channel_id=1, source_target_pairs={{0,1},{1,0},{2,3},{3,2},{4,5},{5,4},{6,7},{7,6},{8,9},{9,8},{10,11... | collective-permute-start | bytes 98312 | tf_op jit(solution)/shard_map/ppermute | solution.py:455
  48.7 0.6 %collective-permute-start.11 = (bf16[128,128]{1,0:T(8,128)(2,1)S(1)}, bf16[128,128]{1,0:T(8,128)(2,1)S(1)}, u32[]{:S(2)}, u32[]{:S(2)}) collective-permute-start(bf16[128,128]{1,0:T(8,128)(2,1)S(1)} %get-tuple-element.44), channel_id=1, source_target_pairs={{0,2},{1,3},{2,0},{3,1},{4,6},{5,7},{6,4},{7,5},{8,10},{9,11},{10,... | collective-permute-start | bytes 98312 | tf_op jit(solution)/shard_map/ppermute | solution.py:459
  49.4 1.1 %collective-permute-start.12 = (bf16[128,128]{1,0:T(8,128)(2,1)S(1)}, bf16[128,128]{1,0:T(8,128)(2,1)S(1)}, u32[]{:S(2)}, u32[]{:S(2)}) collective-permute-start(bf16[128,128]{1,0:T(8,128)(2,1)S(1)} %get-tuple-element.45), channel_id=1, source_target_pairs={{0,3},{1,2},{2,1},{3,0},{4,7},{5,6},{6,5},{7,4},{8,11},{9,10},{10,... | collective-permute-start | bytes 98312 | tf_op jit(solution)/shard_map/ppermute | solution.py:463
  50.5 1.9 %prop.1 = bf16[2,1024,256]{2,1,0:T(8,128)(2,1)S(1)} custom-call(s32[2,8]{1,0:T(2,128)S(1)} %bitcast.19, bf16[2,1024,1024]{2,1,0:T(8,128)(2,1)S(1)} %bitcast.13, bf16[1024,256]{1,0:T(8,128)(2,1)S(1)} %bitcast.17, bf16[128,128]{1,0:T(8,128)(2,1)S(1)} %get-tuple-element.42._tie.own), custom_call_target="tpu_custom_call" | custom-call | flops 1724999936 | tf_op jit(solution)/shard_map/prop/pallas_call | solution.py:225
  52.4 0.0 collective-permute-done.10.near
  52.4 0.0 collective-permute-done.11.across
  52.4 0.3 collective-permute-done.12.far
  52.8 1.3 %waves.1 = bf16[2,1024,128]{2,1,0:T(8,128)(2,1)} custom-call(bf16[128,128]{1,0:T(8,128)(2,1)S(1)} %get-tuple-element.42._tie.own, bf16[128,128]{1,0:T(8,128)(2,1)S(1)} %collective-permute-done.10.near, bf16[128,128]{1,0:T(8,128)(2,1)S(1)} %collective-permute-done.11.across, bf16[128,128]{1,0:T(8,128)(2,1)S(1)} %collective-permute-done.12.far, ...), custom_call_target="tpu_custom_call" | custom-call | flops 1495000064 | tf_op jit(solution)/shard_map/waves/pallas_call | solution.py:444
  (5 shorter events, 0.0 us)
Async XLA Ops:
  0.0 11.3 %copy-start.3 = (bf16[1,1024,256]{2,1,0:T(8,128)(2,1)S(1)}, bf16[1,1024,256]{2,1,0:T(8,128)(2,1)}, u32[]{:S(2)}) copy-start(bf16[1,1024,256]{2,1,0:T(8,128)(2,1)} %param.8) | copy-start | bytes 1572868
  0.0 11.3 %copy-start.4 = (s32[1,8,2]{1,2,0:T(2,128)S(1)}, s32[1,8,2]{1,2,0:T(2,128)}, u32[]{:S(2)}) copy-start(s32[1,8,2]{1,2,0:T(2,128)} %param.9) | copy-start | bytes 196
  4.7 22.7 %copy-start.2 = (bf16[1,2,1024,128]{3,2,1,0:T(8,128)(2,1)S(1)}, bf16[1,2,1024,128]{3,2,1,0:T(8,128)(2,1)}, u32[]{:S(2)}) copy-start(bf16[1,2,1024,128]{3,2,1,0:T(8,128)(2,1)} %param.7) | copy-start | bytes 1572868
  4.7 22.6 %all-to-all-start = ((bf16[16,136,128]{2,1,0:T(8,128)(2,1)}), bf16[16,136,128]{2,1,0:T(8,128)(2,1)S(1)}, u32[]{:S(2)}, u32[]{:S(2)}) async-start(bf16[16,136,128]{2,1,0:T(8,128)(2,1)} %pairs.1), calls=%async_computation | async-start | bytes 1114112 | tf_op jit(solution)/shard_map/all_to_all | solution.py:505
  11.3 2.2 %copy-start = (bf16[1,2,1024,1024]{3,2,1,0:T(8,128)(2,1)S(1)}, bf16[1,2,1024,1024]{3,2,1,0:T(8,128)(2,1)}, u32[]{:S(2)}) copy-start(bf16[1,2,1024,1024]{3,2,1,0:T(8,128)(2,1)} %param.6) | copy-start | bytes 12582916
  14.6 1.0 %copy-start.5 = (bf16[2,256,1024]{2,1,0:T(8,128)(2,1)}, bf16[2,256,1024]{2,1,0:T(8,128)(2,1)S(1)}, u32[]{:S(2)}) copy-start(bf16[2,256,1024]{2,1,0:T(8,128)(2,1)S(1)} %get-tuple-element.26.face_rows) | copy-start | bytes 3145732
  15.6 10.9 %collective-permute-start.4 = (f32[256,256]{1,0:T(8,128)S(1)}, f32[256,256]{1,0:T(8,128)S(1)}, u32[]{:S(2)}, u32[]{:S(2)}) collective-permute-start(f32[256,256]{1,0:T(8,128)S(1)} %get-tuple-element.32), channel_id=1, source_target_pairs={{0,2},{1,3},{2,0},{3,1},{4,6},{5,7},{6,4},{7,5},{8,10},{9,11},{10,... | collective-permute-start | bytes 786440 | tf_op jit(solution)/shard_map/ppermute | solution.py:459
  16.8 15.4 %collective-permute-start.3 = (f32[256,256]{1,0:T(8,128)S(1)}, f32[256,256]{1,0:T(8,128)S(1)}, u32[]{:S(2)}, u32[]{:S(2)}) collective-permute-start(f32[256,256]{1,0:T(8,128)S(1)} %get-tuple-element.31.own), channel_id=1, source_target_pairs={{0,1},{1,0},{2,3},{3,2},{4,5},{5,4},{6,7},{7,6},{8,9},{9,8},{10,11... | collective-permute-start | bytes 786440 | tf_op jit(solution)/shard_map/ppermute | solution.py:455
  26.5 5.7 %collective-permute-start.5 = (f32[256,256]{1,0:T(8,128)S(1)}, f32[256,256]{1,0:T(8,128)S(1)}, u32[]{:S(2)}, u32[]{:S(2)}) collective-permute-start(f32[256,256]{1,0:T(8,128)S(1)} %collective-permute-done.4.across), channel_id=1, source_target_pairs={{0,1},{1,0},{2,3},{3,2},{4,5},{5,4},{6,7},{7,6},{8,9},{9,8},{10,11... | collective-permute-start | bytes 786440 | tf_op jit(solution)/shard_map/ppermute | solution.py:455
  27.4 1.2 %copy-start.6 = (bf16[2,256,1024]{2,1,0:T(8,128)(2,1)S(1)}, bf16[2,256,1024]{2,1,0:T(8,128)(2,1)}, u32[]{:S(2)}) copy-start(bf16[2,256,1024]{2,1,0:T(8,128)(2,1)} %copy-done.5) | copy-start | bytes 3145732
  30.0 5.4 %collective-permute-start = (bf16[128,128]{1,0:T(8,128)(2,1)S(1)}, bf16[128,128]{1,0:T(8,128)(2,1)S(1)}, u32[]{:S(2)}, u32[]{:S(2)}) collective-permute-start(bf16[128,128]{1,0:T(8,128)(2,1)S(1)} %get-tuple-element.28), channel_id=1, source_target_pairs={{0,1},{1,0},{2,3},{3,2},{4,5},{5,4},{6,7},{7,6},{8,9},{9,8},{10,11... | collective-permute-start | bytes 98312 | tf_op jit(solution)/shard_map/ppermute | solution.py:455
  30.1 5.3 %collective-permute-start.1 = (bf16[128,128]{1,0:T(8,128)(2,1)S(1)}, bf16[128,128]{1,0:T(8,128)(2,1)S(1)}, u32[]{:S(2)}, u32[]{:S(2)}) collective-permute-start(bf16[128,128]{1,0:T(8,128)(2,1)S(1)} %get-tuple-element.29), channel_id=1, source_target_pairs={{0,2},{1,3},{2,0},{3,1},{4,6},{5,7},{6,4},{7,5},{8,10},{9,11},{10,... | collective-permute-start | bytes 98312 | tf_op jit(solution)/shard_map/ppermute | solution.py:459
  30.9 4.6 %collective-permute-start.2 = (bf16[128,128]{1,0:T(8,128)(2,1)S(1)}, bf16[128,128]{1,0:T(8,128)(2,1)S(1)}, u32[]{:S(2)}, u32[]{:S(2)}) collective-permute-start(bf16[128,128]{1,0:T(8,128)(2,1)S(1)} %get-tuple-element.30), channel_id=1, source_target_pairs={{0,3},{1,2},{2,1},{3,0},{4,7},{5,6},{6,5},{7,4},{8,11},{9,10},{10,... | collective-permute-start | bytes 98312 | tf_op jit(solution)/shard_map/ppermute | solution.py:463
  33.1 12.3 %collective-permute-start.9 = (bf16[256,256]{1,0:T(8,128)(2,1)S(1)}, bf16[256,256]{1,0:T(8,128)(2,1)S(1)}, u32[]{:S(2)}, u32[]{:S(2)}) collective-permute-start(bf16[256,256]{1,0:T(8,128)(2,1)S(1)} %get-tuple-element.39), channel_id=1, source_target_pairs={{8,12},{9,13},{10,14},{11,15},{24,28},{25,29},{26,30},{27,31}} | collective-permute-start | bytes 393224 | tf_op jit(solution)/shard_map/ppermute | solution.py:482
  35.4 2.2 %copy-start.1 = (bf16[1,2,1024,1024]{3,2,1,0:T(8,128)(2,1)S(1)}, bf16[1,2,1024,1024]{3,2,1,0:T(8,128)(2,1)}, u32[]{:S(2)}) copy-start(bf16[1,2,1024,1024]{3,2,1,0:T(8,128)(2,1)} %param.6) | copy-start | bytes 12582916
  36.4 1.2 %collective-permute-start.6 = (bf16[128,128]{1,0:T(8,128)(2,1)S(1)}, bf16[128,128]{1,0:T(8,128)(2,1)S(1)}, u32[]{:S(2)}, u32[]{:S(2)}) collective-permute-start(bf16[128,128]{1,0:T(8,128)(2,1)S(1)} %get-tuple-element.34.refs_3_.total), channel_id=1, source_target_pairs={{0,4},{1,5},{2,6},{3,7},{16,20},{17,21},{18,22},{19,23}} | collective-permute-start | bytes 98312 | tf_op jit(solution)/shard_map/ppermute | solution.py:482
  38.0 5.0 %collective-permute-start.8 = (bf16[128,128]{1,0:T(8,128)(2,1)S(1)}, bf16[128,128]{1,0:T(8,128)(2,1)S(1)}, u32[]{:S(2)}, u32[]{:S(2)}) collective-permute-start(bf16[128,128]{1,0:T(8,128)(2,1)S(1)} %pair_total.1.refs_3_), channel_id=1, source_target_pairs={{4,12},{5,13},{6,14},{7,15},{20,28},{21,29},{22,30},{23,31}} | collective-permute-start | bytes 98312 | tf_op jit(solution)/shard_map/ppermute | solution.py:482
  38.7 6.7 %collective-permute-start.7 = (bf16[128,128]{1,0:T(8,128)(2,1)S(1)}, bf16[128,128]{1,0:T(8,128)(2,1)S(1)}, u32[]{:S(2)}, u32[]{:S(2)}) collective-permute-start(bf16[128,128]{1,0:T(8,128)(2,1)S(1)} %pair_total.1.refs_3_), channel_id=1, source_target_pairs={{4,8},{5,9},{6,10},{7,11},{8,12},{9,13},{10,14},{11,15},{20,24},{2... | collective-permute-start | bytes 98312 | tf_op jit(solution)/shard_map/ppermute | solution.py:482
  46.2 6.2 %collective-permute-start.10 = (bf16[128,128]{1,0:T(8,128)(2,1)S(1)}, bf16[128,128]{1,0:T(8,128)(2,1)S(1)}, u32[]{:S(2)}, u32[]{:S(2)}) collective-permute-start(bf16[128,128]{1,0:T(8,128)(2,1)S(1)} %get-tuple-element.43), channel_id=1, source_target_pairs={{0,1},{1,0},{2,3},{3,2},{4,5},{5,4},{6,7},{7,6},{8,9},{9,8},{10,11... | collective-permute-start | bytes 98312 | tf_op jit(solution)/shard_map/ppermute | solution.py:455
  48.7 3.7 %collective-permute-start.11 = (bf16[128,128]{1,0:T(8,128)(2,1)S(1)}, bf16[128,128]{1,0:T(8,128)(2,1)S(1)}, u32[]{:S(2)}, u32[]{:S(2)}) collective-permute-start(bf16[128,128]{1,0:T(8,128)(2,1)S(1)} %get-tuple-element.44), channel_id=1, source_target_pairs={{0,2},{1,3},{2,0},{3,1},{4,6},{5,7},{6,4},{7,5},{8,10},{9,11},{10,... | collective-permute-start | bytes 98312 | tf_op jit(solution)/shard_map/ppermute | solution.py:459
  49.4 3.4 %collective-permute-start.12 = (bf16[128,128]{1,0:T(8,128)(2,1)S(1)}, bf16[128,128]{1,0:T(8,128)(2,1)S(1)}, u32[]{:S(2)}, u32[]{:S(2)}) collective-permute-start(bf16[128,128]{1,0:T(8,128)(2,1)S(1)} %get-tuple-element.45), channel_id=1, source_target_pairs={{0,3},{1,2},{2,1},{3,0},{4,7},{5,6},{6,5},{7,4},{8,11},{9,10},{10,... | collective-permute-start | bytes 98312 | tf_op jit(solution)/shard_map/ppermute | solution.py:463

commit v18 on v17

--- a/solution.py
+++ b/solution.py
@@ -236,7 +236,7 @@
     return dot(a[0], b[0]) + (dot(a[0], b[1]) + dot(a[1], b[0]))
 
 
-def chain_kernel(own, near, across, far, _tie, total_out, sent_out, parts, maps):
+def chain_kernel(own, near, across, far, total_out, sent_out, parts, maps):
     collect((own, near, across, far), maps)
     split = [two_parts(maps[j]) for j in range(GROUP)]
     lower, upper = two_parts(times(split[1], split[0])), two_parts(times(split[3], split[2]))
@@ -248,19 +248,19 @@
         parts[1, j] = low
 
 
-def chain(maps, tie):
+def chain(maps):
     face = maps[0].shape[0]
     return call(
         chain_kernel,
         "chain_maps",
-        [IN_VMEM] * GROUP + [IN_PLACE],
+        [IN_VMEM] * GROUP,
         [shape(face, face, dtype=F32), shape(face, face), shape(2, GROUP, face, face)],
         [pltpu.VMEM((GROUP, face, face), F32)],
         0.9,
-    )(*maps, tie)
-
-
-def source_kernel(received, inject, face_rows, source, own, near, across, far, quarters, total, heads, targets, sem):
+    )(*maps)
+
+
+def source_kernel(received, inject, face_rows, _map, source, own, near, across, far, _same_map, quarters, total, heads, targets, sem):
     energies, orbitals, columns = inject.shape
     sections = received.shape[0]
     half = quarters.shape[1]
@@ -297,15 +297,15 @@
         out[...] = quarters[at].astype(BF16)
 
 
-def placed_source(received, inject, face_rows):
+def placed_source(received, inject, face_rows, passed):
     face = face_rows.shape[1]
     energies, orbitals, columns = inject.shape
     sections = received.shape[0]
     return call(
         source_kernel,
         "source_and_face",
-        [IN_VMEM, IN_VMEM, IN_VMEM],
-        [shape(*inject.shape)] + [shape(face // 2, columns)] * GROUP,
+        [IN_VMEM, IN_VMEM, IN_VMEM, IN_PLACE],
+        [shape(*inject.shape)] + [shape(face // 2, columns)] * GROUP + [shape(*passed.shape, dtype=F32)],
         [
             pltpu.VMEM((GROUP, face // 2, columns), F32),
             pltpu.VMEM(inject.shape, F32),
@@ -314,7 +314,8 @@
             pltpu.SemaphoreType.DMA,
         ],
         1.4,
-    )(received, inject, face_rows)
+        aliases={3: 1 + GROUP},
+    )(received, inject, face_rows, passed)
 
 
 def collect(refs, held):
@@ -405,7 +406,7 @@
     )(total, below, whole, *ties)
 
 
-def entering_kernel(below, first, second, got, parts, upto, local, *out):
+def entering_kernel(below, second, first, got, parts, upto, local, *out):
     high, low = two_parts(unpack(second[...].astype(F32)))
     state = unpack(below[...].astype(F32) + first[...].astype(F32)) + dot(got[...], high) + dot(got[...], low)
     sweep_plane(state, parts, upto, local, out)
@@ -508,12 +509,11 @@
     across = to_across(other_map, sections)
     near = to_near(own_map, sections)
 
+    source, *quarters, across = placed_source(received, inject, face_rows, across)
+    shifts = exchange(*quarters, sections)
     far = to_near(across, sections)
-
-    source, *quarters = placed_source(received, inject, face_rows)
-    shifts = exchange(*quarters, sections)
     four = sections // GROUP == 4
-    whole, sent, parts = chain([own_map, near, across, far], quarters[0])
+    whole, sent, parts = chain([own_map, near, across, far])
     got = between(sent, (2, 3)) if four else None
     total, local = plane_total(shifts, parts)
     early = image_and_maps(green, source, parts, total)
@@ -522,7 +522,7 @@
         pair = pair_total(total, below, whole, *early)
         second, first = between(pair, (1, 3)), between(pair, (1, 2), (2, 3))
         image, upto = image_and_maps(green, source, parts, pair, early)
-        entered = entering(entering_kernel, (below, first, second, got, parts, upto, local))
+        entered = entering(entering_kernel, (below, second, first, got, parts, upto, local))
     else:
         base = scan_below(whole, total, sections)
         image, upto = image_and_maps(green, source, parts, base, early)

time: 54.4 us -> 52.6 us (0.967)
  the two profiles are of different devices: /device:TPU:17 before, /device:TPU:29 now
where the time goes in v18:
time: 52.6 us; the launch traced here: 52.2 us
  starting transfers between devices  20.1 us (38%)
  Pallas kernels  15.3 us (29%)
  waiting for transfers between devices  14 us (27%)
  local copies, waits for them, and re-layouts  2.63 us (5%)
    ppermute x3, waiting for transfers between devices, to_across(): lax.ppermute(item, 'sec', [(s, s // GROUP * GROUP + (s % GROUP + CORES) %...  8.58 us
    all_to_all x1, starting transfers between devices, per_device(): lax.all_to_all(outgoing, 'sec', split_axis=0, concat_axis=0, tiled=True)  6.2 us
    pallas_call x1, Pallas kernels, outgoing_pairs(): call(pairs_kernel, 'pairs', [IN_HBM] * 4, shape(sections, CAP * energies...  4.67 us
    ppermute x4, starting transfers between devices, between(): return lax.ppermute(item, 'sec', pairs)  4.67 us
    ppermute x4, starting transfers between devices, to_near(): return lax.ppermute(item, 'sec', [(s, s ^ 1) for s in range(sections)])  4.2 us
    ppermute x4, waiting for transfers between devices, between(): return lax.ppermute(item, 'sec', pairs)  4.19 us
    ppermute x3, starting transfers between devices, to_across(): lax.ppermute(item, 'sec', [(s, s // GROUP * GROUP + (s % GROUP + CORES) %...  3.08 us
    unnamed x10, local copies, waits for them, and re-layouts  2.63 us
  transfers between devices with their start and end apart: 14, of which 5 were waited for; matrix products, arithmetic and copies ran while one was open for 0% of the time, Pallas kernels for 16%

profile of v18, /device:TPU:29, one launch (start us, length us, event | category | flops | bytes accessed | tf_op | source)
XLA Modules:
  0.0 52.2 jit_solution(12667736701401226576)
XLA Ops:
  0.0 0.0 copy-start.3
  0.0 0.0 copy-start.4
  0.0 4.7 %pairs.1 = bf16[16,136,128]{2,1,0:T(8,128)(2,1)} custom-call(s32[16]{0:T(128)} %bitcast.21, s32[2,16]{1,0:T(2,128)} %bitcast.20, bf16[2,1024,1024]{2,1,0:T(8,128)(2,1)} %bitcast.9, bf16[2,1024,128]{2,1,0:T(8,128)(2,1)} %bitcast.14), custom_call_target="tpu_custom_call" | custom-call | flops 4600000000 | tf_op jit(solution)/shard_map/pairs/pallas_call | solution.py:168
  4.7 0.0 copy-start.2
  4.7 6.2 %all-to-all-start = ((bf16[16,136,128]{2,1,0:T(8,128)(2,1)}), bf16[16,136,128]{2,1,0:T(8,128)(2,1)S(1)}, u32[]{:S(2)}, u32[]{:S(2)}) async-start(bf16[16,136,128]{2,1,0:T(8,128)(2,1)} %pairs.1), calls=%async_computation | async-start | bytes 1114112 | tf_op jit(solution)/shard_map/all_to_all | solution.py:506
  10.9 0.0 copy-done.3
  10.9 0.0 copy-done.4
  10.9 0.0 copy-start
  10.9 2.2 %copy-done = bf16[1,2,1024,1024]{3,2,1,0:T(8,128)(2,1)S(1)} copy-done((bf16[1,2,1024,1024]{3,2,1,0:T(8,128)(2,1)S(1)}, bf16[1,2,1024,1024]{3,2,1,0:T(8,128)(2,1)}, u32[]{:S(2)}) %copy-start) | copy-done | bytes 4194328
  13.1 1.1 %face_maps.1 = (f32[256,256]{1,0:T(8,128)S(1)}, f32[256,256]{1,0:T(8,128)S(1)}, bf16[2,256,1024]{2,1,0:T(8,128)(2,1)S(1)}) custom-call(s32[2,8]{1,0:T(2,128)S(1)} %bitcast.18, bf16[2,1024,1024]{2,1,0:T(8,128)(2,1)S(1)} %bitcast.10, bf16[1024,256]{1,0:T(8,128)(2,1)S(1)} %bitcast.16), custom_call_target="tpu_custom_call" | custom-call | flops 1380000000 | tf_op jit(solution)/shard_map/face_maps/pallas_call | solution.py:206
  14.2 1.2 %collective-permute-start = (f32[256,256]{1,0:T(8,128)S(1)}, f32[256,256]{1,0:T(8,128)S(1)}, u32[]{:S(2)}, u32[]{:S(2)}) collective-permute-start(f32[256,256]{1,0:T(8,128)S(1)} %get-tuple-element.28), channel_id=1, source_target_pairs={{0,2},{1,3},{2,0},{3,1},{4,6},{5,7},{6,4},{7,5},{8,10},{9,11},{10,... | collective-permute-start | bytes 786440 | tf_op jit(solution)/shard_map/ppermute | solution.py:460
  15.5 0.6 %collective-permute-start.4 = (f32[256,256]{1,0:T(8,128)S(1)}, f32[256,256]{1,0:T(8,128)S(1)}, u32[]{:S(2)}, u32[]{:S(2)}) collective-permute-start(f32[256,256]{1,0:T(8,128)S(1)} %get-tuple-element.33.own), channel_id=1, source_target_pairs={{0,1},{1,0},{2,3},{3,2},{4,5},{5,4},{6,7},{7,6},{8,9},{9,8},{10,11... | collective-permute-start | bytes 786440 | tf_op jit(solution)/shard_map/ppermute | solution.py:456
  16.1 8.6 %collective-permute-done._map = f32[256,256]{1,0:T(8,128)S(1)} collective-permute-done((f32[256,256]{1,0:T(8,128)S(1)}, f32[256,256]{1,0:T(8,128)S(1)}, u32[]{:S(2)}, u32[]{:S(2)}) %collective-permute-start) | collective-permute-done | bytes 262176 | tf_op jit(solution)/shard_map/ppermute | solution.py:460
  24.7 0.0 all-to-all-done.received
  24.7 0.0 copy-done.2
  24.7 1.4 %source_and_face.1 = (bf16[2,1024,128]{2,1,0:T(8,128)(2,1)S(1)}, bf16[128,128]{1,0:T(8,128)(2,1)S(1)}, bf16[128,128]{1,0:T(8,128)(2,1)S(1)}, bf16[128,128]{1,0:T...) custom-call(bf16[16,136,128]{2,1,0:T(8,128)(2,1)S(1)} %all-to-all-done.rec, ...), custom_call_target="tpu_custom_call", output_to_operand_aliasing={{5}: (3, {})} | custom-call | flops 1610000000 | tf_op jit(solution)/shard_map/source_and_face/pallas_call | solution.py:304
  26.1 1.0 %collective-permute-start.5 = (f32[256,256]{1,0:T(8,128)S(1)}, f32[256,256]{1,0:T(8,128)S(1)}, u32[]{:S(2)}, u32[]{:S(2)}) collective-permute-start(f32[256,256]{1,0:T(8,128)S(1)} %get-tuple-element.34.across), channel_id=1, source_target_pairs={{0,1},{1,0},{2,3},{3,2},{4,5},{5,4},{6,7},{7,6},{8,9},{9,8},{10,11... | collective-permute-start | bytes 786440 | tf_op jit(solution)/shard_map/ppermute | solution.py:456
  27.1 0.1 collective-permute-start.1
  27.2 1.1 %collective-permute-start.2 = (bf16[128,128]{1,0:T(8,128)(2,1)S(1)}, bf16[128,128]{1,0:T(8,128)(2,1)S(1)}, u32[]{:S(2)}, u32[]{:S(2)}) collective-permute-start(bf16[128,128]{1,0:T(8,128)(2,1)S(1)} %get-tuple-element.31), channel_id=1, source_target_pairs={{0,2},{1,3},{2,0},{3,1},{4,6},{5,7},{6,4},{7,5},{8,10},{9,11},{10,... | collective-permute-start | bytes 98312 | tf_op jit(solution)/shard_map/ppermute | solution.py:460
  28.3 1.0 %collective-permute-start.3 = (bf16[128,128]{1,0:T(8,128)(2,1)S(1)}, bf16[128,128]{1,0:T(8,128)(2,1)S(1)}, u32[]{:S(2)}, u32[]{:S(2)}) collective-permute-start(bf16[128,128]{1,0:T(8,128)(2,1)S(1)} %get-tuple-element.32), channel_id=1, source_target_pairs={{0,3},{1,2},{2,1},{3,0},{4,7},{5,6},{6,5},{7,4},{8,11},{9,10},{10,... | collective-permute-start | bytes 98312 | tf_op jit(solution)/shard_map/ppermute | solution.py:464
  29.3 0.0 collective-permute-done.4.near
  29.3 0.0 collective-permute-done.5.far
  29.3 0.8 %chain_maps.1 = (f32[256,256]{1,0:T(8,128)S(1)}, bf16[256,256]{1,0:T(8,128)(2,1)S(1)}, bf16[2,4,256,256]{3,2,1,0:T(8,128)(2,1)S(1)}) custom-call(f32[256,256]{1,0:T(8,128)S(1)} %get-tuple-element.33.own, f32[256,256]{1,0:T(8,128)S(1)} %collective-permute-done.4.near, f32[256,256]{1,0:T(8,128)S(1)} %get-tuple-element.34.across, ...), custom_call_target="tpu_custom_call" | custom-call | flops 1035000000 | tf_op jit(solution)/shard_map/chain_maps/pallas_call | solution.py:253
  30.1 1.3 %collective-permute-start.9 = (bf16[256,256]{1,0:T(8,128)(2,1)S(1)}, bf16[256,256]{1,0:T(8,128)(2,1)S(1)}, u32[]{:S(2)}, u32[]{:S(2)}) collective-permute-start(bf16[256,256]{1,0:T(8,128)(2,1)S(1)} %get-tuple-element.41), channel_id=1, source_target_pairs={{8,12},{9,13},{10,14},{11,15},{24,28},{25,29},{26,30},{27,31}} | collective-permute-start | bytes 393224 | tf_op jit(solution)/shard_map/ppermute | solution.py:483
  31.4 0.0 collective-permute-done.1.near
  31.4 0.0 collective-permute-done.2.across
  31.4 0.8 %collective-permute-done.3.far = bf16[128,128]{1,0:T(8,128)(2,1)S(1)} collective-permute-done((bf16[128,128]{1,0:T(8,128)(2,1)S(1)}, bf16[128,128]{1,0:T(8,128)(2,1)S(1)}, u32[]{:S(2)}, u32[]{:S(2)}) %collective-permute-start.3) | collective-permute-done | bytes 32800 | tf_op jit(solution)/shard_map/ppermute | solution.py:464
  32.3 0.0 copy-start.1
  32.3 0.9 %plane_total.1 = (bf16[128,128]{1,0:T(8,128)(2,1)S(1)}, f32[3,256,128]{2,1,0:T(8,128)S(1)}) custom-call(bf16[128,128]{1,0:T(8,128)(2,1)S(1)} %get-tuple-element.29.own, bf16[128,128]{1,0:T(8,128)(2,1)S(1)} %collective-permute-done.1.near, bf16[128,128]{1,0:T(8,128)(2,1)S(1)} %collective-permute-done.2.across, ...), custom_call_target="tpu_custom_call" | custom-call | flops 3449999872 | tf_op jit(solution)/shard_map/plane_total/pallas_call | solution.py:341
  33.2 0.8 %collective-permute-start.6 = (bf16[128,128]{1,0:T(8,128)(2,1)S(1)}, bf16[128,128]{1,0:T(8,128)(2,1)S(1)}, u32[]{:S(2)}, u32[]{:S(2)}) collective-permute-start(bf16[128,128]{1,0:T(8,128)(2,1)S(1)} %get-tuple-element.36.refs_3_.total), channel_id=1, source_target_pairs={{0,4},{1,5},{2,6},{3,7},{16,20},{17,21},{18,22},{19,23}} | collective-permute-start | bytes 98312 | tf_op jit(solution)/shard_map/ppermute | solution.py:483
  34.0 0.4 copy-done.1
  34.4 0.0 collective-permute-done.6.below
  34.5 0.4 pair_total.1.refs_3_
  34.8 1.3 %collective-permute-start.8 = (bf16[128,128]{1,0:T(8,128)(2,1)S(1)}, bf16[128,128]{1,0:T(8,128)(2,1)S(1)}, u32[]{:S(2)}, u32[]{:S(2)}) collective-permute-start(bf16[128,128]{1,0:T(8,128)(2,1)S(1)} %pair_total.1.refs_3_), channel_id=1, source_target_pairs={{4,8},{5,9},{6,10},{7,11},{8,12},{9,13},{10,14},{11,15},{20,24},{2... | collective-permute-start | bytes 98312 | tf_op jit(solution)/shard_map/ppermute | solution.py:483
  36.1 1.3 %collective-permute-start.7 = (bf16[128,128]{1,0:T(8,128)(2,1)S(1)}, bf16[128,128]{1,0:T(8,128)(2,1)S(1)}, u32[]{:S(2)}, u32[]{:S(2)}) collective-permute-start(bf16[128,128]{1,0:T(8,128)(2,1)S(1)} %pair_total.1.refs_3_), channel_id=1, source_target_pairs={{4,12},{5,13},{6,14},{7,15},{20,28},{21,29},{22,30},{23,31}} | collective-permute-start | bytes 98312 | tf_op jit(solution)/shard_map/ppermute | solution.py:483
  37.4 1.8 %image_and_maps.3 = (f32[2,1024,128]{2,1,0:T(8,128)S(1)}, bf16[2,2,256,256]{3,2,1,0:T(8,128)(2,1)S(1)}) custom-call(bf16[2,1024,1024]{2,1,0:T(8,128)(2,1)S(1)} %bitcast.12, bf16[2,1024,128]{2,1,0:T(8,128)(2,1)S(1)} %get-tuple-element.38.refs_1_, bf16[2,4,256,256]{3,2,1,0:T(8,128)(2,1)S(1)} %get-tuple-element.35.parts.refs_2_, ...), custom_call_target="tpu_custom_call" | custom-call | flops 2300000000 | tf_op jit(solution)/shard_map/image_and_maps/pallas_call | solution.py:375
  39.2 0.3 collective-permute-done.8.first
  39.5 3.9 %collective-permute-done.7.second = bf16[128,128]{1,0:T(8,128)(2,1)S(1)} collective-permute-done((bf16[128,128]{1,0:T(8,128)(2,1)S(1)}, bf16[128,128]{1,0:T(8,128)(2,1)S(1)}, u32[]{:S(2)}, u32[]{:S(2)}) %collective-permute-start.7) | collective-permute-done | bytes 32800 | tf_op jit(solution)/shard_map/ppermute | solution.py:483
  43.4 0.0 collective-permute-done.9.got
  43.4 0.9 %entering.1 = (bf16[128,128]{1,0:T(8,128)(2,1)S(1)}, bf16[128,128]{1,0:T(8,128)(2,1)S(1)}, bf16[128,128]{1,0:T(8,128)(2,1)S(1)}, bf16[128,128]{1,0:T(8,128)(2,1)S(1)}) custom-call(bf16[128,128]{1,0:T(8,128)(2,1)S(1)} %collective-permute-done.6.below, bf16[128,128]{1,0:T(8,128)(2,1)S(1)} %collective-permute-done.7.second, ...), custom_call_target="tpu_custom_call" | custom-call | flops 1610000000 | tf_op jit(solution)/shard_map/entering/pallas_call | solution.py:421
  44.3 2.5 %collective-permute-start.10 = (bf16[128,128]{1,0:T(8,128)(2,1)S(1)}, bf16[128,128]{1,0:T(8,128)(2,1)S(1)}, u32[]{:S(2)}, u32[]{:S(2)}) collective-permute-start(bf16[128,128]{1,0:T(8,128)(2,1)S(1)} %get-tuple-element.45), channel_id=1, source_target_pairs={{0,1},{1,0},{2,3},{3,2},{4,5},{5,4},{6,7},{7,6},{8,9},{9,8},{10,11... | collective-permute-start | bytes 98312 | tf_op jit(solution)/shard_map/ppermute | solution.py:456
  46.8 0.7 %collective-permute-start.11 = (bf16[128,128]{1,0:T(8,128)(2,1)S(1)}, bf16[128,128]{1,0:T(8,128)(2,1)S(1)}, u32[]{:S(2)}, u32[]{:S(2)}) collective-permute-start(bf16[128,128]{1,0:T(8,128)(2,1)S(1)} %get-tuple-element.46), channel_id=1, source_target_pairs={{0,2},{1,3},{2,0},{3,1},{4,6},{5,7},{6,4},{7,5},{8,10},{9,11},{10,... | collective-permute-start | bytes 98312 | tf_op jit(solution)/shard_map/ppermute | solution.py:460
  47.6 1.0 %collective-permute-start.12 = (bf16[128,128]{1,0:T(8,128)(2,1)S(1)}, bf16[128,128]{1,0:T(8,128)(2,1)S(1)}, u32[]{:S(2)}, u32[]{:S(2)}) collective-permute-start(bf16[128,128]{1,0:T(8,128)(2,1)S(1)} %get-tuple-element.47), channel_id=1, source_target_pairs={{0,3},{1,2},{2,1},{3,0},{4,7},{5,6},{6,5},{7,4},{8,11},{9,10},{10,... | collective-permute-start | bytes 98312 | tf_op jit(solution)/shard_map/ppermute | solution.py:464
  48.5 1.9 %prop.1 = bf16[2,1024,256]{2,1,0:T(8,128)(2,1)S(1)} custom-call(s32[2,8]{1,0:T(2,128)S(1)} %bitcast.19, bf16[2,1024,1024]{2,1,0:T(8,128)(2,1)S(1)} %bitcast.13, bf16[1024,256]{1,0:T(8,128)(2,1)S(1)} %bitcast.17, bf16[128,128]{1,0:T(8,128)(2,1)S(1)} %get-tuple-element.44._tie.own), custom_call_target="tpu_custom_call" | custom-call | flops 1724999936 | tf_op jit(solution)/shard_map/prop/pallas_call | solution.py:225
  50.5 0.0 collective-permute-done.10.near
  50.5 0.0 collective-permute-done.11.across
  50.5 0.4 collective-permute-done.12.far
  50.9 1.3 %waves.1 = bf16[2,1024,128]{2,1,0:T(8,128)(2,1)} custom-call(bf16[128,128]{1,0:T(8,128)(2,1)S(1)} %get-tuple-element.44._tie.own, bf16[128,128]{1,0:T(8,128)(2,1)S(1)} %collective-permute-done.10.near, bf16[128,128]{1,0:T(8,128)(2,1)S(1)} %collective-permute-done.11.across, bf16[128,128]{1,0:T(8,128)(2,1)S(1)} %collective-permute-done.12.far, ...), custom_call_target="tpu_custom_call" | custom-call | flops 1495000064 | tf_op jit(solution)/shard_map/waves/pallas_call | solution.py:445
  (1 shorter events, 0.0 us)
Async XLA Ops:
  0.0 10.9 %copy-start.3 = (bf16[1,1024,256]{2,1,0:T(8,128)(2,1)S(1)}, bf16[1,1024,256]{2,1,0:T(8,128)(2,1)}, u32[]{:S(2)}) copy-start(bf16[1,1024,256]{2,1,0:T(8,128)(2,1)} %param.8) | copy-start | bytes 1572868
  0.0 10.9 %copy-start.4 = (s32[1,8,2]{1,2,0:T(2,128)S(1)}, s32[1,8,2]{1,2,0:T(2,128)}, u32[]{:S(2)}) copy-start(s32[1,8,2]{1,2,0:T(2,128)} %param.9) | copy-start | bytes 196
  4.7 20.0 %copy-start.2 = (bf16[1,2,1024,128]{3,2,1,0:T(8,128)(2,1)S(1)}, bf16[1,2,1024,128]{3,2,1,0:T(8,128)(2,1)}, u32[]{:S(2)}) copy-start(bf16[1,2,1024,128]{3,2,1,0:T(8,128)(2,1)} %param.7) | copy-start | bytes 1572868
  4.7 20.0 %all-to-all-start = ((bf16[16,136,128]{2,1,0:T(8,128)(2,1)}), bf16[16,136,128]{2,1,0:T(8,128)(2,1)S(1)}, u32[]{:S(2)}, u32[]{:S(2)}) async-start(bf16[16,136,128]{2,1,0:T(8,128)(2,1)} %pairs.1), calls=%async_computation | async-start | bytes 1114112 | tf_op jit(solution)/shard_map/all_to_all | solution.py:506
  10.9 2.2 %copy-start = (bf16[1,2,1024,1024]{3,2,1,0:T(8,128)(2,1)S(1)}, bf16[1,2,1024,1024]{3,2,1,0:T(8,128)(2,1)}, u32[]{:S(2)}) copy-start(bf16[1,2,1024,1024]{3,2,1,0:T(8,128)(2,1)} %param.6) | copy-start | bytes 12582916
  14.2 10.5 %collective-permute-start = (f32[256,256]{1,0:T(8,128)S(1)}, f32[256,256]{1,0:T(8,128)S(1)}, u32[]{:S(2)}, u32[]{:S(2)}) collective-permute-start(f32[256,256]{1,0:T(8,128)S(1)} %get-tuple-element.28), channel_id=1, source_target_pairs={{0,2},{1,3},{2,0},{3,1},{4,6},{5,7},{6,4},{7,5},{8,10},{9,11},{10,... | collective-permute-start | bytes 786440 | tf_op jit(solution)/shard_map/ppermute | solution.py:460
  15.5 13.8 %collective-permute-start.4 = (f32[256,256]{1,0:T(8,128)S(1)}, f32[256,256]{1,0:T(8,128)S(1)}, u32[]{:S(2)}, u32[]{:S(2)}) collective-permute-start(f32[256,256]{1,0:T(8,128)S(1)} %get-tuple-element.33.own), channel_id=1, source_target_pairs={{0,1},{1,0},{2,3},{3,2},{4,5},{5,4},{6,7},{7,6},{8,9},{9,8},{10,11... | collective-permute-start | bytes 786440 | tf_op jit(solution)/shard_map/ppermute | solution.py:456
  26.1 3.1 %collective-permute-start.5 = (f32[256,256]{1,0:T(8,128)S(1)}, f32[256,256]{1,0:T(8,128)S(1)}, u32[]{:S(2)}, u32[]{:S(2)}) collective-permute-start(f32[256,256]{1,0:T(8,128)S(1)} %get-tuple-element.34.across), channel_id=1, source_target_pairs={{0,1},{1,0},{2,3},{3,2},{4,5},{5,4},{6,7},{7,6},{8,9},{9,8},{10,11... | collective-permute-start | bytes 786440 | tf_op jit(solution)/shard_map/ppermute | solution.py:456
  27.1 4.3 %collective-permute-start.1 = (bf16[128,128]{1,0:T(8,128)(2,1)S(1)}, bf16[128,128]{1,0:T(8,128)(2,1)S(1)}, u32[]{:S(2)}, u32[]{:S(2)}) collective-permute-start(bf16[128,128]{1,0:T(8,128)(2,1)S(1)} %get-tuple-element.30), channel_id=1, source_target_pairs={{0,1},{1,0},{2,3},{3,2},{4,5},{5,4},{6,7},{7,6},{8,9},{9,8},{10,11... | collective-permute-start | bytes 98312 | tf_op jit(solution)/shard_map/ppermute | solution.py:456
  27.2 4.2 %collective-permute-start.2 = (bf16[128,128]{1,0:T(8,128)(2,1)S(1)}, bf16[128,128]{1,0:T(8,128)(2,1)S(1)}, u32[]{:S(2)}, u32[]{:S(2)}) collective-permute-start(bf16[128,128]{1,0:T(8,128)(2,1)S(1)} %get-tuple-element.31), channel_id=1, source_target_pairs={{0,2},{1,3},{2,0},{3,1},{4,6},{5,7},{6,4},{7,5},{8,10},{9,11},{10,... | collective-permute-start | bytes 98312 | tf_op jit(solution)/shard_map/ppermute | solution.py:460
  28.3 4.0 %collective-permute-start.3 = (bf16[128,128]{1,0:T(8,128)(2,1)S(1)}, bf16[128,128]{1,0:T(8,128)(2,1)S(1)}, u32[]{:S(2)}, u32[]{:S(2)}) collective-permute-start(bf16[128,128]{1,0:T(8,128)(2,1)S(1)} %get-tuple-element.32), channel_id=1, source_target_pairs={{0,3},{1,2},{2,1},{3,0},{4,7},{5,6},{6,5},{7,4},{8,11},{9,10},{10,... | collective-permute-start | bytes 98312 | tf_op jit(solution)/shard_map/ppermute | solution.py:464
  30.1 13.3 %collective-permute-start.9 = (bf16[256,256]{1,0:T(8,128)(2,1)S(1)}, bf16[256,256]{1,0:T(8,128)(2,1)S(1)}, u32[]{:S(2)}, u32[]{:S(2)}) collective-permute-start(bf16[256,256]{1,0:T(8,128)(2,1)S(1)} %get-tuple-element.41), channel_id=1, source_target_pairs={{8,12},{9,13},{10,14},{11,15},{24,28},{25,29},{26,30},{27,31}} | collective-permute-start | bytes 393224 | tf_op jit(solution)/shard_map/ppermute | solution.py:483
  32.3 2.2 %copy-start.1 = (bf16[1,2,1024,1024]{3,2,1,0:T(8,128)(2,1)S(1)}, bf16[1,2,1024,1024]{3,2,1,0:T(8,128)(2,1)}, u32[]{:S(2)}) copy-start(bf16[1,2,1024,1024]{3,2,1,0:T(8,128)(2,1)} %param.6) | copy-start | bytes 12582916
  33.2 1.2 %collective-permute-start.6 = (bf16[128,128]{1,0:T(8,128)(2,1)S(1)}, bf16[128,128]{1,0:T(8,128)(2,1)S(1)}, u32[]{:S(2)}, u32[]{:S(2)}) collective-permute-start(bf16[128,128]{1,0:T(8,128)(2,1)S(1)} %get-tuple-element.36.refs_3_.total), channel_id=1, source_target_pairs={{0,4},{1,5},{2,6},{3,7},{16,20},{17,21},{18,22},{19,23}} | collective-permute-start | bytes 98312 | tf_op jit(solution)/shard_map/ppermute | solution.py:483
  34.8 4.7 %collective-permute-start.8 = (bf16[128,128]{1,0:T(8,128)(2,1)S(1)}, bf16[128,128]{1,0:T(8,128)(2,1)S(1)}, u32[]{:S(2)}, u32[]{:S(2)}) collective-permute-start(bf16[128,128]{1,0:T(8,128)(2,1)S(1)} %pair_total.1.refs_3_), channel_id=1, source_target_pairs={{4,8},{5,9},{6,10},{7,11},{8,12},{9,13},{10,14},{11,15},{20,24},{2... | collective-permute-start | bytes 98312 | tf_op jit(solution)/shard_map/ppermute | solution.py:483
  36.1 7.3 %collective-permute-start.7 = (bf16[128,128]{1,0:T(8,128)(2,1)S(1)}, bf16[128,128]{1,0:T(8,128)(2,1)S(1)}, u32[]{:S(2)}, u32[]{:S(2)}) collective-permute-start(bf16[128,128]{1,0:T(8,128)(2,1)S(1)} %pair_total.1.refs_3_), channel_id=1, source_target_pairs={{4,12},{5,13},{6,14},{7,15},{20,28},{21,29},{22,30},{23,31}} | collective-permute-start | bytes 98312 | tf_op jit(solution)/shard_map/ppermute | solution.py:483
  44.3 6.2 %collective-permute-start.10 = (bf16[128,128]{1,0:T(8,128)(2,1)S(1)}, bf16[128,128]{1,0:T(8,128)(2,1)S(1)}, u32[]{:S(2)}, u32[]{:S(2)}) collective-permute-start(bf16[128,128]{1,0:T(8,128)(2,1)S(1)} %get-tuple-element.45), channel_id=1, source_target_pairs={{0,1},{1,0},{2,3},{3,2},{4,5},{5,4},{6,7},{7,6},{8,9},{9,8},{10,11... | collective-permute-start | bytes 98312 | tf_op jit(solution)/shard_map/ppermute | solution.py:456
  46.8 3.7 %collective-permute-start.11 = (bf16[128,128]{1,0:T(8,128)(2,1)S(1)}, bf16[128,128]{1,0:T(8,128)(2,1)S(1)}, u32[]{:S(2)}, u32[]{:S(2)}) collective-permute-start(bf16[128,128]{1,0:T(8,128)(2,1)S(1)} %get-tuple-element.46), channel_id=1, source_target_pairs={{0,2},{1,3},{2,0},{3,1},{4,6},{5,7},{6,4},{7,5},{8,10},{9,11},{10,... | collective-permute-start | bytes 98312 | tf_op jit(solution)/shard_map/ppermute | solution.py:460
  47.6 3.3 %collective-permute-start.12 = (bf16[128,128]{1,0:T(8,128)(2,1)S(1)}, bf16[128,128]{1,0:T(8,128)(2,1)S(1)}, u32[]{:S(2)}, u32[]{:S(2)}) collective-permute-start(bf16[128,128]{1,0:T(8,128)(2,1)S(1)} %get-tuple-element.47), channel_id=1, source_target_pairs={{0,3},{1,2},{2,1},{3,0},{4,7},{5,6},{6,5},{7,4},{8,11},{9,10},{10,... | collective-permute-start | bytes 98312 | tf_op jit(solution)/shard_map/ppermute | solution.py:464

commit v19 on v18

--- a/solution.py
+++ b/solution.py
@@ -327,7 +327,7 @@
     return unpack(shift.astype(F32)) + times((parts[0, j], parts[1, j]), two_parts(state))
 
 
-def total_kernel(own, near, across, far, parts, out, local, shifts):
+def total_kernel(own, near, across, far, parts, _image, out, local, shifts):
     collect((own, near, across, far), shifts)
     state = unpack(shifts[0].astype(F32))
     for j in range(1, GROUP):
@@ -336,22 +336,22 @@
     out[...] = pack(state).astype(BF16)
 
 
-def plane_total(shifts, parts):
+def plane_total(shifts, parts, tie):
     half, columns = shifts[0].shape
     return call(
         total_kernel,
         "plane_total",
-        [IN_VMEM] * (GROUP + 1),
+        [IN_VMEM] * (GROUP + 1) + [IN_PLACE],
         [shape(half, columns), shape(GROUP - 1, 2 * half, columns, dtype=F32)],
         [pltpu.VMEM((GROUP, half, columns), BF16)],
         3.0,
-    )(*shifts, parts)
+    )(*shifts, parts, tie)
 
 
 def work_kernel(early, *refs):
-    green, source, parts, _tie = refs[:4]
-    held, (image, upto) = refs[4:-2], refs[-2:]
-    low_plane = lax.axis_index("sec") // GROUP < 2
+    green, source, parts = refs[:3]
+    held, (image, upto) = refs[3:-2], refs[-2:]
+    low_plane = lax.axis_index("sec") // GROUP == 0
 
     @pl.when(low_plane if early else jnp.logical_not(low_plane))
     def _():
@@ -370,16 +370,16 @@
             upto[...] = held[1][...]
 
 
-def image_and_maps(green, source, parts, tie, held=()):
+def image_and_maps(green, source, parts, held=()):
     _, _, face, _ = parts.shape
     return call(
         functools.partial(work_kernel, not held),
         "image_and_maps",
-        [IN_VMEM] * 3 + [IN_PLACE] + [IN_VMEM] * len(held),
+        [IN_VMEM] * (3 + len(held)),
         [shape(*source.shape, dtype=F32), shape(2, GROUP - 2, face, face)],
         [],
         2.0,
-    )(green, source, parts, tie, *held)
+    )(green, source, parts, *held)
 
 
 def sweep_plane(state, parts, upto, local, out):
@@ -395,20 +395,14 @@
         ref[...] = work[at].astype(BF16)
 
 
-def pair_kernel(total, below, whole, _image, _upto, out):
-    state = unpack(total[...].astype(F32)) + times(two_parts(whole[...]), two_parts(unpack(below[...].astype(F32))))
-    out[...] = pack(state).astype(BF16)
-
-
-def pair_total(total, below, whole, *ties):
-    return call(
-        pair_kernel, "pair_total", [IN_VMEM] * 3 + [IN_PLACE] * 2, shape(*total.shape), [], 0.5
-    )(total, below, whole, *ties)
-
-
-def entering_kernel(below, second, first, got, parts, upto, local, *out):
-    high, low = two_parts(unpack(second[...].astype(F32)))
-    state = unpack(below[...].astype(F32) + first[...].astype(F32)) + dot(got[...], high) + dot(got[...], low)
+def entering_kernel(third, near_one, second, far_one, got, other, parts, upto, local, *out):
+    first_core = place() % CORES == 0
+    first = near_one[...].astype(F32) + far_one[...].astype(F32)
+    state = unpack(third[...].astype(F32))
+    for below, (one, two) in ((second[...].astype(F32), (other, got)), (first, (got, other))):
+        factor = jnp.where(first_core, one[...], two[...])
+        high, low = two_parts(state)
+        state = unpack(below) + dot(factor, high) + dot(factor, low)
     sweep_plane(state, parts, upto, local, out)
 
 
@@ -476,6 +470,17 @@
 def spread(packed):
     half = packed.shape[1] // 2
     return jnp.concatenate([packed[:, :half], packed[:, half:]], axis=0)
+
+
+def maps_up(total_map, sections):
+    pairs = []
+    for i in range(GROUP):
+        if i % CORES == 0:
+            pairs += [(GROUP + i, 2 * GROUP + i), (2 * GROUP + i, 3 * GROUP + i)]
+        else:
+            pairs += [(GROUP + i, 3 * GROUP + i)]
+    got = lax.ppermute(total_map, "sec", pairs)
+    return got, to_near(got, sections)
 
 
 def between(item, *planes):
@@ -514,18 +519,19 @@
     far = to_near(across, sections)
     four = sections // GROUP == 4
     whole, sent, parts = chain([own_map, near, across, far])
-    got = between(sent, (2, 3)) if four else None
-    total, local = plane_total(shifts, parts)
-    early = image_and_maps(green, source, parts, total)
+    early = image_and_maps(green, source, parts)
+    maps = maps_up(sent, sections) if four else []
+    total, local = plane_total(shifts, parts, early[0])
     if four:
-        below = between(total, (0, 1))
-        pair = pair_total(total, below, whole, *early)
-        second, first = between(pair, (1, 3)), between(pair, (1, 2), (2, 3))
-        image, upto = image_and_maps(green, source, parts, pair, early)
-        entered = entering(entering_kernel, (below, second, first, got, parts, upto, local))
+        fourth = between(total, (1, 2), (2, 3))
+        third = between(total, (0, 2), (1, 3))
+        second = between(total, (0, 1))
+        first = between(total, (0, 3))
+        image, upto = image_and_maps(green, source, parts, early)
+        entered = entering(entering_kernel, (first, second, third, fourth, *maps, parts, upto, local))
     else:
         base = scan_below(whole, total, sections)
-        image, upto = image_and_maps(green, source, parts, base, early)
+        image, upto = image_and_maps(green, source, parts, early)
         entered = entering(entering_from_kernel, (base, parts, upto, local))
     arrived = exchange(*entered, sections)
     prop = propagator(tiles, green, coupling, entered[0])

time: 52.6 us -> 52.7 us (level)
  the two profiles are of different devices: /device:TPU:29 before, /device:TPU:0 now
where the time goes in v19:
time: 52.7 us; the launch traced here: 52.3 us
  starting transfers between devices  21.8 us (41%)
  Pallas kernels  15.7 us (30%)
  waiting for transfers between devices  12.4 us (24%)
  local copies, waits for them, and re-layouts  2.2 us (4%)
    ppermute x3, waiting for transfers between devices, to_across(): lax.ppermute(item, 'sec', [(s, s // GROUP * GROUP + (s % GROUP + CORES) %...  10.2 us
    all_to_all x1, starting transfers between devices, per_device(): lax.all_to_all(outgoing, 'sec', split_axis=0, concat_axis=0, tiled=True)  7.55 us
    ppermute x4, starting transfers between devices, between(): return lax.ppermute(item, 'sec', pairs)  7.33 us
    ppermute x3, starting transfers between devices, to_across(): lax.ppermute(item, 'sec', [(s, s // GROUP * GROUP + (s % GROUP + CORES) %...  4.89 us
    pallas_call x1, Pallas kernels, outgoing_pairs(): call(pairs_kernel, 'pairs', [IN_HBM] * 4, shape(sections, CAP * energies...  4.49 us
    unnamed x10, local copies, waits for them, and re-layouts  2.2 us
    pallas_call x2, Pallas kernels, image_and_maps(): call(functools.partial(work_kernel, not held), 'image_and_maps', [IN_VMEM...  1.91 us
    pallas_call x1, Pallas kernels, propagator(): call(prop_kernel, 'prop', [IN_SMEM, IN_VMEM, IN_VMEM, IN_PLACE], shape(en...  1.9 us
  transfers between devices with their start and end apart: 16, of which 5 were waited for; matrix products, arithmetic and copies ran while one was open for 0% of the time, Pallas kernels for 17%

profile of v19, /device:TPU:0, one launch (start us, length us, event | category | flops | bytes accessed | tf_op | source)
XLA Modules:
  0.0 52.3 jit_solution(15637097605670363644)
XLA Ops:
  0.0 4.5 %pairs.1 = bf16[16,136,128]{2,1,0:T(8,128)(2,1)} custom-call(s32[16]{0:T(128)} %bitcast.21, s32[2,16]{1,0:T(2,128)} %bitcast.20, bf16[2,1024,1024]{2,1,0:T(8,128)(2,1)} %bitcast.9, bf16[2,1024,128]{2,1,0:T(8,128)(2,1)} %bitcast.14), custom_call_target="tpu_custom_call" | custom-call | flops 4600000000 | tf_op jit(solution)/shard_map/pairs/pallas_call | solution.py:168
  4.5 0.0 copy-start.2
  4.5 7.6 %all-to-all-start = ((bf16[16,136,128]{2,1,0:T(8,128)(2,1)}), bf16[16,136,128]{2,1,0:T(8,128)(2,1)S(1)}, u32[]{:S(2)}, u32[]{:S(2)}) async-start(bf16[16,136,128]{2,1,0:T(8,128)(2,1)} %pairs.1), calls=%async_computation | async-start | bytes 1114112 | tf_op jit(solution)/shard_map/all_to_all | solution.py:511
  12.1 0.0 copy-done.3
  12.1 0.0 copy-done.4
  12.1 0.0 copy-start
  12.1 2.2 %copy-done = bf16[1,2,1024,1024]{3,2,1,0:T(8,128)(2,1)S(1)} copy-done((bf16[1,2,1024,1024]{3,2,1,0:T(8,128)(2,1)S(1)}, bf16[1,2,1024,1024]{3,2,1,0:T(8,128)(2,1)}, u32[]{:S(2)}) %copy-start) | copy-done | bytes 4194328
  14.3 1.1 %face_maps.1 = (f32[256,256]{1,0:T(8,128)S(1)}, f32[256,256]{1,0:T(8,128)S(1)}, bf16[2,256,1024]{2,1,0:T(8,128)(2,1)S(1)}) custom-call(s32[2,8]{1,0:T(2,128)S(1)} %bitcast.18, bf16[2,1024,1024]{2,1,0:T(8,128)(2,1)S(1)} %bitcast.10, bf16[1024,256]{1,0:T(8,128)(2,1)S(1)} %bitcast.16), custom_call_target="tpu_custom_call" | custom-call | flops 1380000000 | tf_op jit(solution)/shard_map/face_maps/pallas_call | solution.py:206
  15.4 2.0 %collective-permute-start = (f32[256,256]{1,0:T(8,128)S(1)}, f32[256,256]{1,0:T(8,128)S(1)}, u32[]{:S(2)}, u32[]{:S(2)}) collective-permute-start(f32[256,256]{1,0:T(8,128)S(1)} %get-tuple-element.27), channel_id=1, source_target_pairs={{0,2},{1,3},{2,0},{3,1},{4,6},{5,7},{6,4},{7,5},{8,10},{9,11},{10,... | collective-permute-start | bytes 786440 | tf_op jit(solution)/shard_map/ppermute | solution.py:454
  17.4 0.0 collective-permute-start.4
  17.4 9.9 %collective-permute-done._map = f32[256,256]{1,0:T(8,128)S(1)} collective-permute-done((f32[256,256]{1,0:T(8,128)S(1)}, f32[256,256]{1,0:T(8,128)S(1)}, u32[]{:S(2)}, u32[]{:S(2)}) %collective-permute-start) | collective-permute-done | bytes 262176 | tf_op jit(solution)/shard_map/ppermute | solution.py:454
  27.3 0.0 all-to-all-done.received
  27.3 0.0 copy-done.2
  27.3 1.4 %source_and_face.1 = (bf16[2,1024,128]{2,1,0:T(8,128)(2,1)S(1)}, bf16[128,128]{1,0:T(8,128)(2,1)S(1)}, bf16[128,128]{1,0:T(8,128)(2,1)S(1)}, bf16[128,128]{1,0:T...) custom-call(bf16[16,136,128]{2,1,0:T(8,128)(2,1)S(1)} %all-to-all-done.rec, ...), custom_call_target="tpu_custom_call", output_to_operand_aliasing={{5}: (3, {})} | custom-call | flops 1610000000 | tf_op jit(solution)/shard_map/source_and_face/pallas_call | solution.py:304
  28.7 0.1 collective-permute-start.5
  28.8 0.5 collective-permute-start.1
  29.3 1.7 %collective-permute-start.2 = (bf16[128,128]{1,0:T(8,128)(2,1)S(1)}, bf16[128,128]{1,0:T(8,128)(2,1)S(1)}, u32[]{:S(2)}, u32[]{:S(2)}) collective-permute-start(bf16[128,128]{1,0:T(8,128)(2,1)S(1)} %get-tuple-element.30), channel_id=1, source_target_pairs={{0,2},{1,3},{2,0},{3,1},{4,6},{5,7},{6,4},{7,5},{8,10},{9,11},{10,... | collective-permute-start | bytes 98312 | tf_op jit(solution)/shard_map/ppermute | solution.py:454
  31.0 0.0 collective-permute-start.3
  31.0 0.0 collective-permute-done.4.near
  31.0 0.0 collective-permute-done.5.far
  31.0 1.5 %chain_maps.1 = (f32[256,256]{1,0:T(8,128)}, bf16[256,256]{1,0:T(8,128)(2,1)S(1)}, bf16[2,4,256,256]{3,2,1,0:T(8,128)(2,1)S(1)}) custom-call(f32[256,256]{1,0:T(8,128)S(1)} %get-tuple-element.32.own, f32[256,256]{1,0:T(8,128)S(1)} %collective-permute-done.4.near, f32[256,256]{1,0:T(8,128)S(1)} %get-tuple-element.33.across, ...), custom_call_target="tpu_custom_call" | custom-call | flops 1035000000 | tf_op jit(solution)/shard_map/chain_maps/pallas_call | solution.py:253
  32.5 0.7 %collective-permute-start.10 = (bf16[256,256]{1,0:T(8,128)(2,1)S(1)}, bf16[256,256]{1,0:T(8,128)(2,1)S(1)}, u32[]{:S(2)}, u32[]{:S(2)}) collective-permute-start(bf16[256,256]{1,0:T(8,128)(2,1)S(1)} %get-tuple-element.38), channel_id=1, source_target_pairs={{4,8},{8,12},{5,13},{6,10},{10,14},{7,15},{20,24},{24,28},{21,29},... | collective-permute-start | bytes 393224 | tf_op jit(solution)/shard_map/ppermute | solution.py:482
  33.2 1.8 %image_and_maps.2 = (f32[2,1024,128]{2,1,0:T(8,128)S(1)}, bf16[2,2,256,256]{3,2,1,0:T(8,128)(2,1)S(1)}) custom-call(bf16[2,1024,1024]{2,1,0:T(8,128)(2,1)S(1)} %bitcast.11, bf16[2,1024,128]{2,1,0:T(8,128)(2,1)S(1)} %get-tuple-element.35.refs_1_, bf16[2,4,256,256]{3,2,1,0:T(8,128)(2,1)S(1)} %get-tuple-element.34.refs_2_.parts), custom_call_target="tpu_custom_call" | custom-call | flops 2300000000 | tf_op jit(solution)/shard_map/image_and_maps/pallas_call | solution.py:375
  35.0 0.0 collective-permute-done.1.near
  35.0 0.0 collective-permute-done.2.across
  35.0 0.0 collective-permute-done.3.far
  35.0 0.9 %plane_total.1 = (bf16[128,128]{1,0:T(8,128)(2,1)S(1)}, f32[3,256,128]{2,1,0:T(8,128)S(1)}) custom-call(bf16[128,128]{1,0:T(8,128)(2,1)S(1)} %get-tuple-element.28.own, bf16[128,128]{1,0:T(8,128)(2,1)S(1)} %collective-permute-done.1.near, bf16[128,128]{1,0:T(8,128)(2,1)S(1)} %collective-permute-done.2.across, ...), custom_call_target="tpu_custom_call" | custom-call | flops 3449999872 | tf_op jit(solution)/shard_map/plane_total/pallas_call | solution.py:341
  36.0 4.1 %collective-permute-start.6 = (bf16[128,128]{1,0:T(8,128)(2,1)S(1)}, bf16[128,128]{1,0:T(8,128)(2,1)S(1)}, u32[]{:S(2)}, u32[]{:S(2)}) collective-permute-start(bf16[128,128]{1,0:T(8,128)(2,1)S(1)} %get-tuple-element.37), channel_id=1, source_target_pairs={{0,12},{1,13},{2,14},{3,15},{16,28},{17,29},{18,30},{19,31}} | collective-permute-start | bytes 98312 | tf_op jit(solution)/shard_map/ppermute | solution.py:488
  40.1 1.3 %collective-permute-start.7 = (bf16[128,128]{1,0:T(8,128)(2,1)S(1)}, bf16[128,128]{1,0:T(8,128)(2,1)S(1)}, u32[]{:S(2)}, u32[]{:S(2)}) collective-permute-start(bf16[128,128]{1,0:T(8,128)(2,1)S(1)} %get-tuple-element.37), channel_id=1, source_target_pairs={{0,4},{1,5},{2,6},{3,7},{16,20},{17,21},{18,22},{19,23}} | collective-permute-start | bytes 98312 | tf_op jit(solution)/shard_map/ppermute | solution.py:488
  41.4 1.3 %collective-permute-start.8 = (bf16[128,128]{1,0:T(8,128)(2,1)S(1)}, bf16[128,128]{1,0:T(8,128)(2,1)S(1)}, u32[]{:S(2)}, u32[]{:S(2)}) collective-permute-start(bf16[128,128]{1,0:T(8,128)(2,1)S(1)} %get-tuple-element.37), channel_id=1, source_target_pairs={{0,8},{1,9},{2,10},{3,11},{4,12},{5,13},{6,14},{7,15},{16,24},{17,... | collective-permute-start | bytes 98312 | tf_op jit(solution)/shard_map/ppermute | solution.py:488
  42.7 0.7 %collective-permute-start.9 = (bf16[128,128]{1,0:T(8,128)(2,1)S(1)}, bf16[128,128]{1,0:T(8,128)(2,1)S(1)}, u32[]{:S(2)}, u32[]{:S(2)}) collective-permute-start(bf16[128,128]{1,0:T(8,128)(2,1)S(1)} %get-tuple-element.37), channel_id=1, source_target_pairs={{4,8},{5,9},{6,10},{7,11},{8,12},{9,13},{10,14},{11,15},{20,24},{2... | collective-permute-start | bytes 98312 | tf_op jit(solution)/shard_map/ppermute | solution.py:488
  43.4 0.0 collective-permute-done.10.got
  43.4 0.1 collective-permute-start.11
  43.4 0.1 image_and_maps.3
  43.6 0.0 collective-permute-done.6.third
  43.6 0.0 collective-permute-done.7.near_one
  43.6 0.7 %collective-permute-done.8.second = bf16[128,128]{1,0:T(8,128)(2,1)S(1)} collective-permute-done((bf16[128,128]{1,0:T(8,128)(2,1)S(1)}, bf16[128,128]{1,0:T(8,128)(2,1)S(1)}, u32[]{:S(2)}, u32[]{:S(2)}) %collective-permute-start.8) | collective-permute-done | bytes 32800 | tf_op jit(solution)/shard_map/ppermute | solution.py:488
  44.3 0.0 collective-permute-done.9.far_one
  44.3 0.5 collective-permute-done.11.other
  44.8 1.1 %entering.1 = (bf16[128,128]{1,0:T(8,128)(2,1)S(1)}, bf16[128,128]{1,0:T(8,128)(2,1)S(1)}, bf16[128,128]{1,0:T(8,128)(2,1)S(1)}, bf16[128,128]{1,0:T(8,128)(2,1)S(1)}) custom-call(bf16[128,128]{1,0:T(8,128)(2,1)S(1)} %collective-permute-done.6.third, bf16[128,128]{1,0:T(8,128)(2,1)S(1)} %collective-permute-done.7.near_one, ...), custom_call_target="tpu_custom_call" | custom-call | flops 1610000000 | tf_op jit(solution)/shard_map/entering/pallas_call | solution.py:415
  45.9 0.2 collective-permute-start.12
  46.1 1.2 %collective-permute-start.13 = (bf16[128,128]{1,0:T(8,128)(2,1)S(1)}, bf16[128,128]{1,0:T(8,128)(2,1)S(1)}, u32[]{:S(2)}, u32[]{:S(2)}) collective-permute-start(bf16[128,128]{1,0:T(8,128)(2,1)S(1)} %get-tuple-element.44), channel_id=1, source_target_pairs={{0,2},{1,3},{2,0},{3,1},{4,6},{5,7},{6,4},{7,5},{8,10},{9,11},{10,... | collective-permute-start | bytes 98312 | tf_op jit(solution)/shard_map/ppermute | solution.py:454
  47.3 0.5 collective-permute-start.14
  47.8 1.9 %prop.1 = bf16[2,1024,256]{2,1,0:T(8,128)(2,1)S(1)} custom-call(s32[2,8]{1,0:T(2,128)S(1)} %bitcast.19, bf16[2,1024,1024]{2,1,0:T(8,128)(2,1)S(1)} %bitcast.13, bf16[1024,256]{1,0:T(8,128)(2,1)S(1)} %bitcast.17, bf16[128,128]{1,0:T(8,128)(2,1)S(1)} %get-tuple-element.42._tie.own), custom_call_target="tpu_custom_call" | custom-call | flops 1724999936 | tf_op jit(solution)/shard_map/prop/pallas_call | solution.py:225
  49.7 0.0 collective-permute-done.12.near
  49.7 0.3 collective-permute-done.13.across
  50.0 0.9 %collective-permute-done.14.far = bf16[128,128]{1,0:T(8,128)(2,1)S(1)} collective-permute-done((bf16[128,128]{1,0:T(8,128)(2,1)S(1)}, bf16[128,128]{1,0:T(8,128)(2,1)S(1)}, u32[]{:S(2)}, u32[]{:S(2)}) %collective-permute-start.14) | collective-permute-done | bytes 32800 | tf_op jit(solution)/shard_map/ppermute | solution.py:458
  51.0 1.3 %waves.1 = bf16[2,1024,128]{2,1,0:T(8,128)(2,1)} custom-call(bf16[128,128]{1,0:T(8,128)(2,1)S(1)} %get-tuple-element.42._tie.own, bf16[128,128]{1,0:T(8,128)(2,1)S(1)} %collective-permute-done.12.near, bf16[128,128]{1,0:T(8,128)(2,1)S(1)} %collective-permute-done.13.across, bf16[128,128]{1,0:T(8,128)(2,1)S(1)} %collective-permute-done.14.far, ...), custom_call_target="tpu_custom_call" | custom-call | flops 1495000064 | tf_op jit(solution)/shard_map/waves/pallas_call | solution.py:439
  (4 shorter events, 0.0 us)
Async XLA Ops:
  0.0 12.1 %copy-start.3 = (bf16[1,1024,256]{2,1,0:T(8,128)(2,1)S(1)}, bf16[1,1024,256]{2,1,0:T(8,128)(2,1)}, u32[]{:S(2)}) copy-start(bf16[1,1024,256]{2,1,0:T(8,128)(2,1)} %param.8) | copy-start | bytes 1572868
  0.0 12.1 %copy-start.4 = (s32[1,8,2]{1,2,0:T(2,128)S(1)}, s32[1,8,2]{1,2,0:T(2,128)}, u32[]{:S(2)}) copy-start(s32[1,8,2]{1,2,0:T(2,128)} %param.9) | copy-start | bytes 196
  4.5 22.8 %copy-start.2 = (bf16[1,2,1024,128]{3,2,1,0:T(8,128)(2,1)S(1)}, bf16[1,2,1024,128]{3,2,1,0:T(8,128)(2,1)}, u32[]{:S(2)}) copy-start(bf16[1,2,1024,128]{3,2,1,0:T(8,128)(2,1)} %param.7) | copy-start | bytes 1572868
  4.5 22.8 %all-to-all-start = ((bf16[16,136,128]{2,1,0:T(8,128)(2,1)}), bf16[16,136,128]{2,1,0:T(8,128)(2,1)S(1)}, u32[]{:S(2)}, u32[]{:S(2)}) async-start(bf16[16,136,128]{2,1,0:T(8,128)(2,1)} %pairs.1), calls=%async_computation | async-start | bytes 1114112 | tf_op jit(solution)/shard_map/all_to_all | solution.py:511
  12.1 2.2 %copy-start = (bf16[1,2,1024,1024]{3,2,1,0:T(8,128)(2,1)S(1)}, bf16[1,2,1024,1024]{3,2,1,0:T(8,128)(2,1)}, u32[]{:S(2)}) copy-start(bf16[1,2,1024,1024]{3,2,1,0:T(8,128)(2,1)} %param.6) | copy-start | bytes 12582916
  15.4 11.9 %collective-permute-start = (f32[256,256]{1,0:T(8,128)S(1)}, f32[256,256]{1,0:T(8,128)S(1)}, u32[]{:S(2)}, u32[]{:S(2)}) collective-permute-start(f32[256,256]{1,0:T(8,128)S(1)} %get-tuple-element.27), channel_id=1, source_target_pairs={{0,2},{1,3},{2,0},{3,1},{4,6},{5,7},{6,4},{7,5},{8,10},{9,11},{10,... | collective-permute-start | bytes 786440 | tf_op jit(solution)/shard_map/ppermute | solution.py:454
  17.4 13.6 %collective-permute-start.4 = (f32[256,256]{1,0:T(8,128)S(1)}, f32[256,256]{1,0:T(8,128)S(1)}, u32[]{:S(2)}, u32[]{:S(2)}) collective-permute-start(f32[256,256]{1,0:T(8,128)S(1)} %get-tuple-element.32.own), channel_id=1, source_target_pairs={{0,1},{1,0},{2,3},{3,2},{4,5},{5,4},{6,7},{7,6},{8,9},{9,8},{10,11... | collective-permute-start | bytes 786440 | tf_op jit(solution)/shard_map/ppermute | solution.py:450
  27.3 5.9 %copy-start.1 = (bf16[1,2,1024,1024]{3,2,1,0:T(8,128)(2,1)S(1)}, bf16[1,2,1024,1024]{3,2,1,0:T(8,128)(2,1)}, u32[]{:S(2)}) copy-start(bf16[1,2,1024,1024]{3,2,1,0:T(8,128)(2,1)} %param.6) | copy-start | bytes 12582916
  28.7 2.3 %collective-permute-start.5 = (f32[256,256]{1,0:T(8,128)S(1)}, f32[256,256]{1,0:T(8,128)S(1)}, u32[]{:S(2)}, u32[]{:S(2)}) collective-permute-start(f32[256,256]{1,0:T(8,128)S(1)} %get-tuple-element.33.across), channel_id=1, source_target_pairs={{0,1},{1,0},{2,3},{3,2},{4,5},{5,4},{6,7},{7,6},{8,9},{9,8},{10,11... | collective-permute-start | bytes 786440 | tf_op jit(solution)/shard_map/ppermute | solution.py:450
  28.8 6.2 %collective-permute-start.1 = (bf16[128,128]{1,0:T(8,128)(2,1)S(1)}, bf16[128,128]{1,0:T(8,128)(2,1)S(1)}, u32[]{:S(2)}, u32[]{:S(2)}) collective-permute-start(bf16[128,128]{1,0:T(8,128)(2,1)S(1)} %get-tuple-element.29), channel_id=1, source_target_pairs={{0,1},{1,0},{2,3},{3,2},{4,5},{5,4},{6,7},{7,6},{8,9},{9,8},{10,11... | collective-permute-start | bytes 98312 | tf_op jit(solution)/shard_map/ppermute | solution.py:450
  29.3 5.7 %collective-permute-start.2 = (bf16[128,128]{1,0:T(8,128)(2,1)S(1)}, bf16[128,128]{1,0:T(8,128)(2,1)S(1)}, u32[]{:S(2)}, u32[]{:S(2)}) collective-permute-start(bf16[128,128]{1,0:T(8,128)(2,1)S(1)} %get-tuple-element.30), channel_id=1, source_target_pairs={{0,2},{1,3},{2,0},{3,1},{4,6},{5,7},{6,4},{7,5},{8,10},{9,11},{10,... | collective-permute-start | bytes 98312 | tf_op jit(solution)/shard_map/ppermute | solution.py:454
  31.0 4.0 %collective-permute-start.3 = (bf16[128,128]{1,0:T(8,128)(2,1)S(1)}, bf16[128,128]{1,0:T(8,128)(2,1)S(1)}, u32[]{:S(2)}, u32[]{:S(2)}) collective-permute-start(bf16[128,128]{1,0:T(8,128)(2,1)S(1)} %get-tuple-element.31), channel_id=1, source_target_pairs={{0,3},{1,2},{2,1},{3,0},{4,7},{5,6},{6,5},{7,4},{8,11},{9,10},{10,... | collective-permute-start | bytes 98312 | tf_op jit(solution)/shard_map/ppermute | solution.py:458
  32.5 10.8 %collective-permute-start.10 = (bf16[256,256]{1,0:T(8,128)(2,1)S(1)}, bf16[256,256]{1,0:T(8,128)(2,1)S(1)}, u32[]{:S(2)}, u32[]{:S(2)}) collective-permute-start(bf16[256,256]{1,0:T(8,128)(2,1)S(1)} %get-tuple-element.38), channel_id=1, source_target_pairs={{4,8},{8,12},{5,13},{6,10},{10,14},{7,15},{20,24},{24,28},{21,29},... | collective-permute-start | bytes 393224 | tf_op jit(solution)/shard_map/ppermute | solution.py:482
  36.0 7.6 %collective-permute-start.6 = (bf16[128,128]{1,0:T(8,128)(2,1)S(1)}, bf16[128,128]{1,0:T(8,128)(2,1)S(1)}, u32[]{:S(2)}, u32[]{:S(2)}) collective-permute-start(bf16[128,128]{1,0:T(8,128)(2,1)S(1)} %get-tuple-element.37), channel_id=1, source_target_pairs={{0,12},{1,13},{2,14},{3,15},{16,28},{17,29},{18,30},{19,31}} | collective-permute-start | bytes 98312 | tf_op jit(solution)/shard_map/ppermute | solution.py:488
  40.1 3.5 %collective-permute-start.7 = (bf16[128,128]{1,0:T(8,128)(2,1)S(1)}, bf16[128,128]{1,0:T(8,128)(2,1)S(1)}, u32[]{:S(2)}, u32[]{:S(2)}) collective-permute-start(bf16[128,128]{1,0:T(8,128)(2,1)S(1)} %get-tuple-element.37), channel_id=1, source_target_pairs={{0,4},{1,5},{2,6},{3,7},{16,20},{17,21},{18,22},{19,23}} | collective-permute-start | bytes 98312 | tf_op jit(solution)/shard_map/ppermute | solution.py:488
  41.4 2.9 %collective-permute-start.8 = (bf16[128,128]{1,0:T(8,128)(2,1)S(1)}, bf16[128,128]{1,0:T(8,128)(2,1)S(1)}, u32[]{:S(2)}, u32[]{:S(2)}) collective-permute-start(bf16[128,128]{1,0:T(8,128)(2,1)S(1)} %get-tuple-element.37), channel_id=1, source_target_pairs={{0,8},{1,9},{2,10},{3,11},{4,12},{5,13},{6,14},{7,15},{16,24},{17,... | collective-permute-start | bytes 98312 | tf_op jit(solution)/shard_map/ppermute | solution.py:488
  42.7 1.6 %collective-permute-start.9 = (bf16[128,128]{1,0:T(8,128)(2,1)S(1)}, bf16[128,128]{1,0:T(8,128)(2,1)S(1)}, u32[]{:S(2)}, u32[]{:S(2)}) collective-permute-start(bf16[128,128]{1,0:T(8,128)(2,1)S(1)} %get-tuple-element.37), channel_id=1, source_target_pairs={{4,8},{5,9},{6,10},{7,11},{8,12},{9,13},{10,14},{11,15},{20,24},{2... | collective-permute-start | bytes 98312 | tf_op jit(solution)/shard_map/ppermute | solution.py:488
  43.4 1.4 %collective-permute-start.11 = (bf16[256,256]{1,0:T(8,128)(2,1)S(1)}, bf16[256,256]{1,0:T(8,128)(2,1)S(1)}, u32[]{:S(2)}, u32[]{:S(2)}) collective-permute-start(bf16[256,256]{1,0:T(8,128)(2,1)S(1)} %collective-permute-done.10.got), channel_id=1, source_target_pairs={{0,1},{1,0},{2,3},{3,2},{4,5},{5,4},{6,7},{7,6},{8,9},{9,8},{10,11... | collective-permute-start | bytes 393224 | tf_op jit(solution)/shard_map/ppermute | solution.py:450
  45.9 3.8 %collective-permute-start.12 = (bf16[128,128]{1,0:T(8,128)(2,1)S(1)}, bf16[128,128]{1,0:T(8,128)(2,1)S(1)}, u32[]{:S(2)}, u32[]{:S(2)}) collective-permute-start(bf16[128,128]{1,0:T(8,128)(2,1)S(1)} %get-tuple-element.43), channel_id=1, source_target_pairs={{0,1},{1,0},{2,3},{3,2},{4,5},{5,4},{6,7},{7,6},{8,9},{9,8},{10,11... | collective-permute-start | bytes 98312 | tf_op jit(solution)/shard_map/ppermute | solution.py:450
  46.1 3.9 %collective-permute-start.13 = (bf16[128,128]{1,0:T(8,128)(2,1)S(1)}, bf16[128,128]{1,0:T(8,128)(2,1)S(1)}, u32[]{:S(2)}, u32[]{:S(2)}) collective-permute-start(bf16[128,128]{1,0:T(8,128)(2,1)S(1)} %get-tuple-element.44), channel_id=1, source_target_pairs={{0,2},{1,3},{2,0},{3,1},{4,6},{5,7},{6,4},{7,5},{8,10},{9,11},{10,... | collective-permute-start | bytes 98312 | tf_op jit(solution)/shard_map/ppermute | solution.py:454
  47.3 3.6 %collective-permute-start.14 = (bf16[128,128]{1,0:T(8,128)(2,1)S(1)}, bf16[128,128]{1,0:T(8,128)(2,1)S(1)}, u32[]{:S(2)}, u32[]{:S(2)}) collective-permute-start(bf16[128,128]{1,0:T(8,128)(2,1)S(1)} %get-tuple-element.45), channel_id=1, source_target_pairs={{0,3},{1,2},{2,1},{3,0},{4,7},{5,6},{6,5},{7,4},{8,11},{9,10},{10,... | collective-permute-start | bytes 98312 | tf_op jit(solution)/shard_map/ppermute | solution.py:458

commit v20 on v19

--- a/solution.py
+++ b/solution.py
@@ -52,7 +52,7 @@
 def partners():
     here = place()
     across = (here + CORES) % GROUP
-    return here, here ^ 1, across, across ^ 1
+    return here, across ^ 1, across, here ^ 1
 
 
 def dot(a, b):
@@ -236,31 +236,29 @@
     return dot(a[0], b[0]) + (dot(a[0], b[1]) + dot(a[1], b[0]))
 
 
-def chain_kernel(own, near, across, far, total_out, sent_out, parts, maps):
-    collect((own, near, across, far), maps)
+def chain_kernel(own, far, across, near, total_out, parts, maps):
+    collect((own, far, across, near), maps)
     split = [two_parts(maps[j]) for j in range(GROUP)]
     lower, upper = two_parts(times(split[1], split[0])), two_parts(times(split[3], split[2]))
-    total = times(upper, lower)
-    total_out[...] = total
-    sent_out[...] = total.astype(BF16)
+    total_out[...] = times(upper, lower).astype(total_out.dtype)
     for j, (high, low) in enumerate(split):
         parts[0, j] = high
         parts[1, j] = low
 
 
-def chain(maps):
+def chain(maps, dtype):
     face = maps[0].shape[0]
     return call(
         chain_kernel,
         "chain_maps",
         [IN_VMEM] * GROUP,
-        [shape(face, face, dtype=F32), shape(face, face), shape(2, GROUP, face, face)],
+        [shape(face, face, dtype=dtype), shape(2, GROUP, face, face)],
         [pltpu.VMEM((GROUP, face, face), F32)],
         0.9,
     )(*maps)
 
 
-def source_kernel(received, inject, face_rows, _map, source, own, near, across, far, _same_map, quarters, total, heads, targets, sem):
+def source_kernel(received, inject, face_rows, _map, source, own, far, across, near, _same_map, quarters, total, heads, targets, sem):
     energies, orbitals, columns = inject.shape
     sections = received.shape[0]
     half = quarters.shape[1]
@@ -293,7 +291,7 @@
         quarters[e * split] = pack(tall)
         second = jnp.where(left_lanes(tall[:half]), swap_lanes(tall[:half]), tall[half:])
         quarters[e * split + 1] = second
-    for out, at in zip((own, near, across, far), partners()):
+    for out, at in zip((own, far, across, near), partners()):
         out[...] = quarters[at].astype(BF16)
 
 
@@ -327,8 +325,8 @@
     return unpack(shift.astype(F32)) + times((parts[0, j], parts[1, j]), two_parts(state))
 
 
-def total_kernel(own, near, across, far, parts, _image, out, local, shifts):
-    collect((own, near, across, far), shifts)
+def total_kernel(own, far, across, near, parts, _image, out, local, shifts):
+    collect((own, far, across, near), shifts)
     state = unpack(shifts[0].astype(F32))
     for j in range(1, GROUP):
         local[j - 1] = state
@@ -422,27 +420,44 @@
     )(*args)
 
 
-def waves_kernel(own, near, across, far, prop, image, out, arrived):
-    collect((own, near, across, far), arrived)
-    split = GROUP // prop.shape[0]
-    for e in range(prop.shape[0]):
-        near, far = arrived[e * split].astype(F32), arrived[e * split + 1].astype(F32)
-        left = left_lanes(near)
-        top = jnp.where(left, near, swap_lanes(far))
-        low = jnp.where(left, swap_lanes(near), far)
+def waves_kernel(own, far, across, near, prop, image, out, arrived, wave, sem):
+    collect((own, far, across, near), arrived)
+    energies, orbitals, _ = prop.shape
+    split = GROUP // energies
+    pieces = sem.shape[1]
+    size = orbitals // pieces
+    moves = []
+    for e in range(energies):
+        first, second = arrived[e * split].astype(F32), arrived[e * split + 1].astype(F32)
+        left = left_lanes(first)
+        top = jnp.where(left, first, swap_lanes(second))
+        low = jnp.where(left, swap_lanes(first), second)
         incoming = jnp.concatenate([top, low], axis=0).astype(BF16)
-        out[e] = (dot(prop[e], incoming) + image[e]).astype(BF16)
+        for c in range(pieces):
+            at = slice(c * size, (c + 1) * size)
+            wave[e, at, :] = (dot(prop[e, at, :], incoming) + image[e, at, :]).astype(BF16)
+            moves.append(pltpu.make_async_copy(wave.at[e, pl.ds(c * size, size)], out.at[e, pl.ds(c * size, size)], sem.at[e, c]))
+            moves[-1].start()
+    for move in moves:
+        move.wait()
 
 
 def final_waves(arrived, prop, image):
     half, columns = arrived[0].shape
-    return call(
+    energies = prop.shape[0]
+    return pl.pallas_call(
         waves_kernel,
-        "waves",
-        [IN_VMEM] * (GROUP + 2),
-        shape(*image.shape),
-        [pltpu.VMEM((GROUP, half, columns), BF16)],
-        1.3,
+        name="waves",
+        in_specs=[IN_VMEM] * (GROUP + 2),
+        out_shape=shape(*image.shape),
+        out_specs=IN_HBM,
+        scratch_shapes=[
+            pltpu.VMEM((GROUP, half, columns), BF16),
+            pltpu.VMEM(image.shape, BF16),
+            pltpu.SemaphoreType.DMA((energies, 2)),
+        ],
+        compiler_params=pltpu.CompilerParams(vmem_limit_bytes=VMEM_SMALL),
+        cost_estimate=pl.CostEstimate(flops=int(1.3 * PEAK), bytes_accessed=0, transcendentals=0),
     )(*arrived, prop, image)
 
 
@@ -458,9 +473,8 @@
     return lax.ppermute(item, "sec", [(s, s // GROUP * GROUP + (s % GROUP + CORES) % GROUP ^ 1) for s in range(sections)])
 
 
-def exchange(own, near, across, far, sections):
-    across, far = to_across(across, sections), to_far(far, sections)
-    return [own, to_near(near, sections), across, far]
+def exchange(own, far, across, near, sections):
+    return [own, to_far(far, sections), to_across(across, sections), to_near(near, sections)]
 
 
 def up_shift(sections, k):
@@ -518,9 +532,9 @@
     shifts = exchange(*quarters, sections)
     far = to_near(across, sections)
     four = sections // GROUP == 4
-    whole, sent, parts = chain([own_map, near, across, far])
+    total_map, parts = chain([own_map, far, across, near], BF16 if four else F32)
     early = image_and_maps(green, source, parts)
-    maps = maps_up(sent, sections) if four else []
+    maps = maps_up(total_map, sections) if four else []
     total, local = plane_total(shifts, parts, early[0])
     if four:
         fourth = between(total, (1, 2), (2, 3))
@@ -530,7 +544,7 @@
         image, upto = image_and_maps(green, source, parts, early)
         entered = entering(entering_kernel, (first, second, third, fourth, *maps, parts, upto, local))
     else:
-        base = scan_below(whole, total, sections)
+        base = scan_below(total_map, total, sections)
         image, upto = image_and_maps(green, source, parts, early)
         entered = entering(entering_from_kernel, (base, parts, upto, local))
     arrived = exchange(*entered, sections)

time: 52.7 us -> 51.8 us (0.983)
  Pallas kernels: 15.7 us -> 14.9 us
    ppermute x2, starting transfers between devices: 0.48 us -> 2.28 us  [to_far(): lax.ppermute(item, 'sec', [(s, s // GROUP * GROUP + (s % GROUP + CORES) %...]
    ppermute x3, starting transfers between devices: 4.89 us -> 3.71 us  [to_across(): lax.ppermute(item, 'sec', [(s, s // GROUP * GROUP + (s % GROUP + CORES) %...]
    ppermute x2, waiting for transfers between devices: 0.95 us -> 0.01 us  [to_far(): lax.ppermute(item, 'sec', [(s, s // GROUP * GROUP + (s % GROUP + CORES) %...]
    pallas_call x1, Pallas kernels: 1.54 us -> 0.83 us  [chain(): call(chain_kernel, 'chain_maps', [IN_VMEM] * GROUP, [shape(face, face, dt...]
    ppermute x5, starting transfers between devices: 0.86 us -> 0.22 us  [to_near(): return lax.ppermute(item, 'sec', [(s, s ^ 1) for s in range(sections)])]
  transfers between devices with their start and end apart: 16 -> 16, of which waited for: 5 -> 5; matrix products, arithmetic and copies ran while one was open for 0% -> 0% of each run, Pallas kernels for 17% -> 16%
where the time goes in v20:
time: 51.8 us; the launch traced here: 51.4 us
  starting transfers between devices  22.1 us (43%)
  Pallas kernels  14.9 us (29%)
  waiting for transfers between devices  11.9 us (23%)
  local copies, waits for them, and re-layouts  2.2 us (4%)
    ppermute x3, waiting for transfers between devices, to_across(): lax.ppermute(item, 'sec', [(s, s // GROUP * GROUP + (s % GROUP + CORES) %...  10.7 us
    ppermute x4, starting transfers between devices, between(): return lax.ppermute(item, 'sec', pairs)  7.74 us
    all_to_all x1, starting transfers between devices, per_device(): lax.all_to_all(outgoing, 'sec', split_axis=0, concat_axis=0, tiled=True)  7.48 us
    pallas_call x1, Pallas kernels, outgoing_pairs(): call(pairs_kernel, 'pairs', [IN_HBM] * 4, shape(sections, CAP * energies...  4.46 us
    ppermute x3, starting transfers between devices, to_across(): lax.ppermute(item, 'sec', [(s, s // GROUP * GROUP + (s % GROUP + CORES) %...  3.71 us
    ppermute x2, starting transfers between devices, to_far(): lax.ppermute(item, 'sec', [(s, s // GROUP * GROUP + (s % GROUP + CORES) %...  2.28 us
    unnamed x10, local copies, waits for them, and re-layouts  2.2 us
    pallas_call x2, Pallas kernels, image_and_maps(): call(functools.partial(work_kernel, not held), 'image_and_maps', [IN_VMEM...  1.91 us
  transfers between devices with their start and end apart: 16, of which 5 were waited for; matrix products, arithmetic and copies ran while one was open for 0% of the time, Pallas kernels for 16%

profile of v20, /device:TPU:0, one launch (start us, length us, event | category | flops | bytes accessed | tf_op | source)
XLA Modules:
  0.0 51.4 jit_solution(3501741224683864359)
XLA Ops:
  0.0 4.5 %pairs.1 = bf16[16,136,128]{2,1,0:T(8,128)(2,1)} custom-call(s32[16]{0:T(128)} %bitcast.21, s32[2,16]{1,0:T(2,128)} %bitcast.20, bf16[2,1024,1024]{2,1,0:T(8,128)(2,1)} %bitcast.9, bf16[2,1024,128]{2,1,0:T(8,128)(2,1)} %bitcast.14), custom_call_target="tpu_custom_call" | custom-call | flops 4600000000 | tf_op jit(solution)/shard_map/pairs/pallas_call | solution.py:168
  4.5 0.0 copy-start.2
  4.5 7.5 %all-to-all-start = ((bf16[16,136,128]{2,1,0:T(8,128)(2,1)}), bf16[16,136,128]{2,1,0:T(8,128)(2,1)S(1)}, u32[]{:S(2)}, u32[]{:S(2)}) async-start(bf16[16,136,128]{2,1,0:T(8,128)(2,1)} %pairs.1), calls=%async_computation | async-start | bytes 1114112 | tf_op jit(solution)/shard_map/all_to_all | solution.py:525
  12.0 0.0 copy-done.3
  12.0 0.0 copy-done.4
  12.0 0.0 copy-start
  12.0 2.2 %copy-done = bf16[1,2,1024,1024]{3,2,1,0:T(8,128)(2,1)S(1)} copy-done((bf16[1,2,1024,1024]{3,2,1,0:T(8,128)(2,1)S(1)}, bf16[1,2,1024,1024]{3,2,1,0:T(8,128)(2,1)}, u32[]{:S(2)}) %copy-start) | copy-done | bytes 4194328
  14.2 1.1 %face_maps.1 = (f32[256,256]{1,0:T(8,128)S(1)}, f32[256,256]{1,0:T(8,128)S(1)}, bf16[2,256,1024]{2,1,0:T(8,128)(2,1)S(1)}) custom-call(s32[2,8]{1,0:T(2,128)S(1)} %bitcast.18, bf16[2,1024,1024]{2,1,0:T(8,128)(2,1)S(1)} %bitcast.10, bf16[1024,256]{1,0:T(8,128)(2,1)S(1)} %bitcast.16), custom_call_target="tpu_custom_call" | custom-call | flops 1380000000 | tf_op jit(solution)/shard_map/face_maps/pallas_call | solution.py:206
  15.3 2.0 %collective-permute-start = (f32[256,256]{1,0:T(8,128)S(1)}, f32[256,256]{1,0:T(8,128)S(1)}, u32[]{:S(2)}, u32[]{:S(2)}) collective-permute-start(f32[256,256]{1,0:T(8,128)S(1)} %get-tuple-element.27), channel_id=1, source_target_pairs={{0,2},{1,3},{2,0},{3,1},{4,6},{5,7},{6,4},{7,5},{8,10},{9,11},{10,... | collective-permute-start | bytes 786440 | tf_op jit(solution)/shard_map/ppermute | solution.py:469
  17.3 0.0 collective-permute-start.5
  17.3 9.9 %collective-permute-done._map = f32[256,256]{1,0:T(8,128)S(1)} collective-permute-done((f32[256,256]{1,0:T(8,128)S(1)}, f32[256,256]{1,0:T(8,128)S(1)}, u32[]{:S(2)}, u32[]{:S(2)}) %collective-permute-start) | collective-permute-done | bytes 262176 | tf_op jit(solution)/shard_map/ppermute | solution.py:469
  27.2 0.0 all-to-all-done.received
  27.2 0.0 copy-done.2
  27.2 1.4 %source_and_face.1 = (bf16[2,1024,128]{2,1,0:T(8,128)(2,1)S(1)}, bf16[128,128]{1,0:T(8,128)(2,1)S(1)}, bf16[128,128]{1,0:T(8,128)(2,1)S(1)}, bf16[128,128]{1,0:T...) custom-call(bf16[16,136,128]{2,1,0:T(8,128)(2,1)S(1)} %all-to-all-done.rec, ...), custom_call_target="tpu_custom_call", output_to_operand_aliasing={{5}: (3, {})} | custom-call | flops 1610000000 | tf_op jit(solution)/shard_map/source_and_face/pallas_call | solution.py:302
  28.6 0.1 collective-permute-start.4
  28.7 1.8 %collective-permute-start.1 = (bf16[128,128]{1,0:T(8,128)(2,1)S(1)}, bf16[128,128]{1,0:T(8,128)(2,1)S(1)}, u32[]{:S(2)}, u32[]{:S(2)}) collective-permute-start(bf16[128,128]{1,0:T(8,128)(2,1)S(1)} %get-tuple-element.29), channel_id=1, source_target_pairs={{0,3},{1,2},{2,1},{3,0},{4,7},{5,6},{6,5},{7,4},{8,11},{9,10},{10,... | collective-permute-start | bytes 98312 | tf_op jit(solution)/shard_map/ppermute | solution.py:473
  30.5 0.4 collective-permute-start.2
  30.9 0.0 collective-permute-start.3
  30.9 0.0 collective-permute-done.5.near
  30.9 0.0 collective-permute-done.4.far
  30.9 0.8 %chain_maps.1 = (bf16[256,256]{1,0:T(8,128)(2,1)S(1)}, bf16[2,4,256,256]{3,2,1,0:T(8,128)(2,1)S(1)}) custom-call(f32[256,256]{1,0:T(8,128)S(1)} %get-tuple-element.32.own, f32[256,256]{1,0:T(8,128)S(1)} %collective-permute-done.4.far, f32[256,256]{1,0:T(8,128)S(1)} %get-tuple-element.33.across, f32[256,256]{1,0:T(8,128)S(1)} %collective-permute-done.5.near), custom_call_target="tpu_custom_call" | custom-call | flops 1035000000 | tf_op jit(solution)/shard_map/chain_maps/pallas_call | solution.py:251
  31.7 0.7 %collective-permute-start.10 = (bf16[256,256]{1,0:T(8,128)(2,1)S(1)}, bf16[256,256]{1,0:T(8,128)(2,1)S(1)}, u32[]{:S(2)}, u32[]{:S(2)}) collective-permute-start(bf16[256,256]{1,0:T(8,128)(2,1)S(1)} %get-tuple-element.38), channel_id=1, source_target_pairs={{4,8},{8,12},{5,13},{6,10},{10,14},{7,15},{20,24},{24,28},{21,29},... | collective-permute-start | bytes 393224 | tf_op jit(solution)/shard_map/ppermute | solution.py:496
  32.4 1.8 %image_and_maps.2 = (f32[2,1024,128]{2,1,0:T(8,128)S(1)}, bf16[2,2,256,256]{3,2,1,0:T(8,128)(2,1)S(1)}) custom-call(bf16[2,1024,1024]{2,1,0:T(8,128)(2,1)S(1)} %bitcast.11, bf16[2,1024,128]{2,1,0:T(8,128)(2,1)S(1)} %get-tuple-element.35.refs_1_, bf16[2,4,256,256]{3,2,1,0:T(8,128)(2,1)S(1)} %get-tuple-element.34.refs_2_.parts), custom_call_target="tpu_custom_call" | custom-call | flops 2300000000 | tf_op jit(solution)/shard_map/image_and_maps/pallas_call | solution.py:373
  34.2 0.0 collective-permute-done.1.far
  34.2 0.2 collective-permute-done.2.across
  34.4 0.0 collective-permute-done.3.near
  34.4 0.9 %plane_total.1 = (bf16[128,128]{1,0:T(8,128)(2,1)S(1)}, f32[3,256,128]{2,1,0:T(8,128)S(1)}) custom-call(bf16[128,128]{1,0:T(8,128)(2,1)S(1)} %get-tuple-element.28.own, bf16[128,128]{1,0:T(8,128)(2,1)S(1)} %collective-permute-done.1.far, bf16[128,128]{1,0:T(8,128)(2,1)S(1)} %collective-permute-done.2.across, ...), custom_call_target="tpu_custom_call" | custom-call | flops 3449999872 | tf_op jit(solution)/shard_map/plane_total/pallas_call | solution.py:339
  35.4 4.5 %collective-permute-start.6 = (bf16[128,128]{1,0:T(8,128)(2,1)S(1)}, bf16[128,128]{1,0:T(8,128)(2,1)S(1)}, u32[]{:S(2)}, u32[]{:S(2)}) collective-permute-start(bf16[128,128]{1,0:T(8,128)(2,1)S(1)} %get-tuple-element.37), channel_id=1, source_target_pairs={{0,12},{1,13},{2,14},{3,15},{16,28},{17,29},{18,30},{19,31}} | collective-permute-start | bytes 98312 | tf_op jit(solution)/shard_map/ppermute | solution.py:502
  39.9 1.3 %collective-permute-start.7 = (bf16[128,128]{1,0:T(8,128)(2,1)S(1)}, bf16[128,128]{1,0:T(8,128)(2,1)S(1)}, u32[]{:S(2)}, u32[]{:S(2)}) collective-permute-start(bf16[128,128]{1,0:T(8,128)(2,1)S(1)} %get-tuple-element.37), channel_id=1, source_target_pairs={{0,4},{1,5},{2,6},{3,7},{16,20},{17,21},{18,22},{19,23}} | collective-permute-start | bytes 98312 | tf_op jit(solution)/shard_map/ppermute | solution.py:502
  41.2 1.3 %collective-permute-start.8 = (bf16[128,128]{1,0:T(8,128)(2,1)S(1)}, bf16[128,128]{1,0:T(8,128)(2,1)S(1)}, u32[]{:S(2)}, u32[]{:S(2)}) collective-permute-start(bf16[128,128]{1,0:T(8,128)(2,1)S(1)} %get-tuple-element.37), channel_id=1, source_target_pairs={{0,8},{1,9},{2,10},{3,11},{4,12},{5,13},{6,14},{7,15},{16,24},{17,... | collective-permute-start | bytes 98312 | tf_op jit(solution)/shard_map/ppermute | solution.py:502
  42.5 0.7 %collective-permute-start.9 = (bf16[128,128]{1,0:T(8,128)(2,1)S(1)}, bf16[128,128]{1,0:T(8,128)(2,1)S(1)}, u32[]{:S(2)}, u32[]{:S(2)}) collective-permute-start(bf16[128,128]{1,0:T(8,128)(2,1)S(1)} %get-tuple-element.37), channel_id=1, source_target_pairs={{4,8},{5,9},{6,10},{7,11},{8,12},{9,13},{10,14},{11,15},{20,24},{2... | collective-permute-start | bytes 98312 | tf_op jit(solution)/shard_map/ppermute | solution.py:502
  43.1 0.0 collective-permute-done.10.got
  43.1 0.1 collective-permute-start.11
  43.2 0.1 image_and_maps.3
  43.4 0.0 collective-permute-done.6.third
  43.4 0.0 collective-permute-done.7.near_one
  43.4 0.7 %collective-permute-done.8.second = bf16[128,128]{1,0:T(8,128)(2,1)S(1)} collective-permute-done((bf16[128,128]{1,0:T(8,128)(2,1)S(1)}, bf16[128,128]{1,0:T(8,128)(2,1)S(1)}, u32[]{:S(2)}, u32[]{:S(2)}) %collective-permute-start.8) | collective-permute-done | bytes 32800 | tf_op jit(solution)/shard_map/ppermute | solution.py:502
  44.0 0.0 collective-permute-done.9.far_one
  44.0 0.5 collective-permute-done.11.other
  44.6 1.1 %entering.1 = (bf16[128,128]{1,0:T(8,128)(2,1)S(1)}, bf16[128,128]{1,0:T(8,128)(2,1)S(1)}, bf16[128,128]{1,0:T(8,128)(2,1)S(1)}, bf16[128,128]{1,0:T(8,128)(2,1)S(1)}) custom-call(bf16[128,128]{1,0:T(8,128)(2,1)S(1)} %collective-permute-done.6.third, bf16[128,128]{1,0:T(8,128)(2,1)S(1)} %collective-permute-done.7.near_one, ...), custom_call_target="tpu_custom_call" | custom-call | flops 1610000000 | tf_op jit(solution)/shard_map/entering/pallas_call | solution.py:413
  45.6 0.5 collective-permute-start.12
  46.2 1.4 %collective-permute-start.13 = (bf16[128,128]{1,0:T(8,128)(2,1)S(1)}, bf16[128,128]{1,0:T(8,128)(2,1)S(1)}, u32[]{:S(2)}, u32[]{:S(2)}) collective-permute-start(bf16[128,128]{1,0:T(8,128)(2,1)S(1)} %get-tuple-element.44), channel_id=1, source_target_pairs={{0,2},{1,3},{2,0},{3,1},{4,6},{5,7},{6,4},{7,5},{8,10},{9,11},{10,... | collective-permute-start | bytes 98312 | tf_op jit(solution)/shard_map/ppermute | solution.py:469
  47.5 0.1 collective-permute-start.14
  47.6 1.9 %prop.1 = bf16[2,1024,256]{2,1,0:T(8,128)(2,1)S(1)} custom-call(s32[2,8]{1,0:T(2,128)S(1)} %bitcast.19, bf16[2,1024,1024]{2,1,0:T(8,128)(2,1)S(1)} %bitcast.13, bf16[1024,256]{1,0:T(8,128)(2,1)S(1)} %bitcast.17, bf16[128,128]{1,0:T(8,128)(2,1)S(1)} %get-tuple-element.42._tie.own), custom_call_target="tpu_custom_call" | custom-call | flops 1724999936 | tf_op jit(solution)/shard_map/prop/pallas_call | solution.py:225
  49.5 0.0 collective-permute-done.12.far
  49.5 0.6 %collective-permute-done.13.across = bf16[128,128]{1,0:T(8,128)(2,1)S(1)} collective-permute-done((bf16[128,128]{1,0:T(8,128)(2,1)S(1)}, bf16[128,128]{1,0:T(8,128)(2,1)S(1)}, u32[]{:S(2)}, u32[]{:S(2)}) %collective-permute-start.13) | collective-permute-done | bytes 32800 | tf_op jit(solution)/shard_map/ppermute | solution.py:469
  50.1 0.0 collective-permute-done.14.near
  50.1 1.3 %waves.1 = bf16[2,1024,128]{2,1,0:T(8,128)(2,1)} custom-call(bf16[128,128]{1,0:T(8,128)(2,1)S(1)} %get-tuple-element.42._tie.own, bf16[128,128]{1,0:T(8,128)(2,1)S(1)} %collective-permute-done.12.far, bf16[128,128]{1,0:T(8,128)(2,1)S(1)} %collective-permute-done.13.across, bf16[128,128]{1,0:T(8,128)(2,1)S(1)} %collective-permute-done.14.near, ...), custom_call_target="tpu_custom_call" | custom-call | flops 1495000064 | tf_op jit(solution)/shard_map/waves/pallas_call | solution.py:448
  (4 shorter events, 0.0 us)
Async XLA Ops:
  0.0 12.0 %copy-start.3 = (bf16[1,1024,256]{2,1,0:T(8,128)(2,1)S(1)}, bf16[1,1024,256]{2,1,0:T(8,128)(2,1)}, u32[]{:S(2)}) copy-start(bf16[1,1024,256]{2,1,0:T(8,128)(2,1)} %param.8) | copy-start | bytes 1572868
  0.0 12.0 %copy-start.4 = (s32[1,8,2]{1,2,0:T(2,128)S(1)}, s32[1,8,2]{1,2,0:T(2,128)}, u32[]{:S(2)}) copy-start(s32[1,8,2]{1,2,0:T(2,128)} %param.9) | copy-start | bytes 196
  4.5 22.7 %copy-start.2 = (bf16[1,2,1024,128]{3,2,1,0:T(8,128)(2,1)S(1)}, bf16[1,2,1024,128]{3,2,1,0:T(8,128)(2,1)}, u32[]{:S(2)}) copy-start(bf16[1,2,1024,128]{3,2,1,0:T(8,128)(2,1)} %param.7) | copy-start | bytes 1572868
  4.5 22.7 %all-to-all-start = ((bf16[16,136,128]{2,1,0:T(8,128)(2,1)}), bf16[16,136,128]{2,1,0:T(8,128)(2,1)S(1)}, u32[]{:S(2)}, u32[]{:S(2)}) async-start(bf16[16,136,128]{2,1,0:T(8,128)(2,1)} %pairs.1), calls=%async_computation | async-start | bytes 1114112 | tf_op jit(solution)/shard_map/all_to_all | solution.py:525
  12.0 2.2 %copy-start = (bf16[1,2,1024,1024]{3,2,1,0:T(8,128)(2,1)S(1)}, bf16[1,2,1024,1024]{3,2,1,0:T(8,128)(2,1)}, u32[]{:S(2)}) copy-start(bf16[1,2,1024,1024]{3,2,1,0:T(8,128)(2,1)} %param.6) | copy-start | bytes 12582916
  15.3 11.9 %collective-permute-start = (f32[256,256]{1,0:T(8,128)S(1)}, f32[256,256]{1,0:T(8,128)S(1)}, u32[]{:S(2)}, u32[]{:S(2)}) collective-permute-start(f32[256,256]{1,0:T(8,128)S(1)} %get-tuple-element.27), channel_id=1, source_target_pairs={{0,2},{1,3},{2,0},{3,1},{4,6},{5,7},{6,4},{7,5},{8,10},{9,11},{10,... | collective-permute-start | bytes 786440 | tf_op jit(solution)/shard_map/ppermute | solution.py:469
  17.3 13.6 %collective-permute-start.5 = (f32[256,256]{1,0:T(8,128)S(1)}, f32[256,256]{1,0:T(8,128)S(1)}, u32[]{:S(2)}, u32[]{:S(2)}) collective-permute-start(f32[256,256]{1,0:T(8,128)S(1)} %get-tuple-element.32.own), channel_id=1, source_target_pairs={{0,1},{1,0},{2,3},{3,2},{4,5},{5,4},{6,7},{7,6},{8,9},{9,8},{10,11... | collective-permute-start | bytes 786440 | tf_op jit(solution)/shard_map/ppermute | solution.py:465
  27.2 5.2 %copy-start.1 = (bf16[1,2,1024,1024]{3,2,1,0:T(8,128)(2,1)S(1)}, bf16[1,2,1024,1024]{3,2,1,0:T(8,128)(2,1)}, u32[]{:S(2)}) copy-start(bf16[1,2,1024,1024]{3,2,1,0:T(8,128)(2,1)} %param.6) | copy-start | bytes 12582916
  28.6 2.2 %collective-permute-start.4 = (f32[256,256]{1,0:T(8,128)S(1)}, f32[256,256]{1,0:T(8,128)S(1)}, u32[]{:S(2)}, u32[]{:S(2)}) collective-permute-start(f32[256,256]{1,0:T(8,128)S(1)} %get-tuple-element.33.across), channel_id=1, source_target_pairs={{0,1},{1,0},{2,3},{3,2},{4,5},{5,4},{6,7},{7,6},{8,9},{9,8},{10,11... | collective-permute-start | bytes 786440 | tf_op jit(solution)/shard_map/ppermute | solution.py:465
  28.7 5.5 %collective-permute-start.1 = (bf16[128,128]{1,0:T(8,128)(2,1)S(1)}, bf16[128,128]{1,0:T(8,128)(2,1)S(1)}, u32[]{:S(2)}, u32[]{:S(2)}) collective-permute-start(bf16[128,128]{1,0:T(8,128)(2,1)S(1)} %get-tuple-element.29), channel_id=1, source_target_pairs={{0,3},{1,2},{2,1},{3,0},{4,7},{5,6},{6,5},{7,4},{8,11},{9,10},{10,... | collective-permute-start | bytes 98312 | tf_op jit(solution)/shard_map/ppermute | solution.py:473
  30.5 3.9 %collective-permute-start.2 = (bf16[128,128]{1,0:T(8,128)(2,1)S(1)}, bf16[128,128]{1,0:T(8,128)(2,1)S(1)}, u32[]{:S(2)}, u32[]{:S(2)}) collective-permute-start(bf16[128,128]{1,0:T(8,128)(2,1)S(1)} %get-tuple-element.30), channel_id=1, source_target_pairs={{0,2},{1,3},{2,0},{3,1},{4,6},{5,7},{6,4},{7,5},{8,10},{9,11},{10,... | collective-permute-start | bytes 98312 | tf_op jit(solution)/shard_map/ppermute | solution.py:469
  30.9 3.6 %collective-permute-start.3 = (bf16[128,128]{1,0:T(8,128)(2,1)S(1)}, bf16[128,128]{1,0:T(8,128)(2,1)S(1)}, u32[]{:S(2)}, u32[]{:S(2)}) collective-permute-start(bf16[128,128]{1,0:T(8,128)(2,1)S(1)} %get-tuple-element.31), channel_id=1, source_target_pairs={{0,1},{1,0},{2,3},{3,2},{4,5},{5,4},{6,7},{7,6},{8,9},{9,8},{10,11... | collective-permute-start | bytes 98312 | tf_op jit(solution)/shard_map/ppermute | solution.py:465
  31.7 11.4 %collective-permute-start.10 = (bf16[256,256]{1,0:T(8,128)(2,1)S(1)}, bf16[256,256]{1,0:T(8,128)(2,1)S(1)}, u32[]{:S(2)}, u32[]{:S(2)}) collective-permute-start(bf16[256,256]{1,0:T(8,128)(2,1)S(1)} %get-tuple-element.38), channel_id=1, source_target_pairs={{4,8},{8,12},{5,13},{6,10},{10,14},{7,15},{20,24},{24,28},{21,29},... | collective-permute-start | bytes 393224 | tf_op jit(solution)/shard_map/ppermute | solution.py:496
  35.4 8.0 %collective-permute-start.6 = (bf16[128,128]{1,0:T(8,128)(2,1)S(1)}, bf16[128,128]{1,0:T(8,128)(2,1)S(1)}, u32[]{:S(2)}, u32[]{:S(2)}) collective-permute-start(bf16[128,128]{1,0:T(8,128)(2,1)S(1)} %get-tuple-element.37), channel_id=1, source_target_pairs={{0,12},{1,13},{2,14},{3,15},{16,28},{17,29},{18,30},{19,31}} | collective-permute-start | bytes 98312 | tf_op jit(solution)/shard_map/ppermute | solution.py:502
  39.9 3.5 %collective-permute-start.7 = (bf16[128,128]{1,0:T(8,128)(2,1)S(1)}, bf16[128,128]{1,0:T(8,128)(2,1)S(1)}, u32[]{:S(2)}, u32[]{:S(2)}) collective-permute-start(bf16[128,128]{1,0:T(8,128)(2,1)S(1)} %get-tuple-element.37), channel_id=1, source_target_pairs={{0,4},{1,5},{2,6},{3,7},{16,20},{17,21},{18,22},{19,23}} | collective-permute-start | bytes 98312 | tf_op jit(solution)/shard_map/ppermute | solution.py:502
  41.2 2.9 %collective-permute-start.8 = (bf16[128,128]{1,0:T(8,128)(2,1)S(1)}, bf16[128,128]{1,0:T(8,128)(2,1)S(1)}, u32[]{:S(2)}, u32[]{:S(2)}) collective-permute-start(bf16[128,128]{1,0:T(8,128)(2,1)S(1)} %get-tuple-element.37), channel_id=1, source_target_pairs={{0,8},{1,9},{2,10},{3,11},{4,12},{5,13},{6,14},{7,15},{16,24},{17,... | collective-permute-start | bytes 98312 | tf_op jit(solution)/shard_map/ppermute | solution.py:502
  42.5 1.6 %collective-permute-start.9 = (bf16[128,128]{1,0:T(8,128)(2,1)S(1)}, bf16[128,128]{1,0:T(8,128)(2,1)S(1)}, u32[]{:S(2)}, u32[]{:S(2)}) collective-permute-start(bf16[128,128]{1,0:T(8,128)(2,1)S(1)} %get-tuple-element.37), channel_id=1, source_target_pairs={{4,8},{5,9},{6,10},{7,11},{8,12},{9,13},{10,14},{11,15},{20,24},{2... | collective-permute-start | bytes 98312 | tf_op jit(solution)/shard_map/ppermute | solution.py:502
  43.1 1.4 %collective-permute-start.11 = (bf16[256,256]{1,0:T(8,128)(2,1)S(1)}, bf16[256,256]{1,0:T(8,128)(2,1)S(1)}, u32[]{:S(2)}, u32[]{:S(2)}) collective-permute-start(bf16[256,256]{1,0:T(8,128)(2,1)S(1)} %collective-permute-done.10.got), channel_id=1, source_target_pairs={{0,1},{1,0},{2,3},{3,2},{4,5},{5,4},{6,7},{7,6},{8,9},{9,8},{10,11... | collective-permute-start | bytes 393224 | tf_op jit(solution)/shard_map/ppermute | solution.py:465
  45.6 3.8 %collective-permute-start.12 = (bf16[128,128]{1,0:T(8,128)(2,1)S(1)}, bf16[128,128]{1,0:T(8,128)(2,1)S(1)}, u32[]{:S(2)}, u32[]{:S(2)}) collective-permute-start(bf16[128,128]{1,0:T(8,128)(2,1)S(1)} %get-tuple-element.43), channel_id=1, source_target_pairs={{0,3},{1,2},{2,1},{3,0},{4,7},{5,6},{6,5},{7,4},{8,11},{9,10},{10,... | collective-permute-start | bytes 98312 | tf_op jit(solution)/shard_map/ppermute | solution.py:473
  46.2 4.0 %collective-permute-start.13 = (bf16[128,128]{1,0:T(8,128)(2,1)S(1)}, bf16[128,128]{1,0:T(8,128)(2,1)S(1)}, u32[]{:S(2)}, u32[]{:S(2)}) collective-permute-start(bf16[128,128]{1,0:T(8,128)(2,1)S(1)} %get-tuple-element.44), channel_id=1, source_target_pairs={{0,2},{1,3},{2,0},{3,1},{4,6},{5,7},{6,4},{7,5},{8,10},{9,11},{10,... | collective-permute-start | bytes 98312 | tf_op jit(solution)/shard_map/ppermute | solution.py:469
  47.5 2.6 %collective-permute-start.14 = (bf16[128,128]{1,0:T(8,128)(2,1)S(1)}, bf16[128,128]{1,0:T(8,128)(2,1)S(1)}, u32[]{:S(2)}, u32[]{:S(2)}) collective-permute-start(bf16[128,128]{1,0:T(8,128)(2,1)S(1)} %get-tuple-element.45), channel_id=1, source_target_pairs={{0,1},{1,0},{2,3},{3,2},{4,5},{5,4},{6,7},{7,6},{8,9},{9,8},{10,11... | collective-permute-start | bytes 98312 | tf_op jit(solution)/shard_map/ppermute | solution.py:465

commit v21 on v20

--- a/solution.py
+++ b/solution.py
@@ -258,7 +258,7 @@
     )(*maps)
 
 
-def source_kernel(received, inject, face_rows, _map, source, own, far, across, near, _same_map, quarters, total, heads, targets, sem):
+def source_kernel(received, inject, face_rows, source, own, far, across, near, quarters, total, heads, targets, sem):
     energies, orbitals, columns = inject.shape
     sections = received.shape[0]
     half = quarters.shape[1]
@@ -295,15 +295,31 @@
         out[...] = quarters[at].astype(BF16)
 
 
-def placed_source(received, inject, face_rows, passed):
+def after_kernel(_packets, _map, _same_map):
+    pass
+
+
+def handed_on(item, packets):
+    return call(
+        after_kernel,
+        "after_exchange",
+        [IN_PLACE] * 2,
+        [shape(*item.shape, dtype=item.dtype)],
+        [],
+        0.1,
+        aliases={1: 0},
+    )(packets, item)[0]
+
+
+def placed_source(received, inject, face_rows):
     face = face_rows.shape[1]
     energies, orbitals, columns = inject.shape
     sections = received.shape[0]
     return call(
         source_kernel,
         "source_and_face",
-        [IN_VMEM, IN_VMEM, IN_VMEM, IN_PLACE],
-        [shape(*inject.shape)] + [shape(face // 2, columns)] * GROUP + [shape(*passed.shape, dtype=F32)],
+        [IN_VMEM, IN_VMEM, IN_VMEM],
+        [shape(*inject.shape)] + [shape(face // 2, columns)] * GROUP,
         [
             pltpu.VMEM((GROUP, face // 2, columns), F32),
             pltpu.VMEM(inject.shape, F32),
@@ -312,8 +328,7 @@
             pltpu.SemaphoreType.DMA,
         ],
         1.4,
-        aliases={3: 1 + GROUP},
-    )(received, inject, face_rows, passed)
+    )(received, inject, face_rows)
 
 
 def collect(refs, held):
@@ -494,7 +509,7 @@
         else:
             pairs += [(GROUP + i, 3 * GROUP + i)]
     got = lax.ppermute(total_map, "sec", pairs)
-    return got, to_near(got, sections)
+    return got, lax.ppermute(got, "sec", [(s, s ^ 1) for s in range(2 * GROUP, sections)])
 
 
 def between(item, *planes):
@@ -528,9 +543,10 @@
     across = to_across(other_map, sections)
     near = to_near(own_map, sections)
 
-    source, *quarters, across = placed_source(received, inject, face_rows, across)
+    across = handed_on(across, received)
+    far = to_near(across, sections)
+    source, *quarters = placed_source(received, inject, face_rows)
     shifts = exchange(*quarters, sections)
-    far = to_near(across, sections)
     four = sections // GROUP == 4
     total_map, parts = chain([own_map, far, across, near], BF16 if four else F32)
     early = image_and_maps(green, source, parts)

time: 51.8 us -> 51.3 us (level)
  waiting for transfers between devices: 11.9 us -> 10.8 us
  starting transfers between devices: 22.1 us -> 22.7 us
    ppermute x3, starting transfers between devices: 3.71 us -> 3.01 us  [to_across(): lax.ppermute(item, 'sec', [(s, s // GROUP * GROUP + (s % GROUP + CORES) %...]
    ppermute x0 -> x1, starting transfers between devices: none -> 0.67 us  [maps_up(): lax.ppermute(got, 'sec', [(s, s ^ 1) for s in range(2 * GROUP, sections)])]
    ppermute x5 -> x4, starting transfers between devices: 0.22 us -> 0.81 us  [to_near(): return lax.ppermute(item, 'sec', [(s, s ^ 1) for s in range(sections)])]
    ppermute x4, waiting for transfers between devices: 0.67 us -> 0.08 us  [between(): return lax.ppermute(item, 'sec', pairs)]
    pallas_call x1 -> x2, Pallas kernels: 1.41 us -> 1.42 us  [the longest x1 1.42 us: placed_source(): call(source_kernel, 'source_and_face', [IN_VMEM, IN_VMEM, IN_VMEM], [shap...]
  transfers between devices with their start and end apart: 16 -> 16, of which waited for: 5 -> 4; matrix products, arithmetic and copies ran while one was open for 0% -> 0% of each run, Pallas kernels for 16% -> 16%
where the time goes in v21:
time: 51.3 us; the launch traced here: 50.9 us
  starting transfers between devices  22.7 us (44%)
  Pallas kernels  15 us (29%)
  waiting for transfers between devices  10.8 us (21%)
  local copies, waits for them, and re-layouts  2.2 us (4%)
    ppermute x3, waiting for transfers between devices, to_across(): lax.ppermute(item, 'sec', [(s, s // GROUP * GROUP + (s % GROUP + CORES) %...  10.7 us
    ppermute x4, starting transfers between devices, between(): return lax.ppermute(item, 'sec', pairs)  7.73 us
    all_to_all x1, starting transfers between devices, per_device(): lax.all_to_all(outgoing, 'sec', split_axis=0, concat_axis=0, tiled=True)  7.54 us
    pallas_call x1, Pallas kernels, outgoing_pairs(): call(pairs_kernel, 'pairs', [IN_HBM] * 4, shape(sections, CAP * energies...  4.51 us
    ppermute x3, starting transfers between devices, to_across(): lax.ppermute(item, 'sec', [(s, s // GROUP * GROUP + (s % GROUP + CORES) %...  3.01 us
    ppermute x2, starting transfers between devices, to_far(): lax.ppermute(item, 'sec', [(s, s // GROUP * GROUP + (s % GROUP + CORES) %...  2.28 us
    unnamed x10, local copies, waits for them, and re-layouts  2.2 us
    pallas_call x1, Pallas kernels, propagator(): call(prop_kernel, 'prop', [IN_SMEM, IN_VMEM, IN_VMEM, IN_PLACE], shape(en...  1.9 us
  transfers between devices with their start and end apart: 16, of which 4 were waited for; matrix products, arithmetic and copies ran while one was open for 0% of the time, Pallas kernels for 16%

profile of v21, /device:TPU:0, one launch (start us, length us, event | category | flops | bytes accessed | tf_op | source)
XLA Modules:
  0.0 50.9 jit_solution(7209284810288077140)
XLA Ops:
  0.0 4.5 %pairs.1 = bf16[16,136,128]{2,1,0:T(8,128)(2,1)} custom-call(s32[16]{0:T(128)} %bitcast.21, s32[2,16]{1,0:T(2,128)} %bitcast.20, bf16[2,1024,1024]{2,1,0:T(8,128)(2,1)} %bitcast.9, bf16[2,1024,128]{2,1,0:T(8,128)(2,1)} %bitcast.14), custom_call_target="tpu_custom_call" | custom-call | flops 4600000000 | tf_op jit(solution)/shard_map/pairs/pallas_call | solution.py:168
  4.5 0.0 copy-start.2
  4.5 7.5 %all-to-all-start = ((bf16[16,136,128]{2,1,0:T(8,128)(2,1)}), bf16[16,136,128]{2,1,0:T(8,128)(2,1)S(1)}, u32[]{:S(2)}, u32[]{:S(2)}) async-start(bf16[16,136,128]{2,1,0:T(8,128)(2,1)} %pairs.1), calls=%async_computation | async-start | bytes 1114112 | tf_op jit(solution)/shard_map/all_to_all | solution.py:540
  12.1 0.0 copy-done.3
  12.1 0.0 copy-done.4
  12.1 0.0 copy-start
  12.1 2.2 %copy-done = bf16[1,2,1024,1024]{3,2,1,0:T(8,128)(2,1)S(1)} copy-done((bf16[1,2,1024,1024]{3,2,1,0:T(8,128)(2,1)S(1)}, bf16[1,2,1024,1024]{3,2,1,0:T(8,128)(2,1)}, u32[]{:S(2)}) %copy-start) | copy-done | bytes 4194328
  14.3 1.1 %face_maps.1 = (f32[256,256]{1,0:T(8,128)S(1)}, f32[256,256]{1,0:T(8,128)S(1)}, bf16[2,256,1024]{2,1,0:T(8,128)(2,1)S(1)}) custom-call(s32[2,8]{1,0:T(2,128)S(1)} %bitcast.18, bf16[2,1024,1024]{2,1,0:T(8,128)(2,1)S(1)} %bitcast.10, bf16[1024,256]{1,0:T(8,128)(2,1)S(1)} %bitcast.16), custom_call_target="tpu_custom_call" | custom-call | flops 1380000000 | tf_op jit(solution)/shard_map/face_maps/pallas_call | solution.py:206
  15.4 2.0 %collective-permute-start.3 = (f32[256,256]{1,0:T(8,128)S(1)}, f32[256,256]{1,0:T(8,128)S(1)}, u32[]{:S(2)}, u32[]{:S(2)}) collective-permute-start(f32[256,256]{1,0:T(8,128)S(1)} %get-tuple-element.31), channel_id=1, source_target_pairs={{0,2},{1,3},{2,0},{3,1},{4,6},{5,7},{6,4},{7,5},{8,10},{9,11},{10,... | collective-permute-start | bytes 786440 | tf_op jit(solution)/shard_map/ppermute | solution.py:484
  17.4 0.0 collective-permute-start.5
  17.4 9.9 %collective-permute-done.3._map = f32[256,256]{1,0:T(8,128)S(1)} collective-permute-done((f32[256,256]{1,0:T(8,128)S(1)}, f32[256,256]{1,0:T(8,128)S(1)}, u32[]{:S(2)}, u32[]{:S(2)}) %collective-permute-start.3) | collective-permute-done | bytes 262176 | tf_op jit(solution)/shard_map/ppermute | solution.py:484
  27.3 0.0 all-to-all-done.received._packets
  27.3 0.0 collective-permute-start.4
  27.3 0.0 copy-start.1
  27.3 1.4 %source_and_face.1 = (bf16[2,1024,128]{2,1,0:T(8,128)(2,1)S(1)}, bf16[128,128]{1,0:T(8,128)(2,1)S(1)}, bf16[128,128]{1,0:T(8,128)(2,1)S(1)}, bf16[128,128]{1,0:T(8,128)(2,1)S(1)}, bf16[128,128]{1,0:T(8,128)(2,1)S(1)}) custom-call(bf16[16,136,128]{2,1,0:T(8,128)(2,1)S(1)} %all-to-all-done.received._packets, bf16[2,1024,128]{2,1,0:T(8,128)(2,1)S(1)} %bitcast.15, ...), custom_call_target="tpu_custom_call" | custom-call | flops 1610000000 | tf_op jit(solution)/shard_map/source_and_face/pallas_call | solution.py:318
  28.8 1.8 %collective-permute-start = (bf16[128,128]{1,0:T(8,128)(2,1)S(1)}, bf16[128,128]{1,0:T(8,128)(2,1)S(1)}, u32[]{:S(2)}, u32[]{:S(2)}) collective-permute-start(bf16[128,128]{1,0:T(8,128)(2,1)S(1)} %get-tuple-element.27), channel_id=1, source_target_pairs={{0,3},{1,2},{2,1},{3,0},{4,7},{5,6},{6,5},{7,4},{8,11},{9,10},{10,... | collective-permute-start | bytes 98312 | tf_op jit(solution)/shard_map/ppermute | solution.py:488
  30.6 0.4 collective-permute-start.1
  31.0 0.0 collective-permute-start.2
  31.0 0.0 collective-permute-done.5.near
  31.0 0.0 collective-permute-done.4.far
  31.0 0.8 %chain_maps.1 = (bf16[256,256]{1,0:T(8,128)(2,1)S(1)}, bf16[2,4,256,256]{3,2,1,0:T(8,128)(2,1)S(1)}) custom-call(f32[256,256]{1,0:T(8,128)S(1)} %get-tuple-element.30.own, f32[256,256]{1,0:T(8,128)S(1)} %collective-permute-done.4.far, f32[256,256]{1,0:T(8,128)S(1)} %after_exchange.1.across, f32[256,256]{1,0:T(8,128)S(1)} %collective-permute-done.5.near), custom_call_target="tpu_custom_call" | custom-call | flops 1035000000 | tf_op jit(solution)/shard_map/chain_maps/pallas_call | solution.py:251
  31.8 0.7 %collective-permute-start.10 = (bf16[256,256]{1,0:T(8,128)(2,1)S(1)}, bf16[256,256]{1,0:T(8,128)(2,1)S(1)}, u32[]{:S(2)}, u32[]{:S(2)}) collective-permute-start(bf16[256,256]{1,0:T(8,128)(2,1)S(1)} %get-tuple-element.36), channel_id=1, source_target_pairs={{4,8},{8,12},{5,13},{6,10},{10,14},{7,15},{20,24},{24,28},{21,29},... | collective-permute-start | bytes 393224 | tf_op jit(solution)/shard_map/ppermute | solution.py:511
  32.5 1.8 %image_and_maps.2 = (f32[2,1024,128]{2,1,0:T(8,128)S(1)}, bf16[2,2,256,256]{3,2,1,0:T(8,128)(2,1)S(1)}) custom-call(bf16[2,1024,1024]{2,1,0:T(8,128)(2,1)S(1)} %bitcast.11, bf16[2,1024,128]{2,1,0:T(8,128)(2,1)S(1)} %get-tuple-element.33.refs_1_, bf16[2,4,256,256]{3,2,1,0:T(8,128)(2,1)S(1)} %get-tuple-element.32.refs_2_.parts), custom_call_target="tpu_custom_call" | custom-call | flops 2300000000 | tf_op jit(solution)/shard_map/image_and_maps/pallas_call | solution.py:388
  34.3 0.0 collective-permute-done.far
  34.3 0.2 collective-permute-done.1.across
  34.5 0.0 collective-permute-done.2.near
  34.5 1.0 %plane_total.1 = (bf16[128,128]{1,0:T(8,128)(2,1)S(1)}, f32[3,256,128]{2,1,0:T(8,128)S(1)}) custom-call(bf16[128,128]{1,0:T(8,128)(2,1)S(1)} %get-tuple-element.26.own, bf16[128,128]{1,0:T(8,128)(2,1)S(1)} %collective-permute-done.far, bf16[128,128]{1,0:T(8,128)(2,1)S(1)} %collective-permute-done.1.across, bf16[128,128]{1,0:T(8,128)(2,1)S(1)} %collective-permute-done.2.near, ...), custom_call_target="tpu_custom_call" | custom-call | flops 3449999872 | tf_op jit(solution)/shard_map/plane_total/pallas_call | solution.py:354
  35.5 4.5 %collective-permute-start.6 = (bf16[128,128]{1,0:T(8,128)(2,1)S(1)}, bf16[128,128]{1,0:T(8,128)(2,1)S(1)}, u32[]{:S(2)}, u32[]{:S(2)}) collective-permute-start(bf16[128,128]{1,0:T(8,128)(2,1)S(1)} %get-tuple-element.35), channel_id=1, source_target_pairs={{0,12},{1,13},{2,14},{3,15},{16,28},{17,29},{18,30},{19,31}} | collective-permute-start | bytes 98312 | tf_op jit(solution)/shard_map/ppermute | solution.py:517
  39.9 1.3 %collective-permute-start.7 = (bf16[128,128]{1,0:T(8,128)(2,1)S(1)}, bf16[128,128]{1,0:T(8,128)(2,1)S(1)}, u32[]{:S(2)}, u32[]{:S(2)}) collective-permute-start(bf16[128,128]{1,0:T(8,128)(2,1)S(1)} %get-tuple-element.35), channel_id=1, source_target_pairs={{0,4},{1,5},{2,6},{3,7},{16,20},{17,21},{18,22},{19,23}} | collective-permute-start | bytes 98312 | tf_op jit(solution)/shard_map/ppermute | solution.py:517
  41.2 1.3 %collective-permute-start.8 = (bf16[128,128]{1,0:T(8,128)(2,1)S(1)}, bf16[128,128]{1,0:T(8,128)(2,1)S(1)}, u32[]{:S(2)}, u32[]{:S(2)}) collective-permute-start(bf16[128,128]{1,0:T(8,128)(2,1)S(1)} %get-tuple-element.35), channel_id=1, source_target_pairs={{0,8},{1,9},{2,10},{3,11},{4,12},{5,13},{6,14},{7,15},{16,24},{17,... | collective-permute-start | bytes 98312 | tf_op jit(solution)/shard_map/ppermute | solution.py:517
  42.5 0.7 %collective-permute-start.9 = (bf16[128,128]{1,0:T(8,128)(2,1)S(1)}, bf16[128,128]{1,0:T(8,128)(2,1)S(1)}, u32[]{:S(2)}, u32[]{:S(2)}) collective-permute-start(bf16[128,128]{1,0:T(8,128)(2,1)S(1)} %get-tuple-element.35), channel_id=1, source_target_pairs={{4,8},{5,9},{6,10},{7,11},{8,12},{9,13},{10,14},{11,15},{20,24},{2... | collective-permute-start | bytes 98312 | tf_op jit(solution)/shard_map/ppermute | solution.py:517
  43.2 0.0 collective-permute-done.10.got
  43.2 0.7 %collective-permute-start.11 = (bf16[256,256]{1,0:T(8,128)(2,1)S(1)}, bf16[256,256]{1,0:T(8,128)(2,1)S(1)}, u32[]{:S(2)}, u32[]{:S(2)}) collective-permute-start(bf16[256,256]{1,0:T(8,128)(2,1)S(1)} %collective-permute-done.10.got), channel_id=1, source_target_pairs={{8,9},{9,8},{10,11},{11,10},{12,13},{13,12},{14,15},{15,14},{24,25... | collective-permute-start | bytes 393224 | tf_op jit(solution)/shard_map/ppermute | solution.py:512
  43.9 0.1 image_and_maps.3
  44.0 0.0 collective-permute-done.6.third
  44.0 0.0 collective-permute-done.7.near_one
  44.1 0.1 collective-permute-done.8.second
  44.1 0.0 collective-permute-done.9.far_one
  44.1 0.0 collective-permute-done.11.other
  44.1 1.1 %entering.1 = (bf16[128,128]{1,0:T(8,128)(2,1)S(1)}, bf16[128,128]{1,0:T(8,128)(2,1)S(1)}, bf16[128,128]{1,0:T(8,128)(2,1)S(1)}, bf16[128,128]{1,0:T(8,128)(2,1)S(1)}) custom-call(bf16[128,128]{1,0:T(8,128)(2,1)S(1)} %collective-permute-done.6.third, bf16[128,128]{1,0:T(8,128)(2,1)S(1)} %collective-permute-done.7.near_one, ...), custom_call_target="tpu_custom_call" | custom-call | flops 1610000000 | tf_op jit(solution)/shard_map/entering/pallas_call | solution.py:428
  45.2 0.5 collective-permute-start.12
  45.7 0.7 %collective-permute-start.13 = (bf16[128,128]{1,0:T(8,128)(2,1)S(1)}, bf16[128,128]{1,0:T(8,128)(2,1)S(1)}, u32[]{:S(2)}, u32[]{:S(2)}) collective-permute-start(bf16[128,128]{1,0:T(8,128)(2,1)S(1)} %get-tuple-element.42), channel_id=1, source_target_pairs={{0,2},{1,3},{2,0},{3,1},{4,6},{5,7},{6,4},{7,5},{8,10},{9,11},{10,... | collective-permute-start | bytes 98312 | tf_op jit(solution)/shard_map/ppermute | solution.py:484
  46.3 0.8 %collective-permute-start.14 = (bf16[128,128]{1,0:T(8,128)(2,1)S(1)}, bf16[128,128]{1,0:T(8,128)(2,1)S(1)}, u32[]{:S(2)}, u32[]{:S(2)}) collective-permute-start(bf16[128,128]{1,0:T(8,128)(2,1)S(1)} %get-tuple-element.43), channel_id=1, source_target_pairs={{0,1},{1,0},{2,3},{3,2},{4,5},{5,4},{6,7},{7,6},{8,9},{9,8},{10,11... | collective-permute-start | bytes 98312 | tf_op jit(solution)/shard_map/ppermute | solution.py:480
  47.1 1.9 %prop.1 = bf16[2,1024,256]{2,1,0:T(8,128)(2,1)S(1)} custom-call(s32[2,8]{1,0:T(2,128)S(1)} %bitcast.19, bf16[2,1024,1024]{2,1,0:T(8,128)(2,1)S(1)} %bitcast.13, bf16[1024,256]{1,0:T(8,128)(2,1)S(1)} %bitcast.17, bf16[128,128]{1,0:T(8,128)(2,1)S(1)} %get-tuple-element.40._tie.own), custom_call_target="tpu_custom_call" | custom-call | flops 1724999936 | tf_op jit(solution)/shard_map/prop/pallas_call | solution.py:225
  49.1 0.0 collective-permute-done.12.far
  49.1 0.6 %collective-permute-done.13.across = bf16[128,128]{1,0:T(8,128)(2,1)S(1)} collective-permute-done((bf16[128,128]{1,0:T(8,128)(2,1)S(1)}, bf16[128,128]{1,0:T(8,128)(2,1)S(1)}, u32[]{:S(2)}, u32[]{:S(2)}) %collective-permute-start.13) | collective-permute-done | bytes 32800 | tf_op jit(solution)/shard_map/ppermute | solution.py:484
  49.6 0.0 collective-permute-done.14.near
  49.6 1.3 %waves.1 = bf16[2,1024,128]{2,1,0:T(8,128)(2,1)} custom-call(bf16[128,128]{1,0:T(8,128)(2,1)S(1)} %get-tuple-element.40._tie.own, bf16[128,128]{1,0:T(8,128)(2,1)S(1)} %collective-permute-done.12.far, bf16[128,128]{1,0:T(8,128)(2,1)S(1)} %collective-permute-done.13.across, bf16[128,128]{1,0:T(8,128)(2,1)S(1)} %collective-permute-done.14.near, ...), custom_call_target="tpu_custom_call" | custom-call | flops 1495000064 | tf_op jit(solution)/shard_map/waves/pallas_call | solution.py:463
  (5 shorter events, 0.0 us)
Async XLA Ops:
  0.0 12.1 %copy-start.3 = (bf16[1,1024,256]{2,1,0:T(8,128)(2,1)S(1)}, bf16[1,1024,256]{2,1,0:T(8,128)(2,1)}, u32[]{:S(2)}) copy-start(bf16[1,1024,256]{2,1,0:T(8,128)(2,1)} %param.8) | copy-start | bytes 1572868
  0.0 12.1 %copy-start.4 = (s32[1,8,2]{1,2,0:T(2,128)S(1)}, s32[1,8,2]{1,2,0:T(2,128)}, u32[]{:S(2)}) copy-start(s32[1,8,2]{1,2,0:T(2,128)} %param.9) | copy-start | bytes 196
  4.5 22.8 %copy-start.2 = (bf16[1,2,1024,128]{3,2,1,0:T(8,128)(2,1)S(1)}, bf16[1,2,1024,128]{3,2,1,0:T(8,128)(2,1)}, u32[]{:S(2)}) copy-start(bf16[1,2,1024,128]{3,2,1,0:T(8,128)(2,1)} %param.7) | copy-start | bytes 1572868
  4.5 22.8 %all-to-all-start = ((bf16[16,136,128]{2,1,0:T(8,128)(2,1)}), bf16[16,136,128]{2,1,0:T(8,128)(2,1)S(1)}, u32[]{:S(2)}, u32[]{:S(2)}) async-start(bf16[16,136,128]{2,1,0:T(8,128)(2,1)} %pairs.1), calls=%async_computation | async-start | bytes 1114112 | tf_op jit(solution)/shard_map/all_to_all | solution.py:540
  12.1 2.2 %copy-start = (bf16[1,2,1024,1024]{3,2,1,0:T(8,128)(2,1)S(1)}, bf16[1,2,1024,1024]{3,2,1,0:T(8,128)(2,1)}, u32[]{:S(2)}) copy-start(bf16[1,2,1024,1024]{3,2,1,0:T(8,128)(2,1)} %param.6) | copy-start | bytes 12582916
  15.4 11.9 %collective-permute-start.3 = (f32[256,256]{1,0:T(8,128)S(1)}, f32[256,256]{1,0:T(8,128)S(1)}, u32[]{:S(2)}, u32[]{:S(2)}) collective-permute-start(f32[256,256]{1,0:T(8,128)S(1)} %get-tuple-element.31), channel_id=1, source_target_pairs={{0,2},{1,3},{2,0},{3,1},{4,6},{5,7},{6,4},{7,5},{8,10},{9,11},{10,... | collective-permute-start | bytes 786440 | tf_op jit(solution)/shard_map/ppermute | solution.py:484
  17.4 13.6 %collective-permute-start.5 = (f32[256,256]{1,0:T(8,128)S(1)}, f32[256,256]{1,0:T(8,128)S(1)}, u32[]{:S(2)}, u32[]{:S(2)}) collective-permute-start(f32[256,256]{1,0:T(8,128)S(1)} %get-tuple-element.30.own), channel_id=1, source_target_pairs={{0,1},{1,0},{2,3},{3,2},{4,5},{5,4},{6,7},{7,6},{8,9},{9,8},{10,11... | collective-permute-start | bytes 786440 | tf_op jit(solution)/shard_map/ppermute | solution.py:480
  27.3 3.6 %collective-permute-start.4 = (f32[256,256]{1,0:T(8,128)S(1)}, f32[256,256]{1,0:T(8,128)S(1)}, u32[]{:S(2)}, u32[]{:S(2)}) collective-permute-start(f32[256,256]{1,0:T(8,128)S(1)} %after_exchange.1.across), channel_id=1, source_target_pairs={{0,1},{1,0},{2,3},{3,2},{4,5},{5,4},{6,7},{7,6},{8,9},{9,8},{10,11... | collective-permute-start | bytes 786440 | tf_op jit(solution)/shard_map/ppermute | solution.py:480
  27.3 5.2 %copy-start.1 = (bf16[1,2,1024,1024]{3,2,1,0:T(8,128)(2,1)S(1)}, bf16[1,2,1024,1024]{3,2,1,0:T(8,128)(2,1)}, u32[]{:S(2)}) copy-start(bf16[1,2,1024,1024]{3,2,1,0:T(8,128)(2,1)} %param.6) | copy-start | bytes 12582916
  28.8 5.5 %collective-permute-start = (bf16[128,128]{1,0:T(8,128)(2,1)S(1)}, bf16[128,128]{1,0:T(8,128)(2,1)S(1)}, u32[]{:S(2)}, u32[]{:S(2)}) collective-permute-start(bf16[128,128]{1,0:T(8,128)(2,1)S(1)} %get-tuple-element.27), channel_id=1, source_target_pairs={{0,3},{1,2},{2,1},{3,0},{4,7},{5,6},{6,5},{7,4},{8,11},{9,10},{10,... | collective-permute-start | bytes 98312 | tf_op jit(solution)/shard_map/ppermute | solution.py:488
  30.6 3.9 %collective-permute-start.1 = (bf16[128,128]{1,0:T(8,128)(2,1)S(1)}, bf16[128,128]{1,0:T(8,128)(2,1)S(1)}, u32[]{:S(2)}, u32[]{:S(2)}) collective-permute-start(bf16[128,128]{1,0:T(8,128)(2,1)S(1)} %get-tuple-element.28), channel_id=1, source_target_pairs={{0,2},{1,3},{2,0},{3,1},{4,6},{5,7},{6,4},{7,5},{8,10},{9,11},{10,... | collective-permute-start | bytes 98312 | tf_op jit(solution)/shard_map/ppermute | solution.py:484
  31.0 3.5 %collective-permute-start.2 = (bf16[128,128]{1,0:T(8,128)(2,1)S(1)}, bf16[128,128]{1,0:T(8,128)(2,1)S(1)}, u32[]{:S(2)}, u32[]{:S(2)}) collective-permute-start(bf16[128,128]{1,0:T(8,128)(2,1)S(1)} %get-tuple-element.29), channel_id=1, source_target_pairs={{0,1},{1,0},{2,3},{3,2},{4,5},{5,4},{6,7},{7,6},{8,9},{9,8},{10,11... | collective-permute-start | bytes 98312 | tf_op jit(solution)/shard_map/ppermute | solution.py:480
  31.8 11.4 %collective-permute-start.10 = (bf16[256,256]{1,0:T(8,128)(2,1)S(1)}, bf16[256,256]{1,0:T(8,128)(2,1)S(1)}, u32[]{:S(2)}, u32[]{:S(2)}) collective-permute-start(bf16[256,256]{1,0:T(8,128)(2,1)S(1)} %get-tuple-element.36), channel_id=1, source_target_pairs={{4,8},{8,12},{5,13},{6,10},{10,14},{7,15},{20,24},{24,28},{21,29},... | collective-permute-start | bytes 393224 | tf_op jit(solution)/shard_map/ppermute | solution.py:511
  35.5 8.6 %collective-permute-start.6 = (bf16[128,128]{1,0:T(8,128)(2,1)S(1)}, bf16[128,128]{1,0:T(8,128)(2,1)S(1)}, u32[]{:S(2)}, u32[]{:S(2)}) collective-permute-start(bf16[128,128]{1,0:T(8,128)(2,1)S(1)} %get-tuple-element.35), channel_id=1, source_target_pairs={{0,12},{1,13},{2,14},{3,15},{16,28},{17,29},{18,30},{19,31}} | collective-permute-start | bytes 98312 | tf_op jit(solution)/shard_map/ppermute | solution.py:517
  39.9 4.1 %collective-permute-start.7 = (bf16[128,128]{1,0:T(8,128)(2,1)S(1)}, bf16[128,128]{1,0:T(8,128)(2,1)S(1)}, u32[]{:S(2)}, u32[]{:S(2)}) collective-permute-start(bf16[128,128]{1,0:T(8,128)(2,1)S(1)} %get-tuple-element.35), channel_id=1, source_target_pairs={{0,4},{1,5},{2,6},{3,7},{16,20},{17,21},{18,22},{19,23}} | collective-permute-start | bytes 98312 | tf_op jit(solution)/shard_map/ppermute | solution.py:517
  41.2 2.9 %collective-permute-start.8 = (bf16[128,128]{1,0:T(8,128)(2,1)S(1)}, bf16[128,128]{1,0:T(8,128)(2,1)S(1)}, u32[]{:S(2)}, u32[]{:S(2)}) collective-permute-start(bf16[128,128]{1,0:T(8,128)(2,1)S(1)} %get-tuple-element.35), channel_id=1, source_target_pairs={{0,8},{1,9},{2,10},{3,11},{4,12},{5,13},{6,14},{7,15},{16,24},{17,... | collective-permute-start | bytes 98312 | tf_op jit(solution)/shard_map/ppermute | solution.py:517
  42.5 1.6 %collective-permute-start.9 = (bf16[128,128]{1,0:T(8,128)(2,1)S(1)}, bf16[128,128]{1,0:T(8,128)(2,1)S(1)}, u32[]{:S(2)}, u32[]{:S(2)}) collective-permute-start(bf16[128,128]{1,0:T(8,128)(2,1)S(1)} %get-tuple-element.35), channel_id=1, source_target_pairs={{4,8},{5,9},{6,10},{7,11},{8,12},{9,13},{10,14},{11,15},{20,24},{2... | collective-permute-start | bytes 98312 | tf_op jit(solution)/shard_map/ppermute | solution.py:517
  43.2 0.9 %collective-permute-start.11 = (bf16[256,256]{1,0:T(8,128)(2,1)S(1)}, bf16[256,256]{1,0:T(8,128)(2,1)S(1)}, u32[]{:S(2)}, u32[]{:S(2)}) collective-permute-start(bf16[256,256]{1,0:T(8,128)(2,1)S(1)} %collective-permute-done.10.got), channel_id=1, source_target_pairs={{8,9},{9,8},{10,11},{11,10},{12,13},{13,12},{14,15},{15,14},{24,25... | collective-permute-start | bytes 393224 | tf_op jit(solution)/shard_map/ppermute | solution.py:512
  45.2 3.8 %collective-permute-start.12 = (bf16[128,128]{1,0:T(8,128)(2,1)S(1)}, bf16[128,128]{1,0:T(8,128)(2,1)S(1)}, u32[]{:S(2)}, u32[]{:S(2)}) collective-permute-start(bf16[128,128]{1,0:T(8,128)(2,1)S(1)} %get-tuple-element.41), channel_id=1, source_target_pairs={{0,3},{1,2},{2,1},{3,0},{4,7},{5,6},{6,5},{7,4},{8,11},{9,10},{10,... | collective-permute-start | bytes 98312 | tf_op jit(solution)/shard_map/ppermute | solution.py:488
  45.7 3.9 %collective-permute-start.13 = (bf16[128,128]{1,0:T(8,128)(2,1)S(1)}, bf16[128,128]{1,0:T(8,128)(2,1)S(1)}, u32[]{:S(2)}, u32[]{:S(2)}) collective-permute-start(bf16[128,128]{1,0:T(8,128)(2,1)S(1)} %get-tuple-element.42), channel_id=1, source_target_pairs={{0,2},{1,3},{2,0},{3,1},{4,6},{5,7},{6,4},{7,5},{8,10},{9,11},{10,... | collective-permute-start | bytes 98312 | tf_op jit(solution)/shard_map/ppermute | solution.py:484
  46.3 3.3 %collective-permute-start.14 = (bf16[128,128]{1,0:T(8,128)(2,1)S(1)}, bf16[128,128]{1,0:T(8,128)(2,1)S(1)}, u32[]{:S(2)}, u32[]{:S(2)}) collective-permute-start(bf16[128,128]{1,0:T(8,128)(2,1)S(1)} %get-tuple-element.43), channel_id=1, source_target_pairs={{0,1},{1,0},{2,3},{3,2},{4,5},{5,4},{6,7},{7,6},{8,9},{9,8},{10,11... | collective-permute-start | bytes 98312 | tf_op jit(solution)/shard_map/ppermute | solution.py:480

commit v22 on v21

--- a/solution.py
+++ b/solution.py
@@ -232,18 +232,33 @@
     )(pattern, green, coupling, tie)
 
 
-def times(a, b):
-    return dot(a[0], b[0]) + (dot(a[0], b[1]) + dot(a[1], b[0]))
+def times_maps(stack, high, low):
+    face = high.shape[0]
+    y = dot(stack, jnp.concatenate([high, low], axis=1))
+    return y[:face, :face] + (y[:face, face:] + y[face:, :face])
+
+
+def with_low(x):
+    high = x.astype(BF16).astype(F32)
+    return jnp.where(left_lanes(x), high, swap_lanes(x - high)).astype(BF16)
+
+
+def from_stack(y):
+    face = y.shape[0] // 2
+    return y[:face] + (swap_lanes(y[:face]) + y[face:])
+
+
+def stacked(high, low):
+    return jnp.concatenate([high, low], axis=0)
 
 
 def chain_kernel(own, far, across, near, total_out, parts, maps):
     collect((own, far, across, near), maps)
     split = [two_parts(maps[j]) for j in range(GROUP)]
-    lower, upper = two_parts(times(split[1], split[0])), two_parts(times(split[3], split[2]))
-    total_out[...] = times(upper, lower).astype(total_out.dtype)
-    for j, (high, low) in enumerate(split):
-        parts[0, j] = high
-        parts[1, j] = low
+    for j, two in enumerate(split):
+        parts[j] = stacked(*two)
+    lower, upper = two_parts(times_maps(parts[1], *split[0])), two_parts(times_maps(parts[3], *split[2]))
+    total_out[...] = times_maps(stacked(*upper), *lower).astype(total_out.dtype)
 
 
 def chain(maps, dtype):
@@ -252,13 +267,13 @@
         chain_kernel,
         "chain_maps",
         [IN_VMEM] * GROUP,
-        [shape(face, face, dtype=dtype), shape(2, GROUP, face, face)],
+        [shape(face, face, dtype=dtype), shape(GROUP, 2 * face, face)],
         [pltpu.VMEM((GROUP, face, face), F32)],
         0.9,
     )(*maps)
 
 
-def source_kernel(received, inject, face_rows, source, own, far, across, near, quarters, total, heads, targets, sem):
+def source_kernel(received, inject, face_rows, source, own, far, across, near, quarters, heads, targets, sem, *totals):
     energies, orbitals, columns = inject.shape
     sections = received.shape[0]
     half = quarters.shape[1]
@@ -272,21 +287,22 @@
     lax.fori_loop(0, sections, read, 0, unroll=min(sections, 8))
     fetch = pltpu.make_async_copy(heads, targets, sem)
     fetch.start()
-    total[...] = inject[...].astype(F32)
+    for e, total in enumerate(totals):
+        total[...] = inject[e].astype(F32)
     fetch.wait()
 
     def add(s, _):
         for r in range(CAP):
             first = pl.multiple_of(jnp.maximum(targets[s, r], 0) * BLK, BLK)
-            for e in range(energies):
+            for e, total in enumerate(totals):
                 item = received[s, (r * energies + e) * BLK : (r * energies + e + 1) * BLK, :]
-                total[e, pl.ds(first, BLK), :] += item.astype(F32)
+                total[pl.ds(first, BLK), :] += item.astype(F32)
         return 0
 
     lax.fori_loop(0, sections, add, 0, unroll=2)
     split = GROUP // energies
     for e in range(energies):
-        source[e] = total[e].astype(BF16)
+        source[e] = totals[e][...].astype(BF16)
         tall = dot(face_rows[e], source[e])
         quarters[e * split] = pack(tall)
         second = jnp.where(left_lanes(tall[:half]), swap_lanes(tall[:half]), tall[half:])
@@ -322,11 +338,11 @@
         [shape(*inject.shape)] + [shape(face // 2, columns)] * GROUP,
         [
             pltpu.VMEM((GROUP, face // 2, columns), F32),
-            pltpu.VMEM(inject.shape, F32),
             pltpu.VMEM((sections, columns), jnp.int32),
             pltpu.SMEM((sections, columns), jnp.int32),
             pltpu.SemaphoreType.DMA,
-        ],
+        ]
+        + [pltpu.VMEM((orbitals, columns), F32)] * energies,
         1.4,
     )(received, inject, face_rows)
 
@@ -337,7 +353,7 @@
 
 
 def step(parts, j, shift, state):
-    return unpack(shift.astype(F32)) + times((parts[0, j], parts[1, j]), two_parts(state))
+    return unpack(shift.astype(F32)) + from_stack(dot(parts[j], with_low(state)))
 
 
 def total_kernel(own, far, across, near, parts, _image, out, local, shifts):
@@ -370,10 +386,12 @@
     def _():
         for e in range(green.shape[0]):
             image[e] = dot(green[e], source[e])
-        maps = (parts[0, 0], parts[1, 0])
+        face = parts.shape[2]
+        high, low = parts[0, :face, :], parts[0, face:, :]
+        upto[: 2 * face, :] = parts[0]
         for j in range(1, GROUP - 1):
-            maps = two_parts(times((parts[0, j], parts[1, j]), maps))
-            upto[0, j - 1], upto[1, j - 1] = maps
+            high, low = two_parts(times_maps(parts[j], high, low))
+            upto[2 * j * face : 2 * (j + 1) * face, :] = stacked(high, low)
 
     if held:
 
@@ -384,23 +402,23 @@
 
 
 def image_and_maps(green, source, parts, held=()):
-    _, _, face, _ = parts.shape
+    _, _, face = parts.shape
     return call(
         functools.partial(work_kernel, not held),
         "image_and_maps",
         [IN_VMEM] * (3 + len(held)),
-        [shape(*source.shape, dtype=F32), shape(2, GROUP - 2, face, face)],
+        [shape(*source.shape, dtype=F32), shape((GROUP - 1) * 2 * face, face)],
         [],
         2.0,
     )(green, source, parts, *held)
 
 
-def sweep_plane(state, parts, upto, local, out):
-    two = two_parts(state)
+def sweep_plane(state, upto, local, out):
+    y = dot(upto[...], with_low(state))
+    size = 2 * state.shape[0]
     held = [pack(state)]
-    for j in range(1, GROUP):
-        maps = (parts[0, 0], parts[1, 0]) if j == 1 else (upto[0, j - 2], upto[1, j - 2])
-        held.append(pack(local[j - 1] + times(maps, two)))
+    for j in range(GROUP - 1):
+        held.append(pack(local[j] + from_stack(y[j * size : (j + 1) * size])))
     work = out[GROUP]
     for j, item in enumerate(held):
         work[j] = item
@@ -408,19 +426,19 @@
         ref[...] = work[at].astype(BF16)
 
 
-def entering_kernel(third, near_one, second, far_one, got, other, parts, upto, local, *out):
+def entering_kernel(third, near_one, second, far_one, got, other, upto, local, *out):
     first_core = place() % CORES == 0
     first = near_one[...].astype(F32) + far_one[...].astype(F32)
     state = unpack(third[...].astype(F32))
     for below, (one, two) in ((second[...].astype(F32), (other, got)), (first, (got, other))):
         factor = jnp.where(first_core, one[...], two[...])
-        high, low = two_parts(state)
-        state = unpack(below) + dot(factor, high) + dot(factor, low)
-    sweep_plane(state, parts, upto, local, out)
-
-
-def entering_from_kernel(base, parts, upto, local, *out):
-    sweep_plane(unpack(base[...]), parts, upto, local, out)
+        y = dot(factor, with_low(state))
+        state = unpack(below) + (y + swap_lanes(y))
+    sweep_plane(state, upto, local, out)
+
+
+def entering_from_kernel(base, upto, local, *out):
+    sweep_plane(unpack(base[...]), upto, local, out)
 
 
 def entering(body, args):
@@ -558,11 +576,11 @@
         second = between(total, (0, 1))
         first = between(total, (0, 3))
         image, upto = image_and_maps(green, source, parts, early)
-        entered = entering(entering_kernel, (first, second, third, fourth, *maps, parts, upto, local))
+        entered = entering(entering_kernel, (first, second, third, fourth, *maps, upto, local))
     else:
         base = scan_below(total_map, total, sections)
         image, upto = image_and_maps(green, source, parts, early)
-        entered = entering(entering_from_kernel, (base, parts, upto, local))
+        entered = entering(entering_from_kernel, (base, upto, local))
     arrived = exchange(*entered, sections)
     prop = propagator(tiles, green, coupling, entered[0])
     return final_waves(arrived, prop, image)[None]

time: 51.3 us -> 51.8 us (level)
  no operation moved by 1% of the time
where the time goes in v22:
time: 51.8 us; the launch traced here: 51.4 us
  starting transfers between devices  22.8 us (44%)
  Pallas kernels  15.4 us (30%)
  waiting for transfers between devices  10.7 us (21%)
  local copies, waits for them, and re-layouts  2.2 us (4%)
    ppermute x3, waiting for transfers between devices, to_across(): lax.ppermute(item, 'sec', [(s, s // GROUP * GROUP + (s % GROUP + CORES) %...  10.6 us
    ppermute x4, starting transfers between devices, between(): return lax.ppermute(item, 'sec', pairs)  7.73 us
    all_to_all x1, starting transfers between devices, per_device(): lax.all_to_all(outgoing, 'sec', split_axis=0, concat_axis=0, tiled=True)  7.63 us
    pallas_call x1, Pallas kernels, outgoing_pairs(): call(pairs_kernel, 'pairs', [IN_HBM] * 4, shape(sections, CAP * energies...  4.4 us
    ppermute x3, starting transfers between devices, to_across(): lax.ppermute(item, 'sec', [(s, s // GROUP * GROUP + (s % GROUP + CORES) %...  2.99 us
    ppermute x2, starting transfers between devices, to_far(): lax.ppermute(item, 'sec', [(s, s // GROUP * GROUP + (s % GROUP + CORES) %...  2.37 us
    unnamed x10, local copies, waits for them, and re-layouts  2.2 us
    pallas_call x2, Pallas kernels, image_and_maps(): call(functools.partial(work_kernel, not held), 'image_and_maps', [IN_VMEM...  1.98 us
  transfers between devices with their start and end apart: 16, of which 4 were waited for; matrix products, arithmetic and copies ran while one was open for 0% of the time, Pallas kernels for 16%

profile of v22, /device:TPU:0, one launch (start us, length us, event | category | flops | bytes accessed | tf_op | source)
XLA Modules:
  0.0 51.4 jit_solution(7433309284220337417)
XLA Ops:
  0.0 4.4 %pairs.1 = bf16[16,136,128]{2,1,0:T(8,128)(2,1)} custom-call(s32[16]{0:T(128)} %bitcast.21, s32[2,16]{1,0:T(2,128)} %bitcast.20, bf16[2,1024,1024]{2,1,0:T(8,128)(2,1)} %bitcast.9, bf16[2,1024,128]{2,1,0:T(8,128)(2,1)} %bitcast.14), custom_call_target="tpu_custom_call" | custom-call | flops 4600000000 | tf_op jit(solution)/shard_map/pairs/pallas_call | solution.py:168
  4.4 0.0 copy-start.2
  4.4 7.6 %all-to-all-start = ((bf16[16,136,128]{2,1,0:T(8,128)(2,1)}), bf16[16,136,128]{2,1,0:T(8,128)(2,1)S(1)}, u32[]{:S(2)}, u32[]{:S(2)}) async-start(bf16[16,136,128]{2,1,0:T(8,128)(2,1)} %pairs.1), calls=%async_computation | async-start | bytes 1114112 | tf_op jit(solution)/shard_map/all_to_all | solution.py:558
  12.1 0.0 copy-start
  12.1 2.2 %copy-done = bf16[1,2,1024,1024]{3,2,1,0:T(8,128)(2,1)S(1)} copy-done((bf16[1,2,1024,1024]{3,2,1,0:T(8,128)(2,1)S(1)}, bf16[1,2,1024,1024]{3,2,1,0:T(8,128)(2,1)}, u32[]{:S(2)}) %copy-start) | copy-done | bytes 4194328
  14.3 1.1 %face_maps.1 = (f32[256,256]{1,0:T(8,128)S(1)}, f32[256,256]{1,0:T(8,128)S(1)}, bf16[2,256,1024]{2,1,0:T(8,128)(2,1)S(1)}) custom-call(s32[2,8]{1,0:T(2,128)S(1)} %bitcast.18, bf16[2,1024,1024]{2,1,0:T(8,128)(2,1)S(1)} %bitcast.10, bf16[1024,256]{1,0:T(8,128)(2,1)S(1)} %bitcast.16), custom_call_target="tpu_custom_call" | custom-call | flops 1380000000 | tf_op jit(solution)/shard_map/face_maps/pallas_call | solution.py:206
  15.4 2.0 %collective-permute-start.3 = (f32[256,256]{1,0:T(8,128)S(1)}, f32[256,256]{1,0:T(8,128)S(1)}, u32[]{:S(2)}, u32[]{:S(2)}) collective-permute-start(f32[256,256]{1,0:T(8,128)S(1)} %get-tuple-element.31), channel_id=1, source_target_pairs={{0,2},{1,3},{2,0},{3,1},{4,6},{5,7},{6,4},{7,5},{8,10},{9,11},{10,... | collective-permute-start | bytes 786440 | tf_op jit(solution)/shard_map/ppermute | solution.py:502
  17.4 0.0 collective-permute-start.5
  17.4 9.9 %collective-permute-done.3._map = f32[256,256]{1,0:T(8,128)S(1)} collective-permute-done((f32[256,256]{1,0:T(8,128)S(1)}, f32[256,256]{1,0:T(8,128)S(1)}, u32[]{:S(2)}, u32[]{:S(2)}) %collective-permute-start.3) | collective-permute-done | bytes 262176 | tf_op jit(solution)/shard_map/ppermute | solution.py:502
  27.3 0.0 all-to-all-done.received._packets
  27.3 0.0 collective-permute-start.4
  27.3 0.0 copy-done.2
  27.3 0.0 copy-start.1
  27.3 1.4 %source_and_face.1 = (bf16[2,1024,128]{2,1,0:T(8,128)(2,1)S(1)}, bf16[128,128]{1,0:T(8,128)(2,1)S(1)}, bf16[128,128]{1,0:T(8,128)(2,1)S(1)}, bf16[128,128]{1,0:T(8,128)(2,1)S(1)}, bf16[128,128]{1,0:T(8,128)(2,1)S(1)}) custom-call(bf16[16,136,128]{2,1,0:T(8,128)(2,1)S(1)} %all-to-all-done.received._packets, bf16[2,1024,128]{2,1,0:T(8,128)(2,1)S(1)} %bitcast.15, ...), custom_call_target="tpu_custom_call" | custom-call | flops 1610000000 | tf_op jit(solution)/shard_map/source_and_face/pallas_call | solution.py:334
  28.8 1.8 %collective-permute-start = (bf16[128,128]{1,0:T(8,128)(2,1)S(1)}, bf16[128,128]{1,0:T(8,128)(2,1)S(1)}, u32[]{:S(2)}, u32[]{:S(2)}) collective-permute-start(bf16[128,128]{1,0:T(8,128)(2,1)S(1)} %get-tuple-element.27), channel_id=1, source_target_pairs={{0,3},{1,2},{2,1},{3,0},{4,7},{5,6},{6,5},{7,4},{8,11},{9,10},{10,... | collective-permute-start | bytes 98312 | tf_op jit(solution)/shard_map/ppermute | solution.py:506
  30.6 0.4 collective-permute-start.1
  30.9 0.0 collective-permute-start.2
  30.9 0.0 collective-permute-done.5.near
  30.9 0.0 collective-permute-done.4.far
  30.9 0.9 %chain_maps.1 = (bf16[256,256]{1,0:T(8,128)(2,1)S(1)}, bf16[4,512,256]{2,1,0:T(8,128)(2,1)S(1)}) custom-call(f32[256,256]{1,0:T(8,128)S(1)} %get-tuple-element.30.own, f32[256,256]{1,0:T(8,128)S(1)} %collective-permute-done.4.far, f32[256,256]{1,0:T(8,128)S(1)} %after_exchange.1.across, f32[256,256]{1,0:T(8,128)S(1)} %collective-permute-done.5.near), custom_call_target="tpu_custom_call" | custom-call | flops 1035000000 | tf_op jit(solution)/shard_map/chain_maps/pallas_call | solution.py:266
  31.9 0.7 %collective-permute-start.10 = (bf16[256,256]{1,0:T(8,128)(2,1)S(1)}, bf16[256,256]{1,0:T(8,128)(2,1)S(1)}, u32[]{:S(2)}, u32[]{:S(2)}) collective-permute-start(bf16[256,256]{1,0:T(8,128)(2,1)S(1)} %get-tuple-element.36), channel_id=1, source_target_pairs={{4,8},{8,12},{5,13},{6,10},{10,14},{7,15},{20,24},{24,28},{21,29},... | collective-permute-start | bytes 393224 | tf_op jit(solution)/shard_map/ppermute | solution.py:529
  32.5 0.0 copy-done.1
  32.5 1.8 %image_and_maps.2 = (f32[2,1024,128]{2,1,0:T(8,128)S(1)}, bf16[1536,256]{1,0:T(8,128)(2,1)S(1)}) custom-call(bf16[2,1024,1024]{2,1,0:T(8,128)(2,1)S(1)} %bitcast.11, bf16[2,1024,128]{2,1,0:T(8,128)(2,1)S(1)} %get-tuple-element.33.refs_1_, bf16[4,512,256]{2,1,0:T(8,128)(2,1)S(1)} %get-tuple-element.32.refs_2_.parts), custom_call_target="tpu_custom_call" | custom-call | flops 2300000000 | tf_op jit(solution)/shard_map/image_and_maps/pallas_call | solution.py:406
  34.4 0.0 collective-permute-done.far
  34.4 0.1 collective-permute-done.1.across
  34.5 0.0 collective-permute-done.2.near
  34.5 1.2 %plane_total.1 = (bf16[128,128]{1,0:T(8,128)(2,1)S(1)}, f32[3,256,128]{2,1,0:T(8,128)S(1)}) custom-call(bf16[128,128]{1,0:T(8,128)(2,1)S(1)} %get-tuple-element.26.own, bf16[128,128]{1,0:T(8,128)(2,1)S(1)} %collective-permute-done.far, bf16[128,128]{1,0:T(8,128)(2,1)S(1)} %collective-permute-done.1.across, bf16[128,128]{1,0:T(8,128)(2,1)S(1)} %collective-permute-done.2.near, ...), custom_call_target="tpu_custom_call" | custom-call | flops 3449999872 | tf_op jit(solution)/shard_map/plane_total/pallas_call | solution.py:370
  35.6 4.5 %collective-permute-start.6 = (bf16[128,128]{1,0:T(8,128)(2,1)S(1)}, bf16[128,128]{1,0:T(8,128)(2,1)S(1)}, u32[]{:S(2)}, u32[]{:S(2)}) collective-permute-start(bf16[128,128]{1,0:T(8,128)(2,1)S(1)} %get-tuple-element.35), channel_id=1, source_target_pairs={{0,12},{1,13},{2,14},{3,15},{16,28},{17,29},{18,30},{19,31}} | collective-permute-start | bytes 98312 | tf_op jit(solution)/shard_map/ppermute | solution.py:535
  40.1 1.3 %collective-permute-start.7 = (bf16[128,128]{1,0:T(8,128)(2,1)S(1)}, bf16[128,128]{1,0:T(8,128)(2,1)S(1)}, u32[]{:S(2)}, u32[]{:S(2)}) collective-permute-start(bf16[128,128]{1,0:T(8,128)(2,1)S(1)} %get-tuple-element.35), channel_id=1, source_target_pairs={{0,4},{1,5},{2,6},{3,7},{16,20},{17,21},{18,22},{19,23}} | collective-permute-start | bytes 98312 | tf_op jit(solution)/shard_map/ppermute | solution.py:535
  41.4 1.3 %collective-permute-start.8 = (bf16[128,128]{1,0:T(8,128)(2,1)S(1)}, bf16[128,128]{1,0:T(8,128)(2,1)S(1)}, u32[]{:S(2)}, u32[]{:S(2)}) collective-permute-start(bf16[128,128]{1,0:T(8,128)(2,1)S(1)} %get-tuple-element.35), channel_id=1, source_target_pairs={{0,8},{1,9},{2,10},{3,11},{4,12},{5,13},{6,14},{7,15},{16,24},{17,... | collective-permute-start | bytes 98312 | tf_op jit(solution)/shard_map/ppermute | solution.py:535
  42.7 0.7 %collective-permute-start.9 = (bf16[128,128]{1,0:T(8,128)(2,1)S(1)}, bf16[128,128]{1,0:T(8,128)(2,1)S(1)}, u32[]{:S(2)}, u32[]{:S(2)}) collective-permute-start(bf16[128,128]{1,0:T(8,128)(2,1)S(1)} %get-tuple-element.35), channel_id=1, source_target_pairs={{4,8},{5,9},{6,10},{7,11},{8,12},{9,13},{10,14},{11,15},{20,24},{2... | collective-permute-start | bytes 98312 | tf_op jit(solution)/shard_map/ppermute | solution.py:535
  43.4 0.0 collective-permute-done.10.got
  43.4 0.7 %collective-permute-start.11 = (bf16[256,256]{1,0:T(8,128)(2,1)S(1)}, bf16[256,256]{1,0:T(8,128)(2,1)S(1)}, u32[]{:S(2)}, u32[]{:S(2)}) collective-permute-start(bf16[256,256]{1,0:T(8,128)(2,1)S(1)} %collective-permute-done.10.got), channel_id=1, source_target_pairs={{8,9},{9,8},{10,11},{11,10},{12,13},{13,12},{14,15},{15,14},{24,25... | collective-permute-start | bytes 393224 | tf_op jit(solution)/shard_map/ppermute | solution.py:530
  44.1 0.1 image_and_maps.3
  44.2 0.0 collective-permute-done.6.third
  44.3 0.0 collective-permute-done.7.near_one
  44.3 0.1 collective-permute-done.8.second
  44.3 0.0 collective-permute-done.9.far_one
  44.3 0.0 collective-permute-done.11.other
  44.3 1.3 %entering.1 = (bf16[128,128]{1,0:T(8,128)(2,1)S(1)}, bf16[128,128]{1,0:T(8,128)(2,1)S(1)}, bf16[128,128]{1,0:T(8,128)(2,1)S(1)}, bf16[128,128]{1,0:T(8,128)(2,1)S(1)}) custom-call(bf16[128,128]{1,0:T(8,128)(2,1)S(1)} %collective-permute-done.6.third, bf16[128,128]{1,0:T(8,128)(2,1)S(1)} %collective-permute-done.7.near_one, ...), custom_call_target="tpu_custom_call" | custom-call | flops 1610000000 | tf_op jit(solution)/shard_map/entering/pallas_call | solution.py:446
  45.6 0.6 %collective-permute-start.12 = (bf16[128,128]{1,0:T(8,128)(2,1)S(1)}, bf16[128,128]{1,0:T(8,128)(2,1)S(1)}, u32[]{:S(2)}, u32[]{:S(2)}) collective-permute-start(bf16[128,128]{1,0:T(8,128)(2,1)S(1)} %get-tuple-element.41), channel_id=1, source_target_pairs={{0,3},{1,2},{2,1},{3,0},{4,7},{5,6},{6,5},{7,4},{8,11},{9,10},{10,... | collective-permute-start | bytes 98312 | tf_op jit(solution)/shard_map/ppermute | solution.py:506
  46.2 0.6 %collective-permute-start.13 = (bf16[128,128]{1,0:T(8,128)(2,1)S(1)}, bf16[128,128]{1,0:T(8,128)(2,1)S(1)}, u32[]{:S(2)}, u32[]{:S(2)}) collective-permute-start(bf16[128,128]{1,0:T(8,128)(2,1)S(1)} %get-tuple-element.42), channel_id=1, source_target_pairs={{0,2},{1,3},{2,0},{3,1},{4,6},{5,7},{6,4},{7,5},{8,10},{9,11},{10,... | collective-permute-start | bytes 98312 | tf_op jit(solution)/shard_map/ppermute | solution.py:502
  46.8 0.7 %collective-permute-start.14 = (bf16[128,128]{1,0:T(8,128)(2,1)S(1)}, bf16[128,128]{1,0:T(8,128)(2,1)S(1)}, u32[]{:S(2)}, u32[]{:S(2)}) collective-permute-start(bf16[128,128]{1,0:T(8,128)(2,1)S(1)} %get-tuple-element.43), channel_id=1, source_target_pairs={{0,1},{1,0},{2,3},{3,2},{4,5},{5,4},{6,7},{7,6},{8,9},{9,8},{10,11... | collective-permute-start | bytes 98312 | tf_op jit(solution)/shard_map/ppermute | solution.py:498
  47.6 1.9 %prop.1 = bf16[2,1024,256]{2,1,0:T(8,128)(2,1)S(1)} custom-call(s32[2,8]{1,0:T(2,128)S(1)} %bitcast.19, bf16[2,1024,1024]{2,1,0:T(8,128)(2,1)S(1)} %bitcast.13, bf16[1024,256]{1,0:T(8,128)(2,1)S(1)} %bitcast.17, bf16[128,128]{1,0:T(8,128)(2,1)S(1)} %get-tuple-element.40._tie.own), custom_call_target="tpu_custom_call" | custom-call | flops 1724999936 | tf_op jit(solution)/shard_map/prop/pallas_call | solution.py:225
  49.5 0.0 collective-permute-done.12.far
  49.5 0.6 %collective-permute-done.13.across = bf16[128,128]{1,0:T(8,128)(2,1)S(1)} collective-permute-done((bf16[128,128]{1,0:T(8,128)(2,1)S(1)}, bf16[128,128]{1,0:T(8,128)(2,1)S(1)}, u32[]{:S(2)}, u32[]{:S(2)}) %collective-permute-start.13) | collective-permute-done | bytes 32800 | tf_op jit(solution)/shard_map/ppermute | solution.py:502
  50.1 0.0 collective-permute-done.14.near
  50.1 1.3 %waves.1 = bf16[2,1024,128]{2,1,0:T(8,128)(2,1)} custom-call(bf16[128,128]{1,0:T(8,128)(2,1)S(1)} %get-tuple-element.40._tie.own, bf16[128,128]{1,0:T(8,128)(2,1)S(1)} %collective-permute-done.12.far, bf16[128,128]{1,0:T(8,128)(2,1)S(1)} %collective-permute-done.13.across, bf16[128,128]{1,0:T(8,128)(2,1)S(1)} %collective-permute-done.14.near, ...), custom_call_target="tpu_custom_call" | custom-call | flops 1495000064 | tf_op jit(solution)/shard_map/waves/pallas_call | solution.py:481
  (5 shorter events, 0.0 us)
Async XLA Ops:
  0.0 12.1 %copy-start.3 = (bf16[1,1024,256]{2,1,0:T(8,128)(2,1)S(1)}, bf16[1,1024,256]{2,1,0:T(8,128)(2,1)}, u32[]{:S(2)}) copy-start(bf16[1,1024,256]{2,1,0:T(8,128)(2,1)} %param.8) | copy-start | bytes 1572868
  0.0 12.1 %copy-start.4 = (s32[1,8,2]{1,2,0:T(2,128)S(1)}, s32[1,8,2]{1,2,0:T(2,128)}, u32[]{:S(2)}) copy-start(s32[1,8,2]{1,2,0:T(2,128)} %param.9) | copy-start | bytes 196
  4.4 22.9 %copy-start.2 = (bf16[1,2,1024,128]{3,2,1,0:T(8,128)(2,1)S(1)}, bf16[1,2,1024,128]{3,2,1,0:T(8,128)(2,1)}, u32[]{:S(2)}) copy-start(bf16[1,2,1024,128]{3,2,1,0:T(8,128)(2,1)} %param.7) | copy-start | bytes 1572868
  4.4 22.9 %all-to-all-start = ((bf16[16,136,128]{2,1,0:T(8,128)(2,1)}), bf16[16,136,128]{2,1,0:T(8,128)(2,1)S(1)}, u32[]{:S(2)}, u32[]{:S(2)}) async-start(bf16[16,136,128]{2,1,0:T(8,128)(2,1)} %pairs.1), calls=%async_computation | async-start | bytes 1114112 | tf_op jit(solution)/shard_map/all_to_all | solution.py:558
  12.1 2.2 %copy-start = (bf16[1,2,1024,1024]{3,2,1,0:T(8,128)(2,1)S(1)}, bf16[1,2,1024,1024]{3,2,1,0:T(8,128)(2,1)}, u32[]{:S(2)}) copy-start(bf16[1,2,1024,1024]{3,2,1,0:T(8,128)(2,1)} %param.6) | copy-start | bytes 12582916
  15.4 11.9 %collective-permute-start.3 = (f32[256,256]{1,0:T(8,128)S(1)}, f32[256,256]{1,0:T(8,128)S(1)}, u32[]{:S(2)}, u32[]{:S(2)}) collective-permute-start(f32[256,256]{1,0:T(8,128)S(1)} %get-tuple-element.31), channel_id=1, source_target_pairs={{0,2},{1,3},{2,0},{3,1},{4,6},{5,7},{6,4},{7,5},{8,10},{9,11},{10,... | collective-permute-start | bytes 786440 | tf_op jit(solution)/shard_map/ppermute | solution.py:502
  17.4 13.6 %collective-permute-start.5 = (f32[256,256]{1,0:T(8,128)S(1)}, f32[256,256]{1,0:T(8,128)S(1)}, u32[]{:S(2)}, u32[]{:S(2)}) collective-permute-start(f32[256,256]{1,0:T(8,128)S(1)} %get-tuple-element.30.own), channel_id=1, source_target_pairs={{0,1},{1,0},{2,3},{3,2},{4,5},{5,4},{6,7},{7,6},{8,9},{9,8},{10,11... | collective-permute-start | bytes 786440 | tf_op jit(solution)/shard_map/ppermute | solution.py:498
  27.3 3.6 %collective-permute-start.4 = (f32[256,256]{1,0:T(8,128)S(1)}, f32[256,256]{1,0:T(8,128)S(1)}, u32[]{:S(2)}, u32[]{:S(2)}) collective-permute-start(f32[256,256]{1,0:T(8,128)S(1)} %after_exchange.1.across), channel_id=1, source_target_pairs={{0,1},{1,0},{2,3},{3,2},{4,5},{5,4},{6,7},{7,6},{8,9},{9,8},{10,11... | collective-permute-start | bytes 786440 | tf_op jit(solution)/shard_map/ppermute | solution.py:498
  27.3 5.2 %copy-start.1 = (bf16[1,2,1024,1024]{3,2,1,0:T(8,128)(2,1)S(1)}, bf16[1,2,1024,1024]{3,2,1,0:T(8,128)(2,1)}, u32[]{:S(2)}) copy-start(bf16[1,2,1024,1024]{3,2,1,0:T(8,128)(2,1)} %param.6) | copy-start | bytes 12582916
  28.8 5.6 %collective-permute-start = (bf16[128,128]{1,0:T(8,128)(2,1)S(1)}, bf16[128,128]{1,0:T(8,128)(2,1)S(1)}, u32[]{:S(2)}, u32[]{:S(2)}) collective-permute-start(bf16[128,128]{1,0:T(8,128)(2,1)S(1)} %get-tuple-element.27), channel_id=1, source_target_pairs={{0,3},{1,2},{2,1},{3,0},{4,7},{5,6},{6,5},{7,4},{8,11},{9,10},{10,... | collective-permute-start | bytes 98312 | tf_op jit(solution)/shard_map/ppermute | solution.py:506
  30.6 3.9 %collective-permute-start.1 = (bf16[128,128]{1,0:T(8,128)(2,1)S(1)}, bf16[128,128]{1,0:T(8,128)(2,1)S(1)}, u32[]{:S(2)}, u32[]{:S(2)}) collective-permute-start(bf16[128,128]{1,0:T(8,128)(2,1)S(1)} %get-tuple-element.28), channel_id=1, source_target_pairs={{0,2},{1,3},{2,0},{3,1},{4,6},{5,7},{6,4},{7,5},{8,10},{9,11},{10,... | collective-permute-start | bytes 98312 | tf_op jit(solution)/shard_map/ppermute | solution.py:502
  30.9 3.6 %collective-permute-start.2 = (bf16[128,128]{1,0:T(8,128)(2,1)S(1)}, bf16[128,128]{1,0:T(8,128)(2,1)S(1)}, u32[]{:S(2)}, u32[]{:S(2)}) collective-permute-start(bf16[128,128]{1,0:T(8,128)(2,1)S(1)} %get-tuple-element.29), channel_id=1, source_target_pairs={{0,1},{1,0},{2,3},{3,2},{4,5},{5,4},{6,7},{7,6},{8,9},{9,8},{10,11... | collective-permute-start | bytes 98312 | tf_op jit(solution)/shard_map/ppermute | solution.py:498
  31.9 11.6 %collective-permute-start.10 = (bf16[256,256]{1,0:T(8,128)(2,1)S(1)}, bf16[256,256]{1,0:T(8,128)(2,1)S(1)}, u32[]{:S(2)}, u32[]{:S(2)}) collective-permute-start(bf16[256,256]{1,0:T(8,128)(2,1)S(1)} %get-tuple-element.36), channel_id=1, source_target_pairs={{4,8},{8,12},{5,13},{6,10},{10,14},{7,15},{20,24},{24,28},{21,29},... | collective-permute-start | bytes 393224 | tf_op jit(solution)/shard_map/ppermute | solution.py:529
  35.6 8.6 %collective-permute-start.6 = (bf16[128,128]{1,0:T(8,128)(2,1)S(1)}, bf16[128,128]{1,0:T(8,128)(2,1)S(1)}, u32[]{:S(2)}, u32[]{:S(2)}) collective-permute-start(bf16[128,128]{1,0:T(8,128)(2,1)S(1)} %get-tuple-element.35), channel_id=1, source_target_pairs={{0,12},{1,13},{2,14},{3,15},{16,28},{17,29},{18,30},{19,31}} | collective-permute-start | bytes 98312 | tf_op jit(solution)/shard_map/ppermute | solution.py:535
  40.1 4.1 %collective-permute-start.7 = (bf16[128,128]{1,0:T(8,128)(2,1)S(1)}, bf16[128,128]{1,0:T(8,128)(2,1)S(1)}, u32[]{:S(2)}, u32[]{:S(2)}) collective-permute-start(bf16[128,128]{1,0:T(8,128)(2,1)S(1)} %get-tuple-element.35), channel_id=1, source_target_pairs={{0,4},{1,5},{2,6},{3,7},{16,20},{17,21},{18,22},{19,23}} | collective-permute-start | bytes 98312 | tf_op jit(solution)/shard_map/ppermute | solution.py:535
  41.4 2.9 %collective-permute-start.8 = (bf16[128,128]{1,0:T(8,128)(2,1)S(1)}, bf16[128,128]{1,0:T(8,128)(2,1)S(1)}, u32[]{:S(2)}, u32[]{:S(2)}) collective-permute-start(bf16[128,128]{1,0:T(8,128)(2,1)S(1)} %get-tuple-element.35), channel_id=1, source_target_pairs={{0,8},{1,9},{2,10},{3,11},{4,12},{5,13},{6,14},{7,15},{16,24},{17,... | collective-permute-start | bytes 98312 | tf_op jit(solution)/shard_map/ppermute | solution.py:535
  42.7 1.6 %collective-permute-start.9 = (bf16[128,128]{1,0:T(8,128)(2,1)S(1)}, bf16[128,128]{1,0:T(8,128)(2,1)S(1)}, u32[]{:S(2)}, u32[]{:S(2)}) collective-permute-start(bf16[128,128]{1,0:T(8,128)(2,1)S(1)} %get-tuple-element.35), channel_id=1, source_target_pairs={{4,8},{5,9},{6,10},{7,11},{8,12},{9,13},{10,14},{11,15},{20,24},{2... | collective-permute-start | bytes 98312 | tf_op jit(solution)/shard_map/ppermute | solution.py:535
  43.4 0.9 %collective-permute-start.11 = (bf16[256,256]{1,0:T(8,128)(2,1)S(1)}, bf16[256,256]{1,0:T(8,128)(2,1)S(1)}, u32[]{:S(2)}, u32[]{:S(2)}) collective-permute-start(bf16[256,256]{1,0:T(8,128)(2,1)S(1)} %collective-permute-done.10.got), channel_id=1, source_target_pairs={{8,9},{9,8},{10,11},{11,10},{12,13},{13,12},{14,15},{15,14},{24,25... | collective-permute-start | bytes 393224 | tf_op jit(solution)/shard_map/ppermute | solution.py:530
  45.6 3.8 %collective-permute-start.12 = (bf16[128,128]{1,0:T(8,128)(2,1)S(1)}, bf16[128,128]{1,0:T(8,128)(2,1)S(1)}, u32[]{:S(2)}, u32[]{:S(2)}) collective-permute-start(bf16[128,128]{1,0:T(8,128)(2,1)S(1)} %get-tuple-element.41), channel_id=1, source_target_pairs={{0,3},{1,2},{2,1},{3,0},{4,7},{5,6},{6,5},{7,4},{8,11},{9,10},{10,... | collective-permute-start | bytes 98312 | tf_op jit(solution)/shard_map/ppermute | solution.py:506
  46.2 3.9 %collective-permute-start.13 = (bf16[128,128]{1,0:T(8,128)(2,1)S(1)}, bf16[128,128]{1,0:T(8,128)(2,1)S(1)}, u32[]{:S(2)}, u32[]{:S(2)}) collective-permute-start(bf16[128,128]{1,0:T(8,128)(2,1)S(1)} %get-tuple-element.42), channel_id=1, source_target_pairs={{0,2},{1,3},{2,0},{3,1},{4,6},{5,7},{6,4},{7,5},{8,10},{9,11},{10,... | collective-permute-start | bytes 98312 | tf_op jit(solution)/shard_map/ppermute | solution.py:502
  46.8 3.3 %collective-permute-start.14 = (bf16[128,128]{1,0:T(8,128)(2,1)S(1)}, bf16[128,128]{1,0:T(8,128)(2,1)S(1)}, u32[]{:S(2)}, u32[]{:S(2)}) collective-permute-start(bf16[128,128]{1,0:T(8,128)(2,1)S(1)} %get-tuple-element.43), channel_id=1, source_target_pairs={{0,1},{1,0},{2,3},{3,2},{4,5},{5,4},{6,7},{7,6},{8,9},{9,8},{10,11... | collective-permute-start | bytes 98312 | tf_op jit(solution)/shard_map/ppermute | solution.py:498

commit v23 on v21

--- a/solution.py
+++ b/solution.py
@@ -68,22 +68,15 @@
     return high, (x - high.astype(F32)).astype(BF16)
 
 
-def left_lanes(x):
-    return lax.broadcasted_iota(jnp.int32, x.shape, 1) < x.shape[1] // 2
-
-
-def swap_lanes(x):
-    return pltpu.roll(x, x.shape[1] // 2, 1)
-
-
-def pack(tall):
-    half = tall.shape[0] // 2
-    top, low = tall[:half], tall[half:]
-    return jnp.where(left_lanes(top), top, swap_lanes(low))
-
-
-def unpack(packed):
-    return jnp.concatenate([packed, swap_lanes(packed)], axis=0)
+def dot_rows(a, b):
+    return lax.dot_general(a, b, (((1,), (1,)), ((), ())), preferred_element_type=F32)
+
+
+def step_by(state, maps):
+    high, low = two_parts(state)
+    rows = state.shape[0]
+    y = dot_rows(jnp.concatenate([high, low], axis=0), maps[0])
+    return y[:rows] + (y[rows:] + dot_rows(high, maps[1]))
 
 
 def mask_tiles(pattern, coupling):
@@ -261,7 +254,7 @@
 def source_kernel(received, inject, face_rows, source, own, far, across, near, quarters, total, heads, targets, sem):
     energies, orbitals, columns = inject.shape
     sections = received.shape[0]
-    half = quarters.shape[1]
+    wide_rows = quarters.shape[1]
     rows = CAP * energies * BLK
 
     def read(s, _):
@@ -288,9 +281,9 @@
     for e in range(energies):
         source[e] = total[e].astype(BF16)
         tall = dot(face_rows[e], source[e])
-        quarters[e * split] = pack(tall)
-        second = jnp.where(left_lanes(tall[:half]), swap_lanes(tall[:half]), tall[half:])
-        quarters[e * split + 1] = second
+        wide = tall.T
+        for h in range(split):
+            quarters[e * split + h] = wide[h * wide_rows : (h + 1) * wide_rows]
     for out, at in zip((own, far, across, near), partners()):
         out[...] = quarters[at].astype(BF16)
 
@@ -319,9 +312,9 @@
         source_kernel,
         "source_and_face",
         [IN_VMEM, IN_VMEM, IN_VMEM],
-        [shape(*inject.shape)] + [shape(face // 2, columns)] * GROUP,
+        [shape(*inject.shape)] + [shape(columns * energies // GROUP, face)] * GROUP,
         [
-            pltpu.VMEM((GROUP, face // 2, columns), F32),
+            pltpu.VMEM((GROUP, columns * energies // GROUP, face), F32),
             pltpu.VMEM(inject.shape, F32),
             pltpu.VMEM((sections, columns), jnp.int32),
             pltpu.SMEM((sections, columns), jnp.int32),
@@ -336,27 +329,23 @@
         held[at] = ref[...]
 
 
-def step(parts, j, shift, state):
-    return unpack(shift.astype(F32)) + times((parts[0, j], parts[1, j]), two_parts(state))
-
-
 def total_kernel(own, far, across, near, parts, _image, out, local, shifts):
     collect((own, far, across, near), shifts)
-    state = unpack(shifts[0].astype(F32))
+    state = shifts[0].astype(F32)
     for j in range(1, GROUP):
         local[j - 1] = state
-        state = step(parts, j, shifts[j], state)
-    out[...] = pack(state).astype(BF16)
+        state = shifts[j].astype(F32) + step_by(state, (parts[0, j], parts[1, j]))
+    out[...] = state.astype(BF16)
 
 
 def plane_total(shifts, parts, tie):
-    half, columns = shifts[0].shape
+    rows, face = shifts[0].shape
     return call(
         total_kernel,
         "plane_total",
         [IN_VMEM] * (GROUP + 1) + [IN_PLACE],
-        [shape(half, columns), shape(GROUP - 1, 2 * half, columns, dtype=F32)],
-        [pltpu.VMEM((GROUP, half, columns), BF16)],
+        [shape(rows, face), shape(GROUP - 1, rows, face, dtype=F32)],
+        [pltpu.VMEM((GROUP, rows, face), BF16)],
         3.0,
     )(*shifts, parts, tie)
 
@@ -396,11 +385,10 @@
 
 
 def sweep_plane(state, parts, upto, local, out):
-    two = two_parts(state)
-    held = [pack(state)]
+    held = [state]
     for j in range(1, GROUP):
         maps = (parts[0, 0], parts[1, 0]) if j == 1 else (upto[0, j - 2], upto[1, j - 2])
-        held.append(pack(local[j - 1] + times(maps, two)))
+        held.append(local[j - 1] + step_by(state, maps))
     work = out[GROUP]
     for j, item in enumerate(held):
         work[j] = item
@@ -411,16 +399,17 @@
 def entering_kernel(third, near_one, second, far_one, got, other, parts, upto, local, *out):
     first_core = place() % CORES == 0
     first = near_one[...].astype(F32) + far_one[...].astype(F32)
-    state = unpack(third[...].astype(F32))
+    state = third[...].astype(F32)
+    rows = state.shape[0]
     for below, (one, two) in ((second[...].astype(F32), (other, got)), (first, (got, other))):
         factor = jnp.where(first_core, one[...], two[...])
-        high, low = two_parts(state)
-        state = unpack(below) + dot(factor, high) + dot(factor, low)
+        y = dot_rows(jnp.concatenate(two_parts(state), axis=0), factor)
+        state = below + (y[:rows] + y[rows:])
     sweep_plane(state, parts, upto, local, out)
 
 
 def entering_from_kernel(base, parts, upto, local, *out):
-    sweep_plane(unpack(base[...]), parts, upto, local, out)
+    sweep_plane(base[...], parts, upto, local, out)
 
 
 def entering(body, args):
@@ -443,14 +432,10 @@
     size = orbitals // pieces
     moves = []
     for e in range(energies):
-        first, second = arrived[e * split].astype(F32), arrived[e * split + 1].astype(F32)
-        left = left_lanes(first)
-        top = jnp.where(left, first, swap_lanes(second))
-        low = jnp.where(left, swap_lanes(first), second)
-        incoming = jnp.concatenate([top, low], axis=0).astype(BF16)
+        incoming = jnp.concatenate([arrived[e * split + h] for h in range(split)], axis=0)
         for c in range(pieces):
             at = slice(c * size, (c + 1) * size)
-            wave[e, at, :] = (dot(prop[e, at, :], incoming) + image[e, at, :]).astype(BF16)
+            wave[e, at, :] = (dot_rows(prop[e, at, :], incoming) + image[e, at, :]).astype(BF16)
             moves.append(pltpu.make_async_copy(wave.at[e, pl.ds(c * size, size)], out.at[e, pl.ds(c * size, size)], sem.at[e, c]))
             moves[-1].start()
     for move in moves:
@@ -496,11 +481,6 @@
     return [(s, s + GROUP * k) for s in range(sections - GROUP * k)]
 
 
-def spread(packed):
-    half = packed.shape[1] // 2
-    return jnp.concatenate([packed[:, :half], packed[:, half:]], axis=0)
-
-
 def maps_up(total_map, sections):
     pairs = []
     for i in range(GROUP):
@@ -518,17 +498,16 @@
 
 
 def scan_below(total_map, total, sections):
-    shift = lax.ppermute(spread(total).astype(F32), "sec", up_shift(sections, 1))
+    shift = lax.ppermute(total.astype(F32), "sec", up_shift(sections, 1))
     joined = lax.ppermute(total_map, "sec", up_shift(sections, 1))
     stride = 1
     while stride < sections // GROUP:
         other = lax.ppermute(shift, "sec", up_shift(sections, stride))
         other_map = lax.ppermute(joined, "sec", up_shift(sections, stride))
-        shift = shift + dot_wide(joined, other)
+        shift = shift + dot_wide(other, joined.T)
         joined = dot_wide(joined, other_map)
         stride *= 2
-    half = shift.shape[0] // 2
-    return jnp.concatenate([shift[:half], shift[half:]], axis=1)
+    return shift
 
 
 def per_device(green, injected, coupling, pattern, owner, pair_blocks):

time: 51.3 us -> 50.4 us (0.982)
  Pallas kernels: 15 us -> 14.1 us
  transfers between devices with their start and end apart: 16 -> 16, of which waited for: 4 -> 4; matrix products, arithmetic and copies ran while one was open for 0% -> 0% of each run, Pallas kernels for 16% -> 15%
where the time goes in v23:
time: 50.4 us; the launch traced here: 50.1 us
  starting transfers between devices  22.8 us (45%)
  Pallas kernels  14.1 us (28%)
  waiting for transfers between devices  10.8 us (21%)
  local copies, waits for them, and re-layouts  2.2 us (4%)
    ppermute x3, waiting for transfers between devices, to_across(): lax.ppermute(item, 'sec', [(s, s // GROUP * GROUP + (s % GROUP + CORES) %...  10.7 us
    ppermute x4, starting transfers between devices, between(): return lax.ppermute(item, 'sec', pairs)  7.72 us
    all_to_all x1, starting transfers between devices, per_device(): lax.all_to_all(outgoing, 'sec', split_axis=0, concat_axis=0, tiled=True)  7.63 us
    pallas_call x1, Pallas kernels, outgoing_pairs(): call(pairs_kernel, 'pairs', [IN_HBM] * 4, shape(sections, CAP * energies...  4.4 us
    ppermute x3, starting transfers between devices, to_across(): lax.ppermute(item, 'sec', [(s, s // GROUP * GROUP + (s % GROUP + CORES) %...  2.99 us
    ppermute x2, starting transfers between devices, to_far(): lax.ppermute(item, 'sec', [(s, s // GROUP * GROUP + (s % GROUP + CORES) %...  2.28 us
    unnamed x10, local copies, waits for them, and re-layouts  2.2 us
    pallas_call x2, Pallas kernels, image_and_maps(): call(functools.partial(work_kernel, not held), 'image_and_maps', [IN_VMEM...  1.91 us
  transfers between devices with their start and end apart: 16, of which 4 were waited for; matrix products, arithmetic and copies ran while one was open for 0% of the time, Pallas kernels for 15%

profile of v23, /device:TPU:0, one launch (start us, length us, event | category | flops | bytes accessed | tf_op | source)
XLA Modules:
  0.0 50.1 jit_solution(18351442408455537031)
XLA Ops:
  0.0 4.4 %pairs.1 = bf16[16,136,128]{2,1,0:T(8,128)(2,1)} custom-call(s32[16]{0:T(128)} %bitcast.21, s32[2,16]{1,0:T(2,128)} %bitcast.20, bf16[2,1024,1024]{2,1,0:T(8,128)(2,1)} %bitcast.9, bf16[2,1024,128]{2,1,0:T(8,128)(2,1)} %bitcast.14), custom_call_target="tpu_custom_call" | custom-call | flops 4600000000 | tf_op jit(solution)/shard_map/pairs/pallas_call | solution.py:161
  4.4 0.0 copy-start.2
  4.4 7.6 %all-to-all-start = ((bf16[16,136,128]{2,1,0:T(8,128)(2,1)}), bf16[16,136,128]{2,1,0:T(8,128)(2,1)S(1)}, u32[]{:S(2)}, u32[]{:S(2)}) async-start(bf16[16,136,128]{2,1,0:T(8,128)(2,1)} %pairs.1), calls=%async_computation | async-start | bytes 1114112 | tf_op jit(solution)/shard_map/all_to_all | solution.py:519
  12.1 0.0 copy-done.3
  12.1 0.0 copy-done.4
  12.1 0.0 copy-start
  12.1 2.2 %copy-done = bf16[1,2,1024,1024]{3,2,1,0:T(8,128)(2,1)S(1)} copy-done((bf16[1,2,1024,1024]{3,2,1,0:T(8,128)(2,1)S(1)}, bf16[1,2,1024,1024]{3,2,1,0:T(8,128)(2,1)}, u32[]{:S(2)}) %copy-start) | copy-done | bytes 4194328
  14.3 1.1 %face_maps.1 = (f32[256,256]{1,0:T(8,128)S(1)}, f32[256,256]{1,0:T(8,128)S(1)}, bf16[2,256,1024]{2,1,0:T(8,128)(2,1)S(1)}) custom-call(s32[2,8]{1,0:T(2,128)S(1)} %bitcast.18, bf16[2,1024,1024]{2,1,0:T(8,128)(2,1)S(1)} %bitcast.10, bf16[1024,256]{1,0:T(8,128)(2,1)S(1)} %bitcast.16), custom_call_target="tpu_custom_call" | custom-call | flops 1380000000 | tf_op jit(solution)/shard_map/face_maps/pallas_call | solution.py:199
  15.4 2.0 %collective-permute-start.3 = (f32[256,256]{1,0:T(8,128)S(1)}, f32[256,256]{1,0:T(8,128)S(1)}, u32[]{:S(2)}, u32[]{:S(2)}) collective-permute-start(f32[256,256]{1,0:T(8,128)S(1)} %get-tuple-element.31), channel_id=1, source_target_pairs={{0,2},{1,3},{2,0},{3,1},{4,6},{5,7},{6,4},{7,5},{8,10},{9,11},{10,... | collective-permute-start | bytes 786440 | tf_op jit(solution)/shard_map/ppermute | solution.py:469
  17.4 0.0 collective-permute-start.5
  17.4 9.9 %collective-permute-done.3._map = f32[256,256]{1,0:T(8,128)S(1)} collective-permute-done((f32[256,256]{1,0:T(8,128)S(1)}, f32[256,256]{1,0:T(8,128)S(1)}, u32[]{:S(2)}, u32[]{:S(2)}) %collective-permute-start.3) | collective-permute-done | bytes 262176 | tf_op jit(solution)/shard_map/ppermute | solution.py:469
  27.3 0.0 all-to-all-done.received._packets
  27.3 0.0 collective-permute-start.4
  27.3 0.0 copy-start.1
  27.3 1.4 %source_and_face.1 = (bf16[2,1024,128]{2,1,0:T(8,128)(2,1)S(1)}, bf16[64,256]{1,0:T(8,128)(2,1)S(1)}, bf16[64,256]{1,0:T(8,128)(2,1)S(1)}, bf16[64,256]{1,0:T(8,128)(2,1)S(1)}, bf16[64,256]{1,0:T(8,128)(2,1)S(1)}) custom-call(bf16[16,136,128]{2,1,0:T(8,128)(2,1)S(1)} %all-to-all-done.received._packets, bf16[2,1024,128]{2,1,0:T(8,128)(2,1)S(1)} %bitcast.15, ...), custom_call_target="tpu_custom_call" | custom-call | flops 1610000000 | tf_op jit(solution)/shard_map/source_and_face/pallas_call | solution.py:311
  28.8 1.8 %collective-permute-start = (bf16[64,256]{1,0:T(8,128)(2,1)S(1)}, bf16[64,256]{1,0:T(8,128)(2,1)S(1)}, u32[]{:S(2)}, u32[]{:S(2)}) collective-permute-start(bf16[64,256]{1,0:T(8,128)(2,1)S(1)} %get-tuple-element.27), channel_id=1, source_target_pairs={{0,3},{1,2},{2,1},{3,0},{4,7},{5,6},{6,5},{7,4},{8,11},{9,10},{10,... | collective-permute-start | bytes 98312 | tf_op jit(solution)/shard_map/ppermute | solution.py:473
  30.6 0.3 collective-permute-start.1
  30.9 0.0 collective-permute-start.2
  30.9 0.0 collective-permute-done.5.near
  30.9 0.0 collective-permute-done.4.far
  30.9 0.8 %chain_maps.1 = (bf16[256,256]{1,0:T(8,128)(2,1)S(1)}, bf16[2,4,256,256]{3,2,1,0:T(8,128)(2,1)S(1)}) custom-call(f32[256,256]{1,0:T(8,128)S(1)} %get-tuple-element.30.own, f32[256,256]{1,0:T(8,128)S(1)} %collective-permute-done.4.far, f32[256,256]{1,0:T(8,128)S(1)} %after_exchange.1.across, f32[256,256]{1,0:T(8,128)S(1)} %collective-permute-done.5.near), custom_call_target="tpu_custom_call" | custom-call | flops 1035000000 | tf_op jit(solution)/shard_map/chain_maps/pallas_call | solution.py:244
  31.8 0.7 %collective-permute-start.10 = (bf16[256,256]{1,0:T(8,128)(2,1)S(1)}, bf16[256,256]{1,0:T(8,128)(2,1)S(1)}, u32[]{:S(2)}, u32[]{:S(2)}) collective-permute-start(bf16[256,256]{1,0:T(8,128)(2,1)S(1)} %get-tuple-element.36), channel_id=1, source_target_pairs={{4,8},{8,12},{5,13},{6,10},{10,14},{7,15},{20,24},{24,28},{21,29},... | collective-permute-start | bytes 393224 | tf_op jit(solution)/shard_map/ppermute | solution.py:491
  32.5 1.8 %image_and_maps.2 = (f32[2,1024,128]{2,1,0:T(8,128)S(1)}, bf16[2,2,256,256]{3,2,1,0:T(8,128)(2,1)S(1)}) custom-call(bf16[2,1024,1024]{2,1,0:T(8,128)(2,1)S(1)} %bitcast.11, bf16[2,1024,128]{2,1,0:T(8,128)(2,1)S(1)} %get-tuple-element.33.refs_1_, bf16[2,4,256,256]{3,2,1,0:T(8,128)(2,1)S(1)} %get-tuple-element.32.refs_2_.parts), custom_call_target="tpu_custom_call" | custom-call | flops 2300000000 | tf_op jit(solution)/shard_map/image_and_maps/pallas_call | solution.py:377
  34.3 0.0 collective-permute-done.far
  34.3 0.2 collective-permute-done.1.across
  34.5 0.0 collective-permute-done.2.near
  34.5 0.6 %plane_total.1 = (bf16[64,256]{1,0:T(8,128)(2,1)S(1)}, f32[3,64,256]{2,1,0:T(8,128)S(1)}) custom-call(bf16[64,256]{1,0:T(8,128)(2,1)S(1)} %get-tuple-element.26.own, bf16[64,256]{1,0:T(8,128)(2,1)S(1)} %collective-permute-done.far, bf16[64,256]{1,0:T(8,128)(2,1)S(1)} %collective-permute-done.1.across, bf16[64,256]{1,0:T(8,128)(2,1)S(1)} %collective-permute-done.2.near, ...), custom_call_target="tpu_custom_call" | custom-call | flops 3449999872 | tf_op jit(solution)/shard_map/plane_total/pallas_call | solution.py:343
  35.1 4.5 %collective-permute-start.6 = (bf16[64,256]{1,0:T(8,128)(2,1)S(1)}, bf16[64,256]{1,0:T(8,128)(2,1)S(1)}, u32[]{:S(2)}, u32[]{:S(2)}) collective-permute-start(bf16[64,256]{1,0:T(8,128)(2,1)S(1)} %get-tuple-element.35), channel_id=1, source_target_pairs={{0,12},{1,13},{2,14},{3,15},{16,28},{17,29},{18,30},{19,31}} | collective-permute-start | bytes 98312 | tf_op jit(solution)/shard_map/ppermute | solution.py:497
  39.6 1.3 %collective-permute-start.7 = (bf16[64,256]{1,0:T(8,128)(2,1)S(1)}, bf16[64,256]{1,0:T(8,128)(2,1)S(1)}, u32[]{:S(2)}, u32[]{:S(2)}) collective-permute-start(bf16[64,256]{1,0:T(8,128)(2,1)S(1)} %get-tuple-element.35), channel_id=1, source_target_pairs={{0,4},{1,5},{2,6},{3,7},{16,20},{17,21},{18,22},{19,23}} | collective-permute-start | bytes 98312 | tf_op jit(solution)/shard_map/ppermute | solution.py:497
  40.9 1.3 %collective-permute-start.8 = (bf16[64,256]{1,0:T(8,128)(2,1)S(1)}, bf16[64,256]{1,0:T(8,128)(2,1)S(1)}, u32[]{:S(2)}, u32[]{:S(2)}) collective-permute-start(bf16[64,256]{1,0:T(8,128)(2,1)S(1)} %get-tuple-element.35), channel_id=1, source_target_pairs={{0,8},{1,9},{2,10},{3,11},{4,12},{5,13},{6,14},{7,15},{16,24},{17,... | collective-permute-start | bytes 98312 | tf_op jit(solution)/shard_map/ppermute | solution.py:497
  42.2 0.7 %collective-permute-start.9 = (bf16[64,256]{1,0:T(8,128)(2,1)S(1)}, bf16[64,256]{1,0:T(8,128)(2,1)S(1)}, u32[]{:S(2)}, u32[]{:S(2)}) collective-permute-start(bf16[64,256]{1,0:T(8,128)(2,1)S(1)} %get-tuple-element.35), channel_id=1, source_target_pairs={{4,8},{5,9},{6,10},{7,11},{8,12},{9,13},{10,14},{11,15},{20,24},{2... | collective-permute-start | bytes 98312 | tf_op jit(solution)/shard_map/ppermute | solution.py:497
  42.8 0.0 collective-permute-done.10.got
  42.9 0.7 %collective-permute-start.11 = (bf16[256,256]{1,0:T(8,128)(2,1)S(1)}, bf16[256,256]{1,0:T(8,128)(2,1)S(1)}, u32[]{:S(2)}, u32[]{:S(2)}) collective-permute-start(bf16[256,256]{1,0:T(8,128)(2,1)S(1)} %collective-permute-done.10.got), channel_id=1, source_target_pairs={{8,9},{9,8},{10,11},{11,10},{12,13},{13,12},{14,15},{15,14},{24,25... | collective-permute-start | bytes 393224 | tf_op jit(solution)/shard_map/ppermute | solution.py:492
  43.5 0.1 image_and_maps.3
  43.7 0.0 collective-permute-done.6.third
  43.7 0.0 collective-permute-done.7.near_one
  43.7 0.1 collective-permute-done.8.second
  43.8 0.0 collective-permute-done.9.far_one
  43.8 0.0 collective-permute-done.11.other
  43.8 0.7 %entering.1 = (bf16[64,256]{1,0:T(8,128)(2,1)S(1)}, bf16[64,256]{1,0:T(8,128)(2,1)S(1)}, bf16[64,256]{1,0:T(8,128)(2,1)S(1)}, bf16[64,256]{1,0:T(8,128)(2,1)S(1)}) custom-call(bf16[64,256]{1,0:T(8,128)(2,1)S(1)} %collective-permute-done.6.third, bf16[64,256]{1,0:T(8,128)(2,1)S(1)} %collective-permute-done.7.near_one, ...), custom_call_target="tpu_custom_call" | custom-call | flops 1610000000 | tf_op jit(solution)/shard_map/entering/pallas_call | solution.py:417
  44.5 0.5 collective-permute-start.12
  45.0 0.6 %collective-permute-start.13 = (bf16[64,256]{1,0:T(8,128)(2,1)S(1)}, bf16[64,256]{1,0:T(8,128)(2,1)S(1)}, u32[]{:S(2)}, u32[]{:S(2)}) collective-permute-start(bf16[64,256]{1,0:T(8,128)(2,1)S(1)} %get-tuple-element.42), channel_id=1, source_target_pairs={{0,2},{1,3},{2,0},{3,1},{4,6},{5,7},{6,4},{7,5},{8,10},{9,11},{10,... | collective-permute-start | bytes 98312 | tf_op jit(solution)/shard_map/ppermute | solution.py:469
  45.6 0.8 %collective-permute-start.14 = (bf16[64,256]{1,0:T(8,128)(2,1)S(1)}, bf16[64,256]{1,0:T(8,128)(2,1)S(1)}, u32[]{:S(2)}, u32[]{:S(2)}) collective-permute-start(bf16[64,256]{1,0:T(8,128)(2,1)S(1)} %get-tuple-element.43), channel_id=1, source_target_pairs={{0,1},{1,0},{2,3},{3,2},{4,5},{5,4},{6,7},{7,6},{8,9},{9,8},{10,11... | collective-permute-start | bytes 98312 | tf_op jit(solution)/shard_map/ppermute | solution.py:465
  46.4 1.9 %prop.1 = bf16[2,1024,256]{2,1,0:T(8,128)(2,1)S(1)} custom-call(s32[2,8]{1,0:T(2,128)S(1)} %bitcast.19, bf16[2,1024,1024]{2,1,0:T(8,128)(2,1)S(1)} %bitcast.13, bf16[1024,256]{1,0:T(8,128)(2,1)S(1)} %bitcast.17, bf16[64,256]{1,0:T(8,128)(2,1)S(1)} %get-tuple-element.40._tie.own), custom_call_target="tpu_custom_call" | custom-call | flops 1724999936 | tf_op jit(solution)/shard_map/prop/pallas_call | solution.py:218
  48.3 0.0 collective-permute-done.12.far
  48.3 0.5 %collective-permute-done.13.across = bf16[64,256]{1,0:T(8,128)(2,1)S(1)} collective-permute-done((bf16[64,256]{1,0:T(8,128)(2,1)S(1)}, bf16[64,256]{1,0:T(8,128)(2,1)S(1)}, u32[]{:S(2)}, u32[]{:S(2)}) %collective-permute-start.13) | collective-permute-done | bytes 32800 | tf_op jit(solution)/shard_map/ppermute | solution.py:469
  48.9 0.0 collective-permute-done.14.near
  48.9 1.2 %waves.1 = bf16[2,1024,128]{2,1,0:T(8,128)(2,1)} custom-call(bf16[64,256]{1,0:T(8,128)(2,1)S(1)} %get-tuple-element.40._tie.own, bf16[64,256]{1,0:T(8,128)(2,1)S(1)} %collective-permute-done.12.far, bf16[64,256]{1,0:T(8,128)(2,1)S(1)} %collective-permute-done.13.across, bf16[64,256]{1,0:T(8,128)(2,1)S(1)} %collective-permute-done.14.near, ...), custom_call_target="tpu_custom_call" | custom-call | flops 1495000064 | tf_op jit(solution)/shard_map/waves/pallas_call | solution.py:448
  (5 shorter events, 0.0 us)
Async XLA Ops:
  0.0 12.1 %copy-start.3 = (bf16[1,1024,256]{2,1,0:T(8,128)(2,1)S(1)}, bf16[1,1024,256]{2,1,0:T(8,128)(2,1)}, u32[]{:S(2)}) copy-start(bf16[1,1024,256]{2,1,0:T(8,128)(2,1)} %param.8) | copy-start | bytes 1572868
  0.0 12.1 %copy-start.4 = (s32[1,8,2]{1,2,0:T(2,128)S(1)}, s32[1,8,2]{1,2,0:T(2,128)}, u32[]{:S(2)}) copy-start(s32[1,8,2]{1,2,0:T(2,128)} %param.9) | copy-start | bytes 196
  4.4 22.9 %copy-start.2 = (bf16[1,2,1024,128]{3,2,1,0:T(8,128)(2,1)S(1)}, bf16[1,2,1024,128]{3,2,1,0:T(8,128)(2,1)}, u32[]{:S(2)}) copy-start(bf16[1,2,1024,128]{3,2,1,0:T(8,128)(2,1)} %param.7) | copy-start | bytes 1572868
  4.4 22.9 %all-to-all-start = ((bf16[16,136,128]{2,1,0:T(8,128)(2,1)}), bf16[16,136,128]{2,1,0:T(8,128)(2,1)S(1)}, u32[]{:S(2)}, u32[]{:S(2)}) async-start(bf16[16,136,128]{2,1,0:T(8,128)(2,1)} %pairs.1), calls=%async_computation | async-start | bytes 1114112 | tf_op jit(solution)/shard_map/all_to_all | solution.py:519
  12.1 2.2 %copy-start = (bf16[1,2,1024,1024]{3,2,1,0:T(8,128)(2,1)S(1)}, bf16[1,2,1024,1024]{3,2,1,0:T(8,128)(2,1)}, u32[]{:S(2)}) copy-start(bf16[1,2,1024,1024]{3,2,1,0:T(8,128)(2,1)} %param.6) | copy-start | bytes 12582916
  15.4 11.9 %collective-permute-start.3 = (f32[256,256]{1,0:T(8,128)S(1)}, f32[256,256]{1,0:T(8,128)S(1)}, u32[]{:S(2)}, u32[]{:S(2)}) collective-permute-start(f32[256,256]{1,0:T(8,128)S(1)} %get-tuple-element.31), channel_id=1, source_target_pairs={{0,2},{1,3},{2,0},{3,1},{4,6},{5,7},{6,4},{7,5},{8,10},{9,11},{10,... | collective-permute-start | bytes 786440 | tf_op jit(solution)/shard_map/ppermute | solution.py:469
  17.4 13.5 %collective-permute-start.5 = (f32[256,256]{1,0:T(8,128)S(1)}, f32[256,256]{1,0:T(8,128)S(1)}, u32[]{:S(2)}, u32[]{:S(2)}) collective-permute-start(f32[256,256]{1,0:T(8,128)S(1)} %get-tuple-element.30.own), channel_id=1, source_target_pairs={{0,1},{1,0},{2,3},{3,2},{4,5},{5,4},{6,7},{7,6},{8,9},{9,8},{10,11... | collective-permute-start | bytes 786440 | tf_op jit(solution)/shard_map/ppermute | solution.py:465
  27.3 3.6 %collective-permute-start.4 = (f32[256,256]{1,0:T(8,128)S(1)}, f32[256,256]{1,0:T(8,128)S(1)}, u32[]{:S(2)}, u32[]{:S(2)}) collective-permute-start(f32[256,256]{1,0:T(8,128)S(1)} %after_exchange.1.across), channel_id=1, source_target_pairs={{0,1},{1,0},{2,3},{3,2},{4,5},{5,4},{6,7},{7,6},{8,9},{9,8},{10,11... | collective-permute-start | bytes 786440 | tf_op jit(solution)/shard_map/ppermute | solution.py:465
  27.3 5.1 %copy-start.1 = (bf16[1,2,1024,1024]{3,2,1,0:T(8,128)(2,1)S(1)}, bf16[1,2,1024,1024]{3,2,1,0:T(8,128)(2,1)}, u32[]{:S(2)}) copy-start(bf16[1,2,1024,1024]{3,2,1,0:T(8,128)(2,1)} %param.6) | copy-start | bytes 12582916
  28.8 5.5 %collective-permute-start = (bf16[64,256]{1,0:T(8,128)(2,1)S(1)}, bf16[64,256]{1,0:T(8,128)(2,1)S(1)}, u32[]{:S(2)}, u32[]{:S(2)}) collective-permute-start(bf16[64,256]{1,0:T(8,128)(2,1)S(1)} %get-tuple-element.27), channel_id=1, source_target_pairs={{0,3},{1,2},{2,1},{3,0},{4,7},{5,6},{6,5},{7,4},{8,11},{9,10},{10,... | collective-permute-start | bytes 98312 | tf_op jit(solution)/shard_map/ppermute | solution.py:473
  30.6 3.9 %collective-permute-start.1 = (bf16[64,256]{1,0:T(8,128)(2,1)S(1)}, bf16[64,256]{1,0:T(8,128)(2,1)S(1)}, u32[]{:S(2)}, u32[]{:S(2)}) collective-permute-start(bf16[64,256]{1,0:T(8,128)(2,1)S(1)} %get-tuple-element.28), channel_id=1, source_target_pairs={{0,2},{1,3},{2,0},{3,1},{4,6},{5,7},{6,4},{7,5},{8,10},{9,11},{10,... | collective-permute-start | bytes 98312 | tf_op jit(solution)/shard_map/ppermute | solution.py:469
  30.9 3.6 %collective-permute-start.2 = (bf16[64,256]{1,0:T(8,128)(2,1)S(1)}, bf16[64,256]{1,0:T(8,128)(2,1)S(1)}, u32[]{:S(2)}, u32[]{:S(2)}) collective-permute-start(bf16[64,256]{1,0:T(8,128)(2,1)S(1)} %get-tuple-element.29), channel_id=1, source_target_pairs={{0,1},{1,0},{2,3},{3,2},{4,5},{5,4},{6,7},{7,6},{8,9},{9,8},{10,11... | collective-permute-start | bytes 98312 | tf_op jit(solution)/shard_map/ppermute | solution.py:465
  31.8 11.1 %collective-permute-start.10 = (bf16[256,256]{1,0:T(8,128)(2,1)S(1)}, bf16[256,256]{1,0:T(8,128)(2,1)S(1)}, u32[]{:S(2)}, u32[]{:S(2)}) collective-permute-start(bf16[256,256]{1,0:T(8,128)(2,1)S(1)} %get-tuple-element.36), channel_id=1, source_target_pairs={{4,8},{8,12},{5,13},{6,10},{10,14},{7,15},{20,24},{24,28},{21,29},... | collective-permute-start | bytes 393224 | tf_op jit(solution)/shard_map/ppermute | solution.py:491
  35.1 8.6 %collective-permute-start.6 = (bf16[64,256]{1,0:T(8,128)(2,1)S(1)}, bf16[64,256]{1,0:T(8,128)(2,1)S(1)}, u32[]{:S(2)}, u32[]{:S(2)}) collective-permute-start(bf16[64,256]{1,0:T(8,128)(2,1)S(1)} %get-tuple-element.35), channel_id=1, source_target_pairs={{0,12},{1,13},{2,14},{3,15},{16,28},{17,29},{18,30},{19,31}} | collective-permute-start | bytes 98312 | tf_op jit(solution)/shard_map/ppermute | solution.py:497
  39.6 4.1 %collective-permute-start.7 = (bf16[64,256]{1,0:T(8,128)(2,1)S(1)}, bf16[64,256]{1,0:T(8,128)(2,1)S(1)}, u32[]{:S(2)}, u32[]{:S(2)}) collective-permute-start(bf16[64,256]{1,0:T(8,128)(2,1)S(1)} %get-tuple-element.35), channel_id=1, source_target_pairs={{0,4},{1,5},{2,6},{3,7},{16,20},{17,21},{18,22},{19,23}} | collective-permute-start | bytes 98312 | tf_op jit(solution)/shard_map/ppermute | solution.py:497
  40.9 2.9 %collective-permute-start.8 = (bf16[64,256]{1,0:T(8,128)(2,1)S(1)}, bf16[64,256]{1,0:T(8,128)(2,1)S(1)}, u32[]{:S(2)}, u32[]{:S(2)}) collective-permute-start(bf16[64,256]{1,0:T(8,128)(2,1)S(1)} %get-tuple-element.35), channel_id=1, source_target_pairs={{0,8},{1,9},{2,10},{3,11},{4,12},{5,13},{6,14},{7,15},{16,24},{17,... | collective-permute-start | bytes 98312 | tf_op jit(solution)/shard_map/ppermute | solution.py:497
  42.2 1.6 %collective-permute-start.9 = (bf16[64,256]{1,0:T(8,128)(2,1)S(1)}, bf16[64,256]{1,0:T(8,128)(2,1)S(1)}, u32[]{:S(2)}, u32[]{:S(2)}) collective-permute-start(bf16[64,256]{1,0:T(8,128)(2,1)S(1)} %get-tuple-element.35), channel_id=1, source_target_pairs={{4,8},{5,9},{6,10},{7,11},{8,12},{9,13},{10,14},{11,15},{20,24},{2... | collective-permute-start | bytes 98312 | tf_op jit(solution)/shard_map/ppermute | solution.py:497
  42.9 0.9 %collective-permute-start.11 = (bf16[256,256]{1,0:T(8,128)(2,1)S(1)}, bf16[256,256]{1,0:T(8,128)(2,1)S(1)}, u32[]{:S(2)}, u32[]{:S(2)}) collective-permute-start(bf16[256,256]{1,0:T(8,128)(2,1)S(1)} %collective-permute-done.10.got), channel_id=1, source_target_pairs={{8,9},{9,8},{10,11},{11,10},{12,13},{13,12},{14,15},{15,14},{24,25... | collective-permute-start | bytes 393224 | tf_op jit(solution)/shard_map/ppermute | solution.py:492
  44.5 3.8 %collective-permute-start.12 = (bf16[64,256]{1,0:T(8,128)(2,1)S(1)}, bf16[64,256]{1,0:T(8,128)(2,1)S(1)}, u32[]{:S(2)}, u32[]{:S(2)}) collective-permute-start(bf16[64,256]{1,0:T(8,128)(2,1)S(1)} %get-tuple-element.41), channel_id=1, source_target_pairs={{0,3},{1,2},{2,1},{3,0},{4,7},{5,6},{6,5},{7,4},{8,11},{9,10},{10,... | collective-permute-start | bytes 98312 | tf_op jit(solution)/shard_map/ppermute | solution.py:473
  45.0 3.9 %collective-permute-start.13 = (bf16[64,256]{1,0:T(8,128)(2,1)S(1)}, bf16[64,256]{1,0:T(8,128)(2,1)S(1)}, u32[]{:S(2)}, u32[]{:S(2)}) collective-permute-start(bf16[64,256]{1,0:T(8,128)(2,1)S(1)} %get-tuple-element.42), channel_id=1, source_target_pairs={{0,2},{1,3},{2,0},{3,1},{4,6},{5,7},{6,4},{7,5},{8,10},{9,11},{10,... | collective-permute-start | bytes 98312 | tf_op jit(solution)/shard_map/ppermute | solution.py:469
  45.6 3.3 %collective-permute-start.14 = (bf16[64,256]{1,0:T(8,128)(2,1)S(1)}, bf16[64,256]{1,0:T(8,128)(2,1)S(1)}, u32[]{:S(2)}, u32[]{:S(2)}) collective-permute-start(bf16[64,256]{1,0:T(8,128)(2,1)S(1)} %get-tuple-element.43), channel_id=1, source_target_pairs={{0,1},{1,0},{2,3},{3,2},{4,5},{5,4},{6,7},{7,6},{8,9},{9,8},{10,11... | collective-permute-start | bytes 98312 | tf_op jit(solution)/shard_map/ppermute | solution.py:465

commit v24 on v23

--- a/solution.py
+++ b/solution.py
@@ -179,31 +179,61 @@
     )(owner, blocks, green, inject)
 
 
-def maps_kernel(pattern, green, coupling, own, other, face_rows, couple, maps):
+def maps_kernel(pattern_in, green, coupling_in, own, other, pattern, coupling, rows, maps, sem, side):
     energies, orbitals, _ = green.shape
     face = coupling.shape[1]
-    couple[...] = coupling[...]
-    mask_tiles(pattern, couple)
-    for e in range(energies):
-        rows = green[e, orbitals - face :, :]
-        face_rows[e] = rows
-        maps[e] = dot(rows, couple[...])
+    tiles = pltpu.make_async_copy(pattern_in, pattern, side.at[0])
+    whole = pltpu.make_async_copy(coupling_in, coupling, side.at[1])
+    tiles.start()
+    whole.start()
+    moves = [
+        pltpu.make_async_copy(green.at[e, pl.ds(orbitals - face, face)], rows.at[e], sem.at[e]) for e in range(energies)
+    ]
+    for move in moves:
+        move.start()
+    tiles.wait()
+    whole.wait()
+    mask_tiles(pattern, coupling)
+    for e, move in enumerate(moves):
+        move.wait()
+        maps[e] = dot(rows[e], coupling[...])
     mine = place() // CORES
     own[...] = maps[mine]
     other[...] = maps[1 - mine]
 
 
 def face_maps(pattern, green, coupling):
-    orbitals, face = coupling.shape
+    energies, orbitals, _ = green.shape
+    face = coupling.shape[1]
     square = shape(face, face, dtype=F32)
     return call(
         maps_kernel,
         "face_maps",
-        [IN_SMEM, IN_VMEM, IN_VMEM],
-        [square, square, shape(green.shape[0], face, orbitals)],
-        [pltpu.VMEM(coupling.shape, BF16), pltpu.VMEM((green.shape[0], face, face), F32)],
-        1.2,
+        [IN_HBM] * 3,
+        [square, square],
+        [
+            pltpu.SMEM(pattern.shape, jnp.int32),
+            pltpu.VMEM(coupling.shape, BF16),
+            pltpu.VMEM((energies, face, orbitals), BF16),
+            pltpu.VMEM((energies, face, face), F32),
+            pltpu.SemaphoreType.DMA((energies,)),
+            pltpu.SemaphoreType.DMA((2,)),
+        ],
+        2.0,
+        VMEM_WHOLE,
     )(pattern, green, coupling)
+
+
+def rows_kernel(green, _map, out):
+    for e in range(green.shape[0]):
+        out[e] = green[e, green.shape[1] - out.shape[1] :, :]
+
+
+def face_rows_of(green, own_map):
+    energies, _, orbitals = green.shape
+    return call(
+        rows_kernel, "face_rows", [IN_VMEM, IN_PLACE], shape(energies, own_map.shape[0], orbitals), [], 0.4
+    )(green, own_map)
 
 
 def prop_kernel(pattern, green, coupling, _tie, out, couple):
@@ -518,7 +548,8 @@
     outgoing = outgoing_pairs(owner[:, 0], pair_blocks.T, green, inject, sections)
     received = lax.all_to_all(outgoing, "sec", split_axis=0, concat_axis=0, tiled=True)
 
-    own_map, other_map, face_rows = face_maps(tiles, green, coupling)
+    own_map, other_map = face_maps(tiles, green, coupling)
+    face_rows = face_rows_of(green, own_map)
     across = to_across(other_map, sections)
     near = to_near(own_map, sections)
 

time: 50.4 us -> 53.5 us (1.062)
  Pallas kernels: 14.1 us -> 16 us
  local copies, waits for them, and re-layouts: 2.2 us -> 3.16 us
    pallas_call x1 -> x2, Pallas kernels: 1.11 us -> 3.09 us  [the longest x1 3.02 us: face_maps(): call(maps_kernel, 'face_maps', [IN_HBM] * 3, [square, square], [pltpu.SME...]
    unnamed x10 -> x12, local copies, waits for them, and re-layouts: 2.2 us -> 3.16 us
  transfers between devices with their start and end apart: 16 -> 16, of which waited for: 4 -> 3; matrix products, arithmetic and copies ran while one was open for 0% -> 0% of each run, Pallas kernels for 15% -> 18%
where the time goes in v24:
time: 53.5 us; the launch traced here: 53 us
  starting transfers between devices  22.7 us (42%)
  Pallas kernels  16 us (30%)
  waiting for transfers between devices  11 us (21%)
  local copies, waits for them, and re-layouts  3.16 us (6%)
    ppermute x3, waiting for transfers between devices, to_across(): lax.ppermute(item, 'sec', [(s, s // GROUP * GROUP + (s % GROUP + CORES) %...  10.9 us
    ppermute x4, starting transfers between devices, between(): return lax.ppermute(item, 'sec', pairs)  7.77 us
    all_to_all x1, starting transfers between devices, per_device(): lax.all_to_all(outgoing, 'sec', split_axis=0, concat_axis=0, tiled=True)  7.45 us
    pallas_call x1, Pallas kernels, outgoing_pairs(): call(pairs_kernel, 'pairs', [IN_HBM] * 4, shape(sections, CAP * energies...  4.32 us
    unnamed x12, local copies, waits for them, and re-layouts  3.16 us
    pallas_call x1, Pallas kernels, face_maps(): call(maps_kernel, 'face_maps', [IN_HBM] * 3, [square, square], [pltpu.SME...  3.02 us
    ppermute x3, starting transfers between devices, to_across(): lax.ppermute(item, 'sec', [(s, s // GROUP * GROUP + (s % GROUP + CORES) %...  2.95 us
    ppermute x2, starting transfers between devices, to_far(): lax.ppermute(item, 'sec', [(s, s // GROUP * GROUP + (s % GROUP + CORES) %...  2.36 us
  transfers between devices with their start and end apart: 16, of which 3 were waited for; matrix products, arithmetic and copies ran while one was open for 0% of the time, Pallas kernels for 18%

profile of v24, /device:TPU:0, one launch (start us, length us, event | category | flops | bytes accessed | tf_op | source)
XLA Modules:
  0.0 53.0 jit_solution(7681302490381828441)
XLA Ops:
  0.0 4.3 %pairs.1 = bf16[16,136,128]{2,1,0:T(8,128)(2,1)} custom-call(s32[16]{0:T(128)} %bitcast.22, s32[2,16]{1,0:T(2,128)} %bitcast.21, bf16[2,1024,1024]{2,1,0:T(8,128)(2,1)} %bitcast.9, bf16[2,1024,128]{2,1,0:T(8,128)(2,1)} %bitcast.15), custom_call_target="tpu_custom_call" | custom-call | flops 4600000000 | tf_op jit(solution)/shard_map/pairs/pallas_call | solution.py:161
  4.3 7.5 %all-to-all-start = ((bf16[16,136,128]{2,1,0:T(8,128)(2,1)}), bf16[16,136,128]{2,1,0:T(8,128)(2,1)S(1)}, u32[]{:S(2)}, u32[]{:S(2)}) async-start(bf16[16,136,128]{2,1,0:T(8,128)(2,1)} %pairs.1), calls=%async_computation | async-start | bytes 1114112 | tf_op jit(solution)/shard_map/all_to_all | solution.py:549
  11.8 3.0 %face_maps.1 = (f32[256,256]{1,0:T(8,128)}, f32[256,256]{1,0:T(8,128)}) custom-call(s32[2,8]{1,0:T(2,128)} %bitcast.19, bf16[2,1024,1024]{2,1,0:T(8,128)(2,1)} %bitcast.10, bf16[1024,256]{1,0:T(8,128)(2,1)} %bitcast.17), custom_call_target="tpu_custom_call" | custom-call | flops 2300000000 | tf_op jit(solution)/shard_map/face_maps/pallas_call | solution.py:209
  14.8 0.0 copy-start.3
  14.8 2.0 %collective-permute-start.3 = (f32[256,256]{1,0:T(8,128)}, f32[256,256]{1,0:T(8,128)S(1)}, u32[]{:S(2)}, u32[]{:S(2)}) collective-permute-start(f32[256,256]{1,0:T(8,128)} %get-tuple-element.29), channel_id=1, source_target_pairs={{0,2},{1,3},{2,0},{3,1},{4,6},{5,7},{6,4},{7,5},{8,10},{9,11},{10,... | collective-permute-start | bytes 786440 | tf_op jit(solution)/shard_map/ppermute | solution.py:499
  16.8 0.0 collective-permute-start.5
  16.8 10.1 %collective-permute-done.3._map = f32[256,256]{1,0:T(8,128)S(1)} collective-permute-done((f32[256,256]{1,0:T(8,128)}, f32[256,256]{1,0:T(8,128)S(1)}, u32[]{:S(2)}, u32[]{:S(2)}) %collective-permute-start.3) | collective-permute-done | bytes 262176 | tf_op jit(solution)/shard_map/ppermute | solution.py:499
  26.9 0.0 all-to-all-done.received._packets
  26.9 0.0 collective-permute-start.4
  27.0 2.2 %copy-done = bf16[1,2,1024,1024]{3,2,1,0:T(8,128)(2,1)S(1)} copy-done((bf16[1,2,1024,1024]{3,2,1,0:T(8,128)(2,1)S(1)}, bf16[1,2,1024,1024]{3,2,1,0:T(8,128)(2,1)}, u32[]{:S(2)}) %copy-start) | copy-done | bytes 4194328
  29.1 0.9 %copy-done.2 = f32[256,256]{1,0:T(8,128)S(1)} copy-done((f32[256,256]{1,0:T(8,128)S(1)}, f32[256,256]{1,0:T(8,128)}, u32[]{:S(2)}) %copy-start.2) | copy-done | bytes 262168
  30.1 0.1 face_rows.1
  30.2 0.0 copy-start.1
  30.2 1.4 %source_and_face.1 = (bf16[2,1024,128]{2,1,0:T(8,128)(2,1)S(1)}, bf16[64,256]{1,0:T(8,128)(2,1)S(1)}, bf16[64,256]{1,0:T(8,128)(2,1)S(1)}, bf16[64,256]{1,0:T(8,128)(2,1)S(1)}, bf16[64,256]{1,0:T(8,128)(2,1)S(1)}) custom-call(bf16[16,136,128]{2,1,0:T(8,128)(2,1)S(1)} %all-to-all-done.received._packets, bf16[2,1024,128]{2,1,0:T(8,128)(2,1)S(1)} %bitcast.16, ...), custom_call_target="tpu_custom_call" | custom-call | flops 1610000000 | tf_op jit(solution)/shard_map/source_and_face/pallas_call | solution.py:341
  31.6 1.9 %collective-permute-start = (bf16[64,256]{1,0:T(8,128)(2,1)S(1)}, bf16[64,256]{1,0:T(8,128)(2,1)S(1)}, u32[]{:S(2)}, u32[]{:S(2)}) collective-permute-start(bf16[64,256]{1,0:T(8,128)(2,1)S(1)} %get-tuple-element.26), channel_id=1, source_target_pairs={{0,3},{1,2},{2,1},{3,0},{4,7},{5,6},{6,5},{7,4},{8,11},{9,10},{10,... | collective-permute-start | bytes 98312 | tf_op jit(solution)/shard_map/ppermute | solution.py:503
  33.5 0.3 collective-permute-start.1
  33.8 0.0 collective-permute-start.2
  33.8 0.0 collective-permute-done.5.near
  33.8 0.0 collective-permute-done.4.far
  33.8 0.8 %chain_maps.1 = (bf16[256,256]{1,0:T(8,128)(2,1)S(1)}, bf16[2,4,256,256]{3,2,1,0:T(8,128)(2,1)S(1)}) custom-call(f32[256,256]{1,0:T(8,128)S(1)} %copy-done.2, f32[256,256]{1,0:T(8,128)S(1)} %collective-permute-done.4.far, f32[256,256]{1,0:T(8,128)S(1)} %after_exchange.1.across, f32[256,256]{1,0:T(8,128)S(1)} %collective-permute-done.5.near), custom_call_target="tpu_custom_call" | custom-call | flops 1035000000 | tf_op jit(solution)/shard_map/chain_maps/pallas_call | solution.py:274
  34.6 0.7 %collective-permute-start.10 = (bf16[256,256]{1,0:T(8,128)(2,1)S(1)}, bf16[256,256]{1,0:T(8,128)(2,1)S(1)}, u32[]{:S(2)}, u32[]{:S(2)}) collective-permute-start(bf16[256,256]{1,0:T(8,128)(2,1)S(1)} %get-tuple-element.34), channel_id=1, source_target_pairs={{4,8},{8,12},{5,13},{6,10},{10,14},{7,15},{20,24},{24,28},{21,29},... | collective-permute-start | bytes 393224 | tf_op jit(solution)/shard_map/ppermute | solution.py:521
  35.3 1.8 %image_and_maps.2 = (f32[2,1024,128]{2,1,0:T(8,128)S(1)}, bf16[2,2,256,256]{3,2,1,0:T(8,128)(2,1)S(1)}) custom-call(bf16[2,1024,1024]{2,1,0:T(8,128)(2,1)S(1)} %bitcast.12, bf16[2,1024,128]{2,1,0:T(8,128)(2,1)S(1)} %get-tuple-element.31.refs_1_, bf16[2,4,256,256]{3,2,1,0:T(8,128)(2,1)S(1)} %get-tuple-element.30.refs_2_.parts), custom_call_target="tpu_custom_call" | custom-call | flops 2300000000 | tf_op jit(solution)/shard_map/image_and_maps/pallas_call | solution.py:407
  37.1 0.0 collective-permute-done.far
  37.1 0.2 collective-permute-done.1.across
  37.4 0.0 collective-permute-done.2.near
  37.4 0.6 %plane_total.1 = (bf16[64,256]{1,0:T(8,128)(2,1)S(1)}, f32[3,64,256]{2,1,0:T(8,128)S(1)}) custom-call(bf16[64,256]{1,0:T(8,128)(2,1)S(1)} %get-tuple-element.25.own, bf16[64,256]{1,0:T(8,128)(2,1)S(1)} %collective-permute-done.far, bf16[64,256]{1,0:T(8,128)(2,1)S(1)} %collective-permute-done.1.across, bf16[64,256]{1,0:T(8,128)(2,1)S(1)} %collective-permute-done.2.near, ...), custom_call_target="tpu_custom_call" | custom-call | flops 3449999872 | tf_op jit(solution)/shard_map/plane_total/pallas_call | solution.py:373
  38.0 4.5 %collective-permute-start.6 = (bf16[64,256]{1,0:T(8,128)(2,1)S(1)}, bf16[64,256]{1,0:T(8,128)(2,1)S(1)}, u32[]{:S(2)}, u32[]{:S(2)}) collective-permute-start(bf16[64,256]{1,0:T(8,128)(2,1)S(1)} %get-tuple-element.33), channel_id=1, source_target_pairs={{0,12},{1,13},{2,14},{3,15},{16,28},{17,29},{18,30},{19,31}} | collective-permute-start | bytes 98312 | tf_op jit(solution)/shard_map/ppermute | solution.py:527
  42.5 1.3 %collective-permute-start.7 = (bf16[64,256]{1,0:T(8,128)(2,1)S(1)}, bf16[64,256]{1,0:T(8,128)(2,1)S(1)}, u32[]{:S(2)}, u32[]{:S(2)}) collective-permute-start(bf16[64,256]{1,0:T(8,128)(2,1)S(1)} %get-tuple-element.33), channel_id=1, source_target_pairs={{0,4},{1,5},{2,6},{3,7},{16,20},{17,21},{18,22},{19,23}} | collective-permute-start | bytes 98312 | tf_op jit(solution)/shard_map/ppermute | solution.py:527
  43.8 1.3 %collective-permute-start.8 = (bf16[64,256]{1,0:T(8,128)(2,1)S(1)}, bf16[64,256]{1,0:T(8,128)(2,1)S(1)}, u32[]{:S(2)}, u32[]{:S(2)}) collective-permute-start(bf16[64,256]{1,0:T(8,128)(2,1)S(1)} %get-tuple-element.33), channel_id=1, source_target_pairs={{0,8},{1,9},{2,10},{3,11},{4,12},{5,13},{6,14},{7,15},{16,24},{17,... | collective-permute-start | bytes 98312 | tf_op jit(solution)/shard_map/ppermute | solution.py:527
  45.1 0.7 %collective-permute-start.9 = (bf16[64,256]{1,0:T(8,128)(2,1)S(1)}, bf16[64,256]{1,0:T(8,128)(2,1)S(1)}, u32[]{:S(2)}, u32[]{:S(2)}) collective-permute-start(bf16[64,256]{1,0:T(8,128)(2,1)S(1)} %get-tuple-element.33), channel_id=1, source_target_pairs={{4,8},{5,9},{6,10},{7,11},{8,12},{9,13},{10,14},{11,15},{20,24},{2... | collective-permute-start | bytes 98312 | tf_op jit(solution)/shard_map/ppermute | solution.py:527
  45.8 0.0 collective-permute-done.10.got
  45.8 0.7 %collective-permute-start.11 = (bf16[256,256]{1,0:T(8,128)(2,1)S(1)}, bf16[256,256]{1,0:T(8,128)(2,1)S(1)}, u32[]{:S(2)}, u32[]{:S(2)}) collective-permute-start(bf16[256,256]{1,0:T(8,128)(2,1)S(1)} %collective-permute-done.10.got), channel_id=1, source_target_pairs={{8,9},{9,8},{10,11},{11,10},{12,13},{13,12},{14,15},{15,14},{24,25... | collective-permute-start | bytes 393224 | tf_op jit(solution)/shard_map/ppermute | solution.py:522
  46.5 0.1 image_and_maps.3
  46.6 0.0 copy-start.4
  46.6 0.0 copy-start.5
  46.6 0.0 collective-permute-done.6.third
  46.6 0.0 collective-permute-done.7.near_one
  46.7 0.0 collective-permute-done.8.second
  46.7 0.0 collective-permute-done.11.other
  46.7 0.7 %entering.1 = (bf16[64,256]{1,0:T(8,128)(2,1)S(1)}, bf16[64,256]{1,0:T(8,128)(2,1)S(1)}, bf16[64,256]{1,0:T(8,128)(2,1)S(1)}, bf16[64,256]{1,0:T(8,128)(2,1)S(1)}) custom-call(bf16[64,256]{1,0:T(8,128)(2,1)S(1)} %collective-permute-done.6.third, bf16[64,256]{1,0:T(8,128)(2,1)S(1)} %collective-permute-done.7.near_one, ...), custom_call_target="tpu_custom_call" | custom-call | flops 1610000000 | tf_op jit(solution)/shard_map/entering/pallas_call | solution.py:447
  47.4 0.5 collective-permute-start.12
  47.9 0.6 %collective-permute-start.13 = (bf16[64,256]{1,0:T(8,128)(2,1)S(1)}, bf16[64,256]{1,0:T(8,128)(2,1)S(1)}, u32[]{:S(2)}, u32[]{:S(2)}) collective-permute-start(bf16[64,256]{1,0:T(8,128)(2,1)S(1)} %get-tuple-element.40), channel_id=1, source_target_pairs={{0,2},{1,3},{2,0},{3,1},{4,6},{5,7},{6,4},{7,5},{8,10},{9,11},{10,... | collective-permute-start | bytes 98312 | tf_op jit(solution)/shard_map/ppermute | solution.py:499
  48.6 0.8 %collective-permute-start.14 = (bf16[64,256]{1,0:T(8,128)(2,1)S(1)}, bf16[64,256]{1,0:T(8,128)(2,1)S(1)}, u32[]{:S(2)}, u32[]{:S(2)}) collective-permute-start(bf16[64,256]{1,0:T(8,128)(2,1)S(1)} %get-tuple-element.41), channel_id=1, source_target_pairs={{0,1},{1,0},{2,3},{3,2},{4,5},{5,4},{6,7},{7,6},{8,9},{9,8},{10,11... | collective-permute-start | bytes 98312 | tf_op jit(solution)/shard_map/ppermute | solution.py:495
  49.4 1.9 %prop.1 = bf16[2,1024,256]{2,1,0:T(8,128)(2,1)S(1)} custom-call(s32[2,8]{1,0:T(2,128)S(1)} %bitcast.20, bf16[2,1024,1024]{2,1,0:T(8,128)(2,1)S(1)} %bitcast.14, bf16[1024,256]{1,0:T(8,128)(2,1)S(1)} %bitcast.18, bf16[64,256]{1,0:T(8,128)(2,1)S(1)} %get-tuple-element.38._tie.own), custom_call_target="tpu_custom_call" | custom-call | flops 1724999936 | tf_op jit(solution)/shard_map/prop/pallas_call | solution.py:248
  51.3 0.0 collective-permute-done.12.far
  51.3 0.5 %collective-permute-done.13.across = bf16[64,256]{1,0:T(8,128)(2,1)S(1)} collective-permute-done((bf16[64,256]{1,0:T(8,128)(2,1)S(1)}, bf16[64,256]{1,0:T(8,128)(2,1)S(1)}, u32[]{:S(2)}, u32[]{:S(2)}) %collective-permute-start.13) | collective-permute-done | bytes 32800 | tf_op jit(solution)/shard_map/ppermute | solution.py:499
  51.8 0.0 collective-permute-done.14.near
  51.8 1.2 %waves.1 = bf16[2,1024,128]{2,1,0:T(8,128)(2,1)} custom-call(bf16[64,256]{1,0:T(8,128)(2,1)S(1)} %get-tuple-element.38._tie.own, bf16[64,256]{1,0:T(8,128)(2,1)S(1)} %collective-permute-done.12.far, bf16[64,256]{1,0:T(8,128)(2,1)S(1)} %collective-permute-done.13.across, bf16[64,256]{1,0:T(8,128)(2,1)S(1)} %collective-permute-done.14.near, ...), custom_call_target="tpu_custom_call" | custom-call | flops 1495000064 | tf_op jit(solution)/shard_map/waves/pallas_call | solution.py:478
  (8 shorter events, 0.0 us)
Async XLA Ops:
  4.3 22.6 %all-to-all-start = ((bf16[16,136,128]{2,1,0:T(8,128)(2,1)}), bf16[16,136,128]{2,1,0:T(8,128)(2,1)S(1)}, u32[]{:S(2)}, u32[]{:S(2)}) async-start(bf16[16,136,128]{2,1,0:T(8,128)(2,1)} %pairs.1), calls=%async_computation | async-start | bytes 1114112 | tf_op jit(solution)/shard_map/all_to_all | solution.py:549
  14.8 15.4 %copy-start.3 = (bf16[1,2,1024,128]{3,2,1,0:T(8,128)(2,1)S(1)}, bf16[1,2,1024,128]{3,2,1,0:T(8,128)(2,1)}, u32[]{:S(2)}) copy-start(bf16[1,2,1024,128]{3,2,1,0:T(8,128)(2,1)} %param.7) | copy-start | bytes 1572868
  14.8 12.1 %collective-permute-start.3 = (f32[256,256]{1,0:T(8,128)}, f32[256,256]{1,0:T(8,128)S(1)}, u32[]{:S(2)}, u32[]{:S(2)}) collective-permute-start(f32[256,256]{1,0:T(8,128)} %get-tuple-element.29), channel_id=1, source_target_pairs={{0,2},{1,3},{2,0},{3,1},{4,6},{5,7},{6,4},{7,5},{8,10},{9,11},{10,... | collective-permute-start | bytes 786440 | tf_op jit(solution)/shard_map/ppermute | solution.py:499
  16.8 17.0 %collective-permute-start.5 = (f32[256,256]{1,0:T(8,128)}, f32[256,256]{1,0:T(8,128)S(1)}, u32[]{:S(2)}, u32[]{:S(2)}) collective-permute-start(f32[256,256]{1,0:T(8,128)} %get-tuple-element.24._map.own), channel_id=1, source_target_pairs={{0,1},{1,0},{2,3},{3,2},{4,5},{5,4},{6,7},{7,6},{8,9},{9,8},{10,11... | collective-permute-start | bytes 786440 | tf_op jit(solution)/shard_map/ppermute | solution.py:495
  26.9 6.9 %collective-permute-start.4 = (f32[256,256]{1,0:T(8,128)S(1)}, f32[256,256]{1,0:T(8,128)S(1)}, u32[]{:S(2)}, u32[]{:S(2)}) collective-permute-start(f32[256,256]{1,0:T(8,128)S(1)} %after_exchange.1.across), channel_id=1, source_target_pairs={{0,1},{1,0},{2,3},{3,2},{4,5},{5,4},{6,7},{7,6},{8,9},{9,8},{10,11... | collective-permute-start | bytes 786440 | tf_op jit(solution)/shard_map/ppermute | solution.py:495
  27.0 2.2 %copy-start = (bf16[1,2,1024,1024]{3,2,1,0:T(8,128)(2,1)S(1)}, bf16[1,2,1024,1024]{3,2,1,0:T(8,128)(2,1)}, u32[]{:S(2)}) copy-start(bf16[1,2,1024,1024]{3,2,1,0:T(8,128)(2,1)} %param.6) | copy-start | bytes 12582916
  29.1 0.9 %copy-start.2 = (f32[256,256]{1,0:T(8,128)S(1)}, f32[256,256]{1,0:T(8,128)}, u32[]{:S(2)}) copy-start(f32[256,256]{1,0:T(8,128)} %get-tuple-element.24._map.own) | copy-start | bytes 786436
  30.2 5.1 %copy-start.1 = (bf16[1,2,1024,1024]{3,2,1,0:T(8,128)(2,1)S(1)}, bf16[1,2,1024,1024]{3,2,1,0:T(8,128)(2,1)}, u32[]{:S(2)}) copy-start(bf16[1,2,1024,1024]{3,2,1,0:T(8,128)(2,1)} %param.6) | copy-start | bytes 12582916
  31.6 5.5 %collective-permute-start = (bf16[64,256]{1,0:T(8,128)(2,1)S(1)}, bf16[64,256]{1,0:T(8,128)(2,1)S(1)}, u32[]{:S(2)}, u32[]{:S(2)}) collective-permute-start(bf16[64,256]{1,0:T(8,128)(2,1)S(1)} %get-tuple-element.26), channel_id=1, source_target_pairs={{0,3},{1,2},{2,1},{3,0},{4,7},{5,6},{6,5},{7,4},{8,11},{9,10},{10,... | collective-permute-start | bytes 98312 | tf_op jit(solution)/shard_map/ppermute | solution.py:503
  33.5 3.9 %collective-permute-start.1 = (bf16[64,256]{1,0:T(8,128)(2,1)S(1)}, bf16[64,256]{1,0:T(8,128)(2,1)S(1)}, u32[]{:S(2)}, u32[]{:S(2)}) collective-permute-start(bf16[64,256]{1,0:T(8,128)(2,1)S(1)} %get-tuple-element.27), channel_id=1, source_target_pairs={{0,2},{1,3},{2,0},{3,1},{4,6},{5,7},{6,4},{7,5},{8,10},{9,11},{10,... | collective-permute-start | bytes 98312 | tf_op jit(solution)/shard_map/ppermute | solution.py:499
  33.8 3.6 %collective-permute-start.2 = (bf16[64,256]{1,0:T(8,128)(2,1)S(1)}, bf16[64,256]{1,0:T(8,128)(2,1)S(1)}, u32[]{:S(2)}, u32[]{:S(2)}) collective-permute-start(bf16[64,256]{1,0:T(8,128)(2,1)S(1)} %get-tuple-element.28), channel_id=1, source_target_pairs={{0,1},{1,0},{2,3},{3,2},{4,5},{5,4},{6,7},{7,6},{8,9},{9,8},{10,11... | collective-permute-start | bytes 98312 | tf_op jit(solution)/shard_map/ppermute | solution.py:495
  34.6 11.2 %collective-permute-start.10 = (bf16[256,256]{1,0:T(8,128)(2,1)S(1)}, bf16[256,256]{1,0:T(8,128)(2,1)S(1)}, u32[]{:S(2)}, u32[]{:S(2)}) collective-permute-start(bf16[256,256]{1,0:T(8,128)(2,1)S(1)} %get-tuple-element.34), channel_id=1, source_target_pairs={{4,8},{8,12},{5,13},{6,10},{10,14},{7,15},{20,24},{24,28},{21,29},... | collective-permute-start | bytes 393224 | tf_op jit(solution)/shard_map/ppermute | solution.py:521
  38.0 8.6 %collective-permute-start.6 = (bf16[64,256]{1,0:T(8,128)(2,1)S(1)}, bf16[64,256]{1,0:T(8,128)(2,1)S(1)}, u32[]{:S(2)}, u32[]{:S(2)}) collective-permute-start(bf16[64,256]{1,0:T(8,128)(2,1)S(1)} %get-tuple-element.33), channel_id=1, source_target_pairs={{0,12},{1,13},{2,14},{3,15},{16,28},{17,29},{18,30},{19,31}} | collective-permute-start | bytes 98312 | tf_op jit(solution)/shard_map/ppermute | solution.py:527
  42.5 4.1 %collective-permute-start.7 = (bf16[64,256]{1,0:T(8,128)(2,1)S(1)}, bf16[64,256]{1,0:T(8,128)(2,1)S(1)}, u32[]{:S(2)}, u32[]{:S(2)}) collective-permute-start(bf16[64,256]{1,0:T(8,128)(2,1)S(1)} %get-tuple-element.33), channel_id=1, source_target_pairs={{0,4},{1,5},{2,6},{3,7},{16,20},{17,21},{18,22},{19,23}} | collective-permute-start | bytes 98312 | tf_op jit(solution)/shard_map/ppermute | solution.py:527
  43.8 2.9 %collective-permute-start.8 = (bf16[64,256]{1,0:T(8,128)(2,1)S(1)}, bf16[64,256]{1,0:T(8,128)(2,1)S(1)}, u32[]{:S(2)}, u32[]{:S(2)}) collective-permute-start(bf16[64,256]{1,0:T(8,128)(2,1)S(1)} %get-tuple-element.33), channel_id=1, source_target_pairs={{0,8},{1,9},{2,10},{3,11},{4,12},{5,13},{6,14},{7,15},{16,24},{17,... | collective-permute-start | bytes 98312 | tf_op jit(solution)/shard_map/ppermute | solution.py:527
  45.1 1.6 %collective-permute-start.9 = (bf16[64,256]{1,0:T(8,128)(2,1)S(1)}, bf16[64,256]{1,0:T(8,128)(2,1)S(1)}, u32[]{:S(2)}, u32[]{:S(2)}) collective-permute-start(bf16[64,256]{1,0:T(8,128)(2,1)S(1)} %get-tuple-element.33), channel_id=1, source_target_pairs={{4,8},{5,9},{6,10},{7,11},{8,12},{9,13},{10,14},{11,15},{20,24},{2... | collective-permute-start | bytes 98312 | tf_op jit(solution)/shard_map/ppermute | solution.py:527
  45.8 0.9 %collective-permute-start.11 = (bf16[256,256]{1,0:T(8,128)(2,1)S(1)}, bf16[256,256]{1,0:T(8,128)(2,1)S(1)}, u32[]{:S(2)}, u32[]{:S(2)}) collective-permute-start(bf16[256,256]{1,0:T(8,128)(2,1)S(1)} %collective-permute-done.10.got), channel_id=1, source_target_pairs={{8,9},{9,8},{10,11},{11,10},{12,13},{13,12},{14,15},{15,14},{24,25... | collective-permute-start | bytes 393224 | tf_op jit(solution)/shard_map/ppermute | solution.py:522
  46.6 2.8 %copy-start.4 = (bf16[1,1024,256]{2,1,0:T(8,128)(2,1)S(1)}, bf16[1,1024,256]{2,1,0:T(8,128)(2,1)}, u32[]{:S(2)}) copy-start(bf16[1,1024,256]{2,1,0:T(8,128)(2,1)} %param.8) | copy-start | bytes 1572868
  46.6 2.8 %copy-start.5 = (s32[1,8,2]{1,2,0:T(2,128)S(1)}, s32[1,8,2]{1,2,0:T(2,128)}, u32[]{:S(2)}) copy-start(s32[1,8,2]{1,2,0:T(2,128)} %param.9) | copy-start | bytes 196
  47.4 3.9 %collective-permute-start.12 = (bf16[64,256]{1,0:T(8,128)(2,1)S(1)}, bf16[64,256]{1,0:T(8,128)(2,1)S(1)}, u32[]{:S(2)}, u32[]{:S(2)}) collective-permute-start(bf16[64,256]{1,0:T(8,128)(2,1)S(1)} %get-tuple-element.39), channel_id=1, source_target_pairs={{0,3},{1,2},{2,1},{3,0},{4,7},{5,6},{6,5},{7,4},{8,11},{9,10},{10,... | collective-permute-start | bytes 98312 | tf_op jit(solution)/shard_map/ppermute | solution.py:503
  47.9 3.9 %collective-permute-start.13 = (bf16[64,256]{1,0:T(8,128)(2,1)S(1)}, bf16[64,256]{1,0:T(8,128)(2,1)S(1)}, u32[]{:S(2)}, u32[]{:S(2)}) collective-permute-start(bf16[64,256]{1,0:T(8,128)(2,1)S(1)} %get-tuple-element.40), channel_id=1, source_target_pairs={{0,2},{1,3},{2,0},{3,1},{4,6},{5,7},{6,4},{7,5},{8,10},{9,11},{10,... | collective-permute-start | bytes 98312 | tf_op jit(solution)/shard_map/ppermute | solution.py:499
  48.6 3.3 %collective-permute-start.14 = (bf16[64,256]{1,0:T(8,128)(2,1)S(1)}, bf16[64,256]{1,0:T(8,128)(2,1)S(1)}, u32[]{:S(2)}, u32[]{:S(2)}) collective-permute-start(bf16[64,256]{1,0:T(8,128)(2,1)S(1)} %get-tuple-element.41), channel_id=1, source_target_pairs={{0,1},{1,0},{2,3},{3,2},{4,5},{5,4},{6,7},{7,6},{8,9},{9,8},{10,11... | collective-permute-start | bytes 98312 | tf_op jit(solution)/shard_map/ppermute | solution.py:495

commit v25 on v23

--- a/solution.py
+++ b/solution.py
@@ -522,10 +522,10 @@
     across = to_across(other_map, sections)
     near = to_near(own_map, sections)
 
-    across = handed_on(across, received)
-    far = to_near(across, sections)
     source, *quarters = placed_source(received, inject, face_rows)
     shifts = exchange(*quarters, sections)
+    across = handed_on(across, quarters[0])
+    far = to_near(across, sections)
     four = sections // GROUP == 4
     total_map, parts = chain([own_map, far, across, near], BF16 if four else F32)
     early = image_and_maps(green, source, parts)

time: 50.4 us -> 50.8 us (level)
  local copies, waits for them, and re-layouts: 2.2 us -> 4.41 us
  waiting for transfers between devices: 10.8 us -> 9.46 us
  starting transfers between devices: 22.8 us -> 22 us
    ppermute x3, waiting for transfers between devices: 10.7 us -> 0.54 us  [to_across(): lax.ppermute(item, 'sec', [(s, s // GROUP * GROUP + (s % GROUP + CORES) %...]
    all_to_all x1, waiting for transfers between devices: 0.01 us -> 8.82 us  [per_device(): lax.all_to_all(outgoing, 'sec', split_axis=0, concat_axis=0, tiled=True)]
    unnamed x10 -> x14, local copies, waits for them, and re-layouts: 2.2 us -> 4.41 us
    ppermute x2, starting transfers between devices: 2.28 us -> 1.35 us  [to_far(): lax.ppermute(item, 'sec', [(s, s // GROUP * GROUP + (s % GROUP + CORES) %...]
    ppermute x4, starting transfers between devices: 7.72 us -> 7.09 us  [between(): return lax.ppermute(item, 'sec', pairs)]
    ppermute x3, starting transfers between devices: 2.99 us -> 3.58 us  [to_across(): lax.ppermute(item, 'sec', [(s, s // GROUP * GROUP + (s % GROUP + CORES) %...]
  transfers between devices with their start and end apart: 16 -> 16, of which waited for: 4 -> 3; matrix products, arithmetic and copies ran while one was open for 0% -> 0% of each run, Pallas kernels for 15% -> 15%
where the time goes in v25:
time: 50.8 us; the launch traced here: 50.2 us
  starting transfers between devices  22 us (43%)
  Pallas kernels  14 us (28%)
  waiting for transfers between devices  9.46 us (19%)
  local copies, waits for them, and re-layouts  4.41 us (9%)
    all_to_all x1, waiting for transfers between devices, per_device(): lax.all_to_all(outgoing, 'sec', split_axis=0, concat_axis=0, tiled=True)  8.82 us
    all_to_all x1, starting transfers between devices, per_device(): lax.all_to_all(outgoing, 'sec', split_axis=0, concat_axis=0, tiled=True)  7.54 us
    ppermute x4, starting transfers between devices, between(): return lax.ppermute(item, 'sec', pairs)  7.09 us
    unnamed x14, local copies, waits for them, and re-layouts  4.41 us
    pallas_call x1, Pallas kernels, outgoing_pairs(): call(pairs_kernel, 'pairs', [IN_HBM] * 4, shape(sections, CAP * energies...  4.38 us
    ppermute x3, starting transfers between devices, to_across(): lax.ppermute(item, 'sec', [(s, s // GROUP * GROUP + (s % GROUP + CORES) %...  3.58 us
    pallas_call x2, Pallas kernels, image_and_maps(): call(functools.partial(work_kernel, not held), 'image_and_maps', [IN_VMEM...  1.91 us
    pallas_call x1, Pallas kernels, propagator(): call(prop_kernel, 'prop', [IN_SMEM, IN_VMEM, IN_VMEM, IN_PLACE], shape(en...  1.9 us
  transfers between devices with their start and end apart: 16, of which 3 were waited for; matrix products, arithmetic and copies ran while one was open for 0% of the time, Pallas kernels for 15%

profile of v25, /device:TPU:0, one launch (start us, length us, event | category | flops | bytes accessed | tf_op | source)
XLA Modules:
  0.0 50.2 jit_solution(13531745298182017401)
XLA Ops:
  0.0 4.4 %pairs.1 = bf16[16,136,128]{2,1,0:T(8,128)(2,1)} custom-call(s32[16]{0:T(128)} %bitcast.21, s32[2,16]{1,0:T(2,128)} %bitcast.20, bf16[2,1024,1024]{2,1,0:T(8,128)(2,1)} %bitcast.9, bf16[2,1024,128]{2,1,0:T(8,128)(2,1)} %bitcast.14), custom_call_target="tpu_custom_call" | custom-call | flops 4600000000 | tf_op jit(solution)/shard_map/pairs/pallas_call | solution.py:161
  4.4 0.0 copy-start.2
  4.4 7.5 %all-to-all-start = ((bf16[16,136,128]{2,1,0:T(8,128)(2,1)}), bf16[16,136,128]{2,1,0:T(8,128)(2,1)S(1)}, u32[]{:S(2)}, u32[]{:S(2)}) async-start(bf16[16,136,128]{2,1,0:T(8,128)(2,1)} %pairs.1), calls=%async_computation | async-start | bytes 1114112 | tf_op jit(solution)/shard_map/all_to_all | solution.py:519
  12.0 0.0 copy-start
  12.0 2.2 %copy-done = bf16[1,2,1024,1024]{3,2,1,0:T(8,128)(2,1)S(1)} copy-done((bf16[1,2,1024,1024]{3,2,1,0:T(8,128)(2,1)S(1)}, bf16[1,2,1024,1024]{3,2,1,0:T(8,128)(2,1)}, u32[]{:S(2)}) %copy-start) | copy-done | bytes 4194328
  14.2 1.1 %face_maps.1 = (f32[256,256]{1,0:T(8,128)S(1)}, f32[256,256]{1,0:T(8,128)S(1)}, bf16[2,256,1024]{2,1,0:T(8,128)(2,1)S(1)}) custom-call(s32[2,8]{1,0:T(2,128)S(1)} %bitcast.18, bf16[2,1024,1024]{2,1,0:T(8,128)(2,1)S(1)} %bitcast.10, bf16[1024,256]{1,0:T(8,128)(2,1)S(1)} %bitcast.16), custom_call_target="tpu_custom_call" | custom-call | flops 1380000000 | tf_op jit(solution)/shard_map/face_maps/pallas_call | solution.py:199
  15.3 0.0 copy-start.5
  15.3 1.0 %copy-done.5 = bf16[2,256,1024]{2,1,0:T(8,128)(2,1)} copy-done((bf16[2,256,1024]{2,1,0:T(8,128)(2,1)}, bf16[2,256,1024]{2,1,0:T(8,128)(2,1)S(1)}, u32[]{:S(2)}) %copy-start.5) | copy-done | bytes 1048600
  16.3 1.9 %collective-permute-start.3 = (f32[256,256]{1,0:T(8,128)S(1)}, f32[256,256]{1,0:T(8,128)S(1)}, u32[]{:S(2)}, u32[]{:S(2)}) collective-permute-start(f32[256,256]{1,0:T(8,128)S(1)} %get-tuple-element.31), channel_id=1, source_target_pairs={{0,2},{1,3},{2,0},{3,1},{4,6},{5,7},{6,4},{7,5},{8,10},{9,11},{10,... | collective-permute-start | bytes 786440 | tf_op jit(solution)/shard_map/ppermute | solution.py:469
  18.2 0.0 collective-permute-start.5
  18.2 8.8 %all-to-all-done.received = bf16[16,136,128]{2,1,0:T(8,128)(2,1)S(1)} async-done(((bf16[16,136,128]{2,1,0:T(8,128)(2,1)}), bf16[16,136,128]{2,1,0:T(8,128)(2,1)S(1)}, u32[]{:S(2)}, u32[]{:S(2)}) %all-to-all-start) | async-done | bytes 557088 | tf_op jit(solution)/shard_map/all_to_all | solution.py:519
  27.0 1.2 %copy-done.6 = bf16[2,256,1024]{2,1,0:T(8,128)(2,1)S(1)} copy-done((bf16[2,256,1024]{2,1,0:T(8,128)(2,1)S(1)}, bf16[2,256,1024]{2,1,0:T(8,128)(2,1)}, u32[]{:S(2)}) %copy-start.6) | copy-done | bytes 1048600
  28.2 1.4 %source_and_face.1 = (bf16[2,1024,128]{2,1,0:T(8,128)(2,1)S(1)}, bf16[64,256]{1,0:T(8,128)(2,1)S(1)}, bf16[64,256]{1,0:T(8,128)(2,1)S(1)}, bf16[64,256]{1,0:T(8,128)(2,1)S(1)}, bf16[64,256]{1,0:T(8,128)(2,1)S(1)}) custom-call(bf16[16,136,128]{2,1,0:T(8,128)(2,1)S(1)} %all-to-all-done.received, bf16[2,1024,128]{2,1,0:T(8,128)(2,1)S(1)} %bitcast.15, ...), custom_call_target="tpu_custom_call" | custom-call | flops 1610000000 | tf_op jit(solution)/shard_map/source_and_face/pallas_call | solution.py:311
  29.6 0.0 collective-permute-done.3._map
  29.7 0.1 collective-permute-start.4
  29.7 0.9 %collective-permute-start = (bf16[64,256]{1,0:T(8,128)(2,1)S(1)}, bf16[64,256]{1,0:T(8,128)(2,1)S(1)}, u32[]{:S(2)}, u32[]{:S(2)}) collective-permute-start(bf16[64,256]{1,0:T(8,128)(2,1)S(1)} %get-tuple-element.27), channel_id=1, source_target_pairs={{0,3},{1,2},{2,1},{3,0},{4,7},{5,6},{6,5},{7,4},{8,11},{9,10},{10,... | collective-permute-start | bytes 98312 | tf_op jit(solution)/shard_map/ppermute | solution.py:473
  30.6 1.3 %collective-permute-start.1 = (bf16[64,256]{1,0:T(8,128)(2,1)S(1)}, bf16[64,256]{1,0:T(8,128)(2,1)S(1)}, u32[]{:S(2)}, u32[]{:S(2)}) collective-permute-start(bf16[64,256]{1,0:T(8,128)(2,1)S(1)} %get-tuple-element.28), channel_id=1, source_target_pairs={{0,2},{1,3},{2,0},{3,1},{4,6},{5,7},{6,4},{7,5},{8,10},{9,11},{10,... | collective-permute-start | bytes 98312 | tf_op jit(solution)/shard_map/ppermute | solution.py:469
  31.9 0.0 collective-permute-start.2
  31.9 0.0 collective-permute-done.5.near
  31.9 0.0 collective-permute-done.4.far
  31.9 0.8 %chain_maps.1 = (bf16[256,256]{1,0:T(8,128)(2,1)S(1)}, bf16[2,4,256,256]{3,2,1,0:T(8,128)(2,1)S(1)}) custom-call(f32[256,256]{1,0:T(8,128)S(1)} %get-tuple-element.30.own, f32[256,256]{1,0:T(8,128)S(1)} %collective-permute-done.4.far, f32[256,256]{1,0:T(8,128)S(1)} %after_exchange.1.across, f32[256,256]{1,0:T(8,128)S(1)} %collective-permute-done.5.near), custom_call_target="tpu_custom_call" | custom-call | flops 1035000000 | tf_op jit(solution)/shard_map/chain_maps/pallas_call | solution.py:244
  32.7 0.7 %collective-permute-start.10 = (bf16[256,256]{1,0:T(8,128)(2,1)S(1)}, bf16[256,256]{1,0:T(8,128)(2,1)S(1)}, u32[]{:S(2)}, u32[]{:S(2)}) collective-permute-start(bf16[256,256]{1,0:T(8,128)(2,1)S(1)} %get-tuple-element.36), channel_id=1, source_target_pairs={{4,8},{8,12},{5,13},{6,10},{10,14},{7,15},{20,24},{24,28},{21,29},... | collective-permute-start | bytes 393224 | tf_op jit(solution)/shard_map/ppermute | solution.py:491
  33.4 1.8 %image_and_maps.2 = (f32[2,1024,128]{2,1,0:T(8,128)S(1)}, bf16[2,2,256,256]{3,2,1,0:T(8,128)(2,1)S(1)}) custom-call(bf16[2,1024,1024]{2,1,0:T(8,128)(2,1)S(1)} %bitcast.11, bf16[2,1024,128]{2,1,0:T(8,128)(2,1)S(1)} %get-tuple-element.33.refs_1_, bf16[2,4,256,256]{3,2,1,0:T(8,128)(2,1)S(1)} %get-tuple-element.32.refs_2_.parts), custom_call_target="tpu_custom_call" | custom-call | flops 2300000000 | tf_op jit(solution)/shard_map/image_and_maps/pallas_call | solution.py:377
  35.2 0.0 collective-permute-done.far
  35.2 0.0 collective-permute-done.1.across
  35.2 0.0 collective-permute-done.2.near
  35.3 0.6 %plane_total.1 = (bf16[64,256]{1,0:T(8,128)(2,1)S(1)}, f32[3,64,256]{2,1,0:T(8,128)S(1)}) custom-call(bf16[64,256]{1,0:T(8,128)(2,1)S(1)} %get-tuple-element.26._packets.own, bf16[64,256]{1,0:T(8,128)(2,1)S(1)} %collective-permute-done.far, bf16[64,256]{1,0:T(8,128)(2,1)S(1)} %collective-permute-done.1.across, ...), custom_call_target="tpu_custom_call" | custom-call | flops 3449999872 | tf_op jit(solution)/shard_map/plane_total/pallas_call | solution.py:343
  35.9 3.8 %collective-permute-start.6 = (bf16[64,256]{1,0:T(8,128)(2,1)S(1)}, bf16[64,256]{1,0:T(8,128)(2,1)S(1)}, u32[]{:S(2)}, u32[]{:S(2)}) collective-permute-start(bf16[64,256]{1,0:T(8,128)(2,1)S(1)} %get-tuple-element.35), channel_id=1, source_target_pairs={{0,12},{1,13},{2,14},{3,15},{16,28},{17,29},{18,30},{19,31}} | collective-permute-start | bytes 98312 | tf_op jit(solution)/shard_map/ppermute | solution.py:497
  39.7 1.3 %collective-permute-start.7 = (bf16[64,256]{1,0:T(8,128)(2,1)S(1)}, bf16[64,256]{1,0:T(8,128)(2,1)S(1)}, u32[]{:S(2)}, u32[]{:S(2)}) collective-permute-start(bf16[64,256]{1,0:T(8,128)(2,1)S(1)} %get-tuple-element.35), channel_id=1, source_target_pairs={{0,4},{1,5},{2,6},{3,7},{16,20},{17,21},{18,22},{19,23}} | collective-permute-start | bytes 98312 | tf_op jit(solution)/shard_map/ppermute | solution.py:497
  41.0 1.3 %collective-permute-start.8 = (bf16[64,256]{1,0:T(8,128)(2,1)S(1)}, bf16[64,256]{1,0:T(8,128)(2,1)S(1)}, u32[]{:S(2)}, u32[]{:S(2)}) collective-permute-start(bf16[64,256]{1,0:T(8,128)(2,1)S(1)} %get-tuple-element.35), channel_id=1, source_target_pairs={{0,8},{1,9},{2,10},{3,11},{4,12},{5,13},{6,14},{7,15},{16,24},{17,... | collective-permute-start | bytes 98312 | tf_op jit(solution)/shard_map/ppermute | solution.py:497
  42.3 0.7 %collective-permute-start.9 = (bf16[64,256]{1,0:T(8,128)(2,1)S(1)}, bf16[64,256]{1,0:T(8,128)(2,1)S(1)}, u32[]{:S(2)}, u32[]{:S(2)}) collective-permute-start(bf16[64,256]{1,0:T(8,128)(2,1)S(1)} %get-tuple-element.35), channel_id=1, source_target_pairs={{4,8},{5,9},{6,10},{7,11},{8,12},{9,13},{10,14},{11,15},{20,24},{2... | collective-permute-start | bytes 98312 | tf_op jit(solution)/shard_map/ppermute | solution.py:497
  43.0 0.0 collective-permute-done.10.got
  43.0 0.7 %collective-permute-start.11 = (bf16[256,256]{1,0:T(8,128)(2,1)S(1)}, bf16[256,256]{1,0:T(8,128)(2,1)S(1)}, u32[]{:S(2)}, u32[]{:S(2)}) collective-permute-start(bf16[256,256]{1,0:T(8,128)(2,1)S(1)} %collective-permute-done.10.got), channel_id=1, source_target_pairs={{8,9},{9,8},{10,11},{11,10},{12,13},{13,12},{14,15},{15,14},{24,25... | collective-permute-start | bytes 393224 | tf_op jit(solution)/shard_map/ppermute | solution.py:492
  43.7 0.1 image_and_maps.3
  43.8 0.0 collective-permute-done.6.third
  43.8 0.0 collective-permute-done.7.near_one
  43.8 0.1 collective-permute-done.8.second
  43.9 0.0 collective-permute-done.9.far_one
  43.9 0.0 collective-permute-done.11.other
  43.9 0.7 %entering.1 = (bf16[64,256]{1,0:T(8,128)(2,1)S(1)}, bf16[64,256]{1,0:T(8,128)(2,1)S(1)}, bf16[64,256]{1,0:T(8,128)(2,1)S(1)}, bf16[64,256]{1,0:T(8,128)(2,1)S(1)}) custom-call(bf16[64,256]{1,0:T(8,128)(2,1)S(1)} %collective-permute-done.6.third, bf16[64,256]{1,0:T(8,128)(2,1)S(1)} %collective-permute-done.7.near_one, ...), custom_call_target="tpu_custom_call" | custom-call | flops 1610000000 | tf_op jit(solution)/shard_map/entering/pallas_call | solution.py:417
  44.6 0.5 collective-permute-start.12
  45.1 0.4 collective-permute-start.13
  45.5 1.1 %collective-permute-start.14 = (bf16[64,256]{1,0:T(8,128)(2,1)S(1)}, bf16[64,256]{1,0:T(8,128)(2,1)S(1)}, u32[]{:S(2)}, u32[]{:S(2)}) collective-permute-start(bf16[64,256]{1,0:T(8,128)(2,1)S(1)} %get-tuple-element.43), channel_id=1, source_target_pairs={{0,1},{1,0},{2,3},{3,2},{4,5},{5,4},{6,7},{7,6},{8,9},{9,8},{10,11... | collective-permute-start | bytes 98312 | tf_op jit(solution)/shard_map/ppermute | solution.py:465
  46.6 1.9 %prop.1 = bf16[2,1024,256]{2,1,0:T(8,128)(2,1)S(1)} custom-call(s32[2,8]{1,0:T(2,128)S(1)} %bitcast.19, bf16[2,1024,1024]{2,1,0:T(8,128)(2,1)S(1)} %bitcast.13, bf16[1024,256]{1,0:T(8,128)(2,1)S(1)} %bitcast.17, bf16[64,256]{1,0:T(8,128)(2,1)S(1)} %get-tuple-element.40._tie.own), custom_call_target="tpu_custom_call" | custom-call | flops 1724999936 | tf_op jit(solution)/shard_map/prop/pallas_call | solution.py:218
  48.5 0.0 collective-permute-done.12.far
  48.5 0.5 %collective-permute-done.13.across = bf16[64,256]{1,0:T(8,128)(2,1)S(1)} collective-permute-done((bf16[64,256]{1,0:T(8,128)(2,1)S(1)}, bf16[64,256]{1,0:T(8,128)(2,1)S(1)}, u32[]{:S(2)}, u32[]{:S(2)}) %collective-permute-start.13) | collective-permute-done | bytes 32800 | tf_op jit(solution)/shard_map/ppermute | solution.py:469
  49.0 0.0 collective-permute-done.14.near
  49.0 1.2 %waves.1 = bf16[2,1024,128]{2,1,0:T(8,128)(2,1)} custom-call(bf16[64,256]{1,0:T(8,128)(2,1)S(1)} %get-tuple-element.40._tie.own, bf16[64,256]{1,0:T(8,128)(2,1)S(1)} %collective-permute-done.12.far, bf16[64,256]{1,0:T(8,128)(2,1)S(1)} %collective-permute-done.13.across, bf16[64,256]{1,0:T(8,128)(2,1)S(1)} %collective-permute-done.14.near, ...), custom_call_target="tpu_custom_call" | custom-call | flops 1495000064 | tf_op jit(solution)/shard_map/waves/pallas_call | solution.py:448
  (9 shorter events, 0.0 us)
Async XLA Ops:
  0.0 12.0 %copy-start.3 = (bf16[1,1024,256]{2,1,0:T(8,128)(2,1)S(1)}, bf16[1,1024,256]{2,1,0:T(8,128)(2,1)}, u32[]{:S(2)}) copy-start(bf16[1,1024,256]{2,1,0:T(8,128)(2,1)} %param.8) | copy-start | bytes 1572868
  0.0 12.0 %copy-start.4 = (s32[1,8,2]{1,2,0:T(2,128)S(1)}, s32[1,8,2]{1,2,0:T(2,128)}, u32[]{:S(2)}) copy-start(s32[1,8,2]{1,2,0:T(2,128)} %param.9) | copy-start | bytes 196
  4.4 22.6 %copy-start.2 = (bf16[1,2,1024,128]{3,2,1,0:T(8,128)(2,1)S(1)}, bf16[1,2,1024,128]{3,2,1,0:T(8,128)(2,1)}, u32[]{:S(2)}) copy-start(bf16[1,2,1024,128]{3,2,1,0:T(8,128)(2,1)} %param.7) | copy-start | bytes 1572868
  4.4 22.6 %all-to-all-start = ((bf16[16,136,128]{2,1,0:T(8,128)(2,1)}), bf16[16,136,128]{2,1,0:T(8,128)(2,1)S(1)}, u32[]{:S(2)}, u32[]{:S(2)}) async-start(bf16[16,136,128]{2,1,0:T(8,128)(2,1)} %pairs.1), calls=%async_computation | async-start | bytes 1114112 | tf_op jit(solution)/shard_map/all_to_all | solution.py:519
  12.0 2.2 %copy-start = (bf16[1,2,1024,1024]{3,2,1,0:T(8,128)(2,1)S(1)}, bf16[1,2,1024,1024]{3,2,1,0:T(8,128)(2,1)}, u32[]{:S(2)}) copy-start(bf16[1,2,1024,1024]{3,2,1,0:T(8,128)(2,1)} %param.6) | copy-start | bytes 12582916
  15.3 1.0 %copy-start.5 = (bf16[2,256,1024]{2,1,0:T(8,128)(2,1)}, bf16[2,256,1024]{2,1,0:T(8,128)(2,1)S(1)}, u32[]{:S(2)}) copy-start(bf16[2,256,1024]{2,1,0:T(8,128)(2,1)S(1)} %get-tuple-element.25.face_rows) | copy-start | bytes 3145732
  16.3 13.4 %collective-permute-start.3 = (f32[256,256]{1,0:T(8,128)S(1)}, f32[256,256]{1,0:T(8,128)S(1)}, u32[]{:S(2)}, u32[]{:S(2)}) collective-permute-start(f32[256,256]{1,0:T(8,128)S(1)} %get-tuple-element.31), channel_id=1, source_target_pairs={{0,2},{1,3},{2,0},{3,1},{4,6},{5,7},{6,4},{7,5},{8,10},{9,11},{10,... | collective-permute-start | bytes 786440 | tf_op jit(solution)/shard_map/ppermute | solution.py:469
  18.2 13.7 %collective-permute-start.5 = (f32[256,256]{1,0:T(8,128)S(1)}, f32[256,256]{1,0:T(8,128)S(1)}, u32[]{:S(2)}, u32[]{:S(2)}) collective-permute-start(f32[256,256]{1,0:T(8,128)S(1)} %get-tuple-element.30.own), channel_id=1, source_target_pairs={{0,1},{1,0},{2,3},{3,2},{4,5},{5,4},{6,7},{7,6},{8,9},{9,8},{10,11... | collective-permute-start | bytes 786440 | tf_op jit(solution)/shard_map/ppermute | solution.py:465
  27.0 1.2 %copy-start.6 = (bf16[2,256,1024]{2,1,0:T(8,128)(2,1)S(1)}, bf16[2,256,1024]{2,1,0:T(8,128)(2,1)}, u32[]{:S(2)}) copy-start(bf16[2,256,1024]{2,1,0:T(8,128)(2,1)} %copy-done.5) | copy-start | bytes 3145732
  28.2 5.2 %copy-start.1 = (bf16[1,2,1024,1024]{3,2,1,0:T(8,128)(2,1)S(1)}, bf16[1,2,1024,1024]{3,2,1,0:T(8,128)(2,1)}, u32[]{:S(2)}) copy-start(bf16[1,2,1024,1024]{3,2,1,0:T(8,128)(2,1)} %param.6) | copy-start | bytes 12582916
  29.7 2.2 %collective-permute-start.4 = (f32[256,256]{1,0:T(8,128)S(1)}, f32[256,256]{1,0:T(8,128)S(1)}, u32[]{:S(2)}, u32[]{:S(2)}) collective-permute-start(f32[256,256]{1,0:T(8,128)S(1)} %after_exchange.1.across), channel_id=1, source_target_pairs={{0,1},{1,0},{2,3},{3,2},{4,5},{5,4},{6,7},{7,6},{8,9},{9,8},{10,11... | collective-permute-start | bytes 786440 | tf_op jit(solution)/shard_map/ppermute | solution.py:465
  29.7 5.5 %collective-permute-start = (bf16[64,256]{1,0:T(8,128)(2,1)S(1)}, bf16[64,256]{1,0:T(8,128)(2,1)S(1)}, u32[]{:S(2)}, u32[]{:S(2)}) collective-permute-start(bf16[64,256]{1,0:T(8,128)(2,1)S(1)} %get-tuple-element.27), channel_id=1, source_target_pairs={{0,3},{1,2},{2,1},{3,0},{4,7},{5,6},{6,5},{7,4},{8,11},{9,10},{10,... | collective-permute-start | bytes 98312 | tf_op jit(solution)/shard_map/ppermute | solution.py:473
  30.6 4.6 %collective-permute-start.1 = (bf16[64,256]{1,0:T(8,128)(2,1)S(1)}, bf16[64,256]{1,0:T(8,128)(2,1)S(1)}, u32[]{:S(2)}, u32[]{:S(2)}) collective-permute-start(bf16[64,256]{1,0:T(8,128)(2,1)S(1)} %get-tuple-element.28), channel_id=1, source_target_pairs={{0,2},{1,3},{2,0},{3,1},{4,6},{5,7},{6,4},{7,5},{8,10},{9,11},{10,... | collective-permute-start | bytes 98312 | tf_op jit(solution)/shard_map/ppermute | solution.py:469
  31.9 3.4 %collective-permute-start.2 = (bf16[64,256]{1,0:T(8,128)(2,1)S(1)}, bf16[64,256]{1,0:T(8,128)(2,1)S(1)}, u32[]{:S(2)}, u32[]{:S(2)}) collective-permute-start(bf16[64,256]{1,0:T(8,128)(2,1)S(1)} %get-tuple-element.29), channel_id=1, source_target_pairs={{0,1},{1,0},{2,3},{3,2},{4,5},{5,4},{6,7},{7,6},{8,9},{9,8},{10,11... | collective-permute-start | bytes 98312 | tf_op jit(solution)/shard_map/ppermute | solution.py:465
  32.7 10.2 %collective-permute-start.10 = (bf16[256,256]{1,0:T(8,128)(2,1)S(1)}, bf16[256,256]{1,0:T(8,128)(2,1)S(1)}, u32[]{:S(2)}, u32[]{:S(2)}) collective-permute-start(bf16[256,256]{1,0:T(8,128)(2,1)S(1)} %get-tuple-element.36), channel_id=1, source_target_pairs={{4,8},{8,12},{5,13},{6,10},{10,14},{7,15},{20,24},{24,28},{21,29},... | collective-permute-start | bytes 393224 | tf_op jit(solution)/shard_map/ppermute | solution.py:491
  35.9 7.9 %collective-permute-start.6 = (bf16[64,256]{1,0:T(8,128)(2,1)S(1)}, bf16[64,256]{1,0:T(8,128)(2,1)S(1)}, u32[]{:S(2)}, u32[]{:S(2)}) collective-permute-start(bf16[64,256]{1,0:T(8,128)(2,1)S(1)} %get-tuple-element.35), channel_id=1, source_target_pairs={{0,12},{1,13},{2,14},{3,15},{16,28},{17,29},{18,30},{19,31}} | collective-permute-start | bytes 98312 | tf_op jit(solution)/shard_map/ppermute | solution.py:497
  39.7 4.1 %collective-permute-start.7 = (bf16[64,256]{1,0:T(8,128)(2,1)S(1)}, bf16[64,256]{1,0:T(8,128)(2,1)S(1)}, u32[]{:S(2)}, u32[]{:S(2)}) collective-permute-start(bf16[64,256]{1,0:T(8,128)(2,1)S(1)} %get-tuple-element.35), channel_id=1, source_target_pairs={{0,4},{1,5},{2,6},{3,7},{16,20},{17,21},{18,22},{19,23}} | collective-permute-start | bytes 98312 | tf_op jit(solution)/shard_map/ppermute | solution.py:497
  41.0 2.9 %collective-permute-start.8 = (bf16[64,256]{1,0:T(8,128)(2,1)S(1)}, bf16[64,256]{1,0:T(8,128)(2,1)S(1)}, u32[]{:S(2)}, u32[]{:S(2)}) collective-permute-start(bf16[64,256]{1,0:T(8,128)(2,1)S(1)} %get-tuple-element.35), channel_id=1, source_target_pairs={{0,8},{1,9},{2,10},{3,11},{4,12},{5,13},{6,14},{7,15},{16,24},{17,... | collective-permute-start | bytes 98312 | tf_op jit(solution)/shard_map/ppermute | solution.py:497
  42.3 1.6 %collective-permute-start.9 = (bf16[64,256]{1,0:T(8,128)(2,1)S(1)}, bf16[64,256]{1,0:T(8,128)(2,1)S(1)}, u32[]{:S(2)}, u32[]{:S(2)}) collective-permute-start(bf16[64,256]{1,0:T(8,128)(2,1)S(1)} %get-tuple-element.35), channel_id=1, source_target_pairs={{4,8},{5,9},{6,10},{7,11},{8,12},{9,13},{10,14},{11,15},{20,24},{2... | collective-permute-start | bytes 98312 | tf_op jit(solution)/shard_map/ppermute | solution.py:497
  43.0 0.9 %collective-permute-start.11 = (bf16[256,256]{1,0:T(8,128)(2,1)S(1)}, bf16[256,256]{1,0:T(8,128)(2,1)S(1)}, u32[]{:S(2)}, u32[]{:S(2)}) collective-permute-start(bf16[256,256]{1,0:T(8,128)(2,1)S(1)} %collective-permute-done.10.got), channel_id=1, source_target_pairs={{8,9},{9,8},{10,11},{11,10},{12,13},{13,12},{14,15},{15,14},{24,25... | collective-permute-start | bytes 393224 | tf_op jit(solution)/shard_map/ppermute | solution.py:492
  44.6 3.8 %collective-permute-start.12 = (bf16[64,256]{1,0:T(8,128)(2,1)S(1)}, bf16[64,256]{1,0:T(8,128)(2,1)S(1)}, u32[]{:S(2)}, u32[]{:S(2)}) collective-permute-start(bf16[64,256]{1,0:T(8,128)(2,1)S(1)} %get-tuple-element.41), channel_id=1, source_target_pairs={{0,3},{1,2},{2,1},{3,0},{4,7},{5,6},{6,5},{7,4},{8,11},{9,10},{10,... | collective-permute-start | bytes 98312 | tf_op jit(solution)/shard_map/ppermute | solution.py:473
  45.1 3.9 %collective-permute-start.13 = (bf16[64,256]{1,0:T(8,128)(2,1)S(1)}, bf16[64,256]{1,0:T(8,128)(2,1)S(1)}, u32[]{:S(2)}, u32[]{:S(2)}) collective-permute-start(bf16[64,256]{1,0:T(8,128)(2,1)S(1)} %get-tuple-element.42), channel_id=1, source_target_pairs={{0,2},{1,3},{2,0},{3,1},{4,6},{5,7},{6,4},{7,5},{8,10},{9,11},{10,... | collective-permute-start | bytes 98312 | tf_op jit(solution)/shard_map/ppermute | solution.py:469
  45.5 3.5 %collective-permute-start.14 = (bf16[64,256]{1,0:T(8,128)(2,1)S(1)}, bf16[64,256]{1,0:T(8,128)(2,1)S(1)}, u32[]{:S(2)}, u32[]{:S(2)}) collective-permute-start(bf16[64,256]{1,0:T(8,128)(2,1)S(1)} %get-tuple-element.43), channel_id=1, source_target_pairs={{0,1},{1,0},{2,3},{3,2},{4,5},{5,4},{6,7},{7,6},{8,9},{9,8},{10,11... | collective-permute-start | bytes 98312 | tf_op jit(solution)/shard_map/ppermute | solution.py:465

commit v26 on v25

--- a/solution.py
+++ b/solution.py
@@ -520,12 +520,11 @@
 
     own_map, other_map, face_rows = face_maps(tiles, green, coupling)
     across = to_across(other_map, sections)
-    near = to_near(own_map, sections)
 
     source, *quarters = placed_source(received, inject, face_rows)
     shifts = exchange(*quarters, sections)
     across = handed_on(across, quarters[0])
-    far = to_near(across, sections)
+    near, far = to_near(handed_on(own_map, quarters[0]), sections), to_near(across, sections)
     four = sections // GROUP == 4
     total_map, parts = chain([own_map, far, across, near], BF16 if four else F32)
     early = image_and_maps(green, source, parts)

time: 50.8 us -> 51 us (level)
    ppermute x4, starting transfers between devices: 1.14 us -> 1.95 us  [to_near(): return lax.ppermute(item, 'sec', [(s, s ^ 1) for s in range(sections)])]
    ppermute x3, starting transfers between devices: 3.58 us -> 3.03 us  [to_across(): lax.ppermute(item, 'sec', [(s, s // GROUP * GROUP + (s % GROUP + CORES) %...]
    unnamed x14 -> x15, local copies, waits for them, and re-layouts: 4.41 us -> 4.42 us
where the time goes in v26:
time: 51 us; the launch traced here: 50.6 us
  starting transfers between devices  22.2 us (44%)
  Pallas kernels  14.2 us (28%)
  waiting for transfers between devices  9.44 us (19%)
  local copies, waits for them, and re-layouts  4.42 us (9%)
    all_to_all x1, waiting for transfers between devices, per_device(): lax.all_to_all(outgoing, 'sec', split_axis=0, concat_axis=0, tiled=True)  8.8 us
    all_to_all x1, starting transfers between devices, per_device(): lax.all_to_all(outgoing, 'sec', split_axis=0, concat_axis=0, tiled=True)  7.33 us
    ppermute x4, starting transfers between devices, between(): return lax.ppermute(item, 'sec', pairs)  7.26 us
    pallas_call x1, Pallas kernels, outgoing_pairs(): call(pairs_kernel, 'pairs', [IN_HBM] * 4, shape(sections, CAP * energies...  4.56 us
    unnamed x15, local copies, waits for them, and re-layouts  4.42 us
    ppermute x3, starting transfers between devices, to_across(): lax.ppermute(item, 'sec', [(s, s // GROUP * GROUP + (s % GROUP + CORES) %...  3.03 us
    ppermute x4, starting transfers between devices, to_near(): return lax.ppermute(item, 'sec', [(s, s ^ 1) for s in range(sections)])  1.95 us
    pallas_call x2, Pallas kernels, image_and_maps(): call(functools.partial(work_kernel, not held), 'image_and_maps', [IN_VMEM...  1.91 us
  transfers between devices with their start and end apart: 16, of which 3 were waited for; matrix products, arithmetic and copies ran while one was open for 0% of the time, Pallas kernels for 15%

profile of v26, /device:TPU:0, one launch (start us, length us, event | category | flops | bytes accessed | tf_op | source)
XLA Modules:
  0.0 50.6 jit_solution(18184867383526228514)
XLA Ops:
  0.0 4.6 %pairs.1 = bf16[16,136,128]{2,1,0:T(8,128)(2,1)} custom-call(s32[16]{0:T(128)} %bitcast.21, s32[2,16]{1,0:T(2,128)} %bitcast.20, bf16[2,1024,1024]{2,1,0:T(8,128)(2,1)} %bitcast.9, bf16[2,1024,128]{2,1,0:T(8,128)(2,1)} %bitcast.14), custom_call_target="tpu_custom_call" | custom-call | flops 4600000000 | tf_op jit(solution)/shard_map/pairs/pallas_call | solution.py:161
  4.6 0.0 copy-start.2
  4.6 7.3 %all-to-all-start = ((bf16[16,136,128]{2,1,0:T(8,128)(2,1)}), bf16[16,136,128]{2,1,0:T(8,128)(2,1)S(1)}, u32[]{:S(2)}, u32[]{:S(2)}) async-start(bf16[16,136,128]{2,1,0:T(8,128)(2,1)} %pairs.1), calls=%async_computation | async-start | bytes 1114112 | tf_op jit(solution)/shard_map/all_to_all | solution.py:519
  11.9 0.0 copy-start
  12.0 2.2 %copy-done = bf16[1,2,1024,1024]{3,2,1,0:T(8,128)(2,1)S(1)} copy-done((bf16[1,2,1024,1024]{3,2,1,0:T(8,128)(2,1)S(1)}, bf16[1,2,1024,1024]{3,2,1,0:T(8,128)(2,1)}, u32[]{:S(2)}) %copy-start) | copy-done | bytes 4194328
  14.1 1.1 %face_maps.1 = (f32[256,256]{1,0:T(8,128)S(1)}, f32[256,256]{1,0:T(8,128)S(1)}, bf16[2,256,1024]{2,1,0:T(8,128)(2,1)S(1)}) custom-call(s32[2,8]{1,0:T(2,128)S(1)} %bitcast.18, bf16[2,1024,1024]{2,1,0:T(8,128)(2,1)S(1)} %bitcast.10, bf16[1024,256]{1,0:T(8,128)(2,1)S(1)} %bitcast.16), custom_call_target="tpu_custom_call" | custom-call | flops 1380000000 | tf_op jit(solution)/shard_map/face_maps/pallas_call | solution.py:199
  15.3 1.0 %copy-done.5 = bf16[2,256,1024]{2,1,0:T(8,128)(2,1)} copy-done((bf16[2,256,1024]{2,1,0:T(8,128)(2,1)}, bf16[2,256,1024]{2,1,0:T(8,128)(2,1)S(1)}, u32[]{:S(2)}) %copy-start.5) | copy-done | bytes 1048600
  16.2 1.9 %collective-permute-start.3 = (f32[256,256]{1,0:T(8,128)S(1)}, f32[256,256]{1,0:T(8,128)S(1)}, u32[]{:S(2)}, u32[]{:S(2)}) collective-permute-start(f32[256,256]{1,0:T(8,128)S(1)} %get-tuple-element.31), channel_id=1, source_target_pairs={{0,2},{1,3},{2,0},{3,1},{4,6},{5,7},{6,4},{7,5},{8,10},{9,11},{10,... | collective-permute-start | bytes 786440 | tf_op jit(solution)/shard_map/ppermute | solution.py:469
  18.2 8.8 %all-to-all-done.received = bf16[16,136,128]{2,1,0:T(8,128)(2,1)S(1)} async-done(((bf16[16,136,128]{2,1,0:T(8,128)(2,1)}), bf16[16,136,128]{2,1,0:T(8,128)(2,1)S(1)}, u32[]{:S(2)}, u32[]{:S(2)}) %all-to-all-start) | async-done | bytes 557088 | tf_op jit(solution)/shard_map/all_to_all | solution.py:519
  27.0 0.0 copy-done.2
  27.0 1.2 %copy-done.6 = bf16[2,256,1024]{2,1,0:T(8,128)(2,1)S(1)} copy-done((bf16[2,256,1024]{2,1,0:T(8,128)(2,1)S(1)}, bf16[2,256,1024]{2,1,0:T(8,128)(2,1)}, u32[]{:S(2)}) %copy-start.6) | copy-done | bytes 1048600
  28.2 1.4 %source_and_face.1 = (bf16[2,1024,128]{2,1,0:T(8,128)(2,1)S(1)}, bf16[64,256]{1,0:T(8,128)(2,1)S(1)}, bf16[64,256]{1,0:T(8,128)(2,1)S(1)}, bf16[64,256]{1,0:T(8,128)(2,1)S(1)}, bf16[64,256]{1,0:T(8,128)(2,1)S(1)}) custom-call(bf16[16,136,128]{2,1,0:T(8,128)(2,1)S(1)} %all-to-all-done.received, bf16[2,1024,128]{2,1,0:T(8,128)(2,1)S(1)} %bitcast.15, ...), custom_call_target="tpu_custom_call" | custom-call | flops 1610000000 | tf_op jit(solution)/shard_map/source_and_face/pallas_call | solution.py:311
  29.6 0.1 collective-permute-start.5
  29.7 0.0 collective-permute-done.3._map
  29.7 0.5 collective-permute-start.4
  30.2 0.8 %collective-permute-start = (bf16[64,256]{1,0:T(8,128)(2,1)S(1)}, bf16[64,256]{1,0:T(8,128)(2,1)S(1)}, u32[]{:S(2)}, u32[]{:S(2)}) collective-permute-start(bf16[64,256]{1,0:T(8,128)(2,1)S(1)} %get-tuple-element.27), channel_id=1, source_target_pairs={{0,3},{1,2},{2,1},{3,0},{4,7},{5,6},{6,5},{7,4},{8,11},{9,10},{10,... | collective-permute-start | bytes 98312 | tf_op jit(solution)/shard_map/ppermute | solution.py:473
  31.0 0.9 %collective-permute-start.1 = (bf16[64,256]{1,0:T(8,128)(2,1)S(1)}, bf16[64,256]{1,0:T(8,128)(2,1)S(1)}, u32[]{:S(2)}, u32[]{:S(2)}) collective-permute-start(bf16[64,256]{1,0:T(8,128)(2,1)S(1)} %get-tuple-element.28), channel_id=1, source_target_pairs={{0,2},{1,3},{2,0},{3,1},{4,6},{5,7},{6,4},{7,5},{8,10},{9,11},{10,... | collective-permute-start | bytes 98312 | tf_op jit(solution)/shard_map/ppermute | solution.py:469
  31.9 0.2 collective-permute-start.2
  32.1 0.0 collective-permute-done.5.near
  32.1 0.0 collective-permute-done.4.far
  32.1 0.8 %chain_maps.1 = (bf16[256,256]{1,0:T(8,128)(2,1)S(1)}, bf16[2,4,256,256]{3,2,1,0:T(8,128)(2,1)S(1)}) custom-call(f32[256,256]{1,0:T(8,128)S(1)} %get-tuple-element.30.own, f32[256,256]{1,0:T(8,128)S(1)} %collective-permute-done.4.far, f32[256,256]{1,0:T(8,128)S(1)} %after_exchange.2.across, f32[256,256]{1,0:T(8,128)S(1)} %collective-permute-done.5.near), custom_call_target="tpu_custom_call" | custom-call | flops 1035000000 | tf_op jit(solution)/shard_map/chain_maps/pallas_call | solution.py:244
  32.9 0.7 %collective-permute-start.10 = (bf16[256,256]{1,0:T(8,128)(2,1)S(1)}, bf16[256,256]{1,0:T(8,128)(2,1)S(1)}, u32[]{:S(2)}, u32[]{:S(2)}) collective-permute-start(bf16[256,256]{1,0:T(8,128)(2,1)S(1)} %get-tuple-element.36), channel_id=1, source_target_pairs={{4,8},{8,12},{5,13},{6,10},{10,14},{7,15},{20,24},{24,28},{21,29},... | collective-permute-start | bytes 393224 | tf_op jit(solution)/shard_map/ppermute | solution.py:491
  33.6 1.8 %image_and_maps.2 = (f32[2,1024,128]{2,1,0:T(8,128)S(1)}, bf16[2,2,256,256]{3,2,1,0:T(8,128)(2,1)S(1)}) custom-call(bf16[2,1024,1024]{2,1,0:T(8,128)(2,1)S(1)} %bitcast.11, bf16[2,1024,128]{2,1,0:T(8,128)(2,1)S(1)} %get-tuple-element.33.refs_1_, bf16[2,4,256,256]{3,2,1,0:T(8,128)(2,1)S(1)} %get-tuple-element.32.refs_2_.parts), custom_call_target="tpu_custom_call" | custom-call | flops 2300000000 | tf_op jit(solution)/shard_map/image_and_maps/pallas_call | solution.py:377
  35.4 0.0 collective-permute-done.far
  35.4 0.0 collective-permute-done.1.across
  35.4 0.0 collective-permute-done.2.near
  35.4 0.6 %plane_total.1 = (bf16[64,256]{1,0:T(8,128)(2,1)S(1)}, f32[3,64,256]{2,1,0:T(8,128)S(1)}) custom-call(bf16[64,256]{1,0:T(8,128)(2,1)S(1)} %get-tuple-element.26._packets.own, bf16[64,256]{1,0:T(8,128)(2,1)S(1)} %collective-permute-done.far, bf16[64,256]{1,0:T(8,128)(2,1)S(1)} %collective-permute-done.1.across, ...), custom_call_target="tpu_custom_call" | custom-call | flops 3449999872 | tf_op jit(solution)/shard_map/plane_total/pallas_call | solution.py:343
  36.0 4.0 %collective-permute-start.6 = (bf16[64,256]{1,0:T(8,128)(2,1)S(1)}, bf16[64,256]{1,0:T(8,128)(2,1)S(1)}, u32[]{:S(2)}, u32[]{:S(2)}) collective-permute-start(bf16[64,256]{1,0:T(8,128)(2,1)S(1)} %get-tuple-element.35), channel_id=1, source_target_pairs={{0,12},{1,13},{2,14},{3,15},{16,28},{17,29},{18,30},{19,31}} | collective-permute-start | bytes 98312 | tf_op jit(solution)/shard_map/ppermute | solution.py:497
  40.1 1.3 %collective-permute-start.7 = (bf16[64,256]{1,0:T(8,128)(2,1)S(1)}, bf16[64,256]{1,0:T(8,128)(2,1)S(1)}, u32[]{:S(2)}, u32[]{:S(2)}) collective-permute-start(bf16[64,256]{1,0:T(8,128)(2,1)S(1)} %get-tuple-element.35), channel_id=1, source_target_pairs={{0,4},{1,5},{2,6},{3,7},{16,20},{17,21},{18,22},{19,23}} | collective-permute-start | bytes 98312 | tf_op jit(solution)/shard_map/ppermute | solution.py:497
  41.4 1.3 %collective-permute-start.8 = (bf16[64,256]{1,0:T(8,128)(2,1)S(1)}, bf16[64,256]{1,0:T(8,128)(2,1)S(1)}, u32[]{:S(2)}, u32[]{:S(2)}) collective-permute-start(bf16[64,256]{1,0:T(8,128)(2,1)S(1)} %get-tuple-element.35), channel_id=1, source_target_pairs={{0,8},{1,9},{2,10},{3,11},{4,12},{5,13},{6,14},{7,15},{16,24},{17,... | collective-permute-start | bytes 98312 | tf_op jit(solution)/shard_map/ppermute | solution.py:497
  42.7 0.7 %collective-permute-start.9 = (bf16[64,256]{1,0:T(8,128)(2,1)S(1)}, bf16[64,256]{1,0:T(8,128)(2,1)S(1)}, u32[]{:S(2)}, u32[]{:S(2)}) collective-permute-start(bf16[64,256]{1,0:T(8,128)(2,1)S(1)} %get-tuple-element.35), channel_id=1, source_target_pairs={{4,8},{5,9},{6,10},{7,11},{8,12},{9,13},{10,14},{11,15},{20,24},{2... | collective-permute-start | bytes 98312 | tf_op jit(solution)/shard_map/ppermute | solution.py:497
  43.3 0.0 collective-permute-done.10.got
  43.3 0.7 %collective-permute-start.11 = (bf16[256,256]{1,0:T(8,128)(2,1)S(1)}, bf16[256,256]{1,0:T(8,128)(2,1)S(1)}, u32[]{:S(2)}, u32[]{:S(2)}) collective-permute-start(bf16[256,256]{1,0:T(8,128)(2,1)S(1)} %collective-permute-done.10.got), channel_id=1, source_target_pairs={{8,9},{9,8},{10,11},{11,10},{12,13},{13,12},{14,15},{15,14},{24,25... | collective-permute-start | bytes 393224 | tf_op jit(solution)/shard_map/ppermute | solution.py:492
  44.0 0.1 image_and_maps.3
  44.1 0.0 collective-permute-done.6.third
  44.2 0.0 collective-permute-done.7.near_one
  44.2 0.1 collective-permute-done.8.second
  44.2 0.0 collective-permute-done.9.far_one
  44.2 0.0 collective-permute-done.11.other
  44.2 0.7 %entering.1 = (bf16[64,256]{1,0:T(8,128)(2,1)S(1)}, bf16[64,256]{1,0:T(8,128)(2,1)S(1)}, bf16[64,256]{1,0:T(8,128)(2,1)S(1)}, bf16[64,256]{1,0:T(8,128)(2,1)S(1)}) custom-call(bf16[64,256]{1,0:T(8,128)(2,1)S(1)} %collective-permute-done.6.third, bf16[64,256]{1,0:T(8,128)(2,1)S(1)} %collective-permute-done.7.near_one, ...), custom_call_target="tpu_custom_call" | custom-call | flops 1610000000 | tf_op jit(solution)/shard_map/entering/pallas_call | solution.py:417
  45.0 0.5 collective-permute-start.12
  45.4 0.2 collective-permute-start.13
  45.7 1.2 %collective-permute-start.14 = (bf16[64,256]{1,0:T(8,128)(2,1)S(1)}, bf16[64,256]{1,0:T(8,128)(2,1)S(1)}, u32[]{:S(2)}, u32[]{:S(2)}) collective-permute-start(bf16[64,256]{1,0:T(8,128)(2,1)S(1)} %get-tuple-element.43), channel_id=1, source_target_pairs={{0,1},{1,0},{2,3},{3,2},{4,5},{5,4},{6,7},{7,6},{8,9},{9,8},{10,11... | collective-permute-start | bytes 98312 | tf_op jit(solution)/shard_map/ppermute | solution.py:465
  46.9 1.9 %prop.1 = bf16[2,1024,256]{2,1,0:T(8,128)(2,1)S(1)} custom-call(s32[2,8]{1,0:T(2,128)S(1)} %bitcast.19, bf16[2,1024,1024]{2,1,0:T(8,128)(2,1)S(1)} %bitcast.13, bf16[1024,256]{1,0:T(8,128)(2,1)S(1)} %bitcast.17, bf16[64,256]{1,0:T(8,128)(2,1)S(1)} %get-tuple-element.40._tie.own), custom_call_target="tpu_custom_call" | custom-call | flops 1724999936 | tf_op jit(solution)/shard_map/prop/pallas_call | solution.py:218
  48.8 0.0 collective-permute-done.12.far
  48.8 0.5 %collective-permute-done.13.across = bf16[64,256]{1,0:T(8,128)(2,1)S(1)} collective-permute-done((bf16[64,256]{1,0:T(8,128)(2,1)S(1)}, bf16[64,256]{1,0:T(8,128)(2,1)S(1)}, u32[]{:S(2)}, u32[]{:S(2)}) %collective-permute-start.13) | collective-permute-done | bytes 32800 | tf_op jit(solution)/shard_map/ppermute | solution.py:469
  49.4 0.0 collective-permute-done.14.near
  49.4 1.2 %waves.1 = bf16[2,1024,128]{2,1,0:T(8,128)(2,1)} custom-call(bf16[64,256]{1,0:T(8,128)(2,1)S(1)} %get-tuple-element.40._tie.own, bf16[64,256]{1,0:T(8,128)(2,1)S(1)} %collective-permute-done.12.far, bf16[64,256]{1,0:T(8,128)(2,1)S(1)} %collective-permute-done.13.across, bf16[64,256]{1,0:T(8,128)(2,1)S(1)} %collective-permute-done.14.near, ...), custom_call_target="tpu_custom_call" | custom-call | flops 1495000064 | tf_op jit(solution)/shard_map/waves/pallas_call | solution.py:448
  (11 shorter events, 0.0 us)
Async XLA Ops:
  0.0 11.9 %copy-start.3 = (bf16[1,1024,256]{2,1,0:T(8,128)(2,1)S(1)}, bf16[1,1024,256]{2,1,0:T(8,128)(2,1)}, u32[]{:S(2)}) copy-start(bf16[1,1024,256]{2,1,0:T(8,128)(2,1)} %param.8) | copy-start | bytes 1572868
  0.0 11.9 %copy-start.4 = (s32[1,8,2]{1,2,0:T(2,128)S(1)}, s32[1,8,2]{1,2,0:T(2,128)}, u32[]{:S(2)}) copy-start(s32[1,8,2]{1,2,0:T(2,128)} %param.9) | copy-start | bytes 196
  4.6 22.4 %copy-start.2 = (bf16[1,2,1024,128]{3,2,1,0:T(8,128)(2,1)S(1)}, bf16[1,2,1024,128]{3,2,1,0:T(8,128)(2,1)}, u32[]{:S(2)}) copy-start(bf16[1,2,1024,128]{3,2,1,0:T(8,128)(2,1)} %param.7) | copy-start | bytes 1572868
  4.6 22.4 %all-to-all-start = ((bf16[16,136,128]{2,1,0:T(8,128)(2,1)}), bf16[16,136,128]{2,1,0:T(8,128)(2,1)S(1)}, u32[]{:S(2)}, u32[]{:S(2)}) async-start(bf16[16,136,128]{2,1,0:T(8,128)(2,1)} %pairs.1), calls=%async_computation | async-start | bytes 1114112 | tf_op jit(solution)/shard_map/all_to_all | solution.py:519
  11.9 2.2 %copy-start = (bf16[1,2,1024,1024]{3,2,1,0:T(8,128)(2,1)S(1)}, bf16[1,2,1024,1024]{3,2,1,0:T(8,128)(2,1)}, u32[]{:S(2)}) copy-start(bf16[1,2,1024,1024]{3,2,1,0:T(8,128)(2,1)} %param.6) | copy-start | bytes 12582916
  15.2 1.0 %copy-start.5 = (bf16[2,256,1024]{2,1,0:T(8,128)(2,1)}, bf16[2,256,1024]{2,1,0:T(8,128)(2,1)S(1)}, u32[]{:S(2)}) copy-start(bf16[2,256,1024]{2,1,0:T(8,128)(2,1)S(1)} %get-tuple-element.25.face_rows) | copy-start | bytes 3145732
  16.2 13.5 %collective-permute-start.3 = (f32[256,256]{1,0:T(8,128)S(1)}, f32[256,256]{1,0:T(8,128)S(1)}, u32[]{:S(2)}, u32[]{:S(2)}) collective-permute-start(f32[256,256]{1,0:T(8,128)S(1)} %get-tuple-element.31), channel_id=1, source_target_pairs={{0,2},{1,3},{2,0},{3,1},{4,6},{5,7},{6,4},{7,5},{8,10},{9,11},{10,... | collective-permute-start | bytes 786440 | tf_op jit(solution)/shard_map/ppermute | solution.py:469
  27.0 1.2 %copy-start.6 = (bf16[2,256,1024]{2,1,0:T(8,128)(2,1)S(1)}, bf16[2,256,1024]{2,1,0:T(8,128)(2,1)}, u32[]{:S(2)}) copy-start(bf16[2,256,1024]{2,1,0:T(8,128)(2,1)} %copy-done.5) | copy-start | bytes 3145732
  28.2 5.4 %copy-start.1 = (bf16[1,2,1024,1024]{3,2,1,0:T(8,128)(2,1)S(1)}, bf16[1,2,1024,1024]{3,2,1,0:T(8,128)(2,1)}, u32[]{:S(2)}) copy-start(bf16[1,2,1024,1024]{3,2,1,0:T(8,128)(2,1)} %param.6) | copy-start | bytes 12582916
  29.6 2.5 %collective-permute-start.5 = (f32[256,256]{1,0:T(8,128)S(1)}, f32[256,256]{1,0:T(8,128)S(1)}, u32[]{:S(2)}, u32[]{:S(2)}) collective-permute-start(f32[256,256]{1,0:T(8,128)S(1)} %after_exchange.3), channel_id=1, source_target_pairs={{0,1},{1,0},{2,3},{3,2},{4,5},{5,4},{6,7},{7,6},{8,9},{9,8},{10,11... | collective-permute-start | bytes 786440 | tf_op jit(solution)/shard_map/ppermute | solution.py:465
  29.7 2.4 %collective-permute-start.4 = (f32[256,256]{1,0:T(8,128)S(1)}, f32[256,256]{1,0:T(8,128)S(1)}, u32[]{:S(2)}, u32[]{:S(2)}) collective-permute-start(f32[256,256]{1,0:T(8,128)S(1)} %after_exchange.2.across), channel_id=1, source_target_pairs={{0,1},{1,0},{2,3},{3,2},{4,5},{5,4},{6,7},{7,6},{8,9},{9,8},{10,11... | collective-permute-start | bytes 786440 | tf_op jit(solution)/shard_map/ppermute | solution.py:465
  30.2 5.2 %collective-permute-start = (bf16[64,256]{1,0:T(8,128)(2,1)S(1)}, bf16[64,256]{1,0:T(8,128)(2,1)S(1)}, u32[]{:S(2)}, u32[]{:S(2)}) collective-permute-start(bf16[64,256]{1,0:T(8,128)(2,1)S(1)} %get-tuple-element.27), channel_id=1, source_target_pairs={{0,3},{1,2},{2,1},{3,0},{4,7},{5,6},{6,5},{7,4},{8,11},{9,10},{10,... | collective-permute-start | bytes 98312 | tf_op jit(solution)/shard_map/ppermute | solution.py:473
  31.0 4.4 %collective-permute-start.1 = (bf16[64,256]{1,0:T(8,128)(2,1)S(1)}, bf16[64,256]{1,0:T(8,128)(2,1)S(1)}, u32[]{:S(2)}, u32[]{:S(2)}) collective-permute-start(bf16[64,256]{1,0:T(8,128)(2,1)S(1)} %get-tuple-element.28), channel_id=1, source_target_pairs={{0,2},{1,3},{2,0},{3,1},{4,6},{5,7},{6,4},{7,5},{8,10},{9,11},{10,... | collective-permute-start | bytes 98312 | tf_op jit(solution)/shard_map/ppermute | solution.py:469
  31.9 3.5 %collective-permute-start.2 = (bf16[64,256]{1,0:T(8,128)(2,1)S(1)}, bf16[64,256]{1,0:T(8,128)(2,1)S(1)}, u32[]{:S(2)}, u32[]{:S(2)}) collective-permute-start(bf16[64,256]{1,0:T(8,128)(2,1)S(1)} %get-tuple-element.29), channel_id=1, source_target_pairs={{0,1},{1,0},{2,3},{3,2},{4,5},{5,4},{6,7},{7,6},{8,9},{9,8},{10,11... | collective-permute-start | bytes 98312 | tf_op jit(solution)/shard_map/ppermute | solution.py:465
  32.9 10.4 %collective-permute-start.10 = (bf16[256,256]{1,0:T(8,128)(2,1)S(1)}, bf16[256,256]{1,0:T(8,128)(2,1)S(1)}, u32[]{:S(2)}, u32[]{:S(2)}) collective-permute-start(bf16[256,256]{1,0:T(8,128)(2,1)S(1)} %get-tuple-element.36), channel_id=1, source_target_pairs={{4,8},{8,12},{5,13},{6,10},{10,14},{7,15},{20,24},{24,28},{21,29},... | collective-permute-start | bytes 393224 | tf_op jit(solution)/shard_map/ppermute | solution.py:491
  36.0 8.1 %collective-permute-start.6 = (bf16[64,256]{1,0:T(8,128)(2,1)S(1)}, bf16[64,256]{1,0:T(8,128)(2,1)S(1)}, u32[]{:S(2)}, u32[]{:S(2)}) collective-permute-start(bf16[64,256]{1,0:T(8,128)(2,1)S(1)} %get-tuple-element.35), channel_id=1, source_target_pairs={{0,12},{1,13},{2,14},{3,15},{16,28},{17,29},{18,30},{19,31}} | collective-permute-start | bytes 98312 | tf_op jit(solution)/shard_map/ppermute | solution.py:497
  40.1 4.1 %collective-permute-start.7 = (bf16[64,256]{1,0:T(8,128)(2,1)S(1)}, bf16[64,256]{1,0:T(8,128)(2,1)S(1)}, u32[]{:S(2)}, u32[]{:S(2)}) collective-permute-start(bf16[64,256]{1,0:T(8,128)(2,1)S(1)} %get-tuple-element.35), channel_id=1, source_target_pairs={{0,4},{1,5},{2,6},{3,7},{16,20},{17,21},{18,22},{19,23}} | collective-permute-start | bytes 98312 | tf_op jit(solution)/shard_map/ppermute | solution.py:497
  41.4 2.9 %collective-permute-start.8 = (bf16[64,256]{1,0:T(8,128)(2,1)S(1)}, bf16[64,256]{1,0:T(8,128)(2,1)S(1)}, u32[]{:S(2)}, u32[]{:S(2)}) collective-permute-start(bf16[64,256]{1,0:T(8,128)(2,1)S(1)} %get-tuple-element.35), channel_id=1, source_target_pairs={{0,8},{1,9},{2,10},{3,11},{4,12},{5,13},{6,14},{7,15},{16,24},{17,... | collective-permute-start | bytes 98312 | tf_op jit(solution)/shard_map/ppermute | solution.py:497
  42.7 1.6 %collective-permute-start.9 = (bf16[64,256]{1,0:T(8,128)(2,1)S(1)}, bf16[64,256]{1,0:T(8,128)(2,1)S(1)}, u32[]{:S(2)}, u32[]{:S(2)}) collective-permute-start(bf16[64,256]{1,0:T(8,128)(2,1)S(1)} %get-tuple-element.35), channel_id=1, source_target_pairs={{4,8},{5,9},{6,10},{7,11},{8,12},{9,13},{10,14},{11,15},{20,24},{2... | collective-permute-start | bytes 98312 | tf_op jit(solution)/shard_map/ppermute | solution.py:497
  43.3 0.9 %collective-permute-start.11 = (bf16[256,256]{1,0:T(8,128)(2,1)S(1)}, bf16[256,256]{1,0:T(8,128)(2,1)S(1)}, u32[]{:S(2)}, u32[]{:S(2)}) collective-permute-start(bf16[256,256]{1,0:T(8,128)(2,1)S(1)} %collective-permute-done.10.got), channel_id=1, source_target_pairs={{8,9},{9,8},{10,11},{11,10},{12,13},{13,12},{14,15},{15,14},{24,25... | collective-permute-start | bytes 393224 | tf_op jit(solution)/shard_map/ppermute | solution.py:492
  45.0 3.8 %collective-permute-start.12 = (bf16[64,256]{1,0:T(8,128)(2,1)S(1)}, bf16[64,256]{1,0:T(8,128)(2,1)S(1)}, u32[]{:S(2)}, u32[]{:S(2)}) collective-permute-start(bf16[64,256]{1,0:T(8,128)(2,1)S(1)} %get-tuple-element.41), channel_id=1, source_target_pairs={{0,3},{1,2},{2,1},{3,0},{4,7},{5,6},{6,5},{7,4},{8,11},{9,10},{10,... | collective-permute-start | bytes 98312 | tf_op jit(solution)/shard_map/ppermute | solution.py:473
  45.4 3.9 %collective-permute-start.13 = (bf16[64,256]{1,0:T(8,128)(2,1)S(1)}, bf16[64,256]{1,0:T(8,128)(2,1)S(1)}, u32[]{:S(2)}, u32[]{:S(2)}) collective-permute-start(bf16[64,256]{1,0:T(8,128)(2,1)S(1)} %get-tuple-element.42), channel_id=1, source_target_pairs={{0,2},{1,3},{2,0},{3,1},{4,6},{5,7},{6,4},{7,5},{8,10},{9,11},{10,... | collective-permute-start | bytes 98312 | tf_op jit(solution)/shard_map/ppermute | solution.py:469
  45.7 3.7 %collective-permute-start.14 = (bf16[64,256]{1,0:T(8,128)(2,1)S(1)}, bf16[64,256]{1,0:T(8,128)(2,1)S(1)}, u32[]{:S(2)}, u32[]{:S(2)}) collective-permute-start(bf16[64,256]{1,0:T(8,128)(2,1)S(1)} %get-tuple-element.43), channel_id=1, source_target_pairs={{0,1},{1,0},{2,3},{3,2},{4,5},{5,4},{6,7},{7,6},{8,9},{9,8},{10,11... | collective-permute-start | bytes 98312 | tf_op jit(solution)/shard_map/ppermute | solution.py:465

commit v27 on v25

--- a/solution.py
+++ b/solution.py
@@ -179,14 +179,15 @@
     )(owner, blocks, green, inject)
 
 
-def maps_kernel(pattern, green, coupling, own, other, face_rows, couple, maps):
+def maps_kernel(pattern, green, coupling, own, other, *refs):
+    face_rows, (couple, maps) = refs[:-2], refs[-2:]
     energies, orbitals, _ = green.shape
     face = coupling.shape[1]
     couple[...] = coupling[...]
     mask_tiles(pattern, couple)
     for e in range(energies):
         rows = green[e, orbitals - face :, :]
-        face_rows[e] = rows
+        face_rows[e][...] = rows
         maps[e] = dot(rows, couple[...])
     mine = place() // CORES
     own[...] = maps[mine]
@@ -200,7 +201,7 @@
         maps_kernel,
         "face_maps",
         [IN_SMEM, IN_VMEM, IN_VMEM],
-        [square, square, shape(green.shape[0], face, orbitals)],
+        [square, square] + [shape(face, orbitals)] * green.shape[0],
         [pltpu.VMEM(coupling.shape, BF16), pltpu.VMEM((green.shape[0], face, face), F32)],
         1.2,
     )(pattern, green, coupling)
@@ -251,8 +252,10 @@
     )(*maps)
 
 
-def source_kernel(received, inject, face_rows, source, own, far, across, near, quarters, total, heads, targets, sem):
+def source_kernel(received, inject, *refs):
     energies, orbitals, columns = inject.shape
+    face_rows = refs[:energies]
+    source, own, far, across, near, quarters, total, heads, targets, sem = refs[energies:]
     sections = received.shape[0]
     wide_rows = quarters.shape[1]
     rows = CAP * energies * BLK
@@ -280,7 +283,7 @@
     split = GROUP // energies
     for e in range(energies):
         source[e] = total[e].astype(BF16)
-        tall = dot(face_rows[e], source[e])
+        tall = dot(face_rows[e][...], source[e])
         wide = tall.T
         for h in range(split):
             quarters[e * split + h] = wide[h * wide_rows : (h + 1) * wide_rows]
@@ -305,13 +308,13 @@
 
 
 def placed_source(received, inject, face_rows):
-    face = face_rows.shape[1]
+    face = face_rows[0].shape[0]
     energies, orbitals, columns = inject.shape
     sections = received.shape[0]
     return call(
         source_kernel,
         "source_and_face",
-        [IN_VMEM, IN_VMEM, IN_VMEM],
+        [IN_VMEM] * (2 + energies),
         [shape(*inject.shape)] + [shape(columns * energies // GROUP, face)] * GROUP,
         [
             pltpu.VMEM((GROUP, columns * energies // GROUP, face), F32),
@@ -321,7 +324,7 @@
             pltpu.SemaphoreType.DMA,
         ],
         1.4,
-    )(received, inject, face_rows)
+    )(received, inject, *face_rows)
 
 
 def collect(refs, held):
@@ -518,7 +521,7 @@
     outgoing = outgoing_pairs(owner[:, 0], pair_blocks.T, green, inject, sections)
     received = lax.all_to_all(outgoing, "sec", split_axis=0, concat_axis=0, tiled=True)
 
-    own_map, other_map, face_rows = face_maps(tiles, green, coupling)
+    own_map, other_map, *face_rows = face_maps(tiles, green, coupling)
     across = to_across(other_map, sections)
     near = to_near(own_map, sections)
 

time: 50.8 us -> 50.4 us (level)
  transfers between devices with their start and end apart: 16 -> 16, of which waited for: 3 -> 3; matrix products, arithmetic and copies ran while one was open for 0% -> 0% of each run, Pallas kernels for 15% -> 16%
where the time goes in v27:
time: 50.4 us; the launch traced here: 50 us
  starting transfers between devices  22 us (44%)
  Pallas kernels  14 us (28%)
  waiting for transfers between devices  9.65 us (19%)
  local copies, waits for them, and re-layouts  4.03 us (8%)
    all_to_all x1, waiting for transfers between devices, per_device(): lax.all_to_all(outgoing, 'sec', split_axis=0, concat_axis=0, tiled=True)  9.02 us
    all_to_all x1, starting transfers between devices, per_device(): lax.all_to_all(outgoing, 'sec', split_axis=0, concat_axis=0, tiled=True)  7.53 us
    ppermute x4, starting transfers between devices, between(): return lax.ppermute(item, 'sec', pairs)  7.05 us
    pallas_call x1, Pallas kernels, outgoing_pairs(): call(pairs_kernel, 'pairs', [IN_HBM] * 4, shape(sections, CAP * energies...  4.38 us
    unnamed x14, local copies, waits for them, and re-layouts  4.03 us
    ppermute x3, starting transfers between devices, to_across(): lax.ppermute(item, 'sec', [(s, s // GROUP * GROUP + (s % GROUP + CORES) %...  3.64 us
    pallas_call x2, Pallas kernels, image_and_maps(): call(functools.partial(work_kernel, not held), 'image_and_maps', [IN_VMEM...  1.91 us
    pallas_call x1, Pallas kernels, propagator(): call(prop_kernel, 'prop', [IN_SMEM, IN_VMEM, IN_VMEM, IN_PLACE], shape(en...  1.9 us
  transfers between devices with their start and end apart: 16, of which 3 were waited for; matrix products, arithmetic and copies ran while one was open for 0% of the time, Pallas kernels for 16%

profile of v27, /device:TPU:0, one launch (start us, length us, event | category | flops | bytes accessed | tf_op | source)
XLA Modules:
  0.0 50.0 jit_solution(14319383219633995196)
XLA Ops:
  0.0 4.4 %pairs.1 = bf16[16,136,128]{2,1,0:T(8,128)(2,1)} custom-call(s32[16]{0:T(128)} %bitcast.21, s32[2,16]{1,0:T(2,128)} %bitcast.20, bf16[2,1024,1024]{2,1,0:T(8,128)(2,1)} %bitcast.9, bf16[2,1024,128]{2,1,0:T(8,128)(2,1)} %bitcast.14), custom_call_target="tpu_custom_call" | custom-call | flops 4600000000 | tf_op jit(solution)/shard_map/pairs/pallas_call | solution.py:161
  4.4 0.0 copy-start.2
  4.4 7.5 %all-to-all-start = ((bf16[16,136,128]{2,1,0:T(8,128)(2,1)}), bf16[16,136,128]{2,1,0:T(8,128)(2,1)S(1)}, u32[]{:S(2)}, u32[]{:S(2)}) async-start(bf16[16,136,128]{2,1,0:T(8,128)(2,1)} %pairs.1), calls=%async_computation | async-start | bytes 1114112 | tf_op jit(solution)/shard_map/all_to_all | solution.py:522
  12.0 0.0 copy-start
  12.0 2.2 %copy-done = bf16[1,2,1024,1024]{3,2,1,0:T(8,128)(2,1)S(1)} copy-done((bf16[1,2,1024,1024]{3,2,1,0:T(8,128)(2,1)S(1)}, bf16[1,2,1024,1024]{3,2,1,0:T(8,128)(2,1)}, u32[]{:S(2)}) %copy-start) | copy-done | bytes 4194328
  14.2 1.1 %face_maps.1 = (f32[256,256]{1,0:T(8,128)S(1)}, f32[256,256]{1,0:T(8,128)S(1)}, bf16[256,1024]{1,0:T(8,128)(2,1)S(1)}, bf16[256,1024]{1,0:T(8,128)(2,1)S(1)}) custom-call(s32[2,8]{1,0:T(2,128)S(1)} %bitcast.18, bf16[2,1024,1024]{2,1,0:T(8,128)(2,1)S(1)} %bitcast.10, bf16[1024,256]{1,0:T(8,128)(2,1)S(1)} %bitcast.16), custom_call_target="tpu_custom_call" | custom-call | flops 1380000000 | tf_op jit(solution)/shard_map/face_maps/pallas_call | solution.py:200
  15.3 0.0 copy-start.5
  15.3 0.8 %copy-done.5 = bf16[256,1024]{1,0:T(8,128)(2,1)} copy-done((bf16[256,1024]{1,0:T(8,128)(2,1)}, bf16[256,1024]{1,0:T(8,128)(2,1)S(1)}, u32[]{:S(2)}) %copy-start.5) | copy-done | bytes 524312
  16.1 1.9 %collective-permute-start.3 = (f32[256,256]{1,0:T(8,128)S(1)}, f32[256,256]{1,0:T(8,128)S(1)}, u32[]{:S(2)}, u32[]{:S(2)}) collective-permute-start(f32[256,256]{1,0:T(8,128)S(1)} %get-tuple-element.33), channel_id=1, source_target_pairs={{0,2},{1,3},{2,0},{3,1},{4,6},{5,7},{6,4},{7,5},{8,10},{9,11},{10,... | collective-permute-start | bytes 786440 | tf_op jit(solution)/shard_map/ppermute | solution.py:472
  18.0 0.0 collective-permute-start.5
  18.0 9.0 %all-to-all-done.received = bf16[16,136,128]{2,1,0:T(8,128)(2,1)S(1)} async-done(((bf16[16,136,128]{2,1,0:T(8,128)(2,1)}), bf16[16,136,128]{2,1,0:T(8,128)(2,1)S(1)}, u32[]{:S(2)}, u32[]{:S(2)}) %all-to-all-start) | async-done | bytes 557088 | tf_op jit(solution)/shard_map/all_to_all | solution.py:522
  27.0 1.0 %copy-done.6 = bf16[256,1024]{1,0:T(8,128)(2,1)S(1)} copy-done((bf16[256,1024]{1,0:T(8,128)(2,1)S(1)}, bf16[256,1024]{1,0:T(8,128)(2,1)}, u32[]{:S(2)}) %copy-start.6) | copy-done | bytes 524312
  28.1 1.4 %source_and_face.1 = (bf16[2,1024,128]{2,1,0:T(8,128)(2,1)S(1)}, bf16[64,256]{1,0:T(8,128)(2,1)S(1)}, bf16[64,256]{1,0:T(8,128)(2,1)S(1)}, bf16[64,256]{1,0:T(8,128)(2,1)S(1)}, bf16[64,256]{1,0:T(8,128)(2,1)S(1)}) custom-call(bf16[16,136,128]{2,1,0:T(8,128)(2,1)S(1)} %all-to-all-done.received, bf16[2,1024,128]{2,1,0:T(8,128)(2,1)S(1)} %bitcast.15, ...), custom_call_target="tpu_custom_call" | custom-call | flops 1610000000 | tf_op jit(solution)/shard_map/source_and_face/pallas_call | solution.py:314
  29.5 0.0 collective-permute-done.3._map
  29.5 0.1 collective-permute-start.4
  29.6 0.9 %collective-permute-start = (bf16[64,256]{1,0:T(8,128)(2,1)S(1)}, bf16[64,256]{1,0:T(8,128)(2,1)S(1)}, u32[]{:S(2)}, u32[]{:S(2)}) collective-permute-start(bf16[64,256]{1,0:T(8,128)(2,1)S(1)} %get-tuple-element.29), channel_id=1, source_target_pairs={{0,3},{1,2},{2,1},{3,0},{4,7},{5,6},{6,5},{7,4},{8,11},{9,10},{10,... | collective-permute-start | bytes 98312 | tf_op jit(solution)/shard_map/ppermute | solution.py:476
  30.5 1.3 %collective-permute-start.1 = (bf16[64,256]{1,0:T(8,128)(2,1)S(1)}, bf16[64,256]{1,0:T(8,128)(2,1)S(1)}, u32[]{:S(2)}, u32[]{:S(2)}) collective-permute-start(bf16[64,256]{1,0:T(8,128)(2,1)S(1)} %get-tuple-element.30), channel_id=1, source_target_pairs={{0,2},{1,3},{2,0},{3,1},{4,6},{5,7},{6,4},{7,5},{8,10},{9,11},{10,... | collective-permute-start | bytes 98312 | tf_op jit(solution)/shard_map/ppermute | solution.py:472
  31.7 0.0 collective-permute-start.2
  31.7 0.0 collective-permute-done.5.near
  31.7 0.0 collective-permute-done.4.far
  31.7 0.8 %chain_maps.1 = (bf16[256,256]{1,0:T(8,128)(2,1)S(1)}, bf16[2,4,256,256]{3,2,1,0:T(8,128)(2,1)S(1)}) custom-call(f32[256,256]{1,0:T(8,128)S(1)} %get-tuple-element.32.own, f32[256,256]{1,0:T(8,128)S(1)} %collective-permute-done.4.far, f32[256,256]{1,0:T(8,128)S(1)} %after_exchange.1.across, f32[256,256]{1,0:T(8,128)S(1)} %collective-permute-done.5.near), custom_call_target="tpu_custom_call" | custom-call | flops 1035000000 | tf_op jit(solution)/shard_map/chain_maps/pallas_call | solution.py:245
  32.6 0.7 %collective-permute-start.10 = (bf16[256,256]{1,0:T(8,128)(2,1)S(1)}, bf16[256,256]{1,0:T(8,128)(2,1)S(1)}, u32[]{:S(2)}, u32[]{:S(2)}) collective-permute-start(bf16[256,256]{1,0:T(8,128)(2,1)S(1)} %get-tuple-element.38), channel_id=1, source_target_pairs={{4,8},{8,12},{5,13},{6,10},{10,14},{7,15},{20,24},{24,28},{21,29},... | collective-permute-start | bytes 393224 | tf_op jit(solution)/shard_map/ppermute | solution.py:494
  33.3 1.8 %image_and_maps.2 = (f32[2,1024,128]{2,1,0:T(8,128)S(1)}, bf16[2,2,256,256]{3,2,1,0:T(8,128)(2,1)S(1)}) custom-call(bf16[2,1024,1024]{2,1,0:T(8,128)(2,1)S(1)} %bitcast.11, bf16[2,1024,128]{2,1,0:T(8,128)(2,1)S(1)} %get-tuple-element.35.refs_1_, bf16[2,4,256,256]{3,2,1,0:T(8,128)(2,1)S(1)} %get-tuple-element.34.refs_2_.parts), custom_call_target="tpu_custom_call" | custom-call | flops 2300000000 | tf_op jit(solution)/shard_map/image_and_maps/pallas_call | solution.py:380
  35.0 0.0 collective-permute-done.far
  35.1 0.0 collective-permute-done.1.across
  35.1 0.0 collective-permute-done.2.near
  35.1 0.6 %plane_total.1 = (bf16[64,256]{1,0:T(8,128)(2,1)S(1)}, f32[3,64,256]{2,1,0:T(8,128)S(1)}) custom-call(bf16[64,256]{1,0:T(8,128)(2,1)S(1)} %get-tuple-element.28._packets.own, bf16[64,256]{1,0:T(8,128)(2,1)S(1)} %collective-permute-done.far, bf16[64,256]{1,0:T(8,128)(2,1)S(1)} %collective-permute-done.1.across, ...), custom_call_target="tpu_custom_call" | custom-call | flops 3449999872 | tf_op jit(solution)/shard_map/plane_total/pallas_call | solution.py:346
  35.7 3.8 %collective-permute-start.6 = (bf16[64,256]{1,0:T(8,128)(2,1)S(1)}, bf16[64,256]{1,0:T(8,128)(2,1)S(1)}, u32[]{:S(2)}, u32[]{:S(2)}) collective-permute-start(bf16[64,256]{1,0:T(8,128)(2,1)S(1)} %get-tuple-element.37), channel_id=1, source_target_pairs={{0,12},{1,13},{2,14},{3,15},{16,28},{17,29},{18,30},{19,31}} | collective-permute-start | bytes 98312 | tf_op jit(solution)/shard_map/ppermute | solution.py:500
  39.5 1.3 %collective-permute-start.7 = (bf16[64,256]{1,0:T(8,128)(2,1)S(1)}, bf16[64,256]{1,0:T(8,128)(2,1)S(1)}, u32[]{:S(2)}, u32[]{:S(2)}) collective-permute-start(bf16[64,256]{1,0:T(8,128)(2,1)S(1)} %get-tuple-element.37), channel_id=1, source_target_pairs={{0,4},{1,5},{2,6},{3,7},{16,20},{17,21},{18,22},{19,23}} | collective-permute-start | bytes 98312 | tf_op jit(solution)/shard_map/ppermute | solution.py:500
  40.8 1.3 %collective-permute-start.8 = (bf16[64,256]{1,0:T(8,128)(2,1)S(1)}, bf16[64,256]{1,0:T(8,128)(2,1)S(1)}, u32[]{:S(2)}, u32[]{:S(2)}) collective-permute-start(bf16[64,256]{1,0:T(8,128)(2,1)S(1)} %get-tuple-element.37), channel_id=1, source_target_pairs={{0,8},{1,9},{2,10},{3,11},{4,12},{5,13},{6,14},{7,15},{16,24},{17,... | collective-permute-start | bytes 98312 | tf_op jit(solution)/shard_map/ppermute | solution.py:500
  42.1 0.7 %collective-permute-start.9 = (bf16[64,256]{1,0:T(8,128)(2,1)S(1)}, bf16[64,256]{1,0:T(8,128)(2,1)S(1)}, u32[]{:S(2)}, u32[]{:S(2)}) collective-permute-start(bf16[64,256]{1,0:T(8,128)(2,1)S(1)} %get-tuple-element.37), channel_id=1, source_target_pairs={{4,8},{5,9},{6,10},{7,11},{8,12},{9,13},{10,14},{11,15},{20,24},{2... | collective-permute-start | bytes 98312 | tf_op jit(solution)/shard_map/ppermute | solution.py:500
  42.8 0.0 collective-permute-done.10.got
  42.8 0.7 %collective-permute-start.11 = (bf16[256,256]{1,0:T(8,128)(2,1)S(1)}, bf16[256,256]{1,0:T(8,128)(2,1)S(1)}, u32[]{:S(2)}, u32[]{:S(2)}) collective-permute-start(bf16[256,256]{1,0:T(8,128)(2,1)S(1)} %collective-permute-done.10.got), channel_id=1, source_target_pairs={{8,9},{9,8},{10,11},{11,10},{12,13},{13,12},{14,15},{15,14},{24,25... | collective-permute-start | bytes 393224 | tf_op jit(solution)/shard_map/ppermute | solution.py:495
  43.5 0.1 image_and_maps.3
  43.6 0.0 collective-permute-done.6.third
  43.6 0.0 collective-permute-done.7.near_one
  43.6 0.1 collective-permute-done.8.second
  43.7 0.0 collective-permute-done.9.far_one
  43.7 0.0 collective-permute-done.11.other
  43.7 0.7 %entering.1 = (bf16[64,256]{1,0:T(8,128)(2,1)S(1)}, bf16[64,256]{1,0:T(8,128)(2,1)S(1)}, bf16[64,256]{1,0:T(8,128)(2,1)S(1)}, bf16[64,256]{1,0:T(8,128)(2,1)S(1)}) custom-call(bf16[64,256]{1,0:T(8,128)(2,1)S(1)} %collective-permute-done.6.third, bf16[64,256]{1,0:T(8,128)(2,1)S(1)} %collective-permute-done.7.near_one, ...), custom_call_target="tpu_custom_call" | custom-call | flops 1610000000 | tf_op jit(solution)/shard_map/entering/pallas_call | solution.py:420
  44.4 0.5 collective-permute-start.12
  44.9 0.5 collective-permute-start.13
  45.3 1.0 %collective-permute-start.14 = (bf16[64,256]{1,0:T(8,128)(2,1)S(1)}, bf16[64,256]{1,0:T(8,128)(2,1)S(1)}, u32[]{:S(2)}, u32[]{:S(2)}) collective-permute-start(bf16[64,256]{1,0:T(8,128)(2,1)S(1)} %get-tuple-element.45), channel_id=1, source_target_pairs={{0,1},{1,0},{2,3},{3,2},{4,5},{5,4},{6,7},{7,6},{8,9},{9,8},{10,11... | collective-permute-start | bytes 98312 | tf_op jit(solution)/shard_map/ppermute | solution.py:468
  46.3 1.9 %prop.1 = bf16[2,1024,256]{2,1,0:T(8,128)(2,1)S(1)} custom-call(s32[2,8]{1,0:T(2,128)S(1)} %bitcast.19, bf16[2,1024,1024]{2,1,0:T(8,128)(2,1)S(1)} %bitcast.13, bf16[1024,256]{1,0:T(8,128)(2,1)S(1)} %bitcast.17, bf16[64,256]{1,0:T(8,128)(2,1)S(1)} %get-tuple-element.42._tie.own), custom_call_target="tpu_custom_call" | custom-call | flops 1724999936 | tf_op jit(solution)/shard_map/prop/pallas_call | solution.py:219
  48.2 0.0 collective-permute-done.12.far
  48.3 0.5 %collective-permute-done.13.across = bf16[64,256]{1,0:T(8,128)(2,1)S(1)} collective-permute-done((bf16[64,256]{1,0:T(8,128)(2,1)S(1)}, bf16[64,256]{1,0:T(8,128)(2,1)S(1)}, u32[]{:S(2)}, u32[]{:S(2)}) %collective-permute-start.13) | collective-permute-done | bytes 32800 | tf_op jit(solution)/shard_map/ppermute | solution.py:472
  48.8 0.0 collective-permute-done.14.near
  48.8 1.2 %waves.1 = bf16[2,1024,128]{2,1,0:T(8,128)(2,1)} custom-call(bf16[64,256]{1,0:T(8,128)(2,1)S(1)} %get-tuple-element.42._tie.own, bf16[64,256]{1,0:T(8,128)(2,1)S(1)} %collective-permute-done.12.far, bf16[64,256]{1,0:T(8,128)(2,1)S(1)} %collective-permute-done.13.across, bf16[64,256]{1,0:T(8,128)(2,1)S(1)} %collective-permute-done.14.near, ...), custom_call_target="tpu_custom_call" | custom-call | flops 1495000064 | tf_op jit(solution)/shard_map/waves/pallas_call | solution.py:451
  (9 shorter events, 0.0 us)
Async XLA Ops:
  0.0 11.9 %copy-start.3 = (bf16[1,1024,256]{2,1,0:T(8,128)(2,1)S(1)}, bf16[1,1024,256]{2,1,0:T(8,128)(2,1)}, u32[]{:S(2)}) copy-start(bf16[1,1024,256]{2,1,0:T(8,128)(2,1)} %param.8) | copy-start | bytes 1572868
  0.0 11.9 %copy-start.4 = (s32[1,8,2]{1,2,0:T(2,128)S(1)}, s32[1,8,2]{1,2,0:T(2,128)}, u32[]{:S(2)}) copy-start(s32[1,8,2]{1,2,0:T(2,128)} %param.9) | copy-start | bytes 196
  4.4 22.6 %copy-start.2 = (bf16[1,2,1024,128]{3,2,1,0:T(8,128)(2,1)S(1)}, bf16[1,2,1024,128]{3,2,1,0:T(8,128)(2,1)}, u32[]{:S(2)}) copy-start(bf16[1,2,1024,128]{3,2,1,0:T(8,128)(2,1)} %param.7) | copy-start | bytes 1572868
  4.4 22.6 %all-to-all-start = ((bf16[16,136,128]{2,1,0:T(8,128)(2,1)}), bf16[16,136,128]{2,1,0:T(8,128)(2,1)S(1)}, u32[]{:S(2)}, u32[]{:S(2)}) async-start(bf16[16,136,128]{2,1,0:T(8,128)(2,1)} %pairs.1), calls=%async_computation | async-start | bytes 1114112 | tf_op jit(solution)/shard_map/all_to_all | solution.py:522
  12.0 2.2 %copy-start = (bf16[1,2,1024,1024]{3,2,1,0:T(8,128)(2,1)S(1)}, bf16[1,2,1024,1024]{3,2,1,0:T(8,128)(2,1)}, u32[]{:S(2)}) copy-start(bf16[1,2,1024,1024]{3,2,1,0:T(8,128)(2,1)} %param.6) | copy-start | bytes 12582916
  15.3 0.8 %copy-start.5 = (bf16[256,1024]{1,0:T(8,128)(2,1)}, bf16[256,1024]{1,0:T(8,128)(2,1)S(1)}, u32[]{:S(2)}) copy-start(bf16[256,1024]{1,0:T(8,128)(2,1)S(1)} %get-tuple-element.27.refs_1_) | copy-start | bytes 1572868
  16.1 13.4 %collective-permute-start.3 = (f32[256,256]{1,0:T(8,128)S(1)}, f32[256,256]{1,0:T(8,128)S(1)}, u32[]{:S(2)}, u32[]{:S(2)}) collective-permute-start(f32[256,256]{1,0:T(8,128)S(1)} %get-tuple-element.33), channel_id=1, source_target_pairs={{0,2},{1,3},{2,0},{3,1},{4,6},{5,7},{6,4},{7,5},{8,10},{9,11},{10,... | collective-permute-start | bytes 786440 | tf_op jit(solution)/shard_map/ppermute | solution.py:472
  18.0 13.7 %collective-permute-start.5 = (f32[256,256]{1,0:T(8,128)S(1)}, f32[256,256]{1,0:T(8,128)S(1)}, u32[]{:S(2)}, u32[]{:S(2)}) collective-permute-start(f32[256,256]{1,0:T(8,128)S(1)} %get-tuple-element.32.own), channel_id=1, source_target_pairs={{0,1},{1,0},{2,3},{3,2},{4,5},{5,4},{6,7},{7,6},{8,9},{9,8},{10,11... | collective-permute-start | bytes 786440 | tf_op jit(solution)/shard_map/ppermute | solution.py:468
  27.0 1.0 %copy-start.6 = (bf16[256,1024]{1,0:T(8,128)(2,1)S(1)}, bf16[256,1024]{1,0:T(8,128)(2,1)}, u32[]{:S(2)}) copy-start(bf16[256,1024]{1,0:T(8,128)(2,1)} %copy-done.5) | copy-start | bytes 1572868
  28.1 5.2 %copy-start.1 = (bf16[1,2,1024,1024]{3,2,1,0:T(8,128)(2,1)S(1)}, bf16[1,2,1024,1024]{3,2,1,0:T(8,128)(2,1)}, u32[]{:S(2)}) copy-start(bf16[1,2,1024,1024]{3,2,1,0:T(8,128)(2,1)} %param.6) | copy-start | bytes 12582916
  29.5 2.2 %collective-permute-start.4 = (f32[256,256]{1,0:T(8,128)S(1)}, f32[256,256]{1,0:T(8,128)S(1)}, u32[]{:S(2)}, u32[]{:S(2)}) collective-permute-start(f32[256,256]{1,0:T(8,128)S(1)} %after_exchange.1.across), channel_id=1, source_target_pairs={{0,1},{1,0},{2,3},{3,2},{4,5},{5,4},{6,7},{7,6},{8,9},{9,8},{10,11... | collective-permute-start | bytes 786440 | tf_op jit(solution)/shard_map/ppermute | solution.py:468
  29.6 5.5 %collective-permute-start = (bf16[64,256]{1,0:T(8,128)(2,1)S(1)}, bf16[64,256]{1,0:T(8,128)(2,1)S(1)}, u32[]{:S(2)}, u32[]{:S(2)}) collective-permute-start(bf16[64,256]{1,0:T(8,128)(2,1)S(1)} %get-tuple-element.29), channel_id=1, source_target_pairs={{0,3},{1,2},{2,1},{3,0},{4,7},{5,6},{6,5},{7,4},{8,11},{9,10},{10,... | collective-permute-start | bytes 98312 | tf_op jit(solution)/shard_map/ppermute | solution.py:476
  30.5 4.6 %collective-permute-start.1 = (bf16[64,256]{1,0:T(8,128)(2,1)S(1)}, bf16[64,256]{1,0:T(8,128)(2,1)S(1)}, u32[]{:S(2)}, u32[]{:S(2)}) collective-permute-start(bf16[64,256]{1,0:T(8,128)(2,1)S(1)} %get-tuple-element.30), channel_id=1, source_target_pairs={{0,2},{1,3},{2,0},{3,1},{4,6},{5,7},{6,4},{7,5},{8,10},{9,11},{10,... | collective-permute-start | bytes 98312 | tf_op jit(solution)/shard_map/ppermute | solution.py:472
  31.7 3.4 %collective-permute-start.2 = (bf16[64,256]{1,0:T(8,128)(2,1)S(1)}, bf16[64,256]{1,0:T(8,128)(2,1)S(1)}, u32[]{:S(2)}, u32[]{:S(2)}) collective-permute-start(bf16[64,256]{1,0:T(8,128)(2,1)S(1)} %get-tuple-element.31), channel_id=1, source_target_pairs={{0,1},{1,0},{2,3},{3,2},{4,5},{5,4},{6,7},{7,6},{8,9},{9,8},{10,11... | collective-permute-start | bytes 98312 | tf_op jit(solution)/shard_map/ppermute | solution.py:468
  32.6 10.2 %collective-permute-start.10 = (bf16[256,256]{1,0:T(8,128)(2,1)S(1)}, bf16[256,256]{1,0:T(8,128)(2,1)S(1)}, u32[]{:S(2)}, u32[]{:S(2)}) collective-permute-start(bf16[256,256]{1,0:T(8,128)(2,1)S(1)} %get-tuple-element.38), channel_id=1, source_target_pairs={{4,8},{8,12},{5,13},{6,10},{10,14},{7,15},{20,24},{24,28},{21,29},... | collective-permute-start | bytes 393224 | tf_op jit(solution)/shard_map/ppermute | solution.py:494
  35.7 7.9 %collective-permute-start.6 = (bf16[64,256]{1,0:T(8,128)(2,1)S(1)}, bf16[64,256]{1,0:T(8,128)(2,1)S(1)}, u32[]{:S(2)}, u32[]{:S(2)}) collective-permute-start(bf16[64,256]{1,0:T(8,128)(2,1)S(1)} %get-tuple-element.37), channel_id=1, source_target_pairs={{0,12},{1,13},{2,14},{3,15},{16,28},{17,29},{18,30},{19,31}} | collective-permute-start | bytes 98312 | tf_op jit(solution)/shard_map/ppermute | solution.py:500
  39.5 4.1 %collective-permute-start.7 = (bf16[64,256]{1,0:T(8,128)(2,1)S(1)}, bf16[64,256]{1,0:T(8,128)(2,1)S(1)}, u32[]{:S(2)}, u32[]{:S(2)}) collective-permute-start(bf16[64,256]{1,0:T(8,128)(2,1)S(1)} %get-tuple-element.37), channel_id=1, source_target_pairs={{0,4},{1,5},{2,6},{3,7},{16,20},{17,21},{18,22},{19,23}} | collective-permute-start | bytes 98312 | tf_op jit(solution)/shard_map/ppermute | solution.py:500
  40.8 2.9 %collective-permute-start.8 = (bf16[64,256]{1,0:T(8,128)(2,1)S(1)}, bf16[64,256]{1,0:T(8,128)(2,1)S(1)}, u32[]{:S(2)}, u32[]{:S(2)}) collective-permute-start(bf16[64,256]{1,0:T(8,128)(2,1)S(1)} %get-tuple-element.37), channel_id=1, source_target_pairs={{0,8},{1,9},{2,10},{3,11},{4,12},{5,13},{6,14},{7,15},{16,24},{17,... | collective-permute-start | bytes 98312 | tf_op jit(solution)/shard_map/ppermute | solution.py:500
  42.1 1.6 %collective-permute-start.9 = (bf16[64,256]{1,0:T(8,128)(2,1)S(1)}, bf16[64,256]{1,0:T(8,128)(2,1)S(1)}, u32[]{:S(2)}, u32[]{:S(2)}) collective-permute-start(bf16[64,256]{1,0:T(8,128)(2,1)S(1)} %get-tuple-element.37), channel_id=1, source_target_pairs={{4,8},{5,9},{6,10},{7,11},{8,12},{9,13},{10,14},{11,15},{20,24},{2... | collective-permute-start | bytes 98312 | tf_op jit(solution)/shard_map/ppermute | solution.py:500
  42.8 0.9 %collective-permute-start.11 = (bf16[256,256]{1,0:T(8,128)(2,1)S(1)}, bf16[256,256]{1,0:T(8,128)(2,1)S(1)}, u32[]{:S(2)}, u32[]{:S(2)}) collective-permute-start(bf16[256,256]{1,0:T(8,128)(2,1)S(1)} %collective-permute-done.10.got), channel_id=1, source_target_pairs={{8,9},{9,8},{10,11},{11,10},{12,13},{13,12},{14,15},{15,14},{24,25... | collective-permute-start | bytes 393224 | tf_op jit(solution)/shard_map/ppermute | solution.py:495
  44.4 3.8 %collective-permute-start.12 = (bf16[64,256]{1,0:T(8,128)(2,1)S(1)}, bf16[64,256]{1,0:T(8,128)(2,1)S(1)}, u32[]{:S(2)}, u32[]{:S(2)}) collective-permute-start(bf16[64,256]{1,0:T(8,128)(2,1)S(1)} %get-tuple-element.43), channel_id=1, source_target_pairs={{0,3},{1,2},{2,1},{3,0},{4,7},{5,6},{6,5},{7,4},{8,11},{9,10},{10,... | collective-permute-start | bytes 98312 | tf_op jit(solution)/shard_map/ppermute | solution.py:476
  44.9 3.9 %collective-permute-start.13 = (bf16[64,256]{1,0:T(8,128)(2,1)S(1)}, bf16[64,256]{1,0:T(8,128)(2,1)S(1)}, u32[]{:S(2)}, u32[]{:S(2)}) collective-permute-start(bf16[64,256]{1,0:T(8,128)(2,1)S(1)} %get-tuple-element.44), channel_id=1, source_target_pairs={{0,2},{1,3},{2,0},{3,1},{4,6},{5,7},{6,4},{7,5},{8,10},{9,11},{10,... | collective-permute-start | bytes 98312 | tf_op jit(solution)/shard_map/ppermute | solution.py:472
  45.3 3.5 %collective-permute-start.14 = (bf16[64,256]{1,0:T(8,128)(2,1)S(1)}, bf16[64,256]{1,0:T(8,128)(2,1)S(1)}, u32[]{:S(2)}, u32[]{:S(2)}) collective-permute-start(bf16[64,256]{1,0:T(8,128)(2,1)S(1)} %get-tuple-element.45), channel_id=1, source_target_pairs={{0,1},{1,0},{2,3},{3,2},{4,5},{5,4},{6,7},{7,6},{8,9},{9,8},{10,11... | collective-permute-start | bytes 98312 | tf_op jit(solution)/shard_map/ppermute | solution.py:468

commit v28 on v27

--- a/solution.py
+++ b/solution.py
@@ -523,12 +523,11 @@
 
     own_map, other_map, *face_rows = face_maps(tiles, green, coupling)
     across = to_across(other_map, sections)
-    near = to_near(own_map, sections)
 
     source, *quarters = placed_source(received, inject, face_rows)
     shifts = exchange(*quarters, sections)
     across = handed_on(across, quarters[0])
-    far = to_near(across, sections)
+    near, far = to_near(handed_on(own_map, quarters[0]), sections), to_near(across, sections)
     four = sections // GROUP == 4
     total_map, parts = chain([own_map, far, across, near], BF16 if four else F32)
     early = image_and_maps(green, source, parts)

time: 50.4 us -> 50.9 us (level)
    ppermute x4, starting transfers between devices: 1.09 us -> 1.94 us  [to_near(): return lax.ppermute(item, 'sec', [(s, s ^ 1) for s in range(sections)])]
    ppermute x3, starting transfers between devices: 3.64 us -> 3.02 us  [to_across(): lax.ppermute(item, 'sec', [(s, s // GROUP * GROUP + (s % GROUP + CORES) %...]
    unnamed x14 -> x15, local copies, waits for them, and re-layouts: 4.03 us -> 4.05 us
  transfers between devices with their start and end apart: 16 -> 16, of which waited for: 3 -> 3; matrix products, arithmetic and copies ran while one was open for 0% -> 0% of each run, Pallas kernels for 16% -> 15%
where the time goes in v28:
time: 50.9 us; the launch traced here: 50.5 us
  starting transfers between devices  22.4 us (44%)
  Pallas kernels  14.2 us (28%)
  waiting for transfers between devices  9.58 us (19%)
  local copies, waits for them, and re-layouts  4.05 us (8%)
    all_to_all x1, waiting for transfers between devices, per_device(): lax.all_to_all(outgoing, 'sec', split_axis=0, concat_axis=0, tiled=True)  8.97 us
    all_to_all x1, starting transfers between devices, per_device(): lax.all_to_all(outgoing, 'sec', split_axis=0, concat_axis=0, tiled=True)  7.5 us
    ppermute x4, starting transfers between devices, between(): return lax.ppermute(item, 'sec', pairs)  7.27 us
    pallas_call x1, Pallas kernels, outgoing_pairs(): call(pairs_kernel, 'pairs', [IN_HBM] * 4, shape(sections, CAP * energies...  4.47 us
    unnamed x15, local copies, waits for them, and re-layouts  4.05 us
    ppermute x3, starting transfers between devices, to_across(): lax.ppermute(item, 'sec', [(s, s // GROUP * GROUP + (s % GROUP + CORES) %...  3.02 us
    ppermute x4, starting transfers between devices, to_near(): return lax.ppermute(item, 'sec', [(s, s ^ 1) for s in range(sections)])  1.94 us
    pallas_call x1, Pallas kernels, propagator(): call(prop_kernel, 'prop', [IN_SMEM, IN_VMEM, IN_VMEM, IN_PLACE], shape(en...  1.93 us
  transfers between devices with their start and end apart: 16, of which 3 were waited for; matrix products, arithmetic and copies ran while one was open for 0% of the time, Pallas kernels for 15%

profile of v28, /device:TPU:0, one launch (start us, length us, event | category | flops | bytes accessed | tf_op | source)
XLA Modules:
  0.0 50.5 jit_solution(6439078665684339771)
XLA Ops:
  0.0 4.5 %pairs.1 = bf16[16,136,128]{2,1,0:T(8,128)(2,1)} custom-call(s32[16]{0:T(128)} %bitcast.21, s32[2,16]{1,0:T(2,128)} %bitcast.20, bf16[2,1024,1024]{2,1,0:T(8,128)(2,1)} %bitcast.9, bf16[2,1024,128]{2,1,0:T(8,128)(2,1)} %bitcast.14), custom_call_target="tpu_custom_call" | custom-call | flops 4600000000 | tf_op jit(solution)/shard_map/pairs/pallas_call | solution.py:161
  4.5 0.0 copy-start.2
  4.5 7.5 %all-to-all-start = ((bf16[16,136,128]{2,1,0:T(8,128)(2,1)}), bf16[16,136,128]{2,1,0:T(8,128)(2,1)S(1)}, u32[]{:S(2)}, u32[]{:S(2)}) async-start(bf16[16,136,128]{2,1,0:T(8,128)(2,1)} %pairs.1), calls=%async_computation | async-start | bytes 1114112 | tf_op jit(solution)/shard_map/all_to_all | solution.py:522
  12.0 0.0 copy-start
  12.0 2.2 %copy-done = bf16[1,2,1024,1024]{3,2,1,0:T(8,128)(2,1)S(1)} copy-done((bf16[1,2,1024,1024]{3,2,1,0:T(8,128)(2,1)S(1)}, bf16[1,2,1024,1024]{3,2,1,0:T(8,128)(2,1)}, u32[]{:S(2)}) %copy-start) | copy-done | bytes 4194328
  14.2 1.1 %face_maps.1 = (f32[256,256]{1,0:T(8,128)S(1)}, f32[256,256]{1,0:T(8,128)S(1)}, bf16[256,1024]{1,0:T(8,128)(2,1)S(1)}, bf16[256,1024]{1,0:T(8,128)(2,1)S(1)}) custom-call(s32[2,8]{1,0:T(2,128)S(1)} %bitcast.18, bf16[2,1024,1024]{2,1,0:T(8,128)(2,1)S(1)} %bitcast.10, bf16[1024,256]{1,0:T(8,128)(2,1)S(1)} %bitcast.16), custom_call_target="tpu_custom_call" | custom-call | flops 1380000000 | tf_op jit(solution)/shard_map/face_maps/pallas_call | solution.py:200
  15.3 0.0 copy-start.5
  15.4 0.8 %copy-done.5 = bf16[256,1024]{1,0:T(8,128)(2,1)} copy-done((bf16[256,1024]{1,0:T(8,128)(2,1)}, bf16[256,1024]{1,0:T(8,128)(2,1)S(1)}, u32[]{:S(2)}) %copy-start.5) | copy-done | bytes 524312
  16.1 1.9 %collective-permute-start.3 = (f32[256,256]{1,0:T(8,128)S(1)}, f32[256,256]{1,0:T(8,128)S(1)}, u32[]{:S(2)}, u32[]{:S(2)}) collective-permute-start(f32[256,256]{1,0:T(8,128)S(1)} %get-tuple-element.33), channel_id=1, source_target_pairs={{0,2},{1,3},{2,0},{3,1},{4,6},{5,7},{6,4},{7,5},{8,10},{9,11},{10,... | collective-permute-start | bytes 786440 | tf_op jit(solution)/shard_map/ppermute | solution.py:472
  18.1 9.0 %all-to-all-done.received = bf16[16,136,128]{2,1,0:T(8,128)(2,1)S(1)} async-done(((bf16[16,136,128]{2,1,0:T(8,128)(2,1)}), bf16[16,136,128]{2,1,0:T(8,128)(2,1)S(1)}, u32[]{:S(2)}, u32[]{:S(2)}) %all-to-all-start) | async-done | bytes 557088 | tf_op jit(solution)/shard_map/all_to_all | solution.py:522
  27.1 1.0 %copy-done.6 = bf16[256,1024]{1,0:T(8,128)(2,1)S(1)} copy-done((bf16[256,1024]{1,0:T(8,128)(2,1)S(1)}, bf16[256,1024]{1,0:T(8,128)(2,1)}, u32[]{:S(2)}) %copy-start.6) | copy-done | bytes 524312
  28.1 1.4 %source_and_face.1 = (bf16[2,1024,128]{2,1,0:T(8,128)(2,1)S(1)}, bf16[64,256]{1,0:T(8,128)(2,1)S(1)}, bf16[64,256]{1,0:T(8,128)(2,1)S(1)}, bf16[64,256]{1,0:T(8,128)(2,1)S(1)}, bf16[64,256]{1,0:T(8,128)(2,1)S(1)}) custom-call(bf16[16,136,128]{2,1,0:T(8,128)(2,1)S(1)} %all-to-all-done.received, bf16[2,1024,128]{2,1,0:T(8,128)(2,1)S(1)} %bitcast.15, ...), custom_call_target="tpu_custom_call" | custom-call | flops 1610000000 | tf_op jit(solution)/shard_map/source_and_face/pallas_call | solution.py:314
  29.5 0.1 collective-permute-start.5
  29.6 0.0 collective-permute-done.3._map
  29.6 0.5 collective-permute-start.4
  30.1 0.8 %collective-permute-start = (bf16[64,256]{1,0:T(8,128)(2,1)S(1)}, bf16[64,256]{1,0:T(8,128)(2,1)S(1)}, u32[]{:S(2)}, u32[]{:S(2)}) collective-permute-start(bf16[64,256]{1,0:T(8,128)(2,1)S(1)} %get-tuple-element.29), channel_id=1, source_target_pairs={{0,3},{1,2},{2,1},{3,0},{4,7},{5,6},{6,5},{7,4},{8,11},{9,10},{10,... | collective-permute-start | bytes 98312 | tf_op jit(solution)/shard_map/ppermute | solution.py:476
  31.0 0.9 %collective-permute-start.1 = (bf16[64,256]{1,0:T(8,128)(2,1)S(1)}, bf16[64,256]{1,0:T(8,128)(2,1)S(1)}, u32[]{:S(2)}, u32[]{:S(2)}) collective-permute-start(bf16[64,256]{1,0:T(8,128)(2,1)S(1)} %get-tuple-element.30), channel_id=1, source_target_pairs={{0,2},{1,3},{2,0},{3,1},{4,6},{5,7},{6,4},{7,5},{8,10},{9,11},{10,... | collective-permute-start | bytes 98312 | tf_op jit(solution)/shard_map/ppermute | solution.py:472
  31.8 0.2 collective-permute-start.2
  32.0 0.0 collective-permute-done.5.near
  32.0 0.0 collective-permute-done.4.far
  32.0 0.8 %chain_maps.1 = (bf16[256,256]{1,0:T(8,128)(2,1)S(1)}, bf16[2,4,256,256]{3,2,1,0:T(8,128)(2,1)S(1)}) custom-call(f32[256,256]{1,0:T(8,128)S(1)} %get-tuple-element.32.own, f32[256,256]{1,0:T(8,128)S(1)} %collective-permute-done.4.far, f32[256,256]{1,0:T(8,128)S(1)} %after_exchange.2.across, f32[256,256]{1,0:T(8,128)S(1)} %collective-permute-done.5.near), custom_call_target="tpu_custom_call" | custom-call | flops 1035000000 | tf_op jit(solution)/shard_map/chain_maps/pallas_call | solution.py:245
  32.8 0.7 %collective-permute-start.10 = (bf16[256,256]{1,0:T(8,128)(2,1)S(1)}, bf16[256,256]{1,0:T(8,128)(2,1)S(1)}, u32[]{:S(2)}, u32[]{:S(2)}) collective-permute-start(bf16[256,256]{1,0:T(8,128)(2,1)S(1)} %get-tuple-element.38), channel_id=1, source_target_pairs={{4,8},{8,12},{5,13},{6,10},{10,14},{7,15},{20,24},{24,28},{21,29},... | collective-permute-start | bytes 393224 | tf_op jit(solution)/shard_map/ppermute | solution.py:494
  33.5 1.8 %image_and_maps.2 = (f32[2,1024,128]{2,1,0:T(8,128)S(1)}, bf16[2,2,256,256]{3,2,1,0:T(8,128)(2,1)S(1)}) custom-call(bf16[2,1024,1024]{2,1,0:T(8,128)(2,1)S(1)} %bitcast.11, bf16[2,1024,128]{2,1,0:T(8,128)(2,1)S(1)} %get-tuple-element.35.refs_1_, bf16[2,4,256,256]{3,2,1,0:T(8,128)(2,1)S(1)} %get-tuple-element.34.refs_2_.parts), custom_call_target="tpu_custom_call" | custom-call | flops 2300000000 | tf_op jit(solution)/shard_map/image_and_maps/pallas_call | solution.py:380
  35.3 0.0 collective-permute-done.far
  35.3 0.0 collective-permute-done.1.across
  35.3 0.0 collective-permute-done.2.near
  35.3 0.6 %plane_total.1 = (bf16[64,256]{1,0:T(8,128)(2,1)S(1)}, f32[3,64,256]{2,1,0:T(8,128)S(1)}) custom-call(bf16[64,256]{1,0:T(8,128)(2,1)S(1)} %get-tuple-element.28._packets.own, bf16[64,256]{1,0:T(8,128)(2,1)S(1)} %collective-permute-done.far, bf16[64,256]{1,0:T(8,128)(2,1)S(1)} %collective-permute-done.1.across, ...), custom_call_target="tpu_custom_call" | custom-call | flops 3449999872 | tf_op jit(solution)/shard_map/plane_total/pallas_call | solution.py:346
  35.9 4.0 %collective-permute-start.6 = (bf16[64,256]{1,0:T(8,128)(2,1)S(1)}, bf16[64,256]{1,0:T(8,128)(2,1)S(1)}, u32[]{:S(2)}, u32[]{:S(2)}) collective-permute-start(bf16[64,256]{1,0:T(8,128)(2,1)S(1)} %get-tuple-element.37), channel_id=1, source_target_pairs={{0,12},{1,13},{2,14},{3,15},{16,28},{17,29},{18,30},{19,31}} | collective-permute-start | bytes 98312 | tf_op jit(solution)/shard_map/ppermute | solution.py:500
  40.0 1.3 %collective-permute-start.7 = (bf16[64,256]{1,0:T(8,128)(2,1)S(1)}, bf16[64,256]{1,0:T(8,128)(2,1)S(1)}, u32[]{:S(2)}, u32[]{:S(2)}) collective-permute-start(bf16[64,256]{1,0:T(8,128)(2,1)S(1)} %get-tuple-element.37), channel_id=1, source_target_pairs={{0,4},{1,5},{2,6},{3,7},{16,20},{17,21},{18,22},{19,23}} | collective-permute-start | bytes 98312 | tf_op jit(solution)/shard_map/ppermute | solution.py:500
  41.3 1.3 %collective-permute-start.8 = (bf16[64,256]{1,0:T(8,128)(2,1)S(1)}, bf16[64,256]{1,0:T(8,128)(2,1)S(1)}, u32[]{:S(2)}, u32[]{:S(2)}) collective-permute-start(bf16[64,256]{1,0:T(8,128)(2,1)S(1)} %get-tuple-element.37), channel_id=1, source_target_pairs={{0,8},{1,9},{2,10},{3,11},{4,12},{5,13},{6,14},{7,15},{16,24},{17,... | collective-permute-start | bytes 98312 | tf_op jit(solution)/shard_map/ppermute | solution.py:500
  42.6 0.7 %collective-permute-start.9 = (bf16[64,256]{1,0:T(8,128)(2,1)S(1)}, bf16[64,256]{1,0:T(8,128)(2,1)S(1)}, u32[]{:S(2)}, u32[]{:S(2)}) collective-permute-start(bf16[64,256]{1,0:T(8,128)(2,1)S(1)} %get-tuple-element.37), channel_id=1, source_target_pairs={{4,8},{5,9},{6,10},{7,11},{8,12},{9,13},{10,14},{11,15},{20,24},{2... | collective-permute-start | bytes 98312 | tf_op jit(solution)/shard_map/ppermute | solution.py:500
  43.2 0.0 collective-permute-done.10.got
  43.2 0.7 %collective-permute-start.11 = (bf16[256,256]{1,0:T(8,128)(2,1)S(1)}, bf16[256,256]{1,0:T(8,128)(2,1)S(1)}, u32[]{:S(2)}, u32[]{:S(2)}) collective-permute-start(bf16[256,256]{1,0:T(8,128)(2,1)S(1)} %collective-permute-done.10.got), channel_id=1, source_target_pairs={{8,9},{9,8},{10,11},{11,10},{12,13},{13,12},{14,15},{15,14},{24,25... | collective-permute-start | bytes 393224 | tf_op jit(solution)/shard_map/ppermute | solution.py:495
  43.9 0.1 image_and_maps.3
  44.1 0.0 collective-permute-done.6.third
  44.1 0.0 collective-permute-done.7.near_one
  44.1 0.1 collective-permute-done.8.second
  44.1 0.0 collective-permute-done.9.far_one
  44.1 0.0 collective-permute-done.11.other
  44.2 0.7 %entering.1 = (bf16[64,256]{1,0:T(8,128)(2,1)S(1)}, bf16[64,256]{1,0:T(8,128)(2,1)S(1)}, bf16[64,256]{1,0:T(8,128)(2,1)S(1)}, bf16[64,256]{1,0:T(8,128)(2,1)S(1)}) custom-call(bf16[64,256]{1,0:T(8,128)(2,1)S(1)} %collective-permute-done.6.third, bf16[64,256]{1,0:T(8,128)(2,1)S(1)} %collective-permute-done.7.near_one, ...), custom_call_target="tpu_custom_call" | custom-call | flops 1610000000 | tf_op jit(solution)/shard_map/entering/pallas_call | solution.py:420
  44.9 0.5 collective-permute-start.12
  45.4 0.2 collective-permute-start.13
  45.6 1.2 %collective-permute-start.14 = (bf16[64,256]{1,0:T(8,128)(2,1)S(1)}, bf16[64,256]{1,0:T(8,128)(2,1)S(1)}, u32[]{:S(2)}, u32[]{:S(2)}) collective-permute-start(bf16[64,256]{1,0:T(8,128)(2,1)S(1)} %get-tuple-element.45), channel_id=1, source_target_pairs={{0,1},{1,0},{2,3},{3,2},{4,5},{5,4},{6,7},{7,6},{8,9},{9,8},{10,11... | collective-permute-start | bytes 98312 | tf_op jit(solution)/shard_map/ppermute | solution.py:468
  46.8 1.9 %prop.1 = bf16[2,1024,256]{2,1,0:T(8,128)(2,1)S(1)} custom-call(s32[2,8]{1,0:T(2,128)S(1)} %bitcast.19, bf16[2,1024,1024]{2,1,0:T(8,128)(2,1)S(1)} %bitcast.13, bf16[1024,256]{1,0:T(8,128)(2,1)S(1)} %bitcast.17, bf16[64,256]{1,0:T(8,128)(2,1)S(1)} %get-tuple-element.42._tie.own), custom_call_target="tpu_custom_call" | custom-call | flops 1724999936 | tf_op jit(solution)/shard_map/prop/pallas_call | solution.py:219
  48.7 0.0 collective-permute-done.12.far
  48.8 0.5 %collective-permute-done.13.across = bf16[64,256]{1,0:T(8,128)(2,1)S(1)} collective-permute-done((bf16[64,256]{1,0:T(8,128)(2,1)S(1)}, bf16[64,256]{1,0:T(8,128)(2,1)S(1)}, u32[]{:S(2)}, u32[]{:S(2)}) %collective-permute-start.13) | collective-permute-done | bytes 32800 | tf_op jit(solution)/shard_map/ppermute | solution.py:472
  49.3 0.0 collective-permute-done.14.near
  49.3 1.2 %waves.1 = bf16[2,1024,128]{2,1,0:T(8,128)(2,1)} custom-call(bf16[64,256]{1,0:T(8,128)(2,1)S(1)} %get-tuple-element.42._tie.own, bf16[64,256]{1,0:T(8,128)(2,1)S(1)} %collective-permute-done.12.far, bf16[64,256]{1,0:T(8,128)(2,1)S(1)} %collective-permute-done.13.across, bf16[64,256]{1,0:T(8,128)(2,1)S(1)} %collective-permute-done.14.near, ...), custom_call_target="tpu_custom_call" | custom-call | flops 1495000064 | tf_op jit(solution)/shard_map/waves/pallas_call | solution.py:451
  (11 shorter events, 0.0 us)
Async XLA Ops:
  0.0 12.0 %copy-start.3 = (bf16[1,1024,256]{2,1,0:T(8,128)(2,1)S(1)}, bf16[1,1024,256]{2,1,0:T(8,128)(2,1)}, u32[]{:S(2)}) copy-start(bf16[1,1024,256]{2,1,0:T(8,128)(2,1)} %param.8) | copy-start | bytes 1572868
  0.0 12.0 %copy-start.4 = (s32[1,8,2]{1,2,0:T(2,128)S(1)}, s32[1,8,2]{1,2,0:T(2,128)}, u32[]{:S(2)}) copy-start(s32[1,8,2]{1,2,0:T(2,128)} %param.9) | copy-start | bytes 196
  4.5 22.6 %copy-start.2 = (bf16[1,2,1024,128]{3,2,1,0:T(8,128)(2,1)S(1)}, bf16[1,2,1024,128]{3,2,1,0:T(8,128)(2,1)}, u32[]{:S(2)}) copy-start(bf16[1,2,1024,128]{3,2,1,0:T(8,128)(2,1)} %param.7) | copy-start | bytes 1572868
  4.5 22.6 %all-to-all-start = ((bf16[16,136,128]{2,1,0:T(8,128)(2,1)}), bf16[16,136,128]{2,1,0:T(8,128)(2,1)S(1)}, u32[]{:S(2)}, u32[]{:S(2)}) async-start(bf16[16,136,128]{2,1,0:T(8,128)(2,1)} %pairs.1), calls=%async_computation | async-start | bytes 1114112 | tf_op jit(solution)/shard_map/all_to_all | solution.py:522
  12.0 2.2 %copy-start = (bf16[1,2,1024,1024]{3,2,1,0:T(8,128)(2,1)S(1)}, bf16[1,2,1024,1024]{3,2,1,0:T(8,128)(2,1)}, u32[]{:S(2)}) copy-start(bf16[1,2,1024,1024]{3,2,1,0:T(8,128)(2,1)} %param.6) | copy-start | bytes 12582916
  15.3 0.8 %copy-start.5 = (bf16[256,1024]{1,0:T(8,128)(2,1)}, bf16[256,1024]{1,0:T(8,128)(2,1)S(1)}, u32[]{:S(2)}) copy-start(bf16[256,1024]{1,0:T(8,128)(2,1)S(1)} %get-tuple-element.27.refs_1_) | copy-start | bytes 1572868
  16.1 13.5 %collective-permute-start.3 = (f32[256,256]{1,0:T(8,128)S(1)}, f32[256,256]{1,0:T(8,128)S(1)}, u32[]{:S(2)}, u32[]{:S(2)}) collective-permute-start(f32[256,256]{1,0:T(8,128)S(1)} %get-tuple-element.33), channel_id=1, source_target_pairs={{0,2},{1,3},{2,0},{3,1},{4,6},{5,7},{6,4},{7,5},{8,10},{9,11},{10,... | collective-permute-start | bytes 786440 | tf_op jit(solution)/shard_map/ppermute | solution.py:472
  27.1 1.0 %copy-start.6 = (bf16[256,1024]{1,0:T(8,128)(2,1)S(1)}, bf16[256,1024]{1,0:T(8,128)(2,1)}, u32[]{:S(2)}) copy-start(bf16[256,1024]{1,0:T(8,128)(2,1)} %copy-done.5) | copy-start | bytes 1572868
  28.1 5.4 %copy-start.1 = (bf16[1,2,1024,1024]{3,2,1,0:T(8,128)(2,1)S(1)}, bf16[1,2,1024,1024]{3,2,1,0:T(8,128)(2,1)}, u32[]{:S(2)}) copy-start(bf16[1,2,1024,1024]{3,2,1,0:T(8,128)(2,1)} %param.6) | copy-start | bytes 12582916
  29.5 2.5 %collective-permute-start.5 = (f32[256,256]{1,0:T(8,128)S(1)}, f32[256,256]{1,0:T(8,128)S(1)}, u32[]{:S(2)}, u32[]{:S(2)}) collective-permute-start(f32[256,256]{1,0:T(8,128)S(1)} %after_exchange.3), channel_id=1, source_target_pairs={{0,1},{1,0},{2,3},{3,2},{4,5},{5,4},{6,7},{7,6},{8,9},{9,8},{10,11... | collective-permute-start | bytes 786440 | tf_op jit(solution)/shard_map/ppermute | solution.py:468
  29.6 2.4 %collective-permute-start.4 = (f32[256,256]{1,0:T(8,128)S(1)}, f32[256,256]{1,0:T(8,128)S(1)}, u32[]{:S(2)}, u32[]{:S(2)}) collective-permute-start(f32[256,256]{1,0:T(8,128)S(1)} %after_exchange.2.across), channel_id=1, source_target_pairs={{0,1},{1,0},{2,3},{3,2},{4,5},{5,4},{6,7},{7,6},{8,9},{9,8},{10,11... | collective-permute-start | bytes 786440 | tf_op jit(solution)/shard_map/ppermute | solution.py:468
  30.1 5.2 %collective-permute-start = (bf16[64,256]{1,0:T(8,128)(2,1)S(1)}, bf16[64,256]{1,0:T(8,128)(2,1)S(1)}, u32[]{:S(2)}, u32[]{:S(2)}) collective-permute-start(bf16[64,256]{1,0:T(8,128)(2,1)S(1)} %get-tuple-element.29), channel_id=1, source_target_pairs={{0,3},{1,2},{2,1},{3,0},{4,7},{5,6},{6,5},{7,4},{8,11},{9,10},{10,... | collective-permute-start | bytes 98312 | tf_op jit(solution)/shard_map/ppermute | solution.py:476
  31.0 4.4 %collective-permute-start.1 = (bf16[64,256]{1,0:T(8,128)(2,1)S(1)}, bf16[64,256]{1,0:T(8,128)(2,1)S(1)}, u32[]{:S(2)}, u32[]{:S(2)}) collective-permute-start(bf16[64,256]{1,0:T(8,128)(2,1)S(1)} %get-tuple-element.30), channel_id=1, source_target_pairs={{0,2},{1,3},{2,0},{3,1},{4,6},{5,7},{6,4},{7,5},{8,10},{9,11},{10,... | collective-permute-start | bytes 98312 | tf_op jit(solution)/shard_map/ppermute | solution.py:472
  31.8 3.5 %collective-permute-start.2 = (bf16[64,256]{1,0:T(8,128)(2,1)S(1)}, bf16[64,256]{1,0:T(8,128)(2,1)S(1)}, u32[]{:S(2)}, u32[]{:S(2)}) collective-permute-start(bf16[64,256]{1,0:T(8,128)(2,1)S(1)} %get-tuple-element.31), channel_id=1, source_target_pairs={{0,1},{1,0},{2,3},{3,2},{4,5},{5,4},{6,7},{7,6},{8,9},{9,8},{10,11... | collective-permute-start | bytes 98312 | tf_op jit(solution)/shard_map/ppermute | solution.py:468
  32.8 10.4 %collective-permute-start.10 = (bf16[256,256]{1,0:T(8,128)(2,1)S(1)}, bf16[256,256]{1,0:T(8,128)(2,1)S(1)}, u32[]{:S(2)}, u32[]{:S(2)}) collective-permute-start(bf16[256,256]{1,0:T(8,128)(2,1)S(1)} %get-tuple-element.38), channel_id=1, source_target_pairs={{4,8},{8,12},{5,13},{6,10},{10,14},{7,15},{20,24},{24,28},{21,29},... | collective-permute-start | bytes 393224 | tf_op jit(solution)/shard_map/ppermute | solution.py:494
  35.9 8.1 %collective-permute-start.6 = (bf16[64,256]{1,0:T(8,128)(2,1)S(1)}, bf16[64,256]{1,0:T(8,128)(2,1)S(1)}, u32[]{:S(2)}, u32[]{:S(2)}) collective-permute-start(bf16[64,256]{1,0:T(8,128)(2,1)S(1)} %get-tuple-element.37), channel_id=1, source_target_pairs={{0,12},{1,13},{2,14},{3,15},{16,28},{17,29},{18,30},{19,31}} | collective-permute-start | bytes 98312 | tf_op jit(solution)/shard_map/ppermute | solution.py:500
  40.0 4.1 %collective-permute-start.7 = (bf16[64,256]{1,0:T(8,128)(2,1)S(1)}, bf16[64,256]{1,0:T(8,128)(2,1)S(1)}, u32[]{:S(2)}, u32[]{:S(2)}) collective-permute-start(bf16[64,256]{1,0:T(8,128)(2,1)S(1)} %get-tuple-element.37), channel_id=1, source_target_pairs={{0,4},{1,5},{2,6},{3,7},{16,20},{17,21},{18,22},{19,23}} | collective-permute-start | bytes 98312 | tf_op jit(solution)/shard_map/ppermute | solution.py:500
  41.3 2.9 %collective-permute-start.8 = (bf16[64,256]{1,0:T(8,128)(2,1)S(1)}, bf16[64,256]{1,0:T(8,128)(2,1)S(1)}, u32[]{:S(2)}, u32[]{:S(2)}) collective-permute-start(bf16[64,256]{1,0:T(8,128)(2,1)S(1)} %get-tuple-element.37), channel_id=1, source_target_pairs={{0,8},{1,9},{2,10},{3,11},{4,12},{5,13},{6,14},{7,15},{16,24},{17,... | collective-permute-start | bytes 98312 | tf_op jit(solution)/shard_map/ppermute | solution.py:500
  42.6 1.6 %collective-permute-start.9 = (bf16[64,256]{1,0:T(8,128)(2,1)S(1)}, bf16[64,256]{1,0:T(8,128)(2,1)S(1)}, u32[]{:S(2)}, u32[]{:S(2)}) collective-permute-start(bf16[64,256]{1,0:T(8,128)(2,1)S(1)} %get-tuple-element.37), channel_id=1, source_target_pairs={{4,8},{5,9},{6,10},{7,11},{8,12},{9,13},{10,14},{11,15},{20,24},{2... | collective-permute-start | bytes 98312 | tf_op jit(solution)/shard_map/ppermute | solution.py:500
  43.2 0.9 %collective-permute-start.11 = (bf16[256,256]{1,0:T(8,128)(2,1)S(1)}, bf16[256,256]{1,0:T(8,128)(2,1)S(1)}, u32[]{:S(2)}, u32[]{:S(2)}) collective-permute-start(bf16[256,256]{1,0:T(8,128)(2,1)S(1)} %collective-permute-done.10.got), channel_id=1, source_target_pairs={{8,9},{9,8},{10,11},{11,10},{12,13},{13,12},{14,15},{15,14},{24,25... | collective-permute-start | bytes 393224 | tf_op jit(solution)/shard_map/ppermute | solution.py:495
  44.9 3.9 %collective-permute-start.12 = (bf16[64,256]{1,0:T(8,128)(2,1)S(1)}, bf16[64,256]{1,0:T(8,128)(2,1)S(1)}, u32[]{:S(2)}, u32[]{:S(2)}) collective-permute-start(bf16[64,256]{1,0:T(8,128)(2,1)S(1)} %get-tuple-element.43), channel_id=1, source_target_pairs={{0,3},{1,2},{2,1},{3,0},{4,7},{5,6},{6,5},{7,4},{8,11},{9,10},{10,... | collective-permute-start | bytes 98312 | tf_op jit(solution)/shard_map/ppermute | solution.py:476
  45.4 3.9 %collective-permute-start.13 = (bf16[64,256]{1,0:T(8,128)(2,1)S(1)}, bf16[64,256]{1,0:T(8,128)(2,1)S(1)}, u32[]{:S(2)}, u32[]{:S(2)}) collective-permute-start(bf16[64,256]{1,0:T(8,128)(2,1)S(1)} %get-tuple-element.44), channel_id=1, source_target_pairs={{0,2},{1,3},{2,0},{3,1},{4,6},{5,7},{6,4},{7,5},{8,10},{9,11},{10,... | collective-permute-start | bytes 98312 | tf_op jit(solution)/shard_map/ppermute | solution.py:472
  45.6 3.7 %collective-permute-start.14 = (bf16[64,256]{1,0:T(8,128)(2,1)S(1)}, bf16[64,256]{1,0:T(8,128)(2,1)S(1)}, u32[]{:S(2)}, u32[]{:S(2)}) collective-permute-start(bf16[64,256]{1,0:T(8,128)(2,1)S(1)} %get-tuple-element.45), channel_id=1, source_target_pairs={{0,1},{1,0},{2,3},{3,2},{4,5},{5,4},{6,7},{7,6},{8,9},{9,8},{10,11... | collective-permute-start | bytes 98312 | tf_op jit(solution)/shard_map/ppermute | solution.py:468

commit v29 on v27

--- a/solution.py
+++ b/solution.py
@@ -252,12 +252,9 @@
     )(*maps)
 
 
-def source_kernel(received, inject, *refs):
+def source_kernel(received, inject, source, heads, targets, total, sem):
     energies, orbitals, columns = inject.shape
-    face_rows = refs[:energies]
-    source, own, far, across, near, quarters, total, heads, targets, sem = refs[energies:]
     sections = received.shape[0]
-    wide_rows = quarters.shape[1]
     rows = CAP * energies * BLK
 
     def read(s, _):
@@ -280,15 +277,53 @@
         return 0
 
     lax.fori_loop(0, sections, add, 0, unroll=2)
+    source[...] = total[...].astype(BF16)
+
+
+def placed_source(received, inject):
+    energies, orbitals, columns = inject.shape
+    sections = received.shape[0]
+    return call(
+        source_kernel,
+        "source",
+        [IN_VMEM] * 2,
+        shape(*inject.shape),
+        [
+            pltpu.VMEM((sections, columns), jnp.int32),
+            pltpu.SMEM((sections, columns), jnp.int32),
+            pltpu.VMEM(inject.shape, F32),
+            pltpu.SemaphoreType.DMA,
+        ],
+        1.0,
+    )(received, inject)
+
+
+def quarters_kernel(source, *refs):
+    energies = source.shape[0]
+    face_rows = refs[:energies]
+    own, far, across, near, quarters = refs[energies:]
     split = GROUP // energies
+    size = quarters.shape[1]
     for e in range(energies):
-        source[e] = total[e].astype(BF16)
-        tall = dot(face_rows[e][...], source[e])
-        wide = tall.T
+        wide = dot(face_rows[e][...], source[e]).T
         for h in range(split):
-            quarters[e * split + h] = wide[h * wide_rows : (h + 1) * wide_rows]
+            quarters[e * split + h] = wide[h * size : (h + 1) * size]
     for out, at in zip((own, far, across, near), partners()):
         out[...] = quarters[at].astype(BF16)
+
+
+def face_quarters(source, face_rows):
+    energies, _, columns = source.shape
+    face = face_rows[0].shape[0]
+    rows = columns * energies // GROUP
+    return call(
+        quarters_kernel,
+        "face_quarters",
+        [IN_VMEM] * (1 + energies),
+        [shape(rows, face)] * GROUP,
+        [pltpu.VMEM((GROUP, rows, face), F32)],
+        0.6,
+    )(source, *face_rows)
 
 
 def after_kernel(_packets, _map, _same_map):
@@ -305,26 +340,6 @@
         0.1,
         aliases={1: 0},
     )(packets, item)[0]
-
-
-def placed_source(received, inject, face_rows):
-    face = face_rows[0].shape[0]
-    energies, orbitals, columns = inject.shape
-    sections = received.shape[0]
-    return call(
-        source_kernel,
-        "source_and_face",
-        [IN_VMEM] * (2 + energies),
-        [shape(*inject.shape)] + [shape(columns * energies // GROUP, face)] * GROUP,
-        [
-            pltpu.VMEM((GROUP, columns * energies // GROUP, face), F32),
-            pltpu.VMEM(inject.shape, F32),
-            pltpu.VMEM((sections, columns), jnp.int32),
-            pltpu.SMEM((sections, columns), jnp.int32),
-            pltpu.SemaphoreType.DMA,
-        ],
-        1.4,
-    )(received, inject, *face_rows)
 
 
 def collect(refs, held):
@@ -525,7 +540,8 @@
     across = to_across(other_map, sections)
     near = to_near(own_map, sections)
 
-    source, *quarters = placed_source(received, inject, face_rows)
+    source = placed_source(received, inject)
+    quarters = face_quarters(source, face_rows)
     shifts = exchange(*quarters, sections)
     across = handed_on(across, quarters[0])
     far = to_near(across, sections)

time: 50.4 us -> 49.5 us (0.982)
  local copies, waits for them, and re-layouts: 4.03 us -> 3.1 us
    unnamed x14, local copies, waits for them, and re-layouts: 4.03 us -> 3.1 us
    pallas_call x1 -> x2, Pallas kernels: 1.41 us -> 1.42 us  [the longest x1 0.91 us: placed_source(): call(source_kernel, 'source', [IN_VMEM] * 2, shape(*inject.shape), [pltpu...]
where the time goes in v29:
time: 49.5 us; the launch traced here: 49.2 us
  starting transfers between devices  22 us (44%)
  Pallas kernels  14.2 us (29%)
  waiting for transfers between devices  9.65 us (19%)
  local copies, waits for them, and re-layouts  3.1 us (6%)
    all_to_all x1, waiting for transfers between devices, per_device(): lax.all_to_all(outgoing, 'sec', split_axis=0, concat_axis=0, tiled=True)  9.01 us
    all_to_all x1, starting transfers between devices, per_device(): lax.all_to_all(outgoing, 'sec', split_axis=0, concat_axis=0, tiled=True)  7.49 us
    ppermute x4, starting transfers between devices, between(): return lax.ppermute(item, 'sec', pairs)  7.07 us
    pallas_call x1, Pallas kernels, outgoing_pairs(): call(pairs_kernel, 'pairs', [IN_HBM] * 4, shape(sections, CAP * energies...  4.51 us
    ppermute x3, starting transfers between devices, to_across(): lax.ppermute(item, 'sec', [(s, s // GROUP * GROUP + (s % GROUP + CORES) %...  3.68 us
    unnamed x14, local copies, waits for them, and re-layouts  3.1 us
    pallas_call x2, Pallas kernels, image_and_maps(): call(functools.partial(work_kernel, not held), 'image_and_maps', [IN_VMEM...  1.9 us
    pallas_call x1, Pallas kernels, propagator(): call(prop_kernel, 'prop', [IN_SMEM, IN_VMEM, IN_VMEM, IN_PLACE], shape(en...  1.9 us
  transfers between devices with their start and end apart: 16, of which 3 were waited for; matrix products, arithmetic and copies ran while one was open for 0% of the time, Pallas kernels for 16%

profile of v29, /device:TPU:0, one launch (start us, length us, event | category | flops | bytes accessed | tf_op | source)
XLA Modules:
  0.0 49.2 jit_solution(165408919596366570)
XLA Ops:
  0.0 4.5 %pairs.1 = bf16[16,136,128]{2,1,0:T(8,128)(2,1)} custom-call(s32[16]{0:T(128)} %bitcast.21, s32[2,16]{1,0:T(2,128)} %bitcast.20, bf16[2,1024,1024]{2,1,0:T(8,128)(2,1)} %bitcast.9, bf16[2,1024,128]{2,1,0:T(8,128)(2,1)} %bitcast.14), custom_call_target="tpu_custom_call" | custom-call | flops 4600000000 | tf_op jit(solution)/shard_map/pairs/pallas_call | solution.py:161
  4.5 0.0 copy-start.2
  4.5 7.5 %all-to-all-start = ((bf16[16,136,128]{2,1,0:T(8,128)(2,1)}), bf16[16,136,128]{2,1,0:T(8,128)(2,1)S(1)}, u32[]{:S(2)}, u32[]{:S(2)}) async-start(bf16[16,136,128]{2,1,0:T(8,128)(2,1)} %pairs.1), calls=%async_computation | async-start | bytes 1114112 | tf_op jit(solution)/shard_map/all_to_all | solution.py:537
  12.1 0.0 copy-start
  12.1 2.2 %copy-done = bf16[1,2,1024,1024]{3,2,1,0:T(8,128)(2,1)S(1)} copy-done((bf16[1,2,1024,1024]{3,2,1,0:T(8,128)(2,1)S(1)}, bf16[1,2,1024,1024]{3,2,1,0:T(8,128)(2,1)}, u32[]{:S(2)}) %copy-start) | copy-done | bytes 4194328
  14.2 1.1 %face_maps.1 = (f32[256,256]{1,0:T(8,128)S(1)}, f32[256,256]{1,0:T(8,128)S(1)}, bf16[256,1024]{1,0:T(8,128)(2,1)S(1)}, bf16[256,1024]{1,0:T(8,128)(2,1)S(1)}) custom-call(s32[2,8]{1,0:T(2,128)S(1)} %bitcast.18, bf16[2,1024,1024]{2,1,0:T(8,128)(2,1)S(1)} %bitcast.10, bf16[1024,256]{1,0:T(8,128)(2,1)S(1)} %bitcast.16), custom_call_target="tpu_custom_call" | custom-call | flops 1380000000 | tf_op jit(solution)/shard_map/face_maps/pallas_call | solution.py:200
  15.4 0.0 copy-start.5
  15.4 0.8 %copy-done.5 = bf16[256,1024]{1,0:T(8,128)(2,1)} copy-done((bf16[256,1024]{1,0:T(8,128)(2,1)}, bf16[256,1024]{1,0:T(8,128)(2,1)S(1)}, u32[]{:S(2)}) %copy-start.5) | copy-done | bytes 524312
  16.2 1.9 %collective-permute-start.3 = (f32[256,256]{1,0:T(8,128)S(1)}, f32[256,256]{1,0:T(8,128)S(1)}, u32[]{:S(2)}, u32[]{:S(2)}) collective-permute-start(f32[256,256]{1,0:T(8,128)S(1)} %get-tuple-element.32), channel_id=1, source_target_pairs={{0,2},{1,3},{2,0},{3,1},{4,6},{5,7},{6,4},{7,5},{8,10},{9,11},{10,... | collective-permute-start | bytes 786440 | tf_op jit(solution)/shard_map/ppermute | solution.py:487
  18.1 0.0 collective-permute-start.5
  18.1 9.0 %all-to-all-done.received = bf16[16,136,128]{2,1,0:T(8,128)(2,1)S(1)} async-done(((bf16[16,136,128]{2,1,0:T(8,128)(2,1)}), bf16[16,136,128]{2,1,0:T(8,128)(2,1)S(1)}, u32[]{:S(2)}, u32[]{:S(2)}) %all-to-all-start) | async-done | bytes 557088 | tf_op jit(solution)/shard_map/all_to_all | solution.py:537
  27.1 0.9 %source.1.refs_1_ = bf16[2,1024,128]{2,1,0:T(8,128)(2,1)S(1)} custom-call(bf16[16,136,128]{2,1,0:T(8,128)(2,1)S(1)} %all-to-all-done.received, bf16[2,1024,128]{2,1,0:T(8,128)(2,1)S(1)} %bitcast.15), custom_call_target="tpu_custom_call" | custom-call | flops 1150000000 | tf_op jit(solution)/shard_map/source/pallas_call | solution.py:286
  28.0 0.0 copy-start.1
  28.0 0.1 copy-done.6
  28.1 0.5 %face_quarters.1 = (bf16[64,256]{1,0:T(8,128)(2,1)S(1)}, bf16[64,256]{1,0:T(8,128)(2,1)S(1)}, bf16[64,256]{1,0:T(8,128)(2,1)S(1)}, bf16[64,256]{1,0:T(8,128)(2,1)S(1)}) custom-call(bf16[2,1024,128]{2,1,0:T(8,128)(2,1)S(1)} %source.1.refs_1_, bf16[256,1024]{1,0:T(8,128)(2,1)S(1)} %get-tuple-element.25.refs_0_, bf16[256,1024]{1,0:T(8,128)(2,1)S(1)} %copy-done.6), custom_call_target="tpu_custom_call" | custom-call | flops 690000000 | tf_op jit(solution)/shard_map/face_quarters/pallas_call | solution.py:319
  28.7 0.0 collective-permute-done.3._map
  28.7 0.1 collective-permute-start.4
  28.8 0.9 %collective-permute-start = (bf16[64,256]{1,0:T(8,128)(2,1)S(1)}, bf16[64,256]{1,0:T(8,128)(2,1)S(1)}, u32[]{:S(2)}, u32[]{:S(2)}) collective-permute-start(bf16[64,256]{1,0:T(8,128)(2,1)S(1)} %get-tuple-element.28), channel_id=1, source_target_pairs={{0,3},{1,2},{2,1},{3,0},{4,7},{5,6},{6,5},{7,4},{8,11},{9,10},{10,... | collective-permute-start | bytes 98312 | tf_op jit(solution)/shard_map/ppermute | solution.py:491
  29.6 1.3 %collective-permute-start.1 = (bf16[64,256]{1,0:T(8,128)(2,1)S(1)}, bf16[64,256]{1,0:T(8,128)(2,1)S(1)}, u32[]{:S(2)}, u32[]{:S(2)}) collective-permute-start(bf16[64,256]{1,0:T(8,128)(2,1)S(1)} %get-tuple-element.29), channel_id=1, source_target_pairs={{0,2},{1,3},{2,0},{3,1},{4,6},{5,7},{6,4},{7,5},{8,10},{9,11},{10,... | collective-permute-start | bytes 98312 | tf_op jit(solution)/shard_map/ppermute | solution.py:487
  30.9 0.0 collective-permute-start.2
  30.9 0.0 collective-permute-done.5.near
  30.9 0.0 collective-permute-done.4.far
  30.9 0.8 %chain_maps.1 = (bf16[256,256]{1,0:T(8,128)(2,1)S(1)}, bf16[2,4,256,256]{3,2,1,0:T(8,128)(2,1)S(1)}) custom-call(f32[256,256]{1,0:T(8,128)S(1)} %get-tuple-element.31.own, f32[256,256]{1,0:T(8,128)S(1)} %collective-permute-done.4.far, f32[256,256]{1,0:T(8,128)S(1)} %after_exchange.1.across, f32[256,256]{1,0:T(8,128)S(1)} %collective-permute-done.5.near), custom_call_target="tpu_custom_call" | custom-call | flops 1035000000 | tf_op jit(solution)/shard_map/chain_maps/pallas_call | solution.py:245
  31.8 1.8 %image_and_maps.2 = (f32[2,1024,128]{2,1,0:T(8,128)S(1)}, bf16[2,2,256,256]{3,2,1,0:T(8,128)(2,1)S(1)}) custom-call(bf16[2,1024,1024]{2,1,0:T(8,128)(2,1)S(1)} %bitcast.11, bf16[2,1024,128]{2,1,0:T(8,128)(2,1)S(1)} %source.1.refs_1_, bf16[2,4,256,256]{3,2,1,0:T(8,128)(2,1)S(1)} %get-tuple-element.33.refs_2_.parts), custom_call_target="tpu_custom_call" | custom-call | flops 2300000000 | tf_op jit(solution)/shard_map/image_and_maps/pallas_call | solution.py:395
  33.5 0.7 %collective-permute-start.10 = (bf16[256,256]{1,0:T(8,128)(2,1)S(1)}, bf16[256,256]{1,0:T(8,128)(2,1)S(1)}, u32[]{:S(2)}, u32[]{:S(2)}) collective-permute-start(bf16[256,256]{1,0:T(8,128)(2,1)S(1)} %get-tuple-element.36), channel_id=1, source_target_pairs={{4,8},{8,12},{5,13},{6,10},{10,14},{7,15},{20,24},{24,28},{21,29},... | collective-permute-start | bytes 393224 | tf_op jit(solution)/shard_map/ppermute | solution.py:509
  34.2 0.0 collective-permute-done.far
  34.2 0.0 collective-permute-done.1.across
  34.2 0.6 %plane_total.1 = (bf16[64,256]{1,0:T(8,128)(2,1)S(1)}, f32[3,64,256]{2,1,0:T(8,128)S(1)}) custom-call(bf16[64,256]{1,0:T(8,128)(2,1)S(1)} %get-tuple-element.27._packets.own, bf16[64,256]{1,0:T(8,128)(2,1)S(1)} %collective-permute-done.far, bf16[64,256]{1,0:T(8,128)(2,1)S(1)} %collective-permute-done.1.across, ...), custom_call_target="tpu_custom_call" | custom-call | flops 3449999872 | tf_op jit(solution)/shard_map/plane_total/pallas_call | solution.py:361
  34.9 3.8 %collective-permute-start.6 = (bf16[64,256]{1,0:T(8,128)(2,1)S(1)}, bf16[64,256]{1,0:T(8,128)(2,1)S(1)}, u32[]{:S(2)}, u32[]{:S(2)}) collective-permute-start(bf16[64,256]{1,0:T(8,128)(2,1)S(1)} %get-tuple-element.35), channel_id=1, source_target_pairs={{0,12},{1,13},{2,14},{3,15},{16,28},{17,29},{18,30},{19,31}} | collective-permute-start | bytes 98312 | tf_op jit(solution)/shard_map/ppermute | solution.py:515
  38.7 1.3 %collective-permute-start.7 = (bf16[64,256]{1,0:T(8,128)(2,1)S(1)}, bf16[64,256]{1,0:T(8,128)(2,1)S(1)}, u32[]{:S(2)}, u32[]{:S(2)}) collective-permute-start(bf16[64,256]{1,0:T(8,128)(2,1)S(1)} %get-tuple-element.35), channel_id=1, source_target_pairs={{0,4},{1,5},{2,6},{3,7},{16,20},{17,21},{18,22},{19,23}} | collective-permute-start | bytes 98312 | tf_op jit(solution)/shard_map/ppermute | solution.py:515
  40.0 1.3 %collective-permute-start.8 = (bf16[64,256]{1,0:T(8,128)(2,1)S(1)}, bf16[64,256]{1,0:T(8,128)(2,1)S(1)}, u32[]{:S(2)}, u32[]{:S(2)}) collective-permute-start(bf16[64,256]{1,0:T(8,128)(2,1)S(1)} %get-tuple-element.35), channel_id=1, source_target_pairs={{0,8},{1,9},{2,10},{3,11},{4,12},{5,13},{6,14},{7,15},{16,24},{17,... | collective-permute-start | bytes 98312 | tf_op jit(solution)/shard_map/ppermute | solution.py:515
  41.3 0.7 %collective-permute-start.9 = (bf16[64,256]{1,0:T(8,128)(2,1)S(1)}, bf16[64,256]{1,0:T(8,128)(2,1)S(1)}, u32[]{:S(2)}, u32[]{:S(2)}) collective-permute-start(bf16[64,256]{1,0:T(8,128)(2,1)S(1)} %get-tuple-element.35), channel_id=1, source_target_pairs={{4,8},{5,9},{6,10},{7,11},{8,12},{9,13},{10,14},{11,15},{20,24},{2... | collective-permute-start | bytes 98312 | tf_op jit(solution)/shard_map/ppermute | solution.py:515
  42.0 0.0 collective-permute-done.10.got
  42.0 0.7 %collective-permute-start.11 = (bf16[256,256]{1,0:T(8,128)(2,1)S(1)}, bf16[256,256]{1,0:T(8,128)(2,1)S(1)}, u32[]{:S(2)}, u32[]{:S(2)}) collective-permute-start(bf16[256,256]{1,0:T(8,128)(2,1)S(1)} %collective-permute-done.10.got), channel_id=1, source_target_pairs={{8,9},{9,8},{10,11},{11,10},{12,13},{13,12},{14,15},{15,14},{24,25... | collective-permute-start | bytes 393224 | tf_op jit(solution)/shard_map/ppermute | solution.py:510
  42.6 0.1 image_and_maps.3
  42.8 0.0 collective-permute-done.6.third
  42.8 0.1 collective-permute-done.8.second
  42.9 0.0 collective-permute-done.9.far_one
  42.9 0.0 collective-permute-done.11.other
  42.9 0.7 %entering.1 = (bf16[64,256]{1,0:T(8,128)(2,1)S(1)}, bf16[64,256]{1,0:T(8,128)(2,1)S(1)}, bf16[64,256]{1,0:T(8,128)(2,1)S(1)}, bf16[64,256]{1,0:T(8,128)(2,1)S(1)}) custom-call(bf16[64,256]{1,0:T(8,128)(2,1)S(1)} %collective-permute-done.6.third, bf16[64,256]{1,0:T(8,128)(2,1)S(1)} %collective-permute-done.7.near_one, ...), custom_call_target="tpu_custom_call" | custom-call | flops 1610000000 | tf_op jit(solution)/shard_map/entering/pallas_call | solution.py:435
  43.6 0.5 collective-permute-start.12
  44.1 0.5 %collective-permute-start.13 = (bf16[64,256]{1,0:T(8,128)(2,1)S(1)}, bf16[64,256]{1,0:T(8,128)(2,1)S(1)}, u32[]{:S(2)}, u32[]{:S(2)}) collective-permute-start(bf16[64,256]{1,0:T(8,128)(2,1)S(1)} %get-tuple-element.42), channel_id=1, source_target_pairs={{0,2},{1,3},{2,0},{3,1},{4,6},{5,7},{6,4},{7,5},{8,10},{9,11},{10,... | collective-permute-start | bytes 98312 | tf_op jit(solution)/shard_map/ppermute | solution.py:487
  44.6 1.0 %collective-permute-start.14 = (bf16[64,256]{1,0:T(8,128)(2,1)S(1)}, bf16[64,256]{1,0:T(8,128)(2,1)S(1)}, u32[]{:S(2)}, u32[]{:S(2)}) collective-permute-start(bf16[64,256]{1,0:T(8,128)(2,1)S(1)} %get-tuple-element.43), channel_id=1, source_target_pairs={{0,1},{1,0},{2,3},{3,2},{4,5},{5,4},{6,7},{7,6},{8,9},{9,8},{10,11... | collective-permute-start | bytes 98312 | tf_op jit(solution)/shard_map/ppermute | solution.py:483
  45.5 1.9 %prop.1 = bf16[2,1024,256]{2,1,0:T(8,128)(2,1)S(1)} custom-call(s32[2,8]{1,0:T(2,128)S(1)} %bitcast.19, bf16[2,1024,1024]{2,1,0:T(8,128)(2,1)S(1)} %bitcast.13, bf16[1024,256]{1,0:T(8,128)(2,1)S(1)} %bitcast.17, bf16[64,256]{1,0:T(8,128)(2,1)S(1)} %get-tuple-element.40._tie.own), custom_call_target="tpu_custom_call" | custom-call | flops 1724999936 | tf_op jit(solution)/shard_map/prop/pallas_call | solution.py:219
  47.4 0.0 collective-permute-done.12.far
  47.4 0.5 %collective-permute-done.13.across = bf16[64,256]{1,0:T(8,128)(2,1)S(1)} collective-permute-done((bf16[64,256]{1,0:T(8,128)(2,1)S(1)}, bf16[64,256]{1,0:T(8,128)(2,1)S(1)}, u32[]{:S(2)}, u32[]{:S(2)}) %collective-permute-start.13) | collective-permute-done | bytes 32800 | tf_op jit(solution)/shard_map/ppermute | solution.py:487
  48.0 0.0 collective-permute-done.14.near
  48.0 1.2 %waves.1 = bf16[2,1024,128]{2,1,0:T(8,128)(2,1)} custom-call(bf16[64,256]{1,0:T(8,128)(2,1)S(1)} %get-tuple-element.40._tie.own, bf16[64,256]{1,0:T(8,128)(2,1)S(1)} %collective-permute-done.12.far, bf16[64,256]{1,0:T(8,128)(2,1)S(1)} %collective-permute-done.13.across, bf16[64,256]{1,0:T(8,128)(2,1)S(1)} %collective-permute-done.14.near, ...), custom_call_target="tpu_custom_call" | custom-call | flops 1495000064 | tf_op jit(solution)/shard_map/waves/pallas_call | solution.py:466
  (10 shorter events, 0.0 us)
Async XLA Ops:
  0.0 12.0 %copy-start.3 = (bf16[1,1024,256]{2,1,0:T(8,128)(2,1)S(1)}, bf16[1,1024,256]{2,1,0:T(8,128)(2,1)}, u32[]{:S(2)}) copy-start(bf16[1,1024,256]{2,1,0:T(8,128)(2,1)} %param.8) | copy-start | bytes 1572868
  0.0 12.0 %copy-start.4 = (s32[1,8,2]{1,2,0:T(2,128)S(1)}, s32[1,8,2]{1,2,0:T(2,128)}, u32[]{:S(2)}) copy-start(s32[1,8,2]{1,2,0:T(2,128)} %param.9) | copy-start | bytes 196
  4.5 22.6 %copy-start.2 = (bf16[1,2,1024,128]{3,2,1,0:T(8,128)(2,1)S(1)}, bf16[1,2,1024,128]{3,2,1,0:T(8,128)(2,1)}, u32[]{:S(2)}) copy-start(bf16[1,2,1024,128]{3,2,1,0:T(8,128)(2,1)} %param.7) | copy-start | bytes 1572868
  4.5 22.6 %all-to-all-start = ((bf16[16,136,128]{2,1,0:T(8,128)(2,1)}), bf16[16,136,128]{2,1,0:T(8,128)(2,1)S(1)}, u32[]{:S(2)}, u32[]{:S(2)}) async-start(bf16[16,136,128]{2,1,0:T(8,128)(2,1)} %pairs.1), calls=%async_computation | async-start | bytes 1114112 | tf_op jit(solution)/shard_map/all_to_all | solution.py:537
  12.1 2.2 %copy-start = (bf16[1,2,1024,1024]{3,2,1,0:T(8,128)(2,1)S(1)}, bf16[1,2,1024,1024]{3,2,1,0:T(8,128)(2,1)}, u32[]{:S(2)}) copy-start(bf16[1,2,1024,1024]{3,2,1,0:T(8,128)(2,1)} %param.6) | copy-start | bytes 12582916
  15.4 0.8 %copy-start.5 = (bf16[256,1024]{1,0:T(8,128)(2,1)}, bf16[256,1024]{1,0:T(8,128)(2,1)S(1)}, u32[]{:S(2)}) copy-start(bf16[256,1024]{1,0:T(8,128)(2,1)S(1)} %get-tuple-element.26.refs_1_) | copy-start | bytes 1572868
  16.2 12.5 %collective-permute-start.3 = (f32[256,256]{1,0:T(8,128)S(1)}, f32[256,256]{1,0:T(8,128)S(1)}, u32[]{:S(2)}, u32[]{:S(2)}) collective-permute-start(f32[256,256]{1,0:T(8,128)S(1)} %get-tuple-element.32), channel_id=1, source_target_pairs={{0,2},{1,3},{2,0},{3,1},{4,6},{5,7},{6,4},{7,5},{8,10},{9,11},{10,... | collective-permute-start | bytes 786440 | tf_op jit(solution)/shard_map/ppermute | solution.py:487
  18.1 12.8 %collective-permute-start.5 = (f32[256,256]{1,0:T(8,128)S(1)}, f32[256,256]{1,0:T(8,128)S(1)}, u32[]{:S(2)}, u32[]{:S(2)}) collective-permute-start(f32[256,256]{1,0:T(8,128)S(1)} %get-tuple-element.31.own), channel_id=1, source_target_pairs={{0,1},{1,0},{2,3},{3,2},{4,5},{5,4},{6,7},{7,6},{8,9},{9,8},{10,11... | collective-permute-start | bytes 786440 | tf_op jit(solution)/shard_map/ppermute | solution.py:483
  27.1 1.0 %copy-start.6 = (bf16[256,1024]{1,0:T(8,128)(2,1)S(1)}, bf16[256,1024]{1,0:T(8,128)(2,1)}, u32[]{:S(2)}) copy-start(bf16[256,1024]{1,0:T(8,128)(2,1)} %copy-done.5) | copy-start | bytes 1572868
  28.0 3.7 %copy-start.1 = (bf16[1,2,1024,1024]{3,2,1,0:T(8,128)(2,1)S(1)}, bf16[1,2,1024,1024]{3,2,1,0:T(8,128)(2,1)}, u32[]{:S(2)}) copy-start(bf16[1,2,1024,1024]{3,2,1,0:T(8,128)(2,1)} %param.6) | copy-start | bytes 12582916
  28.7 2.2 %collective-permute-start.4 = (f32[256,256]{1,0:T(8,128)S(1)}, f32[256,256]{1,0:T(8,128)S(1)}, u32[]{:S(2)}, u32[]{:S(2)}) collective-permute-start(f32[256,256]{1,0:T(8,128)S(1)} %after_exchange.1.across), channel_id=1, source_target_pairs={{0,1},{1,0},{2,3},{3,2},{4,5},{5,4},{6,7},{7,6},{8,9},{9,8},{10,11... | collective-permute-start | bytes 786440 | tf_op jit(solution)/shard_map/ppermute | solution.py:483
  28.8 5.5 %collective-permute-start = (bf16[64,256]{1,0:T(8,128)(2,1)S(1)}, bf16[64,256]{1,0:T(8,128)(2,1)S(1)}, u32[]{:S(2)}, u32[]{:S(2)}) collective-permute-start(bf16[64,256]{1,0:T(8,128)(2,1)S(1)} %get-tuple-element.28), channel_id=1, source_target_pairs={{0,3},{1,2},{2,1},{3,0},{4,7},{5,6},{6,5},{7,4},{8,11},{9,10},{10,... | collective-permute-start | bytes 98312 | tf_op jit(solution)/shard_map/ppermute | solution.py:491
  29.6 4.6 %collective-permute-start.1 = (bf16[64,256]{1,0:T(8,128)(2,1)S(1)}, bf16[64,256]{1,0:T(8,128)(2,1)S(1)}, u32[]{:S(2)}, u32[]{:S(2)}) collective-permute-start(bf16[64,256]{1,0:T(8,128)(2,1)S(1)} %get-tuple-element.29), channel_id=1, source_target_pairs={{0,2},{1,3},{2,0},{3,1},{4,6},{5,7},{6,4},{7,5},{8,10},{9,11},{10,... | collective-permute-start | bytes 98312 | tf_op jit(solution)/shard_map/ppermute | solution.py:487
  30.9 3.3 %collective-permute-start.2 = (bf16[64,256]{1,0:T(8,128)(2,1)S(1)}, bf16[64,256]{1,0:T(8,128)(2,1)S(1)}, u32[]{:S(2)}, u32[]{:S(2)}) collective-permute-start(bf16[64,256]{1,0:T(8,128)(2,1)S(1)} %get-tuple-element.30), channel_id=1, source_target_pairs={{0,1},{1,0},{2,3},{3,2},{4,5},{5,4},{6,7},{7,6},{8,9},{9,8},{10,11... | collective-permute-start | bytes 98312 | tf_op jit(solution)/shard_map/ppermute | solution.py:483
  33.5 8.4 %collective-permute-start.10 = (bf16[256,256]{1,0:T(8,128)(2,1)S(1)}, bf16[256,256]{1,0:T(8,128)(2,1)S(1)}, u32[]{:S(2)}, u32[]{:S(2)}) collective-permute-start(bf16[256,256]{1,0:T(8,128)(2,1)S(1)} %get-tuple-element.36), channel_id=1, source_target_pairs={{4,8},{8,12},{5,13},{6,10},{10,14},{7,15},{20,24},{24,28},{21,29},... | collective-permute-start | bytes 393224 | tf_op jit(solution)/shard_map/ppermute | solution.py:509
  34.9 7.9 %collective-permute-start.6 = (bf16[64,256]{1,0:T(8,128)(2,1)S(1)}, bf16[64,256]{1,0:T(8,128)(2,1)S(1)}, u32[]{:S(2)}, u32[]{:S(2)}) collective-permute-start(bf16[64,256]{1,0:T(8,128)(2,1)S(1)} %get-tuple-element.35), channel_id=1, source_target_pairs={{0,12},{1,13},{2,14},{3,15},{16,28},{17,29},{18,30},{19,31}} | collective-permute-start | bytes 98312 | tf_op jit(solution)/shard_map/ppermute | solution.py:515
  38.7 4.1 %collective-permute-start.7 = (bf16[64,256]{1,0:T(8,128)(2,1)S(1)}, bf16[64,256]{1,0:T(8,128)(2,1)S(1)}, u32[]{:S(2)}, u32[]{:S(2)}) collective-permute-start(bf16[64,256]{1,0:T(8,128)(2,1)S(1)} %get-tuple-element.35), channel_id=1, source_target_pairs={{0,4},{1,5},{2,6},{3,7},{16,20},{17,21},{18,22},{19,23}} | collective-permute-start | bytes 98312 | tf_op jit(solution)/shard_map/ppermute | solution.py:515
  40.0 2.9 %collective-permute-start.8 = (bf16[64,256]{1,0:T(8,128)(2,1)S(1)}, bf16[64,256]{1,0:T(8,128)(2,1)S(1)}, u32[]{:S(2)}, u32[]{:S(2)}) collective-permute-start(bf16[64,256]{1,0:T(8,128)(2,1)S(1)} %get-tuple-element.35), channel_id=1, source_target_pairs={{0,8},{1,9},{2,10},{3,11},{4,12},{5,13},{6,14},{7,15},{16,24},{17,... | collective-permute-start | bytes 98312 | tf_op jit(solution)/shard_map/ppermute | solution.py:515
  41.3 1.6 %collective-permute-start.9 = (bf16[64,256]{1,0:T(8,128)(2,1)S(1)}, bf16[64,256]{1,0:T(8,128)(2,1)S(1)}, u32[]{:S(2)}, u32[]{:S(2)}) collective-permute-start(bf16[64,256]{1,0:T(8,128)(2,1)S(1)} %get-tuple-element.35), channel_id=1, source_target_pairs={{4,8},{5,9},{6,10},{7,11},{8,12},{9,13},{10,14},{11,15},{20,24},{2... | collective-permute-start | bytes 98312 | tf_op jit(solution)/shard_map/ppermute | solution.py:515
  42.0 0.9 %collective-permute-start.11 = (bf16[256,256]{1,0:T(8,128)(2,1)S(1)}, bf16[256,256]{1,0:T(8,128)(2,1)S(1)}, u32[]{:S(2)}, u32[]{:S(2)}) collective-permute-start(bf16[256,256]{1,0:T(8,128)(2,1)S(1)} %collective-permute-done.10.got), channel_id=1, source_target_pairs={{8,9},{9,8},{10,11},{11,10},{12,13},{13,12},{14,15},{15,14},{24,25... | collective-permute-start | bytes 393224 | tf_op jit(solution)/shard_map/ppermute | solution.py:510
  43.6 3.8 %collective-permute-start.12 = (bf16[64,256]{1,0:T(8,128)(2,1)S(1)}, bf16[64,256]{1,0:T(8,128)(2,1)S(1)}, u32[]{:S(2)}, u32[]{:S(2)}) collective-permute-start(bf16[64,256]{1,0:T(8,128)(2,1)S(1)} %get-tuple-element.41), channel_id=1, source_target_pairs={{0,3},{1,2},{2,1},{3,0},{4,7},{5,6},{6,5},{7,4},{8,11},{9,10},{10,... | collective-permute-start | bytes 98312 | tf_op jit(solution)/shard_map/ppermute | solution.py:491
  44.1 3.9 %collective-permute-start.13 = (bf16[64,256]{1,0:T(8,128)(2,1)S(1)}, bf16[64,256]{1,0:T(8,128)(2,1)S(1)}, u32[]{:S(2)}, u32[]{:S(2)}) collective-permute-start(bf16[64,256]{1,0:T(8,128)(2,1)S(1)} %get-tuple-element.42), channel_id=1, source_target_pairs={{0,2},{1,3},{2,0},{3,1},{4,6},{5,7},{6,4},{7,5},{8,10},{9,11},{10,... | collective-permute-start | bytes 98312 | tf_op jit(solution)/shard_map/ppermute | solution.py:487
  44.6 3.4 %collective-permute-start.14 = (bf16[64,256]{1,0:T(8,128)(2,1)S(1)}, bf16[64,256]{1,0:T(8,128)(2,1)S(1)}, u32[]{:S(2)}, u32[]{:S(2)}) collective-permute-start(bf16[64,256]{1,0:T(8,128)(2,1)S(1)} %get-tuple-element.43), channel_id=1, source_target_pairs={{0,1},{1,0},{2,3},{3,2},{4,5},{5,4},{6,7},{7,6},{8,9},{9,8},{10,11... | collective-permute-start | bytes 98312 | tf_op jit(solution)/shard_map/ppermute | solution.py:483

commit v30 on v29

--- a/solution.py
+++ b/solution.py
@@ -507,7 +507,7 @@
         else:
             pairs += [(GROUP + i, 3 * GROUP + i)]
     got = lax.ppermute(total_map, "sec", pairs)
-    return got, lax.ppermute(got, "sec", [(s, s ^ 1) for s in range(2 * GROUP, sections)])
+    return got, to_near(got, sections)
 
 
 def between(item, *planes):

time: 49.5 us -> 50.1 us (1.012)
  waiting for transfers between devices: 9.65 us -> 10.9 us
  starting transfers between devices: 22 us -> 21.4 us
    ppermute x4 -> x5, starting transfers between devices: 1.03 us -> 0.22 us  [to_near(): return lax.ppermute(item, 'sec', [(s, s ^ 1) for s in range(sections)])]
    ppermute x3, starting transfers between devices: 3.68 us -> 4.44 us  [to_across(): lax.ppermute(item, 'sec', [(s, s // GROUP * GROUP + (s % GROUP + CORES) %...]
    ppermute x1 -> x0, starting transfers between devices: 0.67 us -> none  [maps_up(): lax.ppermute(got, 'sec', [(s, s ^ 1) for s in range(2 * GROUP, sections)])]
    ppermute x4, waiting for transfers between devices: 0.08 us -> 0.67 us  [between(): return lax.ppermute(item, 'sec', pairs)]
    ppermute x4 -> x5, waiting for transfers between devices: 0.01 us -> 0.52 us  [to_near(): return lax.ppermute(item, 'sec', [(s, s ^ 1) for s in range(sections)])]
  transfers between devices with their start and end apart: 16 -> 16, of which waited for: 3 -> 4; matrix products, arithmetic and copies ran while one was open for 0% -> 0% of each run, Pallas kernels for 16% -> 16%
where the time goes in v30:
time: 50.1 us; the launch traced here: 49.8 us
  starting transfers between devices  21.4 us (43%)
  Pallas kernels  14 us (28%)
  waiting for transfers between devices  10.9 us (22%)
  local copies, waits for them, and re-layouts  3.11 us (6%)
    all_to_all x1, waiting for transfers between devices, per_device(): lax.all_to_all(outgoing, 'sec', split_axis=0, concat_axis=0, tiled=True)  9.01 us
    all_to_all x1, starting transfers between devices, per_device(): lax.all_to_all(outgoing, 'sec', split_axis=0, concat_axis=0, tiled=True)  7.55 us
    ppermute x4, starting transfers between devices, between(): return lax.ppermute(item, 'sec', pairs)  7.06 us
    ppermute x3, starting transfers between devices, to_across(): lax.ppermute(item, 'sec', [(s, s // GROUP * GROUP + (s % GROUP + CORES) %...  4.44 us
    pallas_call x1, Pallas kernels, outgoing_pairs(): call(pairs_kernel, 'pairs', [IN_HBM] * 4, shape(sections, CAP * energies...  4.38 us
    unnamed x14, local copies, waits for them, and re-layouts  3.11 us
    pallas_call x2, Pallas kernels, image_and_maps(): call(functools.partial(work_kernel, not held), 'image_and_maps', [IN_VMEM...  1.91 us
    pallas_call x1, Pallas kernels, propagator(): call(prop_kernel, 'prop', [IN_SMEM, IN_VMEM, IN_VMEM, IN_PLACE], shape(en...  1.9 us
  transfers between devices with their start and end apart: 16, of which 4 were waited for; matrix products, arithmetic and copies ran while one was open for 0% of the time, Pallas kernels for 16%

profile of v30, /device:TPU:0, one launch (start us, length us, event | category | flops | bytes accessed | tf_op | source)
XLA Modules:
  0.0 49.8 jit_solution(9353910426136893492)
XLA Ops:
  0.0 4.4 %pairs.1 = bf16[16,136,128]{2,1,0:T(8,128)(2,1)} custom-call(s32[16]{0:T(128)} %bitcast.21, s32[2,16]{1,0:T(2,128)} %bitcast.20, bf16[2,1024,1024]{2,1,0:T(8,128)(2,1)} %bitcast.9, bf16[2,1024,128]{2,1,0:T(8,128)(2,1)} %bitcast.14), custom_call_target="tpu_custom_call" | custom-call | flops 4600000000 | tf_op jit(solution)/shard_map/pairs/pallas_call | solution.py:161
  4.4 0.0 copy-start.2
  4.4 7.5 %all-to-all-start = ((bf16[16,136,128]{2,1,0:T(8,128)(2,1)}), bf16[16,136,128]{2,1,0:T(8,128)(2,1)S(1)}, u32[]{:S(2)}, u32[]{:S(2)}) async-start(bf16[16,136,128]{2,1,0:T(8,128)(2,1)} %pairs.1), calls=%async_computation | async-start | bytes 1114112 | tf_op jit(solution)/shard_map/all_to_all | solution.py:537
  12.0 0.0 copy-start
  12.0 2.2 %copy-done = bf16[1,2,1024,1024]{3,2,1,0:T(8,128)(2,1)S(1)} copy-done((bf16[1,2,1024,1024]{3,2,1,0:T(8,128)(2,1)S(1)}, bf16[1,2,1024,1024]{3,2,1,0:T(8,128)(2,1)}, u32[]{:S(2)}) %copy-start) | copy-done | bytes 4194328
  14.2 1.1 %face_maps.1 = (f32[256,256]{1,0:T(8,128)S(1)}, f32[256,256]{1,0:T(8,128)S(1)}, bf16[256,1024]{1,0:T(8,128)(2,1)S(1)}, bf16[256,1024]{1,0:T(8,128)(2,1)S(1)}) custom-call(s32[2,8]{1,0:T(2,128)S(1)} %bitcast.18, bf16[2,1024,1024]{2,1,0:T(8,128)(2,1)S(1)} %bitcast.10, bf16[1024,256]{1,0:T(8,128)(2,1)S(1)} %bitcast.16), custom_call_target="tpu_custom_call" | custom-call | flops 1380000000 | tf_op jit(solution)/shard_map/face_maps/pallas_call | solution.py:200
  15.3 0.0 copy-start.5
  15.3 0.8 %copy-done.5 = bf16[256,1024]{1,0:T(8,128)(2,1)} copy-done((bf16[256,1024]{1,0:T(8,128)(2,1)}, bf16[256,1024]{1,0:T(8,128)(2,1)S(1)}, u32[]{:S(2)}) %copy-start.5) | copy-done | bytes 524312
  16.1 1.9 %collective-permute-start.3 = (f32[256,256]{1,0:T(8,128)S(1)}, f32[256,256]{1,0:T(8,128)S(1)}, u32[]{:S(2)}, u32[]{:S(2)}) collective-permute-start(f32[256,256]{1,0:T(8,128)S(1)} %get-tuple-element.32), channel_id=1, source_target_pairs={{0,2},{1,3},{2,0},{3,1},{4,6},{5,7},{6,4},{7,5},{8,10},{9,11},{10,... | collective-permute-start | bytes 786440 | tf_op jit(solution)/shard_map/ppermute | solution.py:487
  18.0 0.0 collective-permute-start.5
  18.0 9.0 %all-to-all-done.received = bf16[16,136,128]{2,1,0:T(8,128)(2,1)S(1)} async-done(((bf16[16,136,128]{2,1,0:T(8,128)(2,1)}), bf16[16,136,128]{2,1,0:T(8,128)(2,1)S(1)}, u32[]{:S(2)}, u32[]{:S(2)}) %all-to-all-start) | async-done | bytes 557088 | tf_op jit(solution)/shard_map/all_to_all | solution.py:537
  27.0 0.9 %source.1.refs_1_ = bf16[2,1024,128]{2,1,0:T(8,128)(2,1)S(1)} custom-call(bf16[16,136,128]{2,1,0:T(8,128)(2,1)S(1)} %all-to-all-done.received, bf16[2,1024,128]{2,1,0:T(8,128)(2,1)S(1)} %bitcast.15), custom_call_target="tpu_custom_call" | custom-call | flops 1150000000 | tf_op jit(solution)/shard_map/source/pallas_call | solution.py:286
  27.9 0.0 copy-start.1
  28.0 0.1 copy-done.6
  28.1 0.5 %face_quarters.1 = (bf16[64,256]{1,0:T(8,128)(2,1)S(1)}, bf16[64,256]{1,0:T(8,128)(2,1)S(1)}, bf16[64,256]{1,0:T(8,128)(2,1)S(1)}, bf16[64,256]{1,0:T(8,128)(2,1)S(1)}) custom-call(bf16[2,1024,128]{2,1,0:T(8,128)(2,1)S(1)} %source.1.refs_1_, bf16[256,1024]{1,0:T(8,128)(2,1)S(1)} %get-tuple-element.25.refs_0_, bf16[256,1024]{1,0:T(8,128)(2,1)S(1)} %copy-done.6), custom_call_target="tpu_custom_call" | custom-call | flops 690000000 | tf_op jit(solution)/shard_map/face_quarters/pallas_call | solution.py:319
  28.6 0.0 collective-permute-done.3._map
  28.6 0.1 collective-permute-start.4
  28.7 0.9 %collective-permute-start = (bf16[64,256]{1,0:T(8,128)(2,1)S(1)}, bf16[64,256]{1,0:T(8,128)(2,1)S(1)}, u32[]{:S(2)}, u32[]{:S(2)}) collective-permute-start(bf16[64,256]{1,0:T(8,128)(2,1)S(1)} %get-tuple-element.28), channel_id=1, source_target_pairs={{0,3},{1,2},{2,1},{3,0},{4,7},{5,6},{6,5},{7,4},{8,11},{9,10},{10,... | collective-permute-start | bytes 98312 | tf_op jit(solution)/shard_map/ppermute | solution.py:491
  29.6 1.3 %collective-permute-start.1 = (bf16[64,256]{1,0:T(8,128)(2,1)S(1)}, bf16[64,256]{1,0:T(8,128)(2,1)S(1)}, u32[]{:S(2)}, u32[]{:S(2)}) collective-permute-start(bf16[64,256]{1,0:T(8,128)(2,1)S(1)} %get-tuple-element.29), channel_id=1, source_target_pairs={{0,2},{1,3},{2,0},{3,1},{4,6},{5,7},{6,4},{7,5},{8,10},{9,11},{10,... | collective-permute-start | bytes 98312 | tf_op jit(solution)/shard_map/ppermute | solution.py:487
  30.8 0.0 collective-permute-start.2
  30.8 0.0 collective-permute-done.5.near
  30.8 0.0 collective-permute-done.4.far
  30.8 0.8 %chain_maps.1 = (bf16[256,256]{1,0:T(8,128)(2,1)S(1)}, bf16[2,4,256,256]{3,2,1,0:T(8,128)(2,1)S(1)}) custom-call(f32[256,256]{1,0:T(8,128)S(1)} %get-tuple-element.31.own, f32[256,256]{1,0:T(8,128)S(1)} %collective-permute-done.4.far, f32[256,256]{1,0:T(8,128)S(1)} %after_exchange.1.across, f32[256,256]{1,0:T(8,128)S(1)} %collective-permute-done.5.near), custom_call_target="tpu_custom_call" | custom-call | flops 1035000000 | tf_op jit(solution)/shard_map/chain_maps/pallas_call | solution.py:245
  31.7 1.8 %image_and_maps.2 = (f32[2,1024,128]{2,1,0:T(8,128)S(1)}, bf16[2,2,256,256]{3,2,1,0:T(8,128)(2,1)S(1)}) custom-call(bf16[2,1024,1024]{2,1,0:T(8,128)(2,1)S(1)} %bitcast.11, bf16[2,1024,128]{2,1,0:T(8,128)(2,1)S(1)} %source.1.refs_1_, bf16[2,4,256,256]{3,2,1,0:T(8,128)(2,1)S(1)} %get-tuple-element.33.refs_2_.parts), custom_call_target="tpu_custom_call" | custom-call | flops 2300000000 | tf_op jit(solution)/shard_map/image_and_maps/pallas_call | solution.py:395
  33.5 0.7 %collective-permute-start.10 = (bf16[256,256]{1,0:T(8,128)(2,1)S(1)}, bf16[256,256]{1,0:T(8,128)(2,1)S(1)}, u32[]{:S(2)}, u32[]{:S(2)}) collective-permute-start(bf16[256,256]{1,0:T(8,128)(2,1)S(1)} %get-tuple-element.36), channel_id=1, source_target_pairs={{4,8},{8,12},{5,13},{6,10},{10,14},{7,15},{20,24},{24,28},{21,29},... | collective-permute-start | bytes 393224 | tf_op jit(solution)/shard_map/ppermute | solution.py:509
  34.2 0.0 collective-permute-done.far
  34.2 0.0 collective-permute-done.1.across
  34.2 0.0 collective-permute-done.2.near
  34.2 0.6 %plane_total.1 = (bf16[64,256]{1,0:T(8,128)(2,1)S(1)}, f32[3,64,256]{2,1,0:T(8,128)S(1)}) custom-call(bf16[64,256]{1,0:T(8,128)(2,1)S(1)} %get-tuple-element.27._packets.own, bf16[64,256]{1,0:T(8,128)(2,1)S(1)} %collective-permute-done.far, bf16[64,256]{1,0:T(8,128)(2,1)S(1)} %collective-permute-done.1.across, ...), custom_call_target="tpu_custom_call" | custom-call | flops 3449999872 | tf_op jit(solution)/shard_map/plane_total/pallas_call | solution.py:361
  34.8 3.8 %collective-permute-start.6 = (bf16[64,256]{1,0:T(8,128)(2,1)S(1)}, bf16[64,256]{1,0:T(8,128)(2,1)S(1)}, u32[]{:S(2)}, u32[]{:S(2)}) collective-permute-start(bf16[64,256]{1,0:T(8,128)(2,1)S(1)} %get-tuple-element.35), channel_id=1, source_target_pairs={{0,12},{1,13},{2,14},{3,15},{16,28},{17,29},{18,30},{19,31}} | collective-permute-start | bytes 98312 | tf_op jit(solution)/shard_map/ppermute | solution.py:515
  38.6 1.3 %collective-permute-start.7 = (bf16[64,256]{1,0:T(8,128)(2,1)S(1)}, bf16[64,256]{1,0:T(8,128)(2,1)S(1)}, u32[]{:S(2)}, u32[]{:S(2)}) collective-permute-start(bf16[64,256]{1,0:T(8,128)(2,1)S(1)} %get-tuple-element.35), channel_id=1, source_target_pairs={{0,4},{1,5},{2,6},{3,7},{16,20},{17,21},{18,22},{19,23}} | collective-permute-start | bytes 98312 | tf_op jit(solution)/shard_map/ppermute | solution.py:515
  39.9 1.3 %collective-permute-start.8 = (bf16[64,256]{1,0:T(8,128)(2,1)S(1)}, bf16[64,256]{1,0:T(8,128)(2,1)S(1)}, u32[]{:S(2)}, u32[]{:S(2)}) collective-permute-start(bf16[64,256]{1,0:T(8,128)(2,1)S(1)} %get-tuple-element.35), channel_id=1, source_target_pairs={{0,8},{1,9},{2,10},{3,11},{4,12},{5,13},{6,14},{7,15},{16,24},{17,... | collective-permute-start | bytes 98312 | tf_op jit(solution)/shard_map/ppermute | solution.py:515
  41.2 0.7 %collective-permute-start.9 = (bf16[64,256]{1,0:T(8,128)(2,1)S(1)}, bf16[64,256]{1,0:T(8,128)(2,1)S(1)}, u32[]{:S(2)}, u32[]{:S(2)}) collective-permute-start(bf16[64,256]{1,0:T(8,128)(2,1)S(1)} %get-tuple-element.35), channel_id=1, source_target_pairs={{4,8},{5,9},{6,10},{7,11},{8,12},{9,13},{10,14},{11,15},{20,24},{2... | collective-permute-start | bytes 98312 | tf_op jit(solution)/shard_map/ppermute | solution.py:515
  41.9 0.0 collective-permute-done.10.got
  41.9 0.1 collective-permute-start.11
  42.0 0.1 image_and_maps.3
  42.1 0.0 collective-permute-done.6.third
  42.1 0.7 %collective-permute-done.8.second = bf16[64,256]{1,0:T(8,128)(2,1)S(1)} collective-permute-done((bf16[64,256]{1,0:T(8,128)(2,1)S(1)}, bf16[64,256]{1,0:T(8,128)(2,1)S(1)}, u32[]{:S(2)}, u32[]{:S(2)}) %collective-permute-start.8) | collective-permute-done | bytes 32800 | tf_op jit(solution)/shard_map/ppermute | solution.py:515
  42.8 0.0 collective-permute-done.9.far_one
  42.8 0.5 %collective-permute-done.11.other = bf16[256,256]{1,0:T(8,128)(2,1)S(1)} collective-permute-done((bf16[256,256]{1,0:T(8,128)(2,1)S(1)}, bf16[256,256]{1,0:T(8,128)(2,1)S(1)}, u32[]{:S(2)}, u32[]{:S(2)}) %collective-permute-start.11) | collective-permute-done | bytes 131104 | tf_op jit(solution)/shard_map/ppermute | solution.py:483
  43.3 0.7 %entering.1 = (bf16[64,256]{1,0:T(8,128)(2,1)S(1)}, bf16[64,256]{1,0:T(8,128)(2,1)S(1)}, bf16[64,256]{1,0:T(8,128)(2,1)S(1)}, bf16[64,256]{1,0:T(8,128)(2,1)S(1)}) custom-call(bf16[64,256]{1,0:T(8,128)(2,1)S(1)} %collective-permute-done.6.third, bf16[64,256]{1,0:T(8,128)(2,1)S(1)} %collective-permute-done.7.near_one, ...), custom_call_target="tpu_custom_call" | custom-call | flops 1610000000 | tf_op jit(solution)/shard_map/entering/pallas_call | solution.py:435
  44.0 0.6 %collective-permute-start.12 = (bf16[64,256]{1,0:T(8,128)(2,1)S(1)}, bf16[64,256]{1,0:T(8,128)(2,1)S(1)}, u32[]{:S(2)}, u32[]{:S(2)}) collective-permute-start(bf16[64,256]{1,0:T(8,128)(2,1)S(1)} %get-tuple-element.41), channel_id=1, source_target_pairs={{0,3},{1,2},{2,1},{3,0},{4,7},{5,6},{6,5},{7,4},{8,11},{9,10},{10,... | collective-permute-start | bytes 98312 | tf_op jit(solution)/shard_map/ppermute | solution.py:491
  44.6 1.3 %collective-permute-start.13 = (bf16[64,256]{1,0:T(8,128)(2,1)S(1)}, bf16[64,256]{1,0:T(8,128)(2,1)S(1)}, u32[]{:S(2)}, u32[]{:S(2)}) collective-permute-start(bf16[64,256]{1,0:T(8,128)(2,1)S(1)} %get-tuple-element.42), channel_id=1, source_target_pairs={{0,2},{1,3},{2,0},{3,1},{4,6},{5,7},{6,4},{7,5},{8,10},{9,11},{10,... | collective-permute-start | bytes 98312 | tf_op jit(solution)/shard_map/ppermute | solution.py:487
  45.9 0.1 collective-permute-start.14
  46.0 1.9 %prop.1 = bf16[2,1024,256]{2,1,0:T(8,128)(2,1)S(1)} custom-call(s32[2,8]{1,0:T(2,128)S(1)} %bitcast.19, bf16[2,1024,1024]{2,1,0:T(8,128)(2,1)S(1)} %bitcast.13, bf16[1024,256]{1,0:T(8,128)(2,1)S(1)} %bitcast.17, bf16[64,256]{1,0:T(8,128)(2,1)S(1)} %get-tuple-element.40._tie.own), custom_call_target="tpu_custom_call" | custom-call | flops 1724999936 | tf_op jit(solution)/shard_map/prop/pallas_call | solution.py:219
  47.9 0.0 collective-permute-done.12.far
  47.9 0.7 %collective-permute-done.13.across = bf16[64,256]{1,0:T(8,128)(2,1)S(1)} collective-permute-done((bf16[64,256]{1,0:T(8,128)(2,1)S(1)}, bf16[64,256]{1,0:T(8,128)(2,1)S(1)}, u32[]{:S(2)}, u32[]{:S(2)}) %collective-permute-start.13) | collective-permute-done | bytes 32800 | tf_op jit(solution)/shard_map/ppermute | solution.py:487
  48.6 1.2 %waves.1 = bf16[2,1024,128]{2,1,0:T(8,128)(2,1)} custom-call(bf16[64,256]{1,0:T(8,128)(2,1)S(1)} %get-tuple-element.40._tie.own, bf16[64,256]{1,0:T(8,128)(2,1)S(1)} %collective-permute-done.12.far, bf16[64,256]{1,0:T(8,128)(2,1)S(1)} %collective-permute-done.13.across, bf16[64,256]{1,0:T(8,128)(2,1)S(1)} %collective-permute-done.14.near, ...), custom_call_target="tpu_custom_call" | custom-call | flops 1495000064 | tf_op jit(solution)/shard_map/waves/pallas_call | solution.py:466
  (10 shorter events, 0.0 us)
Async XLA Ops:
  0.0 12.0 %copy-start.3 = (bf16[1,1024,256]{2,1,0:T(8,128)(2,1)S(1)}, bf16[1,1024,256]{2,1,0:T(8,128)(2,1)}, u32[]{:S(2)}) copy-start(bf16[1,1024,256]{2,1,0:T(8,128)(2,1)} %param.8) | copy-start | bytes 1572868
  0.0 12.0 %copy-start.4 = (s32[1,8,2]{1,2,0:T(2,128)S(1)}, s32[1,8,2]{1,2,0:T(2,128)}, u32[]{:S(2)}) copy-start(s32[1,8,2]{1,2,0:T(2,128)} %param.9) | copy-start | bytes 196
  4.4 22.6 %copy-start.2 = (bf16[1,2,1024,128]{3,2,1,0:T(8,128)(2,1)S(1)}, bf16[1,2,1024,128]{3,2,1,0:T(8,128)(2,1)}, u32[]{:S(2)}) copy-start(bf16[1,2,1024,128]{3,2,1,0:T(8,128)(2,1)} %param.7) | copy-start | bytes 1572868
  4.4 22.6 %all-to-all-start = ((bf16[16,136,128]{2,1,0:T(8,128)(2,1)}), bf16[16,136,128]{2,1,0:T(8,128)(2,1)S(1)}, u32[]{:S(2)}, u32[]{:S(2)}) async-start(bf16[16,136,128]{2,1,0:T(8,128)(2,1)} %pairs.1), calls=%async_computation | async-start | bytes 1114112 | tf_op jit(solution)/shard_map/all_to_all | solution.py:537
  12.0 2.2 %copy-start = (bf16[1,2,1024,1024]{3,2,1,0:T(8,128)(2,1)S(1)}, bf16[1,2,1024,1024]{3,2,1,0:T(8,128)(2,1)}, u32[]{:S(2)}) copy-start(bf16[1,2,1024,1024]{3,2,1,0:T(8,128)(2,1)} %param.6) | copy-start | bytes 12582916
  15.3 0.8 %copy-start.5 = (bf16[256,1024]{1,0:T(8,128)(2,1)}, bf16[256,1024]{1,0:T(8,128)(2,1)S(1)}, u32[]{:S(2)}) copy-start(bf16[256,1024]{1,0:T(8,128)(2,1)S(1)} %get-tuple-element.26.refs_1_) | copy-start | bytes 1572868
  16.1 12.5 %collective-permute-start.3 = (f32[256,256]{1,0:T(8,128)S(1)}, f32[256,256]{1,0:T(8,128)S(1)}, u32[]{:S(2)}, u32[]{:S(2)}) collective-permute-start(f32[256,256]{1,0:T(8,128)S(1)} %get-tuple-element.32), channel_id=1, source_target_pairs={{0,2},{1,3},{2,0},{3,1},{4,6},{5,7},{6,4},{7,5},{8,10},{9,11},{10,... | collective-permute-start | bytes 786440 | tf_op jit(solution)/shard_map/ppermute | solution.py:487
  18.0 12.8 %collective-permute-start.5 = (f32[256,256]{1,0:T(8,128)S(1)}, f32[256,256]{1,0:T(8,128)S(1)}, u32[]{:S(2)}, u32[]{:S(2)}) collective-permute-start(f32[256,256]{1,0:T(8,128)S(1)} %get-tuple-element.31.own), channel_id=1, source_target_pairs={{0,1},{1,0},{2,3},{3,2},{4,5},{5,4},{6,7},{7,6},{8,9},{9,8},{10,11... | collective-permute-start | bytes 786440 | tf_op jit(solution)/shard_map/ppermute | solution.py:483
  27.0 1.0 %copy-start.6 = (bf16[256,1024]{1,0:T(8,128)(2,1)S(1)}, bf16[256,1024]{1,0:T(8,128)(2,1)}, u32[]{:S(2)}) copy-start(bf16[256,1024]{1,0:T(8,128)(2,1)} %copy-done.5) | copy-start | bytes 1572868
  27.9 3.7 %copy-start.1 = (bf16[1,2,1024,1024]{3,2,1,0:T(8,128)(2,1)S(1)}, bf16[1,2,1024,1024]{3,2,1,0:T(8,128)(2,1)}, u32[]{:S(2)}) copy-start(bf16[1,2,1024,1024]{3,2,1,0:T(8,128)(2,1)} %param.6) | copy-start | bytes 12582916
  28.6 2.2 %collective-permute-start.4 = (f32[256,256]{1,0:T(8,128)S(1)}, f32[256,256]{1,0:T(8,128)S(1)}, u32[]{:S(2)}, u32[]{:S(2)}) collective-permute-start(f32[256,256]{1,0:T(8,128)S(1)} %after_exchange.1.across), channel_id=1, source_target_pairs={{0,1},{1,0},{2,3},{3,2},{4,5},{5,4},{6,7},{7,6},{8,9},{9,8},{10,11... | collective-permute-start | bytes 786440 | tf_op jit(solution)/shard_map/ppermute | solution.py:483
  28.7 5.5 %collective-permute-start = (bf16[64,256]{1,0:T(8,128)(2,1)S(1)}, bf16[64,256]{1,0:T(8,128)(2,1)S(1)}, u32[]{:S(2)}, u32[]{:S(2)}) collective-permute-start(bf16[64,256]{1,0:T(8,128)(2,1)S(1)} %get-tuple-element.28), channel_id=1, source_target_pairs={{0,3},{1,2},{2,1},{3,0},{4,7},{5,6},{6,5},{7,4},{8,11},{9,10},{10,... | collective-permute-start | bytes 98312 | tf_op jit(solution)/shard_map/ppermute | solution.py:491
  29.6 4.6 %collective-permute-start.1 = (bf16[64,256]{1,0:T(8,128)(2,1)S(1)}, bf16[64,256]{1,0:T(8,128)(2,1)S(1)}, u32[]{:S(2)}, u32[]{:S(2)}) collective-permute-start(bf16[64,256]{1,0:T(8,128)(2,1)S(1)} %get-tuple-element.29), channel_id=1, source_target_pairs={{0,2},{1,3},{2,0},{3,1},{4,6},{5,7},{6,4},{7,5},{8,10},{9,11},{10,... | collective-permute-start | bytes 98312 | tf_op jit(solution)/shard_map/ppermute | solution.py:487
  30.8 3.4 %collective-permute-start.2 = (bf16[64,256]{1,0:T(8,128)(2,1)S(1)}, bf16[64,256]{1,0:T(8,128)(2,1)S(1)}, u32[]{:S(2)}, u32[]{:S(2)}) collective-permute-start(bf16[64,256]{1,0:T(8,128)(2,1)S(1)} %get-tuple-element.30), channel_id=1, source_target_pairs={{0,1},{1,0},{2,3},{3,2},{4,5},{5,4},{6,7},{7,6},{8,9},{9,8},{10,11... | collective-permute-start | bytes 98312 | tf_op jit(solution)/shard_map/ppermute | solution.py:483
  33.5 8.4 %collective-permute-start.10 = (bf16[256,256]{1,0:T(8,128)(2,1)S(1)}, bf16[256,256]{1,0:T(8,128)(2,1)S(1)}, u32[]{:S(2)}, u32[]{:S(2)}) collective-permute-start(bf16[256,256]{1,0:T(8,128)(2,1)S(1)} %get-tuple-element.36), channel_id=1, source_target_pairs={{4,8},{8,12},{5,13},{6,10},{10,14},{7,15},{20,24},{24,28},{21,29},... | collective-permute-start | bytes 393224 | tf_op jit(solution)/shard_map/ppermute | solution.py:509
  34.8 7.3 %collective-permute-start.6 = (bf16[64,256]{1,0:T(8,128)(2,1)S(1)}, bf16[64,256]{1,0:T(8,128)(2,1)S(1)}, u32[]{:S(2)}, u32[]{:S(2)}) collective-permute-start(bf16[64,256]{1,0:T(8,128)(2,1)S(1)} %get-tuple-element.35), channel_id=1, source_target_pairs={{0,12},{1,13},{2,14},{3,15},{16,28},{17,29},{18,30},{19,31}} | collective-permute-start | bytes 98312 | tf_op jit(solution)/shard_map/ppermute | solution.py:515
  38.6 3.5 %collective-permute-start.7 = (bf16[64,256]{1,0:T(8,128)(2,1)S(1)}, bf16[64,256]{1,0:T(8,128)(2,1)S(1)}, u32[]{:S(2)}, u32[]{:S(2)}) collective-permute-start(bf16[64,256]{1,0:T(8,128)(2,1)S(1)} %get-tuple-element.35), channel_id=1, source_target_pairs={{0,4},{1,5},{2,6},{3,7},{16,20},{17,21},{18,22},{19,23}} | collective-permute-start | bytes 98312 | tf_op jit(solution)/shard_map/ppermute | solution.py:515
  39.9 2.9 %collective-permute-start.8 = (bf16[64,256]{1,0:T(8,128)(2,1)S(1)}, bf16[64,256]{1,0:T(8,128)(2,1)S(1)}, u32[]{:S(2)}, u32[]{:S(2)}) collective-permute-start(bf16[64,256]{1,0:T(8,128)(2,1)S(1)} %get-tuple-element.35), channel_id=1, source_target_pairs={{0,8},{1,9},{2,10},{3,11},{4,12},{5,13},{6,14},{7,15},{16,24},{17,... | collective-permute-start | bytes 98312 | tf_op jit(solution)/shard_map/ppermute | solution.py:515
  41.2 1.6 %collective-permute-start.9 = (bf16[64,256]{1,0:T(8,128)(2,1)S(1)}, bf16[64,256]{1,0:T(8,128)(2,1)S(1)}, u32[]{:S(2)}, u32[]{:S(2)}) collective-permute-start(bf16[64,256]{1,0:T(8,128)(2,1)S(1)} %get-tuple-element.35), channel_id=1, source_target_pairs={{4,8},{5,9},{6,10},{7,11},{8,12},{9,13},{10,14},{11,15},{20,24},{2... | collective-permute-start | bytes 98312 | tf_op jit(solution)/shard_map/ppermute | solution.py:515
  41.9 1.4 %collective-permute-start.11 = (bf16[256,256]{1,0:T(8,128)(2,1)S(1)}, bf16[256,256]{1,0:T(8,128)(2,1)S(1)}, u32[]{:S(2)}, u32[]{:S(2)}) collective-permute-start(bf16[256,256]{1,0:T(8,128)(2,1)S(1)} %collective-permute-done.10.got), channel_id=1, source_target_pairs={{0,1},{1,0},{2,3},{3,2},{4,5},{5,4},{6,7},{7,6},{8,9},{9,8},{10,11... | collective-permute-start | bytes 393224 | tf_op jit(solution)/shard_map/ppermute | solution.py:483
  44.0 3.8 %collective-permute-start.12 = (bf16[64,256]{1,0:T(8,128)(2,1)S(1)}, bf16[64,256]{1,0:T(8,128)(2,1)S(1)}, u32[]{:S(2)}, u32[]{:S(2)}) collective-permute-start(bf16[64,256]{1,0:T(8,128)(2,1)S(1)} %get-tuple-element.41), channel_id=1, source_target_pairs={{0,3},{1,2},{2,1},{3,0},{4,7},{5,6},{6,5},{7,4},{8,11},{9,10},{10,... | collective-permute-start | bytes 98312 | tf_op jit(solution)/shard_map/ppermute | solution.py:491
  44.6 3.9 %collective-permute-start.13 = (bf16[64,256]{1,0:T(8,128)(2,1)S(1)}, bf16[64,256]{1,0:T(8,128)(2,1)S(1)}, u32[]{:S(2)}, u32[]{:S(2)}) collective-permute-start(bf16[64,256]{1,0:T(8,128)(2,1)S(1)} %get-tuple-element.42), channel_id=1, source_target_pairs={{0,2},{1,3},{2,0},{3,1},{4,6},{5,7},{6,4},{7,5},{8,10},{9,11},{10,... | collective-permute-start | bytes 98312 | tf_op jit(solution)/shard_map/ppermute | solution.py:487
  45.9 2.7 %collective-permute-start.14 = (bf16[64,256]{1,0:T(8,128)(2,1)S(1)}, bf16[64,256]{1,0:T(8,128)(2,1)S(1)}, u32[]{:S(2)}, u32[]{:S(2)}) collective-permute-start(bf16[64,256]{1,0:T(8,128)(2,1)S(1)} %get-tuple-element.43), channel_id=1, source_target_pairs={{0,1},{1,0},{2,3},{3,2},{4,5},{5,4},{6,7},{7,6},{8,9},{9,8},{10,11... | collective-permute-start | bytes 98312 | tf_op jit(solution)/shard_map/ppermute | solution.py:483

commit v31 on v29

--- a/solution.py
+++ b/solution.py
@@ -88,11 +88,13 @@
             coupling[at] = jnp.where(pattern[j, i] == 1, tile, jnp.zeros_like(tile))
 
 
-def pairs_kernel(owner_in, blocks_in, green, inject_in, out, owner, blocks, inject, held, product, slot_of, counts, sem, side):
+def pairs_kernel(owner_in, blocks_in, green, inject_in, out, owner, blocks, inject, held, product, slot_of, counts, sem, side, done, *packets):
     energies, orbitals, _ = green.shape
     sections = out.shape[0]
     count = owner.shape[0]
     named = held.shape[1] < orbitals
+    parts = sem.shape[1]
+    size = held.shape[1] // parts
     small = [
         pltpu.make_async_copy(src, dst, side.at[k])
         for k, (src, dst) in enumerate(((owner_in, owner), (blocks_in, blocks), (inject_in, inject)))
@@ -100,30 +102,42 @@
     for move in small:
         move.start()
 
-    def copy_of(e, q):
+    def copy_of(e, c, q):
         first = pl.multiple_of(blocks[0, q] * BLK, BLK)
         to = pl.multiple_of(q * BLK, BLK)
-        return pltpu.make_async_copy(green.at[e, pl.ds(first, BLK)], held.at[e, pl.ds(to, BLK)], sem.at[e])
-
-    def whole(e):
-        return pltpu.make_async_copy(green.at[e], held.at[e], sem.at[e])
+        return pltpu.make_async_copy(green.at[e, pl.ds(first, BLK)], held.at[e, pl.ds(to, BLK)], sem.at[e, c])
+
+    def part_of(e, c):
+        at = pl.ds(c * size, size)
+        return pltpu.make_async_copy(green.at[e, at], held.at[e, at], sem.at[e, c])
 
     if not named:
         for e in range(energies):
-            whole(e).start()
+            for c in range(parts):
+                part_of(e, c).start()
     for move in small[:2]:
         move.wait()
     if named:
         for e in range(energies):
-            lax.fori_loop(0, count, lambda q, _, e=e: copy_of(e, q).start(), None, unroll=4)
-    rows = CAP * energies * BLK
-    lane = lax.broadcasted_iota(jnp.int32, (HEAD, out.shape[2]), 1)
+            for c in range(parts):
+                lax.fori_loop(
+                    c * (count // parts),
+                    (c + 1) * (count // parts),
+                    lambda q, _, e=e, c=c: copy_of(e, c, q).start(),
+                    None,
+                    unroll=4,
+                )
+    rows = CAP * BLK
+    head = packets[-1]
+    columns = out.shape[2]
+    lane = lax.broadcasted_iota(jnp.int32, (HEAD, columns), 1)
     none = jnp.where(lane < CAP, -1.0, 0.0).astype(BF16)
 
     def blank(d, _):
         counts[d] = 0
-        out[d, :rows, :] = jnp.zeros((rows, out.shape[2]), BF16)
-        out[d, rows : rows + HEAD, :] = none
+        for packet in packets:
+            packet[d, :rows, :] = jnp.zeros((rows, columns), BF16)
+        head[d, rows : rows + HEAD, :] = none
         return 0
 
     lax.fori_loop(0, sections, blank, 0)
@@ -133,49 +147,60 @@
         r = counts[d]
         counts[d] = r + 1
         slot_of[q] = r
-        head = out[d, rows : rows + HEAD, :].astype(F32)
-        head = jnp.where(lane == r, blocks[1, q].astype(F32), head)
-        out[d, rows : rows + HEAD, :] = head.astype(BF16)
+        line = head[d, rows : rows + HEAD, :].astype(F32)
+        line = jnp.where(lane == r, blocks[1, q].astype(F32), line)
+        head[d, rows : rows + HEAD, :] = line.astype(BF16)
         return 0
 
     lax.fori_loop(0, count, rank, 0)
     small[2].wait()
-    for e in range(energies):
-        whole_held = pltpu.make_async_copy(green.at[e, pl.ds(0, held.shape[1])], held.at[e], sem.at[e])
-        whole_held.wait()
-        product[...] = dot(held[e], inject[e]).astype(BF16)
+    moves = []
+    for e, packet in enumerate(packets):
+        for c in range(parts):
+            part_of(e, c).wait()
+            at = slice(c * size, (c + 1) * size)
+            product[e, at, :] = dot(held[e, at, :], inject[e]).astype(BF16)
 
         def fill(q, _):
             first = pl.multiple_of((q if named else blocks[0, q]) * BLK, BLK)
-            to = pl.multiple_of((slot_of[q] * energies + e) * BLK, BLK)
-            out[owner[q], pl.ds(to, BLK), :] = product[pl.ds(first, BLK), :]
+            to = pl.multiple_of(slot_of[q] * BLK, BLK)
+            packet[owner[q], pl.ds(to, BLK), :] = product[e, pl.ds(first, BLK), :]
             return 0
 
         lax.fori_loop(0, count, fill, 0, unroll=4)
+        moves.append(pltpu.make_async_copy(packet, out.at[:, pl.ds(e * rows, packet.shape[1])], done.at[e]))
+        moves[-1].start()
+    for move in moves:
+        move.wait()
 
 
 def outgoing_pairs(owner, blocks, green, inject, sections):
     energies, orbitals, _ = green.shape
     columns = inject.shape[2]
     rows = min(orbitals, owner.shape[0] * BLK)
-    return call(
+    part = CAP * BLK
+    parts = 2
+    return pl.pallas_call(
         pairs_kernel,
-        "pairs",
-        [IN_HBM] * 4,
-        shape(sections, CAP * energies * BLK + HEAD, columns),
-        [
+        name="pairs",
+        in_specs=[IN_HBM] * 4,
+        out_shape=shape(sections, part * energies + HEAD, columns),
+        out_specs=IN_HBM,
+        scratch_shapes=[
             pltpu.SMEM(owner.shape, jnp.int32),
             pltpu.SMEM(blocks.shape, jnp.int32),
             pltpu.VMEM(inject.shape, BF16),
             pltpu.VMEM((energies, rows, orbitals), BF16),
-            pltpu.VMEM((rows, columns), BF16),
+            pltpu.VMEM((energies, rows, columns), BF16),
             pltpu.SMEM(owner.shape, jnp.int32),
             pltpu.SMEM((sections,), jnp.int32),
+            pltpu.SemaphoreType.DMA((energies, parts)),
+            pltpu.SemaphoreType.DMA((3,)),
             pltpu.SemaphoreType.DMA((energies,)),
-            pltpu.SemaphoreType.DMA((3,)),
-        ],
-        4.0,
-        VMEM_WHOLE,
+        ]
+        + [pltpu.VMEM((sections, part + (HEAD if e == energies - 1 else 0), columns), BF16) for e in range(energies)],
+        compiler_params=pltpu.CompilerParams(vmem_limit_bytes=VMEM_WHOLE),
+        cost_estimate=pl.CostEstimate(flops=int(4.0 * PEAK), bytes_accessed=0, transcendentals=0),
     )(owner, blocks, green, inject)
 
 
@@ -272,7 +297,7 @@
         for r in range(CAP):
             first = pl.multiple_of(jnp.maximum(targets[s, r], 0) * BLK, BLK)
             for e in range(energies):
-                item = received[s, (r * energies + e) * BLK : (r * energies + e + 1) * BLK, :]
+                item = received[s, (e * CAP + r) * BLK : (e * CAP + r + 1) * BLK, :]
                 total[e, pl.ds(first, BLK), :] += item.astype(F32)
         return 0
 

time: 49.5 us -> 49.1 us (level)
  Pallas kernels: 14.2 us -> 13.7 us
where the time goes in v31:
time: 49.1 us; the launch traced here: 48.6 us
  starting transfers between devices  21.9 us (45%)
  Pallas kernels  13.7 us (28%)
  waiting for transfers between devices  9.65 us (20%)
  local copies, waits for them, and re-layouts  3.1 us (6%)
    all_to_all x1, waiting for transfers between devices, per_device(): lax.all_to_all(outgoing, 'sec', split_axis=0, concat_axis=0, tiled=True)  9.01 us
    all_to_all x1, starting transfers between devices, per_device(): lax.all_to_all(outgoing, 'sec', split_axis=0, concat_axis=0, tiled=True)  7.41 us
    ppermute x4, starting transfers between devices, between(): return lax.ppermute(item, 'sec', pairs)  7.06 us
    pallas_call x1, Pallas kernels, outgoing_pairs(): pl.pallas_call(pairs_kernel, name='pairs', in_specs=[IN_HBM] * 4, out_sha...  4.04 us
    ppermute x3, starting transfers between devices, to_across(): lax.ppermute(item, 'sec', [(s, s // GROUP * GROUP + (s % GROUP + CORES) %...  3.68 us
    unnamed x14, local copies, waits for them, and re-layouts  3.1 us
    pallas_call x2, Pallas kernels, image_and_maps(): call(functools.partial(work_kernel, not held), 'image_and_maps', [IN_VMEM...  1.91 us
    pallas_call x1, Pallas kernels, propagator(): call(prop_kernel, 'prop', [IN_SMEM, IN_VMEM, IN_VMEM, IN_PLACE], shape(en...  1.9 us
  transfers between devices with their start and end apart: 16, of which 3 were waited for; matrix products, arithmetic and copies ran while one was open for 0% of the time, Pallas kernels for 16%

profile of v31, /device:TPU:0, one launch (start us, length us, event | category | flops | bytes accessed | tf_op | source)
XLA Modules:
  0.0 48.6 jit_solution(13682636483882866983)
XLA Ops:
  0.0 4.0 %pairs.1 = bf16[16,136,128]{2,1,0:T(8,128)(2,1)} custom-call(s32[16]{0:T(128)} %bitcast.21, s32[2,16]{1,0:T(2,128)} %bitcast.20, bf16[2,1024,1024]{2,1,0:T(8,128)(2,1)} %bitcast.9, bf16[2,1024,128]{2,1,0:T(8,128)(2,1)} %bitcast.14), custom_call_target="tpu_custom_call" | custom-call | flops 4600000000 | tf_op jit(solution)/shard_map/pairs/pallas_call | solution.py:183
  4.1 0.0 copy-start.2
  4.1 7.4 %all-to-all-start = ((bf16[16,136,128]{2,1,0:T(8,128)(2,1)}), bf16[16,136,128]{2,1,0:T(8,128)(2,1)S(1)}, u32[]{:S(2)}, u32[]{:S(2)}) async-start(bf16[16,136,128]{2,1,0:T(8,128)(2,1)} %pairs.1), calls=%async_computation | async-start | bytes 1114112 | tf_op jit(solution)/shard_map/all_to_all | solution.py:562
  11.5 0.0 copy-start
  11.5 2.2 %copy-done = bf16[1,2,1024,1024]{3,2,1,0:T(8,128)(2,1)S(1)} copy-done((bf16[1,2,1024,1024]{3,2,1,0:T(8,128)(2,1)S(1)}, bf16[1,2,1024,1024]{3,2,1,0:T(8,128)(2,1)}, u32[]{:S(2)}) %copy-start) | copy-done | bytes 4194328
  13.7 1.1 %face_maps.1 = (f32[256,256]{1,0:T(8,128)S(1)}, f32[256,256]{1,0:T(8,128)S(1)}, bf16[256,1024]{1,0:T(8,128)(2,1)S(1)}, bf16[256,1024]{1,0:T(8,128)(2,1)S(1)}) custom-call(s32[2,8]{1,0:T(2,128)S(1)} %bitcast.18, bf16[2,1024,1024]{2,1,0:T(8,128)(2,1)S(1)} %bitcast.10, bf16[1024,256]{1,0:T(8,128)(2,1)S(1)} %bitcast.16), custom_call_target="tpu_custom_call" | custom-call | flops 1380000000 | tf_op jit(solution)/shard_map/face_maps/pallas_call | solution.py:225
  14.8 0.0 copy-start.5
  14.8 0.8 %copy-done.5 = bf16[256,1024]{1,0:T(8,128)(2,1)} copy-done((bf16[256,1024]{1,0:T(8,128)(2,1)}, bf16[256,1024]{1,0:T(8,128)(2,1)S(1)}, u32[]{:S(2)}) %copy-start.5) | copy-done | bytes 524312
  15.6 1.9 %collective-permute-start.3 = (f32[256,256]{1,0:T(8,128)S(1)}, f32[256,256]{1,0:T(8,128)S(1)}, u32[]{:S(2)}, u32[]{:S(2)}) collective-permute-start(f32[256,256]{1,0:T(8,128)S(1)} %get-tuple-element.32), channel_id=1, source_target_pairs={{0,2},{1,3},{2,0},{3,1},{4,6},{5,7},{6,4},{7,5},{8,10},{9,11},{10,... | collective-permute-start | bytes 786440 | tf_op jit(solution)/shard_map/ppermute | solution.py:512
  17.5 0.0 collective-permute-start.5
  17.5 9.0 %all-to-all-done.received = bf16[16,136,128]{2,1,0:T(8,128)(2,1)S(1)} async-done(((bf16[16,136,128]{2,1,0:T(8,128)(2,1)}), bf16[16,136,128]{2,1,0:T(8,128)(2,1)S(1)}, u32[]{:S(2)}, u32[]{:S(2)}) %all-to-all-start) | async-done | bytes 557088 | tf_op jit(solution)/shard_map/all_to_all | solution.py:562
  26.6 0.9 %source.1.refs_1_ = bf16[2,1024,128]{2,1,0:T(8,128)(2,1)S(1)} custom-call(bf16[16,136,128]{2,1,0:T(8,128)(2,1)S(1)} %all-to-all-done.received, bf16[2,1024,128]{2,1,0:T(8,128)(2,1)S(1)} %bitcast.15), custom_call_target="tpu_custom_call" | custom-call | flops 1150000000 | tf_op jit(solution)/shard_map/source/pallas_call | solution.py:311
  27.5 0.0 copy-start.1
  27.5 0.1 copy-done.6
  27.6 0.5 %face_quarters.1 = (bf16[64,256]{1,0:T(8,128)(2,1)S(1)}, bf16[64,256]{1,0:T(8,128)(2,1)S(1)}, bf16[64,256]{1,0:T(8,128)(2,1)S(1)}, bf16[64,256]{1,0:T(8,128)(2,1)S(1)}) custom-call(bf16[2,1024,128]{2,1,0:T(8,128)(2,1)S(1)} %source.1.refs_1_, bf16[256,1024]{1,0:T(8,128)(2,1)S(1)} %get-tuple-element.25.refs_0_, bf16[256,1024]{1,0:T(8,128)(2,1)S(1)} %copy-done.6), custom_call_target="tpu_custom_call" | custom-call | flops 690000000 | tf_op jit(solution)/shard_map/face_quarters/pallas_call | solution.py:344
  28.1 0.0 collective-permute-done.3._map
  28.1 0.1 collective-permute-start.4
  28.2 0.9 %collective-permute-start = (bf16[64,256]{1,0:T(8,128)(2,1)S(1)}, bf16[64,256]{1,0:T(8,128)(2,1)S(1)}, u32[]{:S(2)}, u32[]{:S(2)}) collective-permute-start(bf16[64,256]{1,0:T(8,128)(2,1)S(1)} %get-tuple-element.28), channel_id=1, source_target_pairs={{0,3},{1,2},{2,1},{3,0},{4,7},{5,6},{6,5},{7,4},{8,11},{9,10},{10,... | collective-permute-start | bytes 98312 | tf_op jit(solution)/shard_map/ppermute | solution.py:516
  29.1 1.3 %collective-permute-start.1 = (bf16[64,256]{1,0:T(8,128)(2,1)S(1)}, bf16[64,256]{1,0:T(8,128)(2,1)S(1)}, u32[]{:S(2)}, u32[]{:S(2)}) collective-permute-start(bf16[64,256]{1,0:T(8,128)(2,1)S(1)} %get-tuple-element.29), channel_id=1, source_target_pairs={{0,2},{1,3},{2,0},{3,1},{4,6},{5,7},{6,4},{7,5},{8,10},{9,11},{10,... | collective-permute-start | bytes 98312 | tf_op jit(solution)/shard_map/ppermute | solution.py:512
  30.4 0.0 collective-permute-start.2
  30.4 0.0 collective-permute-done.5.near
  30.4 0.0 collective-permute-done.4.far
  30.4 0.8 %chain_maps.1 = (bf16[256,256]{1,0:T(8,128)(2,1)S(1)}, bf16[2,4,256,256]{3,2,1,0:T(8,128)(2,1)S(1)}) custom-call(f32[256,256]{1,0:T(8,128)S(1)} %get-tuple-element.31.own, f32[256,256]{1,0:T(8,128)S(1)} %collective-permute-done.4.far, f32[256,256]{1,0:T(8,128)S(1)} %after_exchange.1.across, f32[256,256]{1,0:T(8,128)S(1)} %collective-permute-done.5.near), custom_call_target="tpu_custom_call" | custom-call | flops 1035000000 | tf_op jit(solution)/shard_map/chain_maps/pallas_call | solution.py:270
  31.2 1.8 %image_and_maps.2 = (f32[2,1024,128]{2,1,0:T(8,128)S(1)}, bf16[2,2,256,256]{3,2,1,0:T(8,128)(2,1)S(1)}) custom-call(bf16[2,1024,1024]{2,1,0:T(8,128)(2,1)S(1)} %bitcast.11, bf16[2,1024,128]{2,1,0:T(8,128)(2,1)S(1)} %source.1.refs_1_, bf16[2,4,256,256]{3,2,1,0:T(8,128)(2,1)S(1)} %get-tuple-element.33.refs_2_.parts), custom_call_target="tpu_custom_call" | custom-call | flops 2300000000 | tf_op jit(solution)/shard_map/image_and_maps/pallas_call | solution.py:420
  33.0 0.7 %collective-permute-start.10 = (bf16[256,256]{1,0:T(8,128)(2,1)S(1)}, bf16[256,256]{1,0:T(8,128)(2,1)S(1)}, u32[]{:S(2)}, u32[]{:S(2)}) collective-permute-start(bf16[256,256]{1,0:T(8,128)(2,1)S(1)} %get-tuple-element.36), channel_id=1, source_target_pairs={{4,8},{8,12},{5,13},{6,10},{10,14},{7,15},{20,24},{24,28},{21,29},... | collective-permute-start | bytes 393224 | tf_op jit(solution)/shard_map/ppermute | solution.py:534
  33.7 0.0 collective-permute-done.far
  33.7 0.0 collective-permute-done.1.across
  33.7 0.0 collective-permute-done.2.near
  33.7 0.6 %plane_total.1 = (bf16[64,256]{1,0:T(8,128)(2,1)S(1)}, f32[3,64,256]{2,1,0:T(8,128)S(1)}) custom-call(bf16[64,256]{1,0:T(8,128)(2,1)S(1)} %get-tuple-element.27._packets.own, bf16[64,256]{1,0:T(8,128)(2,1)S(1)} %collective-permute-done.far, bf16[64,256]{1,0:T(8,128)(2,1)S(1)} %collective-permute-done.1.across, ...), custom_call_target="tpu_custom_call" | custom-call | flops 3449999872 | tf_op jit(solution)/shard_map/plane_total/pallas_call | solution.py:386
  34.3 3.8 %collective-permute-start.6 = (bf16[64,256]{1,0:T(8,128)(2,1)S(1)}, bf16[64,256]{1,0:T(8,128)(2,1)S(1)}, u32[]{:S(2)}, u32[]{:S(2)}) collective-permute-start(bf16[64,256]{1,0:T(8,128)(2,1)S(1)} %get-tuple-element.35), channel_id=1, source_target_pairs={{0,12},{1,13},{2,14},{3,15},{16,28},{17,29},{18,30},{19,31}} | collective-permute-start | bytes 98312 | tf_op jit(solution)/shard_map/ppermute | solution.py:540
  38.1 1.3 %collective-permute-start.7 = (bf16[64,256]{1,0:T(8,128)(2,1)S(1)}, bf16[64,256]{1,0:T(8,128)(2,1)S(1)}, u32[]{:S(2)}, u32[]{:S(2)}) collective-permute-start(bf16[64,256]{1,0:T(8,128)(2,1)S(1)} %get-tuple-element.35), channel_id=1, source_target_pairs={{0,4},{1,5},{2,6},{3,7},{16,20},{17,21},{18,22},{19,23}} | collective-permute-start | bytes 98312 | tf_op jit(solution)/shard_map/ppermute | solution.py:540
  39.4 1.3 %collective-permute-start.8 = (bf16[64,256]{1,0:T(8,128)(2,1)S(1)}, bf16[64,256]{1,0:T(8,128)(2,1)S(1)}, u32[]{:S(2)}, u32[]{:S(2)}) collective-permute-start(bf16[64,256]{1,0:T(8,128)(2,1)S(1)} %get-tuple-element.35), channel_id=1, source_target_pairs={{0,8},{1,9},{2,10},{3,11},{4,12},{5,13},{6,14},{7,15},{16,24},{17,... | collective-permute-start | bytes 98312 | tf_op jit(solution)/shard_map/ppermute | solution.py:540
  40.7 0.7 %collective-permute-start.9 = (bf16[64,256]{1,0:T(8,128)(2,1)S(1)}, bf16[64,256]{1,0:T(8,128)(2,1)S(1)}, u32[]{:S(2)}, u32[]{:S(2)}) collective-permute-start(bf16[64,256]{1,0:T(8,128)(2,1)S(1)} %get-tuple-element.35), channel_id=1, source_target_pairs={{4,8},{5,9},{6,10},{7,11},{8,12},{9,13},{10,14},{11,15},{20,24},{2... | collective-permute-start | bytes 98312 | tf_op jit(solution)/shard_map/ppermute | solution.py:540
  41.4 0.0 collective-permute-done.10.got
  41.4 0.7 %collective-permute-start.11 = (bf16[256,256]{1,0:T(8,128)(2,1)S(1)}, bf16[256,256]{1,0:T(8,128)(2,1)S(1)}, u32[]{:S(2)}, u32[]{:S(2)}) collective-permute-start(bf16[256,256]{1,0:T(8,128)(2,1)S(1)} %collective-permute-done.10.got), channel_id=1, source_target_pairs={{8,9},{9,8},{10,11},{11,10},{12,13},{13,12},{14,15},{15,14},{24,25... | collective-permute-start | bytes 393224 | tf_op jit(solution)/shard_map/ppermute | solution.py:535
  42.1 0.1 image_and_maps.3
  42.2 0.0 collective-permute-done.6.third
  42.2 0.0 collective-permute-done.7.near_one
  42.2 0.1 collective-permute-done.8.second
  42.3 0.0 collective-permute-done.9.far_one
  42.3 0.0 collective-permute-done.11.other
  42.3 0.7 %entering.1 = (bf16[64,256]{1,0:T(8,128)(2,1)S(1)}, bf16[64,256]{1,0:T(8,128)(2,1)S(1)}, bf16[64,256]{1,0:T(8,128)(2,1)S(1)}, bf16[64,256]{1,0:T(8,128)(2,1)S(1)}) custom-call(bf16[64,256]{1,0:T(8,128)(2,1)S(1)} %collective-permute-done.6.third, bf16[64,256]{1,0:T(8,128)(2,1)S(1)} %collective-permute-done.7.near_one, ...), custom_call_target="tpu_custom_call" | custom-call | flops 1610000000 | tf_op jit(solution)/shard_map/entering/pallas_call | solution.py:460
  43.1 0.5 collective-permute-start.12
  43.5 0.5 %collective-permute-start.13 = (bf16[64,256]{1,0:T(8,128)(2,1)S(1)}, bf16[64,256]{1,0:T(8,128)(2,1)S(1)}, u32[]{:S(2)}, u32[]{:S(2)}) collective-permute-start(bf16[64,256]{1,0:T(8,128)(2,1)S(1)} %get-tuple-element.42), channel_id=1, source_target_pairs={{0,2},{1,3},{2,0},{3,1},{4,6},{5,7},{6,4},{7,5},{8,10},{9,11},{10,... | collective-permute-start | bytes 98312 | tf_op jit(solution)/shard_map/ppermute | solution.py:512
  44.0 1.0 %collective-permute-start.14 = (bf16[64,256]{1,0:T(8,128)(2,1)S(1)}, bf16[64,256]{1,0:T(8,128)(2,1)S(1)}, u32[]{:S(2)}, u32[]{:S(2)}) collective-permute-start(bf16[64,256]{1,0:T(8,128)(2,1)S(1)} %get-tuple-element.43), channel_id=1, source_target_pairs={{0,1},{1,0},{2,3},{3,2},{4,5},{5,4},{6,7},{7,6},{8,9},{9,8},{10,11... | collective-permute-start | bytes 98312 | tf_op jit(solution)/shard_map/ppermute | solution.py:508
  45.0 1.9 %prop.1 = bf16[2,1024,256]{2,1,0:T(8,128)(2,1)S(1)} custom-call(s32[2,8]{1,0:T(2,128)S(1)} %bitcast.19, bf16[2,1024,1024]{2,1,0:T(8,128)(2,1)S(1)} %bitcast.13, bf16[1024,256]{1,0:T(8,128)(2,1)S(1)} %bitcast.17, bf16[64,256]{1,0:T(8,128)(2,1)S(1)} %get-tuple-element.40._tie.own), custom_call_target="tpu_custom_call" | custom-call | flops 1724999936 | tf_op jit(solution)/shard_map/prop/pallas_call | solution.py:244
  46.9 0.5 %collective-permute-done.13.across = bf16[64,256]{1,0:T(8,128)(2,1)S(1)} collective-permute-done((bf16[64,256]{1,0:T(8,128)(2,1)S(1)}, bf16[64,256]{1,0:T(8,128)(2,1)S(1)}, u32[]{:S(2)}, u32[]{:S(2)}) %collective-permute-start.13) | collective-permute-done | bytes 32800 | tf_op jit(solution)/shard_map/ppermute | solution.py:512
  47.4 1.2 %waves.1 = bf16[2,1024,128]{2,1,0:T(8,128)(2,1)} custom-call(bf16[64,256]{1,0:T(8,128)(2,1)S(1)} %get-tuple-element.40._tie.own, bf16[64,256]{1,0:T(8,128)(2,1)S(1)} %collective-permute-done.12.far, bf16[64,256]{1,0:T(8,128)(2,1)S(1)} %collective-permute-done.13.across, bf16[64,256]{1,0:T(8,128)(2,1)S(1)} %collective-permute-done.14.near, ...), custom_call_target="tpu_custom_call" | custom-call | flops 1495000064 | tf_op jit(solution)/shard_map/waves/pallas_call | solution.py:491
  (10 shorter events, 0.0 us)
Async XLA Ops:
  0.0 11.5 %copy-start.3 = (bf16[1,1024,256]{2,1,0:T(8,128)(2,1)S(1)}, bf16[1,1024,256]{2,1,0:T(8,128)(2,1)}, u32[]{:S(2)}) copy-start(bf16[1,1024,256]{2,1,0:T(8,128)(2,1)} %param.8) | copy-start | bytes 1572868
  0.0 11.5 %copy-start.4 = (s32[1,8,2]{1,2,0:T(2,128)S(1)}, s32[1,8,2]{1,2,0:T(2,128)}, u32[]{:S(2)}) copy-start(s32[1,8,2]{1,2,0:T(2,128)} %param.9) | copy-start | bytes 196
  4.1 22.5 %copy-start.2 = (bf16[1,2,1024,128]{3,2,1,0:T(8,128)(2,1)S(1)}, bf16[1,2,1024,128]{3,2,1,0:T(8,128)(2,1)}, u32[]{:S(2)}) copy-start(bf16[1,2,1024,128]{3,2,1,0:T(8,128)(2,1)} %param.7) | copy-start | bytes 1572868
  4.1 22.5 %all-to-all-start = ((bf16[16,136,128]{2,1,0:T(8,128)(2,1)}), bf16[16,136,128]{2,1,0:T(8,128)(2,1)S(1)}, u32[]{:S(2)}, u32[]{:S(2)}) async-start(bf16[16,136,128]{2,1,0:T(8,128)(2,1)} %pairs.1), calls=%async_computation | async-start | bytes 1114112 | tf_op jit(solution)/shard_map/all_to_all | solution.py:562
  11.5 2.2 %copy-start = (bf16[1,2,1024,1024]{3,2,1,0:T(8,128)(2,1)S(1)}, bf16[1,2,1024,1024]{3,2,1,0:T(8,128)(2,1)}, u32[]{:S(2)}) copy-start(bf16[1,2,1024,1024]{3,2,1,0:T(8,128)(2,1)} %param.6) | copy-start | bytes 12582916
  14.8 0.8 %copy-start.5 = (bf16[256,1024]{1,0:T(8,128)(2,1)}, bf16[256,1024]{1,0:T(8,128)(2,1)S(1)}, u32[]{:S(2)}) copy-start(bf16[256,1024]{1,0:T(8,128)(2,1)S(1)} %get-tuple-element.26.refs_1_) | copy-start | bytes 1572868
  15.6 12.5 %collective-permute-start.3 = (f32[256,256]{1,0:T(8,128)S(1)}, f32[256,256]{1,0:T(8,128)S(1)}, u32[]{:S(2)}, u32[]{:S(2)}) collective-permute-start(f32[256,256]{1,0:T(8,128)S(1)} %get-tuple-element.32), channel_id=1, source_target_pairs={{0,2},{1,3},{2,0},{3,1},{4,6},{5,7},{6,4},{7,5},{8,10},{9,11},{10,... | collective-permute-start | bytes 786440 | tf_op jit(solution)/shard_map/ppermute | solution.py:512
  17.5 12.8 %collective-permute-start.5 = (f32[256,256]{1,0:T(8,128)S(1)}, f32[256,256]{1,0:T(8,128)S(1)}, u32[]{:S(2)}, u32[]{:S(2)}) collective-permute-start(f32[256,256]{1,0:T(8,128)S(1)} %get-tuple-element.31.own), channel_id=1, source_target_pairs={{0,1},{1,0},{2,3},{3,2},{4,5},{5,4},{6,7},{7,6},{8,9},{9,8},{10,11... | collective-permute-start | bytes 786440 | tf_op jit(solution)/shard_map/ppermute | solution.py:508
  26.6 1.0 %copy-start.6 = (bf16[256,1024]{1,0:T(8,128)(2,1)S(1)}, bf16[256,1024]{1,0:T(8,128)(2,1)}, u32[]{:S(2)}) copy-start(bf16[256,1024]{1,0:T(8,128)(2,1)} %copy-done.5) | copy-start | bytes 1572868
  27.5 3.7 %copy-start.1 = (bf16[1,2,1024,1024]{3,2,1,0:T(8,128)(2,1)S(1)}, bf16[1,2,1024,1024]{3,2,1,0:T(8,128)(2,1)}, u32[]{:S(2)}) copy-start(bf16[1,2,1024,1024]{3,2,1,0:T(8,128)(2,1)} %param.6) | copy-start | bytes 12582916
  28.1 2.2 %collective-permute-start.4 = (f32[256,256]{1,0:T(8,128)S(1)}, f32[256,256]{1,0:T(8,128)S(1)}, u32[]{:S(2)}, u32[]{:S(2)}) collective-permute-start(f32[256,256]{1,0:T(8,128)S(1)} %after_exchange.1.across), channel_id=1, source_target_pairs={{0,1},{1,0},{2,3},{3,2},{4,5},{5,4},{6,7},{7,6},{8,9},{9,8},{10,11... | collective-permute-start | bytes 786440 | tf_op jit(solution)/shard_map/ppermute | solution.py:508
  28.2 5.5 %collective-permute-start = (bf16[64,256]{1,0:T(8,128)(2,1)S(1)}, bf16[64,256]{1,0:T(8,128)(2,1)S(1)}, u32[]{:S(2)}, u32[]{:S(2)}) collective-permute-start(bf16[64,256]{1,0:T(8,128)(2,1)S(1)} %get-tuple-element.28), channel_id=1, source_target_pairs={{0,3},{1,2},{2,1},{3,0},{4,7},{5,6},{6,5},{7,4},{8,11},{9,10},{10,... | collective-permute-start | bytes 98312 | tf_op jit(solution)/shard_map/ppermute | solution.py:516
  29.1 4.6 %collective-permute-start.1 = (bf16[64,256]{1,0:T(8,128)(2,1)S(1)}, bf16[64,256]{1,0:T(8,128)(2,1)S(1)}, u32[]{:S(2)}, u32[]{:S(2)}) collective-permute-start(bf16[64,256]{1,0:T(8,128)(2,1)S(1)} %get-tuple-element.29), channel_id=1, source_target_pairs={{0,2},{1,3},{2,0},{3,1},{4,6},{5,7},{6,4},{7,5},{8,10},{9,11},{10,... | collective-permute-start | bytes 98312 | tf_op jit(solution)/shard_map/ppermute | solution.py:512
  30.4 3.4 %collective-permute-start.2 = (bf16[64,256]{1,0:T(8,128)(2,1)S(1)}, bf16[64,256]{1,0:T(8,128)(2,1)S(1)}, u32[]{:S(2)}, u32[]{:S(2)}) collective-permute-start(bf16[64,256]{1,0:T(8,128)(2,1)S(1)} %get-tuple-element.30), channel_id=1, source_target_pairs={{0,1},{1,0},{2,3},{3,2},{4,5},{5,4},{6,7},{7,6},{8,9},{9,8},{10,11... | collective-permute-start | bytes 98312 | tf_op jit(solution)/shard_map/ppermute | solution.py:508
  33.0 8.4 %collective-permute-start.10 = (bf16[256,256]{1,0:T(8,128)(2,1)S(1)}, bf16[256,256]{1,0:T(8,128)(2,1)S(1)}, u32[]{:S(2)}, u32[]{:S(2)}) collective-permute-start(bf16[256,256]{1,0:T(8,128)(2,1)S(1)} %get-tuple-element.36), channel_id=1, source_target_pairs={{4,8},{8,12},{5,13},{6,10},{10,14},{7,15},{20,24},{24,28},{21,29},... | collective-permute-start | bytes 393224 | tf_op jit(solution)/shard_map/ppermute | solution.py:534
  34.3 7.9 %collective-permute-start.6 = (bf16[64,256]{1,0:T(8,128)(2,1)S(1)}, bf16[64,256]{1,0:T(8,128)(2,1)S(1)}, u32[]{:S(2)}, u32[]{:S(2)}) collective-permute-start(bf16[64,256]{1,0:T(8,128)(2,1)S(1)} %get-tuple-element.35), channel_id=1, source_target_pairs={{0,12},{1,13},{2,14},{3,15},{16,28},{17,29},{18,30},{19,31}} | collective-permute-start | bytes 98312 | tf_op jit(solution)/shard_map/ppermute | solution.py:540
  38.1 4.1 %collective-permute-start.7 = (bf16[64,256]{1,0:T(8,128)(2,1)S(1)}, bf16[64,256]{1,0:T(8,128)(2,1)S(1)}, u32[]{:S(2)}, u32[]{:S(2)}) collective-permute-start(bf16[64,256]{1,0:T(8,128)(2,1)S(1)} %get-tuple-element.35), channel_id=1, source_target_pairs={{0,4},{1,5},{2,6},{3,7},{16,20},{17,21},{18,22},{19,23}} | collective-permute-start | bytes 98312 | tf_op jit(solution)/shard_map/ppermute | solution.py:540
  39.4 2.9 %collective-permute-start.8 = (bf16[64,256]{1,0:T(8,128)(2,1)S(1)}, bf16[64,256]{1,0:T(8,128)(2,1)S(1)}, u32[]{:S(2)}, u32[]{:S(2)}) collective-permute-start(bf16[64,256]{1,0:T(8,128)(2,1)S(1)} %get-tuple-element.35), channel_id=1, source_target_pairs={{0,8},{1,9},{2,10},{3,11},{4,12},{5,13},{6,14},{7,15},{16,24},{17,... | collective-permute-start | bytes 98312 | tf_op jit(solution)/shard_map/ppermute | solution.py:540
  40.7 1.6 %collective-permute-start.9 = (bf16[64,256]{1,0:T(8,128)(2,1)S(1)}, bf16[64,256]{1,0:T(8,128)(2,1)S(1)}, u32[]{:S(2)}, u32[]{:S(2)}) collective-permute-start(bf16[64,256]{1,0:T(8,128)(2,1)S(1)} %get-tuple-element.35), channel_id=1, source_target_pairs={{4,8},{5,9},{6,10},{7,11},{8,12},{9,13},{10,14},{11,15},{20,24},{2... | collective-permute-start | bytes 98312 | tf_op jit(solution)/shard_map/ppermute | solution.py:540
  41.4 0.9 %collective-permute-start.11 = (bf16[256,256]{1,0:T(8,128)(2,1)S(1)}, bf16[256,256]{1,0:T(8,128)(2,1)S(1)}, u32[]{:S(2)}, u32[]{:S(2)}) collective-permute-start(bf16[256,256]{1,0:T(8,128)(2,1)S(1)} %collective-permute-done.10.got), channel_id=1, source_target_pairs={{8,9},{9,8},{10,11},{11,10},{12,13},{13,12},{14,15},{15,14},{24,25... | collective-permute-start | bytes 393224 | tf_op jit(solution)/shard_map/ppermute | solution.py:535
  43.1 3.8 %collective-permute-start.12 = (bf16[64,256]{1,0:T(8,128)(2,1)S(1)}, bf16[64,256]{1,0:T(8,128)(2,1)S(1)}, u32[]{:S(2)}, u32[]{:S(2)}) collective-permute-start(bf16[64,256]{1,0:T(8,128)(2,1)S(1)} %get-tuple-element.41), channel_id=1, source_target_pairs={{0,3},{1,2},{2,1},{3,0},{4,7},{5,6},{6,5},{7,4},{8,11},{9,10},{10,... | collective-permute-start | bytes 98312 | tf_op jit(solution)/shard_map/ppermute | solution.py:516
  43.5 3.9 %collective-permute-start.13 = (bf16[64,256]{1,0:T(8,128)(2,1)S(1)}, bf16[64,256]{1,0:T(8,128)(2,1)S(1)}, u32[]{:S(2)}, u32[]{:S(2)}) collective-permute-start(bf16[64,256]{1,0:T(8,128)(2,1)S(1)} %get-tuple-element.42), channel_id=1, source_target_pairs={{0,2},{1,3},{2,0},{3,1},{4,6},{5,7},{6,4},{7,5},{8,10},{9,11},{10,... | collective-permute-start | bytes 98312 | tf_op jit(solution)/shard_map/ppermute | solution.py:512
  44.0 3.4 %collective-permute-start.14 = (bf16[64,256]{1,0:T(8,128)(2,1)S(1)}, bf16[64,256]{1,0:T(8,128)(2,1)S(1)}, u32[]{:S(2)}, u32[]{:S(2)}) collective-permute-start(bf16[64,256]{1,0:T(8,128)(2,1)S(1)} %get-tuple-element.43), channel_id=1, source_target_pairs={{0,1},{1,0},{2,3},{3,2},{4,5},{5,4},{6,7},{7,6},{8,9},{9,8},{10,11... | collective-permute-start | bytes 98312 | tf_op jit(solution)/shard_map/ppermute | solution.py:508

commit v32 on v31

--- a/solution.py
+++ b/solution.py
@@ -156,18 +156,21 @@
     small[2].wait()
     moves = []
     for e, packet in enumerate(packets):
+
+        def fill(q, _, e=e, packet=packet):
+            first = pl.multiple_of((q if named else blocks[0, q]) * BLK, BLK)
+            to = pl.multiple_of(slot_of[q] * BLK, BLK)
+            packet[owner[q], pl.ds(to, BLK), :] = product[e, pl.ds(first, BLK), :]
+            return 0
+
         for c in range(parts):
             part_of(e, c).wait()
             at = slice(c * size, (c + 1) * size)
             product[e, at, :] = dot(held[e, at, :], inject[e]).astype(BF16)
-
-        def fill(q, _):
-            first = pl.multiple_of((q if named else blocks[0, q]) * BLK, BLK)
-            to = pl.multiple_of(slot_of[q] * BLK, BLK)
-            packet[owner[q], pl.ds(to, BLK), :] = product[e, pl.ds(first, BLK), :]
-            return 0
-
-        lax.fori_loop(0, count, fill, 0, unroll=4)
+            if named:
+                lax.fori_loop(c * (count // parts), (c + 1) * (count // parts), fill, 0, unroll=4)
+        if not named:
+            lax.fori_loop(0, count, fill, 0, unroll=4)
         moves.append(pltpu.make_async_copy(packet, out.at[:, pl.ds(e * rows, packet.shape[1])], done.at[e]))
         moves[-1].start()
     for move in moves:
@@ -179,7 +182,7 @@
     columns = inject.shape[2]
     rows = min(orbitals, owner.shape[0] * BLK)
     part = CAP * BLK
-    parts = 2
+    parts = 4
     return pl.pallas_call(
         pairs_kernel,
         name="pairs",
@@ -396,12 +399,16 @@
 def work_kernel(early, *refs):
     green, source, parts = refs[:3]
     held, (image, upto) = refs[3:-2], refs[-2:]
-    low_plane = lax.axis_index("sec") // GROUP == 0
-
-    @pl.when(low_plane if early else jnp.logical_not(low_plane))
+    plane = lax.axis_index("sec") // GROUP
+    first, second = plane == 0, plane == 1
+
+    @pl.when(first if early else jnp.logical_not(first))
     def _():
         for e in range(green.shape[0]):
             image[e] = dot(green[e], source[e])
+
+    @pl.when(jnp.logical_not(second) if early else second)
+    def _():
         maps = (parts[0, 0], parts[1, 0])
         for j in range(1, GROUP - 1):
             maps = two_parts(times((parts[0, j], parts[1, j]), maps))
@@ -409,9 +416,12 @@
 
     if held:
 
-        @pl.when(low_plane)
+        @pl.when(first)
         def _():
             image[...] = held[0][...]
+
+        @pl.when(jnp.logical_not(second))
+        def _():
             upto[...] = held[1][...]
 
 
@@ -497,7 +507,7 @@
         scratch_shapes=[
             pltpu.VMEM((GROUP, half, columns), BF16),
             pltpu.VMEM(image.shape, BF16),
-            pltpu.SemaphoreType.DMA((energies, 2)),
+            pltpu.SemaphoreType.DMA((energies, 4)),
         ],
         compiler_params=pltpu.CompilerParams(vmem_limit_bytes=VMEM_SMALL),
         cost_estimate=pl.CostEstimate(flops=int(1.3 * PEAK), bytes_accessed=0, transcendentals=0),

time: 49.1 us -> 50.3 us (1.024)
  Pallas kernels: 13.7 us -> 14.3 us
  starting transfers between devices: 21.9 us -> 22.5 us
    ppermute x4, starting transfers between devices: 7.06 us -> 7.57 us  [between(): return lax.ppermute(item, 'sec', pairs)]
where the time goes in v32:
time: 50.3 us; the launch traced here: 49.9 us
  starting transfers between devices  22.5 us (45%)
  Pallas kernels  14.3 us (28%)
  waiting for transfers between devices  9.67 us (19%)
  local copies, waits for them, and re-layouts  3.09 us (6%)
    all_to_all x1, waiting for transfers between devices, per_device(): lax.all_to_all(outgoing, 'sec', split_axis=0, concat_axis=0, tiled=True)  9.01 us
    ppermute x4, starting transfers between devices, between(): return lax.ppermute(item, 'sec', pairs)  7.57 us
    all_to_all x1, starting transfers between devices, per_device(): lax.all_to_all(outgoing, 'sec', split_axis=0, concat_axis=0, tiled=True)  7.5 us
    pallas_call x1, Pallas kernels, outgoing_pairs(): pl.pallas_call(pairs_kernel, name='pairs', in_specs=[IN_HBM] * 4, out_sha...  4.53 us
    ppermute x3, starting transfers between devices, to_across(): lax.ppermute(item, 'sec', [(s, s // GROUP * GROUP + (s % GROUP + CORES) %...  3.68 us
    unnamed x14, local copies, waits for them, and re-layouts  3.09 us
    pallas_call x2, Pallas kernels, image_and_maps(): call(functools.partial(work_kernel, not held), 'image_and_maps', [IN_VMEM...  2.05 us
    pallas_call x1, Pallas kernels, propagator(): call(prop_kernel, 'prop', [IN_SMEM, IN_VMEM, IN_VMEM, IN_PLACE], shape(en...  1.9 us
  transfers between devices with their start and end apart: 16, of which 3 were waited for; matrix products, arithmetic and copies ran while one was open for 0% of the time, Pallas kernels for 16%

profile of v32, /device:TPU:0, one launch (start us, length us, event | category | flops | bytes accessed | tf_op | source)
XLA Modules:
  0.0 49.9 jit_solution(16042853840535576782)
XLA Ops:
  0.0 4.5 %pairs.1 = bf16[16,136,128]{2,1,0:T(8,128)(2,1)} custom-call(s32[16]{0:T(128)} %bitcast.21, s32[2,16]{1,0:T(2,128)} %bitcast.20, bf16[2,1024,1024]{2,1,0:T(8,128)(2,1)} %bitcast.9, bf16[2,1024,128]{2,1,0:T(8,128)(2,1)} %bitcast.14), custom_call_target="tpu_custom_call" | custom-call | flops 4600000000 | tf_op jit(solution)/shard_map/pairs/pallas_call | solution.py:186
  4.5 0.0 copy-start.2
  4.6 7.5 %all-to-all-start = ((bf16[16,136,128]{2,1,0:T(8,128)(2,1)}), bf16[16,136,128]{2,1,0:T(8,128)(2,1)S(1)}, u32[]{:S(2)}, u32[]{:S(2)}) async-start(bf16[16,136,128]{2,1,0:T(8,128)(2,1)} %pairs.1), calls=%async_computation | async-start | bytes 1114112 | tf_op jit(solution)/shard_map/all_to_all | solution.py:572
  12.1 0.0 copy-start
  12.1 2.2 %copy-done = bf16[1,2,1024,1024]{3,2,1,0:T(8,128)(2,1)S(1)} copy-done((bf16[1,2,1024,1024]{3,2,1,0:T(8,128)(2,1)S(1)}, bf16[1,2,1024,1024]{3,2,1,0:T(8,128)(2,1)}, u32[]{:S(2)}) %copy-start) | copy-done | bytes 4194328
  14.3 1.1 %face_maps.1 = (f32[256,256]{1,0:T(8,128)S(1)}, f32[256,256]{1,0:T(8,128)S(1)}, bf16[256,1024]{1,0:T(8,128)(2,1)S(1)}, bf16[256,1024]{1,0:T(8,128)(2,1)S(1)}) custom-call(s32[2,8]{1,0:T(2,128)S(1)} %bitcast.18, bf16[2,1024,1024]{2,1,0:T(8,128)(2,1)S(1)} %bitcast.10, bf16[1024,256]{1,0:T(8,128)(2,1)S(1)} %bitcast.16), custom_call_target="tpu_custom_call" | custom-call | flops 1380000000 | tf_op jit(solution)/shard_map/face_maps/pallas_call | solution.py:228
  15.4 0.0 copy-start.5
  15.4 0.8 %copy-done.5 = bf16[256,1024]{1,0:T(8,128)(2,1)} copy-done((bf16[256,1024]{1,0:T(8,128)(2,1)}, bf16[256,1024]{1,0:T(8,128)(2,1)S(1)}, u32[]{:S(2)}) %copy-start.5) | copy-done | bytes 524312
  16.2 1.9 %collective-permute-start.3 = (f32[256,256]{1,0:T(8,128)S(1)}, f32[256,256]{1,0:T(8,128)S(1)}, u32[]{:S(2)}, u32[]{:S(2)}) collective-permute-start(f32[256,256]{1,0:T(8,128)S(1)} %get-tuple-element.32), channel_id=1, source_target_pairs={{0,2},{1,3},{2,0},{3,1},{4,6},{5,7},{6,4},{7,5},{8,10},{9,11},{10,... | collective-permute-start | bytes 786440 | tf_op jit(solution)/shard_map/ppermute | solution.py:522
  18.1 0.0 collective-permute-start.5
  18.1 9.0 %all-to-all-done.received = bf16[16,136,128]{2,1,0:T(8,128)(2,1)S(1)} async-done(((bf16[16,136,128]{2,1,0:T(8,128)(2,1)}), bf16[16,136,128]{2,1,0:T(8,128)(2,1)S(1)}, u32[]{:S(2)}, u32[]{:S(2)}) %all-to-all-start) | async-done | bytes 557088 | tf_op jit(solution)/shard_map/all_to_all | solution.py:572
  27.1 0.9 %source.1.refs_1_ = bf16[2,1024,128]{2,1,0:T(8,128)(2,1)S(1)} custom-call(bf16[16,136,128]{2,1,0:T(8,128)(2,1)S(1)} %all-to-all-done.received, bf16[2,1024,128]{2,1,0:T(8,128)(2,1)S(1)} %bitcast.15), custom_call_target="tpu_custom_call" | custom-call | flops 1150000000 | tf_op jit(solution)/shard_map/source/pallas_call | solution.py:314
  28.1 0.0 copy-start.1
  28.1 0.1 copy-done.6
  28.2 0.5 %face_quarters.1 = (bf16[64,256]{1,0:T(8,128)(2,1)S(1)}, bf16[64,256]{1,0:T(8,128)(2,1)S(1)}, bf16[64,256]{1,0:T(8,128)(2,1)S(1)}, bf16[64,256]{1,0:T(8,128)(2,1)S(1)}) custom-call(bf16[2,1024,128]{2,1,0:T(8,128)(2,1)S(1)} %source.1.refs_1_, bf16[256,1024]{1,0:T(8,128)(2,1)S(1)} %get-tuple-element.25.refs_0_, bf16[256,1024]{1,0:T(8,128)(2,1)S(1)} %copy-done.6), custom_call_target="tpu_custom_call" | custom-call | flops 690000000 | tf_op jit(solution)/shard_map/face_quarters/pallas_call | solution.py:347
  28.7 0.0 collective-permute-done.3._map
  28.7 0.1 collective-permute-start.4
  28.8 0.9 %collective-permute-start = (bf16[64,256]{1,0:T(8,128)(2,1)S(1)}, bf16[64,256]{1,0:T(8,128)(2,1)S(1)}, u32[]{:S(2)}, u32[]{:S(2)}) collective-permute-start(bf16[64,256]{1,0:T(8,128)(2,1)S(1)} %get-tuple-element.28), channel_id=1, source_target_pairs={{0,3},{1,2},{2,1},{3,0},{4,7},{5,6},{6,5},{7,4},{8,11},{9,10},{10,... | collective-permute-start | bytes 98312 | tf_op jit(solution)/shard_map/ppermute | solution.py:526
  29.7 1.3 %collective-permute-start.1 = (bf16[64,256]{1,0:T(8,128)(2,1)S(1)}, bf16[64,256]{1,0:T(8,128)(2,1)S(1)}, u32[]{:S(2)}, u32[]{:S(2)}) collective-permute-start(bf16[64,256]{1,0:T(8,128)(2,1)S(1)} %get-tuple-element.29), channel_id=1, source_target_pairs={{0,2},{1,3},{2,0},{3,1},{4,6},{5,7},{6,4},{7,5},{8,10},{9,11},{10,... | collective-permute-start | bytes 98312 | tf_op jit(solution)/shard_map/ppermute | solution.py:522
  30.9 0.0 collective-permute-start.2
  30.9 0.0 collective-permute-done.5.near
  30.9 0.0 collective-permute-done.4.far
  30.9 0.8 %chain_maps.1 = (bf16[256,256]{1,0:T(8,128)(2,1)S(1)}, bf16[2,4,256,256]{3,2,1,0:T(8,128)(2,1)S(1)}) custom-call(f32[256,256]{1,0:T(8,128)S(1)} %get-tuple-element.31.own, f32[256,256]{1,0:T(8,128)S(1)} %collective-permute-done.4.far, f32[256,256]{1,0:T(8,128)S(1)} %after_exchange.1.across, f32[256,256]{1,0:T(8,128)S(1)} %collective-permute-done.5.near), custom_call_target="tpu_custom_call" | custom-call | flops 1035000000 | tf_op jit(solution)/shard_map/chain_maps/pallas_call | solution.py:273
  31.8 1.9 %image_and_maps.2 = (f32[2,1024,128]{2,1,0:T(8,128)S(1)}, bf16[2,2,256,256]{3,2,1,0:T(8,128)(2,1)S(1)}) custom-call(bf16[2,1024,1024]{2,1,0:T(8,128)(2,1)S(1)} %bitcast.11, bf16[2,1024,128]{2,1,0:T(8,128)(2,1)S(1)} %source.1.refs_1_, bf16[2,4,256,256]{3,2,1,0:T(8,128)(2,1)S(1)} %get-tuple-element.33.refs_2_.parts), custom_call_target="tpu_custom_call" | custom-call | flops 2300000000 | tf_op jit(solution)/shard_map/image_and_maps/pallas_call | solution.py:430
  33.7 0.7 %collective-permute-start.10 = (bf16[256,256]{1,0:T(8,128)(2,1)S(1)}, bf16[256,256]{1,0:T(8,128)(2,1)S(1)}, u32[]{:S(2)}, u32[]{:S(2)}) collective-permute-start(bf16[256,256]{1,0:T(8,128)(2,1)S(1)} %get-tuple-element.36), channel_id=1, source_target_pairs={{4,8},{8,12},{5,13},{6,10},{10,14},{7,15},{20,24},{24,28},{21,29},... | collective-permute-start | bytes 393224 | tf_op jit(solution)/shard_map/ppermute | solution.py:544
  34.4 0.0 collective-permute-done.far
  34.4 0.0 collective-permute-done.1.across
  34.4 0.0 collective-permute-done.2.near
  34.4 0.6 %plane_total.1 = (bf16[64,256]{1,0:T(8,128)(2,1)S(1)}, f32[3,64,256]{2,1,0:T(8,128)S(1)}) custom-call(bf16[64,256]{1,0:T(8,128)(2,1)S(1)} %get-tuple-element.27._packets.own, bf16[64,256]{1,0:T(8,128)(2,1)S(1)} %collective-permute-done.far, bf16[64,256]{1,0:T(8,128)(2,1)S(1)} %collective-permute-done.1.across, ...), custom_call_target="tpu_custom_call" | custom-call | flops 3449999872 | tf_op jit(solution)/shard_map/plane_total/pallas_call | solution.py:389
  35.0 3.7 %collective-permute-start.6 = (bf16[64,256]{1,0:T(8,128)(2,1)S(1)}, bf16[64,256]{1,0:T(8,128)(2,1)S(1)}, u32[]{:S(2)}, u32[]{:S(2)}) collective-permute-start(bf16[64,256]{1,0:T(8,128)(2,1)S(1)} %get-tuple-element.35), channel_id=1, source_target_pairs={{0,12},{1,13},{2,14},{3,15},{16,28},{17,29},{18,30},{19,31}} | collective-permute-start | bytes 98312 | tf_op jit(solution)/shard_map/ppermute | solution.py:550
  38.7 1.9 %collective-permute-start.7 = (bf16[64,256]{1,0:T(8,128)(2,1)S(1)}, bf16[64,256]{1,0:T(8,128)(2,1)S(1)}, u32[]{:S(2)}, u32[]{:S(2)}) collective-permute-start(bf16[64,256]{1,0:T(8,128)(2,1)S(1)} %get-tuple-element.35), channel_id=1, source_target_pairs={{0,4},{1,5},{2,6},{3,7},{16,20},{17,21},{18,22},{19,23}} | collective-permute-start | bytes 98312 | tf_op jit(solution)/shard_map/ppermute | solution.py:550
  40.7 1.3 %collective-permute-start.8 = (bf16[64,256]{1,0:T(8,128)(2,1)S(1)}, bf16[64,256]{1,0:T(8,128)(2,1)S(1)}, u32[]{:S(2)}, u32[]{:S(2)}) collective-permute-start(bf16[64,256]{1,0:T(8,128)(2,1)S(1)} %get-tuple-element.35), channel_id=1, source_target_pairs={{0,8},{1,9},{2,10},{3,11},{4,12},{5,13},{6,14},{7,15},{16,24},{17,... | collective-permute-start | bytes 98312 | tf_op jit(solution)/shard_map/ppermute | solution.py:550
  42.0 0.7 %collective-permute-start.9 = (bf16[64,256]{1,0:T(8,128)(2,1)S(1)}, bf16[64,256]{1,0:T(8,128)(2,1)S(1)}, u32[]{:S(2)}, u32[]{:S(2)}) collective-permute-start(bf16[64,256]{1,0:T(8,128)(2,1)S(1)} %get-tuple-element.35), channel_id=1, source_target_pairs={{4,8},{5,9},{6,10},{7,11},{8,12},{9,13},{10,14},{11,15},{20,24},{2... | collective-permute-start | bytes 98312 | tf_op jit(solution)/shard_map/ppermute | solution.py:550
  42.6 0.7 %collective-permute-start.11 = (bf16[256,256]{1,0:T(8,128)(2,1)S(1)}, bf16[256,256]{1,0:T(8,128)(2,1)S(1)}, u32[]{:S(2)}, u32[]{:S(2)}) collective-permute-start(bf16[256,256]{1,0:T(8,128)(2,1)S(1)} %collective-permute-done.10.got), channel_id=1, source_target_pairs={{8,9},{9,8},{10,11},{11,10},{12,13},{13,12},{14,15},{15,14},{24,25... | collective-permute-start | bytes 393224 | tf_op jit(solution)/shard_map/ppermute | solution.py:545
  43.3 0.1 image_and_maps.3
  43.5 0.0 collective-permute-done.7.near_one
  43.5 0.1 collective-permute-done.8.second
  43.5 0.0 collective-permute-done.9.far_one
  43.5 0.0 collective-permute-done.11.other
  43.5 0.7 %entering.1 = (bf16[64,256]{1,0:T(8,128)(2,1)S(1)}, bf16[64,256]{1,0:T(8,128)(2,1)S(1)}, bf16[64,256]{1,0:T(8,128)(2,1)S(1)}, bf16[64,256]{1,0:T(8,128)(2,1)S(1)}) custom-call(bf16[64,256]{1,0:T(8,128)(2,1)S(1)} %collective-permute-done.6.third, bf16[64,256]{1,0:T(8,128)(2,1)S(1)} %collective-permute-done.7.near_one, ...), custom_call_target="tpu_custom_call" | custom-call | flops 1610000000 | tf_op jit(solution)/shard_map/entering/pallas_call | solution.py:470
  44.3 0.5 collective-permute-start.12
  44.8 0.5 %collective-permute-start.13 = (bf16[64,256]{1,0:T(8,128)(2,1)S(1)}, bf16[64,256]{1,0:T(8,128)(2,1)S(1)}, u32[]{:S(2)}, u32[]{:S(2)}) collective-permute-start(bf16[64,256]{1,0:T(8,128)(2,1)S(1)} %get-tuple-element.42), channel_id=1, source_target_pairs={{0,2},{1,3},{2,0},{3,1},{4,6},{5,7},{6,4},{7,5},{8,10},{9,11},{10,... | collective-permute-start | bytes 98312 | tf_op jit(solution)/shard_map/ppermute | solution.py:522
  45.3 0.9 %collective-permute-start.14 = (bf16[64,256]{1,0:T(8,128)(2,1)S(1)}, bf16[64,256]{1,0:T(8,128)(2,1)S(1)}, u32[]{:S(2)}, u32[]{:S(2)}) collective-permute-start(bf16[64,256]{1,0:T(8,128)(2,1)S(1)} %get-tuple-element.43), channel_id=1, source_target_pairs={{0,1},{1,0},{2,3},{3,2},{4,5},{5,4},{6,7},{7,6},{8,9},{9,8},{10,11... | collective-permute-start | bytes 98312 | tf_op jit(solution)/shard_map/ppermute | solution.py:518
  46.2 1.9 %prop.1 = bf16[2,1024,256]{2,1,0:T(8,128)(2,1)S(1)} custom-call(s32[2,8]{1,0:T(2,128)S(1)} %bitcast.19, bf16[2,1024,1024]{2,1,0:T(8,128)(2,1)S(1)} %bitcast.13, bf16[1024,256]{1,0:T(8,128)(2,1)S(1)} %bitcast.17, bf16[64,256]{1,0:T(8,128)(2,1)S(1)} %get-tuple-element.40._tie.own), custom_call_target="tpu_custom_call" | custom-call | flops 1724999936 | tf_op jit(solution)/shard_map/prop/pallas_call | solution.py:247
  48.1 0.0 collective-permute-done.12.far
  48.1 0.6 %collective-permute-done.13.across = bf16[64,256]{1,0:T(8,128)(2,1)S(1)} collective-permute-done((bf16[64,256]{1,0:T(8,128)(2,1)S(1)}, bf16[64,256]{1,0:T(8,128)(2,1)S(1)}, u32[]{:S(2)}, u32[]{:S(2)}) %collective-permute-start.13) | collective-permute-done | bytes 32800 | tf_op jit(solution)/shard_map/ppermute | solution.py:522
  48.7 0.0 collective-permute-done.14.near
  48.7 1.2 %waves.1 = bf16[2,1024,128]{2,1,0:T(8,128)(2,1)} custom-call(bf16[64,256]{1,0:T(8,128)(2,1)S(1)} %get-tuple-element.40._tie.own, bf16[64,256]{1,0:T(8,128)(2,1)S(1)} %collective-permute-done.12.far, bf16[64,256]{1,0:T(8,128)(2,1)S(1)} %collective-permute-done.13.across, bf16[64,256]{1,0:T(8,128)(2,1)S(1)} %collective-permute-done.14.near, ...), custom_call_target="tpu_custom_call" | custom-call | flops 1495000064 | tf_op jit(solution)/shard_map/waves/pallas_call | solution.py:501
  (10 shorter events, 0.0 us)
Async XLA Ops:
  0.0 12.1 %copy-start.3 = (bf16[1,1024,256]{2,1,0:T(8,128)(2,1)S(1)}, bf16[1,1024,256]{2,1,0:T(8,128)(2,1)}, u32[]{:S(2)}) copy-start(bf16[1,1024,256]{2,1,0:T(8,128)(2,1)} %param.8) | copy-start | bytes 1572868
  0.0 12.1 %copy-start.4 = (s32[1,8,2]{1,2,0:T(2,128)S(1)}, s32[1,8,2]{1,2,0:T(2,128)}, u32[]{:S(2)}) copy-start(s32[1,8,2]{1,2,0:T(2,128)} %param.9) | copy-start | bytes 196
  4.5 22.6 %copy-start.2 = (bf16[1,2,1024,128]{3,2,1,0:T(8,128)(2,1)S(1)}, bf16[1,2,1024,128]{3,2,1,0:T(8,128)(2,1)}, u32[]{:S(2)}) copy-start(bf16[1,2,1024,128]{3,2,1,0:T(8,128)(2,1)} %param.7) | copy-start | bytes 1572868
  4.6 22.6 %all-to-all-start = ((bf16[16,136,128]{2,1,0:T(8,128)(2,1)}), bf16[16,136,128]{2,1,0:T(8,128)(2,1)S(1)}, u32[]{:S(2)}, u32[]{:S(2)}) async-start(bf16[16,136,128]{2,1,0:T(8,128)(2,1)} %pairs.1), calls=%async_computation | async-start | bytes 1114112 | tf_op jit(solution)/shard_map/all_to_all | solution.py:572
  12.1 2.2 %copy-start = (bf16[1,2,1024,1024]{3,2,1,0:T(8,128)(2,1)S(1)}, bf16[1,2,1024,1024]{3,2,1,0:T(8,128)(2,1)}, u32[]{:S(2)}) copy-start(bf16[1,2,1024,1024]{3,2,1,0:T(8,128)(2,1)} %param.6) | copy-start | bytes 12582916
  15.4 0.8 %copy-start.5 = (bf16[256,1024]{1,0:T(8,128)(2,1)}, bf16[256,1024]{1,0:T(8,128)(2,1)S(1)}, u32[]{:S(2)}) copy-start(bf16[256,1024]{1,0:T(8,128)(2,1)S(1)} %get-tuple-element.26.refs_1_) | copy-start | bytes 1572868
  16.2 12.5 %collective-permute-start.3 = (f32[256,256]{1,0:T(8,128)S(1)}, f32[256,256]{1,0:T(8,128)S(1)}, u32[]{:S(2)}, u32[]{:S(2)}) collective-permute-start(f32[256,256]{1,0:T(8,128)S(1)} %get-tuple-element.32), channel_id=1, source_target_pairs={{0,2},{1,3},{2,0},{3,1},{4,6},{5,7},{6,4},{7,5},{8,10},{9,11},{10,... | collective-permute-start | bytes 786440 | tf_op jit(solution)/shard_map/ppermute | solution.py:522
  18.1 12.8 %collective-permute-start.5 = (f32[256,256]{1,0:T(8,128)S(1)}, f32[256,256]{1,0:T(8,128)S(1)}, u32[]{:S(2)}, u32[]{:S(2)}) collective-permute-start(f32[256,256]{1,0:T(8,128)S(1)} %get-tuple-element.31.own), channel_id=1, source_target_pairs={{0,1},{1,0},{2,3},{3,2},{4,5},{5,4},{6,7},{7,6},{8,9},{9,8},{10,11... | collective-permute-start | bytes 786440 | tf_op jit(solution)/shard_map/ppermute | solution.py:518
  27.1 1.0 %copy-start.6 = (bf16[256,1024]{1,0:T(8,128)(2,1)S(1)}, bf16[256,1024]{1,0:T(8,128)(2,1)}, u32[]{:S(2)}) copy-start(bf16[256,1024]{1,0:T(8,128)(2,1)} %copy-done.5) | copy-start | bytes 1572868
  28.1 3.7 %copy-start.1 = (bf16[1,2,1024,1024]{3,2,1,0:T(8,128)(2,1)S(1)}, bf16[1,2,1024,1024]{3,2,1,0:T(8,128)(2,1)}, u32[]{:S(2)}) copy-start(bf16[1,2,1024,1024]{3,2,1,0:T(8,128)(2,1)} %param.6) | copy-start | bytes 12582916
  28.7 2.2 %collective-permute-start.4 = (f32[256,256]{1,0:T(8,128)S(1)}, f32[256,256]{1,0:T(8,128)S(1)}, u32[]{:S(2)}, u32[]{:S(2)}) collective-permute-start(f32[256,256]{1,0:T(8,128)S(1)} %after_exchange.1.across), channel_id=1, source_target_pairs={{0,1},{1,0},{2,3},{3,2},{4,5},{5,4},{6,7},{7,6},{8,9},{9,8},{10,11... | collective-permute-start | bytes 786440 | tf_op jit(solution)/shard_map/ppermute | solution.py:518
  28.8 5.6 %collective-permute-start = (bf16[64,256]{1,0:T(8,128)(2,1)S(1)}, bf16[64,256]{1,0:T(8,128)(2,1)S(1)}, u32[]{:S(2)}, u32[]{:S(2)}) collective-permute-start(bf16[64,256]{1,0:T(8,128)(2,1)S(1)} %get-tuple-element.28), channel_id=1, source_target_pairs={{0,3},{1,2},{2,1},{3,0},{4,7},{5,6},{6,5},{7,4},{8,11},{9,10},{10,... | collective-permute-start | bytes 98312 | tf_op jit(solution)/shard_map/ppermute | solution.py:526
  29.7 4.7 %collective-permute-start.1 = (bf16[64,256]{1,0:T(8,128)(2,1)S(1)}, bf16[64,256]{1,0:T(8,128)(2,1)S(1)}, u32[]{:S(2)}, u32[]{:S(2)}) collective-permute-start(bf16[64,256]{1,0:T(8,128)(2,1)S(1)} %get-tuple-element.29), channel_id=1, source_target_pairs={{0,2},{1,3},{2,0},{3,1},{4,6},{5,7},{6,4},{7,5},{8,10},{9,11},{10,... | collective-permute-start | bytes 98312 | tf_op jit(solution)/shard_map/ppermute | solution.py:522
  30.9 3.5 %collective-permute-start.2 = (bf16[64,256]{1,0:T(8,128)(2,1)S(1)}, bf16[64,256]{1,0:T(8,128)(2,1)S(1)}, u32[]{:S(2)}, u32[]{:S(2)}) collective-permute-start(bf16[64,256]{1,0:T(8,128)(2,1)S(1)} %get-tuple-element.30), channel_id=1, source_target_pairs={{0,1},{1,0},{2,3},{3,2},{4,5},{5,4},{6,7},{7,6},{8,9},{9,8},{10,11... | collective-permute-start | bytes 98312 | tf_op jit(solution)/shard_map/ppermute | solution.py:518
  33.7 8.9 %collective-permute-start.10 = (bf16[256,256]{1,0:T(8,128)(2,1)S(1)}, bf16[256,256]{1,0:T(8,128)(2,1)S(1)}, u32[]{:S(2)}, u32[]{:S(2)}) collective-permute-start(bf16[256,256]{1,0:T(8,128)(2,1)S(1)} %get-tuple-element.36), channel_id=1, source_target_pairs={{4,8},{8,12},{5,13},{6,10},{10,14},{7,15},{20,24},{24,28},{21,29},... | collective-permute-start | bytes 393224 | tf_op jit(solution)/shard_map/ppermute | solution.py:544
  35.0 8.4 %collective-permute-start.6 = (bf16[64,256]{1,0:T(8,128)(2,1)S(1)}, bf16[64,256]{1,0:T(8,128)(2,1)S(1)}, u32[]{:S(2)}, u32[]{:S(2)}) collective-permute-start(bf16[64,256]{1,0:T(8,128)(2,1)S(1)} %get-tuple-element.35), channel_id=1, source_target_pairs={{0,12},{1,13},{2,14},{3,15},{16,28},{17,29},{18,30},{19,31}} | collective-permute-start | bytes 98312 | tf_op jit(solution)/shard_map/ppermute | solution.py:550
  38.7 4.8 %collective-permute-start.7 = (bf16[64,256]{1,0:T(8,128)(2,1)S(1)}, bf16[64,256]{1,0:T(8,128)(2,1)S(1)}, u32[]{:S(2)}, u32[]{:S(2)}) collective-permute-start(bf16[64,256]{1,0:T(8,128)(2,1)S(1)} %get-tuple-element.35), channel_id=1, source_target_pairs={{0,4},{1,5},{2,6},{3,7},{16,20},{17,21},{18,22},{19,23}} | collective-permute-start | bytes 98312 | tf_op jit(solution)/shard_map/ppermute | solution.py:550
  40.7 2.9 %collective-permute-start.8 = (bf16[64,256]{1,0:T(8,128)(2,1)S(1)}, bf16[64,256]{1,0:T(8,128)(2,1)S(1)}, u32[]{:S(2)}, u32[]{:S(2)}) collective-permute-start(bf16[64,256]{1,0:T(8,128)(2,1)S(1)} %get-tuple-element.35), channel_id=1, source_target_pairs={{0,8},{1,9},{2,10},{3,11},{4,12},{5,13},{6,14},{7,15},{16,24},{17,... | collective-permute-start | bytes 98312 | tf_op jit(solution)/shard_map/ppermute | solution.py:550
  42.0 1.6 %collective-permute-start.9 = (bf16[64,256]{1,0:T(8,128)(2,1)S(1)}, bf16[64,256]{1,0:T(8,128)(2,1)S(1)}, u32[]{:S(2)}, u32[]{:S(2)}) collective-permute-start(bf16[64,256]{1,0:T(8,128)(2,1)S(1)} %get-tuple-element.35), channel_id=1, source_target_pairs={{4,8},{5,9},{6,10},{7,11},{8,12},{9,13},{10,14},{11,15},{20,24},{2... | collective-permute-start | bytes 98312 | tf_op jit(solution)/shard_map/ppermute | solution.py:550
  42.6 0.9 %collective-permute-start.11 = (bf16[256,256]{1,0:T(8,128)(2,1)S(1)}, bf16[256,256]{1,0:T(8,128)(2,1)S(1)}, u32[]{:S(2)}, u32[]{:S(2)}) collective-permute-start(bf16[256,256]{1,0:T(8,128)(2,1)S(1)} %collective-permute-done.10.got), channel_id=1, source_target_pairs={{8,9},{9,8},{10,11},{11,10},{12,13},{13,12},{14,15},{15,14},{24,25... | collective-permute-start | bytes 393224 | tf_op jit(solution)/shard_map/ppermute | solution.py:545
  44.3 3.8 %collective-permute-start.12 = (bf16[64,256]{1,0:T(8,128)(2,1)S(1)}, bf16[64,256]{1,0:T(8,128)(2,1)S(1)}, u32[]{:S(2)}, u32[]{:S(2)}) collective-permute-start(bf16[64,256]{1,0:T(8,128)(2,1)S(1)} %get-tuple-element.41), channel_id=1, source_target_pairs={{0,3},{1,2},{2,1},{3,0},{4,7},{5,6},{6,5},{7,4},{8,11},{9,10},{10,... | collective-permute-start | bytes 98312 | tf_op jit(solution)/shard_map/ppermute | solution.py:526
  44.8 3.9 %collective-permute-start.13 = (bf16[64,256]{1,0:T(8,128)(2,1)S(1)}, bf16[64,256]{1,0:T(8,128)(2,1)S(1)}, u32[]{:S(2)}, u32[]{:S(2)}) collective-permute-start(bf16[64,256]{1,0:T(8,128)(2,1)S(1)} %get-tuple-element.42), channel_id=1, source_target_pairs={{0,2},{1,3},{2,0},{3,1},{4,6},{5,7},{6,4},{7,5},{8,10},{9,11},{10,... | collective-permute-start | bytes 98312 | tf_op jit(solution)/shard_map/ppermute | solution.py:522
  45.3 3.4 %collective-permute-start.14 = (bf16[64,256]{1,0:T(8,128)(2,1)S(1)}, bf16[64,256]{1,0:T(8,128)(2,1)S(1)}, u32[]{:S(2)}, u32[]{:S(2)}) collective-permute-start(bf16[64,256]{1,0:T(8,128)(2,1)S(1)} %get-tuple-element.43), channel_id=1, source_target_pairs={{0,1},{1,0},{2,3},{3,2},{4,5},{5,4},{6,7},{7,6},{8,9},{9,8},{10,11... | collective-permute-start | bytes 98312 | tf_op jit(solution)/shard_map/ppermute | solution.py:518

commit v33 on v32

--- a/solution.py
+++ b/solution.py
@@ -182,7 +182,7 @@
     columns = inject.shape[2]
     rows = min(orbitals, owner.shape[0] * BLK)
     part = CAP * BLK
-    parts = 4
+    parts = 2
     return pl.pallas_call(
         pairs_kernel,
         name="pairs",
@@ -433,7 +433,7 @@
         [IN_VMEM] * (3 + len(held)),
         [shape(*source.shape, dtype=F32), shape(2, GROUP - 2, face, face)],
         [],
-        2.0,
+        2.0 if held else 0.5,
     )(green, source, parts, *held)
 
 

time: 50.3 us -> 49.4 us (0.982)
  starting transfers between devices: 22.5 us -> 21.8 us
    ppermute x4, starting transfers between devices: 7.57 us -> 6.92 us  [between(): return lax.ppermute(item, 'sec', pairs)]
    pallas_call x1, Pallas kernels: 4.53 us -> 4 us  [outgoing_pairs(): pl.pallas_call(pairs_kernel, name='pairs', in_specs=[IN_HBM] * 4, out_sha...]
where the time goes in v33:
time: 49.4 us; the launch traced here: 49 us
  starting transfers between devices  21.8 us (44%)
  Pallas kernels  13.8 us (28%)
  waiting for transfers between devices  10 us (20%)
  local copies, waits for them, and re-layouts  3.1 us (6%)
    all_to_all x1, waiting for transfers between devices, per_device(): lax.all_to_all(outgoing, 'sec', split_axis=0, concat_axis=0, tiled=True)  9.01 us
    all_to_all x1, starting transfers between devices, per_device(): lax.all_to_all(outgoing, 'sec', split_axis=0, concat_axis=0, tiled=True)  7.44 us
    ppermute x4, starting transfers between devices, between(): return lax.ppermute(item, 'sec', pairs)  6.92 us
    pallas_call x1, Pallas kernels, outgoing_pairs(): pl.pallas_call(pairs_kernel, name='pairs', in_specs=[IN_HBM] * 4, out_sha...  4 us
    ppermute x3, starting transfers between devices, to_across(): lax.ppermute(item, 'sec', [(s, s // GROUP * GROUP + (s % GROUP + CORES) %...  3.68 us
    unnamed x14, local copies, waits for them, and re-layouts  3.1 us
    pallas_call x2, Pallas kernels, image_and_maps(): call(functools.partial(work_kernel, not held), 'image_and_maps', [IN_VMEM...  2.05 us
    pallas_call x1, Pallas kernels, propagator(): call(prop_kernel, 'prop', [IN_SMEM, IN_VMEM, IN_VMEM, IN_PLACE], shape(en...  1.9 us
  transfers between devices with their start and end apart: 16, of which 3 were waited for; matrix products, arithmetic and copies ran while one was open for 0% of the time, Pallas kernels for 16%

profile of v33, /device:TPU:0, one launch (start us, length us, event | category | flops | bytes accessed | tf_op | source)
XLA Modules:
  0.0 49.0 jit_solution(342050133431346306)
XLA Ops:
  0.0 4.0 %pairs.1 = bf16[16,136,128]{2,1,0:T(8,128)(2,1)} custom-call(s32[16]{0:T(128)} %bitcast.21, s32[2,16]{1,0:T(2,128)} %bitcast.20, bf16[2,1024,1024]{2,1,0:T(8,128)(2,1)} %bitcast.9, bf16[2,1024,128]{2,1,0:T(8,128)(2,1)} %bitcast.14), custom_call_target="tpu_custom_call" | custom-call | flops 4600000000 | tf_op jit(solution)/shard_map/pairs/pallas_call | solution.py:186
  4.0 0.0 copy-start.2
  4.0 7.4 %all-to-all-start = ((bf16[16,136,128]{2,1,0:T(8,128)(2,1)}), bf16[16,136,128]{2,1,0:T(8,128)(2,1)S(1)}, u32[]{:S(2)}, u32[]{:S(2)}) async-start(bf16[16,136,128]{2,1,0:T(8,128)(2,1)} %pairs.1), calls=%async_computation | async-start | bytes 1114112 | tf_op jit(solution)/shard_map/all_to_all | solution.py:572
  11.5 0.0 copy-start
  11.5 2.2 %copy-done = bf16[1,2,1024,1024]{3,2,1,0:T(8,128)(2,1)S(1)} copy-done((bf16[1,2,1024,1024]{3,2,1,0:T(8,128)(2,1)S(1)}, bf16[1,2,1024,1024]{3,2,1,0:T(8,128)(2,1)}, u32[]{:S(2)}) %copy-start) | copy-done | bytes 4194328
  13.7 1.1 %face_maps.1 = (f32[256,256]{1,0:T(8,128)S(1)}, f32[256,256]{1,0:T(8,128)S(1)}, bf16[256,1024]{1,0:T(8,128)(2,1)S(1)}, bf16[256,1024]{1,0:T(8,128)(2,1)S(1)}) custom-call(s32[2,8]{1,0:T(2,128)S(1)} %bitcast.18, bf16[2,1024,1024]{2,1,0:T(8,128)(2,1)S(1)} %bitcast.10, bf16[1024,256]{1,0:T(8,128)(2,1)S(1)} %bitcast.16), custom_call_target="tpu_custom_call" | custom-call | flops 1380000000 | tf_op jit(solution)/shard_map/face_maps/pallas_call | solution.py:228
  14.8 0.0 copy-start.5
  14.8 0.8 %copy-done.5 = bf16[256,1024]{1,0:T(8,128)(2,1)} copy-done((bf16[256,1024]{1,0:T(8,128)(2,1)}, bf16[256,1024]{1,0:T(8,128)(2,1)S(1)}, u32[]{:S(2)}) %copy-start.5) | copy-done | bytes 524312
  15.6 1.9 %collective-permute-start.3 = (f32[256,256]{1,0:T(8,128)S(1)}, f32[256,256]{1,0:T(8,128)S(1)}, u32[]{:S(2)}, u32[]{:S(2)}) collective-permute-start(f32[256,256]{1,0:T(8,128)S(1)} %get-tuple-element.32), channel_id=1, source_target_pairs={{0,2},{1,3},{2,0},{3,1},{4,6},{5,7},{6,4},{7,5},{8,10},{9,11},{10,... | collective-permute-start | bytes 786440 | tf_op jit(solution)/shard_map/ppermute | solution.py:522
  17.5 0.0 collective-permute-start.5
  17.5 9.0 %all-to-all-done.received = bf16[16,136,128]{2,1,0:T(8,128)(2,1)S(1)} async-done(((bf16[16,136,128]{2,1,0:T(8,128)(2,1)}), bf16[16,136,128]{2,1,0:T(8,128)(2,1)S(1)}, u32[]{:S(2)}, u32[]{:S(2)}) %all-to-all-start) | async-done | bytes 557088 | tf_op jit(solution)/shard_map/all_to_all | solution.py:572
  26.5 0.9 %source.1.refs_1_ = bf16[2,1024,128]{2,1,0:T(8,128)(2,1)S(1)} custom-call(bf16[16,136,128]{2,1,0:T(8,128)(2,1)S(1)} %all-to-all-done.received, bf16[2,1024,128]{2,1,0:T(8,128)(2,1)S(1)} %bitcast.15), custom_call_target="tpu_custom_call" | custom-call | flops 1150000000 | tf_op jit(solution)/shard_map/source/pallas_call | solution.py:314
  27.5 0.0 copy-start.1
  27.5 0.1 copy-done.6
  27.6 0.5 %face_quarters.1 = (bf16[64,256]{1,0:T(8,128)(2,1)S(1)}, bf16[64,256]{1,0:T(8,128)(2,1)S(1)}, bf16[64,256]{1,0:T(8,128)(2,1)S(1)}, bf16[64,256]{1,0:T(8,128)(2,1)S(1)}) custom-call(bf16[2,1024,128]{2,1,0:T(8,128)(2,1)S(1)} %source.1.refs_1_, bf16[256,1024]{1,0:T(8,128)(2,1)S(1)} %get-tuple-element.25.refs_0_, bf16[256,1024]{1,0:T(8,128)(2,1)S(1)} %copy-done.6), custom_call_target="tpu_custom_call" | custom-call | flops 690000000 | tf_op jit(solution)/shard_map/face_quarters/pallas_call | solution.py:347
  28.1 0.0 collective-permute-done.3._map
  28.1 0.1 collective-permute-start.4
  28.2 0.9 %collective-permute-start = (bf16[64,256]{1,0:T(8,128)(2,1)S(1)}, bf16[64,256]{1,0:T(8,128)(2,1)S(1)}, u32[]{:S(2)}, u32[]{:S(2)}) collective-permute-start(bf16[64,256]{1,0:T(8,128)(2,1)S(1)} %get-tuple-element.28), channel_id=1, source_target_pairs={{0,3},{1,2},{2,1},{3,0},{4,7},{5,6},{6,5},{7,4},{8,11},{9,10},{10,... | collective-permute-start | bytes 98312 | tf_op jit(solution)/shard_map/ppermute | solution.py:526
  29.1 1.3 %collective-permute-start.1 = (bf16[64,256]{1,0:T(8,128)(2,1)S(1)}, bf16[64,256]{1,0:T(8,128)(2,1)S(1)}, u32[]{:S(2)}, u32[]{:S(2)}) collective-permute-start(bf16[64,256]{1,0:T(8,128)(2,1)S(1)} %get-tuple-element.29), channel_id=1, source_target_pairs={{0,2},{1,3},{2,0},{3,1},{4,6},{5,7},{6,4},{7,5},{8,10},{9,11},{10,... | collective-permute-start | bytes 98312 | tf_op jit(solution)/shard_map/ppermute | solution.py:522
  30.3 0.0 collective-permute-start.2
  30.3 0.0 collective-permute-done.5.near
  30.3 0.0 collective-permute-done.4.far
  30.3 0.8 %chain_maps.1 = (bf16[256,256]{1,0:T(8,128)(2,1)S(1)}, bf16[2,4,256,256]{3,2,1,0:T(8,128)(2,1)S(1)}) custom-call(f32[256,256]{1,0:T(8,128)S(1)} %get-tuple-element.31.own, f32[256,256]{1,0:T(8,128)S(1)} %collective-permute-done.4.far, f32[256,256]{1,0:T(8,128)S(1)} %after_exchange.1.across, f32[256,256]{1,0:T(8,128)S(1)} %collective-permute-done.5.near), custom_call_target="tpu_custom_call" | custom-call | flops 1035000000 | tf_op jit(solution)/shard_map/chain_maps/pallas_call | solution.py:273
  31.2 0.7 %collective-permute-start.10 = (bf16[256,256]{1,0:T(8,128)(2,1)S(1)}, bf16[256,256]{1,0:T(8,128)(2,1)S(1)}, u32[]{:S(2)}, u32[]{:S(2)}) collective-permute-start(bf16[256,256]{1,0:T(8,128)(2,1)S(1)} %get-tuple-element.36), channel_id=1, source_target_pairs={{4,8},{8,12},{5,13},{6,10},{10,14},{7,15},{20,24},{24,28},{21,29},... | collective-permute-start | bytes 393224 | tf_op jit(solution)/shard_map/ppermute | solution.py:544
  31.9 1.9 %image_and_maps.2 = (f32[2,1024,128]{2,1,0:T(8,128)S(1)}, bf16[2,2,256,256]{3,2,1,0:T(8,128)(2,1)S(1)}) custom-call(bf16[2,1024,1024]{2,1,0:T(8,128)(2,1)S(1)} %bitcast.11, bf16[2,1024,128]{2,1,0:T(8,128)(2,1)S(1)} %source.1.refs_1_, bf16[2,4,256,256]{3,2,1,0:T(8,128)(2,1)S(1)} %get-tuple-element.33.refs_2_.parts), custom_call_target="tpu_custom_call" | custom-call | flops 575000000 | tf_op jit(solution)/shard_map/image_and_maps/pallas_call | solution.py:430
  33.8 0.0 collective-permute-done.far
  33.8 0.0 collective-permute-done.1.across
  33.8 0.0 collective-permute-done.2.near
  33.8 0.6 %plane_total.1 = (bf16[64,256]{1,0:T(8,128)(2,1)S(1)}, f32[3,64,256]{2,1,0:T(8,128)S(1)}) custom-call(bf16[64,256]{1,0:T(8,128)(2,1)S(1)} %get-tuple-element.27._packets.own, bf16[64,256]{1,0:T(8,128)(2,1)S(1)} %collective-permute-done.far, bf16[64,256]{1,0:T(8,128)(2,1)S(1)} %collective-permute-done.1.across, ...), custom_call_target="tpu_custom_call" | custom-call | flops 3449999872 | tf_op jit(solution)/shard_map/plane_total/pallas_call | solution.py:389
  34.4 3.7 %collective-permute-start.6 = (bf16[64,256]{1,0:T(8,128)(2,1)S(1)}, bf16[64,256]{1,0:T(8,128)(2,1)S(1)}, u32[]{:S(2)}, u32[]{:S(2)}) collective-permute-start(bf16[64,256]{1,0:T(8,128)(2,1)S(1)} %get-tuple-element.35), channel_id=1, source_target_pairs={{0,12},{1,13},{2,14},{3,15},{16,28},{17,29},{18,30},{19,31}} | collective-permute-start | bytes 98312 | tf_op jit(solution)/shard_map/ppermute | solution.py:550
  38.1 1.3 %collective-permute-start.7 = (bf16[64,256]{1,0:T(8,128)(2,1)S(1)}, bf16[64,256]{1,0:T(8,128)(2,1)S(1)}, u32[]{:S(2)}, u32[]{:S(2)}) collective-permute-start(bf16[64,256]{1,0:T(8,128)(2,1)S(1)} %get-tuple-element.35), channel_id=1, source_target_pairs={{0,4},{1,5},{2,6},{3,7},{16,20},{17,21},{18,22},{19,23}} | collective-permute-start | bytes 98312 | tf_op jit(solution)/shard_map/ppermute | solution.py:550
  39.4 1.3 %collective-permute-start.8 = (bf16[64,256]{1,0:T(8,128)(2,1)S(1)}, bf16[64,256]{1,0:T(8,128)(2,1)S(1)}, u32[]{:S(2)}, u32[]{:S(2)}) collective-permute-start(bf16[64,256]{1,0:T(8,128)(2,1)S(1)} %get-tuple-element.35), channel_id=1, source_target_pairs={{0,8},{1,9},{2,10},{3,11},{4,12},{5,13},{6,14},{7,15},{16,24},{17,... | collective-permute-start | bytes 98312 | tf_op jit(solution)/shard_map/ppermute | solution.py:550
  40.7 0.7 %collective-permute-start.9 = (bf16[64,256]{1,0:T(8,128)(2,1)S(1)}, bf16[64,256]{1,0:T(8,128)(2,1)S(1)}, u32[]{:S(2)}, u32[]{:S(2)}) collective-permute-start(bf16[64,256]{1,0:T(8,128)(2,1)S(1)} %get-tuple-element.35), channel_id=1, source_target_pairs={{4,8},{5,9},{6,10},{7,11},{8,12},{9,13},{10,14},{11,15},{20,24},{2... | collective-permute-start | bytes 98312 | tf_op jit(solution)/shard_map/ppermute | solution.py:550
  41.4 0.0 collective-permute-done.10.got
  41.4 0.7 %collective-permute-start.11 = (bf16[256,256]{1,0:T(8,128)(2,1)S(1)}, bf16[256,256]{1,0:T(8,128)(2,1)S(1)}, u32[]{:S(2)}, u32[]{:S(2)}) collective-permute-start(bf16[256,256]{1,0:T(8,128)(2,1)S(1)} %collective-permute-done.10.got), channel_id=1, source_target_pairs={{8,9},{9,8},{10,11},{11,10},{12,13},{13,12},{14,15},{15,14},{24,25... | collective-permute-start | bytes 393224 | tf_op jit(solution)/shard_map/ppermute | solution.py:545
  42.1 0.1 image_and_maps.3
  42.2 0.0 collective-permute-done.7.near_one
  42.2 0.1 collective-permute-done.8.second
  42.3 0.0 collective-permute-done.9.far_one
  42.3 0.0 collective-permute-done.11.other
  42.3 0.7 %entering.1 = (bf16[64,256]{1,0:T(8,128)(2,1)S(1)}, bf16[64,256]{1,0:T(8,128)(2,1)S(1)}, bf16[64,256]{1,0:T(8,128)(2,1)S(1)}, bf16[64,256]{1,0:T(8,128)(2,1)S(1)}) custom-call(bf16[64,256]{1,0:T(8,128)(2,1)S(1)} %collective-permute-done.6.third, bf16[64,256]{1,0:T(8,128)(2,1)S(1)} %collective-permute-done.7.near_one, ...), custom_call_target="tpu_custom_call" | custom-call | flops 1610000000 | tf_op jit(solution)/shard_map/entering/pallas_call | solution.py:470
  43.0 0.9 %collective-permute-start.12 = (bf16[64,256]{1,0:T(8,128)(2,1)S(1)}, bf16[64,256]{1,0:T(8,128)(2,1)S(1)}, u32[]{:S(2)}, u32[]{:S(2)}) collective-permute-start(bf16[64,256]{1,0:T(8,128)(2,1)S(1)} %get-tuple-element.41), channel_id=1, source_target_pairs={{0,3},{1,2},{2,1},{3,0},{4,7},{5,6},{6,5},{7,4},{8,11},{9,10},{10,... | collective-permute-start | bytes 98312 | tf_op jit(solution)/shard_map/ppermute | solution.py:526
  43.9 0.5 %collective-permute-start.13 = (bf16[64,256]{1,0:T(8,128)(2,1)S(1)}, bf16[64,256]{1,0:T(8,128)(2,1)S(1)}, u32[]{:S(2)}, u32[]{:S(2)}) collective-permute-start(bf16[64,256]{1,0:T(8,128)(2,1)S(1)} %get-tuple-element.42), channel_id=1, source_target_pairs={{0,2},{1,3},{2,0},{3,1},{4,6},{5,7},{6,4},{7,5},{8,10},{9,11},{10,... | collective-permute-start | bytes 98312 | tf_op jit(solution)/shard_map/ppermute | solution.py:522
  44.4 0.6 %collective-permute-start.14 = (bf16[64,256]{1,0:T(8,128)(2,1)S(1)}, bf16[64,256]{1,0:T(8,128)(2,1)S(1)}, u32[]{:S(2)}, u32[]{:S(2)}) collective-permute-start(bf16[64,256]{1,0:T(8,128)(2,1)S(1)} %get-tuple-element.43), channel_id=1, source_target_pairs={{0,1},{1,0},{2,3},{3,2},{4,5},{5,4},{6,7},{7,6},{8,9},{9,8},{10,11... | collective-permute-start | bytes 98312 | tf_op jit(solution)/shard_map/ppermute | solution.py:518
  45.0 1.9 %prop.1 = bf16[2,1024,256]{2,1,0:T(8,128)(2,1)S(1)} custom-call(s32[2,8]{1,0:T(2,128)S(1)} %bitcast.19, bf16[2,1024,1024]{2,1,0:T(8,128)(2,1)S(1)} %bitcast.13, bf16[1024,256]{1,0:T(8,128)(2,1)S(1)} %bitcast.17, bf16[64,256]{1,0:T(8,128)(2,1)S(1)} %get-tuple-element.40._tie.own), custom_call_target="tpu_custom_call" | custom-call | flops 1724999936 | tf_op jit(solution)/shard_map/prop/pallas_call | solution.py:247
  46.9 0.9 %collective-permute-done.13.across = bf16[64,256]{1,0:T(8,128)(2,1)S(1)} collective-permute-done((bf16[64,256]{1,0:T(8,128)(2,1)S(1)}, bf16[64,256]{1,0:T(8,128)(2,1)S(1)}, u32[]{:S(2)}, u32[]{:S(2)}) %collective-permute-start.13) | collective-permute-done | bytes 32800 | tf_op jit(solution)/shard_map/ppermute | solution.py:522
  47.8 0.0 collective-permute-done.14.near
  47.8 1.2 %waves.1 = bf16[2,1024,128]{2,1,0:T(8,128)(2,1)} custom-call(bf16[64,256]{1,0:T(8,128)(2,1)S(1)} %get-tuple-element.40._tie.own, bf16[64,256]{1,0:T(8,128)(2,1)S(1)} %collective-permute-done.12.far, bf16[64,256]{1,0:T(8,128)(2,1)S(1)} %collective-permute-done.13.across, bf16[64,256]{1,0:T(8,128)(2,1)S(1)} %collective-permute-done.14.near, ...), custom_call_target="tpu_custom_call" | custom-call | flops 1495000064 | tf_op jit(solution)/shard_map/waves/pallas_call | solution.py:501
  (10 shorter events, 0.0 us)
Async XLA Ops:
  0.0 11.5 %copy-start.3 = (bf16[1,1024,256]{2,1,0:T(8,128)(2,1)S(1)}, bf16[1,1024,256]{2,1,0:T(8,128)(2,1)}, u32[]{:S(2)}) copy-start(bf16[1,1024,256]{2,1,0:T(8,128)(2,1)} %param.8) | copy-start | bytes 1572868
  0.0 11.5 %copy-start.4 = (s32[1,8,2]{1,2,0:T(2,128)S(1)}, s32[1,8,2]{1,2,0:T(2,128)}, u32[]{:S(2)}) copy-start(s32[1,8,2]{1,2,0:T(2,128)} %param.9) | copy-start | bytes 196
  4.0 22.5 %copy-start.2 = (bf16[1,2,1024,128]{3,2,1,0:T(8,128)(2,1)S(1)}, bf16[1,2,1024,128]{3,2,1,0:T(8,128)(2,1)}, u32[]{:S(2)}) copy-start(bf16[1,2,1024,128]{3,2,1,0:T(8,128)(2,1)} %param.7) | copy-start | bytes 1572868
  4.0 22.5 %all-to-all-start = ((bf16[16,136,128]{2,1,0:T(8,128)(2,1)}), bf16[16,136,128]{2,1,0:T(8,128)(2,1)S(1)}, u32[]{:S(2)}, u32[]{:S(2)}) async-start(bf16[16,136,128]{2,1,0:T(8,128)(2,1)} %pairs.1), calls=%async_computation | async-start | bytes 1114112 | tf_op jit(solution)/shard_map/all_to_all | solution.py:572
  11.5 2.2 %copy-start = (bf16[1,2,1024,1024]{3,2,1,0:T(8,128)(2,1)S(1)}, bf16[1,2,1024,1024]{3,2,1,0:T(8,128)(2,1)}, u32[]{:S(2)}) copy-start(bf16[1,2,1024,1024]{3,2,1,0:T(8,128)(2,1)} %param.6) | copy-start | bytes 12582916
  14.8 0.8 %copy-start.5 = (bf16[256,1024]{1,0:T(8,128)(2,1)}, bf16[256,1024]{1,0:T(8,128)(2,1)S(1)}, u32[]{:S(2)}) copy-start(bf16[256,1024]{1,0:T(8,128)(2,1)S(1)} %get-tuple-element.26.refs_1_) | copy-start | bytes 1572868
  15.6 12.5 %collective-permute-start.3 = (f32[256,256]{1,0:T(8,128)S(1)}, f32[256,256]{1,0:T(8,128)S(1)}, u32[]{:S(2)}, u32[]{:S(2)}) collective-permute-start(f32[256,256]{1,0:T(8,128)S(1)} %get-tuple-element.32), channel_id=1, source_target_pairs={{0,2},{1,3},{2,0},{3,1},{4,6},{5,7},{6,4},{7,5},{8,10},{9,11},{10,... | collective-permute-start | bytes 786440 | tf_op jit(solution)/shard_map/ppermute | solution.py:522
  17.5 12.8 %collective-permute-start.5 = (f32[256,256]{1,0:T(8,128)S(1)}, f32[256,256]{1,0:T(8,128)S(1)}, u32[]{:S(2)}, u32[]{:S(2)}) collective-permute-start(f32[256,256]{1,0:T(8,128)S(1)} %get-tuple-element.31.own), channel_id=1, source_target_pairs={{0,1},{1,0},{2,3},{3,2},{4,5},{5,4},{6,7},{7,6},{8,9},{9,8},{10,11... | collective-permute-start | bytes 786440 | tf_op jit(solution)/shard_map/ppermute | solution.py:518
  26.5 1.0 %copy-start.6 = (bf16[256,1024]{1,0:T(8,128)(2,1)S(1)}, bf16[256,1024]{1,0:T(8,128)(2,1)}, u32[]{:S(2)}) copy-start(bf16[256,1024]{1,0:T(8,128)(2,1)} %copy-done.5) | copy-start | bytes 1572868
  27.5 4.4 %copy-start.1 = (bf16[1,2,1024,1024]{3,2,1,0:T(8,128)(2,1)S(1)}, bf16[1,2,1024,1024]{3,2,1,0:T(8,128)(2,1)}, u32[]{:S(2)}) copy-start(bf16[1,2,1024,1024]{3,2,1,0:T(8,128)(2,1)} %param.6) | copy-start | bytes 12582916
  28.1 2.2 %collective-permute-start.4 = (f32[256,256]{1,0:T(8,128)S(1)}, f32[256,256]{1,0:T(8,128)S(1)}, u32[]{:S(2)}, u32[]{:S(2)}) collective-permute-start(f32[256,256]{1,0:T(8,128)S(1)} %after_exchange.1.across), channel_id=1, source_target_pairs={{0,1},{1,0},{2,3},{3,2},{4,5},{5,4},{6,7},{7,6},{8,9},{9,8},{10,11... | collective-permute-start | bytes 786440 | tf_op jit(solution)/shard_map/ppermute | solution.py:518
  28.2 5.6 %collective-permute-start = (bf16[64,256]{1,0:T(8,128)(2,1)S(1)}, bf16[64,256]{1,0:T(8,128)(2,1)S(1)}, u32[]{:S(2)}, u32[]{:S(2)}) collective-permute-start(bf16[64,256]{1,0:T(8,128)(2,1)S(1)} %get-tuple-element.28), channel_id=1, source_target_pairs={{0,3},{1,2},{2,1},{3,0},{4,7},{5,6},{6,5},{7,4},{8,11},{9,10},{10,... | collective-permute-start | bytes 98312 | tf_op jit(solution)/shard_map/ppermute | solution.py:526
  29.1 4.7 %collective-permute-start.1 = (bf16[64,256]{1,0:T(8,128)(2,1)S(1)}, bf16[64,256]{1,0:T(8,128)(2,1)S(1)}, u32[]{:S(2)}, u32[]{:S(2)}) collective-permute-start(bf16[64,256]{1,0:T(8,128)(2,1)S(1)} %get-tuple-element.29), channel_id=1, source_target_pairs={{0,2},{1,3},{2,0},{3,1},{4,6},{5,7},{6,4},{7,5},{8,10},{9,11},{10,... | collective-permute-start | bytes 98312 | tf_op jit(solution)/shard_map/ppermute | solution.py:522
  30.3 3.5 %collective-permute-start.2 = (bf16[64,256]{1,0:T(8,128)(2,1)S(1)}, bf16[64,256]{1,0:T(8,128)(2,1)S(1)}, u32[]{:S(2)}, u32[]{:S(2)}) collective-permute-start(bf16[64,256]{1,0:T(8,128)(2,1)S(1)} %get-tuple-element.30), channel_id=1, source_target_pairs={{0,1},{1,0},{2,3},{3,2},{4,5},{5,4},{6,7},{7,6},{8,9},{9,8},{10,11... | collective-permute-start | bytes 98312 | tf_op jit(solution)/shard_map/ppermute | solution.py:518
  31.2 10.2 %collective-permute-start.10 = (bf16[256,256]{1,0:T(8,128)(2,1)S(1)}, bf16[256,256]{1,0:T(8,128)(2,1)S(1)}, u32[]{:S(2)}, u32[]{:S(2)}) collective-permute-start(bf16[256,256]{1,0:T(8,128)(2,1)S(1)} %get-tuple-element.36), channel_id=1, source_target_pairs={{4,8},{8,12},{5,13},{6,10},{10,14},{7,15},{20,24},{24,28},{21,29},... | collective-permute-start | bytes 393224 | tf_op jit(solution)/shard_map/ppermute | solution.py:544
  34.4 7.8 %collective-permute-start.6 = (bf16[64,256]{1,0:T(8,128)(2,1)S(1)}, bf16[64,256]{1,0:T(8,128)(2,1)S(1)}, u32[]{:S(2)}, u32[]{:S(2)}) collective-permute-start(bf16[64,256]{1,0:T(8,128)(2,1)S(1)} %get-tuple-element.35), channel_id=1, source_target_pairs={{0,12},{1,13},{2,14},{3,15},{16,28},{17,29},{18,30},{19,31}} | collective-permute-start | bytes 98312 | tf_op jit(solution)/shard_map/ppermute | solution.py:550
  38.1 4.1 %collective-permute-start.7 = (bf16[64,256]{1,0:T(8,128)(2,1)S(1)}, bf16[64,256]{1,0:T(8,128)(2,1)S(1)}, u32[]{:S(2)}, u32[]{:S(2)}) collective-permute-start(bf16[64,256]{1,0:T(8,128)(2,1)S(1)} %get-tuple-element.35), channel_id=1, source_target_pairs={{0,4},{1,5},{2,6},{3,7},{16,20},{17,21},{18,22},{19,23}} | collective-permute-start | bytes 98312 | tf_op jit(solution)/shard_map/ppermute | solution.py:550
  39.4 2.9 %collective-permute-start.8 = (bf16[64,256]{1,0:T(8,128)(2,1)S(1)}, bf16[64,256]{1,0:T(8,128)(2,1)S(1)}, u32[]{:S(2)}, u32[]{:S(2)}) collective-permute-start(bf16[64,256]{1,0:T(8,128)(2,1)S(1)} %get-tuple-element.35), channel_id=1, source_target_pairs={{0,8},{1,9},{2,10},{3,11},{4,12},{5,13},{6,14},{7,15},{16,24},{17,... | collective-permute-start | bytes 98312 | tf_op jit(solution)/shard_map/ppermute | solution.py:550
  40.7 1.6 %collective-permute-start.9 = (bf16[64,256]{1,0:T(8,128)(2,1)S(1)}, bf16[64,256]{1,0:T(8,128)(2,1)S(1)}, u32[]{:S(2)}, u32[]{:S(2)}) collective-permute-start(bf16[64,256]{1,0:T(8,128)(2,1)S(1)} %get-tuple-element.35), channel_id=1, source_target_pairs={{4,8},{5,9},{6,10},{7,11},{8,12},{9,13},{10,14},{11,15},{20,24},{2... | collective-permute-start | bytes 98312 | tf_op jit(solution)/shard_map/ppermute | solution.py:550
  41.4 0.9 %collective-permute-start.11 = (bf16[256,256]{1,0:T(8,128)(2,1)S(1)}, bf16[256,256]{1,0:T(8,128)(2,1)S(1)}, u32[]{:S(2)}, u32[]{:S(2)}) collective-permute-start(bf16[256,256]{1,0:T(8,128)(2,1)S(1)} %collective-permute-done.10.got), channel_id=1, source_target_pairs={{8,9},{9,8},{10,11},{11,10},{12,13},{13,12},{14,15},{15,14},{24,25... | collective-permute-start | bytes 393224 | tf_op jit(solution)/shard_map/ppermute | solution.py:545
  43.0 3.8 %collective-permute-start.12 = (bf16[64,256]{1,0:T(8,128)(2,1)S(1)}, bf16[64,256]{1,0:T(8,128)(2,1)S(1)}, u32[]{:S(2)}, u32[]{:S(2)}) collective-permute-start(bf16[64,256]{1,0:T(8,128)(2,1)S(1)} %get-tuple-element.41), channel_id=1, source_target_pairs={{0,3},{1,2},{2,1},{3,0},{4,7},{5,6},{6,5},{7,4},{8,11},{9,10},{10,... | collective-permute-start | bytes 98312 | tf_op jit(solution)/shard_map/ppermute | solution.py:526
  43.9 3.9 %collective-permute-start.13 = (bf16[64,256]{1,0:T(8,128)(2,1)S(1)}, bf16[64,256]{1,0:T(8,128)(2,1)S(1)}, u32[]{:S(2)}, u32[]{:S(2)}) collective-permute-start(bf16[64,256]{1,0:T(8,128)(2,1)S(1)} %get-tuple-element.42), channel_id=1, source_target_pairs={{0,2},{1,3},{2,0},{3,1},{4,6},{5,7},{6,4},{7,5},{8,10},{9,11},{10,... | collective-permute-start | bytes 98312 | tf_op jit(solution)/shard_map/ppermute | solution.py:522
  44.4 3.4 %collective-permute-start.14 = (bf16[64,256]{1,0:T(8,128)(2,1)S(1)}, bf16[64,256]{1,0:T(8,128)(2,1)S(1)}, u32[]{:S(2)}, u32[]{:S(2)}) collective-permute-start(bf16[64,256]{1,0:T(8,128)(2,1)S(1)} %get-tuple-element.43), channel_id=1, source_target_pairs={{0,1},{1,0},{2,3},{3,2},{4,5},{5,4},{6,7},{7,6},{8,9},{9,8},{10,11... | collective-permute-start | bytes 98312 | tf_op jit(solution)/shard_map/ppermute | solution.py:518

commit v34 on v31

--- a/solution.py
+++ b/solution.py
@@ -301,7 +301,7 @@
                 total[e, pl.ds(first, BLK), :] += item.astype(F32)
         return 0
 
-    lax.fori_loop(0, sections, add, 0, unroll=2)
+    lax.fori_loop(0, sections, add, 0, unroll=min(sections, 8))
     source[...] = total[...].astype(BF16)
 
 

time: 49.1 us -> 49.1 us (level)
  no operation moved by 1% of the time
where the time goes in v34:
time: 49.1 us; the launch traced here: 48.6 us
  starting transfers between devices  22 us (45%)
  Pallas kernels  13.7 us (28%)
  waiting for transfers between devices  9.65 us (20%)
  local copies, waits for them, and re-layouts  3.08 us (6%)
    all_to_all x1, waiting for transfers between devices, per_device(): lax.all_to_all(outgoing, 'sec', split_axis=0, concat_axis=0, tiled=True)  9.01 us
    all_to_all x1, starting transfers between devices, per_device(): lax.all_to_all(outgoing, 'sec', split_axis=0, concat_axis=0, tiled=True)  7.5 us
    ppermute x4, starting transfers between devices, between(): return lax.ppermute(item, 'sec', pairs)  7.06 us
    pallas_call x1, Pallas kernels, outgoing_pairs(): pl.pallas_call(pairs_kernel, name='pairs', in_specs=[IN_HBM] * 4, out_sha...  3.96 us
    ppermute x3, starting transfers between devices, to_across(): lax.ppermute(item, 'sec', [(s, s // GROUP * GROUP + (s % GROUP + CORES) %...  3.68 us
    unnamed x14, local copies, waits for them, and re-layouts  3.08 us
    pallas_call x2, Pallas kernels, image_and_maps(): call(functools.partial(work_kernel, not held), 'image_and_maps', [IN_VMEM...  1.91 us
    pallas_call x1, Pallas kernels, propagator(): call(prop_kernel, 'prop', [IN_SMEM, IN_VMEM, IN_VMEM, IN_PLACE], shape(en...  1.9 us
  transfers between devices with their start and end apart: 16, of which 3 were waited for; matrix products, arithmetic and copies ran while one was open for 0% of the time, Pallas kernels for 16%

profile of v34, /device:TPU:0, one launch (start us, length us, event | category | flops | bytes accessed | tf_op | source)
XLA Modules:
  0.0 48.6 jit_solution(8397230016355948055)
XLA Ops:
  0.0 4.0 %pairs.1 = bf16[16,136,128]{2,1,0:T(8,128)(2,1)} custom-call(s32[16]{0:T(128)} %bitcast.21, s32[2,16]{1,0:T(2,128)} %bitcast.20, bf16[2,1024,1024]{2,1,0:T(8,128)(2,1)} %bitcast.9, bf16[2,1024,128]{2,1,0:T(8,128)(2,1)} %bitcast.14), custom_call_target="tpu_custom_call" | custom-call | flops 4600000000 | tf_op jit(solution)/shard_map/pairs/pallas_call | solution.py:183
  4.0 0.0 copy-start.2
  4.0 7.5 %all-to-all-start = ((bf16[16,136,128]{2,1,0:T(8,128)(2,1)}), bf16[16,136,128]{2,1,0:T(8,128)(2,1)S(1)}, u32[]{:S(2)}, u32[]{:S(2)}) async-start(bf16[16,136,128]{2,1,0:T(8,128)(2,1)} %pairs.1), calls=%async_computation | async-start | bytes 1114112 | tf_op jit(solution)/shard_map/all_to_all | solution.py:562
  11.5 0.0 copy-start
  11.5 2.2 %copy-done = bf16[1,2,1024,1024]{3,2,1,0:T(8,128)(2,1)S(1)} copy-done((bf16[1,2,1024,1024]{3,2,1,0:T(8,128)(2,1)S(1)}, bf16[1,2,1024,1024]{3,2,1,0:T(8,128)(2,1)}, u32[]{:S(2)}) %copy-start) | copy-done | bytes 4194328
  13.7 1.1 %face_maps.1 = (f32[256,256]{1,0:T(8,128)S(1)}, f32[256,256]{1,0:T(8,128)S(1)}, bf16[256,1024]{1,0:T(8,128)(2,1)S(1)}, bf16[256,1024]{1,0:T(8,128)(2,1)S(1)}) custom-call(s32[2,8]{1,0:T(2,128)S(1)} %bitcast.18, bf16[2,1024,1024]{2,1,0:T(8,128)(2,1)S(1)} %bitcast.10, bf16[1024,256]{1,0:T(8,128)(2,1)S(1)} %bitcast.16), custom_call_target="tpu_custom_call" | custom-call | flops 1380000000 | tf_op jit(solution)/shard_map/face_maps/pallas_call | solution.py:225
  14.8 0.0 copy-start.5
  14.8 0.8 %copy-done.5 = bf16[256,1024]{1,0:T(8,128)(2,1)} copy-done((bf16[256,1024]{1,0:T(8,128)(2,1)}, bf16[256,1024]{1,0:T(8,128)(2,1)S(1)}, u32[]{:S(2)}) %copy-start.5) | copy-done | bytes 524312
  15.6 1.9 %collective-permute-start.3 = (f32[256,256]{1,0:T(8,128)S(1)}, f32[256,256]{1,0:T(8,128)S(1)}, u32[]{:S(2)}, u32[]{:S(2)}) collective-permute-start(f32[256,256]{1,0:T(8,128)S(1)} %get-tuple-element.32), channel_id=1, source_target_pairs={{0,2},{1,3},{2,0},{3,1},{4,6},{5,7},{6,4},{7,5},{8,10},{9,11},{10,... | collective-permute-start | bytes 786440 | tf_op jit(solution)/shard_map/ppermute | solution.py:512
  17.5 0.0 collective-permute-start.5
  17.5 9.0 %all-to-all-done.received = bf16[16,136,128]{2,1,0:T(8,128)(2,1)S(1)} async-done(((bf16[16,136,128]{2,1,0:T(8,128)(2,1)}), bf16[16,136,128]{2,1,0:T(8,128)(2,1)S(1)}, u32[]{:S(2)}, u32[]{:S(2)}) %all-to-all-start) | async-done | bytes 557088 | tf_op jit(solution)/shard_map/all_to_all | solution.py:562
  26.6 0.9 %source.1.refs_1_ = bf16[2,1024,128]{2,1,0:T(8,128)(2,1)S(1)} custom-call(bf16[16,136,128]{2,1,0:T(8,128)(2,1)S(1)} %all-to-all-done.received, bf16[2,1024,128]{2,1,0:T(8,128)(2,1)S(1)} %bitcast.15), custom_call_target="tpu_custom_call" | custom-call | flops 1150000000 | tf_op jit(solution)/shard_map/source/pallas_call | solution.py:311
  27.5 0.0 copy-start.1
  27.5 0.1 copy-done.6
  27.6 0.5 %face_quarters.1 = (bf16[64,256]{1,0:T(8,128)(2,1)S(1)}, bf16[64,256]{1,0:T(8,128)(2,1)S(1)}, bf16[64,256]{1,0:T(8,128)(2,1)S(1)}, bf16[64,256]{1,0:T(8,128)(2,1)S(1)}) custom-call(bf16[2,1024,128]{2,1,0:T(8,128)(2,1)S(1)} %source.1.refs_1_, bf16[256,1024]{1,0:T(8,128)(2,1)S(1)} %get-tuple-element.25.refs_0_, bf16[256,1024]{1,0:T(8,128)(2,1)S(1)} %copy-done.6), custom_call_target="tpu_custom_call" | custom-call | flops 690000000 | tf_op jit(solution)/shard_map/face_quarters/pallas_call | solution.py:344
  28.1 0.0 collective-permute-done.3._map
  28.1 0.1 collective-permute-start.4
  28.2 0.9 %collective-permute-start = (bf16[64,256]{1,0:T(8,128)(2,1)S(1)}, bf16[64,256]{1,0:T(8,128)(2,1)S(1)}, u32[]{:S(2)}, u32[]{:S(2)}) collective-permute-start(bf16[64,256]{1,0:T(8,128)(2,1)S(1)} %get-tuple-element.28), channel_id=1, source_target_pairs={{0,3},{1,2},{2,1},{3,0},{4,7},{5,6},{6,5},{7,4},{8,11},{9,10},{10,... | collective-permute-start | bytes 98312 | tf_op jit(solution)/shard_map/ppermute | solution.py:516
  29.1 1.3 %collective-permute-start.1 = (bf16[64,256]{1,0:T(8,128)(2,1)S(1)}, bf16[64,256]{1,0:T(8,128)(2,1)S(1)}, u32[]{:S(2)}, u32[]{:S(2)}) collective-permute-start(bf16[64,256]{1,0:T(8,128)(2,1)S(1)} %get-tuple-element.29), channel_id=1, source_target_pairs={{0,2},{1,3},{2,0},{3,1},{4,6},{5,7},{6,4},{7,5},{8,10},{9,11},{10,... | collective-permute-start | bytes 98312 | tf_op jit(solution)/shard_map/ppermute | solution.py:512
  30.4 0.0 collective-permute-start.2
  30.4 0.0 collective-permute-done.5.near
  30.4 0.0 collective-permute-done.4.far
  30.4 0.8 %chain_maps.1 = (bf16[256,256]{1,0:T(8,128)(2,1)S(1)}, bf16[2,4,256,256]{3,2,1,0:T(8,128)(2,1)S(1)}) custom-call(f32[256,256]{1,0:T(8,128)S(1)} %get-tuple-element.31.own, f32[256,256]{1,0:T(8,128)S(1)} %collective-permute-done.4.far, f32[256,256]{1,0:T(8,128)S(1)} %after_exchange.1.across, f32[256,256]{1,0:T(8,128)S(1)} %collective-permute-done.5.near), custom_call_target="tpu_custom_call" | custom-call | flops 1035000000 | tf_op jit(solution)/shard_map/chain_maps/pallas_call | solution.py:270
  31.2 1.8 %image_and_maps.2 = (f32[2,1024,128]{2,1,0:T(8,128)S(1)}, bf16[2,2,256,256]{3,2,1,0:T(8,128)(2,1)S(1)}) custom-call(bf16[2,1024,1024]{2,1,0:T(8,128)(2,1)S(1)} %bitcast.11, bf16[2,1024,128]{2,1,0:T(8,128)(2,1)S(1)} %source.1.refs_1_, bf16[2,4,256,256]{3,2,1,0:T(8,128)(2,1)S(1)} %get-tuple-element.33.refs_2_.parts), custom_call_target="tpu_custom_call" | custom-call | flops 2300000000 | tf_op jit(solution)/shard_map/image_and_maps/pallas_call | solution.py:420
  33.0 0.7 %collective-permute-start.10 = (bf16[256,256]{1,0:T(8,128)(2,1)S(1)}, bf16[256,256]{1,0:T(8,128)(2,1)S(1)}, u32[]{:S(2)}, u32[]{:S(2)}) collective-permute-start(bf16[256,256]{1,0:T(8,128)(2,1)S(1)} %get-tuple-element.36), channel_id=1, source_target_pairs={{4,8},{8,12},{5,13},{6,10},{10,14},{7,15},{20,24},{24,28},{21,29},... | collective-permute-start | bytes 393224 | tf_op jit(solution)/shard_map/ppermute | solution.py:534
  33.7 0.0 collective-permute-done.far
  33.7 0.0 collective-permute-done.1.across
  33.7 0.0 collective-permute-done.2.near
  33.7 0.6 %plane_total.1 = (bf16[64,256]{1,0:T(8,128)(2,1)S(1)}, f32[3,64,256]{2,1,0:T(8,128)S(1)}) custom-call(bf16[64,256]{1,0:T(8,128)(2,1)S(1)} %get-tuple-element.27._packets.own, bf16[64,256]{1,0:T(8,128)(2,1)S(1)} %collective-permute-done.far, bf16[64,256]{1,0:T(8,128)(2,1)S(1)} %collective-permute-done.1.across, ...), custom_call_target="tpu_custom_call" | custom-call | flops 3449999872 | tf_op jit(solution)/shard_map/plane_total/pallas_call | solution.py:386
  34.3 3.8 %collective-permute-start.6 = (bf16[64,256]{1,0:T(8,128)(2,1)S(1)}, bf16[64,256]{1,0:T(8,128)(2,1)S(1)}, u32[]{:S(2)}, u32[]{:S(2)}) collective-permute-start(bf16[64,256]{1,0:T(8,128)(2,1)S(1)} %get-tuple-element.35), channel_id=1, source_target_pairs={{0,12},{1,13},{2,14},{3,15},{16,28},{17,29},{18,30},{19,31}} | collective-permute-start | bytes 98312 | tf_op jit(solution)/shard_map/ppermute | solution.py:540
  38.1 1.3 %collective-permute-start.7 = (bf16[64,256]{1,0:T(8,128)(2,1)S(1)}, bf16[64,256]{1,0:T(8,128)(2,1)S(1)}, u32[]{:S(2)}, u32[]{:S(2)}) collective-permute-start(bf16[64,256]{1,0:T(8,128)(2,1)S(1)} %get-tuple-element.35), channel_id=1, source_target_pairs={{0,4},{1,5},{2,6},{3,7},{16,20},{17,21},{18,22},{19,23}} | collective-permute-start | bytes 98312 | tf_op jit(solution)/shard_map/ppermute | solution.py:540
  39.4 1.3 %collective-permute-start.8 = (bf16[64,256]{1,0:T(8,128)(2,1)S(1)}, bf16[64,256]{1,0:T(8,128)(2,1)S(1)}, u32[]{:S(2)}, u32[]{:S(2)}) collective-permute-start(bf16[64,256]{1,0:T(8,128)(2,1)S(1)} %get-tuple-element.35), channel_id=1, source_target_pairs={{0,8},{1,9},{2,10},{3,11},{4,12},{5,13},{6,14},{7,15},{16,24},{17,... | collective-permute-start | bytes 98312 | tf_op jit(solution)/shard_map/ppermute | solution.py:540
  40.7 0.7 %collective-permute-start.9 = (bf16[64,256]{1,0:T(8,128)(2,1)S(1)}, bf16[64,256]{1,0:T(8,128)(2,1)S(1)}, u32[]{:S(2)}, u32[]{:S(2)}) collective-permute-start(bf16[64,256]{1,0:T(8,128)(2,1)S(1)} %get-tuple-element.35), channel_id=1, source_target_pairs={{4,8},{5,9},{6,10},{7,11},{8,12},{9,13},{10,14},{11,15},{20,24},{2... | collective-permute-start | bytes 98312 | tf_op jit(solution)/shard_map/ppermute | solution.py:540
  41.4 0.0 collective-permute-done.10.got
  41.4 0.7 %collective-permute-start.11 = (bf16[256,256]{1,0:T(8,128)(2,1)S(1)}, bf16[256,256]{1,0:T(8,128)(2,1)S(1)}, u32[]{:S(2)}, u32[]{:S(2)}) collective-permute-start(bf16[256,256]{1,0:T(8,128)(2,1)S(1)} %collective-permute-done.10.got), channel_id=1, source_target_pairs={{8,9},{9,8},{10,11},{11,10},{12,13},{13,12},{14,15},{15,14},{24,25... | collective-permute-start | bytes 393224 | tf_op jit(solution)/shard_map/ppermute | solution.py:535
  42.1 0.1 image_and_maps.3
  42.2 0.0 collective-permute-done.6.third
  42.2 0.0 collective-permute-done.7.near_one
  42.2 0.1 collective-permute-done.8.second
  42.3 0.7 %entering.1 = (bf16[64,256]{1,0:T(8,128)(2,1)S(1)}, bf16[64,256]{1,0:T(8,128)(2,1)S(1)}, bf16[64,256]{1,0:T(8,128)(2,1)S(1)}, bf16[64,256]{1,0:T(8,128)(2,1)S(1)}) custom-call(bf16[64,256]{1,0:T(8,128)(2,1)S(1)} %collective-permute-done.6.third, bf16[64,256]{1,0:T(8,128)(2,1)S(1)} %collective-permute-done.7.near_one, ...), custom_call_target="tpu_custom_call" | custom-call | flops 1610000000 | tf_op jit(solution)/shard_map/entering/pallas_call | solution.py:460
  43.1 0.5 collective-permute-start.12
  43.5 0.5 %collective-permute-start.13 = (bf16[64,256]{1,0:T(8,128)(2,1)S(1)}, bf16[64,256]{1,0:T(8,128)(2,1)S(1)}, u32[]{:S(2)}, u32[]{:S(2)}) collective-permute-start(bf16[64,256]{1,0:T(8,128)(2,1)S(1)} %get-tuple-element.42), channel_id=1, source_target_pairs={{0,2},{1,3},{2,0},{3,1},{4,6},{5,7},{6,4},{7,5},{8,10},{9,11},{10,... | collective-permute-start | bytes 98312 | tf_op jit(solution)/shard_map/ppermute | solution.py:512
  44.0 1.0 %collective-permute-start.14 = (bf16[64,256]{1,0:T(8,128)(2,1)S(1)}, bf16[64,256]{1,0:T(8,128)(2,1)S(1)}, u32[]{:S(2)}, u32[]{:S(2)}) collective-permute-start(bf16[64,256]{1,0:T(8,128)(2,1)S(1)} %get-tuple-element.43), channel_id=1, source_target_pairs={{0,1},{1,0},{2,3},{3,2},{4,5},{5,4},{6,7},{7,6},{8,9},{9,8},{10,11... | collective-permute-start | bytes 98312 | tf_op jit(solution)/shard_map/ppermute | solution.py:508
  45.0 1.9 %prop.1 = bf16[2,1024,256]{2,1,0:T(8,128)(2,1)S(1)} custom-call(s32[2,8]{1,0:T(2,128)S(1)} %bitcast.19, bf16[2,1024,1024]{2,1,0:T(8,128)(2,1)S(1)} %bitcast.13, bf16[1024,256]{1,0:T(8,128)(2,1)S(1)} %bitcast.17, bf16[64,256]{1,0:T(8,128)(2,1)S(1)} %get-tuple-element.40._tie.own), custom_call_target="tpu_custom_call" | custom-call | flops 1724999936 | tf_op jit(solution)/shard_map/prop/pallas_call | solution.py:244
  46.9 0.0 collective-permute-done.12.far
  46.9 0.5 %collective-permute-done.13.across = bf16[64,256]{1,0:T(8,128)(2,1)S(1)} collective-permute-done((bf16[64,256]{1,0:T(8,128)(2,1)S(1)}, bf16[64,256]{1,0:T(8,128)(2,1)S(1)}, u32[]{:S(2)}, u32[]{:S(2)}) %collective-permute-start.13) | collective-permute-done | bytes 32800 | tf_op jit(solution)/shard_map/ppermute | solution.py:512
  47.4 0.0 collective-permute-done.14.near
  47.4 1.2 %waves.1 = bf16[2,1024,128]{2,1,0:T(8,128)(2,1)} custom-call(bf16[64,256]{1,0:T(8,128)(2,1)S(1)} %get-tuple-element.40._tie.own, bf16[64,256]{1,0:T(8,128)(2,1)S(1)} %collective-permute-done.12.far, bf16[64,256]{1,0:T(8,128)(2,1)S(1)} %collective-permute-done.13.across, bf16[64,256]{1,0:T(8,128)(2,1)S(1)} %collective-permute-done.14.near, ...), custom_call_target="tpu_custom_call" | custom-call | flops 1495000064 | tf_op jit(solution)/shard_map/waves/pallas_call | solution.py:491
  (10 shorter events, 0.0 us)
Async XLA Ops:
  0.0 11.5 %copy-start.3 = (bf16[1,1024,256]{2,1,0:T(8,128)(2,1)S(1)}, bf16[1,1024,256]{2,1,0:T(8,128)(2,1)}, u32[]{:S(2)}) copy-start(bf16[1,1024,256]{2,1,0:T(8,128)(2,1)} %param.8) | copy-start | bytes 1572868
  0.0 11.5 %copy-start.4 = (s32[1,8,2]{1,2,0:T(2,128)S(1)}, s32[1,8,2]{1,2,0:T(2,128)}, u32[]{:S(2)}) copy-start(s32[1,8,2]{1,2,0:T(2,128)} %param.9) | copy-start | bytes 196
  4.0 22.6 %copy-start.2 = (bf16[1,2,1024,128]{3,2,1,0:T(8,128)(2,1)S(1)}, bf16[1,2,1024,128]{3,2,1,0:T(8,128)(2,1)}, u32[]{:S(2)}) copy-start(bf16[1,2,1024,128]{3,2,1,0:T(8,128)(2,1)} %param.7) | copy-start | bytes 1572868
  4.0 22.6 %all-to-all-start = ((bf16[16,136,128]{2,1,0:T(8,128)(2,1)}), bf16[16,136,128]{2,1,0:T(8,128)(2,1)S(1)}, u32[]{:S(2)}, u32[]{:S(2)}) async-start(bf16[16,136,128]{2,1,0:T(8,128)(2,1)} %pairs.1), calls=%async_computation | async-start | bytes 1114112 | tf_op jit(solution)/shard_map/all_to_all | solution.py:562
  11.5 2.2 %copy-start = (bf16[1,2,1024,1024]{3,2,1,0:T(8,128)(2,1)S(1)}, bf16[1,2,1024,1024]{3,2,1,0:T(8,128)(2,1)}, u32[]{:S(2)}) copy-start(bf16[1,2,1024,1024]{3,2,1,0:T(8,128)(2,1)} %param.6) | copy-start | bytes 12582916
  14.8 0.8 %copy-start.5 = (bf16[256,1024]{1,0:T(8,128)(2,1)}, bf16[256,1024]{1,0:T(8,128)(2,1)S(1)}, u32[]{:S(2)}) copy-start(bf16[256,1024]{1,0:T(8,128)(2,1)S(1)} %get-tuple-element.26.refs_1_) | copy-start | bytes 1572868
  15.6 12.5 %collective-permute-start.3 = (f32[256,256]{1,0:T(8,128)S(1)}, f32[256,256]{1,0:T(8,128)S(1)}, u32[]{:S(2)}, u32[]{:S(2)}) collective-permute-start(f32[256,256]{1,0:T(8,128)S(1)} %get-tuple-element.32), channel_id=1, source_target_pairs={{0,2},{1,3},{2,0},{3,1},{4,6},{5,7},{6,4},{7,5},{8,10},{9,11},{10,... | collective-permute-start | bytes 786440 | tf_op jit(solution)/shard_map/ppermute | solution.py:512
  17.5 12.8 %collective-permute-start.5 = (f32[256,256]{1,0:T(8,128)S(1)}, f32[256,256]{1,0:T(8,128)S(1)}, u32[]{:S(2)}, u32[]{:S(2)}) collective-permute-start(f32[256,256]{1,0:T(8,128)S(1)} %get-tuple-element.31.own), channel_id=1, source_target_pairs={{0,1},{1,0},{2,3},{3,2},{4,5},{5,4},{6,7},{7,6},{8,9},{9,8},{10,11... | collective-permute-start | bytes 786440 | tf_op jit(solution)/shard_map/ppermute | solution.py:508
  26.6 1.0 %copy-start.6 = (bf16[256,1024]{1,0:T(8,128)(2,1)S(1)}, bf16[256,1024]{1,0:T(8,128)(2,1)}, u32[]{:S(2)}) copy-start(bf16[256,1024]{1,0:T(8,128)(2,1)} %copy-done.5) | copy-start | bytes 1572868
  27.5 3.7 %copy-start.1 = (bf16[1,2,1024,1024]{3,2,1,0:T(8,128)(2,1)S(1)}, bf16[1,2,1024,1024]{3,2,1,0:T(8,128)(2,1)}, u32[]{:S(2)}) copy-start(bf16[1,2,1024,1024]{3,2,1,0:T(8,128)(2,1)} %param.6) | copy-start | bytes 12582916
  28.1 2.2 %collective-permute-start.4 = (f32[256,256]{1,0:T(8,128)S(1)}, f32[256,256]{1,0:T(8,128)S(1)}, u32[]{:S(2)}, u32[]{:S(2)}) collective-permute-start(f32[256,256]{1,0:T(8,128)S(1)} %after_exchange.1.across), channel_id=1, source_target_pairs={{0,1},{1,0},{2,3},{3,2},{4,5},{5,4},{6,7},{7,6},{8,9},{9,8},{10,11... | collective-permute-start | bytes 786440 | tf_op jit(solution)/shard_map/ppermute | solution.py:508
  28.2 5.5 %collective-permute-start = (bf16[64,256]{1,0:T(8,128)(2,1)S(1)}, bf16[64,256]{1,0:T(8,128)(2,1)S(1)}, u32[]{:S(2)}, u32[]{:S(2)}) collective-permute-start(bf16[64,256]{1,0:T(8,128)(2,1)S(1)} %get-tuple-element.28), channel_id=1, source_target_pairs={{0,3},{1,2},{2,1},{3,0},{4,7},{5,6},{6,5},{7,4},{8,11},{9,10},{10,... | collective-permute-start | bytes 98312 | tf_op jit(solution)/shard_map/ppermute | solution.py:516
  29.1 4.6 %collective-permute-start.1 = (bf16[64,256]{1,0:T(8,128)(2,1)S(1)}, bf16[64,256]{1,0:T(8,128)(2,1)S(1)}, u32[]{:S(2)}, u32[]{:S(2)}) collective-permute-start(bf16[64,256]{1,0:T(8,128)(2,1)S(1)} %get-tuple-element.29), channel_id=1, source_target_pairs={{0,2},{1,3},{2,0},{3,1},{4,6},{5,7},{6,4},{7,5},{8,10},{9,11},{10,... | collective-permute-start | bytes 98312 | tf_op jit(solution)/shard_map/ppermute | solution.py:512
  30.4 3.4 %collective-permute-start.2 = (bf16[64,256]{1,0:T(8,128)(2,1)S(1)}, bf16[64,256]{1,0:T(8,128)(2,1)S(1)}, u32[]{:S(2)}, u32[]{:S(2)}) collective-permute-start(bf16[64,256]{1,0:T(8,128)(2,1)S(1)} %get-tuple-element.30), channel_id=1, source_target_pairs={{0,1},{1,0},{2,3},{3,2},{4,5},{5,4},{6,7},{7,6},{8,9},{9,8},{10,11... | collective-permute-start | bytes 98312 | tf_op jit(solution)/shard_map/ppermute | solution.py:508
  33.0 8.4 %collective-permute-start.10 = (bf16[256,256]{1,0:T(8,128)(2,1)S(1)}, bf16[256,256]{1,0:T(8,128)(2,1)S(1)}, u32[]{:S(2)}, u32[]{:S(2)}) collective-permute-start(bf16[256,256]{1,0:T(8,128)(2,1)S(1)} %get-tuple-element.36), channel_id=1, source_target_pairs={{4,8},{8,12},{5,13},{6,10},{10,14},{7,15},{20,24},{24,28},{21,29},... | collective-permute-start | bytes 393224 | tf_op jit(solution)/shard_map/ppermute | solution.py:534
  34.3 7.9 %collective-permute-start.6 = (bf16[64,256]{1,0:T(8,128)(2,1)S(1)}, bf16[64,256]{1,0:T(8,128)(2,1)S(1)}, u32[]{:S(2)}, u32[]{:S(2)}) collective-permute-start(bf16[64,256]{1,0:T(8,128)(2,1)S(1)} %get-tuple-element.35), channel_id=1, source_target_pairs={{0,12},{1,13},{2,14},{3,15},{16,28},{17,29},{18,30},{19,31}} | collective-permute-start | bytes 98312 | tf_op jit(solution)/shard_map/ppermute | solution.py:540
  38.1 4.1 %collective-permute-start.7 = (bf16[64,256]{1,0:T(8,128)(2,1)S(1)}, bf16[64,256]{1,0:T(8,128)(2,1)S(1)}, u32[]{:S(2)}, u32[]{:S(2)}) collective-permute-start(bf16[64,256]{1,0:T(8,128)(2,1)S(1)} %get-tuple-element.35), channel_id=1, source_target_pairs={{0,4},{1,5},{2,6},{3,7},{16,20},{17,21},{18,22},{19,23}} | collective-permute-start | bytes 98312 | tf_op jit(solution)/shard_map/ppermute | solution.py:540
  39.4 2.9 %collective-permute-start.8 = (bf16[64,256]{1,0:T(8,128)(2,1)S(1)}, bf16[64,256]{1,0:T(8,128)(2,1)S(1)}, u32[]{:S(2)}, u32[]{:S(2)}) collective-permute-start(bf16[64,256]{1,0:T(8,128)(2,1)S(1)} %get-tuple-element.35), channel_id=1, source_target_pairs={{0,8},{1,9},{2,10},{3,11},{4,12},{5,13},{6,14},{7,15},{16,24},{17,... | collective-permute-start | bytes 98312 | tf_op jit(solution)/shard_map/ppermute | solution.py:540
  40.7 1.6 %collective-permute-start.9 = (bf16[64,256]{1,0:T(8,128)(2,1)S(1)}, bf16[64,256]{1,0:T(8,128)(2,1)S(1)}, u32[]{:S(2)}, u32[]{:S(2)}) collective-permute-start(bf16[64,256]{1,0:T(8,128)(2,1)S(1)} %get-tuple-element.35), channel_id=1, source_target_pairs={{4,8},{5,9},{6,10},{7,11},{8,12},{9,13},{10,14},{11,15},{20,24},{2... | collective-permute-start | bytes 98312 | tf_op jit(solution)/shard_map/ppermute | solution.py:540
  41.4 0.9 %collective-permute-start.11 = (bf16[256,256]{1,0:T(8,128)(2,1)S(1)}, bf16[256,256]{1,0:T(8,128)(2,1)S(1)}, u32[]{:S(2)}, u32[]{:S(2)}) collective-permute-start(bf16[256,256]{1,0:T(8,128)(2,1)S(1)} %collective-permute-done.10.got), channel_id=1, source_target_pairs={{8,9},{9,8},{10,11},{11,10},{12,13},{13,12},{14,15},{15,14},{24,25... | collective-permute-start | bytes 393224 | tf_op jit(solution)/shard_map/ppermute | solution.py:535
  43.1 3.8 %collective-permute-start.12 = (bf16[64,256]{1,0:T(8,128)(2,1)S(1)}, bf16[64,256]{1,0:T(8,128)(2,1)S(1)}, u32[]{:S(2)}, u32[]{:S(2)}) collective-permute-start(bf16[64,256]{1,0:T(8,128)(2,1)S(1)} %get-tuple-element.41), channel_id=1, source_target_pairs={{0,3},{1,2},{2,1},{3,0},{4,7},{5,6},{6,5},{7,4},{8,11},{9,10},{10,... | collective-permute-start | bytes 98312 | tf_op jit(solution)/shard_map/ppermute | solution.py:516
  43.5 3.9 %collective-permute-start.13 = (bf16[64,256]{1,0:T(8,128)(2,1)S(1)}, bf16[64,256]{1,0:T(8,128)(2,1)S(1)}, u32[]{:S(2)}, u32[]{:S(2)}) collective-permute-start(bf16[64,256]{1,0:T(8,128)(2,1)S(1)} %get-tuple-element.42), channel_id=1, source_target_pairs={{0,2},{1,3},{2,0},{3,1},{4,6},{5,7},{6,4},{7,5},{8,10},{9,11},{10,... | collective-permute-start | bytes 98312 | tf_op jit(solution)/shard_map/ppermute | solution.py:512
  44.0 3.4 %collective-permute-start.14 = (bf16[64,256]{1,0:T(8,128)(2,1)S(1)}, bf16[64,256]{1,0:T(8,128)(2,1)S(1)}, u32[]{:S(2)}, u32[]{:S(2)}) collective-permute-start(bf16[64,256]{1,0:T(8,128)(2,1)S(1)} %get-tuple-element.43), channel_id=1, source_target_pairs={{0,1},{1,0},{2,3},{3,2},{4,5},{5,4},{6,7},{7,6},{8,9},{9,8},{10,11... | collective-permute-start | bytes 98312 | tf_op jit(solution)/shard_map/ppermute | solution.py:508

commit v35 on v34

--- a/solution.py
+++ b/solution.py
@@ -372,7 +372,7 @@
         held[at] = ref[...]
 
 
-def total_kernel(own, far, across, near, parts, _image, out, local, shifts):
+def total_kernel(own, across, far, near, parts, _image, out, local, shifts):
     collect((own, far, across, near), shifts)
     state = shifts[0].astype(F32)
     for j in range(1, GROUP):
@@ -390,7 +390,7 @@
         [shape(rows, face), shape(GROUP - 1, rows, face, dtype=F32)],
         [pltpu.VMEM((GROUP, rows, face), BF16)],
         3.0,
-    )(*shifts, parts, tie)
+    )(shifts[0], shifts[2], shifts[1], shifts[3], parts, tie)
 
 
 def work_kernel(early, *refs):

time: 49.1 us -> 49.3 us (level)
    ppermute x3, starting transfers between devices: 3.68 us -> 4.31 us  [to_across(): lax.ppermute(item, 'sec', [(s, s // GROUP * GROUP + (s % GROUP + CORES) %...]
where the time goes in v35:
time: 49.3 us; the launch traced here: 48.8 us
  starting transfers between devices  22 us (45%)
  Pallas kernels  13.7 us (28%)
  waiting for transfers between devices  9.71 us (20%)
  local copies, waits for them, and re-layouts  3.09 us (6%)
    all_to_all x1, waiting for transfers between devices, per_device(): lax.all_to_all(outgoing, 'sec', split_axis=0, concat_axis=0, tiled=True)  9.01 us
    all_to_all x1, starting transfers between devices, per_device(): lax.all_to_all(outgoing, 'sec', split_axis=0, concat_axis=0, tiled=True)  7.51 us
    ppermute x4, starting transfers between devices, between(): return lax.ppermute(item, 'sec', pairs)  7.05 us
    ppermute x3, starting transfers between devices, to_across(): lax.ppermute(item, 'sec', [(s, s // GROUP * GROUP + (s % GROUP + CORES) %...  4.31 us
    pallas_call x1, Pallas kernels, outgoing_pairs(): pl.pallas_call(pairs_kernel, name='pairs', in_specs=[IN_HBM] * 4, out_sha...  3.96 us
    unnamed x14, local copies, waits for them, and re-layouts  3.09 us
    pallas_call x2, Pallas kernels, image_and_maps(): call(functools.partial(work_kernel, not held), 'image_and_maps', [IN_VMEM...  1.91 us
    pallas_call x1, Pallas kernels, propagator(): call(prop_kernel, 'prop', [IN_SMEM, IN_VMEM, IN_VMEM, IN_PLACE], shape(en...  1.9 us
  transfers between devices with their start and end apart: 16, of which 3 were waited for; matrix products, arithmetic and copies ran while one was open for 0% of the time, Pallas kernels for 16%

profile of v35, /device:TPU:0, one launch (start us, length us, event | category | flops | bytes accessed | tf_op | source)
XLA Modules:
  0.0 48.8 jit_solution(16362177592972126061)
XLA Ops:
  0.0 4.0 %pairs.1 = bf16[16,136,128]{2,1,0:T(8,128)(2,1)} custom-call(s32[16]{0:T(128)} %bitcast.21, s32[2,16]{1,0:T(2,128)} %bitcast.20, bf16[2,1024,1024]{2,1,0:T(8,128)(2,1)} %bitcast.9, bf16[2,1024,128]{2,1,0:T(8,128)(2,1)} %bitcast.14), custom_call_target="tpu_custom_call" | custom-call | flops 4600000000 | tf_op jit(solution)/shard_map/pairs/pallas_call | solution.py:183
  4.0 0.0 copy-start.2
  4.0 7.5 %all-to-all-start = ((bf16[16,136,128]{2,1,0:T(8,128)(2,1)}), bf16[16,136,128]{2,1,0:T(8,128)(2,1)S(1)}, u32[]{:S(2)}, u32[]{:S(2)}) async-start(bf16[16,136,128]{2,1,0:T(8,128)(2,1)} %pairs.1), calls=%async_computation | async-start | bytes 1114112 | tf_op jit(solution)/shard_map/all_to_all | solution.py:562
  11.5 0.0 copy-start
  11.5 2.2 %copy-done = bf16[1,2,1024,1024]{3,2,1,0:T(8,128)(2,1)S(1)} copy-done((bf16[1,2,1024,1024]{3,2,1,0:T(8,128)(2,1)S(1)}, bf16[1,2,1024,1024]{3,2,1,0:T(8,128)(2,1)}, u32[]{:S(2)}) %copy-start) | copy-done | bytes 4194328
  13.7 1.1 %face_maps.1 = (f32[256,256]{1,0:T(8,128)S(1)}, f32[256,256]{1,0:T(8,128)S(1)}, bf16[256,1024]{1,0:T(8,128)(2,1)S(1)}, bf16[256,1024]{1,0:T(8,128)(2,1)S(1)}) custom-call(s32[2,8]{1,0:T(2,128)S(1)} %bitcast.18, bf16[2,1024,1024]{2,1,0:T(8,128)(2,1)S(1)} %bitcast.10, bf16[1024,256]{1,0:T(8,128)(2,1)S(1)} %bitcast.16), custom_call_target="tpu_custom_call" | custom-call | flops 1380000000 | tf_op jit(solution)/shard_map/face_maps/pallas_call | solution.py:225
  14.8 0.0 copy-start.5
  14.8 0.8 %copy-done.5 = bf16[256,1024]{1,0:T(8,128)(2,1)} copy-done((bf16[256,1024]{1,0:T(8,128)(2,1)}, bf16[256,1024]{1,0:T(8,128)(2,1)S(1)}, u32[]{:S(2)}) %copy-start.5) | copy-done | bytes 524312
  15.6 1.9 %collective-permute-start.3 = (f32[256,256]{1,0:T(8,128)S(1)}, f32[256,256]{1,0:T(8,128)S(1)}, u32[]{:S(2)}, u32[]{:S(2)}) collective-permute-start(f32[256,256]{1,0:T(8,128)S(1)} %get-tuple-element.32), channel_id=1, source_target_pairs={{0,2},{1,3},{2,0},{3,1},{4,6},{5,7},{6,4},{7,5},{8,10},{9,11},{10,... | collective-permute-start | bytes 786440 | tf_op jit(solution)/shard_map/ppermute | solution.py:512
  17.5 0.0 collective-permute-start.5
  17.6 9.0 %all-to-all-done.received = bf16[16,136,128]{2,1,0:T(8,128)(2,1)S(1)} async-done(((bf16[16,136,128]{2,1,0:T(8,128)(2,1)}), bf16[16,136,128]{2,1,0:T(8,128)(2,1)S(1)}, u32[]{:S(2)}, u32[]{:S(2)}) %all-to-all-start) | async-done | bytes 557088 | tf_op jit(solution)/shard_map/all_to_all | solution.py:562
  26.6 0.9 %source.1.refs_1_ = bf16[2,1024,128]{2,1,0:T(8,128)(2,1)S(1)} custom-call(bf16[16,136,128]{2,1,0:T(8,128)(2,1)S(1)} %all-to-all-done.received, bf16[2,1024,128]{2,1,0:T(8,128)(2,1)S(1)} %bitcast.15), custom_call_target="tpu_custom_call" | custom-call | flops 1150000000 | tf_op jit(solution)/shard_map/source/pallas_call | solution.py:311
  27.5 0.0 copy-start.1
  27.5 0.1 copy-done.6
  27.6 0.5 %face_quarters.1 = (bf16[64,256]{1,0:T(8,128)(2,1)S(1)}, bf16[64,256]{1,0:T(8,128)(2,1)S(1)}, bf16[64,256]{1,0:T(8,128)(2,1)S(1)}, bf16[64,256]{1,0:T(8,128)(2,1)S(1)}) custom-call(bf16[2,1024,128]{2,1,0:T(8,128)(2,1)S(1)} %source.1.refs_1_, bf16[256,1024]{1,0:T(8,128)(2,1)S(1)} %get-tuple-element.25.refs_0_, bf16[256,1024]{1,0:T(8,128)(2,1)S(1)} %copy-done.6), custom_call_target="tpu_custom_call" | custom-call | flops 690000000 | tf_op jit(solution)/shard_map/face_quarters/pallas_call | solution.py:344
  28.1 0.0 collective-permute-done.3._map
  28.1 0.1 collective-permute-start.4
  28.2 1.2 %collective-permute-start = (bf16[64,256]{1,0:T(8,128)(2,1)S(1)}, bf16[64,256]{1,0:T(8,128)(2,1)S(1)}, u32[]{:S(2)}, u32[]{:S(2)}) collective-permute-start(bf16[64,256]{1,0:T(8,128)(2,1)S(1)} %get-tuple-element.28), channel_id=1, source_target_pairs={{0,2},{1,3},{2,0},{3,1},{4,6},{5,7},{6,4},{7,5},{8,10},{9,11},{10,... | collective-permute-start | bytes 98312 | tf_op jit(solution)/shard_map/ppermute | solution.py:512
  29.4 0.7 %collective-permute-start.1 = (bf16[64,256]{1,0:T(8,128)(2,1)S(1)}, bf16[64,256]{1,0:T(8,128)(2,1)S(1)}, u32[]{:S(2)}, u32[]{:S(2)}) collective-permute-start(bf16[64,256]{1,0:T(8,128)(2,1)S(1)} %get-tuple-element.29), channel_id=1, source_target_pairs={{0,3},{1,2},{2,1},{3,0},{4,7},{5,6},{6,5},{7,4},{8,11},{9,10},{10,... | collective-permute-start | bytes 98312 | tf_op jit(solution)/shard_map/ppermute | solution.py:516
  30.1 0.3 collective-permute-start.2
  30.4 0.0 collective-permute-done.5.near
  30.4 0.0 collective-permute-done.4.far
  30.4 0.8 %chain_maps.1 = (bf16[256,256]{1,0:T(8,128)(2,1)S(1)}, bf16[2,4,256,256]{3,2,1,0:T(8,128)(2,1)S(1)}) custom-call(f32[256,256]{1,0:T(8,128)S(1)} %get-tuple-element.31.own, f32[256,256]{1,0:T(8,128)S(1)} %collective-permute-done.4.far, f32[256,256]{1,0:T(8,128)S(1)} %after_exchange.1.across, f32[256,256]{1,0:T(8,128)S(1)} %collective-permute-done.5.near), custom_call_target="tpu_custom_call" | custom-call | flops 1035000000 | tf_op jit(solution)/shard_map/chain_maps/pallas_call | solution.py:270
  31.3 1.8 %image_and_maps.2 = (f32[2,1024,128]{2,1,0:T(8,128)S(1)}, bf16[2,2,256,256]{3,2,1,0:T(8,128)(2,1)S(1)}) custom-call(bf16[2,1024,1024]{2,1,0:T(8,128)(2,1)S(1)} %bitcast.11, bf16[2,1024,128]{2,1,0:T(8,128)(2,1)S(1)} %source.1.refs_1_, bf16[2,4,256,256]{3,2,1,0:T(8,128)(2,1)S(1)} %get-tuple-element.33.refs_2_.parts), custom_call_target="tpu_custom_call" | custom-call | flops 2300000000 | tf_op jit(solution)/shard_map/image_and_maps/pallas_call | solution.py:420
  33.1 0.7 %collective-permute-start.10 = (bf16[256,256]{1,0:T(8,128)(2,1)S(1)}, bf16[256,256]{1,0:T(8,128)(2,1)S(1)}, u32[]{:S(2)}, u32[]{:S(2)}) collective-permute-start(bf16[256,256]{1,0:T(8,128)(2,1)S(1)} %get-tuple-element.36), channel_id=1, source_target_pairs={{4,8},{8,12},{5,13},{6,10},{10,14},{7,15},{20,24},{24,28},{21,29},... | collective-permute-start | bytes 393224 | tf_op jit(solution)/shard_map/ppermute | solution.py:534
  33.8 0.0 collective-permute-done.across
  33.8 0.0 collective-permute-done.1.far
  33.8 0.0 collective-permute-done.2.near
  33.8 0.6 %plane_total.1 = (bf16[64,256]{1,0:T(8,128)(2,1)S(1)}, f32[3,64,256]{2,1,0:T(8,128)S(1)}) custom-call(bf16[64,256]{1,0:T(8,128)(2,1)S(1)} %get-tuple-element.27._packets.own, bf16[64,256]{1,0:T(8,128)(2,1)S(1)} %collective-permute-done.across, bf16[64,256]{1,0:T(8,128)(2,1)S(1)} %collective-permute-done.1.far, ...), custom_call_target="tpu_custom_call" | custom-call | flops 3449999872 | tf_op jit(solution)/shard_map/plane_total/pallas_call | solution.py:386
  34.4 3.8 %collective-permute-start.6 = (bf16[64,256]{1,0:T(8,128)(2,1)S(1)}, bf16[64,256]{1,0:T(8,128)(2,1)S(1)}, u32[]{:S(2)}, u32[]{:S(2)}) collective-permute-start(bf16[64,256]{1,0:T(8,128)(2,1)S(1)} %get-tuple-element.35), channel_id=1, source_target_pairs={{0,12},{1,13},{2,14},{3,15},{16,28},{17,29},{18,30},{19,31}} | collective-permute-start | bytes 98312 | tf_op jit(solution)/shard_map/ppermute | solution.py:540
  38.2 1.3 %collective-permute-start.7 = (bf16[64,256]{1,0:T(8,128)(2,1)S(1)}, bf16[64,256]{1,0:T(8,128)(2,1)S(1)}, u32[]{:S(2)}, u32[]{:S(2)}) collective-permute-start(bf16[64,256]{1,0:T(8,128)(2,1)S(1)} %get-tuple-element.35), channel_id=1, source_target_pairs={{0,4},{1,5},{2,6},{3,7},{16,20},{17,21},{18,22},{19,23}} | collective-permute-start | bytes 98312 | tf_op jit(solution)/shard_map/ppermute | solution.py:540
  39.5 1.3 %collective-permute-start.8 = (bf16[64,256]{1,0:T(8,128)(2,1)S(1)}, bf16[64,256]{1,0:T(8,128)(2,1)S(1)}, u32[]{:S(2)}, u32[]{:S(2)}) collective-permute-start(bf16[64,256]{1,0:T(8,128)(2,1)S(1)} %get-tuple-element.35), channel_id=1, source_target_pairs={{0,8},{1,9},{2,10},{3,11},{4,12},{5,13},{6,14},{7,15},{16,24},{17,... | collective-permute-start | bytes 98312 | tf_op jit(solution)/shard_map/ppermute | solution.py:540
  40.8 0.7 %collective-permute-start.9 = (bf16[64,256]{1,0:T(8,128)(2,1)S(1)}, bf16[64,256]{1,0:T(8,128)(2,1)S(1)}, u32[]{:S(2)}, u32[]{:S(2)}) collective-permute-start(bf16[64,256]{1,0:T(8,128)(2,1)S(1)} %get-tuple-element.35), channel_id=1, source_target_pairs={{4,8},{5,9},{6,10},{7,11},{8,12},{9,13},{10,14},{11,15},{20,24},{2... | collective-permute-start | bytes 98312 | tf_op jit(solution)/shard_map/ppermute | solution.py:540
  41.5 0.0 collective-permute-done.10.got
  41.5 0.7 %collective-permute-start.11 = (bf16[256,256]{1,0:T(8,128)(2,1)S(1)}, bf16[256,256]{1,0:T(8,128)(2,1)S(1)}, u32[]{:S(2)}, u32[]{:S(2)}) collective-permute-start(bf16[256,256]{1,0:T(8,128)(2,1)S(1)} %collective-permute-done.10.got), channel_id=1, source_target_pairs={{8,9},{9,8},{10,11},{11,10},{12,13},{13,12},{14,15},{15,14},{24,25... | collective-permute-start | bytes 393224 | tf_op jit(solution)/shard_map/ppermute | solution.py:535
  42.2 0.1 image_and_maps.3
  42.3 0.0 collective-permute-done.6.third
  42.3 0.1 collective-permute-done.8.second
  42.4 0.0 collective-permute-done.11.other
  42.4 0.7 %entering.1 = (bf16[64,256]{1,0:T(8,128)(2,1)S(1)}, bf16[64,256]{1,0:T(8,128)(2,1)S(1)}, bf16[64,256]{1,0:T(8,128)(2,1)S(1)}, bf16[64,256]{1,0:T(8,128)(2,1)S(1)}) custom-call(bf16[64,256]{1,0:T(8,128)(2,1)S(1)} %collective-permute-done.6.third, bf16[64,256]{1,0:T(8,128)(2,1)S(1)} %collective-permute-done.7.near_one, ...), custom_call_target="tpu_custom_call" | custom-call | flops 1610000000 | tf_op jit(solution)/shard_map/entering/pallas_call | solution.py:460
  43.1 0.3 collective-permute-start.12
  43.4 1.2 %collective-permute-start.13 = (bf16[64,256]{1,0:T(8,128)(2,1)S(1)}, bf16[64,256]{1,0:T(8,128)(2,1)S(1)}, u32[]{:S(2)}, u32[]{:S(2)}) collective-permute-start(bf16[64,256]{1,0:T(8,128)(2,1)S(1)} %get-tuple-element.42), channel_id=1, source_target_pairs={{0,2},{1,3},{2,0},{3,1},{4,6},{5,7},{6,4},{7,5},{8,10},{9,11},{10,... | collective-permute-start | bytes 98312 | tf_op jit(solution)/shard_map/ppermute | solution.py:512
  44.6 0.4 collective-permute-start.14
  45.1 1.9 %prop.1 = bf16[2,1024,256]{2,1,0:T(8,128)(2,1)S(1)} custom-call(s32[2,8]{1,0:T(2,128)S(1)} %bitcast.19, bf16[2,1024,1024]{2,1,0:T(8,128)(2,1)S(1)} %bitcast.13, bf16[1024,256]{1,0:T(8,128)(2,1)S(1)} %bitcast.17, bf16[64,256]{1,0:T(8,128)(2,1)S(1)} %get-tuple-element.40._tie.own), custom_call_target="tpu_custom_call" | custom-call | flops 1724999936 | tf_op jit(solution)/shard_map/prop/pallas_call | solution.py:244
  47.0 0.0 collective-permute-done.12.far
  47.0 0.6 %collective-permute-done.13.across = bf16[64,256]{1,0:T(8,128)(2,1)S(1)} collective-permute-done((bf16[64,256]{1,0:T(8,128)(2,1)S(1)}, bf16[64,256]{1,0:T(8,128)(2,1)S(1)}, u32[]{:S(2)}, u32[]{:S(2)}) %collective-permute-start.13) | collective-permute-done | bytes 32800 | tf_op jit(solution)/shard_map/ppermute | solution.py:512
  47.6 0.0 collective-permute-done.14.near
  47.6 1.2 %waves.1 = bf16[2,1024,128]{2,1,0:T(8,128)(2,1)} custom-call(bf16[64,256]{1,0:T(8,128)(2,1)S(1)} %get-tuple-element.40._tie.own, bf16[64,256]{1,0:T(8,128)(2,1)S(1)} %collective-permute-done.12.far, bf16[64,256]{1,0:T(8,128)(2,1)S(1)} %collective-permute-done.13.across, bf16[64,256]{1,0:T(8,128)(2,1)S(1)} %collective-permute-done.14.near, ...), custom_call_target="tpu_custom_call" | custom-call | flops 1495000064 | tf_op jit(solution)/shard_map/waves/pallas_call | solution.py:491
  (10 shorter events, 0.0 us)
Async XLA Ops:
  0.0 11.5 %copy-start.3 = (bf16[1,1024,256]{2,1,0:T(8,128)(2,1)S(1)}, bf16[1,1024,256]{2,1,0:T(8,128)(2,1)}, u32[]{:S(2)}) copy-start(bf16[1,1024,256]{2,1,0:T(8,128)(2,1)} %param.8) | copy-start | bytes 1572868
  0.0 11.5 %copy-start.4 = (s32[1,8,2]{1,2,0:T(2,128)S(1)}, s32[1,8,2]{1,2,0:T(2,128)}, u32[]{:S(2)}) copy-start(s32[1,8,2]{1,2,0:T(2,128)} %param.9) | copy-start | bytes 196
  4.0 22.6 %copy-start.2 = (bf16[1,2,1024,128]{3,2,1,0:T(8,128)(2,1)S(1)}, bf16[1,2,1024,128]{3,2,1,0:T(8,128)(2,1)}, u32[]{:S(2)}) copy-start(bf16[1,2,1024,128]{3,2,1,0:T(8,128)(2,1)} %param.7) | copy-start | bytes 1572868
  4.0 22.6 %all-to-all-start = ((bf16[16,136,128]{2,1,0:T(8,128)(2,1)}), bf16[16,136,128]{2,1,0:T(8,128)(2,1)S(1)}, u32[]{:S(2)}, u32[]{:S(2)}) async-start(bf16[16,136,128]{2,1,0:T(8,128)(2,1)} %pairs.1), calls=%async_computation | async-start | bytes 1114112 | tf_op jit(solution)/shard_map/all_to_all | solution.py:562
  11.5 2.2 %copy-start = (bf16[1,2,1024,1024]{3,2,1,0:T(8,128)(2,1)S(1)}, bf16[1,2,1024,1024]{3,2,1,0:T(8,128)(2,1)}, u32[]{:S(2)}) copy-start(bf16[1,2,1024,1024]{3,2,1,0:T(8,128)(2,1)} %param.6) | copy-start | bytes 12582916
  14.8 0.8 %copy-start.5 = (bf16[256,1024]{1,0:T(8,128)(2,1)}, bf16[256,1024]{1,0:T(8,128)(2,1)S(1)}, u32[]{:S(2)}) copy-start(bf16[256,1024]{1,0:T(8,128)(2,1)S(1)} %get-tuple-element.26.refs_1_) | copy-start | bytes 1572868
  15.6 12.5 %collective-permute-start.3 = (f32[256,256]{1,0:T(8,128)S(1)}, f32[256,256]{1,0:T(8,128)S(1)}, u32[]{:S(2)}, u32[]{:S(2)}) collective-permute-start(f32[256,256]{1,0:T(8,128)S(1)} %get-tuple-element.32), channel_id=1, source_target_pairs={{0,2},{1,3},{2,0},{3,1},{4,6},{5,7},{6,4},{7,5},{8,10},{9,11},{10,... | collective-permute-start | bytes 786440 | tf_op jit(solution)/shard_map/ppermute | solution.py:512
  17.5 12.9 %collective-permute-start.5 = (f32[256,256]{1,0:T(8,128)S(1)}, f32[256,256]{1,0:T(8,128)S(1)}, u32[]{:S(2)}, u32[]{:S(2)}) collective-permute-start(f32[256,256]{1,0:T(8,128)S(1)} %get-tuple-element.31.own), channel_id=1, source_target_pairs={{0,1},{1,0},{2,3},{3,2},{4,5},{5,4},{6,7},{7,6},{8,9},{9,8},{10,11... | collective-permute-start | bytes 786440 | tf_op jit(solution)/shard_map/ppermute | solution.py:508
  26.6 1.0 %copy-start.6 = (bf16[256,1024]{1,0:T(8,128)(2,1)S(1)}, bf16[256,1024]{1,0:T(8,128)(2,1)}, u32[]{:S(2)}) copy-start(bf16[256,1024]{1,0:T(8,128)(2,1)} %copy-done.5) | copy-start | bytes 1572868
  27.5 3.8 %copy-start.1 = (bf16[1,2,1024,1024]{3,2,1,0:T(8,128)(2,1)S(1)}, bf16[1,2,1024,1024]{3,2,1,0:T(8,128)(2,1)}, u32[]{:S(2)}) copy-start(bf16[1,2,1024,1024]{3,2,1,0:T(8,128)(2,1)} %param.6) | copy-start | bytes 12582916
  28.1 2.3 %collective-permute-start.4 = (f32[256,256]{1,0:T(8,128)S(1)}, f32[256,256]{1,0:T(8,128)S(1)}, u32[]{:S(2)}, u32[]{:S(2)}) collective-permute-start(f32[256,256]{1,0:T(8,128)S(1)} %after_exchange.1.across), channel_id=1, source_target_pairs={{0,1},{1,0},{2,3},{3,2},{4,5},{5,4},{6,7},{7,6},{8,9},{9,8},{10,11... | collective-permute-start | bytes 786440 | tf_op jit(solution)/shard_map/ppermute | solution.py:508
  28.2 5.5 %collective-permute-start = (bf16[64,256]{1,0:T(8,128)(2,1)S(1)}, bf16[64,256]{1,0:T(8,128)(2,1)S(1)}, u32[]{:S(2)}, u32[]{:S(2)}) collective-permute-start(bf16[64,256]{1,0:T(8,128)(2,1)S(1)} %get-tuple-element.28), channel_id=1, source_target_pairs={{0,2},{1,3},{2,0},{3,1},{4,6},{5,7},{6,4},{7,5},{8,10},{9,11},{10,... | collective-permute-start | bytes 98312 | tf_op jit(solution)/shard_map/ppermute | solution.py:512
  29.4 4.3 %collective-permute-start.1 = (bf16[64,256]{1,0:T(8,128)(2,1)S(1)}, bf16[64,256]{1,0:T(8,128)(2,1)S(1)}, u32[]{:S(2)}, u32[]{:S(2)}) collective-permute-start(bf16[64,256]{1,0:T(8,128)(2,1)S(1)} %get-tuple-element.29), channel_id=1, source_target_pairs={{0,3},{1,2},{2,1},{3,0},{4,7},{5,6},{6,5},{7,4},{8,11},{9,10},{10,... | collective-permute-start | bytes 98312 | tf_op jit(solution)/shard_map/ppermute | solution.py:516
  30.1 3.7 %collective-permute-start.2 = (bf16[64,256]{1,0:T(8,128)(2,1)S(1)}, bf16[64,256]{1,0:T(8,128)(2,1)S(1)}, u32[]{:S(2)}, u32[]{:S(2)}) collective-permute-start(bf16[64,256]{1,0:T(8,128)(2,1)S(1)} %get-tuple-element.30), channel_id=1, source_target_pairs={{0,1},{1,0},{2,3},{3,2},{4,5},{5,4},{6,7},{7,6},{8,9},{9,8},{10,11... | collective-permute-start | bytes 98312 | tf_op jit(solution)/shard_map/ppermute | solution.py:508
  33.1 8.4 %collective-permute-start.10 = (bf16[256,256]{1,0:T(8,128)(2,1)S(1)}, bf16[256,256]{1,0:T(8,128)(2,1)S(1)}, u32[]{:S(2)}, u32[]{:S(2)}) collective-permute-start(bf16[256,256]{1,0:T(8,128)(2,1)S(1)} %get-tuple-element.36), channel_id=1, source_target_pairs={{4,8},{8,12},{5,13},{6,10},{10,14},{7,15},{20,24},{24,28},{21,29},... | collective-permute-start | bytes 393224 | tf_op jit(solution)/shard_map/ppermute | solution.py:534
  34.4 7.9 %collective-permute-start.6 = (bf16[64,256]{1,0:T(8,128)(2,1)S(1)}, bf16[64,256]{1,0:T(8,128)(2,1)S(1)}, u32[]{:S(2)}, u32[]{:S(2)}) collective-permute-start(bf16[64,256]{1,0:T(8,128)(2,1)S(1)} %get-tuple-element.35), channel_id=1, source_target_pairs={{0,12},{1,13},{2,14},{3,15},{16,28},{17,29},{18,30},{19,31}} | collective-permute-start | bytes 98312 | tf_op jit(solution)/shard_map/ppermute | solution.py:540
  38.2 4.1 %collective-permute-start.7 = (bf16[64,256]{1,0:T(8,128)(2,1)S(1)}, bf16[64,256]{1,0:T(8,128)(2,1)S(1)}, u32[]{:S(2)}, u32[]{:S(2)}) collective-permute-start(bf16[64,256]{1,0:T(8,128)(2,1)S(1)} %get-tuple-element.35), channel_id=1, source_target_pairs={{0,4},{1,5},{2,6},{3,7},{16,20},{17,21},{18,22},{19,23}} | collective-permute-start | bytes 98312 | tf_op jit(solution)/shard_map/ppermute | solution.py:540
  39.5 2.9 %collective-permute-start.8 = (bf16[64,256]{1,0:T(8,128)(2,1)S(1)}, bf16[64,256]{1,0:T(8,128)(2,1)S(1)}, u32[]{:S(2)}, u32[]{:S(2)}) collective-permute-start(bf16[64,256]{1,0:T(8,128)(2,1)S(1)} %get-tuple-element.35), channel_id=1, source_target_pairs={{0,8},{1,9},{2,10},{3,11},{4,12},{5,13},{6,14},{7,15},{16,24},{17,... | collective-permute-start | bytes 98312 | tf_op jit(solution)/shard_map/ppermute | solution.py:540
  40.8 1.6 %collective-permute-start.9 = (bf16[64,256]{1,0:T(8,128)(2,1)S(1)}, bf16[64,256]{1,0:T(8,128)(2,1)S(1)}, u32[]{:S(2)}, u32[]{:S(2)}) collective-permute-start(bf16[64,256]{1,0:T(8,128)(2,1)S(1)} %get-tuple-element.35), channel_id=1, source_target_pairs={{4,8},{5,9},{6,10},{7,11},{8,12},{9,13},{10,14},{11,15},{20,24},{2... | collective-permute-start | bytes 98312 | tf_op jit(solution)/shard_map/ppermute | solution.py:540
  41.5 0.9 %collective-permute-start.11 = (bf16[256,256]{1,0:T(8,128)(2,1)S(1)}, bf16[256,256]{1,0:T(8,128)(2,1)S(1)}, u32[]{:S(2)}, u32[]{:S(2)}) collective-permute-start(bf16[256,256]{1,0:T(8,128)(2,1)S(1)} %collective-permute-done.10.got), channel_id=1, source_target_pairs={{8,9},{9,8},{10,11},{11,10},{12,13},{13,12},{14,15},{15,14},{24,25... | collective-permute-start | bytes 393224 | tf_op jit(solution)/shard_map/ppermute | solution.py:535
  43.1 3.8 %collective-permute-start.12 = (bf16[64,256]{1,0:T(8,128)(2,1)S(1)}, bf16[64,256]{1,0:T(8,128)(2,1)S(1)}, u32[]{:S(2)}, u32[]{:S(2)}) collective-permute-start(bf16[64,256]{1,0:T(8,128)(2,1)S(1)} %get-tuple-element.41), channel_id=1, source_target_pairs={{0,3},{1,2},{2,1},{3,0},{4,7},{5,6},{6,5},{7,4},{8,11},{9,10},{10,... | collective-permute-start | bytes 98312 | tf_op jit(solution)/shard_map/ppermute | solution.py:516
  43.4 4.1 %collective-permute-start.13 = (bf16[64,256]{1,0:T(8,128)(2,1)S(1)}, bf16[64,256]{1,0:T(8,128)(2,1)S(1)}, u32[]{:S(2)}, u32[]{:S(2)}) collective-permute-start(bf16[64,256]{1,0:T(8,128)(2,1)S(1)} %get-tuple-element.42), channel_id=1, source_target_pairs={{0,2},{1,3},{2,0},{3,1},{4,6},{5,7},{6,4},{7,5},{8,10},{9,11},{10,... | collective-permute-start | bytes 98312 | tf_op jit(solution)/shard_map/ppermute | solution.py:512
  44.6 2.9 %collective-permute-start.14 = (bf16[64,256]{1,0:T(8,128)(2,1)S(1)}, bf16[64,256]{1,0:T(8,128)(2,1)S(1)}, u32[]{:S(2)}, u32[]{:S(2)}) collective-permute-start(bf16[64,256]{1,0:T(8,128)(2,1)S(1)} %get-tuple-element.43), channel_id=1, source_target_pairs={{0,1},{1,0},{2,3},{3,2},{4,5},{5,4},{6,7},{7,6},{8,9},{9,8},{10,11... | collective-permute-start | bytes 98312 | tf_op jit(solution)/shard_map/ppermute | solution.py:508

commit v36 on v34

--- a/solution.py
+++ b/solution.py
@@ -330,11 +330,11 @@
     split = GROUP // energies
     size = quarters.shape[1]
     for e in range(energies):
-        wide = dot(face_rows[e][...], source[e]).T
+        wide = dot(face_rows[e][...], source[e]).astype(BF16).T
         for h in range(split):
             quarters[e * split + h] = wide[h * size : (h + 1) * size]
     for out, at in zip((own, far, across, near), partners()):
-        out[...] = quarters[at].astype(BF16)
+        out[...] = quarters[at]
 
 
 def face_quarters(source, face_rows):
@@ -346,7 +346,7 @@
         "face_quarters",
         [IN_VMEM] * (1 + energies),
         [shape(rows, face)] * GROUP,
-        [pltpu.VMEM((GROUP, rows, face), F32)],
+        [pltpu.VMEM((GROUP, rows, face), BF16)],
         0.6,
     )(source, *face_rows)
 

time: 49.1 us -> 49 us (level)
  no operation moved by 1% of the time
where the time goes in v36:
time: 49 us; the launch traced here: 48.6 us
  starting transfers between devices  22 us (45%)
  Pallas kernels  13.6 us (28%)
  waiting for transfers between devices  9.65 us (20%)
  local copies, waits for them, and re-layouts  3.09 us (6%)
    all_to_all x1, waiting for transfers between devices, per_device(): lax.all_to_all(outgoing, 'sec', split_axis=0, concat_axis=0, tiled=True)  9.01 us
    all_to_all x1, starting transfers between devices, per_device(): lax.all_to_all(outgoing, 'sec', split_axis=0, concat_axis=0, tiled=True)  7.5 us
    ppermute x4, starting transfers between devices, between(): return lax.ppermute(item, 'sec', pairs)  7.06 us
    pallas_call x1, Pallas kernels, outgoing_pairs(): pl.pallas_call(pairs_kernel, name='pairs', in_specs=[IN_HBM] * 4, out_sha...  3.96 us
    ppermute x3, starting transfers between devices, to_across(): lax.ppermute(item, 'sec', [(s, s // GROUP * GROUP + (s % GROUP + CORES) %...  3.72 us
    unnamed x14, local copies, waits for them, and re-layouts  3.09 us
    pallas_call x2, Pallas kernels, image_and_maps(): call(functools.partial(work_kernel, not held), 'image_and_maps', [IN_VMEM...  1.91 us
    pallas_call x1, Pallas kernels, propagator(): call(prop_kernel, 'prop', [IN_SMEM, IN_VMEM, IN_VMEM, IN_PLACE], shape(en...  1.9 us
  transfers between devices with their start and end apart: 16, of which 3 were waited for; matrix products, arithmetic and copies ran while one was open for 0% of the time, Pallas kernels for 16%

profile of v36, /device:TPU:0, one launch (start us, length us, event | category | flops | bytes accessed | tf_op | source)
XLA Modules:
  0.0 48.6 jit_solution(16235062813178615399)
XLA Ops:
  0.0 4.0 %pairs.1 = bf16[16,136,128]{2,1,0:T(8,128)(2,1)} custom-call(s32[16]{0:T(128)} %bitcast.21, s32[2,16]{1,0:T(2,128)} %bitcast.20, bf16[2,1024,1024]{2,1,0:T(8,128)(2,1)} %bitcast.9, bf16[2,1024,128]{2,1,0:T(8,128)(2,1)} %bitcast.14), custom_call_target="tpu_custom_call" | custom-call | flops 4600000000 | tf_op jit(solution)/shard_map/pairs/pallas_call | solution.py:183
  4.0 0.0 copy-start.2
  4.0 7.5 %all-to-all-start = ((bf16[16,136,128]{2,1,0:T(8,128)(2,1)}), bf16[16,136,128]{2,1,0:T(8,128)(2,1)S(1)}, u32[]{:S(2)}, u32[]{:S(2)}) async-start(bf16[16,136,128]{2,1,0:T(8,128)(2,1)} %pairs.1), calls=%async_computation | async-start | bytes 1114112 | tf_op jit(solution)/shard_map/all_to_all | solution.py:562
  11.5 0.0 copy-start
  11.5 2.2 %copy-done = bf16[1,2,1024,1024]{3,2,1,0:T(8,128)(2,1)S(1)} copy-done((bf16[1,2,1024,1024]{3,2,1,0:T(8,128)(2,1)S(1)}, bf16[1,2,1024,1024]{3,2,1,0:T(8,128)(2,1)}, u32[]{:S(2)}) %copy-start) | copy-done | bytes 4194328
  13.7 1.1 %face_maps.1 = (f32[256,256]{1,0:T(8,128)S(1)}, f32[256,256]{1,0:T(8,128)S(1)}, bf16[256,1024]{1,0:T(8,128)(2,1)S(1)}, bf16[256,1024]{1,0:T(8,128)(2,1)S(1)}) custom-call(s32[2,8]{1,0:T(2,128)S(1)} %bitcast.18, bf16[2,1024,1024]{2,1,0:T(8,128)(2,1)S(1)} %bitcast.10, bf16[1024,256]{1,0:T(8,128)(2,1)S(1)} %bitcast.16), custom_call_target="tpu_custom_call" | custom-call | flops 1380000000 | tf_op jit(solution)/shard_map/face_maps/pallas_call | solution.py:225
  14.8 0.0 copy-start.5
  14.8 0.8 %copy-done.5 = bf16[256,1024]{1,0:T(8,128)(2,1)} copy-done((bf16[256,1024]{1,0:T(8,128)(2,1)}, bf16[256,1024]{1,0:T(8,128)(2,1)S(1)}, u32[]{:S(2)}) %copy-start.5) | copy-done | bytes 524312
  15.6 1.9 %collective-permute-start.3 = (f32[256,256]{1,0:T(8,128)S(1)}, f32[256,256]{1,0:T(8,128)S(1)}, u32[]{:S(2)}, u32[]{:S(2)}) collective-permute-start(f32[256,256]{1,0:T(8,128)S(1)} %get-tuple-element.32), channel_id=1, source_target_pairs={{0,2},{1,3},{2,0},{3,1},{4,6},{5,7},{6,4},{7,5},{8,10},{9,11},{10,... | collective-permute-start | bytes 786440 | tf_op jit(solution)/shard_map/ppermute | solution.py:512
  17.5 0.0 collective-permute-start.5
  17.5 9.0 %all-to-all-done.received = bf16[16,136,128]{2,1,0:T(8,128)(2,1)S(1)} async-done(((bf16[16,136,128]{2,1,0:T(8,128)(2,1)}), bf16[16,136,128]{2,1,0:T(8,128)(2,1)S(1)}, u32[]{:S(2)}, u32[]{:S(2)}) %all-to-all-start) | async-done | bytes 557088 | tf_op jit(solution)/shard_map/all_to_all | solution.py:562
  26.6 0.9 %source.1.refs_1_ = bf16[2,1024,128]{2,1,0:T(8,128)(2,1)S(1)} custom-call(bf16[16,136,128]{2,1,0:T(8,128)(2,1)S(1)} %all-to-all-done.received, bf16[2,1024,128]{2,1,0:T(8,128)(2,1)S(1)} %bitcast.15), custom_call_target="tpu_custom_call" | custom-call | flops 1150000000 | tf_op jit(solution)/shard_map/source/pallas_call | solution.py:311
  27.5 0.0 copy-start.1
  27.5 0.1 copy-done.6
  27.6 0.5 %face_quarters.1 = (bf16[64,256]{1,0:T(8,128)(2,1)S(1)}, bf16[64,256]{1,0:T(8,128)(2,1)S(1)}, bf16[64,256]{1,0:T(8,128)(2,1)S(1)}, bf16[64,256]{1,0:T(8,128)(2,1)S(1)}) custom-call(bf16[2,1024,128]{2,1,0:T(8,128)(2,1)S(1)} %source.1.refs_1_, bf16[256,1024]{1,0:T(8,128)(2,1)S(1)} %get-tuple-element.25.refs_0_, bf16[256,1024]{1,0:T(8,128)(2,1)S(1)} %copy-done.6), custom_call_target="tpu_custom_call" | custom-call | flops 690000000 | tf_op jit(solution)/shard_map/face_quarters/pallas_call | solution.py:344
  28.1 0.0 collective-permute-done.3._map
  28.1 0.1 collective-permute-start.4
  28.2 0.9 %collective-permute-start = (bf16[64,256]{1,0:T(8,128)(2,1)S(1)}, bf16[64,256]{1,0:T(8,128)(2,1)S(1)}, u32[]{:S(2)}, u32[]{:S(2)}) collective-permute-start(bf16[64,256]{1,0:T(8,128)(2,1)S(1)} %get-tuple-element.28), channel_id=1, source_target_pairs={{0,3},{1,2},{2,1},{3,0},{4,7},{5,6},{6,5},{7,4},{8,11},{9,10},{10,... | collective-permute-start | bytes 98312 | tf_op jit(solution)/shard_map/ppermute | solution.py:516
  29.1 1.3 %collective-permute-start.1 = (bf16[64,256]{1,0:T(8,128)(2,1)S(1)}, bf16[64,256]{1,0:T(8,128)(2,1)S(1)}, u32[]{:S(2)}, u32[]{:S(2)}) collective-permute-start(bf16[64,256]{1,0:T(8,128)(2,1)S(1)} %get-tuple-element.29), channel_id=1, source_target_pairs={{0,2},{1,3},{2,0},{3,1},{4,6},{5,7},{6,4},{7,5},{8,10},{9,11},{10,... | collective-permute-start | bytes 98312 | tf_op jit(solution)/shard_map/ppermute | solution.py:512
  30.3 0.0 collective-permute-start.2
  30.3 0.0 collective-permute-done.5.near
  30.3 0.0 collective-permute-done.4.far
  30.3 0.8 %chain_maps.1 = (bf16[256,256]{1,0:T(8,128)(2,1)S(1)}, bf16[2,4,256,256]{3,2,1,0:T(8,128)(2,1)S(1)}) custom-call(f32[256,256]{1,0:T(8,128)S(1)} %get-tuple-element.31.own, f32[256,256]{1,0:T(8,128)S(1)} %collective-permute-done.4.far, f32[256,256]{1,0:T(8,128)S(1)} %after_exchange.1.across, f32[256,256]{1,0:T(8,128)S(1)} %collective-permute-done.5.near), custom_call_target="tpu_custom_call" | custom-call | flops 1035000000 | tf_op jit(solution)/shard_map/chain_maps/pallas_call | solution.py:270
  31.2 1.8 %image_and_maps.2 = (f32[2,1024,128]{2,1,0:T(8,128)S(1)}, bf16[2,2,256,256]{3,2,1,0:T(8,128)(2,1)S(1)}) custom-call(bf16[2,1024,1024]{2,1,0:T(8,128)(2,1)S(1)} %bitcast.11, bf16[2,1024,128]{2,1,0:T(8,128)(2,1)S(1)} %source.1.refs_1_, bf16[2,4,256,256]{3,2,1,0:T(8,128)(2,1)S(1)} %get-tuple-element.33.refs_2_.parts), custom_call_target="tpu_custom_call" | custom-call | flops 2300000000 | tf_op jit(solution)/shard_map/image_and_maps/pallas_call | solution.py:420
  33.0 0.7 %collective-permute-start.10 = (bf16[256,256]{1,0:T(8,128)(2,1)S(1)}, bf16[256,256]{1,0:T(8,128)(2,1)S(1)}, u32[]{:S(2)}, u32[]{:S(2)}) collective-permute-start(bf16[256,256]{1,0:T(8,128)(2,1)S(1)} %get-tuple-element.36), channel_id=1, source_target_pairs={{4,8},{8,12},{5,13},{6,10},{10,14},{7,15},{20,24},{24,28},{21,29},... | collective-permute-start | bytes 393224 | tf_op jit(solution)/shard_map/ppermute | solution.py:534
  33.7 0.0 collective-permute-done.far
  33.7 0.0 collective-permute-done.1.across
  33.7 0.0 collective-permute-done.2.near
  33.7 0.6 %plane_total.1 = (bf16[64,256]{1,0:T(8,128)(2,1)S(1)}, f32[3,64,256]{2,1,0:T(8,128)S(1)}) custom-call(bf16[64,256]{1,0:T(8,128)(2,1)S(1)} %get-tuple-element.27._packets.own, bf16[64,256]{1,0:T(8,128)(2,1)S(1)} %collective-permute-done.far, bf16[64,256]{1,0:T(8,128)(2,1)S(1)} %collective-permute-done.1.across, ...), custom_call_target="tpu_custom_call" | custom-call | flops 3449999872 | tf_op jit(solution)/shard_map/plane_total/pallas_call | solution.py:386
  34.3 3.8 %collective-permute-start.6 = (bf16[64,256]{1,0:T(8,128)(2,1)S(1)}, bf16[64,256]{1,0:T(8,128)(2,1)S(1)}, u32[]{:S(2)}, u32[]{:S(2)}) collective-permute-start(bf16[64,256]{1,0:T(8,128)(2,1)S(1)} %get-tuple-element.35), channel_id=1, source_target_pairs={{0,12},{1,13},{2,14},{3,15},{16,28},{17,29},{18,30},{19,31}} | collective-permute-start | bytes 98312 | tf_op jit(solution)/shard_map/ppermute | solution.py:540
  38.1 1.3 %collective-permute-start.7 = (bf16[64,256]{1,0:T(8,128)(2,1)S(1)}, bf16[64,256]{1,0:T(8,128)(2,1)S(1)}, u32[]{:S(2)}, u32[]{:S(2)}) collective-permute-start(bf16[64,256]{1,0:T(8,128)(2,1)S(1)} %get-tuple-element.35), channel_id=1, source_target_pairs={{0,4},{1,5},{2,6},{3,7},{16,20},{17,21},{18,22},{19,23}} | collective-permute-start | bytes 98312 | tf_op jit(solution)/shard_map/ppermute | solution.py:540
  39.4 1.3 %collective-permute-start.8 = (bf16[64,256]{1,0:T(8,128)(2,1)S(1)}, bf16[64,256]{1,0:T(8,128)(2,1)S(1)}, u32[]{:S(2)}, u32[]{:S(2)}) collective-permute-start(bf16[64,256]{1,0:T(8,128)(2,1)S(1)} %get-tuple-element.35), channel_id=1, source_target_pairs={{0,8},{1,9},{2,10},{3,11},{4,12},{5,13},{6,14},{7,15},{16,24},{17,... | collective-permute-start | bytes 98312 | tf_op jit(solution)/shard_map/ppermute | solution.py:540
  40.7 0.7 %collective-permute-start.9 = (bf16[64,256]{1,0:T(8,128)(2,1)S(1)}, bf16[64,256]{1,0:T(8,128)(2,1)S(1)}, u32[]{:S(2)}, u32[]{:S(2)}) collective-permute-start(bf16[64,256]{1,0:T(8,128)(2,1)S(1)} %get-tuple-element.35), channel_id=1, source_target_pairs={{4,8},{5,9},{6,10},{7,11},{8,12},{9,13},{10,14},{11,15},{20,24},{2... | collective-permute-start | bytes 98312 | tf_op jit(solution)/shard_map/ppermute | solution.py:540
  41.4 0.0 collective-permute-done.10.got
  41.4 0.7 %collective-permute-start.11 = (bf16[256,256]{1,0:T(8,128)(2,1)S(1)}, bf16[256,256]{1,0:T(8,128)(2,1)S(1)}, u32[]{:S(2)}, u32[]{:S(2)}) collective-permute-start(bf16[256,256]{1,0:T(8,128)(2,1)S(1)} %collective-permute-done.10.got), channel_id=1, source_target_pairs={{8,9},{9,8},{10,11},{11,10},{12,13},{13,12},{14,15},{15,14},{24,25... | collective-permute-start | bytes 393224 | tf_op jit(solution)/shard_map/ppermute | solution.py:535
  42.1 0.1 image_and_maps.3
  42.2 0.0 collective-permute-done.6.third
  42.2 0.0 collective-permute-done.7.near_one
  42.2 0.1 collective-permute-done.8.second
  42.3 0.0 collective-permute-done.9.far_one
  42.3 0.0 collective-permute-done.11.other
  42.3 0.7 %entering.1 = (bf16[64,256]{1,0:T(8,128)(2,1)S(1)}, bf16[64,256]{1,0:T(8,128)(2,1)S(1)}, bf16[64,256]{1,0:T(8,128)(2,1)S(1)}, bf16[64,256]{1,0:T(8,128)(2,1)S(1)}) custom-call(bf16[64,256]{1,0:T(8,128)(2,1)S(1)} %collective-permute-done.6.third, bf16[64,256]{1,0:T(8,128)(2,1)S(1)} %collective-permute-done.7.near_one, ...), custom_call_target="tpu_custom_call" | custom-call | flops 1610000000 | tf_op jit(solution)/shard_map/entering/pallas_call | solution.py:460
  43.0 0.5 collective-permute-start.12
  43.5 0.5 %collective-permute-start.13 = (bf16[64,256]{1,0:T(8,128)(2,1)S(1)}, bf16[64,256]{1,0:T(8,128)(2,1)S(1)}, u32[]{:S(2)}, u32[]{:S(2)}) collective-permute-start(bf16[64,256]{1,0:T(8,128)(2,1)S(1)} %get-tuple-element.42), channel_id=1, source_target_pairs={{0,2},{1,3},{2,0},{3,1},{4,6},{5,7},{6,4},{7,5},{8,10},{9,11},{10,... | collective-permute-start | bytes 98312 | tf_op jit(solution)/shard_map/ppermute | solution.py:512
  44.0 0.9 %collective-permute-start.14 = (bf16[64,256]{1,0:T(8,128)(2,1)S(1)}, bf16[64,256]{1,0:T(8,128)(2,1)S(1)}, u32[]{:S(2)}, u32[]{:S(2)}) collective-permute-start(bf16[64,256]{1,0:T(8,128)(2,1)S(1)} %get-tuple-element.43), channel_id=1, source_target_pairs={{0,1},{1,0},{2,3},{3,2},{4,5},{5,4},{6,7},{7,6},{8,9},{9,8},{10,11... | collective-permute-start | bytes 98312 | tf_op jit(solution)/shard_map/ppermute | solution.py:508
  45.0 1.9 %prop.1 = bf16[2,1024,256]{2,1,0:T(8,128)(2,1)S(1)} custom-call(s32[2,8]{1,0:T(2,128)S(1)} %bitcast.19, bf16[2,1024,1024]{2,1,0:T(8,128)(2,1)S(1)} %bitcast.13, bf16[1024,256]{1,0:T(8,128)(2,1)S(1)} %bitcast.17, bf16[64,256]{1,0:T(8,128)(2,1)S(1)} %get-tuple-element.40._tie.own), custom_call_target="tpu_custom_call" | custom-call | flops 1724999936 | tf_op jit(solution)/shard_map/prop/pallas_call | solution.py:244
  46.9 0.5 %collective-permute-done.13.across = bf16[64,256]{1,0:T(8,128)(2,1)S(1)} collective-permute-done((bf16[64,256]{1,0:T(8,128)(2,1)S(1)}, bf16[64,256]{1,0:T(8,128)(2,1)S(1)}, u32[]{:S(2)}, u32[]{:S(2)}) %collective-permute-start.13) | collective-permute-done | bytes 32800 | tf_op jit(solution)/shard_map/ppermute | solution.py:512
  47.4 1.2 %waves.1 = bf16[2,1024,128]{2,1,0:T(8,128)(2,1)} custom-call(bf16[64,256]{1,0:T(8,128)(2,1)S(1)} %get-tuple-element.40._tie.own, bf16[64,256]{1,0:T(8,128)(2,1)S(1)} %collective-permute-done.12.far, bf16[64,256]{1,0:T(8,128)(2,1)S(1)} %collective-permute-done.13.across, bf16[64,256]{1,0:T(8,128)(2,1)S(1)} %collective-permute-done.14.near, ...), custom_call_target="tpu_custom_call" | custom-call | flops 1495000064 | tf_op jit(solution)/shard_map/waves/pallas_call | solution.py:491
  (10 shorter events, 0.0 us)
Async XLA Ops:
  0.0 11.5 %copy-start.3 = (bf16[1,1024,256]{2,1,0:T(8,128)(2,1)S(1)}, bf16[1,1024,256]{2,1,0:T(8,128)(2,1)}, u32[]{:S(2)}) copy-start(bf16[1,1024,256]{2,1,0:T(8,128)(2,1)} %param.8) | copy-start | bytes 1572868
  0.0 11.5 %copy-start.4 = (s32[1,8,2]{1,2,0:T(2,128)S(1)}, s32[1,8,2]{1,2,0:T(2,128)}, u32[]{:S(2)}) copy-start(s32[1,8,2]{1,2,0:T(2,128)} %param.9) | copy-start | bytes 196
  4.0 22.6 %copy-start.2 = (bf16[1,2,1024,128]{3,2,1,0:T(8,128)(2,1)S(1)}, bf16[1,2,1024,128]{3,2,1,0:T(8,128)(2,1)}, u32[]{:S(2)}) copy-start(bf16[1,2,1024,128]{3,2,1,0:T(8,128)(2,1)} %param.7) | copy-start | bytes 1572868
  4.0 22.6 %all-to-all-start = ((bf16[16,136,128]{2,1,0:T(8,128)(2,1)}), bf16[16,136,128]{2,1,0:T(8,128)(2,1)S(1)}, u32[]{:S(2)}, u32[]{:S(2)}) async-start(bf16[16,136,128]{2,1,0:T(8,128)(2,1)} %pairs.1), calls=%async_computation | async-start | bytes 1114112 | tf_op jit(solution)/shard_map/all_to_all | solution.py:562
  11.5 2.2 %copy-start = (bf16[1,2,1024,1024]{3,2,1,0:T(8,128)(2,1)S(1)}, bf16[1,2,1024,1024]{3,2,1,0:T(8,128)(2,1)}, u32[]{:S(2)}) copy-start(bf16[1,2,1024,1024]{3,2,1,0:T(8,128)(2,1)} %param.6) | copy-start | bytes 12582916
  14.8 0.8 %copy-start.5 = (bf16[256,1024]{1,0:T(8,128)(2,1)}, bf16[256,1024]{1,0:T(8,128)(2,1)S(1)}, u32[]{:S(2)}) copy-start(bf16[256,1024]{1,0:T(8,128)(2,1)S(1)} %get-tuple-element.26.refs_1_) | copy-start | bytes 1572868
  15.6 12.5 %collective-permute-start.3 = (f32[256,256]{1,0:T(8,128)S(1)}, f32[256,256]{1,0:T(8,128)S(1)}, u32[]{:S(2)}, u32[]{:S(2)}) collective-permute-start(f32[256,256]{1,0:T(8,128)S(1)} %get-tuple-element.32), channel_id=1, source_target_pairs={{0,2},{1,3},{2,0},{3,1},{4,6},{5,7},{6,4},{7,5},{8,10},{9,11},{10,... | collective-permute-start | bytes 786440 | tf_op jit(solution)/shard_map/ppermute | solution.py:512
  17.5 12.8 %collective-permute-start.5 = (f32[256,256]{1,0:T(8,128)S(1)}, f32[256,256]{1,0:T(8,128)S(1)}, u32[]{:S(2)}, u32[]{:S(2)}) collective-permute-start(f32[256,256]{1,0:T(8,128)S(1)} %get-tuple-element.31.own), channel_id=1, source_target_pairs={{0,1},{1,0},{2,3},{3,2},{4,5},{5,4},{6,7},{7,6},{8,9},{9,8},{10,11... | collective-permute-start | bytes 786440 | tf_op jit(solution)/shard_map/ppermute | solution.py:508
  26.6 1.0 %copy-start.6 = (bf16[256,1024]{1,0:T(8,128)(2,1)S(1)}, bf16[256,1024]{1,0:T(8,128)(2,1)}, u32[]{:S(2)}) copy-start(bf16[256,1024]{1,0:T(8,128)(2,1)} %copy-done.5) | copy-start | bytes 1572868
  27.5 3.7 %copy-start.1 = (bf16[1,2,1024,1024]{3,2,1,0:T(8,128)(2,1)S(1)}, bf16[1,2,1024,1024]{3,2,1,0:T(8,128)(2,1)}, u32[]{:S(2)}) copy-start(bf16[1,2,1024,1024]{3,2,1,0:T(8,128)(2,1)} %param.6) | copy-start | bytes 12582916
  28.1 2.2 %collective-permute-start.4 = (f32[256,256]{1,0:T(8,128)S(1)}, f32[256,256]{1,0:T(8,128)S(1)}, u32[]{:S(2)}, u32[]{:S(2)}) collective-permute-start(f32[256,256]{1,0:T(8,128)S(1)} %after_exchange.1.across), channel_id=1, source_target_pairs={{0,1},{1,0},{2,3},{3,2},{4,5},{5,4},{6,7},{7,6},{8,9},{9,8},{10,11... | collective-permute-start | bytes 786440 | tf_op jit(solution)/shard_map/ppermute | solution.py:508
  28.2 5.5 %collective-permute-start = (bf16[64,256]{1,0:T(8,128)(2,1)S(1)}, bf16[64,256]{1,0:T(8,128)(2,1)S(1)}, u32[]{:S(2)}, u32[]{:S(2)}) collective-permute-start(bf16[64,256]{1,0:T(8,128)(2,1)S(1)} %get-tuple-element.28), channel_id=1, source_target_pairs={{0,3},{1,2},{2,1},{3,0},{4,7},{5,6},{6,5},{7,4},{8,11},{9,10},{10,... | collective-permute-start | bytes 98312 | tf_op jit(solution)/shard_map/ppermute | solution.py:516
  29.1 4.6 %collective-permute-start.1 = (bf16[64,256]{1,0:T(8,128)(2,1)S(1)}, bf16[64,256]{1,0:T(8,128)(2,1)S(1)}, u32[]{:S(2)}, u32[]{:S(2)}) collective-permute-start(bf16[64,256]{1,0:T(8,128)(2,1)S(1)} %get-tuple-element.29), channel_id=1, source_target_pairs={{0,2},{1,3},{2,0},{3,1},{4,6},{5,7},{6,4},{7,5},{8,10},{9,11},{10,... | collective-permute-start | bytes 98312 | tf_op jit(solution)/shard_map/ppermute | solution.py:512
  30.3 3.4 %collective-permute-start.2 = (bf16[64,256]{1,0:T(8,128)(2,1)S(1)}, bf16[64,256]{1,0:T(8,128)(2,1)S(1)}, u32[]{:S(2)}, u32[]{:S(2)}) collective-permute-start(bf16[64,256]{1,0:T(8,128)(2,1)S(1)} %get-tuple-element.30), channel_id=1, source_target_pairs={{0,1},{1,0},{2,3},{3,2},{4,5},{5,4},{6,7},{7,6},{8,9},{9,8},{10,11... | collective-permute-start | bytes 98312 | tf_op jit(solution)/shard_map/ppermute | solution.py:508
  33.0 8.4 %collective-permute-start.10 = (bf16[256,256]{1,0:T(8,128)(2,1)S(1)}, bf16[256,256]{1,0:T(8,128)(2,1)S(1)}, u32[]{:S(2)}, u32[]{:S(2)}) collective-permute-start(bf16[256,256]{1,0:T(8,128)(2,1)S(1)} %get-tuple-element.36), channel_id=1, source_target_pairs={{4,8},{8,12},{5,13},{6,10},{10,14},{7,15},{20,24},{24,28},{21,29},... | collective-permute-start | bytes 393224 | tf_op jit(solution)/shard_map/ppermute | solution.py:534
  34.3 7.9 %collective-permute-start.6 = (bf16[64,256]{1,0:T(8,128)(2,1)S(1)}, bf16[64,256]{1,0:T(8,128)(2,1)S(1)}, u32[]{:S(2)}, u32[]{:S(2)}) collective-permute-start(bf16[64,256]{1,0:T(8,128)(2,1)S(1)} %get-tuple-element.35), channel_id=1, source_target_pairs={{0,12},{1,13},{2,14},{3,15},{16,28},{17,29},{18,30},{19,31}} | collective-permute-start | bytes 98312 | tf_op jit(solution)/shard_map/ppermute | solution.py:540
  38.1 4.1 %collective-permute-start.7 = (bf16[64,256]{1,0:T(8,128)(2,1)S(1)}, bf16[64,256]{1,0:T(8,128)(2,1)S(1)}, u32[]{:S(2)}, u32[]{:S(2)}) collective-permute-start(bf16[64,256]{1,0:T(8,128)(2,1)S(1)} %get-tuple-element.35), channel_id=1, source_target_pairs={{0,4},{1,5},{2,6},{3,7},{16,20},{17,21},{18,22},{19,23}} | collective-permute-start | bytes 98312 | tf_op jit(solution)/shard_map/ppermute | solution.py:540
  39.4 2.9 %collective-permute-start.8 = (bf16[64,256]{1,0:T(8,128)(2,1)S(1)}, bf16[64,256]{1,0:T(8,128)(2,1)S(1)}, u32[]{:S(2)}, u32[]{:S(2)}) collective-permute-start(bf16[64,256]{1,0:T(8,128)(2,1)S(1)} %get-tuple-element.35), channel_id=1, source_target_pairs={{0,8},{1,9},{2,10},{3,11},{4,12},{5,13},{6,14},{7,15},{16,24},{17,... | collective-permute-start | bytes 98312 | tf_op jit(solution)/shard_map/ppermute | solution.py:540
  40.7 1.6 %collective-permute-start.9 = (bf16[64,256]{1,0:T(8,128)(2,1)S(1)}, bf16[64,256]{1,0:T(8,128)(2,1)S(1)}, u32[]{:S(2)}, u32[]{:S(2)}) collective-permute-start(bf16[64,256]{1,0:T(8,128)(2,1)S(1)} %get-tuple-element.35), channel_id=1, source_target_pairs={{4,8},{5,9},{6,10},{7,11},{8,12},{9,13},{10,14},{11,15},{20,24},{2... | collective-permute-start | bytes 98312 | tf_op jit(solution)/shard_map/ppermute | solution.py:540
  41.4 0.9 %collective-permute-start.11 = (bf16[256,256]{1,0:T(8,128)(2,1)S(1)}, bf16[256,256]{1,0:T(8,128)(2,1)S(1)}, u32[]{:S(2)}, u32[]{:S(2)}) collective-permute-start(bf16[256,256]{1,0:T(8,128)(2,1)S(1)} %collective-permute-done.10.got), channel_id=1, source_target_pairs={{8,9},{9,8},{10,11},{11,10},{12,13},{13,12},{14,15},{15,14},{24,25... | collective-permute-start | bytes 393224 | tf_op jit(solution)/shard_map/ppermute | solution.py:535
  43.0 3.8 %collective-permute-start.12 = (bf16[64,256]{1,0:T(8,128)(2,1)S(1)}, bf16[64,256]{1,0:T(8,128)(2,1)S(1)}, u32[]{:S(2)}, u32[]{:S(2)}) collective-permute-start(bf16[64,256]{1,0:T(8,128)(2,1)S(1)} %get-tuple-element.41), channel_id=1, source_target_pairs={{0,3},{1,2},{2,1},{3,0},{4,7},{5,6},{6,5},{7,4},{8,11},{9,10},{10,... | collective-permute-start | bytes 98312 | tf_op jit(solution)/shard_map/ppermute | solution.py:516
  43.5 3.9 %collective-permute-start.13 = (bf16[64,256]{1,0:T(8,128)(2,1)S(1)}, bf16[64,256]{1,0:T(8,128)(2,1)S(1)}, u32[]{:S(2)}, u32[]{:S(2)}) collective-permute-start(bf16[64,256]{1,0:T(8,128)(2,1)S(1)} %get-tuple-element.42), channel_id=1, source_target_pairs={{0,2},{1,3},{2,0},{3,1},{4,6},{5,7},{6,4},{7,5},{8,10},{9,11},{10,... | collective-permute-start | bytes 98312 | tf_op jit(solution)/shard_map/ppermute | solution.py:512
  44.0 3.4 %collective-permute-start.14 = (bf16[64,256]{1,0:T(8,128)(2,1)S(1)}, bf16[64,256]{1,0:T(8,128)(2,1)S(1)}, u32[]{:S(2)}, u32[]{:S(2)}) collective-permute-start(bf16[64,256]{1,0:T(8,128)(2,1)S(1)} %get-tuple-element.43), channel_id=1, source_target_pairs={{0,1},{1,0},{2,3},{3,2},{4,5},{5,4},{6,7},{7,6},{8,9},{9,8},{10,11... | collective-permute-start | bytes 98312 | tf_op jit(solution)/shard_map/ppermute | solution.py:508

commit v37 on v36

--- a/solution.py
+++ b/solution.py
@@ -434,9 +434,9 @@
         held.append(local[j - 1] + step_by(state, maps))
     work = out[GROUP]
     for j, item in enumerate(held):
-        work[j] = item
+        work[j] = item.astype(BF16)
     for ref, at in zip(out, partners()):
-        ref[...] = work[at].astype(BF16)
+        ref[...] = work[at]
 
 
 def entering_kernel(third, near_one, second, far_one, got, other, parts, upto, local, *out):
@@ -462,7 +462,7 @@
         "entering",
         [IN_VMEM] * len(args),
         [shape(half, columns)] * GROUP,
-        [pltpu.VMEM((GROUP, half, columns), F32)],
+        [pltpu.VMEM((GROUP, half, columns), BF16)],
         1.4,
     )(*args)
 

time: 49 us -> 49 us (level)
  no operation moved by 1% of the time
where the time goes in v37:
time: 49 us; the launch traced here: 48.6 us
  starting transfers between devices  22 us (45%)
  Pallas kernels  13.6 us (28%)
  waiting for transfers between devices  9.65 us (20%)
  local copies, waits for them, and re-layouts  3.08 us (6%)
    all_to_all x1, waiting for transfers between devices, per_device(): lax.all_to_all(outgoing, 'sec', split_axis=0, concat_axis=0, tiled=True)  9.01 us
    all_to_all x1, starting transfers between devices, per_device(): lax.all_to_all(outgoing, 'sec', split_axis=0, concat_axis=0, tiled=True)  7.5 us
    ppermute x4, starting transfers between devices, between(): return lax.ppermute(item, 'sec', pairs)  7.06 us
    pallas_call x1, Pallas kernels, outgoing_pairs(): pl.pallas_call(pairs_kernel, name='pairs', in_specs=[IN_HBM] * 4, out_sha...  3.96 us
    ppermute x3, starting transfers between devices, to_across(): lax.ppermute(item, 'sec', [(s, s // GROUP * GROUP + (s % GROUP + CORES) %...  3.73 us
    unnamed x14, local copies, waits for them, and re-layouts  3.08 us
    pallas_call x2, Pallas kernels, image_and_maps(): call(functools.partial(work_kernel, not held), 'image_and_maps', [IN_VMEM...  1.91 us
    pallas_call x1, Pallas kernels, propagator(): call(prop_kernel, 'prop', [IN_SMEM, IN_VMEM, IN_VMEM, IN_PLACE], shape(en...  1.9 us
  transfers between devices with their start and end apart: 16, of which 3 were waited for; matrix products, arithmetic and copies ran while one was open for 0% of the time, Pallas kernels for 16%

profile of v37, /device:TPU:0, one launch (start us, length us, event | category | flops | bytes accessed | tf_op | source)
XLA Modules:
  0.0 48.6 jit_solution(11478601340552517601)
XLA Ops:
  0.0 4.0 %pairs.1 = bf16[16,136,128]{2,1,0:T(8,128)(2,1)} custom-call(s32[16]{0:T(128)} %bitcast.21, s32[2,16]{1,0:T(2,128)} %bitcast.20, bf16[2,1024,1024]{2,1,0:T(8,128)(2,1)} %bitcast.9, bf16[2,1024,128]{2,1,0:T(8,128)(2,1)} %bitcast.14), custom_call_target="tpu_custom_call" | custom-call | flops 4600000000 | tf_op jit(solution)/shard_map/pairs/pallas_call | solution.py:183
  4.0 0.0 copy-start.2
  4.0 7.5 %all-to-all-start = ((bf16[16,136,128]{2,1,0:T(8,128)(2,1)}), bf16[16,136,128]{2,1,0:T(8,128)(2,1)S(1)}, u32[]{:S(2)}, u32[]{:S(2)}) async-start(bf16[16,136,128]{2,1,0:T(8,128)(2,1)} %pairs.1), calls=%async_computation | async-start | bytes 1114112 | tf_op jit(solution)/shard_map/all_to_all | solution.py:562
  11.5 0.0 copy-start
  11.5 2.2 %copy-done = bf16[1,2,1024,1024]{3,2,1,0:T(8,128)(2,1)S(1)} copy-done((bf16[1,2,1024,1024]{3,2,1,0:T(8,128)(2,1)S(1)}, bf16[1,2,1024,1024]{3,2,1,0:T(8,128)(2,1)}, u32[]{:S(2)}) %copy-start) | copy-done | bytes 4194328
  13.7 1.1 %face_maps.1 = (f32[256,256]{1,0:T(8,128)S(1)}, f32[256,256]{1,0:T(8,128)S(1)}, bf16[256,1024]{1,0:T(8,128)(2,1)S(1)}, bf16[256,1024]{1,0:T(8,128)(2,1)S(1)}) custom-call(s32[2,8]{1,0:T(2,128)S(1)} %bitcast.18, bf16[2,1024,1024]{2,1,0:T(8,128)(2,1)S(1)} %bitcast.10, bf16[1024,256]{1,0:T(8,128)(2,1)S(1)} %bitcast.16), custom_call_target="tpu_custom_call" | custom-call | flops 1380000000 | tf_op jit(solution)/shard_map/face_maps/pallas_call | solution.py:225
  14.8 0.0 copy-start.5
  14.8 0.8 %copy-done.5 = bf16[256,1024]{1,0:T(8,128)(2,1)} copy-done((bf16[256,1024]{1,0:T(8,128)(2,1)}, bf16[256,1024]{1,0:T(8,128)(2,1)S(1)}, u32[]{:S(2)}) %copy-start.5) | copy-done | bytes 524312
  15.6 1.9 %collective-permute-start.3 = (f32[256,256]{1,0:T(8,128)S(1)}, f32[256,256]{1,0:T(8,128)S(1)}, u32[]{:S(2)}, u32[]{:S(2)}) collective-permute-start(f32[256,256]{1,0:T(8,128)S(1)} %get-tuple-element.32), channel_id=1, source_target_pairs={{0,2},{1,3},{2,0},{3,1},{4,6},{5,7},{6,4},{7,5},{8,10},{9,11},{10,... | collective-permute-start | bytes 786440 | tf_op jit(solution)/shard_map/ppermute | solution.py:512
  17.5 0.0 collective-permute-start.5
  17.5 9.0 %all-to-all-done.received = bf16[16,136,128]{2,1,0:T(8,128)(2,1)S(1)} async-done(((bf16[16,136,128]{2,1,0:T(8,128)(2,1)}), bf16[16,136,128]{2,1,0:T(8,128)(2,1)S(1)}, u32[]{:S(2)}, u32[]{:S(2)}) %all-to-all-start) | async-done | bytes 557088 | tf_op jit(solution)/shard_map/all_to_all | solution.py:562
  26.6 0.9 %source.1.refs_1_ = bf16[2,1024,128]{2,1,0:T(8,128)(2,1)S(1)} custom-call(bf16[16,136,128]{2,1,0:T(8,128)(2,1)S(1)} %all-to-all-done.received, bf16[2,1024,128]{2,1,0:T(8,128)(2,1)S(1)} %bitcast.15), custom_call_target="tpu_custom_call" | custom-call | flops 1150000000 | tf_op jit(solution)/shard_map/source/pallas_call | solution.py:311
  27.5 0.0 copy-start.1
  27.5 0.1 copy-done.6
  27.6 0.5 %face_quarters.1 = (bf16[64,256]{1,0:T(8,128)(2,1)S(1)}, bf16[64,256]{1,0:T(8,128)(2,1)S(1)}, bf16[64,256]{1,0:T(8,128)(2,1)S(1)}, bf16[64,256]{1,0:T(8,128)(2,1)S(1)}) custom-call(bf16[2,1024,128]{2,1,0:T(8,128)(2,1)S(1)} %source.1.refs_1_, bf16[256,1024]{1,0:T(8,128)(2,1)S(1)} %get-tuple-element.25.refs_0_, bf16[256,1024]{1,0:T(8,128)(2,1)S(1)} %copy-done.6), custom_call_target="tpu_custom_call" | custom-call | flops 690000000 | tf_op jit(solution)/shard_map/face_quarters/pallas_call | solution.py:344
  28.1 0.0 collective-permute-done.3._map
  28.1 0.1 collective-permute-start.4
  28.2 0.9 %collective-permute-start = (bf16[64,256]{1,0:T(8,128)(2,1)S(1)}, bf16[64,256]{1,0:T(8,128)(2,1)S(1)}, u32[]{:S(2)}, u32[]{:S(2)}) collective-permute-start(bf16[64,256]{1,0:T(8,128)(2,1)S(1)} %get-tuple-element.28), channel_id=1, source_target_pairs={{0,3},{1,2},{2,1},{3,0},{4,7},{5,6},{6,5},{7,4},{8,11},{9,10},{10,... | collective-permute-start | bytes 98312 | tf_op jit(solution)/shard_map/ppermute | solution.py:516
  29.1 1.3 %collective-permute-start.1 = (bf16[64,256]{1,0:T(8,128)(2,1)S(1)}, bf16[64,256]{1,0:T(8,128)(2,1)S(1)}, u32[]{:S(2)}, u32[]{:S(2)}) collective-permute-start(bf16[64,256]{1,0:T(8,128)(2,1)S(1)} %get-tuple-element.29), channel_id=1, source_target_pairs={{0,2},{1,3},{2,0},{3,1},{4,6},{5,7},{6,4},{7,5},{8,10},{9,11},{10,... | collective-permute-start | bytes 98312 | tf_op jit(solution)/shard_map/ppermute | solution.py:512
  30.3 0.0 collective-permute-start.2
  30.3 0.0 collective-permute-done.5.near
  30.3 0.0 collective-permute-done.4.far
  30.3 0.8 %chain_maps.1 = (bf16[256,256]{1,0:T(8,128)(2,1)S(1)}, bf16[2,4,256,256]{3,2,1,0:T(8,128)(2,1)S(1)}) custom-call(f32[256,256]{1,0:T(8,128)S(1)} %get-tuple-element.31.own, f32[256,256]{1,0:T(8,128)S(1)} %collective-permute-done.4.far, f32[256,256]{1,0:T(8,128)S(1)} %after_exchange.1.across, f32[256,256]{1,0:T(8,128)S(1)} %collective-permute-done.5.near), custom_call_target="tpu_custom_call" | custom-call | flops 1035000000 | tf_op jit(solution)/shard_map/chain_maps/pallas_call | solution.py:270
  31.2 1.8 %image_and_maps.2 = (f32[2,1024,128]{2,1,0:T(8,128)S(1)}, bf16[2,2,256,256]{3,2,1,0:T(8,128)(2,1)S(1)}) custom-call(bf16[2,1024,1024]{2,1,0:T(8,128)(2,1)S(1)} %bitcast.11, bf16[2,1024,128]{2,1,0:T(8,128)(2,1)S(1)} %source.1.refs_1_, bf16[2,4,256,256]{3,2,1,0:T(8,128)(2,1)S(1)} %get-tuple-element.33.refs_2_.parts), custom_call_target="tpu_custom_call" | custom-call | flops 2300000000 | tf_op jit(solution)/shard_map/image_and_maps/pallas_call | solution.py:420
  33.0 0.7 %collective-permute-start.10 = (bf16[256,256]{1,0:T(8,128)(2,1)S(1)}, bf16[256,256]{1,0:T(8,128)(2,1)S(1)}, u32[]{:S(2)}, u32[]{:S(2)}) collective-permute-start(bf16[256,256]{1,0:T(8,128)(2,1)S(1)} %get-tuple-element.36), channel_id=1, source_target_pairs={{4,8},{8,12},{5,13},{6,10},{10,14},{7,15},{20,24},{24,28},{21,29},... | collective-permute-start | bytes 393224 | tf_op jit(solution)/shard_map/ppermute | solution.py:534
  33.7 0.0 collective-permute-done.far
  33.7 0.0 collective-permute-done.1.across
  33.7 0.0 collective-permute-done.2.near
  33.7 0.6 %plane_total.1 = (bf16[64,256]{1,0:T(8,128)(2,1)S(1)}, f32[3,64,256]{2,1,0:T(8,128)S(1)}) custom-call(bf16[64,256]{1,0:T(8,128)(2,1)S(1)} %get-tuple-element.27._packets.own, bf16[64,256]{1,0:T(8,128)(2,1)S(1)} %collective-permute-done.far, bf16[64,256]{1,0:T(8,128)(2,1)S(1)} %collective-permute-done.1.across, ...), custom_call_target="tpu_custom_call" | custom-call | flops 3449999872 | tf_op jit(solution)/shard_map/plane_total/pallas_call | solution.py:386
  34.3 3.8 %collective-permute-start.6 = (bf16[64,256]{1,0:T(8,128)(2,1)S(1)}, bf16[64,256]{1,0:T(8,128)(2,1)S(1)}, u32[]{:S(2)}, u32[]{:S(2)}) collective-permute-start(bf16[64,256]{1,0:T(8,128)(2,1)S(1)} %get-tuple-element.35), channel_id=1, source_target_pairs={{0,12},{1,13},{2,14},{3,15},{16,28},{17,29},{18,30},{19,31}} | collective-permute-start | bytes 98312 | tf_op jit(solution)/shard_map/ppermute | solution.py:540
  38.1 1.3 %collective-permute-start.7 = (bf16[64,256]{1,0:T(8,128)(2,1)S(1)}, bf16[64,256]{1,0:T(8,128)(2,1)S(1)}, u32[]{:S(2)}, u32[]{:S(2)}) collective-permute-start(bf16[64,256]{1,0:T(8,128)(2,1)S(1)} %get-tuple-element.35), channel_id=1, source_target_pairs={{0,4},{1,5},{2,6},{3,7},{16,20},{17,21},{18,22},{19,23}} | collective-permute-start | bytes 98312 | tf_op jit(solution)/shard_map/ppermute | solution.py:540
  39.4 1.3 %collective-permute-start.8 = (bf16[64,256]{1,0:T(8,128)(2,1)S(1)}, bf16[64,256]{1,0:T(8,128)(2,1)S(1)}, u32[]{:S(2)}, u32[]{:S(2)}) collective-permute-start(bf16[64,256]{1,0:T(8,128)(2,1)S(1)} %get-tuple-element.35), channel_id=1, source_target_pairs={{0,8},{1,9},{2,10},{3,11},{4,12},{5,13},{6,14},{7,15},{16,24},{17,... | collective-permute-start | bytes 98312 | tf_op jit(solution)/shard_map/ppermute | solution.py:540
  40.7 0.7 %collective-permute-start.9 = (bf16[64,256]{1,0:T(8,128)(2,1)S(1)}, bf16[64,256]{1,0:T(8,128)(2,1)S(1)}, u32[]{:S(2)}, u32[]{:S(2)}) collective-permute-start(bf16[64,256]{1,0:T(8,128)(2,1)S(1)} %get-tuple-element.35), channel_id=1, source_target_pairs={{4,8},{5,9},{6,10},{7,11},{8,12},{9,13},{10,14},{11,15},{20,24},{2... | collective-permute-start | bytes 98312 | tf_op jit(solution)/shard_map/ppermute | solution.py:540
  41.4 0.0 collective-permute-done.10.got
  41.4 0.7 %collective-permute-start.11 = (bf16[256,256]{1,0:T(8,128)(2,1)S(1)}, bf16[256,256]{1,0:T(8,128)(2,1)S(1)}, u32[]{:S(2)}, u32[]{:S(2)}) collective-permute-start(bf16[256,256]{1,0:T(8,128)(2,1)S(1)} %collective-permute-done.10.got), channel_id=1, source_target_pairs={{8,9},{9,8},{10,11},{11,10},{12,13},{13,12},{14,15},{15,14},{24,25... | collective-permute-start | bytes 393224 | tf_op jit(solution)/shard_map/ppermute | solution.py:535
  42.1 0.1 image_and_maps.3
  42.2 0.0 collective-permute-done.6.third
  42.2 0.0 collective-permute-done.7.near_one
  42.2 0.1 collective-permute-done.8.second
  42.3 0.0 collective-permute-done.9.far_one
  42.3 0.0 collective-permute-done.11.other
  42.3 0.7 %entering.1 = (bf16[64,256]{1,0:T(8,128)(2,1)S(1)}, bf16[64,256]{1,0:T(8,128)(2,1)S(1)}, bf16[64,256]{1,0:T(8,128)(2,1)S(1)}, bf16[64,256]{1,0:T(8,128)(2,1)S(1)}) custom-call(bf16[64,256]{1,0:T(8,128)(2,1)S(1)} %collective-permute-done.6.third, bf16[64,256]{1,0:T(8,128)(2,1)S(1)} %collective-permute-done.7.near_one, ...), custom_call_target="tpu_custom_call" | custom-call | flops 1610000000 | tf_op jit(solution)/shard_map/entering/pallas_call | solution.py:460
  43.0 0.5 collective-permute-start.12
  43.5 0.5 %collective-permute-start.13 = (bf16[64,256]{1,0:T(8,128)(2,1)S(1)}, bf16[64,256]{1,0:T(8,128)(2,1)S(1)}, u32[]{:S(2)}, u32[]{:S(2)}) collective-permute-start(bf16[64,256]{1,0:T(8,128)(2,1)S(1)} %get-tuple-element.42), channel_id=1, source_target_pairs={{0,2},{1,3},{2,0},{3,1},{4,6},{5,7},{6,4},{7,5},{8,10},{9,11},{10,... | collective-permute-start | bytes 98312 | tf_op jit(solution)/shard_map/ppermute | solution.py:512
  44.0 0.9 %collective-permute-start.14 = (bf16[64,256]{1,0:T(8,128)(2,1)S(1)}, bf16[64,256]{1,0:T(8,128)(2,1)S(1)}, u32[]{:S(2)}, u32[]{:S(2)}) collective-permute-start(bf16[64,256]{1,0:T(8,128)(2,1)S(1)} %get-tuple-element.43), channel_id=1, source_target_pairs={{0,1},{1,0},{2,3},{3,2},{4,5},{5,4},{6,7},{7,6},{8,9},{9,8},{10,11... | collective-permute-start | bytes 98312 | tf_op jit(solution)/shard_map/ppermute | solution.py:508
  45.0 1.9 %prop.1 = bf16[2,1024,256]{2,1,0:T(8,128)(2,1)S(1)} custom-call(s32[2,8]{1,0:T(2,128)S(1)} %bitcast.19, bf16[2,1024,1024]{2,1,0:T(8,128)(2,1)S(1)} %bitcast.13, bf16[1024,256]{1,0:T(8,128)(2,1)S(1)} %bitcast.17, bf16[64,256]{1,0:T(8,128)(2,1)S(1)} %get-tuple-element.40._tie.own), custom_call_target="tpu_custom_call" | custom-call | flops 1724999936 | tf_op jit(solution)/shard_map/prop/pallas_call | solution.py:244
  46.9 0.5 %collective-permute-done.13.across = bf16[64,256]{1,0:T(8,128)(2,1)S(1)} collective-permute-done((bf16[64,256]{1,0:T(8,128)(2,1)S(1)}, bf16[64,256]{1,0:T(8,128)(2,1)S(1)}, u32[]{:S(2)}, u32[]{:S(2)}) %collective-permute-start.13) | collective-permute-done | bytes 32800 | tf_op jit(solution)/shard_map/ppermute | solution.py:512
  47.4 1.2 %waves.1 = bf16[2,1024,128]{2,1,0:T(8,128)(2,1)} custom-call(bf16[64,256]{1,0:T(8,128)(2,1)S(1)} %get-tuple-element.40._tie.own, bf16[64,256]{1,0:T(8,128)(2,1)S(1)} %collective-permute-done.12.far, bf16[64,256]{1,0:T(8,128)(2,1)S(1)} %collective-permute-done.13.across, bf16[64,256]{1,0:T(8,128)(2,1)S(1)} %collective-permute-done.14.near, ...), custom_call_target="tpu_custom_call" | custom-call | flops 1495000064 | tf_op jit(solution)/shard_map/waves/pallas_call | solution.py:491
  (10 shorter events, 0.0 us)
Async XLA Ops:
  0.0 11.5 %copy-start.3 = (bf16[1,1024,256]{2,1,0:T(8,128)(2,1)S(1)}, bf16[1,1024,256]{2,1,0:T(8,128)(2,1)}, u32[]{:S(2)}) copy-start(bf16[1,1024,256]{2,1,0:T(8,128)(2,1)} %param.8) | copy-start | bytes 1572868
  0.0 11.5 %copy-start.4 = (s32[1,8,2]{1,2,0:T(2,128)S(1)}, s32[1,8,2]{1,2,0:T(2,128)}, u32[]{:S(2)}) copy-start(s32[1,8,2]{1,2,0:T(2,128)} %param.9) | copy-start | bytes 196
  4.0 22.6 %copy-start.2 = (bf16[1,2,1024,128]{3,2,1,0:T(8,128)(2,1)S(1)}, bf16[1,2,1024,128]{3,2,1,0:T(8,128)(2,1)}, u32[]{:S(2)}) copy-start(bf16[1,2,1024,128]{3,2,1,0:T(8,128)(2,1)} %param.7) | copy-start | bytes 1572868
  4.0 22.6 %all-to-all-start = ((bf16[16,136,128]{2,1,0:T(8,128)(2,1)}), bf16[16,136,128]{2,1,0:T(8,128)(2,1)S(1)}, u32[]{:S(2)}, u32[]{:S(2)}) async-start(bf16[16,136,128]{2,1,0:T(8,128)(2,1)} %pairs.1), calls=%async_computation | async-start | bytes 1114112 | tf_op jit(solution)/shard_map/all_to_all | solution.py:562
  11.5 2.2 %copy-start = (bf16[1,2,1024,1024]{3,2,1,0:T(8,128)(2,1)S(1)}, bf16[1,2,1024,1024]{3,2,1,0:T(8,128)(2,1)}, u32[]{:S(2)}) copy-start(bf16[1,2,1024,1024]{3,2,1,0:T(8,128)(2,1)} %param.6) | copy-start | bytes 12582916
  14.8 0.8 %copy-start.5 = (bf16[256,1024]{1,0:T(8,128)(2,1)}, bf16[256,1024]{1,0:T(8,128)(2,1)S(1)}, u32[]{:S(2)}) copy-start(bf16[256,1024]{1,0:T(8,128)(2,1)S(1)} %get-tuple-element.26.refs_1_) | copy-start | bytes 1572868
  15.6 12.5 %collective-permute-start.3 = (f32[256,256]{1,0:T(8,128)S(1)}, f32[256,256]{1,0:T(8,128)S(1)}, u32[]{:S(2)}, u32[]{:S(2)}) collective-permute-start(f32[256,256]{1,0:T(8,128)S(1)} %get-tuple-element.32), channel_id=1, source_target_pairs={{0,2},{1,3},{2,0},{3,1},{4,6},{5,7},{6,4},{7,5},{8,10},{9,11},{10,... | collective-permute-start | bytes 786440 | tf_op jit(solution)/shard_map/ppermute | solution.py:512
  17.5 12.8 %collective-permute-start.5 = (f32[256,256]{1,0:T(8,128)S(1)}, f32[256,256]{1,0:T(8,128)S(1)}, u32[]{:S(2)}, u32[]{:S(2)}) collective-permute-start(f32[256,256]{1,0:T(8,128)S(1)} %get-tuple-element.31.own), channel_id=1, source_target_pairs={{0,1},{1,0},{2,3},{3,2},{4,5},{5,4},{6,7},{7,6},{8,9},{9,8},{10,11... | collective-permute-start | bytes 786440 | tf_op jit(solution)/shard_map/ppermute | solution.py:508
  26.6 1.0 %copy-start.6 = (bf16[256,1024]{1,0:T(8,128)(2,1)S(1)}, bf16[256,1024]{1,0:T(8,128)(2,1)}, u32[]{:S(2)}) copy-start(bf16[256,1024]{1,0:T(8,128)(2,1)} %copy-done.5) | copy-start | bytes 1572868
  27.5 3.7 %copy-start.1 = (bf16[1,2,1024,1024]{3,2,1,0:T(8,128)(2,1)S(1)}, bf16[1,2,1024,1024]{3,2,1,0:T(8,128)(2,1)}, u32[]{:S(2)}) copy-start(bf16[1,2,1024,1024]{3,2,1,0:T(8,128)(2,1)} %param.6) | copy-start | bytes 12582916
  28.1 2.2 %collective-permute-start.4 = (f32[256,256]{1,0:T(8,128)S(1)}, f32[256,256]{1,0:T(8,128)S(1)}, u32[]{:S(2)}, u32[]{:S(2)}) collective-permute-start(f32[256,256]{1,0:T(8,128)S(1)} %after_exchange.1.across), channel_id=1, source_target_pairs={{0,1},{1,0},{2,3},{3,2},{4,5},{5,4},{6,7},{7,6},{8,9},{9,8},{10,11... | collective-permute-start | bytes 786440 | tf_op jit(solution)/shard_map/ppermute | solution.py:508
  28.2 5.5 %collective-permute-start = (bf16[64,256]{1,0:T(8,128)(2,1)S(1)}, bf16[64,256]{1,0:T(8,128)(2,1)S(1)}, u32[]{:S(2)}, u32[]{:S(2)}) collective-permute-start(bf16[64,256]{1,0:T(8,128)(2,1)S(1)} %get-tuple-element.28), channel_id=1, source_target_pairs={{0,3},{1,2},{2,1},{3,0},{4,7},{5,6},{6,5},{7,4},{8,11},{9,10},{10,... | collective-permute-start | bytes 98312 | tf_op jit(solution)/shard_map/ppermute | solution.py:516
  29.1 4.6 %collective-permute-start.1 = (bf16[64,256]{1,0:T(8,128)(2,1)S(1)}, bf16[64,256]{1,0:T(8,128)(2,1)S(1)}, u32[]{:S(2)}, u32[]{:S(2)}) collective-permute-start(bf16[64,256]{1,0:T(8,128)(2,1)S(1)} %get-tuple-element.29), channel_id=1, source_target_pairs={{0,2},{1,3},{2,0},{3,1},{4,6},{5,7},{6,4},{7,5},{8,10},{9,11},{10,... | collective-permute-start | bytes 98312 | tf_op jit(solution)/shard_map/ppermute | solution.py:512
  30.3 3.4 %collective-permute-start.2 = (bf16[64,256]{1,0:T(8,128)(2,1)S(1)}, bf16[64,256]{1,0:T(8,128)(2,1)S(1)}, u32[]{:S(2)}, u32[]{:S(2)}) collective-permute-start(bf16[64,256]{1,0:T(8,128)(2,1)S(1)} %get-tuple-element.30), channel_id=1, source_target_pairs={{0,1},{1,0},{2,3},{3,2},{4,5},{5,4},{6,7},{7,6},{8,9},{9,8},{10,11... | collective-permute-start | bytes 98312 | tf_op jit(solution)/shard_map/ppermute | solution.py:508
  33.0 8.4 %collective-permute-start.10 = (bf16[256,256]{1,0:T(8,128)(2,1)S(1)}, bf16[256,256]{1,0:T(8,128)(2,1)S(1)}, u32[]{:S(2)}, u32[]{:S(2)}) collective-permute-start(bf16[256,256]{1,0:T(8,128)(2,1)S(1)} %get-tuple-element.36), channel_id=1, source_target_pairs={{4,8},{8,12},{5,13},{6,10},{10,14},{7,15},{20,24},{24,28},{21,29},... | collective-permute-start | bytes 393224 | tf_op jit(solution)/shard_map/ppermute | solution.py:534
  34.3 7.9 %collective-permute-start.6 = (bf16[64,256]{1,0:T(8,128)(2,1)S(1)}, bf16[64,256]{1,0:T(8,128)(2,1)S(1)}, u32[]{:S(2)}, u32[]{:S(2)}) collective-permute-start(bf16[64,256]{1,0:T(8,128)(2,1)S(1)} %get-tuple-element.35), channel_id=1, source_target_pairs={{0,12},{1,13},{2,14},{3,15},{16,28},{17,29},{18,30},{19,31}} | collective-permute-start | bytes 98312 | tf_op jit(solution)/shard_map/ppermute | solution.py:540
  38.1 4.1 %collective-permute-start.7 = (bf16[64,256]{1,0:T(8,128)(2,1)S(1)}, bf16[64,256]{1,0:T(8,128)(2,1)S(1)}, u32[]{:S(2)}, u32[]{:S(2)}) collective-permute-start(bf16[64,256]{1,0:T(8,128)(2,1)S(1)} %get-tuple-element.35), channel_id=1, source_target_pairs={{0,4},{1,5},{2,6},{3,7},{16,20},{17,21},{18,22},{19,23}} | collective-permute-start | bytes 98312 | tf_op jit(solution)/shard_map/ppermute | solution.py:540
  39.4 2.9 %collective-permute-start.8 = (bf16[64,256]{1,0:T(8,128)(2,1)S(1)}, bf16[64,256]{1,0:T(8,128)(2,1)S(1)}, u32[]{:S(2)}, u32[]{:S(2)}) collective-permute-start(bf16[64,256]{1,0:T(8,128)(2,1)S(1)} %get-tuple-element.35), channel_id=1, source_target_pairs={{0,8},{1,9},{2,10},{3,11},{4,12},{5,13},{6,14},{7,15},{16,24},{17,... | collective-permute-start | bytes 98312 | tf_op jit(solution)/shard_map/ppermute | solution.py:540
  40.7 1.6 %collective-permute-start.9 = (bf16[64,256]{1,0:T(8,128)(2,1)S(1)}, bf16[64,256]{1,0:T(8,128)(2,1)S(1)}, u32[]{:S(2)}, u32[]{:S(2)}) collective-permute-start(bf16[64,256]{1,0:T(8,128)(2,1)S(1)} %get-tuple-element.35), channel_id=1, source_target_pairs={{4,8},{5,9},{6,10},{7,11},{8,12},{9,13},{10,14},{11,15},{20,24},{2... | collective-permute-start | bytes 98312 | tf_op jit(solution)/shard_map/ppermute | solution.py:540
  41.4 0.9 %collective-permute-start.11 = (bf16[256,256]{1,0:T(8,128)(2,1)S(1)}, bf16[256,256]{1,0:T(8,128)(2,1)S(1)}, u32[]{:S(2)}, u32[]{:S(2)}) collective-permute-start(bf16[256,256]{1,0:T(8,128)(2,1)S(1)} %collective-permute-done.10.got), channel_id=1, source_target_pairs={{8,9},{9,8},{10,11},{11,10},{12,13},{13,12},{14,15},{15,14},{24,25... | collective-permute-start | bytes 393224 | tf_op jit(solution)/shard_map/ppermute | solution.py:535
  43.0 3.8 %collective-permute-start.12 = (bf16[64,256]{1,0:T(8,128)(2,1)S(1)}, bf16[64,256]{1,0:T(8,128)(2,1)S(1)}, u32[]{:S(2)}, u32[]{:S(2)}) collective-permute-start(bf16[64,256]{1,0:T(8,128)(2,1)S(1)} %get-tuple-element.41), channel_id=1, source_target_pairs={{0,3},{1,2},{2,1},{3,0},{4,7},{5,6},{6,5},{7,4},{8,11},{9,10},{10,... | collective-permute-start | bytes 98312 | tf_op jit(solution)/shard_map/ppermute | solution.py:516
  43.5 3.9 %collective-permute-start.13 = (bf16[64,256]{1,0:T(8,128)(2,1)S(1)}, bf16[64,256]{1,0:T(8,128)(2,1)S(1)}, u32[]{:S(2)}, u32[]{:S(2)}) collective-permute-start(bf16[64,256]{1,0:T(8,128)(2,1)S(1)} %get-tuple-element.42), channel_id=1, source_target_pairs={{0,2},{1,3},{2,0},{3,1},{4,6},{5,7},{6,4},{7,5},{8,10},{9,11},{10,... | collective-permute-start | bytes 98312 | tf_op jit(solution)/shard_map/ppermute | solution.py:512
  44.0 3.4 %collective-permute-start.14 = (bf16[64,256]{1,0:T(8,128)(2,1)S(1)}, bf16[64,256]{1,0:T(8,128)(2,1)S(1)}, u32[]{:S(2)}, u32[]{:S(2)}) collective-permute-start(bf16[64,256]{1,0:T(8,128)(2,1)S(1)} %get-tuple-element.43), channel_id=1, source_target_pairs={{0,1},{1,0},{2,3},{3,2},{4,5},{5,4},{6,7},{7,6},{8,9},{9,8},{10,11... | collective-permute-start | bytes 98312 | tf_op jit(solution)/shard_map/ppermute | solution.py:508

commit v38 on v34

--- a/solution.py
+++ b/solution.py
@@ -79,13 +79,13 @@
     return y[:rows] + (y[rows:] + dot_rows(high, maps[1]))
 
 
-def mask_tiles(pattern, coupling):
+def mask_tiles(pattern, coupling, couple):
     high, wide = coupling.shape[0] // pattern.shape[1], coupling.shape[1] // pattern.shape[0]
     for i in range(pattern.shape[1]):
         for j in range(pattern.shape[0]):
             at = (slice(i * high, (i + 1) * high), slice(j * wide, (j + 1) * wide))
             tile = coupling[at]
-            coupling[at] = jnp.where(pattern[j, i] == 1, tile, jnp.zeros_like(tile))
+            couple[at] = jnp.where(pattern[j, i] == 1, tile, jnp.zeros_like(tile))
 
 
 def pairs_kernel(owner_in, blocks_in, green, inject_in, out, owner, blocks, inject, held, product, slot_of, counts, sem, side, done, *packets):
@@ -208,8 +208,7 @@
     face_rows, (couple, maps) = refs[:-2], refs[-2:]
     energies, orbitals, _ = green.shape
     face = coupling.shape[1]
-    couple[...] = coupling[...]
-    mask_tiles(pattern, couple)
+    mask_tiles(pattern, coupling, couple)
     for e in range(energies):
         rows = green[e, orbitals - face :, :]
         face_rows[e][...] = rows
@@ -233,8 +232,7 @@
 
 
 def prop_kernel(pattern, green, coupling, _tie, out, couple):
-    couple[...] = coupling[...]
-    mask_tiles(pattern, couple)
+    mask_tiles(pattern, coupling, couple)
     for e in range(green.shape[0]):
         out[e] = dot(green[e], couple[...]).astype(BF16)
 

time: 49.1 us -> 49.1 us (level)
  no operation moved by 1% of the time
where the time goes in v38:
time: 49.1 us; the launch traced here: 48.6 us
  starting transfers between devices  22 us (45%)
  Pallas kernels  13.6 us (28%)
  waiting for transfers between devices  9.74 us (20%)
  local copies, waits for them, and re-layouts  3.08 us (6%)
    all_to_all x1, waiting for transfers between devices, per_device(): lax.all_to_all(outgoing, 'sec', split_axis=0, concat_axis=0, tiled=True)  9.05 us
    all_to_all x1, starting transfers between devices, per_device(): lax.all_to_all(outgoing, 'sec', split_axis=0, concat_axis=0, tiled=True)  7.49 us
    ppermute x4, starting transfers between devices, between(): return lax.ppermute(item, 'sec', pairs)  7.06 us
    pallas_call x1, Pallas kernels, outgoing_pairs(): pl.pallas_call(pairs_kernel, name='pairs', in_specs=[IN_HBM] * 4, out_sha...  3.96 us
    ppermute x3, starting transfers between devices, to_across(): lax.ppermute(item, 'sec', [(s, s // GROUP * GROUP + (s % GROUP + CORES) %...  3.65 us
    unnamed x14, local copies, waits for them, and re-layouts  3.08 us
    pallas_call x2, Pallas kernels, image_and_maps(): call(functools.partial(work_kernel, not held), 'image_and_maps', [IN_VMEM...  1.91 us
    pallas_call x1, Pallas kernels, propagator(): call(prop_kernel, 'prop', [IN_SMEM, IN_VMEM, IN_VMEM, IN_PLACE], shape(en...  1.85 us
  transfers between devices with their start and end apart: 16, of which 3 were waited for; matrix products, arithmetic and copies ran while one was open for 0% of the time, Pallas kernels for 16%

profile of v38, /device:TPU:0, one launch (start us, length us, event | category | flops | bytes accessed | tf_op | source)
XLA Modules:
  0.0 48.6 jit_solution(7450024517067799287)
XLA Ops:
  0.0 4.0 %pairs.1 = bf16[16,136,128]{2,1,0:T(8,128)(2,1)} custom-call(s32[16]{0:T(128)} %bitcast.21, s32[2,16]{1,0:T(2,128)} %bitcast.20, bf16[2,1024,1024]{2,1,0:T(8,128)(2,1)} %bitcast.9, bf16[2,1024,128]{2,1,0:T(8,128)(2,1)} %bitcast.14), custom_call_target="tpu_custom_call" | custom-call | flops 4600000000 | tf_op jit(solution)/shard_map/pairs/pallas_call | solution.py:183
  4.0 0.0 copy-start.2
  4.0 7.5 %all-to-all-start = ((bf16[16,136,128]{2,1,0:T(8,128)(2,1)}), bf16[16,136,128]{2,1,0:T(8,128)(2,1)S(1)}, u32[]{:S(2)}, u32[]{:S(2)}) async-start(bf16[16,136,128]{2,1,0:T(8,128)(2,1)} %pairs.1), calls=%async_computation | async-start | bytes 1114112 | tf_op jit(solution)/shard_map/all_to_all | solution.py:560
  11.5 0.0 copy-start
  11.5 2.2 %copy-done = bf16[1,2,1024,1024]{3,2,1,0:T(8,128)(2,1)S(1)} copy-done((bf16[1,2,1024,1024]{3,2,1,0:T(8,128)(2,1)S(1)}, bf16[1,2,1024,1024]{3,2,1,0:T(8,128)(2,1)}, u32[]{:S(2)}) %copy-start) | copy-done | bytes 4194328
  13.7 1.1 %face_maps.1 = (f32[256,256]{1,0:T(8,128)S(1)}, f32[256,256]{1,0:T(8,128)S(1)}, bf16[256,1024]{1,0:T(8,128)(2,1)S(1)}, bf16[256,1024]{1,0:T(8,128)(2,1)S(1)}) custom-call(s32[2,8]{1,0:T(2,128)S(1)} %bitcast.18, bf16[2,1024,1024]{2,1,0:T(8,128)(2,1)S(1)} %bitcast.10, bf16[1024,256]{1,0:T(8,128)(2,1)S(1)} %bitcast.16), custom_call_target="tpu_custom_call" | custom-call | flops 1380000000 | tf_op jit(solution)/shard_map/face_maps/pallas_call | solution.py:224
  14.8 0.0 copy-start.5
  14.8 0.8 %copy-done.5 = bf16[256,1024]{1,0:T(8,128)(2,1)} copy-done((bf16[256,1024]{1,0:T(8,128)(2,1)}, bf16[256,1024]{1,0:T(8,128)(2,1)S(1)}, u32[]{:S(2)}) %copy-start.5) | copy-done | bytes 524312
  15.6 1.9 %collective-permute-start.3 = (f32[256,256]{1,0:T(8,128)S(1)}, f32[256,256]{1,0:T(8,128)S(1)}, u32[]{:S(2)}, u32[]{:S(2)}) collective-permute-start(f32[256,256]{1,0:T(8,128)S(1)} %get-tuple-element.32), channel_id=1, source_target_pairs={{0,2},{1,3},{2,0},{3,1},{4,6},{5,7},{6,4},{7,5},{8,10},{9,11},{10,... | collective-permute-start | bytes 786440 | tf_op jit(solution)/shard_map/ppermute | solution.py:510
  17.5 0.0 collective-permute-start.5
  17.5 9.1 %all-to-all-done.received = bf16[16,136,128]{2,1,0:T(8,128)(2,1)S(1)} async-done(((bf16[16,136,128]{2,1,0:T(8,128)(2,1)}), bf16[16,136,128]{2,1,0:T(8,128)(2,1)S(1)}, u32[]{:S(2)}, u32[]{:S(2)}) %all-to-all-start) | async-done | bytes 557088 | tf_op jit(solution)/shard_map/all_to_all | solution.py:560
  26.6 0.9 %source.1.refs_1_ = bf16[2,1024,128]{2,1,0:T(8,128)(2,1)S(1)} custom-call(bf16[16,136,128]{2,1,0:T(8,128)(2,1)S(1)} %all-to-all-done.received, bf16[2,1024,128]{2,1,0:T(8,128)(2,1)S(1)} %bitcast.15), custom_call_target="tpu_custom_call" | custom-call | flops 1150000000 | tf_op jit(solution)/shard_map/source/pallas_call | solution.py:309
  27.5 0.0 copy-start.1
  27.5 0.1 copy-done.6
  27.6 0.5 %face_quarters.1 = (bf16[64,256]{1,0:T(8,128)(2,1)S(1)}, bf16[64,256]{1,0:T(8,128)(2,1)S(1)}, bf16[64,256]{1,0:T(8,128)(2,1)S(1)}, bf16[64,256]{1,0:T(8,128)(2,1)S(1)}) custom-call(bf16[2,1024,128]{2,1,0:T(8,128)(2,1)S(1)} %source.1.refs_1_, bf16[256,1024]{1,0:T(8,128)(2,1)S(1)} %get-tuple-element.25.refs_0_, bf16[256,1024]{1,0:T(8,128)(2,1)S(1)} %copy-done.6), custom_call_target="tpu_custom_call" | custom-call | flops 690000000 | tf_op jit(solution)/shard_map/face_quarters/pallas_call | solution.py:342
  28.1 0.0 collective-permute-done.3._map
  28.1 0.1 collective-permute-start.4
  28.2 0.9 %collective-permute-start = (bf16[64,256]{1,0:T(8,128)(2,1)S(1)}, bf16[64,256]{1,0:T(8,128)(2,1)S(1)}, u32[]{:S(2)}, u32[]{:S(2)}) collective-permute-start(bf16[64,256]{1,0:T(8,128)(2,1)S(1)} %get-tuple-element.28), channel_id=1, source_target_pairs={{0,3},{1,2},{2,1},{3,0},{4,7},{5,6},{6,5},{7,4},{8,11},{9,10},{10,... | collective-permute-start | bytes 98312 | tf_op jit(solution)/shard_map/ppermute | solution.py:514
  29.1 1.3 %collective-permute-start.1 = (bf16[64,256]{1,0:T(8,128)(2,1)S(1)}, bf16[64,256]{1,0:T(8,128)(2,1)S(1)}, u32[]{:S(2)}, u32[]{:S(2)}) collective-permute-start(bf16[64,256]{1,0:T(8,128)(2,1)S(1)} %get-tuple-element.29), channel_id=1, source_target_pairs={{0,2},{1,3},{2,0},{3,1},{4,6},{5,7},{6,4},{7,5},{8,10},{9,11},{10,... | collective-permute-start | bytes 98312 | tf_op jit(solution)/shard_map/ppermute | solution.py:510
  30.4 0.0 collective-permute-start.2
  30.4 0.0 collective-permute-done.5.near
  30.4 0.0 collective-permute-done.4.far
  30.4 0.8 %chain_maps.1 = (bf16[256,256]{1,0:T(8,128)(2,1)S(1)}, bf16[2,4,256,256]{3,2,1,0:T(8,128)(2,1)S(1)}) custom-call(f32[256,256]{1,0:T(8,128)S(1)} %get-tuple-element.31.own, f32[256,256]{1,0:T(8,128)S(1)} %collective-permute-done.4.far, f32[256,256]{1,0:T(8,128)S(1)} %after_exchange.1.across, f32[256,256]{1,0:T(8,128)S(1)} %collective-permute-done.5.near), custom_call_target="tpu_custom_call" | custom-call | flops 1035000000 | tf_op jit(solution)/shard_map/chain_maps/pallas_call | solution.py:268
  31.2 1.8 %image_and_maps.2 = (f32[2,1024,128]{2,1,0:T(8,128)S(1)}, bf16[2,2,256,256]{3,2,1,0:T(8,128)(2,1)S(1)}) custom-call(bf16[2,1024,1024]{2,1,0:T(8,128)(2,1)S(1)} %bitcast.11, bf16[2,1024,128]{2,1,0:T(8,128)(2,1)S(1)} %source.1.refs_1_, bf16[2,4,256,256]{3,2,1,0:T(8,128)(2,1)S(1)} %get-tuple-element.33.refs_2_.parts), custom_call_target="tpu_custom_call" | custom-call | flops 2300000000 | tf_op jit(solution)/shard_map/image_and_maps/pallas_call | solution.py:418
  33.0 0.7 %collective-permute-start.10 = (bf16[256,256]{1,0:T(8,128)(2,1)S(1)}, bf16[256,256]{1,0:T(8,128)(2,1)S(1)}, u32[]{:S(2)}, u32[]{:S(2)}) collective-permute-start(bf16[256,256]{1,0:T(8,128)(2,1)S(1)} %get-tuple-element.36), channel_id=1, source_target_pairs={{4,8},{8,12},{5,13},{6,10},{10,14},{7,15},{20,24},{24,28},{21,29},... | collective-permute-start | bytes 393224 | tf_op jit(solution)/shard_map/ppermute | solution.py:532
  33.7 0.0 collective-permute-done.far
  33.7 0.0 collective-permute-done.1.across
  33.7 0.0 collective-permute-done.2.near
  33.7 0.6 %plane_total.1 = (bf16[64,256]{1,0:T(8,128)(2,1)S(1)}, f32[3,64,256]{2,1,0:T(8,128)S(1)}) custom-call(bf16[64,256]{1,0:T(8,128)(2,1)S(1)} %get-tuple-element.27._packets.own, bf16[64,256]{1,0:T(8,128)(2,1)S(1)} %collective-permute-done.far, bf16[64,256]{1,0:T(8,128)(2,1)S(1)} %collective-permute-done.1.across, ...), custom_call_target="tpu_custom_call" | custom-call | flops 3449999872 | tf_op jit(solution)/shard_map/plane_total/pallas_call | solution.py:384
  34.3 3.8 %collective-permute-start.6 = (bf16[64,256]{1,0:T(8,128)(2,1)S(1)}, bf16[64,256]{1,0:T(8,128)(2,1)S(1)}, u32[]{:S(2)}, u32[]{:S(2)}) collective-permute-start(bf16[64,256]{1,0:T(8,128)(2,1)S(1)} %get-tuple-element.35), channel_id=1, source_target_pairs={{0,12},{1,13},{2,14},{3,15},{16,28},{17,29},{18,30},{19,31}} | collective-permute-start | bytes 98312 | tf_op jit(solution)/shard_map/ppermute | solution.py:538
  38.1 1.3 %collective-permute-start.7 = (bf16[64,256]{1,0:T(8,128)(2,1)S(1)}, bf16[64,256]{1,0:T(8,128)(2,1)S(1)}, u32[]{:S(2)}, u32[]{:S(2)}) collective-permute-start(bf16[64,256]{1,0:T(8,128)(2,1)S(1)} %get-tuple-element.35), channel_id=1, source_target_pairs={{0,4},{1,5},{2,6},{3,7},{16,20},{17,21},{18,22},{19,23}} | collective-permute-start | bytes 98312 | tf_op jit(solution)/shard_map/ppermute | solution.py:538
  39.4 1.3 %collective-permute-start.8 = (bf16[64,256]{1,0:T(8,128)(2,1)S(1)}, bf16[64,256]{1,0:T(8,128)(2,1)S(1)}, u32[]{:S(2)}, u32[]{:S(2)}) collective-permute-start(bf16[64,256]{1,0:T(8,128)(2,1)S(1)} %get-tuple-element.35), channel_id=1, source_target_pairs={{0,8},{1,9},{2,10},{3,11},{4,12},{5,13},{6,14},{7,15},{16,24},{17,... | collective-permute-start | bytes 98312 | tf_op jit(solution)/shard_map/ppermute | solution.py:538
  40.7 0.7 %collective-permute-start.9 = (bf16[64,256]{1,0:T(8,128)(2,1)S(1)}, bf16[64,256]{1,0:T(8,128)(2,1)S(1)}, u32[]{:S(2)}, u32[]{:S(2)}) collective-permute-start(bf16[64,256]{1,0:T(8,128)(2,1)S(1)} %get-tuple-element.35), channel_id=1, source_target_pairs={{4,8},{5,9},{6,10},{7,11},{8,12},{9,13},{10,14},{11,15},{20,24},{2... | collective-permute-start | bytes 98312 | tf_op jit(solution)/shard_map/ppermute | solution.py:538
  41.4 0.0 collective-permute-done.10.got
  41.4 0.7 %collective-permute-start.11 = (bf16[256,256]{1,0:T(8,128)(2,1)S(1)}, bf16[256,256]{1,0:T(8,128)(2,1)S(1)}, u32[]{:S(2)}, u32[]{:S(2)}) collective-permute-start(bf16[256,256]{1,0:T(8,128)(2,1)S(1)} %collective-permute-done.10.got), channel_id=1, source_target_pairs={{8,9},{9,8},{10,11},{11,10},{12,13},{13,12},{14,15},{15,14},{24,25... | collective-permute-start | bytes 393224 | tf_op jit(solution)/shard_map/ppermute | solution.py:533
  42.1 0.1 image_and_maps.3
  42.2 0.0 collective-permute-done.6.third
  42.2 0.0 collective-permute-done.7.near_one
  42.2 0.1 collective-permute-done.8.second
  42.3 0.0 collective-permute-done.9.far_one
  42.3 0.0 collective-permute-done.11.other
  42.3 0.7 %entering.1 = (bf16[64,256]{1,0:T(8,128)(2,1)S(1)}, bf16[64,256]{1,0:T(8,128)(2,1)S(1)}, bf16[64,256]{1,0:T(8,128)(2,1)S(1)}, bf16[64,256]{1,0:T(8,128)(2,1)S(1)}) custom-call(bf16[64,256]{1,0:T(8,128)(2,1)S(1)} %collective-permute-done.6.third, bf16[64,256]{1,0:T(8,128)(2,1)S(1)} %collective-permute-done.7.near_one, ...), custom_call_target="tpu_custom_call" | custom-call | flops 1610000000 | tf_op jit(solution)/shard_map/entering/pallas_call | solution.py:458
  43.1 0.5 collective-permute-start.12
  43.5 0.5 collective-permute-start.13
  44.0 1.0 %collective-permute-start.14 = (bf16[64,256]{1,0:T(8,128)(2,1)S(1)}, bf16[64,256]{1,0:T(8,128)(2,1)S(1)}, u32[]{:S(2)}, u32[]{:S(2)}) collective-permute-start(bf16[64,256]{1,0:T(8,128)(2,1)S(1)} %get-tuple-element.43), channel_id=1, source_target_pairs={{0,1},{1,0},{2,3},{3,2},{4,5},{5,4},{6,7},{7,6},{8,9},{9,8},{10,11... | collective-permute-start | bytes 98312 | tf_op jit(solution)/shard_map/ppermute | solution.py:506
  45.0 1.9 %prop.1 = bf16[2,1024,256]{2,1,0:T(8,128)(2,1)S(1)} custom-call(s32[2,8]{1,0:T(2,128)S(1)} %bitcast.19, bf16[2,1024,1024]{2,1,0:T(8,128)(2,1)S(1)} %bitcast.13, bf16[1024,256]{1,0:T(8,128)(2,1)S(1)} %bitcast.17, bf16[64,256]{1,0:T(8,128)(2,1)S(1)} %get-tuple-element.40._tie.own), custom_call_target="tpu_custom_call" | custom-call | flops 1724999936 | tf_op jit(solution)/shard_map/prop/pallas_call | solution.py:242
  46.9 0.6 %collective-permute-done.13.across = bf16[64,256]{1,0:T(8,128)(2,1)S(1)} collective-permute-done((bf16[64,256]{1,0:T(8,128)(2,1)S(1)}, bf16[64,256]{1,0:T(8,128)(2,1)S(1)}, u32[]{:S(2)}, u32[]{:S(2)}) %collective-permute-start.13) | collective-permute-done | bytes 32800 | tf_op jit(solution)/shard_map/ppermute | solution.py:510
  47.4 1.2 %waves.1 = bf16[2,1024,128]{2,1,0:T(8,128)(2,1)} custom-call(bf16[64,256]{1,0:T(8,128)(2,1)S(1)} %get-tuple-element.40._tie.own, bf16[64,256]{1,0:T(8,128)(2,1)S(1)} %collective-permute-done.12.far, bf16[64,256]{1,0:T(8,128)(2,1)S(1)} %collective-permute-done.13.across, bf16[64,256]{1,0:T(8,128)(2,1)S(1)} %collective-permute-done.14.near, ...), custom_call_target="tpu_custom_call" | custom-call | flops 1495000064 | tf_op jit(solution)/shard_map/waves/pallas_call | solution.py:489
  (10 shorter events, 0.0 us)
Async XLA Ops:
  0.0 11.5 %copy-start.3 = (bf16[1,1024,256]{2,1,0:T(8,128)(2,1)S(1)}, bf16[1,1024,256]{2,1,0:T(8,128)(2,1)}, u32[]{:S(2)}) copy-start(bf16[1,1024,256]{2,1,0:T(8,128)(2,1)} %param.8) | copy-start | bytes 1572868
  0.0 11.5 %copy-start.4 = (s32[1,8,2]{1,2,0:T(2,128)S(1)}, s32[1,8,2]{1,2,0:T(2,128)}, u32[]{:S(2)}) copy-start(s32[1,8,2]{1,2,0:T(2,128)} %param.9) | copy-start | bytes 196
  4.0 22.6 %copy-start.2 = (bf16[1,2,1024,128]{3,2,1,0:T(8,128)(2,1)S(1)}, bf16[1,2,1024,128]{3,2,1,0:T(8,128)(2,1)}, u32[]{:S(2)}) copy-start(bf16[1,2,1024,128]{3,2,1,0:T(8,128)(2,1)} %param.7) | copy-start | bytes 1572868
  4.0 22.6 %all-to-all-start = ((bf16[16,136,128]{2,1,0:T(8,128)(2,1)}), bf16[16,136,128]{2,1,0:T(8,128)(2,1)S(1)}, u32[]{:S(2)}, u32[]{:S(2)}) async-start(bf16[16,136,128]{2,1,0:T(8,128)(2,1)} %pairs.1), calls=%async_computation | async-start | bytes 1114112 | tf_op jit(solution)/shard_map/all_to_all | solution.py:560
  11.5 2.2 %copy-start = (bf16[1,2,1024,1024]{3,2,1,0:T(8,128)(2,1)S(1)}, bf16[1,2,1024,1024]{3,2,1,0:T(8,128)(2,1)}, u32[]{:S(2)}) copy-start(bf16[1,2,1024,1024]{3,2,1,0:T(8,128)(2,1)} %param.6) | copy-start | bytes 12582916
  14.8 0.8 %copy-start.5 = (bf16[256,1024]{1,0:T(8,128)(2,1)}, bf16[256,1024]{1,0:T(8,128)(2,1)S(1)}, u32[]{:S(2)}) copy-start(bf16[256,1024]{1,0:T(8,128)(2,1)S(1)} %get-tuple-element.26.refs_1_) | copy-start | bytes 1572868
  15.6 12.5 %collective-permute-start.3 = (f32[256,256]{1,0:T(8,128)S(1)}, f32[256,256]{1,0:T(8,128)S(1)}, u32[]{:S(2)}, u32[]{:S(2)}) collective-permute-start(f32[256,256]{1,0:T(8,128)S(1)} %get-tuple-element.32), channel_id=1, source_target_pairs={{0,2},{1,3},{2,0},{3,1},{4,6},{5,7},{6,4},{7,5},{8,10},{9,11},{10,... | collective-permute-start | bytes 786440 | tf_op jit(solution)/shard_map/ppermute | solution.py:510
  17.5 12.9 %collective-permute-start.5 = (f32[256,256]{1,0:T(8,128)S(1)}, f32[256,256]{1,0:T(8,128)S(1)}, u32[]{:S(2)}, u32[]{:S(2)}) collective-permute-start(f32[256,256]{1,0:T(8,128)S(1)} %get-tuple-element.31.own), channel_id=1, source_target_pairs={{0,1},{1,0},{2,3},{3,2},{4,5},{5,4},{6,7},{7,6},{8,9},{9,8},{10,11... | collective-permute-start | bytes 786440 | tf_op jit(solution)/shard_map/ppermute | solution.py:506
  26.6 1.0 %copy-start.6 = (bf16[256,1024]{1,0:T(8,128)(2,1)S(1)}, bf16[256,1024]{1,0:T(8,128)(2,1)}, u32[]{:S(2)}) copy-start(bf16[256,1024]{1,0:T(8,128)(2,1)} %copy-done.5) | copy-start | bytes 1572868
  27.5 3.7 %copy-start.1 = (bf16[1,2,1024,1024]{3,2,1,0:T(8,128)(2,1)S(1)}, bf16[1,2,1024,1024]{3,2,1,0:T(8,128)(2,1)}, u32[]{:S(2)}) copy-start(bf16[1,2,1024,1024]{3,2,1,0:T(8,128)(2,1)} %param.6) | copy-start | bytes 12582916
  28.1 2.2 %collective-permute-start.4 = (f32[256,256]{1,0:T(8,128)S(1)}, f32[256,256]{1,0:T(8,128)S(1)}, u32[]{:S(2)}, u32[]{:S(2)}) collective-permute-start(f32[256,256]{1,0:T(8,128)S(1)} %after_exchange.1.across), channel_id=1, source_target_pairs={{0,1},{1,0},{2,3},{3,2},{4,5},{5,4},{6,7},{7,6},{8,9},{9,8},{10,11... | collective-permute-start | bytes 786440 | tf_op jit(solution)/shard_map/ppermute | solution.py:506
  28.2 5.5 %collective-permute-start = (bf16[64,256]{1,0:T(8,128)(2,1)S(1)}, bf16[64,256]{1,0:T(8,128)(2,1)S(1)}, u32[]{:S(2)}, u32[]{:S(2)}) collective-permute-start(bf16[64,256]{1,0:T(8,128)(2,1)S(1)} %get-tuple-element.28), channel_id=1, source_target_pairs={{0,3},{1,2},{2,1},{3,0},{4,7},{5,6},{6,5},{7,4},{8,11},{9,10},{10,... | collective-permute-start | bytes 98312 | tf_op jit(solution)/shard_map/ppermute | solution.py:514
  29.1 4.6 %collective-permute-start.1 = (bf16[64,256]{1,0:T(8,128)(2,1)S(1)}, bf16[64,256]{1,0:T(8,128)(2,1)S(1)}, u32[]{:S(2)}, u32[]{:S(2)}) collective-permute-start(bf16[64,256]{1,0:T(8,128)(2,1)S(1)} %get-tuple-element.29), channel_id=1, source_target_pairs={{0,2},{1,3},{2,0},{3,1},{4,6},{5,7},{6,4},{7,5},{8,10},{9,11},{10,... | collective-permute-start | bytes 98312 | tf_op jit(solution)/shard_map/ppermute | solution.py:510
  30.4 3.3 %collective-permute-start.2 = (bf16[64,256]{1,0:T(8,128)(2,1)S(1)}, bf16[64,256]{1,0:T(8,128)(2,1)S(1)}, u32[]{:S(2)}, u32[]{:S(2)}) collective-permute-start(bf16[64,256]{1,0:T(8,128)(2,1)S(1)} %get-tuple-element.30), channel_id=1, source_target_pairs={{0,1},{1,0},{2,3},{3,2},{4,5},{5,4},{6,7},{7,6},{8,9},{9,8},{10,11... | collective-permute-start | bytes 98312 | tf_op jit(solution)/shard_map/ppermute | solution.py:506
  33.0 8.4 %collective-permute-start.10 = (bf16[256,256]{1,0:T(8,128)(2,1)S(1)}, bf16[256,256]{1,0:T(8,128)(2,1)S(1)}, u32[]{:S(2)}, u32[]{:S(2)}) collective-permute-start(bf16[256,256]{1,0:T(8,128)(2,1)S(1)} %get-tuple-element.36), channel_id=1, source_target_pairs={{4,8},{8,12},{5,13},{6,10},{10,14},{7,15},{20,24},{24,28},{21,29},... | collective-permute-start | bytes 393224 | tf_op jit(solution)/shard_map/ppermute | solution.py:532
  34.3 7.9 %collective-permute-start.6 = (bf16[64,256]{1,0:T(8,128)(2,1)S(1)}, bf16[64,256]{1,0:T(8,128)(2,1)S(1)}, u32[]{:S(2)}, u32[]{:S(2)}) collective-permute-start(bf16[64,256]{1,0:T(8,128)(2,1)S(1)} %get-tuple-element.35), channel_id=1, source_target_pairs={{0,12},{1,13},{2,14},{3,15},{16,28},{17,29},{18,30},{19,31}} | collective-permute-start | bytes 98312 | tf_op jit(solution)/shard_map/ppermute | solution.py:538
  38.1 4.1 %collective-permute-start.7 = (bf16[64,256]{1,0:T(8,128)(2,1)S(1)}, bf16[64,256]{1,0:T(8,128)(2,1)S(1)}, u32[]{:S(2)}, u32[]{:S(2)}) collective-permute-start(bf16[64,256]{1,0:T(8,128)(2,1)S(1)} %get-tuple-element.35), channel_id=1, source_target_pairs={{0,4},{1,5},{2,6},{3,7},{16,20},{17,21},{18,22},{19,23}} | collective-permute-start | bytes 98312 | tf_op jit(solution)/shard_map/ppermute | solution.py:538
  39.4 2.9 %collective-permute-start.8 = (bf16[64,256]{1,0:T(8,128)(2,1)S(1)}, bf16[64,256]{1,0:T(8,128)(2,1)S(1)}, u32[]{:S(2)}, u32[]{:S(2)}) collective-permute-start(bf16[64,256]{1,0:T(8,128)(2,1)S(1)} %get-tuple-element.35), channel_id=1, source_target_pairs={{0,8},{1,9},{2,10},{3,11},{4,12},{5,13},{6,14},{7,15},{16,24},{17,... | collective-permute-start | bytes 98312 | tf_op jit(solution)/shard_map/ppermute | solution.py:538
  40.7 1.6 %collective-permute-start.9 = (bf16[64,256]{1,0:T(8,128)(2,1)S(1)}, bf16[64,256]{1,0:T(8,128)(2,1)S(1)}, u32[]{:S(2)}, u32[]{:S(2)}) collective-permute-start(bf16[64,256]{1,0:T(8,128)(2,1)S(1)} %get-tuple-element.35), channel_id=1, source_target_pairs={{4,8},{5,9},{6,10},{7,11},{8,12},{9,13},{10,14},{11,15},{20,24},{2... | collective-permute-start | bytes 98312 | tf_op jit(solution)/shard_map/ppermute | solution.py:538
  41.4 0.9 %collective-permute-start.11 = (bf16[256,256]{1,0:T(8,128)(2,1)S(1)}, bf16[256,256]{1,0:T(8,128)(2,1)S(1)}, u32[]{:S(2)}, u32[]{:S(2)}) collective-permute-start(bf16[256,256]{1,0:T(8,128)(2,1)S(1)} %collective-permute-done.10.got), channel_id=1, source_target_pairs={{8,9},{9,8},{10,11},{11,10},{12,13},{13,12},{14,15},{15,14},{24,25... | collective-permute-start | bytes 393224 | tf_op jit(solution)/shard_map/ppermute | solution.py:533
  43.1 3.8 %collective-permute-start.12 = (bf16[64,256]{1,0:T(8,128)(2,1)S(1)}, bf16[64,256]{1,0:T(8,128)(2,1)S(1)}, u32[]{:S(2)}, u32[]{:S(2)}) collective-permute-start(bf16[64,256]{1,0:T(8,128)(2,1)S(1)} %get-tuple-element.41), channel_id=1, source_target_pairs={{0,3},{1,2},{2,1},{3,0},{4,7},{5,6},{6,5},{7,4},{8,11},{9,10},{10,... | collective-permute-start | bytes 98312 | tf_op jit(solution)/shard_map/ppermute | solution.py:514
  43.5 3.9 %collective-permute-start.13 = (bf16[64,256]{1,0:T(8,128)(2,1)S(1)}, bf16[64,256]{1,0:T(8,128)(2,1)S(1)}, u32[]{:S(2)}, u32[]{:S(2)}) collective-permute-start(bf16[64,256]{1,0:T(8,128)(2,1)S(1)} %get-tuple-element.42), channel_id=1, source_target_pairs={{0,2},{1,3},{2,0},{3,1},{4,6},{5,7},{6,4},{7,5},{8,10},{9,11},{10,... | collective-permute-start | bytes 98312 | tf_op jit(solution)/shard_map/ppermute | solution.py:510
  44.0 3.4 %collective-permute-start.14 = (bf16[64,256]{1,0:T(8,128)(2,1)S(1)}, bf16[64,256]{1,0:T(8,128)(2,1)S(1)}, u32[]{:S(2)}, u32[]{:S(2)}) collective-permute-start(bf16[64,256]{1,0:T(8,128)(2,1)S(1)} %get-tuple-element.43), channel_id=1, source_target_pairs={{0,1},{1,0},{2,3},{3,2},{4,5},{5,4},{6,7},{7,6},{8,9},{9,8},{10,11... | collective-permute-start | bytes 98312 | tf_op jit(solution)/shard_map/ppermute | solution.py:506
